TPU v7x, 32 devices: a whole 2x2x4 slice. The times are simulated.
32 devices in a mesh: seq: 4 (over y, x), rep: 8 (over z, core).
Axes of the slice: x: 2, y: 2, z: 4, core: 2. Of those that a mesh axis runs over, the one named last changes fastest.
Arguments:
- inputs: bfloat16 [8, 4096, 768], P('rep', 'seq'), may hold values from -6 to 6
- trunk_grad: bfloat16 [8, 2048, 1536], P('rep', None, 'seq'), may hold values from -6 to 6
- weights: bfloat16 [5, 768, 1536], P(None, 'rep', 'seq'), may hold values from -0.09375 to 0.09375
Outputs:
- input_grad: bfloat16 [8, 4096, 768], P('rep', 'seq')
- weight_grad: float32 [5, 768, 1536], P(None, 'rep', 'seq')
All inputs are finite; a program needn't handle non-finite values.
Results may differ from a plain program's by a relative error of at most 0.0027.
Values may be sent and summed in bfloat16 or wider, within the bound.
No kernel may reach another device: no remote copies, remote signals or barrier semaphores. Data moves between devices by JAX's collectives and lax.ppermute only.
A program may use at most 192 MiB of HBM per device.

v0:
```python
import jax
import jax.numpy as jnp
from jax import lax
from jax.sharding import PartitionSpec as P


def with_halo(value, sides, width):
    for axis, dim in sides:
        peers, length = (lax.axis_size(axis), value.shape[dim])
        up = [(i, (i + 1) % peers) for i in range(peers - 1)]
        down = [(j, i) for i, j in up]
        last = lax.slice_in_dim(value, length - width, length, axis=dim)
        leading = lax.slice_in_dim(value, 0, width, axis=dim)
        before = lax.ppermute(last, axis, up)
        after = lax.ppermute(leading, axis, down)
        value = jnp.concatenate([before, value, after], axis=dim)
    return value


def contract_last(left, right):
    return lax.dot_general(
        left, right, (((1,), (1,)), ((), ())), preferred_element_type=jnp.float32
    )


def contract_first(left, right):
    return lax.dot_general(
        left, right, (((0,), (0,)), ((), ())), preferred_element_type=jnp.float32
    )


def on_device(inputs, trunk_grad, weights):
    taps = weights.shape[0]
    grad = lax.all_to_all(trunk_grad, "seq", split_axis=1, concat_axis=2, tiled=True)
    grad_up = jnp.repeat(grad.astype(jnp.float32) * 0.5, 2, axis=1).astype(jnp.bfloat16)
    rows = grad_up.shape[1]
    padded = with_halo(grad_up, (("seq", 1),), 2)
    shifts = [padded[0, 4 - k : 4 - k + rows] for k in range(taps)]
    inputs_f = inputs[0].astype(jnp.float32)
    act_vals, back = jax.vjp(jax.nn.gelu, inputs_f)
    slope = back(jnp.ones_like(inputs_f))[0]
    act = act_vals.astype(jnp.bfloat16)
    in_width = inputs.shape[2]
    columns = lax.all_gather(weights, "seq", axis=2, tiled=True)
    piece = lax.all_gather(columns, "rep", axis=1, tiled=True)
    result = contract_last(shifts[0], piece[0])
    for project_k in range(1, taps):
        result = result + contract_last(shifts[project_k], piece[project_k])
    input_grad = (result * slope + grad_up[0, :, :in_width].astype(jnp.float32)).astype(
        jnp.bfloat16
    )
    scale_factor = float(rows * lax.axis_size("seq") * lax.axis_size("rep")) ** (-0.5)
    terms = jnp.stack([contract_first(act, shifts[k]) for k in range(taps)]) * scale_factor
    partial_sum = lax.psum_scatter(terms, "rep", scatter_dimension=1, tiled=True)
    weight_grad = lax.psum_scatter(partial_sum, "seq", scatter_dimension=2, tiled=True)
    return (input_grad[None], weight_grad)


def solution(mesh):
    in_specs = (P("rep", "seq", None), P("rep", None, "seq"), P(None, "rep", "seq"))
    out_specs = (P("rep", "seq", None), P(None, "rep", "seq"))
    return jax.shard_map(
        on_device, mesh=mesh, in_specs=in_specs, out_specs=out_specs, check_vma=False
    )
```

profile of v0, /device:TPU:9, one launch (start us, length us, event | category | flops | bytes accessed | tf_op | source)
XLA Modules:
  0.0 507.5 jit_solution(11445706456149775581)
XLA Ops:
  8.0 4.6 copy.14
  12.6 0.5 broadcast.102
  13.1 34.4 %reduce = bf16[2048,384]{1,0:T(8,128)(2,1)} reduce(bf16[2048,1,384]{2,1,0:T(2,128)(2,1)S(1)} %bitcast.111, bf16[]{:T(256)} %broadcast.102), dimensions={1}, to_apply=%bitcast.110.reduce_sub_computation | reduce | bytes 3145730
  47.5 3.8 reshape.52
  51.3 4.4 all-to-all-start
  55.6 0.0 all-gather.3.cloned.1.call-start
  55.7 0.7 all-gather.3.cloned.1.call-update
  56.4 0.0 reduce-scatter.3.cloned.1.call-start
  56.4 21.8 %all-to-all-done = bf16[4,2,98304]{2,1,0:T(2,128)(2,1)} async-done(((bf16[4,2,98304]{2,1,0:T(2,128)(2,1)}), bf16[4,2,98304]{2,1,0:T(2,128)(2,1)}, u32[]{:S(2)}, u32[]{:S(2)}) %all-to-all-start) | async-done | bytes 1572896 | tf_op jit(solution)/shard_map/all_to_all | solution.py:34
  78.3 3.1 reshape.53
  81.3 1.5 multiply_convert_fusion
  82.8 1.7 copy.10
  84.5 1.6 copy.11
  86.1 3.1 broadcast_in_dim.8
  89.2 2.7 convert_element_type.73
  91.9 0.8 fusion.43
  92.7 1.3 collective-permute-start
  94.0 3.8 constant_dynamic-update-slice_fusion.1
  97.8 2.7 broadcast_in_dim.9
  100.5 4.2 collective-permute-start.1
  104.7 0.0 collective-permute-done
  104.7 0.6 constant_dynamic-update-slice_fusion
  105.3 6.0 %bitcast_dynamic-update-slice_fusion.4 = f32[5,768,1536]{2,1,0:T(8,128)S(1)} fusion(bf16[1,1026,1536]{2,1,0:T(8,128)(2,1)} %constant_dynamic-update-slice_fusion, bf16[1,1024,768]{2,1,0:T(8,128)(2,1)} %param.3), kind=kOutput, calls=%fused_computation.14 | convolution fusion | flops 2423783424 | bytes 9437184 | tf_op jit(solution)/shard_map/dot_general | solution.py:27
  111.3 0.0 copy-done.3
  111.3 0.0 copy-done.6
  111.3 0.0 copy-start.1
  111.3 3.5 bitcast_dynamic-update-slice_fusion.3
  114.8 3.0 bitcast_dynamic-update-slice_fusion.2
  117.8 0.0 collective-permute-done.1
  117.8 0.0 copy-done
  117.9 3.7 bitcast_dynamic-update-slice_fusion.1
  121.6 3.5 bitcast_dynamic-update-slice_fusion
  125.1 8.3 %broadcast_multiply_fusion = f32[5,768,1536]{2,1,0:T(8,128)} fusion(f32[5,768,1536]{2,1,0:T(8,128)S(1)} %bitcast_dynamic-update-slice_fusion), kind=kLoop, calls=%fused_computation | loop fusion | flops 5898240 | bytes 47185920 | tf_op jit(solution)/shard_map/mul | solution.py:53
  133.4 0.0 reduce-scatter.3.cloned.1.call-update
  133.4 0.0 all-gather.5.cloned.1.call-start
  133.5 0.0 all-gather.3.cloned.1.call-done
  133.5 0.5 all-gather.5.cloned.1.call-update
  134.0 0.0 reduce-scatter.5.cloned.1.call-start
  134.1 233.0 %reduce-scatter.3.cloned.1.call-done = f32[5,96,1536]{2,1,0:T(8,128)} async-done(((f32[5,768,1536]{2,1,0:T(8,128)}), f32[5,96,1536]{2,1,0:T(8,128)}) %reduce-scatter.3.cloned.1.call-update) | async-done | bytes 2949136 | tf_op jit(solution)/shard_map/reduce_scatter | solution.py:54
  367.0 0.0 reduce-scatter.5.cloned.1.call-update
  367.1 108.7 %all-gather.5.cloned.1.call-done = bf16[5,768,1536]{2,1,0:T(8,128)(2,1)} async-done(((bf16[5,96,1536]{2,1,0:T(8,128)(2,1)}), bf16[5,768,1536]{2,1,0:T(8,128)(2,1)}) %all-gather.5.cloned.1.call-update) | async-done | bytes 11796496 | tf_op jit(solution)/shard_map/all_gather | solution.py:45
  475.7 6.1 %fusion.26 = f32[1024,768]{1,0:T(8,128)} fusion(bf16[5,768,1536]{2,1,0:T(8,128)(2,1)} %all-gather.5.cloned.1.call-done, bf16[1,2,1536]{2,1,0:T(2,128)(2,1)S(1)} %collective-permute-done.1, bf16[1,1024,1536]{2,1,0:T(8,128)(2,1)S(1)} %copy-done), kind=kOutput, calls=%fused_computation.45 | convolution fusion | flops 2422210560 | bytes 8656896 | tf_op jit(solution)/shard_map/dot_general | solution.py:21
  481.8 1.0 copy-done.5
  482.9 2.6 fusion.24
  485.5 2.6 fusion.27
  488.2 0.0 copy-start.7
  488.2 4.3 fusion.23
  492.5 7.6 %fusion.31 = bf16[1,1024,768]{2,1,0:T(8,128)(2,1)} fusion(bf16[1,1024,1536]{2,1,0:T(8,128)(2,1)S(1)} %copy-done, bf16[1,1024,768]{2,1,0:T(8,128)(2,1)S(1)} %copy-done.7, f32[1024,768]{1,0:T(8,128)} %fusion.26, f32[1024,768]{1,0:T(8,128)S(1)} %fusion.27, f32[1024,768]{1,0:T(8,128)} %fusion.23, f32[1024,768]{1,0:T(8,128)S(1)} %fusion.24, ...), kind=kOutput, calls=%fused_computation.52 | convolution fusion | flops 2442657792 | bytes 22812672 | tf_op jit(solution)/shard_map/dot_general | solution.py:21
  (11 shorter events, 0.0 us)
Async XLA Ops:
  51.3 27.0 %all-to-all-start = ((bf16[4,2,98304]{2,1,0:T(2,128)(2,1)}), bf16[4,2,98304]{2,1,0:T(2,128)(2,1)}, u32[]{:S(2)}, u32[]{:S(2)}) async-start(bf16[4,2,98304]{2,1,0:T(2,128)(2,1)} %reshape.52), calls=%async_computation | async-start | bytes 3145728 | tf_op jit(solution)/shard_map/all_to_all | solution.py:34
  55.6 77.9 %all-gather.3.cloned.1.call-start = ((), (), s32[]{:S(2)}) async-start(), calls=%async_computation.3 | async-start | bytes 1843200 | tf_op jit(solution)/shard_map/all_gather | solution.py:44
  56.4 310.7 %reduce-scatter.3.cloned.1.call-start = ((), (), s32[]{:S(2)}) async-start(), calls=%async_computation.5 | async-start | bytes 26542080 | tf_op jit(solution)/shard_map/reduce_scatter | solution.py:54
  92.7 12.0 %collective-permute-start = (bf16[1,2,1536]{2,1,0:T(2,128)(2,1)S(1)}, bf16[1,2,1536]{2,1,0:T(2,128)(2,1)S(1)}, u32[]{:S(2)}, u32[]{:S(2)}) collective-permute-start(bf16[1,2,1536]{2,1,0:T(2,128)(2,1)S(1)} %get-tuple-element.2), channel_id=1, source_target_pairs={{8,0},{16,8},{24,16},{9,1},{17,9},{25,17},{10,2},{18,10},{26,18},{... | collective-permute-start | bytes 18440 | tf_op jit(solution)/shard_map/ppermute | solution.py:15
  100.5 17.3 %collective-permute-start.1 = (bf16[1,2,1536]{2,1,0:T(2,128)(2,1)S(1)}, bf16[1,2,1536]{2,1,0:T(2,128)(2,1)S(1)}, u32[]{:S(2)}, u32[]{:S(2)}) collective-permute-start(bf16[1,2,1536]{2,1,0:T(2,128)(2,1)S(1)} %get-tuple-element.3), channel_id=1, source_target_pairs={{0,8},{8,16},{16,24},{1,9},{9,17},{17,25},{2,10},{10,18},{18,26},{... | collective-permute-start | bytes 18440 | tf_op jit(solution)/shard_map/ppermute | solution.py:14
  105.3 6.0 %copy-start.3 = (bf16[1,1026,1536]{2,1,0:T(8,128)(2,1)S(1)}, bf16[1,1026,1536]{2,1,0:T(8,128)(2,1)}, u32[]{:S(2)}) copy-start(bf16[1,1026,1536]{2,1,0:T(8,128)(2,1)} %constant_dynamic-update-slice_fusion) | copy-start | bytes 9455620
  105.3 6.0 %copy-start.6 = (bf16[1,1024,768]{2,1,0:T(8,128)(2,1)S(1)}, bf16[1,1024,768]{2,1,0:T(8,128)(2,1)}, u32[]{:S(2)}) copy-start(bf16[1,1024,768]{2,1,0:T(8,128)(2,1)} %param.3) | copy-start | bytes 4718596
  111.3 3.5 copy-start.1
  114.8 3.0 copy-start
  133.4 342.3 %all-gather.5.cloned.1.call-start = ((), (), s32[]{:S(2)}) async-start(), calls=%async_computation.4 | async-start | bytes 13271040 | tf_op jit(solution)/shard_map/all_gather | solution.py:45
  134.0 366.1 %reduce-scatter.5.cloned.1.call-start = ((), (), s32[]{:S(2)}) async-start(), calls=%async_computation.6 | async-start | bytes 3686400 | tf_op jit(solution)/shard_map/reduce_scatter | solution.py:55
  475.7 6.1 %copy-start.4 = (bf16[1,1026,1536]{2,1,0:T(8,128)(2,1)S(1)}, bf16[1,1026,1536]{2,1,0:T(8,128)(2,1)}, u32[]{:S(2)}) copy-start(bf16[1,1026,1536]{2,1,0:T(8,128)(2,1)} %constant_dynamic-update-slice_fusion) | copy-start | bytes 9455620
  475.7 7.2 %copy-start.5 = (bf16[5,768,1536]{2,1,0:T(8,128)(2,1)S(1)}, bf16[5,768,1536]{2,1,0:T(8,128)(2,1)}, u32[]{:S(2)}) copy-start(bf16[5,768,1536]{2,1,0:T(8,128)(2,1)} %all-gather.5.cloned.1.call-done) | copy-start | bytes 35389444
  482.9 2.7 copy-start.2
  488.2 4.3 copy-start.7
Sparse Core Ops, SparseCore 0:
  58.3 36.6 all-gather.2
  367.2 41.8 reduce-scatter.4
Sparse Core Ops, SparseCore 1:
  133.5 233.5 reduce-scatter.2
  368.5 107.1 all-gather.4
where the time goes:
time: 512 us; the launch traced here: 508 us
  waiting for transfers between devices  365 us (71%)
  other arithmetic  44.3 us (9%)
  matrix products  43 us (8%)
  local copies, waits for them, and re-layouts  29.9 us (6%)
  between operations  15.7 us (3%)
  starting transfers between devices  9.97 us (2%)
    reduce_scatter x1, waiting for transfers between devices, on_device(): lax.psum_scatter(terms, 'rep', scatter_dimension=1, tiled=True)  233 us
    all_gather x1, waiting for transfers between devices, on_device(): piece = lax.all_gather(columns, 'rep', axis=1, tiled=True)  109 us
    unnamed x1, other arithmetic  34.4 us
    dot_general x5, matrix products, contract_last(): lax.dot_general(left, right, (((1,), (1,)), ((), ())), preferred_element_...  23.3 us
    all_to_all x1, waiting for transfers between devices, on_device(): lax.all_to_all(trunk_grad, 'seq', split_axis=1, concat_axis=2, tiled=True)  21.8 us
    dot_general x5, matrix products, contract_first(): lax.dot_general(left, right, (((0,), (0,)), ((), ())), preferred_element_...  19.7 us
    unnamed x21, local copies, waits for them, and re-layouts  16.8 us
  transfers between devices with their start and end apart: 7, of which 3 were waited for; matrix products, arithmetic and copies ran while one was open for 14% of the time, Pallas kernels for 0%

commit v1 on v0

v1 whole, which is shorter than its diff:
```python
import functools
import math

import jax
import jax.numpy as jnp
from jax import lax
from jax.experimental import pallas as pl
from jax.experimental.pallas import tpu as pltpu
from jax.sharding import PartitionSpec as P

HALO = 8
LANES = 128
ROOT = math.sqrt(2.0 / math.pi)
CUBIC = 0.044715


def from_peer(value, axis, distance):
    peers = lax.axis_size(axis)
    return lax.ppermute(value, axis, [(i, i ^ distance) for i in range(peers)])


def gather_halves(top, bottom, axis):
    found = {0: (top, bottom)}
    for distance in range(1, lax.axis_size(axis)):
        high = 1 << (distance.bit_length() - 1)
        low = distance & -distance
        if high == low:
            found[distance] = (from_peer(top, axis, high), from_peer(bottom, axis, high))
    for distance in range(1, lax.axis_size(axis)):
        high = 1 << (distance.bit_length() - 1)
        low = distance & -distance
        if high != low:
            found[distance] = (
                from_peer(found[distance ^ high][0], axis, high),
                from_peer(found[distance ^ low][1], axis, low),
            )
    return found


def act_kernel(x_ref, top_ref, bottom_ref, scratch):
    half, width = top_ref.shape[0], x_ref.shape[2]

    def rows(step, out_ref, base):
        start = pl.multiple_of(step * 64, 64)
        x = x_ref[0, pl.ds(pl.multiple_of(base + 2 * start, 128), 128), :].astype(jnp.float32)
        act = x * (0.5 * (1.0 + jnp.tanh(ROOT * (x + CUBIC * (x * x * x)))))
        for c in range(width // LANES):
            scratch[c] = act[:, c * LANES : (c + 1) * LANES]
        for parity in range(2):
            for c in range(width // LANES):
                picked = scratch[c, pl.ds(parity, 64, stride=2), :].astype(jnp.bfloat16)
                left = parity * width + c * LANES
                out_ref[pl.ds(start, 64), left : left + LANES] = picked

    @pl.loop(0, half // 64)
    def _(step):
        rows(step, top_ref, 0)

    @pl.loop(0, half // 64)
    def _(step):
        rows(step, bottom_ref, 2 * half)


def activate(inputs):
    fine, width = inputs.shape[1:]
    half = jax.ShapeDtypeStruct((fine // 4, 2 * width), jnp.bfloat16)
    return pl.pallas_call(
        act_kernel,
        out_shape=(half, half),
        in_specs=[pl.BlockSpec(memory_space=pltpu.VMEM)],
        out_specs=[pl.BlockSpec(memory_space=pltpu.VMEM)] * 2,
        scratch_shapes=[pltpu.VMEM((width // LANES, 128, LANES), jnp.float32)],
        compiler_params=pltpu.CompilerParams(vmem_limit_bytes=24 << 20),
        name="act",
    )(inputs)


def input_grad_kernel(seqs, reps, stacked, place, *refs):
    count = 2 * seqs
    x_ref, grads, pieces = refs[0], refs[1 : 1 + seqs], refs[1 + seqs : 1 + seqs + 2 * count]
    out_ref, wv, gv, products, fine, again, sems, grad_sems = refs[1 + seqs + 2 * count :]
    me, rep = place[0], place[1]
    taps, _, rows, _ = wv.shape
    block = grads[0].shape[1]
    coarse = x_ref.shape[1] // 2
    width = x_ref.shape[2]
    copies = []
    for distance in range(seqs):
        owner = me ^ distance
        columns = pl.ds(pl.multiple_of(owner * block, block), block)
        copy = pltpu.make_async_copy(grads[distance], gv.at[:, columns], grad_sems.at[distance])
        copy.start()
        copies.append(copy)
    for flip in range(2):
        for distance in range(seqs):
            columns = pl.ds(pl.multiple_of((me ^ distance) * block, block), block)
            for half in range(2):
                piece = pieces[flip * count + 2 * distance + half]
                for j in range(stacked):
                    owner = rep ^ flip ^ (2 * (half * stacked + j))
                    slot = flip * seqs * 2 * stacked + (2 * distance + half) * stacked + j
                    copy = pltpu.make_async_copy(
                        piece.at[j], wv.at[:, owner, :, columns], sems.at[slot]
                    )
                    copy.start()
                    copies.append(copy)
    for copy in copies:
        copy.wait()
    tile = max(1, reps // 2)

    @pl.loop(0, taps)
    def _(k):
        for part in range(reps // tile):
            kernel = wv[k, part * tile : (part + 1) * tile].reshape(tile * rows, wv.shape[3])
            products[k, :, part * tile * rows : (part + 1) * tile * rows] = lax.dot_general(
                gv[...], kernel, (((1,), (1,)), ((), ())), preferred_element_type=jnp.float32
            )

    step = 64

    @pl.loop(0, coarse // step)
    def _(i):
        base = pl.multiple_of(i * step, step)

        def shifted(k, by):
            window = products[k, pl.ds(base, step + 2 * HALO), :]
            return window[HALO + by : HALO + by + step]

        skip = gv[pl.ds(pl.multiple_of(base, 8), step + 2 * HALO), :width].astype(jnp.float32)
        skip = skip[HALO : HALO + step]
        shared = shifted(0, 1) + shifted(2, 0) + shifted(4, -1)
        even = shared + shifted(1, 0) + shifted(3, -1)
        odd = shared + shifted(1, 1) + shifted(3, 0)
        for c in range(width // LANES):
            lanes = slice(c * LANES, (c + 1) * LANES)
            fine[c, pl.ds(0, step, stride=2), :] = even[:, lanes]
            fine[c, pl.ds(1, step, stride=2), :] = odd[:, lanes]
            again[c, pl.ds(0, step, stride=2), :] = skip[:, lanes]
            again[c, pl.ds(1, step, stride=2), :] = skip[:, lanes]
            span = pl.ds(pl.multiple_of(2 * base, 2 * step), 2 * step)
            x = x_ref[0, span, lanes].astype(jnp.float32)
            tanh = jnp.tanh(ROOT * (x + CUBIC * (x * x * x)))
            slope = 0.5 * (1.0 + tanh) + 0.5 * x * (1.0 - tanh * tanh) * (
                ROOT * (1.0 + 3.0 * CUBIC * (x * x))
            )
            out_ref[0, span, lanes] = (0.5 * (fine[c] * slope + again[c])).astype(jnp.bfloat16)


def input_gradient(place, inputs, grads, kept, swapped):
    seqs, reps = len(grads), 2 * 2 * kept[0].shape[0]
    stacked, taps, rows, block = kept[0].shape
    window = grads[0].shape[0]
    width = inputs.shape[2]
    any_spec = pl.BlockSpec(memory_space=pl.ANY)
    vmem = pl.BlockSpec(memory_space=pltpu.VMEM)
    operands = (inputs, *grads, *kept, *swapped)
    return pl.pallas_call(
        functools.partial(input_grad_kernel, seqs, reps, stacked),
        out_shape=jax.ShapeDtypeStruct(inputs.shape, jnp.bfloat16),
        grid_spec=pltpu.PrefetchScalarGridSpec(
            num_scalar_prefetch=1,
            grid=(1,),
            in_specs=[pl.BlockSpec(inputs.shape, lambda i, place: (0, 0, 0))]
            + [any_spec] * (len(operands) - 1),
            out_specs=pl.BlockSpec(inputs.shape, lambda i, place: (0, 0, 0)),
            scratch_shapes=[
                pltpu.VMEM((taps, reps, rows, seqs * block), jnp.bfloat16),
                pltpu.VMEM((window, seqs * block), jnp.bfloat16),
                pltpu.VMEM((taps, window, width), jnp.float32),
                pltpu.VMEM((width // LANES, 128, LANES), jnp.float32),
                pltpu.VMEM((width // LANES, 128, LANES), jnp.float32),
                pltpu.SemaphoreType.DMA((seqs * reps,)),
                pltpu.SemaphoreType.DMA((seqs,)),
            ],
        ),
        compiler_params=pltpu.CompilerParams(vmem_limit_bytes=52 << 20),
        cost_estimate=pl.CostEstimate(
            flops=2 * taps * window * width * seqs * block,
            bytes_accessed=20 << 20,
            transcendentals=inputs.size,
        ),
        name="input_grad",
    )(place, *operands)


def input_gradient_unaligned(place, inputs, grads, kept, swapped):
    me, rep = place[0], place[1]
    seqs, (stacked, taps, rows, block) = len(grads), kept[0].shape
    reps = 4 * stacked
    window, coarse = grads[0].shape[0], inputs.shape[1] // 2
    grad = jnp.zeros((window, seqs * block), jnp.bfloat16)
    kernel = jnp.zeros((taps, reps * rows, seqs * block), jnp.bfloat16)
    for distance in range(seqs):
        left = (me ^ distance) * block
        grad = lax.dynamic_update_slice(grad, grads[distance], (0, left))
        for flip, pieces in enumerate((kept, swapped)):
            for half in range(2):
                for j in range(stacked):
                    owner = rep ^ flip ^ (2 * (half * stacked + j))
                    piece = pieces[2 * distance + half][j]
                    kernel = lax.dynamic_update_slice(kernel, piece, (0, owner * rows, left))
    products = lax.dot_general(
        grad, kernel, (((1,), (2,)), ((), ())), preferred_element_type=jnp.float32
    )

    def shifted(k, by):
        return products[HALO + by : HALO + by + coarse, k]

    shared = shifted(0, 1) + shifted(2, 0) + shifted(4, -1)
    even = shared + shifted(1, 0) + shifted(3, -1)
    odd = shared + shifted(1, 1) + shifted(3, 0)
    total = jnp.stack([even, odd], axis=1).reshape(inputs.shape[1:])
    x = inputs[0].astype(jnp.float32)
    tanh = jnp.tanh(ROOT * (x + CUBIC * (x * x * x)))
    slope = 0.5 * (1.0 + tanh) + 0.5 * x * (1.0 - tanh * tanh) * (
        ROOT * (1.0 + 3.0 * CUBIC * (x * x))
    )
    skip = jnp.repeat(grad[HALO : HALO + coarse, : inputs.shape[2]].astype(jnp.float32), 2, axis=0)
    return (0.5 * (total * slope + skip)).astype(jnp.bfloat16)[None]


def on_device(inputs, trunk_grad, weights):
    seqs, reps = lax.axis_size("seq"), lax.axis_size("rep")
    me, rep = lax.axis_index("seq"), lax.axis_index("rep")
    taps, rows, block = weights.shape
    fine, width = inputs.shape[1:]
    coarse = fine // 2

    act = gather_halves(*activate(inputs), "seq")

    columns = [weights] + [from_peer(weights, "rep", 2 * j) for j in range(1, reps // 2)]
    kept = gather_halves(
        jnp.stack(columns[: reps // 4]), jnp.stack(columns[reps // 4 :]), "seq"
    )
    kept = [half for distance in range(seqs) for half in kept[distance]]
    swapped = [from_peer(half, "rep", 1) for half in kept]

    trunk = trunk_grad[0]
    edged = jnp.pad(trunk, ((HALO, HALO), (0, 0)))
    grads = []
    for distance in range(seqs):
        window = lax.dynamic_slice_in_dim(edged, (me ^ distance) * coarse, coarse + 2 * HALO, 0)
        grads.append(from_peer(window, "seq", distance) if distance else window)

    zeros = jnp.zeros((1, block), jnp.bfloat16)
    later = jnp.concatenate([trunk[1:], zeros])
    earlier = jnp.concatenate([zeros, trunk[:-1]])
    shifts = jnp.concatenate([later, trunk, earlier], axis=1)
    total = None
    for distance in range(seqs):
        for half in range(2):
            start = (me ^ distance) * coarse + half * (coarse // 2)
            matching = lax.dynamic_slice_in_dim(shifts, start, coarse // 2, 0)
            term = lax.dot_general(
                act[distance][half], matching, (((0,), (0,)), ((), ())), preferred_element_type=jnp.float32
            )
            total = term if total is None else total + term
    even, odd = total[:width], total[width:]
    (even_l, even_c, even_e), (odd_l, odd_c, odd_e) = (
        [part[:, i * block : (i + 1) * block] for i in range(3)] for part in (even, odd)
    )
    scale = 0.5 * float(fine * seqs * reps) ** (-0.5)
    terms = scale * jnp.stack(
        [even_l + odd_l, even_c + odd_l, even_c + odd_c, even_e + odd_c, even_e + odd_e]
    )
    terms = terms.reshape(taps, reps // 2, 2, rows, block)
    core, plane = rep % 2, rep // 2
    mine = lax.dynamic_index_in_dim(terms, core, 2, keepdims=False)
    theirs = lax.dynamic_index_in_dim(terms, 1 - core, 2, keepdims=False)
    mine = mine + from_peer(theirs.astype(jnp.bfloat16), "rep", 1).astype(jnp.float32)
    weight_grad = lax.dynamic_index_in_dim(mine, plane, 1, keepdims=False)
    for j in range(1, reps // 2):
        leaving = lax.dynamic_index_in_dim(mine, plane ^ j, 1, keepdims=False)
        arrived = from_peer(leaving.astype(jnp.bfloat16), "rep", 2 * j)
        weight_grad = weight_grad + arrived.astype(jnp.float32)

    place = jnp.stack([me, rep]).astype(jnp.int32)
    gradient = input_gradient if block % LANES == 0 else input_gradient_unaligned
    input_grad = gradient(place, inputs, grads, kept, swapped)
    return (input_grad, weight_grad)


def solution(mesh):
    in_specs = (P("rep", "seq", None), P("rep", None, "seq"), P(None, "rep", "seq"))
    out_specs = (P("rep", "seq", None), P(None, "rep", "seq"))
    return jax.shard_map(
        on_device, mesh=mesh, in_specs=in_specs, out_specs=out_specs, check_vma=False
    )
```

time: 512 us -> 207 us (0.40)
  waiting for transfers between devices: 365 us -> 73 us
  other arithmetic: 44.3 us -> 16.7 us
  Pallas kernels: 0 us -> 23.2 us
  starting transfers between devices: 9.97 us -> 27.7 us
  between operations: 15.7 us -> 0.88 us
  matrix products: 43 us -> 29.6 us
    reduce_scatter x2 -> x0, waiting for transfers between devices: 233 us -> none  [the longest x1 233 us: on_device(): lax.psum_scatter(terms, 'rep', scatter_dimension=1, tiled=True)]
    all_gather x2 -> x0, waiting for transfers between devices: 109 us -> none  [the longest x1 109 us: on_device(): piece = lax.all_gather(columns, 'rep', axis=1, tiled=True)]
    ppermute x2 -> x30, waiting for transfers between devices: 0.01 us -> 73 us  [from_peer(): return lax.ppermute(value, axis, [(i, i ^ distance) for i in range(peers)])]
    unnamed x1 -> x0, other arithmetic: 34.4 us -> none
    pallas_call x0 -> x2, Pallas kernels: none -> 23.2 us  [the longest x1 21.4 us: input_gradient(): pl.pallas_call(functools.partial(input_grad_kernel, seqs, reps, stacked),...]
    ppermute x2 -> x30, starting transfers between devices: 5.45 us -> 27.7 us  [from_peer(): return lax.ppermute(value, axis, [(i, i ^ distance) for i in range(peers)])]
    all_to_all x1 -> x0, waiting for transfers between devices: 21.8 us -> none  [on_device(): lax.all_to_all(trunk_grad, 'seq', split_axis=1, concat_axis=2, tiled=True)]
    dot_general x10 -> x8, matrix products: 43 us -> 29.6 us  [on_device(): lax.dot_general(act[distance][half], matching, (((0,), (0,)), ((), ())),...]
  transfers between devices with their start and end apart: 7 -> 30, of which waited for: 3 -> 9; matrix products, arithmetic and copies ran while one was open for 14% -> 36% of each run, Pallas kernels for 0% -> 10%
where the time goes in v1:
time: 207 us; the launch traced here: 205 us
  waiting for transfers between devices  73 us (35%)
  local copies, waits for them, and re-layouts  33.5 us (16%)
  matrix products  29.6 us (14%)
  starting transfers between devices  27.7 us (13%)
  Pallas kernels  23.2 us (11%)
  other arithmetic  16.7 us (8%)
    ppermute x30, waiting for transfers between devices, from_peer(): return lax.ppermute(value, axis, [(i, i ^ distance) for i in range(peers)])  73 us
    dot_general x8, matrix products, on_device(): lax.dot_general(act[distance][half], matching, (((0,), (0,)), ((), ())),...  29.6 us
    ppermute x30, starting transfers between devices, from_peer(): return lax.ppermute(value, axis, [(i, i ^ distance) for i in range(peers)])  27.7 us
    pallas_call x1, Pallas kernels, input_gradient(): pl.pallas_call(functools.partial(input_grad_kernel, seqs, reps, stacked),...  21.4 us
    unnamed x30, local copies, waits for them, and re-layouts  13.3 us
  transfers between devices with their start and end apart: 30, of which 9 were waited for; matrix products, arithmetic and copies ran while one was open for 36% of the time, Pallas kernels for 10%

profile of v1, /device:TPU:9, one launch (start us, length us, event | category | flops | bytes accessed | tf_op | source)
XLA Modules:
  0.0 204.5 jit_solution(16771217657437762274)
XLA Ops:
  0.6 1.4 copy-done
  2.0 1.8 act.1
  3.8 1.3 collective-permute-start.23
  5.1 1.2 collective-permute-start.21
  6.3 2.3 %collective-permute-start.4 = (bf16[5,96,384]{2,1,0:T(8,128)(2,1)}, bf16[5,96,384]{2,1,0:T(8,128)(2,1)}, u32[]{:S(2)}, u32[]{:S(2)}) collective-permute-start(bf16[5,96,384]{2,1,0:T(8,128)(2,1)} %param.5), channel_id=1, source_target_pairs={{0,4},{1,5},{2,6},{3,7},{4,0},{5,1},{6,2},{7,3},{8,12},{9,13},{10,... | collective-permute-start | bytes 1105928 | tf_op jit(solution)/shard_map/ppermute | solution.py:19
  8.6 1.2 collective-permute-start.3
  9.9 4.0 %slice_bitcast_fusion.1 = (bf16[2047,384]{1,0:T(8,128)(2,1)}, bf16[2047,384]{1,0:T(8,128)(2,1)}) fusion(bf16[1,2048,384]{2,1,0:T(8,128)(2,1)} %param.4), kind=kLoop, calls=%fused_computation.18 | loop fusion | bytes 6288384 | tf_op jit(solution)/shard_map/slice | solution.py:246
  13.9 3.6 %fusion.7 = bf16[2048,1152]{1,0:T(8,128)(2,1)S(1)} fusion(bf16[2047,384]{1,0:T(8,128)(2,1)} %get-tuple-element.15, bf16[2047,384]{1,0:T(8,128)(2,1)} %get-tuple-element.14, bf16[2048,384]{1,0:T(8,128)(2,1)} %bitcast.50), kind=kLoop, calls=%fused_computation.12 | loop fusion | flops 23592960 | bytes 9435648 | tf_op jit(solution)/shard_map/concatenate | solution.py:248
  19.6 4.0 %convolution_add_fusion.2 = f32[1152,1536]{1,0:T(8,128)} fusion(f32[1152,1536]{1,0:T(8,128)S(1)} %fusion.23, bf16[256,1536]{1,0:T(8,128)(2,1)S(1)} %get-tuple-element.5, bf16[2048,1152]{1,0:T(8,128)(2,1)S(1)} %fusion.7, s32[]{:T(128)S(6)} %select_n.72), kind=kOutput, calls=%fused_computation.4 | convolution fusion | flops 907739136 | bytes 15532036 | tf_op jit(solution)/shard_map/dot_general | solution.py:254
  23.6 2.5 %pad_dynamic-slice_fusion = (bf16[528,384]{1,0:T(8,128)(2,1)}, bf16[528,384]{1,0:T(8,128)(2,1)}, bf16[528,384]{1,0:T(8,128)(2,1)}, bf16[528,384]{1,0:T(8,128)(2,1)S(1)}) fusion(s32[]{:T(128)S(6)} %select_n.70, bf16[2048,384]{1,0:T(8,128)(2,1)} %bitcast.51, s32[]{:T(128)S(6)} %select_n.68, s32[]{:T(128)S(6)} %select_n.69, s32[]{:T(128)S(6)} %select_n.67), kind=kLoop, calls=%fused_computation.25 | loop fusion | bytes 3194896 | tf_op jit(solution)/shard_map/dynamic_slice | solution.py:242
  26.1 6.9 %collective-permute-done.4 = bf16[5,96,384]{2,1,0:T(8,128)(2,1)} collective-permute-done((bf16[5,96,384]{2,1,0:T(8,128)(2,1)}, bf16[5,96,384]{2,1,0:T(8,128)(2,1)}, u32[]{:S(2)}, u32[]{:S(2)}) %collective-permute-start.4) | collective-permute-done | bytes 368672 | tf_op jit(solution)/shard_map/ppermute | solution.py:19
  33.2 7.7 %collective-permute-done.5 = bf16[5,96,384]{2,1,0:T(8,128)(2,1)} collective-permute-done((bf16[5,96,384]{2,1,0:T(8,128)(2,1)}, bf16[5,96,384]{2,1,0:T(8,128)(2,1)}, u32[]{:S(2)}, u32[]{:S(2)}) %collective-permute-start.5) | collective-permute-done | bytes 368672 | tf_op jit(solution)/shard_map/ppermute | solution.py:19
  41.2 2.0 pad_maximum_fusion.1.refs_6_
  43.9 1.2 collective-permute-start
  45.2 2.0 pad_maximum_fusion.refs_5_
  48.3 2.4 %fusion.15 = f32[1152,1536]{1,0:T(8,128)S(1)} fusion(bf16[256,1536]{1,0:T(8,128)(2,1)} %copy-done.6, bf16[2048,1152]{1,0:T(8,128)(2,1)} %copy-done.2, s32[]{:T(128)S(6)} %select_n.76), kind=kOutput, calls=%fused_computation.40 | convolution fusion | flops 905969664 | bytes 8454148 | tf_op jit(solution)/shard_map/dot_general | solution.py:254
  50.8 1.3 collective-permute-start.2
  52.0 2.4 %fusion.19 = f32[1152,1536]{1,0:T(8,128)S(1)} fusion(bf16[256,1536]{1,0:T(8,128)(2,1)} %collective-permute-done.21, bf16[2048,1152]{1,0:T(8,128)(2,1)} %copy-done.2, s32[]{:T(128)S(6)} %select_n.74), kind=kOutput, calls=%fused_computation.44 | convolution fusion | flops 905969664 | bytes 8454148 | tf_op jit(solution)/shard_map/dot_general | solution.py:254
  54.5 1.3 collective-permute-start.25
  55.8 3.9 %collective-permute-done.20 = bf16[256,1536]{1,0:T(8,128)(2,1)} collective-permute-done((bf16[256,1536]{1,0:T(8,128)(2,1)S(1)}, bf16[256,1536]{1,0:T(8,128)(2,1)}, u32[]{:S(2)}, u32[]{:S(2)}) %collective-permute-start.20) | collective-permute-done | bytes 786464 | tf_op jit(solution)/shard_map/ppermute | solution.py:19
  59.9 5.1 %fusion.17 = f32[1152,1536]{1,0:T(8,128)} fusion(bf16[256,1536]{1,0:T(8,128)(2,1)S(1)} %collective-permute-done.22, bf16[2048,1152]{1,0:T(8,128)(2,1)} %copy-done.2, s32[]{:T(128)S(6)} %select_n.75), kind=kOutput, calls=%fused_computation.42 | convolution fusion | flops 905969664 | bytes 8454148 | tf_op jit(solution)/shard_map/dot_general | solution.py:254
  65.0 10.2 %fusion.5 = f32[1152,1536]{1,0:T(8,128)} fusion(f32[1152,1536]{1,0:T(8,128)S(1)} %fusion.15, f32[1152,1536]{1,0:T(8,128)} %fusion.17, f32[1152,1536]{1,0:T(8,128)S(1)} %fusion.19, f32[1152,1536]{1,0:T(8,128)} %convolution_add_fusion.2, bf16[256,1536]{1,0:T(8,128)(2,1)} %collective-permute-done.20, bf16[2048,1152]{1,0:T(8,128)(2,1)} %copy-done.2, ...), kind=kOutput, calls=%fused_computation.10 | convolution fusion | flops 913047552 | bytes 36765700 | tf_op jit(solution)/shard_map/dot_general | solution.py:254
  75.2 18.6 %collective-permute-done.25 = bf16[256,1536]{1,0:T(8,128)(2,1)S(1)} collective-permute-done((bf16[256,1536]{1,0:T(8,128)(2,1)S(1)}, bf16[256,1536]{1,0:T(8,128)(2,1)S(1)}, u32[]{:S(2)}, u32[]{:S(2)}) %collective-permute-start.25) | collective-permute-done | bytes 786464 | tf_op jit(solution)/shard_map/ppermute | solution.py:19
  94.0 2.2 %fusion.12 = f32[1152,1536]{1,0:T(8,128)S(1)} fusion(bf16[256,1536]{1,0:T(8,128)(2,1)S(1)} %collective-permute-done.25, bf16[2048,1152]{1,0:T(8,128)(2,1)} %copy-done.2, s32[]{:T(128)S(6)} %select_n.78), kind=kOutput, calls=%fused_computation.37 | convolution fusion | flops 905969664 | bytes 8454148 | tf_op jit(solution)/shard_map/dot_general | solution.py:254
  96.5 2.2 %fusion.6 = f32[1536,1152]{0,1:T(8,128)S(1)} fusion(f32[1152,1536]{1,0:T(8,128)S(1)} %fusion.12, f32[1152,1536]{1,0:T(8,128)S(1)} %copy-done.1, bf16[256,1536]{1,0:T(8,128)(2,1)S(1)} %collective-permute-done.24, bf16[2048,1152]{1,0:T(8,128)(2,1)} %copy-done.2, s32[]{:T(128)S(6)} %select_n.77), kind=kOutput, calls=%fused_computation.11 | convolution fusion | flops 909508608 | bytes 22609924 | tf_op jit(solution)/shard_map/dot_general | solution.py:254
  98.7 2.5 %slice_add_fusion = (f32[768,384]{0,1:T(8,128)S(1)}, f32[768,384]{0,1:T(8,128)}, f32[768,384]{0,1:T(8,128)}, f32[768,384]{0,1:T(8,128)}, f32[768,384]{0,1:T(8,128)}) fusion(f32[1536,1152]{0,1:T(8,128)S(1)} %fusion.6), kind=kLoop, calls=%fused_computation.20 | loop fusion | flops 1474560 | bytes 12976128 | tf_op jit(solution)/shard_map/add | solution.py:264
  101.2 2.7 %copy.10 = f32[768,384]{1,0:T(8,128)} copy(f32[768,384]{0,1:T(8,128)} %get-tuple-element.10) | data formatting | bytes 2359296 | tf_op jit(solution)/shard_map/add | solution.py:264
  103.9 2.4 %constant_dynamic-update-slice_fusion.4 = f32[5,4,2,96,384]{4,3,2,1,0:T(8,128)} fusion(f32[1,4,2,96,384]{4,3,2,1,0:T(8,128)} %bitcast.56), kind=kLoop, calls=%fused_computation.57 | loop fusion | bytes 2359296
  106.3 2.7 %copy.11 = f32[768,384]{1,0:T(8,128)} copy(f32[768,384]{0,1:T(8,128)} %get-tuple-element.9) | data formatting | bytes 2359296 | tf_op jit(solution)/shard_map/add | solution.py:264
  108.9 2.8 %copy.12 = f32[768,384]{1,0:T(8,128)} copy(f32[768,384]{0,1:T(8,128)} %get-tuple-element.8) | data formatting | bytes 2359296 | tf_op jit(solution)/shard_map/add | solution.py:264
  111.7 2.6 %copy.13 = f32[768,384]{1,0:T(8,128)} copy(f32[768,384]{0,1:T(8,128)} %get-tuple-element.7) | data formatting | bytes 2359296 | tf_op jit(solution)/shard_map/add | solution.py:264
  114.3 1.6 copy.14
  115.9 2.5 %constant_dynamic-update-slice_fusion.3 = f32[5,4,2,96,384]{4,3,2,1,0:T(8,128)} fusion(f32[5,4,2,96,384]{4,3,2,1,0:T(8,128)} %constant_dynamic-update-slice_fusion.4, f32[1,4,2,96,384]{4,3,2,1,0:T(8,128)} %bitcast.54), kind=kLoop, calls=%fused_computation.56 | loop fusion | bytes 2359296
  118.4 2.4 %constant_dynamic-update-slice_fusion.2 = f32[5,4,2,96,384]{4,3,2,1,0:T(8,128)} fusion(f32[5,4,2,96,384]{4,3,2,1,0:T(8,128)} %constant_dynamic-update-slice_fusion.3, f32[1,4,2,96,384]{4,3,2,1,0:T(8,128)} %bitcast.55), kind=kLoop, calls=%fused_computation.55 | loop fusion | bytes 2359296
  123.0 3.3 %broadcast_multiply_fusion = f32[5,4,2,96,384]{4,3,2,1,0:T(8,128)S(1)} fusion(f32[5,4,2,96,384]{4,3,2,1,0:T(8,128)} %constant_dynamic-update-slice_fusion), kind=kLoop, calls=%fused_computation.16 | loop fusion | flops 1474560 | bytes 11796480 | tf_op jit(solution)/shard_map/mul | solution.py:263
  126.3 1.3 collective-permute-start.6
  127.6 1.2 collective-permute-start.8
  128.9 2.5 %collective-permute-start.13 = (bf16[2,5,96,384]{3,2,1,0:T(8,128)(2,1)}, bf16[2,5,96,384]{3,2,1,0:T(8,128)(2,1)S(1)}, u32[]{:S(2)}, u32[]{:S(2)}) collective-permute-start(bf16[2,5,96,384]{3,2,1,0:T(8,128)(2,1)} %pad_maximum_fusion.1.refs_6_), channel_id=1, source_target_pairs={{0,1},{1,0},{2,3},{3,2},{4,5},{5,4},{6,7},{7,6},{8,9},{9,8},{10,11... | collective-permute-start | bytes 2211848 | tf_op jit(solution)/shard_map/ppermute | solution.py:19
  131.6 11.0 %collective-permute-done.6.refs_7_ = bf16[2,5,96,384]{3,2,1,0:T(8,128)(2,1)} collective-permute-done((bf16[2,5,96,384]{3,2,1,0:T(8,128)(2,1)S(1)}, bf16[2,5,96,384]{3,2,1,0:T(8,128)(2,1)}, u32[]{:S(2)}, u32[]{:S(2)}) %collective-permute-start.6) | collective-permute-done | bytes 737312 | tf_op jit(solution)/shard_map/ppermute | solution.py:19
  142.6 2.8 %collective-permute-start.12 = (bf16[2,5,96,384]{3,2,1,0:T(8,128)(2,1)S(1)}, bf16[2,5,96,384]{3,2,1,0:T(8,128)(2,1)S(1)}, u32[]{:S(2)}, u32[]{:S(2)}) collective-permute-start(bf16[2,5,96,384]{3,2,1,0:T(8,128)(2,1)S(1)} %copy-done.8), channel_id=1, source_target_pairs={{0,1},{1,0},{2,3},{3,2},{4,5},{5,4},{6,7},{7,6},{8,9},{9,8},{10,11... | collective-permute-start | bytes 2211848 | tf_op jit(solution)/shard_map/ppermute | solution.py:19
  145.4 1.2 collective-permute-start.11
  146.6 1.2 collective-permute-start.10
  148.5 15.3 %collective-permute-done.11.refs_12_ = bf16[2,5,96,384]{3,2,1,0:T(8,128)(2,1)} collective-permute-done((bf16[2,5,96,384]{3,2,1,0:T(8,128)(2,1)}, bf16[2,5,96,384]{3,2,1,0:T(8,128)(2,1)}, u32[]{:S(2)}, u32[]{:S(2)}) %collective-permute-start.11) | collective-permute-done | bytes 737312 | tf_op jit(solution)/shard_map/ppermute | solution.py:19
  166.8 2.2 %bitcast_add_fusion = f32[5,4,96,384]{3,2,1,0:T(8,128)S(1)} fusion(bf16[5,4,96,384]{3,2,1,0:T(8,128)(2,1)S(1)} %collective-permute-done.26, f32[5,4,2,96,384]{4,3,2,1,0:T(8,128)} %copy-done.3, s32[]{:T(128)S(6)} %select_n.80), kind=kLoop, calls=%fused_computation.14 | loop fusion | flops 1474560 | bytes 7372804 | tf_op jit(solution)/shard_map/add | solution.py:270
  169.2 3.4 %collective-permute-start.28 = (bf16[5,96,384]{2,1,0:T(8,128)(2,1)S(1)}, bf16[5,96,384]{2,1,0:T(8,128)(2,1)S(1)}, u32[]{:S(2)}, u32[]{:S(2)}) collective-permute-start(bf16[5,96,384]{2,1,0:T(8,128)(2,1)S(1)} %get-tuple-element.13), channel_id=1, source_target_pairs={{0,4},{1,5},{2,6},{3,7},{4,0},{5,1},{6,2},{7,3},{8,12},{9,13},{10,... | collective-permute-start | bytes 1105928 | tf_op jit(solution)/shard_map/ppermute | solution.py:19
  172.6 21.4 %input_grad.1 = bf16[1,1024,768]{2,1,0:T(8,128)(2,1)} custom-call(s32[2]{0:T(128)S(1)} %pad_add_fusion.place, bf16[1,1024,768]{2,1,0:T(8,128)(2,1)} %x_ref.1, bf16[528,384]{1,0:T(8,128)(2,1)S(1)} %get-tuple-element.19.refs_1_, bf16[528,384]{1,0:T(8,128)(2,1)S(1)} %collective-permute-done.refs_2_, bf16[528,384]{1,0:T(8,128)(2,1)S(1)} %collective-permute-done.1.refs_3_, ...), custom_call_target="tpu_custom_call" | custom-call | flops 6228541440 | bytes 20971520 | tf_op jit(solution)/shard_map/input_grad/pallas_call | solution.py:157
  194.0 1.6 collective-permute-done.28
  195.6 7.9 %collective-permute-done.29 = bf16[5,96,384]{2,1,0:T(8,128)(2,1)S(1)} collective-permute-done((bf16[5,96,384]{2,1,0:T(8,128)(2,1)S(1)}, bf16[5,96,384]{2,1,0:T(8,128)(2,1)S(1)}, u32[]{:S(2)}, u32[]{:S(2)}) %collective-permute-start.29) | collective-permute-done | bytes 368672 | tf_op jit(solution)/shard_map/ppermute | solution.py:19
  (70 shorter events, 12.6 us)
Async XLA Ops:
  0.6 1.4 copy-start
  3.8 43.4 %collective-permute-start.23 = (bf16[256,1536]{1,0:T(8,128)(2,1)S(1)}, bf16[256,1536]{1,0:T(8,128)(2,1)S(1)}, u32[]{:S(2)}, u32[]{:S(2)}) collective-permute-start(bf16[256,1536]{1,0:T(8,128)(2,1)S(1)} %get-tuple-element.5), channel_id=1, source_target_pairs={{0,16},{8,24},{16,0},{24,8},{1,17},{9,25},{17,1},{25,9},{2,18},{10... | collective-permute-start | bytes 2359304 | tf_op jit(solution)/shard_map/ppermute | solution.py:19
  5.1 45.6 %collective-permute-start.21 = (bf16[256,1536]{1,0:T(8,128)(2,1)S(1)}, bf16[256,1536]{1,0:T(8,128)(2,1)}, u32[]{:S(2)}, u32[]{:S(2)}) collective-permute-start(bf16[256,1536]{1,0:T(8,128)(2,1)S(1)} %get-tuple-element.5), channel_id=1, source_target_pairs={{0,8},{8,0},{16,24},{24,16},{1,9},{9,1},{17,25},{25,17},{2,10},{10... | collective-permute-start | bytes 2359304 | tf_op jit(solution)/shard_map/ppermute | solution.py:19
  6.3 26.7 %collective-permute-start.4 = (bf16[5,96,384]{2,1,0:T(8,128)(2,1)}, bf16[5,96,384]{2,1,0:T(8,128)(2,1)}, u32[]{:S(2)}, u32[]{:S(2)}) collective-permute-start(bf16[5,96,384]{2,1,0:T(8,128)(2,1)} %param.5), channel_id=1, source_target_pairs={{0,4},{1,5},{2,6},{3,7},{4,0},{5,1},{6,2},{7,3},{8,12},{9,13},{10,... | collective-permute-start | bytes 1105928 | tf_op jit(solution)/shard_map/ppermute | solution.py:19
  8.6 32.3 %collective-permute-start.5 = (bf16[5,96,384]{2,1,0:T(8,128)(2,1)}, bf16[5,96,384]{2,1,0:T(8,128)(2,1)}, u32[]{:S(2)}, u32[]{:S(2)}) collective-permute-start(bf16[5,96,384]{2,1,0:T(8,128)(2,1)} %param.5), channel_id=1, source_target_pairs={{0,6},{1,7},{2,4},{3,5},{4,2},{5,3},{6,0},{7,1},{8,14},{9,15},{10,... | collective-permute-start | bytes 1105928 | tf_op jit(solution)/shard_map/ppermute | solution.py:19
  8.6 34.6 %collective-permute-start.3 = (bf16[5,96,384]{2,1,0:T(8,128)(2,1)}, bf16[5,96,384]{2,1,0:T(8,128)(2,1)S(1)}, u32[]{:S(2)}, u32[]{:S(2)}) collective-permute-start(bf16[5,96,384]{2,1,0:T(8,128)(2,1)} %param.5), channel_id=1, source_target_pairs={{0,2},{1,3},{2,0},{3,1},{4,6},{5,7},{6,4},{7,5},{8,10},{9,11},{10,... | collective-permute-start | bytes 1105928 | tf_op jit(solution)/shard_map/ppermute | solution.py:19
  17.5 2.1 %copy-start.2 = (bf16[2048,1152]{1,0:T(8,128)(2,1)}, bf16[2048,1152]{1,0:T(8,128)(2,1)S(1)}, u32[]{:S(2)}) copy-start(bf16[2048,1152]{1,0:T(8,128)(2,1)S(1)} %fusion.7) | copy-start | bytes 14155780
  33.0 21.5 %collective-permute-start.22 = (bf16[256,1536]{1,0:T(8,128)(2,1)S(1)}, bf16[256,1536]{1,0:T(8,128)(2,1)S(1)}, u32[]{:S(2)}, u32[]{:S(2)}) collective-permute-start(bf16[256,1536]{1,0:T(8,128)(2,1)S(1)} %get-tuple-element.4), channel_id=1, source_target_pairs={{0,16},{8,24},{16,0},{24,8},{1,17},{9,25},{17,1},{25,9},{2,18},{10... | collective-permute-start | bytes 2359304 | tf_op jit(solution)/shard_map/ppermute | solution.py:19
  40.9 18.7 %collective-permute-start.20 = (bf16[256,1536]{1,0:T(8,128)(2,1)S(1)}, bf16[256,1536]{1,0:T(8,128)(2,1)}, u32[]{:S(2)}, u32[]{:S(2)}) collective-permute-start(bf16[256,1536]{1,0:T(8,128)(2,1)S(1)} %get-tuple-element.4), channel_id=1, source_target_pairs={{0,8},{8,0},{16,24},{24,16},{1,9},{9,1},{17,25},{25,17},{2,10},{10... | collective-permute-start | bytes 2359304 | tf_op jit(solution)/shard_map/ppermute | solution.py:19
  43.2 0.7 copy-start.9
  43.9 82.4 %collective-permute-start = (bf16[528,384]{1,0:T(8,128)(2,1)}, bf16[528,384]{1,0:T(8,128)(2,1)S(1)}, u32[]{:S(2)}, u32[]{:S(2)}) collective-permute-start(bf16[528,384]{1,0:T(8,128)(2,1)} %get-tuple-element.17), channel_id=1, source_target_pairs={{0,8},{8,0},{16,24},{24,16},{1,9},{9,1},{17,25},{25,17},{2,10},{10... | collective-permute-start | bytes 1216520 | tf_op jit(solution)/shard_map/ppermute | solution.py:19
  47.2 0.9 copy-start.6
  48.1 79.5 %collective-permute-start.1 = (bf16[528,384]{1,0:T(8,128)(2,1)}, bf16[528,384]{1,0:T(8,128)(2,1)S(1)}, u32[]{:S(2)}, u32[]{:S(2)}) collective-permute-start(bf16[528,384]{1,0:T(8,128)(2,1)} %get-tuple-element.18), channel_id=1, source_target_pairs={{0,16},{8,24},{16,0},{24,8},{1,17},{9,25},{17,1},{25,9},{2,18},{10... | collective-permute-start | bytes 1216520 | tf_op jit(solution)/shard_map/ppermute | solution.py:19
  50.7 3.7 %copy-start.7 = (bf16[256,1536]{1,0:T(8,128)(2,1)S(1)}, bf16[256,1536]{1,0:T(8,128)(2,1)}, u32[]{:S(2)}) copy-start(bf16[256,1536]{1,0:T(8,128)(2,1)} %copy-done.6) | copy-start | bytes 2359300
  50.8 78.1 %collective-permute-start.2 = (bf16[528,384]{1,0:T(8,128)(2,1)}, bf16[528,384]{1,0:T(8,128)(2,1)S(1)}, u32[]{:S(2)}, u32[]{:S(2)}) collective-permute-start(bf16[528,384]{1,0:T(8,128)(2,1)} %get-tuple-element.16), channel_id=1, source_target_pairs={{0,24},{8,16},{16,8},{24,0},{1,25},{9,17},{17,9},{25,1},{2,26},{10... | collective-permute-start | bytes 1216520 | tf_op jit(solution)/shard_map/ppermute | solution.py:19
  54.5 39.3 %collective-permute-start.25 = (bf16[256,1536]{1,0:T(8,128)(2,1)S(1)}, bf16[256,1536]{1,0:T(8,128)(2,1)S(1)}, u32[]{:S(2)}, u32[]{:S(2)}) collective-permute-start(bf16[256,1536]{1,0:T(8,128)(2,1)S(1)} %copy-done.7), channel_id=1, source_target_pairs={{0,8},{8,0},{16,24},{24,16},{1,9},{9,1},{17,25},{25,17},{2,10},{10... | collective-permute-start | bytes 2359304 | tf_op jit(solution)/shard_map/ppermute | solution.py:19
  59.6 36.6 %collective-permute-start.24 = (bf16[256,1536]{1,0:T(8,128)(2,1)}, bf16[256,1536]{1,0:T(8,128)(2,1)S(1)}, u32[]{:S(2)}, u32[]{:S(2)}) collective-permute-start(bf16[256,1536]{1,0:T(8,128)(2,1)} %collective-permute-done.20), channel_id=1, source_target_pairs={{0,16},{8,24},{16,0},{24,8},{1,17},{9,25},{17,1},{25,9},{2,18},{10... | collective-permute-start | bytes 2359304 | tf_op jit(solution)/shard_map/ppermute | solution.py:19
  75.2 21.4 %copy-start.1 = (f32[1152,1536]{1,0:T(8,128)S(1)}, f32[1152,1536]{1,0:T(8,128)}, u32[]{:S(2)}) copy-start(f32[1152,1536]{1,0:T(8,128)} %fusion.5) | copy-start | bytes 21233668
  93.8 37.7 %collective-permute-start.9 = (bf16[2,5,96,384]{3,2,1,0:T(8,128)(2,1)}, bf16[2,5,96,384]{3,2,1,0:T(8,128)(2,1)}, u32[]{:S(2)}, u32[]{:S(2)}) collective-permute-start(bf16[2,5,96,384]{3,2,1,0:T(8,128)(2,1)} %pad_maximum_fusion.1.refs_6_), channel_id=1, source_target_pairs={{0,16},{8,24},{16,0},{24,8},{1,17},{9,25},{17,1},{25,9},{2,18},{10... | collective-permute-start | bytes 2211848 | tf_op jit(solution)/shard_map/ppermute | solution.py:19
  96.2 49.2 %collective-permute-start.7 = (bf16[2,5,96,384]{3,2,1,0:T(8,128)(2,1)}, bf16[2,5,96,384]{3,2,1,0:T(8,128)(2,1)}, u32[]{:S(2)}, u32[]{:S(2)}) collective-permute-start(bf16[2,5,96,384]{3,2,1,0:T(8,128)(2,1)} %pad_maximum_fusion.1.refs_6_), channel_id=1, source_target_pairs={{0,8},{8,0},{16,24},{24,16},{1,9},{9,1},{17,25},{25,17},{2,10},{10... | collective-permute-start | bytes 2211848 | tf_op jit(solution)/shard_map/ppermute | solution.py:19
  115.9 4.9 %copy-start.4 = (f32[768,384]{1,0:T(8,128)S(1)}, f32[768,384]{1,0:T(8,128)}, u32[]{:S(2)}) copy-start(f32[768,384]{1,0:T(8,128)} %copy.13) | copy-start | bytes 3538948
  115.9 6.0 %copy-start.5 = (f32[768,384]{1,0:T(8,128)S(1)}, f32[768,384]{1,0:T(8,128)}, u32[]{:S(2)}) copy-start(f32[768,384]{1,0:T(8,128)} %copy.14) | copy-start | bytes 3538948
  123.0 3.3 %copy-start.8 = (bf16[2,5,96,384]{3,2,1,0:T(8,128)(2,1)S(1)}, bf16[2,5,96,384]{3,2,1,0:T(8,128)(2,1)}, u32[]{:S(2)}) copy-start(bf16[2,5,96,384]{3,2,1,0:T(8,128)(2,1)} %pad_maximum_fusion.refs_5_) | copy-start | bytes 2211844
  126.3 5.0 %copy-start.3 = (f32[5,4,2,96,384]{4,3,2,1,0:T(8,128)}, f32[5,4,2,96,384]{4,3,2,1,0:T(8,128)S(1)}, u32[]{:S(2)}) copy-start(f32[5,4,2,96,384]{4,3,2,1,0:T(8,128)S(1)} %broadcast_multiply_fusion) | copy-start | bytes 17694724
  126.3 16.2 %collective-permute-start.6 = (bf16[2,5,96,384]{3,2,1,0:T(8,128)(2,1)S(1)}, bf16[2,5,96,384]{3,2,1,0:T(8,128)(2,1)}, u32[]{:S(2)}, u32[]{:S(2)}) collective-permute-start(bf16[2,5,96,384]{3,2,1,0:T(8,128)(2,1)S(1)} %copy-done.8), channel_id=1, source_target_pairs={{0,8},{8,0},{16,24},{24,16},{1,9},{9,1},{17,25},{25,17},{2,10},{10... | collective-permute-start | bytes 2211848 | tf_op jit(solution)/shard_map/ppermute | solution.py:19
  127.6 19.0 %collective-permute-start.8 = (bf16[2,5,96,384]{3,2,1,0:T(8,128)(2,1)S(1)}, bf16[2,5,96,384]{3,2,1,0:T(8,128)(2,1)}, u32[]{:S(2)}, u32[]{:S(2)}) collective-permute-start(bf16[2,5,96,384]{3,2,1,0:T(8,128)(2,1)S(1)} %copy-done.8), channel_id=1, source_target_pairs={{0,16},{8,24},{16,0},{24,8},{1,17},{9,25},{17,1},{25,9},{2,18},{10... | collective-permute-start | bytes 2211848 | tf_op jit(solution)/shard_map/ppermute | solution.py:19
  128.9 19.0 %collective-permute-start.13 = (bf16[2,5,96,384]{3,2,1,0:T(8,128)(2,1)}, bf16[2,5,96,384]{3,2,1,0:T(8,128)(2,1)S(1)}, u32[]{:S(2)}, u32[]{:S(2)}) collective-permute-start(bf16[2,5,96,384]{3,2,1,0:T(8,128)(2,1)} %pad_maximum_fusion.1.refs_6_), channel_id=1, source_target_pairs={{0,1},{1,0},{2,3},{3,2},{4,5},{5,4},{6,7},{7,6},{8,9},{9,8},{10,11... | collective-permute-start | bytes 2211848 | tf_op jit(solution)/shard_map/ppermute | solution.py:19
  131.5 34.4 %collective-permute-start.26 = (bf16[5,4,96,384]{3,2,1,0:T(8,128)(2,1)S(1)}, bf16[5,4,96,384]{3,2,1,0:T(8,128)(2,1)S(1)}, u32[]{:S(2)}, u32[]{:S(2)}) collective-permute-start(bf16[5,4,96,384]{3,2,1,0:T(8,128)(2,1)S(1)} %fusion.9), channel_id=1, source_target_pairs={{0,1},{1,0},{2,3},{3,2},{4,5},{5,4},{6,7},{7,6},{8,9},{9,8},{10,11... | collective-permute-start | bytes 4423688 | tf_op jit(solution)/shard_map/ppermute | solution.py:19
  142.6 5.9 %collective-permute-start.12 = (bf16[2,5,96,384]{3,2,1,0:T(8,128)(2,1)S(1)}, bf16[2,5,96,384]{3,2,1,0:T(8,128)(2,1)S(1)}, u32[]{:S(2)}, u32[]{:S(2)}) collective-permute-start(bf16[2,5,96,384]{3,2,1,0:T(8,128)(2,1)S(1)} %copy-done.8), channel_id=1, source_target_pairs={{0,1},{1,0},{2,3},{3,2},{4,5},{5,4},{6,7},{7,6},{8,9},{9,8},{10,11... | collective-permute-start | bytes 2211848 | tf_op jit(solution)/shard_map/ppermute | solution.py:19
  145.4 18.4 %collective-permute-start.11 = (bf16[2,5,96,384]{3,2,1,0:T(8,128)(2,1)}, bf16[2,5,96,384]{3,2,1,0:T(8,128)(2,1)}, u32[]{:S(2)}, u32[]{:S(2)}) collective-permute-start(bf16[2,5,96,384]{3,2,1,0:T(8,128)(2,1)} %collective-permute-done.9.refs_10_), channel_id=1, source_target_pairs={{0,8},{8,0},{16,24},{24,16},{1,9},{9,1},{17,25},{25,17},{2,10},{10... | collective-permute-start | bytes 2211848 | tf_op jit(solution)/shard_map/ppermute | solution.py:19
  146.6 18.1 %collective-permute-start.10 = (bf16[2,5,96,384]{3,2,1,0:T(8,128)(2,1)}, bf16[2,5,96,384]{3,2,1,0:T(8,128)(2,1)}, u32[]{:S(2)}, u32[]{:S(2)}) collective-permute-start(bf16[2,5,96,384]{3,2,1,0:T(8,128)(2,1)} %collective-permute-done.6.refs_7_), channel_id=1, source_target_pairs={{0,16},{8,24},{16,0},{24,8},{1,17},{9,25},{17,1},{25,9},{2,18},{10... | collective-permute-start | bytes 2211848 | tf_op jit(solution)/shard_map/ppermute | solution.py:19
  147.9 18.1 %copy-start.10 = (bf16[2,5,96,384]{3,2,1,0:T(8,128)(2,1)}, bf16[2,5,96,384]{3,2,1,0:T(8,128)(2,1)S(1)}, u32[]{:S(2)}) copy-start(bf16[2,5,96,384]{3,2,1,0:T(8,128)(2,1)S(1)} %collective-permute-done.13.refs_14_) | copy-start | bytes 2211844
  147.9 18.0 %collective-permute-start.17 = (bf16[2,5,96,384]{3,2,1,0:T(8,128)(2,1)}, bf16[2,5,96,384]{3,2,1,0:T(8,128)(2,1)S(1)}, u32[]{:S(2)}, u32[]{:S(2)}) collective-permute-start(bf16[2,5,96,384]{3,2,1,0:T(8,128)(2,1)} %collective-permute-done.9.refs_10_), channel_id=1, source_target_pairs={{0,1},{1,0},{2,3},{3,2},{4,5},{5,4},{6,7},{7,6},{8,9},{9,8},{10,11... | collective-permute-start | bytes 2211848 | tf_op jit(solution)/shard_map/ppermute | solution.py:19
  148.4 17.5 %copy-start.11 = (bf16[2,5,96,384]{3,2,1,0:T(8,128)(2,1)}, bf16[2,5,96,384]{3,2,1,0:T(8,128)(2,1)S(1)}, u32[]{:S(2)}) copy-start(bf16[2,5,96,384]{3,2,1,0:T(8,128)(2,1)S(1)} %collective-permute-done.12.refs_13_) | copy-start | bytes 2211844
  148.4 20.7 %collective-permute-start.14 = (bf16[2,5,96,384]{3,2,1,0:T(8,128)(2,1)}, bf16[2,5,96,384]{3,2,1,0:T(8,128)(2,1)}, u32[]{:S(2)}, u32[]{:S(2)}) collective-permute-start(bf16[2,5,96,384]{3,2,1,0:T(8,128)(2,1)} %collective-permute-done.6.refs_7_), channel_id=1, source_target_pairs={{0,1},{1,0},{2,3},{3,2},{4,5},{5,4},{6,7},{7,6},{8,9},{9,8},{10,11... | collective-permute-start | bytes 2211848 | tf_op jit(solution)/shard_map/ppermute | solution.py:19
  163.8 5.4 %collective-permute-start.15 = (bf16[2,5,96,384]{3,2,1,0:T(8,128)(2,1)}, bf16[2,5,96,384]{3,2,1,0:T(8,128)(2,1)}, u32[]{:S(2)}, u32[]{:S(2)}) collective-permute-start(bf16[2,5,96,384]{3,2,1,0:T(8,128)(2,1)} %collective-permute-done.7.refs_8_), channel_id=1, source_target_pairs={{0,1},{1,0},{2,3},{3,2},{4,5},{5,4},{6,7},{7,6},{8,9},{9,8},{10,11... | collective-permute-start | bytes 2211848 | tf_op jit(solution)/shard_map/ppermute | solution.py:19
  164.7 7.8 %collective-permute-start.16 = (bf16[2,5,96,384]{3,2,1,0:T(8,128)(2,1)}, bf16[2,5,96,384]{3,2,1,0:T(8,128)(2,1)}, u32[]{:S(2)}, u32[]{:S(2)}) collective-permute-start(bf16[2,5,96,384]{3,2,1,0:T(8,128)(2,1)} %collective-permute-done.8.refs_9_), channel_id=1, source_target_pairs={{0,1},{1,0},{2,3},{3,2},{4,5},{5,4},{6,7},{7,6},{8,9},{9,8},{10,11... | collective-permute-start | bytes 2211848 | tf_op jit(solution)/shard_map/ppermute | solution.py:19
  165.9 0.9 copy-start.12
  165.9 6.7 %collective-permute-start.19 = (bf16[2,5,96,384]{3,2,1,0:T(8,128)(2,1)}, bf16[2,5,96,384]{3,2,1,0:T(8,128)(2,1)}, u32[]{:S(2)}, u32[]{:S(2)}) collective-permute-start(bf16[2,5,96,384]{3,2,1,0:T(8,128)(2,1)} %collective-permute-done.11.refs_12_), channel_id=1, source_target_pairs={{0,1},{1,0},{2,3},{3,2},{4,5},{5,4},{6,7},{7,6},{8,9},{9,8},{10,11... | collective-permute-start | bytes 2211848 | tf_op jit(solution)/shard_map/ppermute | solution.py:19
  166.7 5.9 %collective-permute-start.18 = (bf16[2,5,96,384]{3,2,1,0:T(8,128)(2,1)}, bf16[2,5,96,384]{3,2,1,0:T(8,128)(2,1)}, u32[]{:S(2)}, u32[]{:S(2)}) collective-permute-start(bf16[2,5,96,384]{3,2,1,0:T(8,128)(2,1)} %collective-permute-done.10.refs_11_), channel_id=1, source_target_pairs={{0,1},{1,0},{2,3},{3,2},{4,5},{5,4},{6,7},{7,6},{8,9},{9,8},{10,11... | collective-permute-start | bytes 2211848 | tf_op jit(solution)/shard_map/ppermute | solution.py:19
  169.1 24.9 %collective-permute-start.27 = (bf16[5,96,384]{2,1,0:T(8,128)(2,1)S(1)}, bf16[5,96,384]{2,1,0:T(8,128)(2,1)S(1)}, u32[]{:S(2)}, u32[]{:S(2)}) collective-permute-start(bf16[5,96,384]{2,1,0:T(8,128)(2,1)S(1)} %get-tuple-element.11), channel_id=1, source_target_pairs={{0,2},{1,3},{2,0},{3,1},{4,6},{5,7},{6,4},{7,5},{8,10},{9,11},{10,... | collective-permute-start | bytes 1105928 | tf_op jit(solution)/shard_map/ppermute | solution.py:19
  169.2 26.4 %collective-permute-start.28 = (bf16[5,96,384]{2,1,0:T(8,128)(2,1)S(1)}, bf16[5,96,384]{2,1,0:T(8,128)(2,1)S(1)}, u32[]{:S(2)}, u32[]{:S(2)}) collective-permute-start(bf16[5,96,384]{2,1,0:T(8,128)(2,1)S(1)} %get-tuple-element.13), channel_id=1, source_target_pairs={{0,4},{1,5},{2,6},{3,7},{4,0},{5,1},{6,2},{7,3},{8,12},{9,13},{10,... | collective-permute-start | bytes 1105928 | tf_op jit(solution)/shard_map/ppermute | solution.py:19
  172.6 30.9 %collective-permute-start.29 = (bf16[5,96,384]{2,1,0:T(8,128)(2,1)S(1)}, bf16[5,96,384]{2,1,0:T(8,128)(2,1)S(1)}, u32[]{:S(2)}, u32[]{:S(2)}) collective-permute-start(bf16[5,96,384]{2,1,0:T(8,128)(2,1)S(1)} %get-tuple-element.12), channel_id=1, source_target_pairs={{0,6},{1,7},{2,4},{3,5},{4,2},{5,3},{6,0},{7,1},{8,14},{9,15},{10,... | collective-permute-start | bytes 1105928 | tf_op jit(solution)/shard_map/ppermute | solution.py:19

commit v2 on v1

v2 whole, which is shorter than its diff:
```python
import functools
import math

import jax
import jax.numpy as jnp
from jax import lax
from jax.experimental import pallas as pl
from jax.experimental.pallas import tpu as pltpu
from jax.sharding import PartitionSpec as P

HALO = 8
LANES = 128
ROOT = math.sqrt(2.0 / math.pi)
CUBIC = 0.044715


def from_peer(value, axis, distance):
    peers = lax.axis_size(axis)
    return lax.ppermute(value, axis, [(i, i ^ distance) for i in range(peers)])


def after(value, *earlier):
    anywhere = pl.BlockSpec(memory_space=pl.ANY)
    return pl.pallas_call(
        lambda *refs: None,
        out_shape=jax.ShapeDtypeStruct(value.shape, value.dtype),
        in_specs=[anywhere] * (1 + len(earlier)),
        out_specs=anywhere,
        input_output_aliases={0: 0},
        name="after",
    )(value, *earlier)


def half_of(piece, which):
    if len(piece) == 2:
        return piece[which]
    size = piece[0].shape[0] // 2
    return lax.slice_in_dim(piece[0], which * size, (which + 1) * size, axis=0)


def gather_square(value, axis):
    found = {0: (value,)}
    near = [d for d in range(1, lax.axis_size(axis)) if d & (d - 1) == 0]
    for distance in near:
        found[distance] = (from_peer(value, axis, distance),)
    for distance in range(1, lax.axis_size(axis)):
        if distance not in near:
            high = 1 << (distance.bit_length() - 1)
            low = distance & -distance
            found[distance] = (
                from_peer(half_of(found[distance ^ high], 0), axis, high),
                from_peer(half_of(found[distance ^ low], 1), axis, low),
            )
    return found


def gather_line(value, axis, count, unit):
    found, mask = {0: value}, count - 1
    while mask:
        for distance in list(found):
            found[distance ^ mask] = from_peer(found[distance], axis, mask * unit)
        mask >>= 1
    return [found[distance] for distance in range(count)]


def act_kernel(x_ref, out_ref, scratch):
    width = x_ref.shape[2]

    @pl.loop(0, out_ref.shape[0] // 64)
    def _(step):
        start = pl.multiple_of(step * 64, 64)
        x = x_ref[0, pl.ds(pl.multiple_of(2 * start, 128), 128), :].astype(jnp.float32)
        act = x * (0.5 * (1.0 + jnp.tanh(ROOT * (x + CUBIC * (x * x * x)))))
        for c in range(width // LANES):
            scratch[c] = act[:, c * LANES : (c + 1) * LANES]
        for parity in range(2):
            for c in range(width // LANES):
                picked = scratch[c, pl.ds(parity, 64, stride=2), :].astype(jnp.bfloat16)
                left = parity * width + c * LANES
                out_ref[pl.ds(start, 64), left : left + LANES] = picked


def activate(inputs):
    fine, width = inputs.shape[1:]
    return pl.pallas_call(
        act_kernel,
        out_shape=jax.ShapeDtypeStruct((fine // 2, 2 * width), jnp.bfloat16),
        in_specs=[pl.BlockSpec(memory_space=pltpu.VMEM)],
        out_specs=pl.BlockSpec(memory_space=pltpu.VMEM),
        scratch_shapes=[pltpu.VMEM((width // LANES, 128, LANES), jnp.float32)],
        compiler_params=pltpu.CompilerParams(vmem_limit_bytes=24 << 20),
        name="act",
    )(inputs)


def weight_grad_kernel(layout, scale, place, shifts_ref, *refs):
    pieces, (mine_ref, theirs_ref) = refs[: len(layout)], refs[len(layout) : len(layout) + 2]
    held, shifts, total, sems, shift_sem = refs[len(layout) + 2 :]
    me, core, plane = place[0], place[1] % 2, place[1] // 2
    planes, taps, rows, block = mine_ref.shape
    coarse = pieces[0].shape[0]
    width = total.shape[0] // 2
    copies = [pltpu.make_async_copy(shifts_ref, shifts, shift_sem)]
    for i, (distance, first, size) in enumerate(layout):
        start = pl.multiple_of((me ^ distance) * coarse + first, 16)
        copies.append(
            pltpu.make_async_copy(pieces[i], held.at[pl.ds(start, size)], sems.at[i])
        )
    for copy in copies:
        copy.start()
    for copy in copies:
        copy.wait()
    tile = 256

    @pl.loop(0, 2 * width // tile)
    def _(i):
        span = pl.ds(pl.multiple_of(i * tile, tile), tile)
        total[span, :] = lax.dot_general(
            held[:, span], shifts[...], (((0,), (0,)), ((), ())), preferred_element_type=jnp.float32
        )

    for out_ref, parity, kind in ((theirs_ref, 1 - core, jnp.bfloat16), (mine_ref, core, jnp.float32)):

        @pl.loop(0, planes)
        def _(j):
            start = ((plane ^ j) * 2 + parity) * rows
            even = pl.ds(pl.multiple_of(start, 16), rows)
            odd = pl.ds(pl.multiple_of(width + start, 16), rows)
            for k, (left, right) in enumerate(((0, 0), (1, 0), (1, 1), (2, 1), (2, 2))):
                term = total[even, left * block : (left + 1) * block]
                term += total[odd, right * block : (right + 1) * block]
                out_ref[j, k] = (scale * term).astype(kind)


def kernel_gradient(place, act, shifts, scale, planes, taps, rows):
    coarse, both = act[0][0].shape
    layout, pieces = [], []
    for distance, parts in act.items():
        first = 0
        for part in parts:
            layout.append((distance, first, part.shape[0]))
            pieces.append(part)
            first += part.shape[0]
    positions, block = len(act) * coarse, shifts.shape[1] // 3
    anywhere = pl.BlockSpec(memory_space=pl.ANY)
    shape = (planes, taps, rows, block)
    whole = pl.BlockSpec(shape, lambda i, place: (0, 0, 0, 0))
    return pl.pallas_call(
        functools.partial(weight_grad_kernel, layout, scale),
        out_shape=(
            jax.ShapeDtypeStruct(shape, jnp.float32),
            jax.ShapeDtypeStruct(shape, jnp.bfloat16),
        ),
        grid_spec=pltpu.PrefetchScalarGridSpec(
            num_scalar_prefetch=1,
            grid=(1,),
            in_specs=[anywhere] * (1 + len(pieces)),
            out_specs=[whole, whole],
            scratch_shapes=[
                pltpu.VMEM((positions, both), jnp.bfloat16),
                pltpu.VMEM(shifts.shape, jnp.bfloat16),
                pltpu.VMEM((both, shifts.shape[1]), jnp.float32),
                pltpu.SemaphoreType.DMA((len(pieces),)),
                pltpu.SemaphoreType.DMA,
            ],
        ),
        compiler_params=pltpu.CompilerParams(vmem_limit_bytes=48 << 20),
        cost_estimate=pl.CostEstimate(
            flops=2 * positions * both * shifts.shape[1], bytes_accessed=16 << 20, transcendentals=0
        ),
        name="weight_grad",
    )(place, shifts, *pieces)


def kernel_gradient_unaligned(place, act, shifts, scale, planes, taps, rows):
    coarse, both = act[0][0].shape
    width, block = both // 2, shifts.shape[1] // 3
    total = jnp.zeros((both, shifts.shape[1]), jnp.float32)
    for distance, parts in act.items():
        first = (place[0] ^ distance) * coarse
        for part in parts:
            matching = lax.dynamic_slice_in_dim(shifts, first, part.shape[0], 0)
            first = first + part.shape[0]
            total = total + lax.dot_general(
                part, matching, (((0,), (0,)), ((), ())), preferred_element_type=jnp.float32
            )
    terms = []
    for left, right in ((0, 0), (1, 0), (1, 1), (2, 1), (2, 2)):
        even = total[:width, left * block : (left + 1) * block]
        odd = total[width:, right * block : (right + 1) * block]
        terms.append(scale * (even + odd))
    terms = jnp.stack(terms).reshape(taps, planes, 2, rows, block)
    core, plane = place[1] % 2, place[1] // 2
    outs = []
    for parity in (core, 1 - core):
        blocks = lax.dynamic_index_in_dim(terms, parity, 2, keepdims=False)
        outs.append(
            jnp.stack(
                [
                    lax.dynamic_index_in_dim(blocks, plane ^ j, 1, keepdims=False)
                    for j in range(planes)
                ]
            )
        )
    return outs[0], outs[1].astype(jnp.bfloat16)


def input_grad_kernel(seqs, layout, place, *refs):
    x_ref, grads = refs[0], refs[1 : 1 + seqs]
    pieces = refs[1 + seqs : 1 + seqs + len(layout)]
    out_ref, wv, gv, products, fine, again, sems, grad_sems = refs[1 + seqs + len(layout) :]
    me, rep = place[0], place[1]
    taps, reps, rows, _ = wv.shape
    block = grads[0].shape[1]
    coarse = x_ref.shape[1] // 2
    width = x_ref.shape[2]
    copies = []
    for distance in range(seqs):
        columns = pl.ds(pl.multiple_of((me ^ distance) * block, block), block)
        copies.append(
            pltpu.make_async_copy(grads[distance], gv.at[:, columns], grad_sems.at[distance])
        )
    for i, (distance, flip, first) in enumerate(layout):
        columns = pl.ds(pl.multiple_of((me ^ distance) * block, block), block)
        for j in range(pieces[i].shape[0]):
            owner = rep ^ flip ^ (2 * (first + j))
            copies.append(
                pltpu.make_async_copy(
                    pieces[i].at[j], wv.at[:, owner, :, columns], sems.at[i, j]
                )
            )
    for copy in copies:
        copy.start()
    for copy in copies:
        copy.wait()
    tile = max(1, reps // 2)

    @pl.loop(0, taps)
    def _(k):
        for part in range(reps // tile):
            kernel = wv[k, part * tile : (part + 1) * tile].reshape(tile * rows, wv.shape[3])
            products[k, :, part * tile * rows : (part + 1) * tile * rows] = lax.dot_general(
                gv[...], kernel, (((1,), (1,)), ((), ())), preferred_element_type=jnp.float32
            )

    step = 64

    @pl.loop(0, coarse // step)
    def _(i):
        base = pl.multiple_of(i * step, step)

        def shifted(k, by):
            window = products[k, pl.ds(base, step + 2 * HALO), :]
            return window[HALO + by : HALO + by + step]

        skip = gv[pl.ds(pl.multiple_of(base, 8), step + 2 * HALO), :width].astype(jnp.float32)
        skip = skip[HALO : HALO + step]
        shared = shifted(0, 1) + shifted(2, 0) + shifted(4, -1)
        even = shared + shifted(1, 0) + shifted(3, -1)
        odd = shared + shifted(1, 1) + shifted(3, 0)
        for c in range(width // LANES):
            lanes = slice(c * LANES, (c + 1) * LANES)
            fine[c, pl.ds(0, step, stride=2), :] = even[:, lanes]
            fine[c, pl.ds(1, step, stride=2), :] = odd[:, lanes]
            again[c, pl.ds(0, step, stride=2), :] = skip[:, lanes]
            again[c, pl.ds(1, step, stride=2), :] = skip[:, lanes]
            span = pl.ds(pl.multiple_of(2 * base, 2 * step), 2 * step)
            x = x_ref[0, span, lanes].astype(jnp.float32)
            tanh = jnp.tanh(ROOT * (x + CUBIC * (x * x * x)))
            slope = 0.5 * (1.0 + tanh) + 0.5 * x * (1.0 - tanh * tanh) * (
                ROOT * (1.0 + 3.0 * CUBIC * (x * x))
            )
            out_ref[0, span, lanes] = (0.5 * (fine[c] * slope + again[c])).astype(jnp.bfloat16)


def ordered(kept, swapped):
    layout, pieces = [], []
    for flip, found in enumerate((kept, swapped)):
        for distance, parts in found.items():
            first = 0
            for part in parts:
                layout.append((distance, flip, first))
                pieces.append(part)
                first += part.shape[0]
    return layout, pieces


def input_gradient(place, inputs, grads, kept, swapped):
    planes, taps, rows, block = kept[0][0].shape
    seqs, reps = len(grads), 2 * planes
    layout, pieces = ordered(kept, swapped)
    window = grads[0].shape[0]
    width = inputs.shape[2]
    anywhere = pl.BlockSpec(memory_space=pl.ANY)
    operands = (inputs, *grads, *pieces)
    return pl.pallas_call(
        functools.partial(input_grad_kernel, seqs, layout),
        out_shape=jax.ShapeDtypeStruct(inputs.shape, jnp.bfloat16),
        grid_spec=pltpu.PrefetchScalarGridSpec(
            num_scalar_prefetch=1,
            grid=(1,),
            in_specs=[pl.BlockSpec(inputs.shape, lambda i, place: (0, 0, 0))]
            + [anywhere] * (len(operands) - 1),
            out_specs=pl.BlockSpec(inputs.shape, lambda i, place: (0, 0, 0)),
            scratch_shapes=[
                pltpu.VMEM((taps, reps, rows, seqs * block), jnp.bfloat16),
                pltpu.VMEM((window, seqs * block), jnp.bfloat16),
                pltpu.VMEM((taps, window, width), jnp.float32),
                pltpu.VMEM((width // LANES, 128, LANES), jnp.float32),
                pltpu.VMEM((width // LANES, 128, LANES), jnp.float32),
                pltpu.SemaphoreType.DMA((len(pieces), planes)),
                pltpu.SemaphoreType.DMA((seqs,)),
            ],
        ),
        compiler_params=pltpu.CompilerParams(vmem_limit_bytes=52 << 20),
        cost_estimate=pl.CostEstimate(
            flops=2 * taps * window * width * seqs * block,
            bytes_accessed=20 << 20,
            transcendentals=inputs.size,
        ),
        name="input_grad",
    )(place, *operands)


def input_gradient_unaligned(place, inputs, grads, kept, swapped):
    me, rep = place[0], place[1]
    planes, taps, rows, block = kept[0][0].shape
    seqs, reps = len(grads), 2 * planes
    window, coarse = grads[0].shape[0], inputs.shape[1] // 2
    grad = jnp.zeros((window, seqs * block), jnp.bfloat16)
    for distance in range(seqs):
        grad = lax.dynamic_update_slice(grad, grads[distance], (0, (me ^ distance) * block))
    kernel = jnp.zeros((taps, reps * rows, seqs * block), jnp.bfloat16)
    for (distance, flip, first), part in zip(*ordered(kept, swapped)):
        for j in range(part.shape[0]):
            owner = rep ^ flip ^ (2 * (first + j))
            spot = (0, owner * rows, (me ^ distance) * block)
            kernel = lax.dynamic_update_slice(kernel, part[j], spot)
    products = lax.dot_general(
        grad, kernel, (((1,), (2,)), ((), ())), preferred_element_type=jnp.float32
    )

    def shifted(k, by):
        return products[HALO + by : HALO + by + coarse, k]

    shared = shifted(0, 1) + shifted(2, 0) + shifted(4, -1)
    even = shared + shifted(1, 0) + shifted(3, -1)
    odd = shared + shifted(1, 1) + shifted(3, 0)
    total = jnp.stack([even, odd], axis=1).reshape(inputs.shape[1:])
    x = inputs[0].astype(jnp.float32)
    tanh = jnp.tanh(ROOT * (x + CUBIC * (x * x * x)))
    slope = 0.5 * (1.0 + tanh) + 0.5 * x * (1.0 - tanh * tanh) * (
        ROOT * (1.0 + 3.0 * CUBIC * (x * x))
    )
    skip = jnp.repeat(grad[HALO : HALO + coarse, : inputs.shape[2]].astype(jnp.float32), 2, axis=0)
    return (0.5 * (total * slope + skip)).astype(jnp.bfloat16)[None]


def on_device(inputs, trunk_grad, weights):
    seqs, reps = lax.axis_size("seq"), lax.axis_size("rep")
    me, rep = lax.axis_index("seq"), lax.axis_index("rep")
    place = jnp.stack([me, rep]).astype(jnp.int32)
    taps, rows, block = weights.shape
    fine, width = inputs.shape[1:]
    coarse, planes = fine // 2, reps // 2

    act = gather_square(activate(inputs), "seq")
    near = [act[1][0], act[2][0]] if seqs > 2 else []
    far = act[3] if seqs > 2 else ()

    column = after(jnp.stack(gather_line(weights, "rep", planes, 2)), *far)
    kept = gather_square(column, "seq")
    swapped = {d: tuple(from_peer(part, "rep", 1) for part in kept[d]) for d in kept}

    trunk = trunk_grad[0]
    edged = after(jnp.pad(trunk, ((HALO, HALO), (0, 0))), *near)
    grads = []
    for distance in range(seqs):
        window = lax.dynamic_slice_in_dim(edged, (me ^ distance) * coarse, coarse + 2 * HALO, 0)
        grads.append(from_peer(window, "seq", distance) if distance else window)

    zeros = jnp.zeros((1, block), jnp.bfloat16)
    later = jnp.concatenate([trunk[1:], zeros])
    earlier = jnp.concatenate([zeros, trunk[:-1]])
    shifts = jnp.concatenate([later, trunk, earlier], axis=1)
    scale = 0.5 * float(fine * seqs * reps) ** (-0.5)
    aligned = block % LANES == 0
    terms = kernel_gradient if aligned else kernel_gradient_unaligned
    mine, theirs = terms(place, act, shifts, scale, planes, taps, rows)
    arrived = from_peer(theirs, "rep", 1)
    weight_grad = mine[0] + arrived[0].astype(jnp.float32)
    for j in range(1, planes):
        leaving = (mine[j] + arrived[j].astype(jnp.float32)).astype(jnp.bfloat16)
        weight_grad = weight_grad + from_peer(leaving, "rep", 2 * j).astype(jnp.float32)

    gradient = input_gradient if aligned else input_gradient_unaligned
    input_grad = gradient(place, inputs, grads, kept, swapped)
    return (input_grad, weight_grad)


def solution(mesh):
    in_specs = (P("rep", "seq", None), P("rep", None, "seq"), P(None, "rep", "seq"))
    out_specs = (P("rep", "seq", None), P(None, "rep", "seq"))
    return jax.shard_map(
        on_device, mesh=mesh, in_specs=in_specs, out_specs=out_specs, check_vma=False
    )
```

time: 207 us -> 202 us (0.976)
  waiting for transfers between devices: 73 us -> 103 us
  matrix products: 29.6 us -> 0 us
  local copies, waits for them, and re-layouts: 33.5 us -> 11.2 us
  Pallas kernels: 23.2 us -> 39.2 us
  starting transfers between devices: 27.7 us -> 40.2 us
  other arithmetic: 16.7 us -> 6.89 us
    ppermute x30 -> x23, waiting for transfers between devices: 73 us -> 103 us  [from_peer(): return lax.ppermute(value, axis, [(i, i ^ distance) for i in range(peers)])]
    dot_general x8 -> x0, matrix products: 29.6 us -> none  [on_device(): lax.dot_general(act[distance][half], matching, (((0,), (0,)), ((), ())),...]
    pallas_call x2 -> x5, Pallas kernels: 23.2 us -> 39.2 us  [the longest x1 21.4 us: input_gradient(): pl.pallas_call(functools.partial(input_grad_kernel, seqs, layout), out_sh...]
    ppermute x30 -> x23, starting transfers between devices: 27.7 us -> 40.2 us  [from_peer(): return lax.ppermute(value, axis, [(i, i ^ distance) for i in range(peers)])]
    add x5 -> x0, local copies, waits for them, and re-layouts: 12.3 us -> none  [the longest x1 2.77 us: on_device(): even_c + odd_c]
    unnamed x30, local copies, waits for them, and re-layouts: 13.3 us -> 3.19 us
    add x3 -> x1, other arithmetic: 5.64 us -> 1.06 us  [on_device(): weight_grad + from_peer(leaving, 'rep', 2 * j).astype(jnp.float32)]
    slice x0 -> x4, local copies, waits for them, and re-layouts: none -> 4.45 us  [half_of(): return lax.slice_in_dim(piece[0], which * size, (which + 1) * size, axis=0)]
  transfers between devices with their start and end apart: 30 -> 23, of which waited for: 9 -> 10; matrix products, arithmetic and copies ran while one was open for 36% -> 7% of each run, Pallas kernels for 10% -> 8%
where the time goes in v2:
time: 202 us
  waiting for transfers between devices  103 us (51%)
  starting transfers between devices  40.2 us (20%)
  Pallas kernels  39.2 us (19%)
  local copies, waits for them, and re-layouts  11.2 us (6%)
  other arithmetic  6.89 us (3%)
    ppermute x23, waiting for transfers between devices, from_peer(): return lax.ppermute(value, axis, [(i, i ^ distance) for i in range(peers)])  103 us
    ppermute x23, starting transfers between devices, from_peer(): return lax.ppermute(value, axis, [(i, i ^ distance) for i in range(peers)])  40.2 us
    pallas_call x1, Pallas kernels, input_gradient(): pl.pallas_call(functools.partial(input_grad_kernel, seqs, layout), out_sh...  21.4 us
    pallas_call x1, Pallas kernels, kernel_gradient(): pl.pallas_call(functools.partial(weight_grad_kernel, layout, scale), out_...  16 us
    slice x4, local copies, waits for them, and re-layouts, half_of(): return lax.slice_in_dim(piece[0], which * size, (which + 1) * size, axis=0)  4.45 us
  transfers between devices with their start and end apart: 23, of which 10 were waited for; matrix products, arithmetic and copies ran while one was open for 7% of the time, Pallas kernels for 8%

profile of v2, /device:TPU:9, one launch (start us, length us, event | category | flops | bytes accessed | tf_op | source)
XLA Modules:
  0.0 201.5 jit_solution(13492067759577424358)
XLA Ops:
  0.6 1.4 copy-done.1
  2.0 1.8 act.1.refs_0_
  3.8 1.3 collective-permute-start
  5.1 1.2 collective-permute-start.1
  6.3 1.3 collective-permute-start.6
  7.6 2.2 %collective-permute-start.5 = (bf16[5,96,384]{2,1,0:T(8,128)(2,1)S(1)}, bf16[5,96,384]{2,1,0:T(8,128)(2,1)}, u32[]{:S(2)}, u32[]{:S(2)}) collective-permute-start(bf16[5,96,384]{2,1,0:T(8,128)(2,1)S(1)} %copy-done.7), channel_id=1, source_target_pairs={{0,2},{1,3},{2,0},{3,1},{4,6},{5,7},{6,4},{7,5},{8,10},{9,11},{10,... | collective-permute-start | bytes 1105928 | tf_op jit(solution)/shard_map/ppermute | solution.py:19
  9.8 0.5 slice_bitcast_fusion.1
  10.4 28.8 %collective-permute-done.refs_1_ = bf16[512,1536]{1,0:T(8,128)(2,1)S(1)} collective-permute-done((bf16[512,1536]{1,0:T(8,128)(2,1)S(1)}, bf16[512,1536]{1,0:T(8,128)(2,1)S(1)}, u32[]{:S(2)}, u32[]{:S(2)}) %collective-permute-start) | collective-permute-done | bytes 1572896 | tf_op jit(solution)/shard_map/ppermute | solution.py:19
  39.1 1.0 slice.64
  40.2 1.2 collective-permute-start.8
  41.4 1.0 slice.65
  42.5 1.2 collective-permute-start.9
  43.7 3.0 %fusion.2.shifts_ref = bf16[2048,1152]{1,0:T(8,128)(2,1)} fusion(bf16[2047,384]{1,0:T(8,128)(2,1)S(1)} %get-tuple-element.14, bf16[2047,384]{1,0:T(8,128)(2,1)S(1)} %get-tuple-element.13, bf16[2048,384]{1,0:T(8,128)(2,1)S(1)} %bitcast.23), kind=kLoop, calls=%fused_computation.4 | loop fusion | flops 23592960 | bytes 9435648 | tf_op jit(solution)/shard_map/concatenate | solution.py:385
  46.9 11.1 %collective-permute-done.8.refs_1_.refs_3_ = bf16[256,1536]{1,0:T(8,128)(2,1)} collective-permute-done((bf16[256,1536]{1,0:T(8,128)(2,1)}, bf16[256,1536]{1,0:T(8,128)(2,1)}, u32[]{:S(2)}, u32[]{:S(2)}) %collective-permute-start.8) | collective-permute-done | bytes 786464 | tf_op jit(solution)/shard_map/ppermute | solution.py:19
  58.0 2.0 collective-permute-done.9.refs_2_.refs_4_
  60.0 16.0 %weight_grad.1 = (f32[4,5,96,384]{3,2,1,0:T(8,128)}, bf16[4,5,96,384]{3,2,1,0:T(8,128)(2,1)}) custom-call(s32[2]{0:T(128)S(1)} %pad_add_fusion.place, bf16[2048,1152]{1,0:T(8,128)(2,1)} %fusion.2.shifts_ref, bf16[512,1536]{1,0:T(8,128)(2,1)S(1)} %act.1.refs_0_, bf16[512,1536]{1,0:T(8,128)(2,1)S(1)} %collective-permute-done.refs_1_, ...), custom_call_target="tpu_custom_call" | custom-call | flops 7247757312 | bytes 16777216 | tf_op jit(solution)/shard_map/weight_grad/pallas_call | solution.py:148
  76.0 2.8 %collective-permute-start.19 = (bf16[4,5,96,384]{3,2,1,0:T(8,128)(2,1)}, bf16[4,5,96,384]{3,2,1,0:T(8,128)(2,1)S(1)}, u32[]{:S(2)}, u32[]{:S(2)}) collective-permute-start(bf16[4,5,96,384]{3,2,1,0:T(8,128)(2,1)} %get-tuple-element.5), channel_id=1, source_target_pairs={{0,1},{1,0},{2,3},{3,2},{4,5},{5,4},{6,7},{7,6},{8,9},{9,8},{10,11... | collective-permute-start | bytes 4423688 | tf_op jit(solution)/shard_map/ppermute | solution.py:19
  78.8 2.5 %pad_maximum_fusion.refs_0_ = bf16[4,5,96,384]{3,2,1,0:T(8,128)(2,1)} fusion(bf16[1,5,96,384]{3,2,1,0:T(8,128)(2,1)} %bitcast.6, bf16[1,5,96,384]{3,2,1,0:T(8,128)(2,1)S(1)} %bitcast.26, bf16[1,5,96,384]{3,2,1,0:T(8,128)(2,1)} %bitcast.4, bf16[1,5,96,384]{3,2,1,0:T(8,128)(2,1)S(1)} %bitcast.25), kind=kLoop, calls=%fused_computation.8 | loop fusion | flops 2211840 | bytes 2949120 | tf_op jit(solution)/shard_map/stack | solution.py:371
  81.3 1.2 collective-permute-start.10
  82.4 0.3 collective-permute-start.11
  82.7 1.3 pad.6.refs_0_
  84.0 1.7 constant_dynamic-slice_fusion
  85.7 1.2 collective-permute-start.2
  86.9 0.4 collective-permute-start.3
  87.3 1.2 collective-permute-start.4
  88.4 0.3 fusion.6
  88.8 35.3 %collective-permute-done.2.refs_2_ = bf16[528,384]{1,0:T(8,128)(2,1)S(1)} collective-permute-done((bf16[528,384]{1,0:T(8,128)(2,1)S(1)}, bf16[528,384]{1,0:T(8,128)(2,1)S(1)}, u32[]{:S(2)}, u32[]{:S(2)}) %collective-permute-start.2) | collective-permute-done | bytes 405536 | tf_op jit(solution)/shard_map/ppermute | solution.py:19
  124.2 2.3 %collective-permute-start.21 = (bf16[5,96,384]{2,1,0:T(8,128)(2,1)S(1)}, bf16[5,96,384]{2,1,0:T(8,128)(2,1)S(1)}, u32[]{:S(2)}, u32[]{:S(2)}) collective-permute-start(bf16[5,96,384]{2,1,0:T(8,128)(2,1)S(1)} %get-tuple-element.8), channel_id=1, source_target_pairs={{0,4},{1,5},{2,6},{3,7},{4,0},{5,1},{6,2},{7,3},{8,12},{9,13},{10,... | collective-permute-start | bytes 1105928 | tf_op jit(solution)/shard_map/ppermute | solution.py:19
  126.5 0.2 collective-permute-start.22
  126.7 1.2 slice.66
  127.9 1.2 slice.67
  129.1 4.5 %collective-permute-done.3.refs_3_ = bf16[528,384]{1,0:T(8,128)(2,1)S(1)} collective-permute-done((bf16[528,384]{1,0:T(8,128)(2,1)S(1)}, bf16[528,384]{1,0:T(8,128)(2,1)S(1)}, u32[]{:S(2)}, u32[]{:S(2)}) %collective-permute-start.3) | collective-permute-done | bytes 405536 | tf_op jit(solution)/shard_map/ppermute | solution.py:19
  133.6 1.1 collective-permute-start.14
  134.7 0.3 collective-permute-start.12
  135.0 2.7 %collective-permute-done.20 = bf16[5,96,384]{2,1,0:T(8,128)(2,1)S(1)} collective-permute-done((bf16[5,96,384]{2,1,0:T(8,128)(2,1)S(1)}, bf16[5,96,384]{2,1,0:T(8,128)(2,1)S(1)}, u32[]{:S(2)}, u32[]{:S(2)}) %collective-permute-start.20) | collective-permute-done | bytes 368672 | tf_op jit(solution)/shard_map/ppermute | solution.py:19
  137.7 2.1 %collective-permute-start.15 = (bf16[4,5,96,384]{3,2,1,0:T(8,128)(2,1)}, bf16[4,5,96,384]{3,2,1,0:T(8,128)(2,1)S(1)}, u32[]{:S(2)}, u32[]{:S(2)}) collective-permute-start(bf16[4,5,96,384]{3,2,1,0:T(8,128)(2,1)} %collective-permute-done.10.refs_6_), channel_id=1, source_target_pairs={{0,1},{1,0},{2,3},{3,2},{4,5},{5,4},{6,7},{7,6},{8,9},{9,8},{10,11... | collective-permute-start | bytes 4423688 | tf_op jit(solution)/shard_map/ppermute | solution.py:19
  139.9 2.0 collective-permute-done.21
  141.8 11.3 %collective-permute-start.16 = (bf16[4,5,96,384]{3,2,1,0:T(8,128)(2,1)}, bf16[4,5,96,384]{3,2,1,0:T(8,128)(2,1)S(1)}, u32[]{:S(2)}, u32[]{:S(2)}) collective-permute-start(bf16[4,5,96,384]{3,2,1,0:T(8,128)(2,1)} %collective-permute-done.11.refs_7_), channel_id=1, source_target_pairs={{0,1},{1,0},{2,3},{3,2},{4,5},{5,4},{6,7},{7,6},{8,9},{9,8},{10,11... | collective-permute-start | bytes 4423688 | tf_op jit(solution)/shard_map/ppermute | solution.py:19
  153.1 4.5 %collective-permute-done.22 = bf16[5,96,384]{2,1,0:T(8,128)(2,1)S(1)} collective-permute-done((bf16[5,96,384]{2,1,0:T(8,128)(2,1)S(1)}, bf16[5,96,384]{2,1,0:T(8,128)(2,1)S(1)}, u32[]{:S(2)}, u32[]{:S(2)}) %collective-permute-start.22) | collective-permute-done | bytes 368672 | tf_op jit(solution)/shard_map/ppermute | solution.py:19
  157.6 1.2 collective-permute-start.13
  158.8 2.7 %collective-permute-start.17 = (bf16[2,5,96,384]{3,2,1,0:T(8,128)(2,1)S(1)}, bf16[2,5,96,384]{3,2,1,0:T(8,128)(2,1)S(1)}, u32[]{:S(2)}, u32[]{:S(2)}) collective-permute-start(bf16[2,5,96,384]{3,2,1,0:T(8,128)(2,1)S(1)} %collective-permute-done.12.refs_8_), channel_id=1, source_target_pairs={{0,1},{1,0},{2,3},{3,2},{4,5},{5,4},{6,7},{7,6},{8,9},{9,8},{10,11... | collective-permute-start | bytes 2211848 | tf_op jit(solution)/shard_map/ppermute | solution.py:19
  161.4 11.8 %collective-permute-done.13.refs_9_ = bf16[2,5,96,384]{3,2,1,0:T(8,128)(2,1)S(1)} collective-permute-done((bf16[2,5,96,384]{3,2,1,0:T(8,128)(2,1)S(1)}, bf16[2,5,96,384]{3,2,1,0:T(8,128)(2,1)S(1)}, u32[]{:S(2)}, u32[]{:S(2)}) %collective-permute-start.13) | collective-permute-done | bytes 737312 | tf_op jit(solution)/shard_map/ppermute | solution.py:19
  173.2 3.3 %collective-permute-start.18 = (bf16[2,5,96,384]{3,2,1,0:T(8,128)(2,1)S(1)}, bf16[2,5,96,384]{3,2,1,0:T(8,128)(2,1)S(1)}, u32[]{:S(2)}, u32[]{:S(2)}) collective-permute-start(bf16[2,5,96,384]{3,2,1,0:T(8,128)(2,1)S(1)} %collective-permute-done.13.refs_9_), channel_id=1, source_target_pairs={{0,1},{1,0},{2,3},{3,2},{4,5},{5,4},{6,7},{7,6},{8,9},{9,8},{10,11... | collective-permute-start | bytes 2211848 | tf_op jit(solution)/shard_map/ppermute | solution.py:19
  176.5 1.1 fusion.5
  177.6 0.7 collective-permute-done.18.refs_14_
  178.4 1.4 copy-done.14
  179.9 0.2 copy-done.13
  180.1 21.4 %input_grad.1 = bf16[1,1024,768]{2,1,0:T(8,128)(2,1)} custom-call(s32[2]{0:T(128)S(1)} %pad_add_fusion.place, bf16[1,1024,768]{2,1,0:T(8,128)(2,1)} %refs_0_.1, bf16[528,384]{1,0:T(8,128)(2,1)S(1)} %get-tuple-element.12.refs_1_, bf16[528,384]{1,0:T(8,128)(2,1)S(1)} %collective-permute-done.2.refs_2_, bf16[528,384]{1,0:T(8,128)(2,1)S(1)} %collective-permute-done.3.refs_3_, ...), custom_call_target="tpu_custom_call" | custom-call | flops 6228541440 | bytes 20971520 | tf_op jit(solution)/shard_map/input_grad/pallas_call | solution.py:296
  (45 shorter events, 0.6 us)
Async XLA Ops:
  0.6 1.4 copy-start.1
  2.0 4.3 %copy-start.7 = (bf16[5,96,384]{2,1,0:T(8,128)(2,1)S(1)}, bf16[5,96,384]{2,1,0:T(8,128)(2,1)}, u32[]{:S(2)}) copy-start(bf16[5,96,384]{2,1,0:T(8,128)(2,1)} %param.5) | copy-start | bytes 1105924
  2.0 7.8 %copy-start.2 = (bf16[1,2048,384]{2,1,0:T(8,128)(2,1)S(1)}, bf16[1,2048,384]{2,1,0:T(8,128)(2,1)}, u32[]{:S(2)}) copy-start(bf16[1,2048,384]{2,1,0:T(8,128)(2,1)} %param.4) | copy-start | bytes 4718596
  3.8 35.3 %collective-permute-start = (bf16[512,1536]{1,0:T(8,128)(2,1)S(1)}, bf16[512,1536]{1,0:T(8,128)(2,1)S(1)}, u32[]{:S(2)}, u32[]{:S(2)}) collective-permute-start(bf16[512,1536]{1,0:T(8,128)(2,1)S(1)} %act.1.refs_0_), channel_id=1, source_target_pairs={{0,8},{8,0},{16,24},{24,16},{1,9},{9,1},{17,25},{25,17},{2,10},{10... | collective-permute-start | bytes 4718600 | tf_op jit(solution)/shard_map/ppermute | solution.py:19
  5.1 36.3 %collective-permute-start.1 = (bf16[512,1536]{1,0:T(8,128)(2,1)S(1)}, bf16[512,1536]{1,0:T(8,128)(2,1)S(1)}, u32[]{:S(2)}, u32[]{:S(2)}) collective-permute-start(bf16[512,1536]{1,0:T(8,128)(2,1)S(1)} %act.1.refs_0_), channel_id=1, source_target_pairs={{0,16},{8,24},{16,0},{24,8},{1,17},{9,25},{17,1},{25,9},{2,18},{10... | collective-permute-start | bytes 4718600 | tf_op jit(solution)/shard_map/ppermute | solution.py:19
  6.3 40.4 %collective-permute-start.6 = (bf16[5,96,384]{2,1,0:T(8,128)(2,1)S(1)}, bf16[5,96,384]{2,1,0:T(8,128)(2,1)}, u32[]{:S(2)}, u32[]{:S(2)}) collective-permute-start(bf16[5,96,384]{2,1,0:T(8,128)(2,1)S(1)} %copy-done.7), channel_id=1, source_target_pairs={{0,6},{1,7},{2,4},{3,5},{4,2},{5,3},{6,0},{7,1},{8,14},{9,15},{10,... | collective-permute-start | bytes 1105928 | tf_op jit(solution)/shard_map/ppermute | solution.py:19
  7.6 71.2 %collective-permute-start.5 = (bf16[5,96,384]{2,1,0:T(8,128)(2,1)S(1)}, bf16[5,96,384]{2,1,0:T(8,128)(2,1)}, u32[]{:S(2)}, u32[]{:S(2)}) collective-permute-start(bf16[5,96,384]{2,1,0:T(8,128)(2,1)S(1)} %copy-done.7), channel_id=1, source_target_pairs={{0,2},{1,3},{2,0},{3,1},{4,6},{5,7},{6,4},{7,5},{8,10},{9,11},{10,... | collective-permute-start | bytes 1105928 | tf_op jit(solution)/shard_map/ppermute | solution.py:19
  39.1 20.8 %copy-start = (bf16[512,1536]{1,0:T(8,128)(2,1)}, bf16[512,1536]{1,0:T(8,128)(2,1)S(1)}, u32[]{:S(2)}) copy-start(bf16[512,1536]{1,0:T(8,128)(2,1)S(1)} %collective-permute-done.refs_1_) | copy-start | bytes 4718596
  40.2 17.8 %collective-permute-start.8 = (bf16[256,1536]{1,0:T(8,128)(2,1)}, bf16[256,1536]{1,0:T(8,128)(2,1)}, u32[]{:S(2)}, u32[]{:S(2)}) collective-permute-start(bf16[256,1536]{1,0:T(8,128)(2,1)} %slice.64), channel_id=1, source_target_pairs={{0,16},{8,24},{16,0},{24,8},{1,17},{9,25},{17,1},{25,9},{2,18},{10... | collective-permute-start | bytes 2359304 | tf_op jit(solution)/shard_map/ppermute | solution.py:19
  41.4 5.2 %copy-start.5 = (bf16[512,1536]{1,0:T(8,128)(2,1)}, bf16[512,1536]{1,0:T(8,128)(2,1)S(1)}, u32[]{:S(2)}) copy-start(bf16[512,1536]{1,0:T(8,128)(2,1)S(1)} %collective-permute-done.1.refs_2_) | copy-start | bytes 4718596
  42.5 17.5 %collective-permute-start.9 = (bf16[256,1536]{1,0:T(8,128)(2,1)}, bf16[256,1536]{1,0:T(8,128)(2,1)}, u32[]{:S(2)}, u32[]{:S(2)}) collective-permute-start(bf16[256,1536]{1,0:T(8,128)(2,1)} %slice.65), channel_id=1, source_target_pairs={{0,8},{8,0},{16,24},{24,16},{1,9},{9,1},{17,25},{25,17},{2,10},{10... | collective-permute-start | bytes 2359304 | tf_op jit(solution)/shard_map/ppermute | solution.py:19
  46.8 32.0 %collective-permute-start.7 = (bf16[5,96,384]{2,1,0:T(8,128)(2,1)}, bf16[5,96,384]{2,1,0:T(8,128)(2,1)S(1)}, u32[]{:S(2)}, u32[]{:S(2)}) collective-permute-start(bf16[5,96,384]{2,1,0:T(8,128)(2,1)} %collective-permute-done.6), channel_id=1, source_target_pairs={{0,2},{1,3},{2,0},{3,1},{4,6},{5,7},{6,4},{7,5},{8,10},{9,11},{10,... | collective-permute-start | bytes 1105928 | tf_op jit(solution)/shard_map/ppermute | solution.py:19
  76.0 11.3 %collective-permute-start.19 = (bf16[4,5,96,384]{3,2,1,0:T(8,128)(2,1)}, bf16[4,5,96,384]{3,2,1,0:T(8,128)(2,1)S(1)}, u32[]{:S(2)}, u32[]{:S(2)}) collective-permute-start(bf16[4,5,96,384]{3,2,1,0:T(8,128)(2,1)} %get-tuple-element.5), channel_id=1, source_target_pairs={{0,1},{1,0},{2,3},{3,2},{4,5},{5,4},{6,7},{7,6},{8,9},{9,8},{10,11... | collective-permute-start | bytes 4423688 | tf_op jit(solution)/shard_map/ppermute | solution.py:19
  81.3 1.4 copy-start.3
  81.3 43.0 %collective-permute-start.10 = (bf16[4,5,96,384]{3,2,1,0:T(8,128)(2,1)}, bf16[4,5,96,384]{3,2,1,0:T(8,128)(2,1)}, u32[]{:S(2)}, u32[]{:S(2)}) collective-permute-start(bf16[4,5,96,384]{3,2,1,0:T(8,128)(2,1)} %after.3.refs_5_), channel_id=1, source_target_pairs={{0,8},{8,0},{16,24},{24,16},{1,9},{9,1},{17,25},{25,17},{2,10},{10... | collective-permute-start | bytes 4423688 | tf_op jit(solution)/shard_map/ppermute | solution.py:19
  82.4 44.1 %collective-permute-start.11 = (bf16[4,5,96,384]{3,2,1,0:T(8,128)(2,1)}, bf16[4,5,96,384]{3,2,1,0:T(8,128)(2,1)}, u32[]{:S(2)}, u32[]{:S(2)}) collective-permute-start(bf16[4,5,96,384]{3,2,1,0:T(8,128)(2,1)} %after.3.refs_5_), channel_id=1, source_target_pairs={{0,16},{8,24},{16,0},{24,8},{1,17},{9,25},{17,1},{25,9},{2,18},{10... | collective-permute-start | bytes 4423688 | tf_op jit(solution)/shard_map/ppermute | solution.py:19
  84.0 4.4 %copy-start.6 = (f32[4,5,96,384]{3,2,1,0:T(8,128)S(1)}, f32[4,5,96,384]{3,2,1,0:T(8,128)}, u32[]{:S(2)}) copy-start(f32[4,5,96,384]{3,2,1,0:T(8,128)} %get-tuple-element.4) | copy-start | bytes 8847364
  85.7 38.3 %collective-permute-start.2 = (bf16[528,384]{1,0:T(8,128)(2,1)S(1)}, bf16[528,384]{1,0:T(8,128)(2,1)S(1)}, u32[]{:S(2)}, u32[]{:S(2)}) collective-permute-start(bf16[528,384]{1,0:T(8,128)(2,1)S(1)} %get-tuple-element.11), channel_id=1, source_target_pairs={{0,8},{8,0},{16,24},{24,16},{1,9},{9,1},{17,25},{25,17},{2,10},{10... | collective-permute-start | bytes 1216520 | tf_op jit(solution)/shard_map/ppermute | solution.py:19
  86.9 46.7 %collective-permute-start.3 = (bf16[528,384]{1,0:T(8,128)(2,1)S(1)}, bf16[528,384]{1,0:T(8,128)(2,1)S(1)}, u32[]{:S(2)}, u32[]{:S(2)}) collective-permute-start(bf16[528,384]{1,0:T(8,128)(2,1)S(1)} %get-tuple-element.10), channel_id=1, source_target_pairs={{0,16},{8,24},{16,0},{24,8},{1,17},{9,25},{17,1},{25,9},{2,18},{10... | collective-permute-start | bytes 1216520 | tf_op jit(solution)/shard_map/ppermute | solution.py:19
  87.3 47.4 %collective-permute-start.4 = (bf16[528,384]{1,0:T(8,128)(2,1)S(1)}, bf16[528,384]{1,0:T(8,128)(2,1)S(1)}, u32[]{:S(2)}, u32[]{:S(2)}) collective-permute-start(bf16[528,384]{1,0:T(8,128)(2,1)S(1)} %get-tuple-element.9), channel_id=1, source_target_pairs={{0,24},{8,16},{16,8},{24,0},{1,25},{9,17},{17,9},{25,1},{2,26},{10... | collective-permute-start | bytes 1216520 | tf_op jit(solution)/shard_map/ppermute | solution.py:19
  88.7 44.9 %copy-start.4 = (bf16[4,5,96,384]{3,2,1,0:T(8,128)(2,1)S(1)}, bf16[4,5,96,384]{3,2,1,0:T(8,128)(2,1)}, u32[]{:S(2)}) copy-start(bf16[4,5,96,384]{3,2,1,0:T(8,128)(2,1)} %after.3.refs_5_) | copy-start | bytes 4423684
  124.1 13.7 %collective-permute-start.20 = (bf16[5,96,384]{2,1,0:T(8,128)(2,1)S(1)}, bf16[5,96,384]{2,1,0:T(8,128)(2,1)S(1)}, u32[]{:S(2)}, u32[]{:S(2)}) collective-permute-start(bf16[5,96,384]{2,1,0:T(8,128)(2,1)S(1)} %get-tuple-element.6), channel_id=1, source_target_pairs={{0,2},{1,3},{2,0},{3,1},{4,6},{5,7},{6,4},{7,5},{8,10},{9,11},{10,... | collective-permute-start | bytes 1105928 | tf_op jit(solution)/shard_map/ppermute | solution.py:19
  124.2 17.6 %collective-permute-start.21 = (bf16[5,96,384]{2,1,0:T(8,128)(2,1)S(1)}, bf16[5,96,384]{2,1,0:T(8,128)(2,1)S(1)}, u32[]{:S(2)}, u32[]{:S(2)}) collective-permute-start(bf16[5,96,384]{2,1,0:T(8,128)(2,1)S(1)} %get-tuple-element.8), channel_id=1, source_target_pairs={{0,4},{1,5},{2,6},{3,7},{4,0},{5,1},{6,2},{7,3},{8,12},{9,13},{10,... | collective-permute-start | bytes 1105928 | tf_op jit(solution)/shard_map/ppermute | solution.py:19
  126.5 31.1 %collective-permute-start.22 = (bf16[5,96,384]{2,1,0:T(8,128)(2,1)S(1)}, bf16[5,96,384]{2,1,0:T(8,128)(2,1)S(1)}, u32[]{:S(2)}, u32[]{:S(2)}) collective-permute-start(bf16[5,96,384]{2,1,0:T(8,128)(2,1)S(1)} %get-tuple-element.7), channel_id=1, source_target_pairs={{0,6},{1,7},{2,4},{3,5},{4,2},{5,3},{6,0},{7,1},{8,14},{9,15},{10,... | collective-permute-start | bytes 1105928 | tf_op jit(solution)/shard_map/ppermute | solution.py:19
  133.6 44.0 %collective-permute-start.14 = (bf16[4,5,96,384]{3,2,1,0:T(8,128)(2,1)S(1)}, bf16[4,5,96,384]{3,2,1,0:T(8,128)(2,1)S(1)}, u32[]{:S(2)}, u32[]{:S(2)}) collective-permute-start(bf16[4,5,96,384]{3,2,1,0:T(8,128)(2,1)S(1)} %copy-done.4), channel_id=1, source_target_pairs={{0,1},{1,0},{2,3},{3,2},{4,5},{5,4},{6,7},{7,6},{8,9},{9,8},{10,11... | collective-permute-start | bytes 4423688 | tf_op jit(solution)/shard_map/ppermute | solution.py:19
  134.7 24.0 %collective-permute-start.12 = (bf16[2,5,96,384]{3,2,1,0:T(8,128)(2,1)S(1)}, bf16[2,5,96,384]{3,2,1,0:T(8,128)(2,1)S(1)}, u32[]{:S(2)}, u32[]{:S(2)}) collective-permute-start(bf16[2,5,96,384]{3,2,1,0:T(8,128)(2,1)S(1)} %slice.66), channel_id=1, source_target_pairs={{0,16},{8,24},{16,0},{24,8},{1,17},{9,25},{17,1},{25,9},{2,18},{10... | collective-permute-start | bytes 2211848 | tf_op jit(solution)/shard_map/ppermute | solution.py:19
  137.7 39.9 %collective-permute-start.15 = (bf16[4,5,96,384]{3,2,1,0:T(8,128)(2,1)}, bf16[4,5,96,384]{3,2,1,0:T(8,128)(2,1)S(1)}, u32[]{:S(2)}, u32[]{:S(2)}) collective-permute-start(bf16[4,5,96,384]{3,2,1,0:T(8,128)(2,1)} %collective-permute-done.10.refs_6_), channel_id=1, source_target_pairs={{0,1},{1,0},{2,3},{3,2},{4,5},{5,4},{6,7},{7,6},{8,9},{9,8},{10,11... | collective-permute-start | bytes 4423688 | tf_op jit(solution)/shard_map/ppermute | solution.py:19
  141.8 35.8 %collective-permute-start.16 = (bf16[4,5,96,384]{3,2,1,0:T(8,128)(2,1)}, bf16[4,5,96,384]{3,2,1,0:T(8,128)(2,1)S(1)}, u32[]{:S(2)}, u32[]{:S(2)}) collective-permute-start(bf16[4,5,96,384]{3,2,1,0:T(8,128)(2,1)} %collective-permute-done.11.refs_7_), channel_id=1, source_target_pairs={{0,1},{1,0},{2,3},{3,2},{4,5},{5,4},{6,7},{7,6},{8,9},{9,8},{10,11... | collective-permute-start | bytes 4423688 | tf_op jit(solution)/shard_map/ppermute | solution.py:19
  157.6 15.6 %collective-permute-start.13 = (bf16[2,5,96,384]{3,2,1,0:T(8,128)(2,1)S(1)}, bf16[2,5,96,384]{3,2,1,0:T(8,128)(2,1)S(1)}, u32[]{:S(2)}, u32[]{:S(2)}) collective-permute-start(bf16[2,5,96,384]{3,2,1,0:T(8,128)(2,1)S(1)} %slice.67), channel_id=1, source_target_pairs={{0,8},{8,0},{16,24},{24,16},{1,9},{9,1},{17,25},{25,17},{2,10},{10... | collective-permute-start | bytes 2211848 | tf_op jit(solution)/shard_map/ppermute | solution.py:19
  158.8 21.0 %copy-start.11 = (bf16[2,5,96,384]{3,2,1,0:T(8,128)(2,1)}, bf16[2,5,96,384]{3,2,1,0:T(8,128)(2,1)S(1)}, u32[]{:S(2)}) copy-start(bf16[2,5,96,384]{3,2,1,0:T(8,128)(2,1)S(1)} %collective-permute-done.12.refs_8_) | copy-start | bytes 2211844
  158.8 18.8 %collective-permute-start.17 = (bf16[2,5,96,384]{3,2,1,0:T(8,128)(2,1)S(1)}, bf16[2,5,96,384]{3,2,1,0:T(8,128)(2,1)S(1)}, u32[]{:S(2)}, u32[]{:S(2)}) collective-permute-start(bf16[2,5,96,384]{3,2,1,0:T(8,128)(2,1)S(1)} %collective-permute-done.12.refs_8_), channel_id=1, source_target_pairs={{0,1},{1,0},{2,3},{3,2},{4,5},{5,4},{6,7},{7,6},{8,9},{9,8},{10,11... | collective-permute-start | bytes 2211848 | tf_op jit(solution)/shard_map/ppermute | solution.py:19
  173.2 6.6 %copy-start.12 = (bf16[2,5,96,384]{3,2,1,0:T(8,128)(2,1)}, bf16[2,5,96,384]{3,2,1,0:T(8,128)(2,1)S(1)}, u32[]{:S(2)}) copy-start(bf16[2,5,96,384]{3,2,1,0:T(8,128)(2,1)S(1)} %collective-permute-done.13.refs_9_) | copy-start | bytes 2211844
  173.2 5.1 %collective-permute-start.18 = (bf16[2,5,96,384]{3,2,1,0:T(8,128)(2,1)S(1)}, bf16[2,5,96,384]{3,2,1,0:T(8,128)(2,1)S(1)}, u32[]{:S(2)}, u32[]{:S(2)}) collective-permute-start(bf16[2,5,96,384]{3,2,1,0:T(8,128)(2,1)S(1)} %collective-permute-done.13.refs_9_), channel_id=1, source_target_pairs={{0,1},{1,0},{2,3},{3,2},{4,5},{5,4},{6,7},{7,6},{8,9},{9,8},{10,11... | collective-permute-start | bytes 2211848 | tf_op jit(solution)/shard_map/ppermute | solution.py:19
  177.6 2.2 %copy-start.8 = (bf16[4,5,96,384]{3,2,1,0:T(8,128)(2,1)}, bf16[4,5,96,384]{3,2,1,0:T(8,128)(2,1)S(1)}, u32[]{:S(2)}) copy-start(bf16[4,5,96,384]{3,2,1,0:T(8,128)(2,1)S(1)} %collective-permute-done.14.refs_10_) | copy-start | bytes 4423684
  177.6 2.2 %copy-start.9 = (bf16[4,5,96,384]{3,2,1,0:T(8,128)(2,1)}, bf16[4,5,96,384]{3,2,1,0:T(8,128)(2,1)S(1)}, u32[]{:S(2)}) copy-start(bf16[4,5,96,384]{3,2,1,0:T(8,128)(2,1)S(1)} %collective-permute-done.15.refs_11_) | copy-start | bytes 4423684
  177.6 2.3 %copy-start.10 = (bf16[4,5,96,384]{3,2,1,0:T(8,128)(2,1)}, bf16[4,5,96,384]{3,2,1,0:T(8,128)(2,1)S(1)}, u32[]{:S(2)}) copy-start(bf16[4,5,96,384]{3,2,1,0:T(8,128)(2,1)S(1)} %collective-permute-done.16.refs_12_) | copy-start | bytes 4423684
  177.6 2.5 %copy-start.13 = (bf16[2,5,96,384]{3,2,1,0:T(8,128)(2,1)}, bf16[2,5,96,384]{3,2,1,0:T(8,128)(2,1)S(1)}, u32[]{:S(2)}) copy-start(bf16[2,5,96,384]{3,2,1,0:T(8,128)(2,1)S(1)} %collective-permute-done.17.refs_13_) | copy-start | bytes 2211844
  178.4 1.4 copy-start.14

commit v3 on v0

v3 whole, which is shorter than its diff:
```python
import functools
import math

import jax
import jax.numpy as jnp
from jax import lax
from jax.experimental import pallas as pl
from jax.experimental.pallas import tpu as pltpu
from jax.sharding import PartitionSpec as P

HALO = 8
LANES = 128
SPLIT = 3
ROOT = math.sqrt(2.0 / math.pi)
CUBIC = 0.044715
ANYWHERE = pl.BlockSpec(memory_space=pl.ANY)
ROW_OFFSETS = ((1, 1), (0, 1), (0, 0), (-1, 0), (-1, -1))
GRAD_PARTS = ((0, 0), (1, 0), (1, 1), (2, 1), (2, 2))


def from_peer(value, axis, distance):
    peers = lax.axis_size(axis)
    return lax.ppermute(value, axis, [(i, i ^ distance) for i in range(peers)])


def after(value, *earlier):
    return pl.pallas_call(
        lambda *refs: None,
        out_shape=jax.ShapeDtypeStruct(value.shape, value.dtype),
        in_specs=[ANYWHERE] * (1 + len(earlier)),
        out_specs=ANYWHERE,
        input_output_aliases={0: 0},
        name="after",
    )(value, *earlier)


def half_of(piece, which):
    if len(piece) == 2:
        return piece[which]
    size = piece[0].shape[0] // 2
    return lax.slice_in_dim(piece[0], which * size, (which + 1) * size, axis=0)


def gather_square(value, axis):
    found = {0: (value,)}
    near = [d for d in range(1, lax.axis_size(axis)) if d & (d - 1) == 0]
    for distance in near:
        found[distance] = (from_peer(value, axis, distance),)
    for distance in range(1, lax.axis_size(axis)):
        if distance not in near:
            high = 1 << (distance.bit_length() - 1)
            low = distance & -distance
            found[distance] = (
                from_peer(half_of(found[distance ^ high], 0), axis, high),
                from_peer(half_of(found[distance ^ low], 1), axis, low),
            )
    return found


def line_masks(count):
    masks = []
    while count > 1:
        masks.append(count - 1)
        count //= 2
    return masks


def gather_line(value, axis, count, unit):
    found = {0: value}
    for mask in line_masks(count):
        for distance in list(found):
            found[distance ^ mask] = from_peer(found[distance], axis, mask * unit)
    return [found[distance] for distance in range(count)]


def reduce_line(blocks, axis, count, unit):
    held, masks = [[0]], line_masks(count)
    for mask in masks:
        held.append(held[-1] + [d ^ mask for d in held[-1]])
    blocks = dict(enumerate(blocks))
    for mask, keep in reversed(list(zip(masks, held))):
        leaving = jnp.stack([blocks[d ^ mask].astype(jnp.bfloat16) for d in keep])
        arrived = from_peer(leaving, axis, mask * unit)
        blocks = {d: blocks[d] + arrived[n].astype(jnp.float32) for n, d in enumerate(keep)}
    return blocks[0]


def gelu_slope(x):
    tanh = jnp.tanh(ROOT * (x + CUBIC * (x * x * x)))
    return 0.5 * (1.0 + tanh) + 0.5 * x * (1.0 - tanh * tanh) * (
        ROOT * (1.0 + 3.0 * CUBIC * (x * x))
    )


def act_kernel(x_ref, out_ref, scratch):
    width = x_ref.shape[2]

    @pl.loop(0, out_ref.shape[0] // 64)
    def _(step):
        start = pl.multiple_of(step * 64, 64)
        x = x_ref[0, pl.ds(pl.multiple_of(2 * start, 128), 128), :].astype(jnp.float32)
        act = x * (0.5 * (1.0 + jnp.tanh(ROOT * (x + CUBIC * (x * x * x)))))
        for c in range(width // LANES):
            scratch[c] = act[:, c * LANES : (c + 1) * LANES]
        for parity in range(2):
            for c in range(width // LANES):
                picked = scratch[c, pl.ds(parity, 64, stride=2), :].astype(jnp.bfloat16)
                left = parity * width + c * LANES
                out_ref[pl.ds(start, 64), left : left + LANES] = picked


def activate(inputs):
    fine, width = inputs.shape[1:]
    return pl.pallas_call(
        act_kernel,
        out_shape=jax.ShapeDtypeStruct((fine // 2, 2 * width), jnp.bfloat16),
        in_specs=[pl.BlockSpec(memory_space=pltpu.VMEM)],
        out_specs=pl.BlockSpec(memory_space=pltpu.VMEM),
        scratch_shapes=[pltpu.VMEM((width // LANES, 128, LANES), jnp.float32)],
        compiler_params=pltpu.CompilerParams(vmem_limit_bytes=24 << 20),
        name="act",
    )(inputs)


def act_layout(act):
    layout, pieces = [], []
    for distance, parts in act.items():
        first = 0
        for part in parts:
            layout.append((distance, first, part.shape[0]))
            pieces.append(part)
            first += part.shape[0]
    return layout, pieces


def start_act(place, coarse, layout, pieces, shifts_ref, held, shifts, sems, shift_sems):
    copies, row = [], 0
    for i, (distance, first, size) in enumerate(layout):
        start = pl.multiple_of((place[0] ^ distance) * coarse + first, 16)
        spot = pl.ds(row, size)
        copies.append(pltpu.make_async_copy(pieces[i], held.at[spot], sems.at[i]))
        copies.append(
            pltpu.make_async_copy(shifts_ref.at[pl.ds(start, size)], shifts.at[spot], shift_sems.at[i])
        )
        row += size
    for copy in copies:
        copy.start()
    return copies


def early_terms(place, act, shifts, coarse):
    layout, pieces = act_layout(act)
    both, columns = pieces[0].shape[1], shifts.shape[1]
    rows = sum(size for _, _, size in layout)
    tile = 256

    def kernel(place, shifts_ref, *refs):
        pieces, total = refs[: len(layout)], refs[len(layout)]
        held, shifts, sems, shift_sems = refs[len(layout) + 1 :]
        copies = start_act(
            place, coarse, layout, pieces, shifts_ref, held, shifts, sems, shift_sems
        )
        for copy in copies:
            copy.wait()

        @pl.loop(0, both // tile)
        def _(i):
            span = pl.ds(pl.multiple_of(i * tile, tile), tile)
            total[span, :] = lax.dot_general(
                held[:, span], shifts[...], (((0,), (0,)), ((), ())), preferred_element_type=jnp.float32
            )

    return pl.pallas_call(
        kernel,
        out_shape=jax.ShapeDtypeStruct((both, columns), jnp.float32),
        grid_spec=pltpu.PrefetchScalarGridSpec(
            num_scalar_prefetch=1,
            grid=(1,),
            in_specs=[ANYWHERE] * (1 + len(pieces)),
            out_specs=pl.BlockSpec((both, columns), lambda i, place: (0, 0)),
            scratch_shapes=[
                pltpu.VMEM((rows, both), jnp.bfloat16),
                pltpu.VMEM((rows, columns), jnp.bfloat16),
                pltpu.SemaphoreType.DMA((len(pieces),)),
                pltpu.SemaphoreType.DMA((len(pieces),)),
            ],
        ),
        compiler_params=pltpu.CompilerParams(vmem_limit_bytes=48 << 20),
        cost_estimate=pl.CostEstimate(
            flops=2 * rows * both * columns, bytes_accessed=16 << 20, transcendentals=0
        ),
        name="weight_grad_early",
    )(place, shifts, *pieces)


def late_terms(place, act, shifts, early, coarse, scale, planes, taps, rows):
    layout, pieces = act_layout(act)
    both, columns = early.shape
    width, block = both // 2, columns // 3
    count = sum(size for _, _, size in layout)
    tile = 256
    shape = (planes, taps, rows, block)

    def kernel(place, shifts_ref, early_ref, *refs):
        pieces, (mine_ref, theirs_ref) = refs[: len(layout)], refs[len(layout) : len(layout) + 2]
        held, shifts, total, sems, shift_sems, early_sems = refs[len(layout) + 2 :]
        core, plane = place[1] % 2, place[1] // 2
        copies = start_act(
            place, coarse, layout, pieces, shifts_ref, held, shifts, sems, shift_sems
        )

        def fetch(i):
            span = pl.ds(pl.multiple_of(i * tile, tile), tile)
            return pltpu.make_async_copy(early_ref.at[span], total.at[span], early_sems.at[i])

        for i in range(both // tile):
            fetch(i).start()
        for copy in copies:
            copy.wait()

        @pl.loop(0, both // tile)
        def _(i):
            span = pl.ds(pl.multiple_of(i * tile, tile), tile)
            term = lax.dot_general(
                held[:, span], shifts[...], (((0,), (0,)), ((), ())), preferred_element_type=jnp.float32
            )
            fetch(i).wait()
            total[span, :] += term

        for out_ref, parity, kind in (
            (theirs_ref, 1 - core, jnp.bfloat16),
            (mine_ref, core, jnp.float32),
        ):

            @pl.loop(0, planes)
            def _(j):
                start = ((plane ^ j) * 2 + parity) * rows
                even = pl.ds(pl.multiple_of(start, 16), rows)
                odd = pl.ds(pl.multiple_of(width + start, 16), rows)
                for k, (left, right) in enumerate(GRAD_PARTS):
                    term = total[even, left * block : (left + 1) * block]
                    term += total[odd, right * block : (right + 1) * block]
                    out_ref[j, k] = (scale * term).astype(kind)

    whole = pl.BlockSpec(shape, lambda i, place: (0, 0, 0, 0))
    return pl.pallas_call(
        kernel,
        out_shape=(
            jax.ShapeDtypeStruct(shape, jnp.float32),
            jax.ShapeDtypeStruct(shape, jnp.bfloat16),
        ),
        grid_spec=pltpu.PrefetchScalarGridSpec(
            num_scalar_prefetch=1,
            grid=(1,),
            in_specs=[ANYWHERE] * (2 + len(pieces)),
            out_specs=[whole, whole],
            scratch_shapes=[
                pltpu.VMEM((count, both), jnp.bfloat16),
                pltpu.VMEM((count, columns), jnp.bfloat16),
                pltpu.VMEM((both, columns), jnp.float32),
                pltpu.SemaphoreType.DMA((len(pieces),)),
                pltpu.SemaphoreType.DMA((len(pieces),)),
                pltpu.SemaphoreType.DMA((both // tile,)),
            ],
        ),
        compiler_params=pltpu.CompilerParams(vmem_limit_bytes=48 << 20),
        cost_estimate=pl.CostEstimate(
            flops=2 * count * both * columns, bytes_accessed=16 << 20, transcendentals=0
        ),
        name="weight_grad_late",
    )(place, shifts, early, *pieces)


def terms_unaligned(place, act, shifts, coarse, scale, planes, taps, rows):
    both = act[0][0].shape[1]
    width, block = both // 2, shifts.shape[1] // 3
    total = jnp.zeros((both, shifts.shape[1]), jnp.float32)
    for (distance, first, size), part in zip(*act_layout(act)):
        start = (place[0] ^ distance) * coarse + first
        matching = lax.dynamic_slice_in_dim(shifts, start, size, 0)
        total = total + lax.dot_general(
            part, matching, (((0,), (0,)), ((), ())), preferred_element_type=jnp.float32
        )
    terms = []
    for left, right in GRAD_PARTS:
        even = total[:width, left * block : (left + 1) * block]
        odd = total[width:, right * block : (right + 1) * block]
        terms.append(scale * (even + odd))
    terms = jnp.stack(terms).reshape(taps, planes, 2, rows, block)
    core, plane = place[1] % 2, place[1] // 2
    outs = []
    for parity in (core, 1 - core):
        blocks = lax.dynamic_index_in_dim(terms, parity, 2, keepdims=False)
        picked = [
            lax.dynamic_index_in_dim(blocks, plane ^ j, 1, keepdims=False) for j in range(planes)
        ]
        outs.append(jnp.stack(picked))
    return outs[0], outs[1].astype(jnp.bfloat16)


def input_terms(place, grads, entries, first_tap, sums, inputs, reps):
    arrays, index = [], {}
    for array, *_ in entries:
        if id(array) not in index:
            index[id(array)] = len(arrays)
            arrays.append(array)
    distances = sorted({entry[2] for entry in entries})
    window, block = grads[0].shape
    coarse = window - 2 * HALO
    taps, rows = arrays[0].shape[1:3]
    width, depth = reps * rows, len(distances) * block
    last, begun = inputs is not None, sums is not None
    shown = width // block if last else 0
    used = list(range(len(grads))) if last else distances
    tile, step = reps // 2, 64
    operands = [grads[d] for d in used] + arrays
    if begun:
        operands.append(sums)
    if last:
        operands.append(inputs)

    def kernel(place, *refs):
        own = refs[: len(used)]
        pieces = refs[len(used) : len(used) + len(arrays)]
        refs = refs[len(used) + len(arrays) :]
        if begun:
            sums_ref, refs = refs[0], refs[1:]
        if last:
            x_ref, refs = refs[0], refs[1:]
        out_ref, refs = refs[0], refs[1:]
        wv, gv, products, sems, grad_sems = refs[:5]
        refs = refs[5:]
        if last:
            skips, fine, again, skip_sems, sum_sem, held = refs
        me, rep = place[0], place[1]
        copies, skip_copies = [], []
        for slot, distance in enumerate(distances):
            spot = pl.ds(slot * block, block)
            source = own[used.index(distance)]
            copies.append(pltpu.make_async_copy(source, gv.at[:, spot], grad_sems.at[slot]))
        for number, (array, at, distance, flip, plane) in enumerate(entries):
            spot = pl.ds(distances.index(distance) * block, block)
            owner = rep ^ flip ^ (2 * plane)
            copies.append(
                pltpu.make_async_copy(
                    pieces[index[id(array)]].at[at], wv.at[:, owner, :, spot], sems.at[number]
                )
            )
        if last:
            for slot in range(len(used)):
                copy = pltpu.make_async_copy(own[slot], skips.at[me ^ slot], skip_sems.at[slot])
                skip_copies.append(copy)
            skip_copies.append(pltpu.make_async_copy(sums_ref, held, sum_sem))
        for copy in copies + skip_copies:
            copy.start()
        for copy in copies:
            copy.wait()

        @pl.loop(0, taps)
        def _(k):
            for part in range(reps // tile):
                kernel = wv[k, part * tile : (part + 1) * tile].reshape(tile * rows, depth)
                products[k, :, part * tile * rows : (part + 1) * tile * rows] = lax.dot_general(
                    gv[...], kernel, (((1,), (1,)), ((), ())), preferred_element_type=jnp.float32
                )

        for copy in skip_copies:
            copy.wait()

        @pl.loop(0, coarse // step)
        def _(i):
            base = pl.multiple_of(i * step, step)
            spot = pl.ds(base, step)
            for c in range(width // LANES):
                lanes = slice(c * LANES, (c + 1) * LANES)
                totals = []
                for parity in range(2):
                    total = None
                    if begun:
                        total = (held if last else sums_ref)[parity, spot, lanes]
                    for by in (0, 1, -1):
                        wanted = [
                            k for k in range(taps) if ROW_OFFSETS[first_tap + k][parity] == by
                        ]
                        if not wanted:
                            continue
                        part = sum(
                            products[k, pl.ds(base, step + 2 * HALO), lanes] for k in wanted
                        )
                        part = part[HALO + by : HALO + by + step]
                        total = part if total is None else total + part
                    totals.append(total)
                if not last:
                    out_ref[0, spot, lanes], out_ref[1, spot, lanes] = totals
                    continue
                place_c = c * LANES // block, slice(c * LANES % block, c * LANES % block + LANES)
                skip = skips[place_c[0], pl.ds(base, step + 2 * HALO), place_c[1]]
                skip = skip.astype(jnp.float32)[HALO : HALO + step]
                for parity in range(2):
                    fine[c, pl.ds(parity, step, stride=2), :] = totals[parity]
                    again[c, pl.ds(parity, step, stride=2), :] = skip
                span = pl.ds(pl.multiple_of(2 * base, 2 * step), 2 * step)
                slope = gelu_slope(x_ref[0, span, lanes].astype(jnp.float32))
                out_ref[0, span, lanes] = (0.5 * (fine[c] * slope + again[c])).astype(jnp.bfloat16)

    scratch = [
        pltpu.VMEM((taps, reps, rows, depth), jnp.bfloat16),
        pltpu.VMEM((window, depth), jnp.bfloat16),
        pltpu.VMEM((taps, window, width), jnp.float32),
        pltpu.SemaphoreType.DMA((len(entries),)),
        pltpu.SemaphoreType.DMA((len(distances),)),
    ]
    in_specs = [ANYWHERE] * (len(used) + len(arrays))
    sums_shape = (2, coarse, width)
    sums_spec = pl.BlockSpec(sums_shape, lambda i, place: (0, 0, 0))
    if begun:
        in_specs.append(ANYWHERE if last else sums_spec)
    if last:
        in_specs.append(pl.BlockSpec(inputs.shape, lambda i, place: (0, 0, 0)))
        out_shape, out_spec = jax.ShapeDtypeStruct(inputs.shape, jnp.bfloat16), in_specs[-1]
        strip = pltpu.VMEM((width // LANES, 2 * step, LANES), jnp.float32)
        scratch += [
            pltpu.VMEM((len(used), window, block), jnp.bfloat16),
            strip,
            strip,
            pltpu.SemaphoreType.DMA((len(used),)),
            pltpu.SemaphoreType.DMA,
            pltpu.VMEM(sums_shape, jnp.float32),
        ]
    else:
        out_shape, out_spec = jax.ShapeDtypeStruct(sums_shape, jnp.float32), sums_spec
    return pl.pallas_call(
        kernel,
        out_shape=out_shape,
        grid_spec=pltpu.PrefetchScalarGridSpec(
            num_scalar_prefetch=1,
            grid=(1,),
            in_specs=in_specs,
            out_specs=out_spec,
            scratch_shapes=scratch,
        ),
        compiler_params=pltpu.CompilerParams(vmem_limit_bytes=52 << 20),
        cost_estimate=pl.CostEstimate(
            flops=2 * taps * window * width * depth,
            bytes_accessed=20 << 20,
            transcendentals=0,
        ),
        name="input_grad_late" if last else "input_grad_early",
    )(place, *operands)


def input_gradient_unaligned(place, inputs, grads, parts, taps, reps):
    seqs = len(grads)
    window, block = grads[0].shape
    coarse, width = window - 2 * HALO, inputs.shape[2]
    rows = width // reps
    grad = jnp.zeros((window, seqs * block), jnp.bfloat16)
    for distance in range(seqs):
        spot = (0, (place[0] ^ distance) * block)
        grad = lax.dynamic_update_slice(grad, grads[distance], spot)
    kernel = jnp.zeros((taps, width, seqs * block), jnp.bfloat16)
    for first_tap, entries in parts:
        for array, at, distance, flip, plane in entries:
            owner = place[1] ^ flip ^ (2 * plane)
            spot = (first_tap, owner * rows, (place[0] ^ distance) * block)
            kernel = lax.dynamic_update_slice(kernel, array[at], spot)
    products = lax.dot_general(
        grad, kernel, (((1,), (2,)), ((), ())), preferred_element_type=jnp.float32
    )
    totals = []
    for parity in range(2):
        total = 0.0
        for k in range(taps):
            start = HALO + ROW_OFFSETS[k][parity]
            total = total + products[start : start + coarse, k]
        totals.append(total)
    total = jnp.stack(totals, axis=1).reshape(inputs.shape[1:])
    slope = gelu_slope(inputs[0].astype(jnp.float32))
    skip = jnp.repeat(grad[HALO : HALO + coarse, :width].astype(jnp.float32), 2, axis=0)
    return (0.5 * (total * slope + skip)).astype(jnp.bfloat16)[None]


def on_device(inputs, trunk_grad, weights):
    seqs, reps = lax.axis_size("seq"), lax.axis_size("rep")
    me, rep = lax.axis_index("seq"), lax.axis_index("rep")
    place = jnp.stack([me, rep]).astype(jnp.int32)
    taps, rows, block = weights.shape
    fine, width = inputs.shape[1:]
    coarse, planes = fine // 2, reps // 2
    aligned = block % LANES == 0

    last_taps = weights[SPLIT:]
    across = jnp.stack(
        [last_taps] + [from_peer(last_taps, "seq", d) for d in range(1, seqs)]
    )
    act = gather_square(activate(inputs), "seq")
    near = [act[d][0] for d in act if len(act[d]) == 1 and d]
    far = [part for d in act if len(act[d]) == 2 for part in act[d]]
    first_columns = jnp.stack(gather_line(weights[:SPLIT], "rep", planes, 2))
    lines = gather_line(across, "rep", planes, 2)
    other_lines = [from_peer(line, "rep", 1) for line in lines]
    last_entries = [
        (line, distance, distance, flip, plane)
        for flip, found in enumerate((lines, other_lines))
        for plane, line in enumerate(found)
        for distance in range(seqs)
    ]

    trunk = trunk_grad[0]
    edged = after(jnp.pad(trunk, ((HALO, HALO), (0, 0))), *near)
    grads = []
    for distance in range(seqs):
        window = lax.dynamic_slice_in_dim(edged, (me ^ distance) * coarse, coarse + 2 * HALO, 0)
        grads.append(from_peer(window, "seq", distance) if distance else window)

    kept = gather_square(after(first_columns, *far), "seq")
    swapped = {d: tuple(from_peer(part, "rep", 1) for part in kept[d]) for d in kept}
    first_entries = []
    for flip, found in enumerate((kept, swapped)):
        for distance, parts in found.items():
            plane = 0
            for part in parts:
                for at in range(part.shape[0]):
                    first_entries.append((part, at, distance, flip, plane))
                    plane += 1

    zeros = jnp.zeros((1, block), jnp.bfloat16)
    later = jnp.concatenate([trunk[1:], zeros])
    earlier = jnp.concatenate([zeros, trunk[:-1]])
    shifts = jnp.concatenate([later, trunk, earlier], axis=1)
    scale = 0.5 * float(fine * seqs * reps) ** (-0.5)
    if aligned:
        soon = {d: act[d] for d in act if len(act[d]) == 1}
        rest = {d: act[d] for d in act if len(act[d]) == 2}
        early = early_terms(place, soon, shifts, coarse)
        mine, theirs = late_terms(place, rest, shifts, early, coarse, scale, planes, taps, rows)
    else:
        mine, theirs = terms_unaligned(place, act, shifts, coarse, scale, planes, taps, rows)
    arrived = from_peer(theirs, "rep", 1)
    summed = [mine[j] + arrived[j].astype(jnp.float32) for j in range(planes)]
    weight_grad = reduce_line(summed, "rep", planes, 2)

    if aligned:
        soon = [entry for entry in first_entries if len(kept[entry[2]]) == 1]
        rest = [entry for entry in first_entries if len(kept[entry[2]]) == 2]
        sums = input_terms(place, grads, last_entries, SPLIT, None, None, reps)
        sums = input_terms(place, grads, soon, 0, sums, None, reps)
        input_grad = input_terms(place, grads, rest, 0, sums, inputs, reps)
    else:
        parts = ((0, first_entries), (SPLIT, last_entries))
        input_grad = input_gradient_unaligned(place, inputs, grads, parts, taps, reps)
    return (input_grad, weight_grad)


def solution(mesh):
    in_specs = (P("rep", "seq", None), P("rep", None, "seq"), P(None, "rep", "seq"))
    out_specs = (P("rep", "seq", None), P(None, "rep", "seq"))
    return jax.shard_map(
        on_device, mesh=mesh, in_specs=in_specs, out_specs=out_specs, check_vma=False
    )
```

time: 512 us -> 229 us (0.45)
  waiting for transfers between devices: 365 us -> 103 us
  Pallas kernels: 0 us -> 56.2 us
  matrix products: 43 us -> 0 us
  other arithmetic: 44.3 us -> 12.5 us
  starting transfers between devices: 9.97 us -> 38 us
  between operations: 15.7 us -> 0.94 us
  local copies, waits for them, and re-layouts: 29.9 us -> 15.7 us
    reduce_scatter x2 -> x0, waiting for transfers between devices: 233 us -> none  [the longest x1 233 us: on_device(): lax.psum_scatter(terms, 'rep', scatter_dimension=1, tiled=True)]
    all_gather x2 -> x0, waiting for transfers between devices: 109 us -> none  [the longest x1 109 us: on_device(): piece = lax.all_gather(columns, 'rep', axis=1, tiled=True)]
    ppermute x2 -> x32, waiting for transfers between devices: 0.01 us -> 103 us  [from_peer(): return lax.ppermute(value, axis, [(i, i ^ distance) for i in range(peers)])]
    pallas_call x0 -> x8, Pallas kernels: none -> 56.2 us  [the longest x3 31.8 us: input_terms(): pl.pallas_call(kernel, out_shape=out_shape, grid_spec=pltpu.PrefetchScala...]
    dot_general x10 -> x0, matrix products: 43 us -> none  [the longest x5 23.3 us: contract_last(): lax.dot_general(left, right, (((1,), (1,)), ((), ())), preferred_element_...]
    unnamed x1 -> x0, other arithmetic: 34.4 us -> none
    ppermute x2 -> x32, starting transfers between devices: 5.45 us -> 38 us  [from_peer(): return lax.ppermute(value, axis, [(i, i ^ distance) for i in range(peers)])]
    all_to_all x1 -> x0, waiting for transfers between devices: 21.8 us -> none  [on_device(): lax.all_to_all(trunk_grad, 'seq', split_axis=1, concat_axis=2, tiled=True)]
  transfers between devices with their start and end apart: 7 -> 32, of which waited for: 3 -> 8; matrix products, arithmetic and copies ran while one was open for 14% -> 9% of each run, Pallas kernels for 0% -> 24%
where the time goes in v3:
time: 229 us; the launch traced here: 227 us
  waiting for transfers between devices  103 us (45%)
  Pallas kernels  56.2 us (25%)
  starting transfers between devices  38 us (17%)
  local copies, waits for them, and re-layouts  15.7 us (7%)
  other arithmetic  12.5 us (5%)
    ppermute x32, waiting for transfers between devices, from_peer(): return lax.ppermute(value, axis, [(i, i ^ distance) for i in range(peers)])  103 us
    ppermute x32, starting transfers between devices, from_peer(): return lax.ppermute(value, axis, [(i, i ^ distance) for i in range(peers)])  38 us
    pallas_call x3, Pallas kernels, input_terms(): pl.pallas_call(kernel, out_shape=out_shape, grid_spec=pltpu.PrefetchScala...  31.8 us
    pallas_call x1, Pallas kernels, early_terms(): pl.pallas_call(kernel, out_shape=jax.ShapeDtypeStruct((both, columns), jn...  12.9 us
    pallas_call x1, Pallas kernels, late_terms(): pl.pallas_call(kernel, out_shape=(jax.ShapeDtypeStruct(shape, jnp.float32...  9.69 us
    unnamed x38, local copies, waits for them, and re-layouts  6.23 us
  transfers between devices with their start and end apart: 32, of which 8 were waited for; matrix products, arithmetic and copies ran while one was open for 9% of the time, Pallas kernels for 24%

profile of v3, /device:TPU:9, one launch (start us, length us, event | category | flops | bytes accessed | tf_op | source)
XLA Modules:
  0.0 226.8 jit_solution(2609156760570446538)
XLA Ops:
  0.6 1.4 copy-done
  2.0 1.8 act.1.refs_0_
  3.8 1.3 collective-permute-start
  5.1 1.2 collective-permute-start.1
  6.3 1.6 slice_bitcast_fusion.2
  8.1 1.2 collective-permute-start.19
  9.3 1.2 collective-permute-start.20
  11.1 28.0 %collective-permute-done.refs_1_ = bf16[512,1536]{1,0:T(8,128)(2,1)S(1)} collective-permute-done((bf16[512,1536]{1,0:T(8,128)(2,1)S(1)}, bf16[512,1536]{1,0:T(8,128)(2,1)S(1)}, u32[]{:S(2)}, u32[]{:S(2)}) %collective-permute-start) | collective-permute-done | bytes 1572896 | tf_op jit(solution)/shard_map/ppermute | solution.py:23
  39.2 1.0 slice.80
  40.2 1.2 collective-permute-start.8
  41.4 1.0 slice.81
  42.5 1.2 collective-permute-start.9
  43.7 3.0 %fusion.2.shifts_ref = bf16[2048,1152]{1,0:T(8,128)(2,1)} fusion(bf16[2047,384]{1,0:T(8,128)(2,1)S(1)} %get-tuple-element.13, bf16[2047,384]{1,0:T(8,128)(2,1)S(1)} %get-tuple-element.12, bf16[2048,384]{1,0:T(8,128)(2,1)S(1)} %bitcast.20), kind=kLoop, calls=%fused_computation.4 | loop fusion | flops 23592960 | bytes 9435648 | tf_op jit(solution)/shard_map/concatenate | solution.py:530
  46.7 1.9 pad_maximum_fusion.2.refs_4_
  48.6 1.3 collective-permute-start.23
  49.9 1.4 copy-done.4
  51.3 12.9 %weight_grad_early.1.early_ref = f32[1536,1152]{1,0:T(8,128)} custom-call(s32[2]{0:T(128)S(1)} %pad_add_fusion.place, bf16[2048,1152]{1,0:T(8,128)(2,1)} %fusion.2.shifts_ref, bf16[512,1536]{1,0:T(8,128)(2,1)S(1)} %copy-done.4, bf16[512,1536]{1,0:T(8,128)(2,1)S(1)} %collective-permute-done.refs_1_, bf16[512,1536]{1,0:T(8,128)(2,1)S(1)} %collective-permute-done.1.refs_2_), custom_call_target="tpu_custom_call" | custom-call | flops 5435817984 | bytes 16777216 | tf_op jit(solution)/shard_map/weight_grad_early/pallas_call | solution.py:173
  64.3 9.7 %weight_grad_late.1 = (f32[4,5,96,384]{3,2,1,0:T(8,128)S(1)}, bf16[4,5,96,384]{3,2,1,0:T(8,128)(2,1)}) custom-call(s32[2]{0:T(128)S(1)} %pad_add_fusion.place, bf16[2048,1152]{1,0:T(8,128)(2,1)} %fusion.2.shifts_ref, f32[1536,1152]{1,0:T(8,128)} %weight_grad_early.1.early_ref, bf16[256,1536]{1,0:T(8,128)(2,1)} %collective-permute-done.8.refs_1_.refs_0_, ...), custom_call_target="tpu_custom_call" | custom-call | flops 1811939328 | bytes 16777216 | tf_op jit(solution)/shard_map/weight_grad_late/pallas_call | solution.py:246
  74.0 4.4 %collective-permute-start.29 = (bf16[4,5,96,384]{3,2,1,0:T(8,128)(2,1)}, bf16[4,5,96,384]{3,2,1,0:T(8,128)(2,1)}, u32[]{:S(2)}, u32[]{:S(2)}) collective-permute-start(bf16[4,5,96,384]{3,2,1,0:T(8,128)(2,1)} %get-tuple-element.5), channel_id=1, source_target_pairs={{0,1},{1,0},{2,3},{3,2},{4,5},{5,4},{6,7},{7,6},{8,9},{9,8},{10,11... | collective-permute-start | bytes 4423688 | tf_op jit(solution)/shard_map/ppermute | solution.py:23
  78.4 2.2 collective-permute-start.22
  80.7 1.5 collective-permute-start.5
  82.2 5.1 %collective-permute-done.6 = bf16[3,96,384]{2,1,0:T(8,128)(2,1)} collective-permute-done((bf16[3,96,384]{2,1,0:T(8,128)(2,1)S(1)}, bf16[3,96,384]{2,1,0:T(8,128)(2,1)}, u32[]{:S(2)}, u32[]{:S(2)}) %collective-permute-start.6) | collective-permute-done | bytes 221216 | tf_op jit(solution)/shard_map/ppermute | solution.py:23
  87.4 1.3 collective-permute-start.25
  88.6 28.0 %collective-permute-done.5 = bf16[3,96,384]{2,1,0:T(8,128)(2,1)} collective-permute-done((bf16[3,96,384]{2,1,0:T(8,128)(2,1)S(1)}, bf16[3,96,384]{2,1,0:T(8,128)(2,1)}, u32[]{:S(2)}, u32[]{:S(2)}) %collective-permute-start.5) | collective-permute-done | bytes 221216 | tf_op jit(solution)/shard_map/ppermute | solution.py:23
  116.6 1.3 collective-permute-start.7
  117.9 5.3 %collective-permute-done.7 = bf16[3,96,384]{2,1,0:T(8,128)(2,1)} collective-permute-done((bf16[3,96,384]{2,1,0:T(8,128)(2,1)}, bf16[3,96,384]{2,1,0:T(8,128)(2,1)}, u32[]{:S(2)}, u32[]{:S(2)}) %collective-permute-start.7) | collective-permute-done | bytes 221216 | tf_op jit(solution)/shard_map/ppermute | solution.py:23
  123.2 1.5 collective-permute-start.28
  124.8 2.8 %pad.6.refs_0_ = bf16[2064,384]{1,0:T(8,128)(2,1)} pad(bf16[2048,384]{1,0:T(8,128)(2,1)} %bitcast.19, bf16[]{:T(256)} %constant.5.clone.1), padding=8_8x0_0 | pad | bytes 3158018 | tf_op jit(solution)/shard_map/jit(_pad)/pad | solution.py:510
  128.0 2.2 pad_maximum_fusion.refs_0_
  130.2 2.4 %constant_dynamic-slice_fusion = (bf16[528,384]{1,0:T(8,128)(2,1)}, bf16[528,384]{1,0:T(8,128)(2,1)}, bf16[528,384]{1,0:T(8,128)(2,1)}, bf16[528,384]{1,0:T(8,128)(2,1)S(1)}) fusion(bf16[2064,384]{1,0:T(8,128)(2,1)} %after.2, s32[]{:T(128)S(6)} %select_n.15, s32[]{:T(128)S(6)} %select_n.14, s32[]{:T(128)S(6)} %select_n.13, s32[]{:T(128)S(6)} %select_n.12), kind=kLoop, calls=%fused_computation.15 | loop fusion | bytes 3244048 | tf_op jit(solution)/shard_map/dynamic_slice | solution.py:513
  132.7 1.7 collective-permute-start.10
  134.4 1.2 collective-permute-start.12
  135.6 1.3 add_convert_fusion.2
  137.7 1.4 collective-permute-start.30
  139.1 24.1 %collective-permute-done.2.refs_1_ = bf16[528,384]{1,0:T(8,128)(2,1)S(1)} collective-permute-done((bf16[528,384]{1,0:T(8,128)(2,1)S(1)}, bf16[528,384]{1,0:T(8,128)(2,1)S(1)}, u32[]{:S(2)}, u32[]{:S(2)}) %collective-permute-start.2) | collective-permute-done | bytes 405536 | tf_op jit(solution)/shard_map/ppermute | solution.py:23
  164.3 2.1 collective-permute-start.4
  167.0 7.9 %collective-permute-done.4.refs_3_ = bf16[528,384]{1,0:T(8,128)(2,1)S(1)} collective-permute-done((bf16[528,384]{1,0:T(8,128)(2,1)S(1)}, bf16[528,384]{1,0:T(8,128)(2,1)S(1)}, u32[]{:S(2)}, u32[]{:S(2)}) %collective-permute-start.4) | collective-permute-done | bytes 405536 | tf_op jit(solution)/shard_map/ppermute | solution.py:23
  174.9 1.2 collective-permute-start.11
  176.2 2.1 collective-permute-start.13
  178.3 1.9 add_convert_fusion
  180.2 4.5 %collective-permute-done.11.refs_4_ = bf16[2,3,96,384]{3,2,1,0:T(8,128)(2,1)} collective-permute-done((bf16[2,3,96,384]{3,2,1,0:T(8,128)(2,1)S(1)}, bf16[2,3,96,384]{3,2,1,0:T(8,128)(2,1)}, u32[]{:S(2)}, u32[]{:S(2)}) %collective-permute-start.11) | collective-permute-done | bytes 442400 | tf_op jit(solution)/shard_map/ppermute | solution.py:23
  184.7 2.9 %collective-permute-start.14 = (bf16[2,3,96,384]{3,2,1,0:T(8,128)(2,1)}, bf16[2,3,96,384]{3,2,1,0:T(8,128)(2,1)S(1)}, u32[]{:S(2)}, u32[]{:S(2)}) collective-permute-start(bf16[2,3,96,384]{3,2,1,0:T(8,128)(2,1)} %collective-permute-done.11.refs_4_), channel_id=1, source_target_pairs={{0,1},{1,0},{2,3},{3,2},{4,5},{5,4},{6,7},{7,6},{8,9},{9,8},{10,11... | collective-permute-start | bytes 1327112 | tf_op jit(solution)/shard_map/ppermute | solution.py:23
  187.6 1.8 collective-permute-start.15
  189.4 9.2 %input_grad_early.2.refs_9_ = f32[2,512,768]{2,1,0:T(8,128)} custom-call(s32[2]{0:T(128)S(1)} %pad_add_fusion.place, bf16[528,384]{1,0:T(8,128)(2,1)S(1)} %get-tuple-element.11.refs_0_, bf16[528,384]{1,0:T(8,128)(2,1)S(1)} %collective-permute-done.2.refs_1_, bf16[528,384]{1,0:T(8,128)(2,1)S(1)} %collective-permute-done.3.refs_2_, ...), custom_call_target="tpu_custom_call" | custom-call | flops 2491416576 | bytes 20971520 | tf_op jit(solution)/shard_map/input_grad_early/pallas_call | solution.py:432
  199.5 1.0 copy-done.11
  200.5 12.4 %input_grad_early.3.refs_8_ = f32[2,512,768]{2,1,0:T(8,128)} custom-call(s32[2]{0:T(128)S(1)} %pad_add_fusion.place, bf16[528,384]{1,0:T(8,128)(2,1)S(1)} %get-tuple-element.11.refs_0_, bf16[528,384]{1,0:T(8,128)(2,1)S(1)} %collective-permute-done.2.refs_1_, bf16[528,384]{1,0:T(8,128)(2,1)S(1)} %collective-permute-done.3.refs_2_, ...), custom_call_target="tpu_custom_call" | custom-call | flops 2802843648 | bytes 20971520 | tf_op jit(solution)/shard_map/input_grad_early/pallas_call | solution.py:432
  214.4 10.3 %input_grad_late.1 = bf16[1,1024,768]{2,1,0:T(8,128)(2,1)} custom-call(s32[2]{0:T(128)S(1)} %pad_add_fusion.place, bf16[528,384]{1,0:T(8,128)(2,1)S(1)} %get-tuple-element.11.refs_0_, bf16[528,384]{1,0:T(8,128)(2,1)S(1)} %collective-permute-done.2.refs_1_, bf16[528,384]{1,0:T(8,128)(2,1)S(1)} %collective-permute-done.3.refs_2_, ...), custom_call_target="tpu_custom_call" | custom-call | flops 934281216 | bytes 20971520 | tf_op jit(solution)/shard_map/input_grad_late/pallas_call | solution.py:432
  224.7 2.0 add_bitcast_fusion
  (79 shorter events, 6.4 us)
Async XLA Ops:
  0.6 1.4 copy-start
  2.0 8.6 %copy-start.5 = (bf16[1,2048,384]{2,1,0:T(8,128)(2,1)S(1)}, bf16[1,2048,384]{2,1,0:T(8,128)(2,1)}, u32[]{:S(2)}) copy-start(bf16[1,2048,384]{2,1,0:T(8,128)(2,1)} %param.4) | copy-start | bytes 4718596
  3.8 7.3 %copy-start.3 = (bf16[512,1536]{1,0:T(8,128)(2,1)}, bf16[512,1536]{1,0:T(8,128)(2,1)S(1)}, u32[]{:S(2)}) copy-start(bf16[512,1536]{1,0:T(8,128)(2,1)S(1)} %act.1.refs_0_) | copy-start | bytes 4718596
  3.8 35.3 %collective-permute-start = (bf16[512,1536]{1,0:T(8,128)(2,1)S(1)}, bf16[512,1536]{1,0:T(8,128)(2,1)S(1)}, u32[]{:S(2)}, u32[]{:S(2)}) collective-permute-start(bf16[512,1536]{1,0:T(8,128)(2,1)S(1)} %act.1.refs_0_), channel_id=1, source_target_pairs={{0,8},{8,0},{16,24},{24,16},{1,9},{9,1},{17,25},{25,17},{2,10},{10... | collective-permute-start | bytes 4718600 | tf_op jit(solution)/shard_map/ppermute | solution.py:23
  5.1 36.3 %collective-permute-start.1 = (bf16[512,1536]{1,0:T(8,128)(2,1)S(1)}, bf16[512,1536]{1,0:T(8,128)(2,1)S(1)}, u32[]{:S(2)}, u32[]{:S(2)}) collective-permute-start(bf16[512,1536]{1,0:T(8,128)(2,1)S(1)} %act.1.refs_0_), channel_id=1, source_target_pairs={{0,16},{8,24},{16,0},{24,8},{1,17},{9,25},{17,1},{25,9},{2,18},{10... | collective-permute-start | bytes 4718600 | tf_op jit(solution)/shard_map/ppermute | solution.py:23
  7.9 38.8 %collective-permute-start.21 = (bf16[2,96,384]{2,1,0:T(8,128)(2,1)}, bf16[2,96,384]{2,1,0:T(8,128)(2,1)S(1)}, u32[]{:S(2)}, u32[]{:S(2)}) collective-permute-start(bf16[2,96,384]{2,1,0:T(8,128)(2,1)} %get-tuple-element.15), channel_id=1, source_target_pairs={{0,24},{8,16},{16,8},{24,0},{1,25},{9,17},{17,9},{25,1},{2,26},{10... | collective-permute-start | bytes 442376 | tf_op jit(solution)/shard_map/ppermute | solution.py:23
  8.1 38.6 %collective-permute-start.19 = (bf16[2,96,384]{2,1,0:T(8,128)(2,1)}, bf16[2,96,384]{2,1,0:T(8,128)(2,1)}, u32[]{:S(2)}, u32[]{:S(2)}) collective-permute-start(bf16[2,96,384]{2,1,0:T(8,128)(2,1)} %get-tuple-element.15), channel_id=1, source_target_pairs={{0,8},{8,0},{16,24},{24,16},{1,9},{9,1},{17,25},{25,17},{2,10},{10... | collective-permute-start | bytes 442376 | tf_op jit(solution)/shard_map/ppermute | solution.py:23
  9.3 37.4 %collective-permute-start.20 = (bf16[2,96,384]{2,1,0:T(8,128)(2,1)}, bf16[2,96,384]{2,1,0:T(8,128)(2,1)}, u32[]{:S(2)}, u32[]{:S(2)}) collective-permute-start(bf16[2,96,384]{2,1,0:T(8,128)(2,1)} %get-tuple-element.15), channel_id=1, source_target_pairs={{0,16},{8,24},{16,0},{24,8},{1,17},{9,25},{17,1},{25,9},{2,18},{10... | collective-permute-start | bytes 442376 | tf_op jit(solution)/shard_map/ppermute | solution.py:23
  39.2 10.7 %copy-start.1 = (bf16[512,1536]{1,0:T(8,128)(2,1)}, bf16[512,1536]{1,0:T(8,128)(2,1)S(1)}, u32[]{:S(2)}) copy-start(bf16[512,1536]{1,0:T(8,128)(2,1)S(1)} %collective-permute-done.refs_1_) | copy-start | bytes 4718596
  40.2 24.1 %collective-permute-start.8 = (bf16[256,1536]{1,0:T(8,128)(2,1)}, bf16[256,1536]{1,0:T(8,128)(2,1)}, u32[]{:S(2)}, u32[]{:S(2)}) collective-permute-start(bf16[256,1536]{1,0:T(8,128)(2,1)} %slice.80), channel_id=1, source_target_pairs={{0,16},{8,24},{16,0},{24,8},{1,17},{9,25},{17,1},{25,9},{2,18},{10... | collective-permute-start | bytes 2359304 | tf_op jit(solution)/shard_map/ppermute | solution.py:23
  41.4 8.5 %copy-start.2 = (bf16[512,1536]{1,0:T(8,128)(2,1)}, bf16[512,1536]{1,0:T(8,128)(2,1)S(1)}, u32[]{:S(2)}) copy-start(bf16[512,1536]{1,0:T(8,128)(2,1)S(1)} %collective-permute-done.1.refs_2_) | copy-start | bytes 4718596
  42.5 21.8 %collective-permute-start.9 = (bf16[256,1536]{1,0:T(8,128)(2,1)}, bf16[256,1536]{1,0:T(8,128)(2,1)}, u32[]{:S(2)}, u32[]{:S(2)}) collective-permute-start(bf16[256,1536]{1,0:T(8,128)(2,1)} %slice.81), channel_id=1, source_target_pairs={{0,8},{8,0},{16,24},{24,16},{1,9},{9,1},{17,25},{25,17},{2,10},{10... | collective-permute-start | bytes 2359304 | tf_op jit(solution)/shard_map/ppermute | solution.py:23
  48.6 32.0 %collective-permute-start.23 = (bf16[4,2,96,384]{3,2,1,0:T(8,128)(2,1)}, bf16[4,2,96,384]{3,2,1,0:T(8,128)(2,1)}, u32[]{:S(2)}, u32[]{:S(2)}) collective-permute-start(bf16[4,2,96,384]{3,2,1,0:T(8,128)(2,1)} %pad_maximum_fusion.2.refs_4_), channel_id=1, source_target_pairs={{0,6},{1,7},{2,4},{3,5},{4,2},{5,3},{6,0},{7,1},{8,14},{9,15},{10,... | collective-permute-start | bytes 1769480 | tf_op jit(solution)/shard_map/ppermute | solution.py:23
  49.9 1.4 copy-start.4
  64.3 16.3 %copy-start.18 = (bf16[5,96,384]{2,1,0:T(8,128)(2,1)S(1)}, bf16[5,96,384]{2,1,0:T(8,128)(2,1)}, u32[]{:S(2)}) copy-start(bf16[5,96,384]{2,1,0:T(8,128)(2,1)} %param.5) | copy-start | bytes 1105924
  74.0 60.4 %collective-permute-start.29 = (bf16[4,5,96,384]{3,2,1,0:T(8,128)(2,1)}, bf16[4,5,96,384]{3,2,1,0:T(8,128)(2,1)}, u32[]{:S(2)}, u32[]{:S(2)}) collective-permute-start(bf16[4,5,96,384]{3,2,1,0:T(8,128)(2,1)} %get-tuple-element.5), channel_id=1, source_target_pairs={{0,1},{1,0},{2,3},{3,2},{4,5},{5,4},{6,7},{7,6},{8,9},{9,8},{10,11... | collective-permute-start | bytes 4423688 | tf_op jit(solution)/shard_map/ppermute | solution.py:23
  78.4 46.4 %collective-permute-start.22 = (bf16[4,2,96,384]{3,2,1,0:T(8,128)(2,1)}, bf16[4,2,96,384]{3,2,1,0:T(8,128)(2,1)}, u32[]{:S(2)}, u32[]{:S(2)}) collective-permute-start(bf16[4,2,96,384]{3,2,1,0:T(8,128)(2,1)} %pad_maximum_fusion.2.refs_4_), channel_id=1, source_target_pairs={{0,2},{1,3},{2,0},{3,1},{4,6},{5,7},{6,4},{7,5},{8,10},{9,11},{10,... | collective-permute-start | bytes 1769480 | tf_op jit(solution)/shard_map/ppermute | solution.py:23
  80.6 47.0 %collective-permute-start.24 = (bf16[4,2,96,384]{3,2,1,0:T(8,128)(2,1)}, bf16[4,2,96,384]{3,2,1,0:T(8,128)(2,1)}, u32[]{:S(2)}, u32[]{:S(2)}) collective-permute-start(bf16[4,2,96,384]{3,2,1,0:T(8,128)(2,1)} %collective-permute-done.23.refs_7_), channel_id=1, source_target_pairs={{0,2},{1,3},{2,0},{3,1},{4,6},{5,7},{6,4},{7,5},{8,10},{9,11},{10,... | collective-permute-start | bytes 1769480 | tf_op jit(solution)/shard_map/ppermute | solution.py:23
  80.6 6.7 %collective-permute-start.6 = (bf16[3,96,384]{2,1,0:T(8,128)(2,1)S(1)}, bf16[3,96,384]{2,1,0:T(8,128)(2,1)}, u32[]{:S(2)}, u32[]{:S(2)}) collective-permute-start(bf16[3,96,384]{2,1,0:T(8,128)(2,1)S(1)} %get-tuple-element.17), channel_id=1, source_target_pairs={{0,6},{1,7},{2,4},{3,5},{4,2},{5,3},{6,0},{7,1},{8,14},{9,15},{10,... | collective-permute-start | bytes 663560 | tf_op jit(solution)/shard_map/ppermute | solution.py:23
  80.7 35.9 %collective-permute-start.5 = (bf16[3,96,384]{2,1,0:T(8,128)(2,1)S(1)}, bf16[3,96,384]{2,1,0:T(8,128)(2,1)}, u32[]{:S(2)}, u32[]{:S(2)}) collective-permute-start(bf16[3,96,384]{2,1,0:T(8,128)(2,1)S(1)} %get-tuple-element.17), channel_id=1, source_target_pairs={{0,2},{1,3},{2,0},{3,1},{4,6},{5,7},{6,4},{7,5},{8,10},{9,11},{10,... | collective-permute-start | bytes 663560 | tf_op jit(solution)/shard_map/ppermute | solution.py:23
  87.4 45.3 %collective-permute-start.25 = (bf16[4,2,96,384]{3,2,1,0:T(8,128)(2,1)}, bf16[4,2,96,384]{3,2,1,0:T(8,128)(2,1)}, u32[]{:S(2)}, u32[]{:S(2)}) collective-permute-start(bf16[4,2,96,384]{3,2,1,0:T(8,128)(2,1)} %pad_maximum_fusion.2.refs_4_), channel_id=1, source_target_pairs={{0,1},{1,0},{2,3},{3,2},{4,5},{5,4},{6,7},{7,6},{8,9},{9,8},{10,11... | collective-permute-start | bytes 1769480 | tf_op jit(solution)/shard_map/ppermute | solution.py:23
  116.6 6.6 %collective-permute-start.7 = (bf16[3,96,384]{2,1,0:T(8,128)(2,1)}, bf16[3,96,384]{2,1,0:T(8,128)(2,1)}, u32[]{:S(2)}, u32[]{:S(2)}) collective-permute-start(bf16[3,96,384]{2,1,0:T(8,128)(2,1)} %collective-permute-done.6), channel_id=1, source_target_pairs={{0,2},{1,3},{2,0},{3,1},{4,6},{5,7},{6,4},{7,5},{8,10},{9,11},{10,... | collective-permute-start | bytes 663560 | tf_op jit(solution)/shard_map/ppermute | solution.py:23
  123.2 13.7 %collective-permute-start.28 = (bf16[4,2,96,384]{3,2,1,0:T(8,128)(2,1)}, bf16[4,2,96,384]{3,2,1,0:T(8,128)(2,1)}, u32[]{:S(2)}, u32[]{:S(2)}) collective-permute-start(bf16[4,2,96,384]{3,2,1,0:T(8,128)(2,1)} %collective-permute-done.23.refs_7_), channel_id=1, source_target_pairs={{0,1},{1,0},{2,3},{3,2},{4,5},{5,4},{6,7},{7,6},{8,9},{9,8},{10,11... | collective-permute-start | bytes 1769480 | tf_op jit(solution)/shard_map/ppermute | solution.py:23
  124.8 12.5 %collective-permute-start.26 = (bf16[4,2,96,384]{3,2,1,0:T(8,128)(2,1)}, bf16[4,2,96,384]{3,2,1,0:T(8,128)(2,1)}, u32[]{:S(2)}, u32[]{:S(2)}) collective-permute-start(bf16[4,2,96,384]{3,2,1,0:T(8,128)(2,1)} %collective-permute-done.22.refs_5_), channel_id=1, source_target_pairs={{0,1},{1,0},{2,3},{3,2},{4,5},{5,4},{6,7},{7,6},{8,9},{9,8},{10,11... | collective-permute-start | bytes 1769480 | tf_op jit(solution)/shard_map/ppermute | solution.py:23
  127.5 10.2 %collective-permute-start.27 = (bf16[4,2,96,384]{3,2,1,0:T(8,128)(2,1)}, bf16[4,2,96,384]{3,2,1,0:T(8,128)(2,1)}, u32[]{:S(2)}, u32[]{:S(2)}) collective-permute-start(bf16[4,2,96,384]{3,2,1,0:T(8,128)(2,1)} %collective-permute-done.24.refs_6_), channel_id=1, source_target_pairs={{0,1},{1,0},{2,3},{3,2},{4,5},{5,4},{6,7},{7,6},{8,9},{9,8},{10,11... | collective-permute-start | bytes 1769480 | tf_op jit(solution)/shard_map/ppermute | solution.py:23
  132.7 4.3 %copy-start.17 = (bf16[528,384]{1,0:T(8,128)(2,1)S(1)}, bf16[528,384]{1,0:T(8,128)(2,1)}, u32[]{:S(2)}) copy-start(bf16[528,384]{1,0:T(8,128)(2,1)} %get-tuple-element.10) | copy-start | bytes 1216516
  132.7 4.6 %copy-start.16 = (bf16[528,384]{1,0:T(8,128)(2,1)S(1)}, bf16[528,384]{1,0:T(8,128)(2,1)}, u32[]{:S(2)}) copy-start(bf16[528,384]{1,0:T(8,128)(2,1)} %get-tuple-element.9) | copy-start | bytes 1216516
  132.7 30.5 %copy-start.6 = (bf16[4,3,96,384]{3,2,1,0:T(8,128)(2,1)S(1)}, bf16[4,3,96,384]{3,2,1,0:T(8,128)(2,1)}, u32[]{:S(2)}) copy-start(bf16[4,3,96,384]{3,2,1,0:T(8,128)(2,1)} %after.3.refs_3_) | copy-start | bytes 2654212
  132.7 31.6 %copy-start.15 = (bf16[528,384]{1,0:T(8,128)(2,1)S(1)}, bf16[528,384]{1,0:T(8,128)(2,1)}, u32[]{:S(2)}) copy-start(bf16[528,384]{1,0:T(8,128)(2,1)} %get-tuple-element.8) | copy-start | bytes 1216516
  132.7 33.6 %collective-permute-start.10 = (bf16[4,3,96,384]{3,2,1,0:T(8,128)(2,1)}, bf16[4,3,96,384]{3,2,1,0:T(8,128)(2,1)S(1)}, u32[]{:S(2)}, u32[]{:S(2)}) collective-permute-start(bf16[4,3,96,384]{3,2,1,0:T(8,128)(2,1)} %after.3.refs_3_), channel_id=1, source_target_pairs={{0,8},{8,0},{16,24},{24,16},{1,9},{9,1},{17,25},{25,17},{2,10},{10... | collective-permute-start | bytes 2654216 | tf_op jit(solution)/shard_map/ppermute | solution.py:23
  134.4 32.4 %collective-permute-start.12 = (bf16[4,3,96,384]{3,2,1,0:T(8,128)(2,1)}, bf16[4,3,96,384]{3,2,1,0:T(8,128)(2,1)S(1)}, u32[]{:S(2)}, u32[]{:S(2)}) collective-permute-start(bf16[4,3,96,384]{3,2,1,0:T(8,128)(2,1)} %after.3.refs_3_), channel_id=1, source_target_pairs={{0,16},{8,24},{16,0},{24,8},{1,17},{9,25},{17,1},{25,9},{2,18},{10... | collective-permute-start | bytes 2654216 | tf_op jit(solution)/shard_map/ppermute | solution.py:23
  137.0 26.2 %collective-permute-start.2 = (bf16[528,384]{1,0:T(8,128)(2,1)S(1)}, bf16[528,384]{1,0:T(8,128)(2,1)S(1)}, u32[]{:S(2)}, u32[]{:S(2)}) collective-permute-start(bf16[528,384]{1,0:T(8,128)(2,1)S(1)} %copy-done.17), channel_id=1, source_target_pairs={{0,8},{8,0},{16,24},{24,16},{1,9},{9,1},{17,25},{25,17},{2,10},{10... | collective-permute-start | bytes 1216520 | tf_op jit(solution)/shard_map/ppermute | solution.py:23
  137.3 27.0 %collective-permute-start.3 = (bf16[528,384]{1,0:T(8,128)(2,1)S(1)}, bf16[528,384]{1,0:T(8,128)(2,1)S(1)}, u32[]{:S(2)}, u32[]{:S(2)}) collective-permute-start(bf16[528,384]{1,0:T(8,128)(2,1)S(1)} %copy-done.16), channel_id=1, source_target_pairs={{0,16},{8,24},{16,0},{24,8},{1,17},{9,25},{17,1},{25,9},{2,18},{10... | collective-permute-start | bytes 1216520 | tf_op jit(solution)/shard_map/ppermute | solution.py:23
  137.7 38.5 %collective-permute-start.30 = (bf16[2,5,96,384]{3,2,1,0:T(8,128)(2,1)S(1)}, bf16[2,5,96,384]{3,2,1,0:T(8,128)(2,1)S(1)}, u32[]{:S(2)}, u32[]{:S(2)}) collective-permute-start(bf16[2,5,96,384]{3,2,1,0:T(8,128)(2,1)S(1)} %pad_maximum_fusion.1), channel_id=1, source_target_pairs={{0,2},{1,3},{2,0},{3,1},{4,6},{5,7},{6,4},{7,5},{8,10},{9,11},{10,... | collective-permute-start | bytes 2211848 | tf_op jit(solution)/shard_map/ppermute | solution.py:23
  163.2 26.2 %collective-permute-start.16 = (bf16[4,3,96,384]{3,2,1,0:T(8,128)(2,1)S(1)}, bf16[4,3,96,384]{3,2,1,0:T(8,128)(2,1)S(1)}, u32[]{:S(2)}, u32[]{:S(2)}) collective-permute-start(bf16[4,3,96,384]{3,2,1,0:T(8,128)(2,1)S(1)} %copy-done.6), channel_id=1, source_target_pairs={{0,1},{1,0},{2,3},{3,2},{4,5},{5,4},{6,7},{7,6},{8,9},{9,8},{10,11... | collective-permute-start | bytes 2654216 | tf_op jit(solution)/shard_map/ppermute | solution.py:23
  164.3 10.7 %collective-permute-start.4 = (bf16[528,384]{1,0:T(8,128)(2,1)S(1)}, bf16[528,384]{1,0:T(8,128)(2,1)S(1)}, u32[]{:S(2)}, u32[]{:S(2)}) collective-permute-start(bf16[528,384]{1,0:T(8,128)(2,1)S(1)} %copy-done.15), channel_id=1, source_target_pairs={{0,24},{8,16},{16,8},{24,0},{1,25},{9,17},{17,9},{25,1},{2,26},{10... | collective-permute-start | bytes 1216520 | tf_op jit(solution)/shard_map/ppermute | solution.py:23
  166.3 32.2 %copy-start.7 = (bf16[4,3,96,384]{3,2,1,0:T(8,128)(2,1)}, bf16[4,3,96,384]{3,2,1,0:T(8,128)(2,1)S(1)}, u32[]{:S(2)}) copy-start(bf16[4,3,96,384]{3,2,1,0:T(8,128)(2,1)S(1)} %collective-permute-done.10.refs_4_) | copy-start | bytes 2654212
  166.3 32.3 %collective-permute-start.17 = (bf16[4,3,96,384]{3,2,1,0:T(8,128)(2,1)S(1)}, bf16[4,3,96,384]{3,2,1,0:T(8,128)(2,1)S(1)}, u32[]{:S(2)}, u32[]{:S(2)}) collective-permute-start(bf16[4,3,96,384]{3,2,1,0:T(8,128)(2,1)S(1)} %collective-permute-done.10.refs_4_), channel_id=1, source_target_pairs={{0,1},{1,0},{2,3},{3,2},{4,5},{5,4},{6,7},{7,6},{8,9},{9,8},{10,11... | collective-permute-start | bytes 2654216 | tf_op jit(solution)/shard_map/ppermute | solution.py:23
  166.8 31.7 %copy-start.8 = (bf16[4,3,96,384]{3,2,1,0:T(8,128)(2,1)}, bf16[4,3,96,384]{3,2,1,0:T(8,128)(2,1)S(1)}, u32[]{:S(2)}) copy-start(bf16[4,3,96,384]{3,2,1,0:T(8,128)(2,1)S(1)} %collective-permute-done.12.refs_5_) | copy-start | bytes 2654212
  166.8 31.8 %collective-permute-start.18 = (bf16[4,3,96,384]{3,2,1,0:T(8,128)(2,1)S(1)}, bf16[4,3,96,384]{3,2,1,0:T(8,128)(2,1)S(1)}, u32[]{:S(2)}, u32[]{:S(2)}) collective-permute-start(bf16[4,3,96,384]{3,2,1,0:T(8,128)(2,1)S(1)} %collective-permute-done.12.refs_5_), channel_id=1, source_target_pairs={{0,1},{1,0},{2,3},{3,2},{4,5},{5,4},{6,7},{7,6},{8,9},{9,8},{10,11... | collective-permute-start | bytes 2654216 | tf_op jit(solution)/shard_map/ppermute | solution.py:23
  174.9 9.7 %collective-permute-start.11 = (bf16[2,3,96,384]{3,2,1,0:T(8,128)(2,1)S(1)}, bf16[2,3,96,384]{3,2,1,0:T(8,128)(2,1)}, u32[]{:S(2)}, u32[]{:S(2)}) collective-permute-start(bf16[2,3,96,384]{3,2,1,0:T(8,128)(2,1)S(1)} %slice.82), channel_id=1, source_target_pairs={{0,16},{8,24},{16,0},{24,8},{1,17},{9,25},{17,1},{25,9},{2,18},{10... | collective-permute-start | bytes 1327112 | tf_op jit(solution)/shard_map/ppermute | solution.py:23
  176.2 11.4 %collective-permute-start.13 = (bf16[2,3,96,384]{3,2,1,0:T(8,128)(2,1)S(1)}, bf16[2,3,96,384]{3,2,1,0:T(8,128)(2,1)S(1)}, u32[]{:S(2)}, u32[]{:S(2)}) collective-permute-start(bf16[2,3,96,384]{3,2,1,0:T(8,128)(2,1)S(1)} %slice.83), channel_id=1, source_target_pairs={{0,8},{8,0},{16,24},{24,16},{1,9},{9,1},{17,25},{25,17},{2,10},{10... | collective-permute-start | bytes 1327112 | tf_op jit(solution)/shard_map/ppermute | solution.py:23
  184.7 28.2 %collective-permute-start.14 = (bf16[2,3,96,384]{3,2,1,0:T(8,128)(2,1)}, bf16[2,3,96,384]{3,2,1,0:T(8,128)(2,1)S(1)}, u32[]{:S(2)}, u32[]{:S(2)}) collective-permute-start(bf16[2,3,96,384]{3,2,1,0:T(8,128)(2,1)} %collective-permute-done.11.refs_4_), channel_id=1, source_target_pairs={{0,1},{1,0},{2,3},{3,2},{4,5},{5,4},{6,7},{7,6},{8,9},{9,8},{10,11... | collective-permute-start | bytes 1327112 | tf_op jit(solution)/shard_map/ppermute | solution.py:23
  187.6 11.0 %copy-start.12 = (bf16[2,3,96,384]{3,2,1,0:T(8,128)(2,1)}, bf16[2,3,96,384]{3,2,1,0:T(8,128)(2,1)S(1)}, u32[]{:S(2)}) copy-start(bf16[2,3,96,384]{3,2,1,0:T(8,128)(2,1)S(1)} %collective-permute-done.13.refs_5_) | copy-start | bytes 1327108
  187.6 25.2 %collective-permute-start.15 = (bf16[2,3,96,384]{3,2,1,0:T(8,128)(2,1)S(1)}, bf16[2,3,96,384]{3,2,1,0:T(8,128)(2,1)S(1)}, u32[]{:S(2)}, u32[]{:S(2)}) collective-permute-start(bf16[2,3,96,384]{3,2,1,0:T(8,128)(2,1)S(1)} %collective-permute-done.13.refs_5_), channel_id=1, source_target_pairs={{0,1},{1,0},{2,3},{3,2},{4,5},{5,4},{6,7},{7,6},{8,9},{9,8},{10,11... | collective-permute-start | bytes 1327112 | tf_op jit(solution)/shard_map/ppermute | solution.py:23
  189.4 9.2 %copy-start.9 = (bf16[4,3,96,384]{3,2,1,0:T(8,128)(2,1)}, bf16[4,3,96,384]{3,2,1,0:T(8,128)(2,1)S(1)}, u32[]{:S(2)}) copy-start(bf16[4,3,96,384]{3,2,1,0:T(8,128)(2,1)S(1)} %collective-permute-done.16.refs_6_) | copy-start | bytes 2654212
  189.4 35.3 %collective-permute-start.31 = (bf16[1,5,96,384]{3,2,1,0:T(8,128)(2,1)}, bf16[1,5,96,384]{3,2,1,0:T(8,128)(2,1)S(1)}, u32[]{:S(2)}, u32[]{:S(2)}) collective-permute-start(bf16[1,5,96,384]{3,2,1,0:T(8,128)(2,1)} %add_convert_fusion), channel_id=1, source_target_pairs={{0,6},{1,7},{2,4},{3,5},{4,2},{5,3},{6,0},{7,1},{8,14},{9,15},{10,... | collective-permute-start | bytes 1105928 | tf_op jit(solution)/shard_map/ppermute | solution.py:23
  199.5 1.0 copy-start.11
  (3 other events, 2.4 us)

commit v4 on v3

--- a/solution.py
+++ b/solution.py
@@ -10,7 +10,7 @@
 
 HALO = 8
 LANES = 128
-SPLIT = 3
+SPLIT = 2
 ROOT = math.sqrt(2.0 / math.pi)
 CUBIC = 0.044715
 ANYWHERE = pl.BlockSpec(memory_space=pl.ANY)
@@ -41,20 +41,23 @@
     return lax.slice_in_dim(piece[0], which * size, (which + 1) * size, axis=0)
 
 
-def gather_square(value, axis):
-    found = {0: (value,)}
-    near = [d for d in range(1, lax.axis_size(axis)) if d & (d - 1) == 0]
-    for distance in near:
-        found[distance] = (from_peer(value, axis, distance),)
+def gather_near(value, axis):
+    distances = [d for d in range(1, lax.axis_size(axis)) if d & (d - 1) == 0]
+    return {d: (from_peer(value, axis, d),) for d in distances}
+
+
+def gather_far(found, axis, *earlier):
+    far = {}
     for distance in range(1, lax.axis_size(axis)):
-        if distance not in near:
-            high = 1 << (distance.bit_length() - 1)
-            low = distance & -distance
-            found[distance] = (
-                from_peer(half_of(found[distance ^ high], 0), axis, high),
-                from_peer(half_of(found[distance ^ low], 1), axis, low),
-            )
-    return found
+        high = 1 << (distance.bit_length() - 1)
+        low = distance & -distance
+        if high != low:
+            known = {**found, **far}
+            halves = half_of(known[distance ^ high], 0), half_of(known[distance ^ low], 1)
+            if earlier:
+                halves = [after(half, *earlier) for half in halves]
+            far[distance] = (from_peer(halves[0], axis, high), from_peer(halves[1], axis, low))
+    return far
 
 
 def line_masks(count):
@@ -63,14 +66,6 @@
         masks.append(count - 1)
         count //= 2
     return masks
-
-
-def gather_line(value, axis, count, unit):
-    found = {0: value}
-    for mask in line_masks(count):
-        for distance in list(found):
-            found[distance ^ mask] = from_peer(found[distance], axis, mask * unit)
-    return [found[distance] for distance in range(count)]
 
 
 def reduce_line(blocks, axis, count, unit):
@@ -298,6 +293,13 @@
     return outs[0], outs[1].astype(jnp.bfloat16)
 
 
+def owner_of(owner, rep):
+    if isinstance(owner, int):
+        return owner
+    plane, flip = owner
+    return 2 * plane + (rep % 2 ^ flip)
+
+
 def input_terms(place, grads, entries, first_tap, sums, inputs, reps):
     arrays, index = [], {}
     for array, *_ in entries:
@@ -307,7 +309,7 @@
     distances = sorted({entry[2] for entry in entries})
     window, block = grads[0].shape
     coarse = window - 2 * HALO
-    taps, rows = arrays[0].shape[1:3]
+    taps, rows = arrays[0].shape[-3:-1]
     width, depth = reps * rows, len(distances) * block
     last, begun = inputs is not None, sums is not None
     shown = width // block if last else 0
@@ -338,14 +340,11 @@
             spot = pl.ds(slot * block, block)
             source = own[used.index(distance)]
             copies.append(pltpu.make_async_copy(source, gv.at[:, spot], grad_sems.at[slot]))
-        for number, (array, at, distance, flip, plane) in enumerate(entries):
+        for number, (array, at, distance, owner) in enumerate(entries):
             spot = pl.ds(distances.index(distance) * block, block)
-            owner = rep ^ flip ^ (2 * plane)
-            copies.append(
-                pltpu.make_async_copy(
-                    pieces[index[id(array)]].at[at], wv.at[:, owner, :, spot], sems.at[number]
-                )
-            )
+            source = pieces[index[id(array)]].at[at]
+            target = wv.at[:, owner_of(owner, rep), :, spot]
+            copies.append(pltpu.make_async_copy(source, target, sems.at[number]))
         if last:
             for slot in range(len(used)):
                 copy = pltpu.make_async_copy(own[slot], skips.at[me ^ slot], skip_sems.at[slot])
@@ -460,9 +459,9 @@
         grad = lax.dynamic_update_slice(grad, grads[distance], spot)
     kernel = jnp.zeros((taps, width, seqs * block), jnp.bfloat16)
     for first_tap, entries in parts:
-        for array, at, distance, flip, plane in entries:
-            owner = place[1] ^ flip ^ (2 * plane)
-            spot = (first_tap, owner * rows, (place[0] ^ distance) * block)
+        for array, at, distance, owner in entries:
+            row = owner_of(owner, place[1]) * rows
+            spot = (first_tap, row, (place[0] ^ distance) * block)
             kernel = lax.dynamic_update_slice(kernel, array[at], spot)
     products = lax.dot_general(
         grad, kernel, (((1,), (2,)), ((), ())), preferred_element_type=jnp.float32
@@ -493,18 +492,14 @@
     across = jnp.stack(
         [last_taps] + [from_peer(last_taps, "seq", d) for d in range(1, seqs)]
     )
-    act = gather_square(activate(inputs), "seq")
-    near = [act[d][0] for d in act if len(act[d]) == 1 and d]
+    last = lax.all_gather(across, "rep")
+    last_entries = [(last, (r, d), d, r) for r in range(reps) for d in range(seqs)]
+
+    act = {0: (activate(inputs),)}
+    act.update(gather_near(act[0][0], "seq"))
+    near = [act[d][0] for d in act if d]
+    act.update(gather_far(act, "seq", across))
     far = [part for d in act if len(act[d]) == 2 for part in act[d]]
-    first_columns = jnp.stack(gather_line(weights[:SPLIT], "rep", planes, 2))
-    lines = gather_line(across, "rep", planes, 2)
-    other_lines = [from_peer(line, "rep", 1) for line in lines]
-    last_entries = [
-        (line, distance, distance, flip, plane)
-        for flip, found in enumerate((lines, other_lines))
-        for plane, line in enumerate(found)
-        for distance in range(seqs)
-    ]
 
     trunk = trunk_grad[0]
     edged = after(jnp.pad(trunk, ((HALO, HALO), (0, 0))), *near)
@@ -513,16 +508,23 @@
         window = lax.dynamic_slice_in_dim(edged, (me ^ distance) * coarse, coarse + 2 * HALO, 0)
         grads.append(from_peer(window, "seq", distance) if distance else window)
 
-    kept = gather_square(after(first_columns, *far), "seq")
-    swapped = {d: tuple(from_peer(part, "rep", 1) for part in kept[d]) for d in kept}
-    first_entries = []
-    for flip, found in enumerate((kept, swapped)):
-        for distance, parts in found.items():
-            plane = 0
-            for part in parts:
-                for at in range(part.shape[0]):
-                    first_entries.append((part, at, distance, flip, plane))
-                    plane += 1
+    first = lax.all_gather(weights[:SPLIT], "rep")
+    column = lax.dynamic_index_in_dim(
+        first.reshape(planes, 2, *first.shape[1:]), rep % 2, 1, keepdims=False
+    )
+    column = after(column, *far, *grads[1:])
+    kept = {0: (column,)}
+    kept.update(gather_near(column, "seq"))
+    kept.update(gather_far(kept, "seq"))
+    first_entries = [(first, r, 0, r) for r in range(reps)]
+    for distance, parts in kept.items():
+        plane = 0
+        for part in parts if distance else ():
+            other = from_peer(part, "rep", 1)
+            for at in range(part.shape[0]):
+                first_entries.append((part, at, distance, (plane, 0)))
+                first_entries.append((other, at, distance, (plane, 1)))
+                plane += 1
 
     zeros = jnp.zeros((1, block), jnp.bfloat16)
     later = jnp.concatenate([trunk[1:], zeros])

time: 229 us -> 196 us (0.86)
  waiting for transfers between devices: 103 us -> 64.5 us
  between operations: 0.94 us -> 14.2 us
  starting transfers between devices: 38 us -> 26.6 us
    ppermute x32 -> x21, waiting for transfers between devices: 103 us -> 64.5 us  [from_peer(): return lax.ppermute(value, axis, [(i, i ^ distance) for i in range(peers)])]
    ppermute x32 -> x21, starting transfers between devices: 38 us -> 26.5 us  [from_peer(): return lax.ppermute(value, axis, [(i, i ^ distance) for i in range(peers)])]
    unnamed x38 -> x24, local copies, waits for them, and re-layouts: 6.23 us -> 1.53 us
    slice x1, local copies, waits for them, and re-layouts: 0.51 us -> 3.98 us  [on_device(): later = jnp.concatenate([trunk[1:], zeros])]
    concatenate x1, other arithmetic: 2.95 us -> 5.94 us  [on_device(): shifts = jnp.concatenate([later, trunk, earlier], axis=1)]
  transfers between devices with their start and end apart: 32 -> 23, of which waited for: 8 -> 9; matrix products, arithmetic and copies ran while one was open for 9% -> 14% of each run, Pallas kernels for 24% -> 25%
where the time goes in v4:
time: 196 us; the launch traced here: 193 us
  waiting for transfers between devices  64.5 us (33%)
  Pallas kernels  57.6 us (29%)
  starting transfers between devices  26.6 us (14%)
  local copies, waits for them, and re-layouts  16.8 us (9%)
  between operations  14.2 us (7%)
  other arithmetic  13.3 us (7%)
    ppermute x21, waiting for transfers between devices, from_peer(): return lax.ppermute(value, axis, [(i, i ^ distance) for i in range(peers)])  64.5 us
    pallas_call x3, Pallas kernels, input_terms(): pl.pallas_call(kernel, out_shape=out_shape, grid_spec=pltpu.PrefetchScala...  31.4 us
    ppermute x21, starting transfers between devices, from_peer(): return lax.ppermute(value, axis, [(i, i ^ distance) for i in range(peers)])  26.5 us
    pallas_call x1, Pallas kernels, early_terms(): pl.pallas_call(kernel, out_shape=jax.ShapeDtypeStruct((both, columns), jn...  13.4 us
    pallas_call x1, Pallas kernels, late_terms(): pl.pallas_call(kernel, out_shape=(jax.ShapeDtypeStruct(shape, jnp.float32...  9.86 us
    concatenate x1, other arithmetic, on_device(): shifts = jnp.concatenate([later, trunk, earlier], axis=1)  5.94 us
    slice x1, local copies, waits for them, and re-layouts, on_device(): later = jnp.concatenate([trunk[1:], zeros])  3.98 us
  transfers between devices with their start and end apart: 23, of which 9 were waited for; matrix products, arithmetic and copies ran while one was open for 14% of the time, Pallas kernels for 25%

profile of v4, /device:TPU:9, one launch (start us, length us, event | category | flops | bytes accessed | tf_op | source)
XLA Modules:
  0.0 193.0 jit_solution(9627241322193665335)
XLA Ops:
  7.2 1.7 slice.60
  9.0 1.0 slice_bitcast_fusion.2
  10.0 1.3 collective-permute-start.6
  11.3 1.2 collective-permute-start.5
  12.7 3.6 %collective-permute-done.6 = bf16[3,96,384]{2,1,0:T(8,128)(2,1)S(1)} collective-permute-done((bf16[3,96,384]{2,1,0:T(8,128)(2,1)S(1)}, bf16[3,96,384]{2,1,0:T(8,128)(2,1)S(1)}, u32[]{:S(2)}, u32[]{:S(2)}) %collective-permute-start.6) | collective-permute-done | bytes 221216 | tf_op jit(solution)/shard_map/ppermute | solution.py:23
  16.3 0.9 collective-permute-done.5
  17.2 4.7 %collective-permute-done.7 = bf16[3,96,384]{2,1,0:T(8,128)(2,1)S(1)} collective-permute-done((bf16[3,96,384]{2,1,0:T(8,128)(2,1)S(1)}, bf16[3,96,384]{2,1,0:T(8,128)(2,1)S(1)}, u32[]{:S(2)}, u32[]{:S(2)}) %collective-permute-start.7) | collective-permute-done | bytes 221216 | tf_op jit(solution)/shard_map/ppermute | solution.py:23
  21.9 1.1 pad_maximum_fusion.refs_1_
  23.0 2.9 %act.1.refs_0_ = bf16[512,1536]{1,0:T(8,128)(2,1)} custom-call(bf16[1,1024,768]{2,1,0:T(8,128)(2,1)S(1)} %copy-done), custom_call_target="tpu_custom_call" | custom-call | tf_op jit(solution)/shard_map/act/pallas_call | solution.py:109
  25.9 1.2 collective-permute-start.1
  27.2 1.2 collective-permute-start
  28.4 4.0 %slice_bitcast_fusion.1 = (bf16[2047,384]{1,0:T(8,128)(2,1)}, bf16[2047,384]{1,0:T(8,128)(2,1)}) fusion(bf16[1,2048,384]{2,1,0:T(8,128)(2,1)} %param.4), kind=kLoop, calls=%fused_computation.7 | loop fusion | bytes 6288384 | tf_op jit(solution)/shard_map/slice | solution.py:530
  32.4 27.8 %collective-permute-done.1.refs_2_ = bf16[512,1536]{1,0:T(8,128)(2,1)S(1)} collective-permute-done((bf16[512,1536]{1,0:T(8,128)(2,1)}, bf16[512,1536]{1,0:T(8,128)(2,1)S(1)}, u32[]{:S(2)}, u32[]{:S(2)}) %collective-permute-start.1) | collective-permute-done | bytes 1572896 | tf_op jit(solution)/shard_map/ppermute | solution.py:23
  60.2 1.0 slice.81.refs_0_
  61.2 1.2 collective-permute-start.9
  62.4 1.0 slice.80.refs_0_
  63.4 1.2 collective-permute-start.8
  64.7 5.9 %fusion.2.shifts_ref = bf16[2048,1152]{1,0:T(8,128)(2,1)} fusion(bf16[2047,384]{1,0:T(8,128)(2,1)} %get-tuple-element.13, bf16[2047,384]{1,0:T(8,128)(2,1)} %get-tuple-element.12, bf16[2048,384]{1,0:T(8,128)(2,1)} %bitcast.21), kind=kLoop, calls=%fused_computation.4 | loop fusion | flops 23592960 | bytes 9435648 | tf_op jit(solution)/shard_map/concatenate | solution.py:532
  70.7 13.4 %weight_grad_early.1.early_ref = f32[1536,1152]{1,0:T(8,128)} custom-call(s32[2]{0:T(128)S(1)} %pad_add_fusion.place, bf16[2048,1152]{1,0:T(8,128)(2,1)} %fusion.2.shifts_ref, bf16[512,1536]{1,0:T(8,128)(2,1)} %act.1.refs_0_, bf16[512,1536]{1,0:T(8,128)(2,1)S(1)} %collective-permute-done.refs_1_, bf16[512,1536]{1,0:T(8,128)(2,1)S(1)} %collective-permute-done.1.refs_2_), custom_call_target="tpu_custom_call" | custom-call | flops 5435817984 | bytes 16777216 | tf_op jit(solution)/shard_map/weight_grad_early/pallas_call | solution.py:168
  84.1 9.9 %weight_grad_late.1 = (f32[4,5,96,384]{3,2,1,0:T(8,128)S(1)}, bf16[4,5,96,384]{3,2,1,0:T(8,128)(2,1)}) custom-call(s32[2]{0:T(128)S(1)} %pad_add_fusion.place, bf16[2048,1152]{1,0:T(8,128)(2,1)} %fusion.2.shifts_ref, f32[1536,1152]{1,0:T(8,128)} %weight_grad_early.1.early_ref, bf16[256,1536]{1,0:T(8,128)(2,1)} %collective-permute-done.8.refs_1_.refs_0_, ...), custom_call_target="tpu_custom_call" | custom-call | flops 1811939328 | bytes 16777216 | tf_op jit(solution)/shard_map/weight_grad_late/pallas_call | solution.py:241
  94.0 3.5 %collective-permute-start.18 = (bf16[4,5,96,384]{3,2,1,0:T(8,128)(2,1)}, bf16[4,5,96,384]{3,2,1,0:T(8,128)(2,1)}, u32[]{:S(2)}, u32[]{:S(2)}) collective-permute-start(bf16[4,5,96,384]{3,2,1,0:T(8,128)(2,1)} %get-tuple-element.5), channel_id=1, source_target_pairs={{0,1},{1,0},{2,3},{3,2},{4,5},{5,4},{6,7},{7,6},{8,9},{9,8},{10,11... | collective-permute-start | bytes 4423688 | tf_op jit(solution)/shard_map/ppermute | solution.py:23
  97.5 2.7 %pad.6.refs_0_ = bf16[2064,384]{1,0:T(8,128)(2,1)} pad(bf16[2048,384]{1,0:T(8,128)(2,1)} %bitcast.22, bf16[]{:T(256)} %constant.29.clone.1), padding=8_8x0_0 | pad | bytes 3158018 | tf_op jit(solution)/shard_map/jit(_pad)/pad | solution.py:505
  100.3 0.6 collective-permute-done.18
  100.9 1.3 add_convert_fusion.2
  102.2 0.9 pad_maximum_fusion.1
  103.2 0.9 constant_dynamic-slice_fusion
  104.5 1.1 collective-permute-start.3
  105.6 1.1 collective-permute-start.2
  106.8 1.9 dynamic-slice_bitcast_fusion.refs_0_
  108.7 6.6 %collective-permute-done.4.refs_5_.refs_3_ = bf16[528,384]{1,0:T(8,128)(2,1)S(1)} collective-permute-done((bf16[528,384]{1,0:T(8,128)(2,1)}, bf16[528,384]{1,0:T(8,128)(2,1)S(1)}, u32[]{:S(2)}, u32[]{:S(2)}) %collective-permute-start.4) | collective-permute-done | bytes 405536 | tf_op jit(solution)/shard_map/ppermute | solution.py:23
  115.3 8.5 %collective-permute-done.3.refs_4_.refs_2_ = bf16[528,384]{1,0:T(8,128)(2,1)S(1)} collective-permute-done((bf16[528,384]{1,0:T(8,128)(2,1)S(1)}, bf16[528,384]{1,0:T(8,128)(2,1)S(1)}, u32[]{:S(2)}, u32[]{:S(2)}) %collective-permute-start.3) | collective-permute-done | bytes 405536 | tf_op jit(solution)/shard_map/ppermute | solution.py:23
  123.8 0.7 copy-done.1
  124.5 0.8 copy-done.3
  125.3 1.7 collective-permute-start.13
  127.4 1.6 add_convert_fusion
  129.1 2.3 %collective-permute-start.20 = (bf16[1,5,96,384]{3,2,1,0:T(8,128)(2,1)S(1)}, bf16[1,5,96,384]{3,2,1,0:T(8,128)(2,1)S(1)}, u32[]{:S(2)}, u32[]{:S(2)}) collective-permute-start(bf16[1,5,96,384]{3,2,1,0:T(8,128)(2,1)S(1)} %add_convert_fusion), channel_id=1, source_target_pairs={{0,6},{1,7},{2,4},{3,5},{4,2},{5,3},{6,0},{7,1},{8,14},{9,15},{10,... | collective-permute-start | bytes 1105928 | tf_op jit(solution)/shard_map/ppermute | solution.py:23
  131.4 8.4 %collective-permute-done.13.refs_6_ = bf16[4,2,96,384]{3,2,1,0:T(8,128)(2,1)} collective-permute-done((bf16[4,2,96,384]{3,2,1,0:T(8,128)(2,1)}, bf16[4,2,96,384]{3,2,1,0:T(8,128)(2,1)}, u32[]{:S(2)}, u32[]{:S(2)}) %collective-permute-start.13) | collective-permute-done | bytes 589856 | tf_op jit(solution)/shard_map/ppermute | solution.py:23
  139.8 1.0 slice.83
  140.8 2.0 %collective-permute-start.14 = (bf16[2,2,96,384]{3,2,1,0:T(8,128)(2,1)S(1)}, bf16[2,2,96,384]{3,2,1,0:T(8,128)(2,1)S(1)}, u32[]{:S(2)}, u32[]{:S(2)}) collective-permute-start(bf16[2,2,96,384]{3,2,1,0:T(8,128)(2,1)S(1)} %slice.83), channel_id=1, source_target_pairs={{0,8},{8,0},{16,24},{24,16},{1,9},{9,1},{17,25},{25,17},{2,10},{10... | collective-permute-start | bytes 884744 | tf_op jit(solution)/shard_map/ppermute | solution.py:23
  142.9 0.5 collective-permute-start.11
  143.3 1.9 collective-permute-start.17
  145.2 3.3 %collective-permute-done.14.refs_6_ = bf16[2,2,96,384]{3,2,1,0:T(8,128)(2,1)S(1)} collective-permute-done((bf16[2,2,96,384]{3,2,1,0:T(8,128)(2,1)S(1)}, bf16[2,2,96,384]{3,2,1,0:T(8,128)(2,1)S(1)}, u32[]{:S(2)}, u32[]{:S(2)}) %collective-permute-start.14) | collective-permute-done | bytes 294944 | tf_op jit(solution)/shard_map/ppermute | solution.py:23
  148.5 2.3 %collective-permute-start.15 = (bf16[2,2,96,384]{3,2,1,0:T(8,128)(2,1)S(1)}, bf16[2,2,96,384]{3,2,1,0:T(8,128)(2,1)S(1)}, u32[]{:S(2)}, u32[]{:S(2)}) collective-permute-start(bf16[2,2,96,384]{3,2,1,0:T(8,128)(2,1)S(1)} %collective-permute-done.14.refs_6_), channel_id=1, source_target_pairs={{0,1},{1,0},{2,3},{3,2},{4,5},{5,4},{6,7},{7,6},{8,9},{9,8},{10,11... | collective-permute-start | bytes 884744 | tf_op jit(solution)/shard_map/ppermute | solution.py:23
  150.8 1.6 collective-permute-start.12
  152.4 2.4 %add_bitcast_fusion = f32[5,96,384]{2,1,0:T(8,128)} fusion(bf16[1,5,96,384]{3,2,1,0:T(8,128)(2,1)S(1)} %collective-permute-done.20, f32[4,5,96,384]{3,2,1,0:T(8,128)} %copy-done.7, bf16[2,5,96,384]{3,2,1,0:T(8,128)(2,1)} %copy-done.11, bf16[4,5,96,384]{3,2,1,0:T(8,128)(2,1)} %collective-permute-done.18), kind=kLoop, calls=%fused_computation.10 | loop fusion | flops 1105920 | bytes 2580480 | tf_op jit(solution)/shard_map/add | solution.py:79
  154.7 11.9 %input_grad_early.2.refs_8_ = f32[2,512,768]{2,1,0:T(8,128)} custom-call(s32[2]{0:T(128)S(1)} %pad_add_fusion.place, bf16[528,384]{1,0:T(8,128)(2,1)S(1)} %get-tuple-element.11.refs_0_, bf16[528,384]{1,0:T(8,128)(2,1)S(1)} %copy-done.4, bf16[528,384]{1,0:T(8,128)(2,1)S(1)} %copy-done.2, bf16[528,384]{1,0:T(8,128)(2,1)S(1)} %copy-done.9, ...), custom_call_target="tpu_custom_call" | custom-call | flops 3737124864 | bytes 20971520 | tf_op jit(solution)/shard_map/input_grad_early/pallas_call | solution.py:431
  166.7 10.0 %input_grad_early.3.refs_8_ = f32[2,512,768]{2,1,0:T(8,128)} custom-call(s32[2]{0:T(128)S(1)} %pad_add_fusion.place, bf16[528,384]{1,0:T(8,128)(2,1)S(1)} %get-tuple-element.11.refs_0_, bf16[528,384]{1,0:T(8,128)(2,1)S(1)} %copy-done.4, bf16[528,384]{1,0:T(8,128)(2,1)S(1)} %copy-done.2, bf16[8,2,96,384]{3,2,1,0:T(8,128)(2,1)} %bitcast.24, ...), custom_call_target="tpu_custom_call" | custom-call | flops 1868562432 | bytes 20971520 | tf_op jit(solution)/shard_map/input_grad_early/pallas_call | solution.py:431
  176.7 9.5 %input_grad_late.1 = bf16[1,1024,768]{2,1,0:T(8,128)(2,1)} custom-call(s32[2]{0:T(128)S(1)} %pad_add_fusion.place, bf16[528,384]{1,0:T(8,128)(2,1)S(1)} %get-tuple-element.11.refs_0_, bf16[528,384]{1,0:T(8,128)(2,1)S(1)} %copy-done.4, bf16[528,384]{1,0:T(8,128)(2,1)} %copy-done.1, bf16[528,384]{1,0:T(8,128)(2,1)} %copy-done.8, ...), custom_call_target="tpu_custom_call" | custom-call | flops 622854144 | bytes 20971520 | tf_op jit(solution)/shard_map/input_grad_late/pallas_call | solution.py:431
  (51 shorter events, 1.3 us)
Async XLA Ops:
  7.2 15.9 %copy-start = (bf16[1,1024,768]{2,1,0:T(8,128)(2,1)S(1)}, bf16[1,1024,768]{2,1,0:T(8,128)(2,1)}, u32[]{:S(2)}) copy-start(bf16[1,1024,768]{2,1,0:T(8,128)(2,1)} %refs_9_.1) | copy-start | bytes 4718596
  7.2 99.6 %all-gather.5.cloned.1.call-start = ((), (), s32[]{:S(2)}) async-start(), calls=%async_computation | async-start | bytes 1327104 | tf_op jit(solution)/shard_map/all_gather | solution.py:511
  8.9 145.8 %all-gather.7.cloned.1.call-start = ((), (), s32[]{:S(2)}) async-start(), calls=%async_computation.1 | async-start | bytes 7962624 | tf_op jit(solution)/shard_map/all_gather | solution.py:495
  10.0 6.4 %collective-permute-start.6 = (bf16[3,96,384]{2,1,0:T(8,128)(2,1)S(1)}, bf16[3,96,384]{2,1,0:T(8,128)(2,1)S(1)}, u32[]{:S(2)}, u32[]{:S(2)}) collective-permute-start(bf16[3,96,384]{2,1,0:T(8,128)(2,1)S(1)} %get-tuple-element.15), channel_id=1, source_target_pairs={{0,16},{8,24},{16,0},{24,8},{1,17},{9,25},{17,1},{25,9},{2,18},{10... | collective-permute-start | bytes 663560 | tf_op jit(solution)/shard_map/ppermute | solution.py:23
  11.3 6.0 %collective-permute-start.5 = (bf16[3,96,384]{2,1,0:T(8,128)(2,1)S(1)}, bf16[3,96,384]{2,1,0:T(8,128)(2,1)S(1)}, u32[]{:S(2)}, u32[]{:S(2)}) collective-permute-start(bf16[3,96,384]{2,1,0:T(8,128)(2,1)S(1)} %get-tuple-element.15), channel_id=1, source_target_pairs={{0,8},{8,0},{16,24},{24,16},{1,9},{9,1},{17,25},{25,17},{2,10},{10... | collective-permute-start | bytes 663560 | tf_op jit(solution)/shard_map/ppermute | solution.py:23
  12.5 9.4 %collective-permute-start.7 = (bf16[3,96,384]{2,1,0:T(8,128)(2,1)S(1)}, bf16[3,96,384]{2,1,0:T(8,128)(2,1)S(1)}, u32[]{:S(2)}, u32[]{:S(2)}) collective-permute-start(bf16[3,96,384]{2,1,0:T(8,128)(2,1)S(1)} %get-tuple-element.15), channel_id=1, source_target_pairs={{0,24},{8,16},{16,8},{24,0},{1,25},{9,17},{17,9},{25,1},{2,26},{10... | collective-permute-start | bytes 663560 | tf_op jit(solution)/shard_map/ppermute | solution.py:23
  25.9 34.2 %collective-permute-start.1 = (bf16[512,1536]{1,0:T(8,128)(2,1)}, bf16[512,1536]{1,0:T(8,128)(2,1)S(1)}, u32[]{:S(2)}, u32[]{:S(2)}) collective-permute-start(bf16[512,1536]{1,0:T(8,128)(2,1)} %act.1.refs_0_), channel_id=1, source_target_pairs={{0,16},{8,24},{16,0},{24,8},{1,17},{9,25},{17,1},{25,9},{2,18},{10... | collective-permute-start | bytes 4718600 | tf_op jit(solution)/shard_map/ppermute | solution.py:23
  27.2 35.3 %collective-permute-start = (bf16[512,1536]{1,0:T(8,128)(2,1)}, bf16[512,1536]{1,0:T(8,128)(2,1)S(1)}, u32[]{:S(2)}, u32[]{:S(2)}) collective-permute-start(bf16[512,1536]{1,0:T(8,128)(2,1)} %act.1.refs_0_), channel_id=1, source_target_pairs={{0,8},{8,0},{16,24},{24,16},{1,9},{9,1},{17,25},{25,17},{2,10},{10... | collective-permute-start | bytes 4718600 | tf_op jit(solution)/shard_map/ppermute | solution.py:23
  60.2 10.5 %copy-start.5 = (bf16[512,1536]{1,0:T(8,128)(2,1)}, bf16[512,1536]{1,0:T(8,128)(2,1)S(1)}, u32[]{:S(2)}) copy-start(bf16[512,1536]{1,0:T(8,128)(2,1)S(1)} %collective-permute-done.1.refs_2_) | copy-start | bytes 4718596
  61.2 22.9 %collective-permute-start.9 = (bf16[256,1536]{1,0:T(8,128)(2,1)}, bf16[256,1536]{1,0:T(8,128)(2,1)}, u32[]{:S(2)}, u32[]{:S(2)}) collective-permute-start(bf16[256,1536]{1,0:T(8,128)(2,1)} %after.6), channel_id=1, source_target_pairs={{0,8},{8,0},{16,24},{24,16},{1,9},{9,1},{17,25},{25,17},{2,10},{10... | collective-permute-start | bytes 2359304 | tf_op jit(solution)/shard_map/ppermute | solution.py:23
  62.4 8.2 %copy-start.6 = (bf16[512,1536]{1,0:T(8,128)(2,1)}, bf16[512,1536]{1,0:T(8,128)(2,1)S(1)}, u32[]{:S(2)}) copy-start(bf16[512,1536]{1,0:T(8,128)(2,1)S(1)} %collective-permute-done.refs_1_) | copy-start | bytes 4718596
  63.4 20.7 %collective-permute-start.8 = (bf16[256,1536]{1,0:T(8,128)(2,1)}, bf16[256,1536]{1,0:T(8,128)(2,1)}, u32[]{:S(2)}, u32[]{:S(2)}) collective-permute-start(bf16[256,1536]{1,0:T(8,128)(2,1)} %after.5), channel_id=1, source_target_pairs={{0,16},{8,24},{16,0},{24,8},{1,17},{9,25},{17,1},{25,9},{2,18},{10... | collective-permute-start | bytes 2359304 | tf_op jit(solution)/shard_map/ppermute | solution.py:23
  94.0 6.9 %copy-start.7 = (f32[4,5,96,384]{3,2,1,0:T(8,128)}, f32[4,5,96,384]{3,2,1,0:T(8,128)S(1)}, u32[]{:S(2)}) copy-start(f32[4,5,96,384]{3,2,1,0:T(8,128)S(1)} %get-tuple-element.4) | copy-start | bytes 8847364
  94.0 6.9 %collective-permute-start.18 = (bf16[4,5,96,384]{3,2,1,0:T(8,128)(2,1)}, bf16[4,5,96,384]{3,2,1,0:T(8,128)(2,1)}, u32[]{:S(2)}, u32[]{:S(2)}) collective-permute-start(bf16[4,5,96,384]{3,2,1,0:T(8,128)(2,1)} %get-tuple-element.5), channel_id=1, source_target_pairs={{0,1},{1,0},{2,3},{3,2},{4,5},{5,4},{6,7},{7,6},{8,9},{9,8},{10,11... | collective-permute-start | bytes 4423688 | tf_op jit(solution)/shard_map/ppermute | solution.py:23
  100.3 2.9 %copy-start.10 = (bf16[2064,384]{1,0:T(8,128)(2,1)S(1)}, bf16[2064,384]{1,0:T(8,128)(2,1)}, u32[]{:S(2)}) copy-start(bf16[2064,384]{1,0:T(8,128)(2,1)} %after.4) | copy-start | bytes 4755460
  103.2 24.3 %collective-permute-start.19 = (bf16[2,5,96,384]{3,2,1,0:T(8,128)(2,1)}, bf16[2,5,96,384]{3,2,1,0:T(8,128)(2,1)S(1)}, u32[]{:S(2)}, u32[]{:S(2)}) collective-permute-start(bf16[2,5,96,384]{3,2,1,0:T(8,128)(2,1)} %pad_maximum_fusion.1), channel_id=1, source_target_pairs={{0,2},{1,3},{2,0},{3,1},{4,6},{5,7},{6,4},{7,5},{8,10},{9,11},{10,... | collective-permute-start | bytes 2211848 | tf_op jit(solution)/shard_map/ppermute | solution.py:23
  104.1 11.2 %collective-permute-start.4 = (bf16[528,384]{1,0:T(8,128)(2,1)}, bf16[528,384]{1,0:T(8,128)(2,1)S(1)}, u32[]{:S(2)}, u32[]{:S(2)}) collective-permute-start(bf16[528,384]{1,0:T(8,128)(2,1)} %get-tuple-element.8), channel_id=1, source_target_pairs={{0,24},{8,16},{16,8},{24,0},{1,25},{9,17},{17,9},{25,1},{2,26},{10... | collective-permute-start | bytes 1216520 | tf_op jit(solution)/shard_map/ppermute | solution.py:23
  104.5 19.3 %collective-permute-start.3 = (bf16[528,384]{1,0:T(8,128)(2,1)S(1)}, bf16[528,384]{1,0:T(8,128)(2,1)S(1)}, u32[]{:S(2)}, u32[]{:S(2)}) collective-permute-start(bf16[528,384]{1,0:T(8,128)(2,1)S(1)} %get-tuple-element.9), channel_id=1, source_target_pairs={{0,16},{8,24},{16,0},{24,8},{1,17},{9,25},{17,1},{25,9},{2,18},{10... | collective-permute-start | bytes 1216520 | tf_op jit(solution)/shard_map/ppermute | solution.py:23
  105.6 18.2 %collective-permute-start.2 = (bf16[528,384]{1,0:T(8,128)(2,1)S(1)}, bf16[528,384]{1,0:T(8,128)(2,1)S(1)}, u32[]{:S(2)}, u32[]{:S(2)}) collective-permute-start(bf16[528,384]{1,0:T(8,128)(2,1)S(1)} %get-tuple-element.10), channel_id=1, source_target_pairs={{0,8},{8,0},{16,24},{24,16},{1,9},{9,1},{17,25},{25,17},{2,10},{10... | collective-permute-start | bytes 1216520 | tf_op jit(solution)/shard_map/ppermute | solution.py:23
  115.3 8.5 %copy-start.8 = (bf16[528,384]{1,0:T(8,128)(2,1)}, bf16[528,384]{1,0:T(8,128)(2,1)S(1)}, u32[]{:S(2)}) copy-start(bf16[528,384]{1,0:T(8,128)(2,1)S(1)} %collective-permute-done.4.refs_5_.refs_3_) | copy-start | bytes 1216516
  123.8 0.7 copy-start.1
  124.5 0.8 copy-start.3
  125.3 29.4 %copy-start.2 = (bf16[528,384]{1,0:T(8,128)(2,1)S(1)}, bf16[528,384]{1,0:T(8,128)(2,1)}, u32[]{:S(2)}) copy-start(bf16[528,384]{1,0:T(8,128)(2,1)} %copy-done.1) | copy-start | bytes 1216516
  125.3 29.4 %copy-start.4 = (bf16[528,384]{1,0:T(8,128)(2,1)S(1)}, bf16[528,384]{1,0:T(8,128)(2,1)}, u32[]{:S(2)}) copy-start(bf16[528,384]{1,0:T(8,128)(2,1)} %copy-done.3) | copy-start | bytes 1216516
  125.3 29.4 %copy-start.9 = (bf16[528,384]{1,0:T(8,128)(2,1)S(1)}, bf16[528,384]{1,0:T(8,128)(2,1)}, u32[]{:S(2)}) copy-start(bf16[528,384]{1,0:T(8,128)(2,1)} %copy-done.8) | copy-start | bytes 1216516
  125.3 14.5 %collective-permute-start.13 = (bf16[4,2,96,384]{3,2,1,0:T(8,128)(2,1)}, bf16[4,2,96,384]{3,2,1,0:T(8,128)(2,1)}, u32[]{:S(2)}, u32[]{:S(2)}) collective-permute-start(bf16[4,2,96,384]{3,2,1,0:T(8,128)(2,1)} %after.7), channel_id=1, source_target_pairs={{0,16},{8,24},{16,0},{24,8},{1,17},{9,25},{17,1},{25,9},{2,18},{10... | collective-permute-start | bytes 1769480 | tf_op jit(solution)/shard_map/ppermute | solution.py:23
  127.0 15.8 %collective-permute-start.10 = (bf16[4,2,96,384]{3,2,1,0:T(8,128)(2,1)}, bf16[4,2,96,384]{3,2,1,0:T(8,128)(2,1)S(1)}, u32[]{:S(2)}, u32[]{:S(2)}) collective-permute-start(bf16[4,2,96,384]{3,2,1,0:T(8,128)(2,1)} %after.7), channel_id=1, source_target_pairs={{0,8},{8,0},{16,24},{24,16},{1,9},{9,1},{17,25},{25,17},{2,10},{10... | collective-permute-start | bytes 1769480 | tf_op jit(solution)/shard_map/ppermute | solution.py:23
  127.4 12.3 %copy-start.11 = (bf16[2,5,96,384]{3,2,1,0:T(8,128)(2,1)}, bf16[2,5,96,384]{3,2,1,0:T(8,128)(2,1)S(1)}, u32[]{:S(2)}) copy-start(bf16[2,5,96,384]{3,2,1,0:T(8,128)(2,1)S(1)} %collective-permute-done.19) | copy-start | bytes 2211844
  129.1 23.3 %collective-permute-start.20 = (bf16[1,5,96,384]{3,2,1,0:T(8,128)(2,1)S(1)}, bf16[1,5,96,384]{3,2,1,0:T(8,128)(2,1)S(1)}, u32[]{:S(2)}, u32[]{:S(2)}) collective-permute-start(bf16[1,5,96,384]{3,2,1,0:T(8,128)(2,1)S(1)} %add_convert_fusion), channel_id=1, source_target_pairs={{0,6},{1,7},{2,4},{3,5},{4,2},{5,3},{6,0},{7,1},{8,14},{9,15},{10,... | collective-permute-start | bytes 1105928 | tf_op jit(solution)/shard_map/ppermute | solution.py:23
  140.8 7.7 %collective-permute-start.14 = (bf16[2,2,96,384]{3,2,1,0:T(8,128)(2,1)S(1)}, bf16[2,2,96,384]{3,2,1,0:T(8,128)(2,1)S(1)}, u32[]{:S(2)}, u32[]{:S(2)}) collective-permute-start(bf16[2,2,96,384]{3,2,1,0:T(8,128)(2,1)S(1)} %slice.83), channel_id=1, source_target_pairs={{0,8},{8,0},{16,24},{24,16},{1,9},{9,1},{17,25},{25,17},{2,10},{10... | collective-permute-start | bytes 884744 | tf_op jit(solution)/shard_map/ppermute | solution.py:23
  142.9 7.9 %collective-permute-start.11 = (bf16[2,2,96,384]{3,2,1,0:T(8,128)(2,1)S(1)}, bf16[2,2,96,384]{3,2,1,0:T(8,128)(2,1)S(1)}, u32[]{:S(2)}, u32[]{:S(2)}) collective-permute-start(bf16[2,2,96,384]{3,2,1,0:T(8,128)(2,1)S(1)} %slice.82), channel_id=1, source_target_pairs={{0,16},{8,24},{16,0},{24,8},{1,17},{9,25},{17,1},{25,9},{2,18},{10... | collective-permute-start | bytes 884744 | tf_op jit(solution)/shard_map/ppermute | solution.py:23
  143.3 23.4 %collective-permute-start.17 = (bf16[4,2,96,384]{3,2,1,0:T(8,128)(2,1)}, bf16[4,2,96,384]{3,2,1,0:T(8,128)(2,1)}, u32[]{:S(2)}, u32[]{:S(2)}) collective-permute-start(bf16[4,2,96,384]{3,2,1,0:T(8,128)(2,1)} %collective-permute-done.13.refs_6_), channel_id=1, source_target_pairs={{0,1},{1,0},{2,3},{3,2},{4,5},{5,4},{6,7},{7,6},{8,9},{9,8},{10,11... | collective-permute-start | bytes 1769480 | tf_op jit(solution)/shard_map/ppermute | solution.py:23
  145.2 21.5 %collective-permute-start.16 = (bf16[4,2,96,384]{3,2,1,0:T(8,128)(2,1)S(1)}, bf16[4,2,96,384]{3,2,1,0:T(8,128)(2,1)}, u32[]{:S(2)}, u32[]{:S(2)}) collective-permute-start(bf16[4,2,96,384]{3,2,1,0:T(8,128)(2,1)S(1)} %collective-permute-done.10.refs_4_), channel_id=1, source_target_pairs={{0,1},{1,0},{2,3},{3,2},{4,5},{5,4},{6,7},{7,6},{8,9},{9,8},{10,11... | collective-permute-start | bytes 1769480 | tf_op jit(solution)/shard_map/ppermute | solution.py:23
  148.5 28.2 %collective-permute-start.15 = (bf16[2,2,96,384]{3,2,1,0:T(8,128)(2,1)S(1)}, bf16[2,2,96,384]{3,2,1,0:T(8,128)(2,1)S(1)}, u32[]{:S(2)}, u32[]{:S(2)}) collective-permute-start(bf16[2,2,96,384]{3,2,1,0:T(8,128)(2,1)S(1)} %collective-permute-done.14.refs_6_), channel_id=1, source_target_pairs={{0,1},{1,0},{2,3},{3,2},{4,5},{5,4},{6,7},{7,6},{8,9},{9,8},{10,11... | collective-permute-start | bytes 884744 | tf_op jit(solution)/shard_map/ppermute | solution.py:23
  150.8 25.9 %collective-permute-start.12 = (bf16[2,2,96,384]{3,2,1,0:T(8,128)(2,1)S(1)}, bf16[2,2,96,384]{3,2,1,0:T(8,128)(2,1)S(1)}, u32[]{:S(2)}, u32[]{:S(2)}) collective-permute-start(bf16[2,2,96,384]{3,2,1,0:T(8,128)(2,1)S(1)} %collective-permute-done.11.refs_4_), channel_id=1, source_target_pairs={{0,1},{1,0},{2,3},{3,2},{4,5},{5,4},{6,7},{7,6},{8,9},{9,8},{10,11... | collective-permute-start | bytes 884744 | tf_op jit(solution)/shard_map/ppermute | solution.py:23
Sparse Core Ops, SparseCore 0:
  9.6 24.1 all-gather.4
  35.5 68.5 all-gather.6

commit v5 on v4

--- a/solution.py
+++ b/solution.py
@@ -10,7 +10,7 @@
 
 HALO = 8
 LANES = 128
-SPLIT = 2
+SPLIT = 3
 ROOT = math.sqrt(2.0 / math.pi)
 CUBIC = 0.044715
 ANYWHERE = pl.BlockSpec(memory_space=pl.ANY)
@@ -293,176 +293,179 @@
     return outs[0], outs[1].astype(jnp.bfloat16)
 
 
-def owner_of(owner, rep):
-    if isinstance(owner, int):
-        return owner
-    plane, flip = owner
-    return 2 * plane + (rep % 2 ^ flip)
-
-
-def input_terms(place, grads, entries, first_tap, sums, inputs, reps):
-    arrays, index = [], {}
-    for array, *_ in entries:
-        if id(array) not in index:
-            index[id(array)] = len(arrays)
-            arrays.append(array)
-    distances = sorted({entry[2] for entry in entries})
+def shifted_total(products, first_tap, taps, base, step, lanes, parity):
+    total = None
+    for by in (0, 1, -1):
+        wanted = [k for k in range(taps) if ROW_OFFSETS[first_tap + k][parity] == by]
+        if wanted:
+            part = sum(products[k, pl.ds(base, step + 2 * HALO), lanes] for k in wanted)
+            part = part[HALO + by : HALO + by + step]
+            total = part if total is None else total + part
+    return total
+
+
+def start_products(place, own, kernel_ref, gv, wv, sems, grad_sems):
+    seqs, block = len(own), own[0].shape[1]
+    for distance in range(seqs):
+        spot = pl.ds(pl.multiple_of((place[0] ^ distance) * block, block), block)
+        pltpu.make_async_copy(own[distance], gv.at[:, spot], grad_sems.at[distance]).start()
+    for k in range(wv.shape[0]):
+        for s in range(seqs):
+            kernel_copy(kernel_ref, wv, sems, k, s, block).start()
+
+
+def kernel_copy(kernel_ref, wv, sems, k, s, block):
+    target = wv.at[k, :, :, pl.ds(s * block, block)]
+    return pltpu.make_async_copy(kernel_ref.at[:, s, k], target, sems.at[k, s])
+
+
+def finish_products(own, kernel_ref, gv, wv, products, sems, grad_sems):
+    seqs, block = len(own), own[0].shape[1]
+    taps, reps, rows, depth = wv.shape
+    for distance in range(seqs):
+        spot = pl.ds(distance * block, block)
+        pltpu.make_async_copy(own[distance], gv.at[:, spot], grad_sems.at[distance]).wait()
+    tile = reps // 2
+
+    @pl.loop(0, taps)
+    def _(k):
+        for s in range(seqs):
+            kernel_copy(kernel_ref, wv, sems, k, s, block).wait()
+        for part in range(2):
+            kernel = wv[k, part * tile : (part + 1) * tile].reshape(tile * rows, depth)
+            products[k, :, part * tile * rows : (part + 1) * tile * rows] = lax.dot_general(
+                gv[...], kernel, (((1,), (1,)), ((), ())), preferred_element_type=jnp.float32
+            )
+
+
+STEP = 64
+
+
+def early_gradient(place, inputs, grads, kernel, first_tap):
     window, block = grads[0].shape
-    coarse = window - 2 * HALO
-    taps, rows = arrays[0].shape[-3:-1]
-    width, depth = reps * rows, len(distances) * block
-    last, begun = inputs is not None, sums is not None
-    shown = width // block if last else 0
-    used = list(range(len(grads))) if last else distances
-    tile, step = reps // 2, 64
-    operands = [grads[d] for d in used] + arrays
-    if begun:
-        operands.append(sums)
-    if last:
-        operands.append(inputs)
-
-    def kernel(place, *refs):
-        own = refs[: len(used)]
-        pieces = refs[len(used) : len(used) + len(arrays)]
-        refs = refs[len(used) + len(arrays) :]
-        if begun:
-            sums_ref, refs = refs[0], refs[1:]
-        if last:
-            x_ref, refs = refs[0], refs[1:]
-        out_ref, refs = refs[0], refs[1:]
-        wv, gv, products, sems, grad_sems = refs[:5]
-        refs = refs[5:]
-        if last:
-            skips, fine, again, skip_sems, sum_sem, held = refs
-        me, rep = place[0], place[1]
-        copies, skip_copies = [], []
-        for slot, distance in enumerate(distances):
-            spot = pl.ds(slot * block, block)
-            source = own[used.index(distance)]
-            copies.append(pltpu.make_async_copy(source, gv.at[:, spot], grad_sems.at[slot]))
-        for number, (array, at, distance, owner) in enumerate(entries):
-            spot = pl.ds(distances.index(distance) * block, block)
-            source = pieces[index[id(array)]].at[at]
-            target = wv.at[:, owner_of(owner, rep), :, spot]
-            copies.append(pltpu.make_async_copy(source, target, sems.at[number]))
-        if last:
-            for slot in range(len(used)):
-                copy = pltpu.make_async_copy(own[slot], skips.at[me ^ slot], skip_sems.at[slot])
-                skip_copies.append(copy)
-            skip_copies.append(pltpu.make_async_copy(sums_ref, held, sum_sem))
-        for copy in copies + skip_copies:
-            copy.start()
-        for copy in copies:
-            copy.wait()
-
-        @pl.loop(0, taps)
-        def _(k):
-            for part in range(reps // tile):
-                kernel = wv[k, part * tile : (part + 1) * tile].reshape(tile * rows, depth)
-                products[k, :, part * tile * rows : (part + 1) * tile * rows] = lax.dot_general(
-                    gv[...], kernel, (((1,), (1,)), ((), ())), preferred_element_type=jnp.float32
-                )
-
-        for copy in skip_copies:
-            copy.wait()
-
-        @pl.loop(0, coarse // step)
+    coarse, width = window - 2 * HALO, inputs.shape[2]
+    reps, seqs, taps, rows, _ = kernel.shape
+    depth, shape = seqs * block, (2, coarse, width)
+
+    def body(place, x_ref, *refs):
+        own, kernel_ref, out_ref, slope_ref = refs[:seqs], refs[seqs], refs[seqs + 1], refs[seqs + 2]
+        wv, gv, products, strip, sems, grad_sems = refs[seqs + 3 :]
+        start_products(place, own, kernel_ref, gv, wv, sems, grad_sems)
+        finish_products(own, kernel_ref, gv, wv, products, sems, grad_sems)
+
+        @pl.loop(0, coarse // STEP)
         def _(i):
-            base = pl.multiple_of(i * step, step)
-            spot = pl.ds(base, step)
+            base = pl.multiple_of(i * STEP, STEP)
+            spot, span = pl.ds(base, STEP), pl.ds(pl.multiple_of(2 * base, 2 * STEP), 2 * STEP)
             for c in range(width // LANES):
                 lanes = slice(c * LANES, (c + 1) * LANES)
-                totals = []
+                strip[c] = 0.5 * gelu_slope(x_ref[0, span, lanes].astype(jnp.float32))
+                skip = gv[pl.ds(base, STEP + 2 * HALO), lanes].astype(jnp.float32)
+                skip = 0.5 * skip[HALO : HALO + STEP]
                 for parity in range(2):
-                    total = None
-                    if begun:
-                        total = (held if last else sums_ref)[parity, spot, lanes]
-                    for by in (0, 1, -1):
-                        wanted = [
-                            k for k in range(taps) if ROW_OFFSETS[first_tap + k][parity] == by
-                        ]
-                        if not wanted:
-                            continue
-                        part = sum(
-                            products[k, pl.ds(base, step + 2 * HALO), lanes] for k in wanted
-                        )
-                        part = part[HALO + by : HALO + by + step]
-                        total = part if total is None else total + part
-                    totals.append(total)
-                if not last:
-                    out_ref[0, spot, lanes], out_ref[1, spot, lanes] = totals
-                    continue
-                place_c = c * LANES // block, slice(c * LANES % block, c * LANES % block + LANES)
-                skip = skips[place_c[0], pl.ds(base, step + 2 * HALO), place_c[1]]
-                skip = skip.astype(jnp.float32)[HALO : HALO + step]
-                for parity in range(2):
-                    fine[c, pl.ds(parity, step, stride=2), :] = totals[parity]
-                    again[c, pl.ds(parity, step, stride=2), :] = skip
-                span = pl.ds(pl.multiple_of(2 * base, 2 * step), 2 * step)
-                slope = gelu_slope(x_ref[0, span, lanes].astype(jnp.float32))
-                out_ref[0, span, lanes] = (0.5 * (fine[c] * slope + again[c])).astype(jnp.bfloat16)
-
-    scratch = [
-        pltpu.VMEM((taps, reps, rows, depth), jnp.bfloat16),
-        pltpu.VMEM((window, depth), jnp.bfloat16),
-        pltpu.VMEM((taps, window, width), jnp.float32),
-        pltpu.SemaphoreType.DMA((len(entries),)),
-        pltpu.SemaphoreType.DMA((len(distances),)),
-    ]
-    in_specs = [ANYWHERE] * (len(used) + len(arrays))
-    sums_shape = (2, coarse, width)
-    sums_spec = pl.BlockSpec(sums_shape, lambda i, place: (0, 0, 0))
-    if begun:
-        in_specs.append(ANYWHERE if last else sums_spec)
-    if last:
-        in_specs.append(pl.BlockSpec(inputs.shape, lambda i, place: (0, 0, 0)))
-        out_shape, out_spec = jax.ShapeDtypeStruct(inputs.shape, jnp.bfloat16), in_specs[-1]
-        strip = pltpu.VMEM((width // LANES, 2 * step, LANES), jnp.float32)
-        scratch += [
-            pltpu.VMEM((len(used), window, block), jnp.bfloat16),
-            strip,
-            strip,
-            pltpu.SemaphoreType.DMA((len(used),)),
-            pltpu.SemaphoreType.DMA,
-            pltpu.VMEM(sums_shape, jnp.float32),
-        ]
-    else:
-        out_shape, out_spec = jax.ShapeDtypeStruct(sums_shape, jnp.float32), sums_spec
+                    slope = strip[c, pl.ds(parity, STEP, stride=2), :]
+                    total = shifted_total(products, first_tap, taps, base, STEP, lanes, parity)
+                    slope_ref[parity, spot, lanes] = slope
+                    out_ref[parity, spot, lanes] = total * slope + skip
+
+    whole = pl.BlockSpec(shape, lambda i, place: (0, 0, 0))
     return pl.pallas_call(
-        kernel,
-        out_shape=out_shape,
+        body,
+        out_shape=[jax.ShapeDtypeStruct(shape, jnp.float32)] * 2,
         grid_spec=pltpu.PrefetchScalarGridSpec(
             num_scalar_prefetch=1,
             grid=(1,),
-            in_specs=in_specs,
-            out_specs=out_spec,
-            scratch_shapes=scratch,
+            in_specs=[pl.BlockSpec(inputs.shape, lambda i, place: (0, 0, 0))]
+            + [ANYWHERE] * (seqs + 1),
+            out_specs=[whole, whole],
+            scratch_shapes=[
+                pltpu.VMEM((taps, reps, rows, depth), jnp.bfloat16),
+                pltpu.VMEM((window, depth), jnp.bfloat16),
+                pltpu.VMEM((taps, window, width), jnp.float32),
+                pltpu.VMEM((width // LANES, 2 * STEP, LANES), jnp.float32),
+                pltpu.SemaphoreType.DMA((taps, seqs)),
+                pltpu.SemaphoreType.DMA((seqs,)),
+            ],
         ),
         compiler_params=pltpu.CompilerParams(vmem_limit_bytes=52 << 20),
         cost_estimate=pl.CostEstimate(
-            flops=2 * taps * window * width * depth,
-            bytes_accessed=20 << 20,
-            transcendentals=0,
-        ),
-        name="input_grad_late" if last else "input_grad_early",
-    )(place, *operands)
-
-
-def input_gradient_unaligned(place, inputs, grads, parts, taps, reps):
+            flops=2 * taps * window * width * depth, bytes_accessed=20 << 20, transcendentals=0
+        ),
+        name="input_grad_early",
+    )(place, inputs, *grads, kernel)
+
+
+def late_gradient(place, grads, kernel, first_tap, begun, slope, like):
+    window, block = grads[0].shape
+    coarse, width = window - 2 * HALO, like.shape[2]
+    reps, seqs, taps, rows, _ = kernel.shape
+    depth, shape = seqs * block, (2, coarse, width)
+
+    def body(place, *refs):
+        own, kernel_ref, begun_ref, slope_ref, out_ref = refs[:seqs], *refs[seqs : seqs + 4]
+        wv, gv, products, begun, slope, strip, sems, grad_sems, early_sems = refs[seqs + 4 :]
+        start_products(place, own, kernel_ref, gv, wv, sems, grad_sems)
+        copies = [
+            pltpu.make_async_copy(begun_ref, begun, early_sems.at[0]),
+            pltpu.make_async_copy(slope_ref, slope, early_sems.at[1]),
+        ]
+        for copy in copies:
+            copy.start()
+        finish_products(own, kernel_ref, gv, wv, products, sems, grad_sems)
+        for copy in copies:
+            copy.wait()
+
+        @pl.loop(0, coarse // STEP)
+        def _(i):
+            base = pl.multiple_of(i * STEP, STEP)
+            spot, span = pl.ds(base, STEP), pl.ds(pl.multiple_of(2 * base, 2 * STEP), 2 * STEP)
+            for c in range(width // LANES):
+                lanes = slice(c * LANES, (c + 1) * LANES)
+                for parity in range(2):
+                    total = shifted_total(products, first_tap, taps, base, STEP, lanes, parity)
+                    strip[c, pl.ds(parity, STEP, stride=2), :] = (
+                        begun[parity, spot, lanes] + total * slope[parity, spot, lanes]
+                    )
+                out_ref[0, span, lanes] = strip[c].astype(jnp.bfloat16)
+
+    return pl.pallas_call(
+        body,
+        out_shape=jax.ShapeDtypeStruct(like.shape, jnp.bfloat16),
+        grid_spec=pltpu.PrefetchScalarGridSpec(
+            num_scalar_prefetch=1,
+            grid=(1,),
+            in_specs=[ANYWHERE] * (seqs + 3),
+            out_specs=pl.BlockSpec(like.shape, lambda i, place: (0, 0, 0)),
+            scratch_shapes=[
+                pltpu.VMEM((taps, reps, rows, depth), jnp.bfloat16),
+                pltpu.VMEM((window, depth), jnp.bfloat16),
+                pltpu.VMEM((taps, window, width), jnp.float32),
+                pltpu.VMEM(shape, jnp.float32),
+                pltpu.VMEM(shape, jnp.float32),
+                pltpu.VMEM((width // LANES, 2 * STEP, LANES), jnp.float32),
+                pltpu.SemaphoreType.DMA((taps, seqs)),
+                pltpu.SemaphoreType.DMA((seqs,)),
+                pltpu.SemaphoreType.DMA((2,)),
+            ],
+        ),
+        compiler_params=pltpu.CompilerParams(vmem_limit_bytes=52 << 20),
+        cost_estimate=pl.CostEstimate(
+            flops=2 * taps * window * width * depth, bytes_accessed=20 << 20, transcendentals=0
+        ),
+        name="input_grad_late",
+    )(place, *grads, kernel, begun, slope)
+
+
+def input_gradient_unaligned(place, inputs, grads, kernel):
     seqs = len(grads)
     window, block = grads[0].shape
     coarse, width = window - 2 * HALO, inputs.shape[2]
-    rows = width // reps
     grad = jnp.zeros((window, seqs * block), jnp.bfloat16)
     for distance in range(seqs):
         spot = (0, (place[0] ^ distance) * block)
         grad = lax.dynamic_update_slice(grad, grads[distance], spot)
-    kernel = jnp.zeros((taps, width, seqs * block), jnp.bfloat16)
-    for first_tap, entries in parts:
-        for array, at, distance, owner in entries:
-            row = owner_of(owner, place[1]) * rows
-            spot = (first_tap, row, (place[0] ^ distance) * block)
-            kernel = lax.dynamic_update_slice(kernel, array[at], spot)
+    taps = kernel.shape[2]
+    kernel = kernel.transpose(2, 0, 3, 1, 4).reshape(taps, width, seqs * block)
     products = lax.dot_general(
         grad, kernel, (((1,), (2,)), ((), ())), preferred_element_type=jnp.float32
     )
@@ -488,18 +491,14 @@
     coarse, planes = fine // 2, reps // 2
     aligned = block % LANES == 0
 
-    last_taps = weights[SPLIT:]
-    across = jnp.stack(
-        [last_taps] + [from_peer(last_taps, "seq", d) for d in range(1, seqs)]
-    )
-    last = lax.all_gather(across, "rep")
-    last_entries = [(last, (r, d), d, r) for r in range(reps) for d in range(seqs)]
+    first = lax.all_gather(weights[:SPLIT], ("rep", "seq")).reshape(reps, seqs, SPLIT, rows, block)
+    last = lax.all_gather(weights[SPLIT:], ("rep", "seq"))
+    last = last.reshape(reps, seqs, taps - SPLIT, rows, block)
 
     act = {0: (activate(inputs),)}
     act.update(gather_near(act[0][0], "seq"))
     near = [act[d][0] for d in act if d]
-    act.update(gather_far(act, "seq", across))
-    far = [part for d in act if len(act[d]) == 2 for part in act[d]]
+    act.update(gather_far(act, "seq"))
 
     trunk = trunk_grad[0]
     edged = after(jnp.pad(trunk, ((HALO, HALO), (0, 0))), *near)
@@ -507,24 +506,6 @@
     for distance in range(seqs):
         window = lax.dynamic_slice_in_dim(edged, (me ^ distance) * coarse, coarse + 2 * HALO, 0)
         grads.append(from_peer(window, "seq", distance) if distance else window)
-
-    first = lax.all_gather(weights[:SPLIT], "rep")
-    column = lax.dynamic_index_in_dim(
-        first.reshape(planes, 2, *first.shape[1:]), rep % 2, 1, keepdims=False
-    )
-    column = after(column, *far, *grads[1:])
-    kept = {0: (column,)}
-    kept.update(gather_near(column, "seq"))
-    kept.update(gather_far(kept, "seq"))
-    first_entries = [(first, r, 0, r) for r in range(reps)]
-    for distance, parts in kept.items():
-        plane = 0
-        for part in parts if distance else ():
-            other = from_peer(part, "rep", 1)
-            for at in range(part.shape[0]):
-                first_entries.append((part, at, distance, (plane, 0)))
-                first_entries.append((other, at, distance, (plane, 1)))
-                plane += 1
 
     zeros = jnp.zeros((1, block), jnp.bfloat16)
     later = jnp.concatenate([trunk[1:], zeros])
@@ -543,14 +524,11 @@
     weight_grad = reduce_line(summed, "rep", planes, 2)
 
     if aligned:
-        soon = [entry for entry in first_entries if len(kept[entry[2]]) == 1]
-        rest = [entry for entry in first_entries if len(kept[entry[2]]) == 2]
-        sums = input_terms(place, grads, last_entries, SPLIT, None, None, reps)
-        sums = input_terms(place, grads, soon, 0, sums, None, reps)
-        input_grad = input_terms(place, grads, rest, 0, sums, inputs, reps)
+        begun, slope = early_gradient(place, inputs, grads, first, 0)
+        input_grad = late_gradient(place, grads, last, SPLIT, begun, slope, inputs)
     else:
-        parts = ((0, first_entries), (SPLIT, last_entries))
-        input_grad = input_gradient_unaligned(place, inputs, grads, parts, taps, reps)
+        kernel = jnp.concatenate([first, last], axis=2)
+        input_grad = input_gradient_unaligned(place, inputs, grads, kernel)
     return (input_grad, weight_grad)
 
 

time: 196 us -> 194 us (0.990); the launches traced: 193 us -> 193 us
  waiting for transfers between devices: 64.5 us -> 89.9 us
  Pallas kernels: 57.6 us -> 47.2 us
  starting transfers between devices: 26.6 us -> 16.3 us
  other arithmetic: 13.3 us -> 6.36 us
  local copies, waits for them, and re-layouts: 16.8 us -> 19.2 us
    ppermute x21 -> x10, waiting for transfers between devices: 64.5 us -> 87.4 us  [from_peer(): return lax.ppermute(value, axis, [(i, i ^ distance) for i in range(peers)])]
    ppermute x21 -> x10, starting transfers between devices: 26.5 us -> 16.2 us  [from_peer(): return lax.ppermute(value, axis, [(i, i ^ distance) for i in range(peers)])]
    pallas_call x3 -> x2, Pallas kernels: 31.4 us -> 23.6 us  [the longest x1 15.3 us: early_gradient(): pl.pallas_call(body, out_shape=[jax.ShapeDtypeStruct(shape, jnp.float32)]...]
    unnamed x24 -> x34, local copies, waits for them, and re-layouts: 1.53 us -> 8.99 us
    slice x1, local copies, waits for them, and re-layouts: 3.98 us -> 0.55 us  [on_device(): later = jnp.concatenate([trunk[1:], zeros])]
    concatenate x1, other arithmetic: 5.94 us -> 3.02 us  [on_device(): shifts = jnp.concatenate([later, trunk, earlier], axis=1)]
    all_gather x2, waiting for transfers between devices: 0.01 us -> 2.42 us  [the longest x1 2.42 us: on_device(): last = lax.all_gather(weights[SPLIT:], ('rep', 'seq'))]
  transfers between devices with their start and end apart: 23 -> 12, of which waited for: 9 -> 8; matrix products, arithmetic and copies ran while one was open for 14% -> 8% of each run, Pallas kernels for 25% -> 20%
where the time goes in v5:
time: 194 us; the launch traced here: 193 us
  waiting for transfers between devices  89.9 us (46%)
  Pallas kernels  47.2 us (24%)
  local copies, waits for them, and re-layouts  19.2 us (10%)
  starting transfers between devices  16.3 us (8%)
  between operations  14.2 us (7%)
  other arithmetic  6.36 us (3%)
    ppermute x10, waiting for transfers between devices, from_peer(): return lax.ppermute(value, axis, [(i, i ^ distance) for i in range(peers)])  87.4 us
    ppermute x10, starting transfers between devices, from_peer(): return lax.ppermute(value, axis, [(i, i ^ distance) for i in range(peers)])  16.2 us
    pallas_call x1, Pallas kernels, early_gradient(): pl.pallas_call(body, out_shape=[jax.ShapeDtypeStruct(shape, jnp.float32)]...  15.3 us
    pallas_call x1, Pallas kernels, early_terms(): pl.pallas_call(kernel, out_shape=jax.ShapeDtypeStruct((both, columns), jn...  13.1 us
    unnamed x34, local copies, waits for them, and re-layouts  8.99 us
    pallas_call x1, Pallas kernels, late_terms(): pl.pallas_call(kernel, out_shape=(jax.ShapeDtypeStruct(shape, jnp.float32...  8.75 us
    pallas_call x1, Pallas kernels, late_gradient(): pl.pallas_call(body, out_shape=jax.ShapeDtypeStruct(like.shape, jnp.bfloa...  8.34 us
  transfers between devices with their start and end apart: 12, of which 8 were waited for; matrix products, arithmetic and copies ran while one was open for 8% of the time, Pallas kernels for 20%

profile of v5, /device:TPU:9, one launch (start us, length us, event | category | flops | bytes accessed | tf_op | source)
XLA Modules:
  0.0 193.1 jit_solution(18005878638847496134)
XLA Ops:
  7.2 0.0 all-gather.7.cloned.1.call-start
  7.2 1.6 slice.55
  8.9 0.0 all-gather.7.cloned.1.call-update
  8.9 0.0 all-gather.5.cloned.1.call-start
  8.9 1.6 slice.54
  10.6 1.4 copy-done.2
  12.0 1.8 act.1.refs_0_
  13.7 1.3 collective-permute-start
  15.0 1.2 collective-permute-start.1
  16.3 0.5 slice_bitcast_fusion.1
  16.8 40.1 %collective-permute-done.refs_1_ = bf16[512,1536]{1,0:T(8,128)(2,1)S(1)} collective-permute-done((bf16[512,1536]{1,0:T(8,128)(2,1)S(1)}, bf16[512,1536]{1,0:T(8,128)(2,1)S(1)}, u32[]{:S(2)}, u32[]{:S(2)}) %collective-permute-start) | collective-permute-done | bytes 1572896 | tf_op jit(solution)/shard_map/ppermute | solution.py:23
  57.0 1.0 slice.72
  57.9 1.2 collective-permute-start.5
  59.2 1.0 slice.73
  60.2 1.2 collective-permute-start.6
  61.4 3.0 %fusion.2.shifts_ref = bf16[2048,1152]{1,0:T(8,128)(2,1)} fusion(bf16[2047,384]{1,0:T(8,128)(2,1)S(1)} %get-tuple-element.17, bf16[2047,384]{1,0:T(8,128)(2,1)S(1)} %get-tuple-element.16, bf16[2048,384]{1,0:T(8,128)(2,1)S(1)} %bitcast.12), kind=kLoop, calls=%fused_computation.4 | loop fusion | flops 23592960 | bytes 9435648 | tf_op jit(solution)/shard_map/concatenate | solution.py:513
  64.4 0.1 pad_add_fusion.place
  64.5 1.4 copy-done.4
  65.9 13.1 %weight_grad_early.1.early_ref = f32[1536,1152]{1,0:T(8,128)} custom-call(s32[2]{0:T(128)S(1)} %pad_add_fusion.place, bf16[2048,1152]{1,0:T(8,128)(2,1)} %fusion.2.shifts_ref, bf16[512,1536]{1,0:T(8,128)(2,1)S(1)} %copy-done.4, bf16[512,1536]{1,0:T(8,128)(2,1)S(1)} %collective-permute-done.refs_1_, bf16[512,1536]{1,0:T(8,128)(2,1)S(1)} %collective-permute-done.1.refs_2_), custom_call_target="tpu_custom_call" | custom-call | flops 5435817984 | bytes 16777216 | tf_op jit(solution)/shard_map/weight_grad_early/pallas_call | solution.py:168
  79.0 4.6 %collective-permute-done.5.refs_0_ = bf16[256,1536]{1,0:T(8,128)(2,1)} collective-permute-done((bf16[256,1536]{1,0:T(8,128)(2,1)}, bf16[256,1536]{1,0:T(8,128)(2,1)}, u32[]{:S(2)}, u32[]{:S(2)}) %collective-permute-start.5) | collective-permute-done | bytes 786464 | tf_op jit(solution)/shard_map/ppermute | solution.py:23
  83.6 3.9 %collective-permute-done.6.refs_1_ = bf16[256,1536]{1,0:T(8,128)(2,1)} collective-permute-done((bf16[256,1536]{1,0:T(8,128)(2,1)}, bf16[256,1536]{1,0:T(8,128)(2,1)}, u32[]{:S(2)}, u32[]{:S(2)}) %collective-permute-start.6) | collective-permute-done | bytes 786464 | tf_op jit(solution)/shard_map/ppermute | solution.py:23
  87.5 8.8 %weight_grad_late.1 = (f32[4,5,96,384]{3,2,1,0:T(8,128)S(1)}, bf16[4,5,96,384]{3,2,1,0:T(8,128)(2,1)S(1)}) custom-call(s32[2]{0:T(128)S(1)} %pad_add_fusion.place, bf16[2048,1152]{1,0:T(8,128)(2,1)} %fusion.2.shifts_ref, f32[1536,1152]{1,0:T(8,128)} %weight_grad_early.1.early_ref, bf16[256,1536]{1,0:T(8,128)(2,1)} %collective-permute-done.5.refs_0_, ...), custom_call_target="tpu_custom_call" | custom-call | flops 1811939328 | bytes 16777216 | tf_op jit(solution)/shard_map/weight_grad_late/pallas_call | solution.py:241
  96.2 5.7 %collective-permute-start.7 = (bf16[4,5,96,384]{3,2,1,0:T(8,128)(2,1)S(1)}, bf16[4,5,96,384]{3,2,1,0:T(8,128)(2,1)S(1)}, u32[]{:S(2)}, u32[]{:S(2)}) collective-permute-start(bf16[4,5,96,384]{3,2,1,0:T(8,128)(2,1)S(1)} %get-tuple-element.9), channel_id=1, source_target_pairs={{0,1},{1,0},{2,3},{3,2},{4,5},{5,4},{6,7},{7,6},{8,9},{9,8},{10,11... | collective-permute-start | bytes 4423688 | tf_op jit(solution)/shard_map/ppermute | solution.py:23
  101.9 2.9 %collective-permute-done.7 = bf16[4,5,96,384]{3,2,1,0:T(8,128)(2,1)S(1)} collective-permute-done((bf16[4,5,96,384]{3,2,1,0:T(8,128)(2,1)S(1)}, bf16[4,5,96,384]{3,2,1,0:T(8,128)(2,1)S(1)}, u32[]{:S(2)}, u32[]{:S(2)}) %collective-permute-start.7) | collective-permute-done | bytes 1474592 | tf_op jit(solution)/shard_map/ppermute | solution.py:23
  104.8 0.2 add_convert_fusion.2
  105.0 0.1 pad_maximum_fusion
  105.1 0.3 collective-permute-start.8
  105.4 19.9 %collective-permute-done.8 = bf16[2,5,96,384]{3,2,1,0:T(8,128)(2,1)S(1)} collective-permute-done((bf16[2,5,96,384]{3,2,1,0:T(8,128)(2,1)S(1)}, bf16[2,5,96,384]{3,2,1,0:T(8,128)(2,1)S(1)}, u32[]{:S(2)}, u32[]{:S(2)}) %collective-permute-start.8) | collective-permute-done | bytes 737312 | tf_op jit(solution)/shard_map/ppermute | solution.py:23
  125.3 0.9 copy-done.15
  126.1 0.9 add_convert_fusion
  127.0 2.5 %collective-permute-start.9 = (bf16[1,5,96,384]{3,2,1,0:T(8,128)(2,1)}, bf16[1,5,96,384]{3,2,1,0:T(8,128)(2,1)}, u32[]{:S(2)}, u32[]{:S(2)}) collective-permute-start(bf16[1,5,96,384]{3,2,1,0:T(8,128)(2,1)} %add_convert_fusion), channel_id=1, source_target_pairs={{0,6},{1,7},{2,4},{3,5},{4,2},{5,3},{6,0},{7,1},{8,14},{9,15},{10,... | collective-permute-start | bytes 1105928 | tf_op jit(solution)/shard_map/ppermute | solution.py:23
  129.5 2.8 %pad.6.refs_0_ = bf16[2064,384]{1,0:T(8,128)(2,1)} pad(bf16[2048,384]{1,0:T(8,128)(2,1)} %bitcast.11, bf16[]{:T(256)} %constant.5.clone.1), padding=8_8x0_0 | pad | bytes 3158018 | tf_op jit(solution)/shard_map/jit(_pad)/pad | solution.py:504
  132.3 1.7 constant_dynamic-slice_fusion
  134.0 0.8 collective-permute-start.2
  134.8 0.1 collective-permute-start.3
  134.9 1.8 collective-permute-start.4
  136.7 15.7 %collective-permute-done.9 = bf16[1,5,96,384]{3,2,1,0:T(8,128)(2,1)} collective-permute-done((bf16[1,5,96,384]{3,2,1,0:T(8,128)(2,1)}, bf16[1,5,96,384]{3,2,1,0:T(8,128)(2,1)}, u32[]{:S(2)}, u32[]{:S(2)}) %collective-permute-start.9) | collective-permute-done | bytes 368672 | tf_op jit(solution)/shard_map/ppermute | solution.py:23
  152.4 2.2 %add_bitcast_fusion = f32[5,96,384]{2,1,0:T(8,128)} fusion(bf16[1,5,96,384]{3,2,1,0:T(8,128)(2,1)} %collective-permute-done.9, f32[4,5,96,384]{3,2,1,0:T(8,128)S(1)} %get-tuple-element.8, bf16[2,5,96,384]{3,2,1,0:T(8,128)(2,1)S(1)} %copy-done.16, bf16[4,5,96,384]{3,2,1,0:T(8,128)(2,1)} %copy-done.14), kind=kLoop, calls=%fused_computation.9 | loop fusion | flops 1105920 | bytes 2580480 | tf_op jit(solution)/shard_map/add | solution.py:79
  154.6 0.7 copy-done.5
  155.3 0.8 copy-done.8
  156.1 0.3 collective-permute-done.4.refs_3_
  156.4 0.8 copy-done.11
  157.2 1.0 copy-done.6
  158.2 1.0 copy-done.9
  159.2 1.0 copy-done.12
  160.2 15.3 %input_grad_early.1 = (f32[2,512,768]{2,1,0:T(8,128)}, f32[2,512,768]{2,1,0:T(8,128)}) custom-call(s32[2]{0:T(128)S(1)} %pad_add_fusion.place, bf16[1,1024,768]{2,1,0:T(8,128)(2,1)} %x_ref.3, bf16[528,384]{1,0:T(8,128)(2,1)S(1)} %get-tuple-element.15.refs_0_, bf16[528,384]{1,0:T(8,128)(2,1)S(1)} %copy-done.6, bf16[528,384]{1,0:T(8,128)(2,1)S(1)} %copy-done.9, ...), custom_call_target="tpu_custom_call" | custom-call | flops 3737124864 | bytes 20971520 | tf_op jit(solution)/shard_map/input_grad_early/pallas_call | solution.py:372
  175.5 2.4 %all-gather.5.cloned.1.call-done = bf16[64,96,384]{2,1,0:T(8,128)(2,1)} async-done(((bf16[2,96,384]{2,1,0:T(8,128)(2,1)}), bf16[64,96,384]{2,1,0:T(8,128)(2,1)}) %all-gather.5.cloned.1.call-update) | async-done | bytes 4718608 | tf_op jit(solution)/shard_map/all_gather | solution.py:495
  177.9 8.3 %input_grad_late.1 = bf16[1,1024,768]{2,1,0:T(8,128)(2,1)} custom-call(s32[2]{0:T(128)S(1)} %pad_add_fusion.place, bf16[528,384]{1,0:T(8,128)(2,1)S(1)} %get-tuple-element.15.refs_0_, bf16[528,384]{1,0:T(8,128)(2,1)S(1)} %copy-done.7, bf16[528,384]{1,0:T(8,128)(2,1)S(1)} %copy-done.10, bf16[528,384]{1,0:T(8,128)(2,1)S(1)} %copy-done.12, ...), custom_call_target="tpu_custom_call" | custom-call | flops 2491416576 | bytes 20971520 | tf_op jit(solution)/shard_map/input_grad_late/pallas_call | solution.py:431
  (31 shorter events, 0.1 us)
Async XLA Ops:
  7.2 150.0 %all-gather.7.cloned.1.call-start = ((), (), s32[]{:S(2)}) async-start(), calls=%async_computation.1 | async-start | bytes 7299072 | tf_op jit(solution)/shard_map/all_gather | solution.py:494
  8.9 169.0 %all-gather.5.cloned.1.call-start = ((), (), s32[]{:S(2)}) async-start(), calls=%async_computation | async-start | bytes 4866048 | tf_op jit(solution)/shard_map/all_gather | solution.py:495
  10.5 1.4 copy-start.2
  12.0 4.3 %copy-start.13 = (bf16[1,2048,384]{2,1,0:T(8,128)(2,1)S(1)}, bf16[1,2048,384]{2,1,0:T(8,128)(2,1)}, u32[]{:S(2)}) copy-start(bf16[1,2048,384]{2,1,0:T(8,128)(2,1)} %param.4) | copy-start | bytes 4718596
  13.7 3.1 %copy-start.3 = (bf16[512,1536]{1,0:T(8,128)(2,1)}, bf16[512,1536]{1,0:T(8,128)(2,1)S(1)}, u32[]{:S(2)}) copy-start(bf16[512,1536]{1,0:T(8,128)(2,1)S(1)} %act.1.refs_0_) | copy-start | bytes 4718596
  13.7 43.2 %collective-permute-start = (bf16[512,1536]{1,0:T(8,128)(2,1)S(1)}, bf16[512,1536]{1,0:T(8,128)(2,1)S(1)}, u32[]{:S(2)}, u32[]{:S(2)}) collective-permute-start(bf16[512,1536]{1,0:T(8,128)(2,1)S(1)} %act.1.refs_0_), channel_id=1, source_target_pairs={{0,8},{8,0},{16,24},{24,16},{1,9},{9,1},{17,25},{25,17},{2,10},{10... | collective-permute-start | bytes 4718600 | tf_op jit(solution)/shard_map/ppermute | solution.py:23
  15.0 44.2 %collective-permute-start.1 = (bf16[512,1536]{1,0:T(8,128)(2,1)S(1)}, bf16[512,1536]{1,0:T(8,128)(2,1)S(1)}, u32[]{:S(2)}, u32[]{:S(2)}) collective-permute-start(bf16[512,1536]{1,0:T(8,128)(2,1)S(1)} %act.1.refs_0_), channel_id=1, source_target_pairs={{0,16},{8,24},{16,0},{24,8},{1,17},{9,25},{17,1},{25,9},{2,18},{10... | collective-permute-start | bytes 4718600 | tf_op jit(solution)/shard_map/ppermute | solution.py:23
  57.0 7.5 %copy-start = (bf16[512,1536]{1,0:T(8,128)(2,1)}, bf16[512,1536]{1,0:T(8,128)(2,1)S(1)}, u32[]{:S(2)}) copy-start(bf16[512,1536]{1,0:T(8,128)(2,1)S(1)} %collective-permute-done.refs_1_) | copy-start | bytes 4718596
  57.9 25.6 %collective-permute-start.5 = (bf16[256,1536]{1,0:T(8,128)(2,1)}, bf16[256,1536]{1,0:T(8,128)(2,1)}, u32[]{:S(2)}, u32[]{:S(2)}) collective-permute-start(bf16[256,1536]{1,0:T(8,128)(2,1)} %slice.72), channel_id=1, source_target_pairs={{0,16},{8,24},{16,0},{24,8},{1,17},{9,25},{17,1},{25,9},{2,18},{10... | collective-permute-start | bytes 2359304 | tf_op jit(solution)/shard_map/ppermute | solution.py:23
  59.2 5.3 %copy-start.1 = (bf16[512,1536]{1,0:T(8,128)(2,1)}, bf16[512,1536]{1,0:T(8,128)(2,1)S(1)}, u32[]{:S(2)}) copy-start(bf16[512,1536]{1,0:T(8,128)(2,1)S(1)} %collective-permute-done.1.refs_2_) | copy-start | bytes 4718596
  60.2 27.3 %collective-permute-start.6 = (bf16[256,1536]{1,0:T(8,128)(2,1)}, bf16[256,1536]{1,0:T(8,128)(2,1)}, u32[]{:S(2)}, u32[]{:S(2)}) collective-permute-start(bf16[256,1536]{1,0:T(8,128)(2,1)} %slice.73), channel_id=1, source_target_pairs={{0,8},{8,0},{16,24},{24,16},{1,9},{9,1},{17,25},{25,17},{2,10},{10... | collective-permute-start | bytes 2359304 | tf_op jit(solution)/shard_map/ppermute | solution.py:23
  64.5 1.4 copy-start.4
  96.2 8.6 %collective-permute-start.7 = (bf16[4,5,96,384]{3,2,1,0:T(8,128)(2,1)S(1)}, bf16[4,5,96,384]{3,2,1,0:T(8,128)(2,1)S(1)}, u32[]{:S(2)}, u32[]{:S(2)}) collective-permute-start(bf16[4,5,96,384]{3,2,1,0:T(8,128)(2,1)S(1)} %get-tuple-element.9), channel_id=1, source_target_pairs={{0,1},{1,0},{2,3},{3,2},{4,5},{5,4},{6,7},{7,6},{8,9},{9,8},{10,11... | collective-permute-start | bytes 4423688 | tf_op jit(solution)/shard_map/ppermute | solution.py:23
  104.8 22.2 %copy-start.14 = (bf16[4,5,96,384]{3,2,1,0:T(8,128)(2,1)}, bf16[4,5,96,384]{3,2,1,0:T(8,128)(2,1)S(1)}, u32[]{:S(2)}) copy-start(bf16[4,5,96,384]{3,2,1,0:T(8,128)(2,1)S(1)} %collective-permute-done.7) | copy-start | bytes 4423684
  105.1 20.2 %collective-permute-start.8 = (bf16[2,5,96,384]{3,2,1,0:T(8,128)(2,1)S(1)}, bf16[2,5,96,384]{3,2,1,0:T(8,128)(2,1)S(1)}, u32[]{:S(2)}, u32[]{:S(2)}) collective-permute-start(bf16[2,5,96,384]{3,2,1,0:T(8,128)(2,1)S(1)} %pad_maximum_fusion), channel_id=1, source_target_pairs={{0,2},{1,3},{2,0},{3,1},{4,6},{5,7},{6,4},{7,5},{8,10},{9,11},{10,... | collective-permute-start | bytes 2211848 | tf_op jit(solution)/shard_map/ppermute | solution.py:23
  125.3 0.9 copy-start.15
  127.0 25.4 %collective-permute-start.9 = (bf16[1,5,96,384]{3,2,1,0:T(8,128)(2,1)}, bf16[1,5,96,384]{3,2,1,0:T(8,128)(2,1)}, u32[]{:S(2)}, u32[]{:S(2)}) collective-permute-start(bf16[1,5,96,384]{3,2,1,0:T(8,128)(2,1)} %add_convert_fusion), channel_id=1, source_target_pairs={{0,6},{1,7},{2,4},{3,5},{4,2},{5,3},{6,0},{7,1},{8,14},{9,15},{10,... | collective-permute-start | bytes 1105928 | tf_op jit(solution)/shard_map/ppermute | solution.py:23
  132.3 20.1 %copy-start.16 = (bf16[2,5,96,384]{3,2,1,0:T(8,128)(2,1)S(1)}, bf16[2,5,96,384]{3,2,1,0:T(8,128)(2,1)}, u32[]{:S(2)}) copy-start(bf16[2,5,96,384]{3,2,1,0:T(8,128)(2,1)} %copy-done.15) | copy-start | bytes 2211844
  134.0 20.6 %collective-permute-start.2 = (bf16[528,384]{1,0:T(8,128)(2,1)S(1)}, bf16[528,384]{1,0:T(8,128)(2,1)S(1)}, u32[]{:S(2)}, u32[]{:S(2)}) collective-permute-start(bf16[528,384]{1,0:T(8,128)(2,1)S(1)} %get-tuple-element.14), channel_id=1, source_target_pairs={{0,8},{8,0},{16,24},{24,16},{1,9},{9,1},{17,25},{25,17},{2,10},{10... | collective-permute-start | bytes 1216520 | tf_op jit(solution)/shard_map/ppermute | solution.py:23
  134.8 20.5 %collective-permute-start.3 = (bf16[528,384]{1,0:T(8,128)(2,1)S(1)}, bf16[528,384]{1,0:T(8,128)(2,1)S(1)}, u32[]{:S(2)}, u32[]{:S(2)}) collective-permute-start(bf16[528,384]{1,0:T(8,128)(2,1)S(1)} %get-tuple-element.13), channel_id=1, source_target_pairs={{0,16},{8,24},{16,0},{24,8},{1,17},{9,25},{17,1},{25,9},{2,18},{10... | collective-permute-start | bytes 1216520 | tf_op jit(solution)/shard_map/ppermute | solution.py:23
  134.9 21.5 %collective-permute-start.4 = (bf16[528,384]{1,0:T(8,128)(2,1)S(1)}, bf16[528,384]{1,0:T(8,128)(2,1)S(1)}, u32[]{:S(2)}, u32[]{:S(2)}) collective-permute-start(bf16[528,384]{1,0:T(8,128)(2,1)S(1)} %get-tuple-element.12), channel_id=1, source_target_pairs={{0,24},{8,16},{16,8},{24,0},{1,25},{9,17},{17,9},{25,1},{2,26},{10... | collective-permute-start | bytes 1216520 | tf_op jit(solution)/shard_map/ppermute | solution.py:23
  154.6 0.8 copy-start.5
  155.3 0.8 copy-start.8
  156.4 0.8 copy-start.11
  157.2 1.0 copy-start.6
  158.2 1.0 copy-start.9
  159.2 1.0 copy-start.12
  160.2 17.7 %copy-start.7 = (bf16[528,384]{1,0:T(8,128)(2,1)S(1)}, bf16[528,384]{1,0:T(8,128)(2,1)}, u32[]{:S(2)}) copy-start(bf16[528,384]{1,0:T(8,128)(2,1)} %copy-done.5) | copy-start | bytes 1216516
  160.2 17.7 %copy-start.10 = (bf16[528,384]{1,0:T(8,128)(2,1)S(1)}, bf16[528,384]{1,0:T(8,128)(2,1)}, u32[]{:S(2)}) copy-start(bf16[528,384]{1,0:T(8,128)(2,1)} %copy-done.8) | copy-start | bytes 1216516
Sparse Core Ops, SparseCore 0:
  10.9 94.4 all-gather.6
  108.3 69.5 all-gather.4

commit v6 on v5

--- a/solution.py
+++ b/solution.py
@@ -293,65 +293,105 @@
     return outs[0], outs[1].astype(jnp.bfloat16)
 
 
-def shifted_total(products, first_tap, taps, base, step, lanes, parity):
+STEP = 64
+
+
+def shifted_total(products, first_tap, taps, base, lanes, parity):
     total = None
     for by in (0, 1, -1):
         wanted = [k for k in range(taps) if ROW_OFFSETS[first_tap + k][parity] == by]
         if wanted:
-            part = sum(products[k, pl.ds(base, step + 2 * HALO), lanes] for k in wanted)
-            part = part[HALO + by : HALO + by + step]
+            part = sum(products[k, pl.ds(base, STEP + 2 * HALO), lanes] for k in wanted)
+            part = part[HALO + by : HALO + by + STEP]
             total = part if total is None else total + part
     return total
 
 
-def start_products(place, own, kernel_ref, gv, wv, sems, grad_sems):
-    seqs, block = len(own), own[0].shape[1]
-    for distance in range(seqs):
-        spot = pl.ds(pl.multiple_of((place[0] ^ distance) * block, block), block)
-        pltpu.make_async_copy(own[distance], gv.at[:, spot], grad_sems.at[distance]).start()
-    for k in range(wv.shape[0]):
-        for s in range(seqs):
-            kernel_copy(kernel_ref, wv, sems, k, s, block).start()
-
-
-def kernel_copy(kernel_ref, wv, sems, k, s, block):
-    target = wv.at[k, :, :, pl.ds(s * block, block)]
-    return pltpu.make_async_copy(kernel_ref.at[:, s, k], target, sems.at[k, s])
-
-
-def finish_products(own, kernel_ref, gv, wv, products, sems, grad_sems):
-    seqs, block = len(own), own[0].shape[1]
-    taps, reps, rows, depth = wv.shape
-    for distance in range(seqs):
-        spot = pl.ds(distance * block, block)
-        pltpu.make_async_copy(own[distance], gv.at[:, spot], grad_sems.at[distance]).wait()
-    tile = reps // 2
-
-    @pl.loop(0, taps)
-    def _(k):
-        for s in range(seqs):
-            kernel_copy(kernel_ref, wv, sems, k, s, block).wait()
-        for part in range(2):
-            kernel = wv[k, part * tile : (part + 1) * tile].reshape(tile * rows, depth)
-            products[k, :, part * tile * rows : (part + 1) * tile * rows] = lax.dot_general(
-                gv[...], kernel, (((1,), (1,)), ((), ())), preferred_element_type=jnp.float32
-            )
-
-
-STEP = 64
-
-
-def early_gradient(place, inputs, grads, kernel, first_tap):
+def gradient_stage(place, grads, run, pieces, begun, inputs, shape, last):
+    first_tap, taps = run
     window, block = grads[0].shape
-    coarse, width = window - 2 * HALO, inputs.shape[2]
-    reps, seqs, taps, rows, _ = kernel.shape
-    depth, shape = seqs * block, (2, coarse, width)
-
-    def body(place, x_ref, *refs):
-        own, kernel_ref, out_ref, slope_ref = refs[:seqs], refs[seqs], refs[seqs + 1], refs[seqs + 2]
-        wv, gv, products, strip, sems, grad_sems = refs[seqs + 3 :]
-        start_products(place, own, kernel_ref, gv, wv, sems, grad_sems)
-        finish_products(own, kernel_ref, gv, wv, products, sems, grad_sems)
+    _, fine, width = shape
+    coarse, seqs = fine // 2, len(grads)
+    rows = pieces[0][0].shape[-2]
+    planes = width // (2 * rows)
+    whole = pieces[0][3] is None
+    distances = list(range(seqs)) if whole else sorted({piece[3] for piece in pieces})
+    depth, planar = len(distances) * block, (2, coarse, width)
+    used = list(range(seqs)) if inputs is not None else distances
+    shown = width // block
+    operands = [grads[d] for d in used] + [piece[0] for piece in pieces]
+    operands += list(begun) if begun else [inputs]
+
+    def body(place, *refs):
+        own, refs = refs[: len(used)], refs[len(used) :]
+        sources, refs = refs[: len(pieces)], refs[len(pieces) :]
+        if begun:
+            begun_ref, slope_ref, out_ref = refs[:3]
+            wv, gv, products, strip, sems, grad_sems, sums, slopes, sum_sems = refs[3:]
+        else:
+            x_ref, out_ref, slope_ref = refs[:3]
+            wv, gv, products, strip, sems, grad_sems, skips, skip_sems = refs[3:]
+        me, core = place[0], place[1] % 2
+
+        def kernel_copy(number, k, s=None):
+            array, plane, flip, distance = pieces[number]
+            ref = sources[number]
+            if whole:
+                spot = pl.ds(s * block, block)
+                return pltpu.make_async_copy(
+                    ref.at[:, :, s, k], wv.at[k, :, :, :, spot], sems.at[k, number * seqs + s]
+                )
+            spot = pl.ds(distances.index(distance) * block, block)
+            if flip is None:
+                target = wv.at[k, :, :, :, spot]
+                return pltpu.make_async_copy(ref.at[:, :, k], target, sems.at[k, number])
+            span = pl.ds(plane, array.shape[0])
+            target = wv.at[k, span, core ^ flip, :, spot]
+            return pltpu.make_async_copy(ref.at[:, k], target, sems.at[k, number])
+
+        def kernel_copies(k):
+            for number in range(len(pieces)):
+                for s in range(seqs) if whole else (None,):
+                    yield kernel_copy(number, k, s)
+
+        early, late = [], []
+        for slot, distance in enumerate(distances):
+            left = (me ^ distance) * block if whole else slot * block
+            spot = pl.ds(pl.multiple_of(left, block), block)
+            source = own[used.index(distance)]
+            early.append(pltpu.make_async_copy(source, gv.at[:, spot], grad_sems.at[slot]))
+        if begun:
+            late.append(pltpu.make_async_copy(begun_ref, sums, sum_sems.at[0]))
+            late.append(pltpu.make_async_copy(slope_ref, slopes, sum_sems.at[1]))
+        else:
+            for d in used:
+                late.append(pltpu.make_async_copy(own[d], skips.at[me ^ d], skip_sems.at[d]))
+        for copy in early:
+            copy.start()
+        for k in range(taps):
+            for copy in kernel_copies(k):
+                copy.start()
+        for copy in late:
+            copy.start()
+        for copy in early:
+            copy.wait()
+
+        @pl.loop(0, taps)
+        def _(k):
+            for copy in kernel_copies(k):
+                copy.wait()
+            span = planes // 2 * 2 * rows
+            for part in range(2):
+                kernel = wv[k, part * (planes // 2) : (part + 1) * (planes // 2)]
+                products[k, :, part * span : (part + 1) * span] = lax.dot_general(
+                    gv[...],
+                    kernel.reshape(span, depth),
+                    (((1,), (1,)), ((), ())),
+                    preferred_element_type=jnp.float32,
+                )
+
+        for copy in late:
+            copy.wait()
 
         @pl.loop(0, coarse // STEP)
         def _(i):
@@ -359,101 +399,74 @@
             spot, span = pl.ds(base, STEP), pl.ds(pl.multiple_of(2 * base, 2 * STEP), 2 * STEP)
             for c in range(width // LANES):
                 lanes = slice(c * LANES, (c + 1) * LANES)
-                strip[c] = 0.5 * gelu_slope(x_ref[0, span, lanes].astype(jnp.float32))
-                skip = gv[pl.ds(base, STEP + 2 * HALO), lanes].astype(jnp.float32)
-                skip = 0.5 * skip[HALO : HALO + STEP]
+                if not begun:
+                    strip[c] = 0.5 * gelu_slope(x_ref[0, span, lanes].astype(jnp.float32))
+                    left = c * LANES % block
+                    skip = skips[
+                        c * LANES // block, pl.ds(base, STEP + 2 * HALO), left : left + LANES
+                    ].astype(jnp.float32)
+                    skip = 0.5 * skip[HALO : HALO + STEP]
                 for parity in range(2):
-                    slope = strip[c, pl.ds(parity, STEP, stride=2), :]
-                    total = shifted_total(products, first_tap, taps, base, STEP, lanes, parity)
-                    slope_ref[parity, spot, lanes] = slope
-                    out_ref[parity, spot, lanes] = total * slope + skip
-
-    whole = pl.BlockSpec(shape, lambda i, place: (0, 0, 0))
+                    total = shifted_total(products, first_tap, taps, base, lanes, parity)
+                    if begun:
+                        total = sums[parity, spot, lanes] + total * slopes[parity, spot, lanes]
+                    else:
+                        slope = strip[c, pl.ds(parity, STEP, stride=2), :]
+                        slope_ref[parity, spot, lanes] = slope
+                        total = total * slope + skip
+                    if last:
+                        strip[c, pl.ds(parity, STEP, stride=2), :] = total
+                    else:
+                        out_ref[parity, spot, lanes] = total
+                if last:
+                    out_ref[0, span, lanes] = strip[c].astype(jnp.bfloat16)
+
+    block_of = lambda shape: pl.BlockSpec(shape, lambda i, place: (0, 0, 0))
+    in_specs = [ANYWHERE] * (len(used) + len(pieces))
+    scratch = [
+        pltpu.VMEM((taps, planes, 2, rows, depth), jnp.bfloat16),
+        pltpu.VMEM((window, depth), jnp.bfloat16),
+        pltpu.VMEM((taps, window, width), jnp.float32),
+        pltpu.VMEM((width // LANES, 2 * STEP, LANES), jnp.float32),
+        pltpu.SemaphoreType.DMA((taps, len(pieces) * (seqs if whole else 1))),
+        pltpu.SemaphoreType.DMA((len(distances),)),
+    ]
+    planes_out = jax.ShapeDtypeStruct(planar, jnp.float32)
+    if begun:
+        in_specs += [ANYWHERE] * 2
+        scratch += [
+            pltpu.VMEM(planar, jnp.float32),
+            pltpu.VMEM(planar, jnp.float32),
+            pltpu.SemaphoreType.DMA((2,)),
+        ]
+    else:
+        in_specs.append(block_of(shape))
+        scratch += [
+            pltpu.VMEM((seqs, window, block), jnp.bfloat16),
+            pltpu.SemaphoreType.DMA((seqs,)),
+        ]
+    if last:
+        out_shape, out_specs = jax.ShapeDtypeStruct(shape, jnp.bfloat16), block_of(shape)
+    elif begun:
+        out_shape, out_specs = planes_out, block_of(planar)
+    else:
+        out_shape, out_specs = [planes_out] * 2, [block_of(planar)] * 2
     return pl.pallas_call(
         body,
-        out_shape=[jax.ShapeDtypeStruct(shape, jnp.float32)] * 2,
+        out_shape=out_shape,
         grid_spec=pltpu.PrefetchScalarGridSpec(
             num_scalar_prefetch=1,
             grid=(1,),
-            in_specs=[pl.BlockSpec(inputs.shape, lambda i, place: (0, 0, 0))]
-            + [ANYWHERE] * (seqs + 1),
-            out_specs=[whole, whole],
-            scratch_shapes=[
-                pltpu.VMEM((taps, reps, rows, depth), jnp.bfloat16),
-                pltpu.VMEM((window, depth), jnp.bfloat16),
-                pltpu.VMEM((taps, window, width), jnp.float32),
-                pltpu.VMEM((width // LANES, 2 * STEP, LANES), jnp.float32),
-                pltpu.SemaphoreType.DMA((taps, seqs)),
-                pltpu.SemaphoreType.DMA((seqs,)),
-            ],
-        ),
-        compiler_params=pltpu.CompilerParams(vmem_limit_bytes=52 << 20),
+            in_specs=in_specs,
+            out_specs=out_specs,
+            scratch_shapes=scratch,
+        ),
+        compiler_params=pltpu.CompilerParams(vmem_limit_bytes=56 << 20),
         cost_estimate=pl.CostEstimate(
             flops=2 * taps * window * width * depth, bytes_accessed=20 << 20, transcendentals=0
         ),
-        name="input_grad_early",
-    )(place, inputs, *grads, kernel)
-
-
-def late_gradient(place, grads, kernel, first_tap, begun, slope, like):
-    window, block = grads[0].shape
-    coarse, width = window - 2 * HALO, like.shape[2]
-    reps, seqs, taps, rows, _ = kernel.shape
-    depth, shape = seqs * block, (2, coarse, width)
-
-    def body(place, *refs):
-        own, kernel_ref, begun_ref, slope_ref, out_ref = refs[:seqs], *refs[seqs : seqs + 4]
-        wv, gv, products, begun, slope, strip, sems, grad_sems, early_sems = refs[seqs + 4 :]
-        start_products(place, own, kernel_ref, gv, wv, sems, grad_sems)
-        copies = [
-            pltpu.make_async_copy(begun_ref, begun, early_sems.at[0]),
-            pltpu.make_async_copy(slope_ref, slope, early_sems.at[1]),
-        ]
-        for copy in copies:
-            copy.start()
-        finish_products(own, kernel_ref, gv, wv, products, sems, grad_sems)
-        for copy in copies:
-            copy.wait()
-
-        @pl.loop(0, coarse // STEP)
-        def _(i):
-            base = pl.multiple_of(i * STEP, STEP)
-            spot, span = pl.ds(base, STEP), pl.ds(pl.multiple_of(2 * base, 2 * STEP), 2 * STEP)
-            for c in range(width // LANES):
-                lanes = slice(c * LANES, (c + 1) * LANES)
-                for parity in range(2):
-                    total = shifted_total(products, first_tap, taps, base, STEP, lanes, parity)
-                    strip[c, pl.ds(parity, STEP, stride=2), :] = (
-                        begun[parity, spot, lanes] + total * slope[parity, spot, lanes]
-                    )
-                out_ref[0, span, lanes] = strip[c].astype(jnp.bfloat16)
-
-    return pl.pallas_call(
-        body,
-        out_shape=jax.ShapeDtypeStruct(like.shape, jnp.bfloat16),
-        grid_spec=pltpu.PrefetchScalarGridSpec(
-            num_scalar_prefetch=1,
-            grid=(1,),
-            in_specs=[ANYWHERE] * (seqs + 3),
-            out_specs=pl.BlockSpec(like.shape, lambda i, place: (0, 0, 0)),
-            scratch_shapes=[
-                pltpu.VMEM((taps, reps, rows, depth), jnp.bfloat16),
-                pltpu.VMEM((window, depth), jnp.bfloat16),
-                pltpu.VMEM((taps, window, width), jnp.float32),
-                pltpu.VMEM(shape, jnp.float32),
-                pltpu.VMEM(shape, jnp.float32),
-                pltpu.VMEM((width // LANES, 2 * STEP, LANES), jnp.float32),
-                pltpu.SemaphoreType.DMA((taps, seqs)),
-                pltpu.SemaphoreType.DMA((seqs,)),
-                pltpu.SemaphoreType.DMA((2,)),
-            ],
-        ),
-        compiler_params=pltpu.CompilerParams(vmem_limit_bytes=52 << 20),
-        cost_estimate=pl.CostEstimate(
-            flops=2 * taps * window * width * depth, bytes_accessed=20 << 20, transcendentals=0
-        ),
-        name="input_grad_late",
-    )(place, *grads, kernel, begun, slope)
+        name="input_grad",
+    )(place, *operands)
 
 
 def input_gradient_unaligned(place, inputs, grads, kernel):
@@ -491,14 +504,15 @@
     coarse, planes = fine // 2, reps // 2
     aligned = block % LANES == 0
 
-    first = lax.all_gather(weights[:SPLIT], ("rep", "seq")).reshape(reps, seqs, SPLIT, rows, block)
+    first = lax.all_gather(weights[:SPLIT], "rep").reshape(planes, 2, SPLIT, rows, block)
     last = lax.all_gather(weights[SPLIT:], ("rep", "seq"))
-    last = last.reshape(reps, seqs, taps - SPLIT, rows, block)
+    last = last.reshape(planes, 2, seqs, taps - SPLIT, rows, block)
 
     act = {0: (activate(inputs),)}
     act.update(gather_near(act[0][0], "seq"))
     near = [act[d][0] for d in act if d]
     act.update(gather_far(act, "seq"))
+    far = [part for d in act if len(act[d]) == 2 for part in act[d]]
 
     trunk = trunk_grad[0]
     edged = after(jnp.pad(trunk, ((HALO, HALO), (0, 0))), *near)
@@ -507,16 +521,30 @@
         window = lax.dynamic_slice_in_dim(edged, (me ^ distance) * coarse, coarse + 2 * HALO, 0)
         grads.append(from_peer(window, "seq", distance) if distance else window)
 
+    column = lax.dynamic_index_in_dim(first, rep % 2, 1, keepdims=False)
+    column = after(column, *grads[1:])
+    kept = {0: (column,)}
+    kept.update(gather_near(column, "seq"))
+    kept.update(gather_far(kept, "seq"))
+    soon, rest = [(first, 0, None, 0)], []
+    for distance, parts in kept.items():
+        plane = 0
+        for part in parts if distance else ():
+            share = soon if len(parts) == 1 else rest
+            share.append((part, plane, 0, distance))
+            share.append((from_peer(part, "rep", 1), plane, 1, distance))
+            plane += part.shape[0]
+
     zeros = jnp.zeros((1, block), jnp.bfloat16)
     later = jnp.concatenate([trunk[1:], zeros])
     earlier = jnp.concatenate([zeros, trunk[:-1]])
     shifts = jnp.concatenate([later, trunk, earlier], axis=1)
     scale = 0.5 * float(fine * seqs * reps) ** (-0.5)
     if aligned:
-        soon = {d: act[d] for d in act if len(act[d]) == 1}
-        rest = {d: act[d] for d in act if len(act[d]) == 2}
-        early = early_terms(place, soon, shifts, coarse)
-        mine, theirs = late_terms(place, rest, shifts, early, coarse, scale, planes, taps, rows)
+        near = {d: act[d] for d in act if len(act[d]) == 1}
+        far = {d: tuple(after(p, *grads[1:]) for p in act[d]) for d in act if len(act[d]) == 2}
+        early = early_terms(place, near, shifts, coarse)
+        mine, theirs = late_terms(place, far, shifts, early, coarse, scale, planes, taps, rows)
     else:
         mine, theirs = terms_unaligned(place, act, shifts, coarse, scale, planes, taps, rows)
     arrived = from_peer(theirs, "rep", 1)
@@ -524,10 +552,17 @@
     weight_grad = reduce_line(summed, "rep", planes, 2)
 
     if aligned:
-        begun, slope = early_gradient(place, inputs, grads, first, 0)
-        input_grad = late_gradient(place, grads, last, SPLIT, begun, slope, inputs)
+        stage = functools.partial(gradient_stage, place, grads, shape=inputs.shape)
+        begun, slope = stage((0, SPLIT), soon, None, inputs, last=False)
+        begun = stage((SPLIT, taps - SPLIT), [(last, 0, None, None)], (begun, slope), None, last=False)
+        input_grad = stage((0, SPLIT), rest, (begun, slope), None, last=True)
     else:
-        kernel = jnp.concatenate([first, last], axis=2)
+        kernel = jnp.zeros((planes, 2, seqs, SPLIT, rows, block), jnp.bfloat16)
+        for part, plane, flip, distance in soon + rest:
+            part = part if flip is None else part[:, None]
+            spot = (plane, 0 if flip is None else rep % 2 ^ flip, me ^ distance, 0, 0, 0)
+            kernel = lax.dynamic_update_slice(kernel, part[:, :, None], spot)
+        kernel = jnp.concatenate([kernel, last], axis=3).reshape(reps, seqs, taps, rows, block)
         input_grad = input_gradient_unaligned(place, inputs, grads, kernel)
     return (input_grad, weight_grad)
 

time: 194 us -> 194 us (level)
  waiting for transfers between devices: 89.9 us -> 77.4 us
  Pallas kernels: 47.2 us -> 55.6 us
  starting transfers between devices: 16.3 us -> 22.2 us
  local copies, waits for them, and re-layouts: 19.2 us -> 16 us
    ppermute x10 -> x18, waiting for transfers between devices: 87.4 us -> 77.4 us  [from_peer(): return lax.ppermute(value, axis, [(i, i ^ distance) for i in range(peers)])]
    pallas_call x2 -> x3, Pallas kernels: 23.6 us -> 31.2 us  [gradient_stage(): pl.pallas_call(body, out_shape=out_shape, grid_spec=pltpu.PrefetchScalarG...]
    ppermute x10 -> x18, starting transfers between devices: 16.2 us -> 22.2 us  [from_peer(): return lax.ppermute(value, axis, [(i, i ^ distance) for i in range(peers)])]
    unnamed x34, local copies, waits for them, and re-layouts: 8.99 us -> 4.21 us
    all_gather x1, waiting for transfers between devices: 2.42 us -> 0.01 us  [on_device(): last = lax.all_gather(weights[SPLIT:], ('rep', 'seq'))]
    squeeze x0 -> x1, local copies, waits for them, and re-layouts: none -> 2.16 us  [on_device(): column = lax.dynamic_index_in_dim(first, rep % 2, 1, keepdims=False)]
  transfers between devices with their start and end apart: 12 -> 20, of which waited for: 8 -> 6; matrix products, arithmetic and copies ran while one was open for 8% -> 9% of each run, Pallas kernels for 20% -> 25%
where the time goes in v6:
time: 194 us; the launch traced here: 193 us
  waiting for transfers between devices  77.4 us (40%)
  Pallas kernels  55.6 us (29%)
  starting transfers between devices  22.2 us (11%)
  local copies, waits for them, and re-layouts  16 us (8%)
  between operations  14.2 us (7%)
  other arithmetic  7.47 us (4%)
    ppermute x18, waiting for transfers between devices, from_peer(): return lax.ppermute(value, axis, [(i, i ^ distance) for i in range(peers)])  77.4 us
    pallas_call x3, Pallas kernels, gradient_stage(): pl.pallas_call(body, out_shape=out_shape, grid_spec=pltpu.PrefetchScalarG...  31.2 us
    ppermute x18, starting transfers between devices, from_peer(): return lax.ppermute(value, axis, [(i, i ^ distance) for i in range(peers)])  22.2 us
    pallas_call x1, Pallas kernels, early_terms(): pl.pallas_call(kernel, out_shape=jax.ShapeDtypeStruct((both, columns), jn...  13 us
    pallas_call x1, Pallas kernels, late_terms(): pl.pallas_call(kernel, out_shape=(jax.ShapeDtypeStruct(shape, jnp.float32...  9.68 us
    unnamed x34, local copies, waits for them, and re-layouts  4.21 us
  transfers between devices with their start and end apart: 20, of which 6 were waited for; matrix products, arithmetic and copies ran while one was open for 9% of the time, Pallas kernels for 25%

profile of v6, /device:TPU:9, one launch (start us, length us, event | category | flops | bytes accessed | tf_op | source)
XLA Modules:
  0.0 192.9 jit_solution(16010608667042299900)
XLA Ops:
  7.2 1.6 slice.60
  8.9 1.6 slice.63
  10.5 1.4 copy-done.4
  11.9 1.8 act.1.refs_0_
  13.7 1.3 collective-permute-start
  15.0 1.2 collective-permute-start.1
  16.2 0.5 slice_bitcast_fusion.1
  16.8 32.3 %collective-permute-done.refs_1_ = bf16[512,1536]{1,0:T(8,128)(2,1)S(1)} collective-permute-done((bf16[512,1536]{1,0:T(8,128)(2,1)S(1)}, bf16[512,1536]{1,0:T(8,128)(2,1)S(1)}, u32[]{:S(2)}, u32[]{:S(2)}) %collective-permute-start) | collective-permute-done | bytes 1572896 | tf_op jit(solution)/shard_map/ppermute | solution.py:23
  49.1 1.0 slice.82
  50.0 1.2 collective-permute-start.13
  51.3 1.0 slice.83
  52.3 1.2 collective-permute-start.14
  53.5 3.0 %fusion.2.shifts_ref = bf16[2048,1152]{1,0:T(8,128)(2,1)} fusion(bf16[2047,384]{1,0:T(8,128)(2,1)S(1)} %get-tuple-element.17, bf16[2047,384]{1,0:T(8,128)(2,1)S(1)} %get-tuple-element.16, bf16[2048,384]{1,0:T(8,128)(2,1)S(1)} %bitcast.13), kind=kLoop, calls=%fused_computation.4 | loop fusion | flops 23592960 | bytes 9435648 | tf_op jit(solution)/shard_map/concatenate | solution.py:541
  56.5 1.3 pad.6.refs_0_
  57.8 0.1 pad_add_fusion.place
  57.9 2.5 %constant_dynamic-slice_fusion = (bf16[528,384]{1,0:T(8,128)(2,1)}, bf16[528,384]{1,0:T(8,128)(2,1)S(1)}, bf16[528,384]{1,0:T(8,128)(2,1)S(1)}, bf16[528,384]{1,0:T(8,128)(2,1)S(1)}) fusion(bf16[2064,384]{1,0:T(8,128)(2,1)} %after.4, s32[]{:T(128)S(6)} %select_n.28, s32[]{:T(128)S(6)} %select_n.27, s32[]{:T(128)S(6)} %select_n.26, s32[]{:T(128)S(6)} %select_n.23), kind=kLoop, calls=%fused_computation.14 | loop fusion | bytes 3244048 | tf_op jit(solution)/shard_map/dynamic_slice | solution.py:521
  60.4 0.2 collective-permute-start.2
  60.6 1.2 collective-permute-start.3
  61.8 1.2 collective-permute-start.4
  63.0 13.0 %weight_grad_early.1.early_ref = f32[1536,1152]{1,0:T(8,128)} custom-call(s32[2]{0:T(128)S(1)} %pad_add_fusion.place, bf16[2048,1152]{1,0:T(8,128)(2,1)} %fusion.2.shifts_ref, bf16[512,1536]{1,0:T(8,128)(2,1)S(1)} %copy-done.6, bf16[512,1536]{1,0:T(8,128)(2,1)S(1)} %copy-done.1, bf16[512,1536]{1,0:T(8,128)(2,1)S(1)} %copy-done.3), custom_call_target="tpu_custom_call" | custom-call | flops 5435817984 | bytes 16777216 | tf_op jit(solution)/shard_map/weight_grad_early/pallas_call | solution.py:168
  76.0 5.8 %collective-permute-done.2.refs_3_.refs_0_ = bf16[528,384]{1,0:T(8,128)(2,1)S(1)} collective-permute-done((bf16[528,384]{1,0:T(8,128)(2,1)S(1)}, bf16[528,384]{1,0:T(8,128)(2,1)S(1)}, u32[]{:S(2)}, u32[]{:S(2)}) %collective-permute-start.2) | collective-permute-done | bytes 405536 | tf_op jit(solution)/shard_map/ppermute | solution.py:23
  81.8 11.4 %collective-permute-done.3.refs_1_ = bf16[528,384]{1,0:T(8,128)(2,1)S(1)} collective-permute-done((bf16[528,384]{1,0:T(8,128)(2,1)S(1)}, bf16[528,384]{1,0:T(8,128)(2,1)S(1)}, u32[]{:S(2)}, u32[]{:S(2)}) %collective-permute-start.3) | collective-permute-done | bytes 405536 | tf_op jit(solution)/shard_map/ppermute | solution.py:23
  93.2 0.7 copy-done.10
  94.0 0.1 copy-done.11
  94.1 9.7 %weight_grad_late.1 = (f32[4,5,96,384]{3,2,1,0:T(8,128)S(1)}, bf16[4,5,96,384]{3,2,1,0:T(8,128)(2,1)}) custom-call(s32[2]{0:T(128)S(1)} %pad_add_fusion.place, bf16[2048,1152]{1,0:T(8,128)(2,1)} %fusion.2.shifts_ref, f32[1536,1152]{1,0:T(8,128)} %weight_grad_early.1.early_ref, bf16[256,1536]{1,0:T(8,128)(2,1)} %after.6.refs_0_, bf16[256,1536]{1,0:T(8,128)(2,1)} %after.7.refs_1_), custom_call_target="tpu_custom_call" | custom-call | flops 1811939328 | bytes 16777216 | tf_op jit(solution)/shard_map/weight_grad_late/pallas_call | solution.py:241
  103.8 7.5 %collective-permute-start.15 = (bf16[4,5,96,384]{3,2,1,0:T(8,128)(2,1)}, bf16[4,5,96,384]{3,2,1,0:T(8,128)(2,1)}, u32[]{:S(2)}, u32[]{:S(2)}) collective-permute-start(bf16[4,5,96,384]{3,2,1,0:T(8,128)(2,1)} %get-tuple-element.9), channel_id=1, source_target_pairs={{0,1},{1,0},{2,3},{3,2},{4,5},{5,4},{6,7},{7,6},{8,9},{9,8},{10,11... | collective-permute-start | bytes 4423688 | tf_op jit(solution)/shard_map/ppermute | solution.py:23
  111.3 2.2 %dynamic-slice_bitcast_fusion.refs_0_ = bf16[4,3,96,384]{3,2,1,0:T(8,128)(2,1)} fusion(bf16[4,2,3,96,384]{4,3,2,1,0:T(8,128)(2,1)} %bitcast.16, s32[]{:T(128)S(6)} %select_n.25), kind=kLoop, calls=%fused_computation.8 | loop fusion | bytes 1769476 | tf_op jit(solution)/shard_map/jit(dynamic_index_in_dim)/squeeze | solution.py:524
  113.5 2.2 %collective-permute-start.5 = (bf16[4,3,96,384]{3,2,1,0:T(8,128)(2,1)}, bf16[4,3,96,384]{3,2,1,0:T(8,128)(2,1)S(1)}, u32[]{:S(2)}, u32[]{:S(2)}) collective-permute-start(bf16[4,3,96,384]{3,2,1,0:T(8,128)(2,1)} %after.5), channel_id=1, source_target_pairs={{0,8},{8,0},{16,24},{24,16},{1,9},{9,1},{17,25},{25,17},{2,10},{10... | collective-permute-start | bytes 2654216 | tf_op jit(solution)/shard_map/ppermute | solution.py:23
  115.7 1.3 add_convert_fusion.2
  116.9 0.1 pad_maximum_fusion
  117.0 0.4 collective-permute-start.16
  117.4 18.4 %collective-permute-done.5.refs_5_ = bf16[4,3,96,384]{3,2,1,0:T(8,128)(2,1)S(1)} collective-permute-done((bf16[4,3,96,384]{3,2,1,0:T(8,128)(2,1)}, bf16[4,3,96,384]{3,2,1,0:T(8,128)(2,1)S(1)}, u32[]{:S(2)}, u32[]{:S(2)}) %collective-permute-start.5) | collective-permute-done | bytes 884768 | tf_op jit(solution)/shard_map/ppermute | solution.py:23
  135.8 0.6 collective-permute-start.11
  136.5 0.3 collective-permute-done.8.refs_7_
  136.8 1.2 collective-permute-start.12
  138.0 0.1 collective-permute-start.9
  138.2 0.1 collective-permute-start.6
  138.3 1.1 add_convert_fusion
  139.4 1.5 collective-permute-start.17
  140.8 9.1 %collective-permute-done.9.refs_3_ = bf16[2,3,96,384]{3,2,1,0:T(8,128)(2,1)S(1)} collective-permute-done((bf16[2,3,96,384]{3,2,1,0:T(8,128)(2,1)S(1)}, bf16[2,3,96,384]{3,2,1,0:T(8,128)(2,1)S(1)}, u32[]{:S(2)}, u32[]{:S(2)}) %collective-permute-start.9) | collective-permute-done | bytes 442400 | tf_op jit(solution)/shard_map/ppermute | solution.py:23
  150.0 0.7 collective-permute-start.10
  150.6 0.3 collective-permute-start.7
  150.9 0.9 copy-done.15
  151.9 0.9 copy-done.16
  152.8 14.5 %input_grad.3 = (f32[2,512,768]{2,1,0:T(8,128)}, f32[2,512,768]{2,1,0:T(8,128)}) custom-call(s32[2]{0:T(128)} %copy-done.7, bf16[528,384]{1,0:T(8,128)(2,1)} %get-tuple-element.12.refs_0_, bf16[528,384]{1,0:T(8,128)(2,1)} %copy-done.10, bf16[528,384]{1,0:T(8,128)(2,1)} %copy-done.11, bf16[528,384]{1,0:T(8,128)(2,1)} %copy-done.9, ...), custom_call_target="tpu_custom_call" | custom-call | flops 2802843648 | bytes 20971520 | tf_op jit(solution)/shard_map/input_grad/pallas_call | solution.py:454
  167.4 2.0 %add_bitcast_fusion = f32[5,96,384]{2,1,0:T(8,128)} fusion(bf16[1,5,96,384]{3,2,1,0:T(8,128)(2,1)S(1)} %collective-permute-done.17, f32[4,5,96,384]{3,2,1,0:T(8,128)S(1)} %get-tuple-element.8, bf16[2,5,96,384]{3,2,1,0:T(8,128)(2,1)S(1)} %collective-permute-done.16, bf16[4,5,96,384]{3,2,1,0:T(8,128)(2,1)} %collective-permute-done.15), kind=kLoop, calls=%fused_computation.10 | loop fusion | flops 1105920 | bytes 2580480 | tf_op jit(solution)/shard_map/add | solution.py:79
  169.4 8.9 %input_grad.4.refs_5_ = f32[2,512,768]{2,1,0:T(8,128)} custom-call(s32[2]{0:T(128)} %copy-done.7, bf16[528,384]{1,0:T(8,128)(2,1)} %get-tuple-element.12.refs_0_, bf16[528,384]{1,0:T(8,128)(2,1)} %copy-done.10, bf16[528,384]{1,0:T(8,128)(2,1)} %copy-done.11, bf16[528,384]{1,0:T(8,128)(2,1)} %copy-done.9, bf16[4,2,4,2,96,384]{5,4,3,2,1,0:T(8,128)(2,1)} %bitcast.15, ...), custom_call_target="tpu_custom_call" | custom-call | flops 2491416576 | bytes 20971520 | tf_op jit(solution)/shard_map/input_grad/pallas_call | solution.py:454
  178.3 7.7 %input_grad.5 = bf16[1,1024,768]{2,1,0:T(8,128)(2,1)} custom-call(s32[2]{0:T(128)} %copy-done.7, bf16[528,384]{1,0:T(8,128)(2,1)} %copy-done.9, bf16[2,3,96,384]{3,2,1,0:T(8,128)(2,1)} %collective-permute-done.6.refs_1_, bf16[2,3,96,384]{3,2,1,0:T(8,128)(2,1)} %collective-permute-done.7.refs_2_, bf16[2,3,96,384]{3,2,1,0:T(8,128)(2,1)} %copy-done.12, ...), custom_call_target="tpu_custom_call" | custom-call | flops 934281216 | bytes 20971520 | tf_op jit(solution)/shard_map/input_grad/pallas_call | solution.py:454
  (54 shorter events, 0.3 us)
Async XLA Ops:
  7.2 104.2 %all-gather.5.cloned.1.call-start = ((), (), s32[]{:S(2)}) async-start(), calls=%async_computation | async-start | bytes 1990656 | tf_op jit(solution)/shard_map/all_gather | solution.py:507
  8.9 160.5 %all-gather.7.cloned.1.call-start = ((), (), s32[]{:S(2)}) async-start(), calls=%async_computation.1 | async-start | bytes 4866048 | tf_op jit(solution)/shard_map/all_gather | solution.py:508
  10.5 1.4 copy-start.4
  11.9 4.3 %copy-start.8 = (bf16[1,2048,384]{2,1,0:T(8,128)(2,1)S(1)}, bf16[1,2048,384]{2,1,0:T(8,128)(2,1)}, u32[]{:S(2)}) copy-start(bf16[1,2048,384]{2,1,0:T(8,128)(2,1)} %param.4) | copy-start | bytes 4718596
  13.7 3.0 %copy-start.5 = (bf16[512,1536]{1,0:T(8,128)(2,1)}, bf16[512,1536]{1,0:T(8,128)(2,1)S(1)}, u32[]{:S(2)}) copy-start(bf16[512,1536]{1,0:T(8,128)(2,1)S(1)} %act.1.refs_0_) | copy-start | bytes 4718596
  13.7 35.3 %collective-permute-start = (bf16[512,1536]{1,0:T(8,128)(2,1)S(1)}, bf16[512,1536]{1,0:T(8,128)(2,1)S(1)}, u32[]{:S(2)}, u32[]{:S(2)}) collective-permute-start(bf16[512,1536]{1,0:T(8,128)(2,1)S(1)} %act.1.refs_0_), channel_id=1, source_target_pairs={{0,8},{8,0},{16,24},{24,16},{1,9},{9,1},{17,25},{25,17},{2,10},{10... | collective-permute-start | bytes 4718600 | tf_op jit(solution)/shard_map/ppermute | solution.py:23
  15.0 36.3 %collective-permute-start.1 = (bf16[512,1536]{1,0:T(8,128)(2,1)S(1)}, bf16[512,1536]{1,0:T(8,128)(2,1)S(1)}, u32[]{:S(2)}, u32[]{:S(2)}) collective-permute-start(bf16[512,1536]{1,0:T(8,128)(2,1)S(1)} %act.1.refs_0_), channel_id=1, source_target_pairs={{0,16},{8,24},{16,0},{24,8},{1,17},{9,25},{17,1},{25,9},{2,18},{10... | collective-permute-start | bytes 4718600 | tf_op jit(solution)/shard_map/ppermute | solution.py:23
  49.1 7.4 %copy-start = (bf16[512,1536]{1,0:T(8,128)(2,1)}, bf16[512,1536]{1,0:T(8,128)(2,1)S(1)}, u32[]{:S(2)}) copy-start(bf16[512,1536]{1,0:T(8,128)(2,1)S(1)} %collective-permute-done.refs_1_) | copy-start | bytes 4718596
  50.0 43.2 %collective-permute-start.13 = (bf16[256,1536]{1,0:T(8,128)(2,1)}, bf16[256,1536]{1,0:T(8,128)(2,1)}, u32[]{:S(2)}, u32[]{:S(2)}) collective-permute-start(bf16[256,1536]{1,0:T(8,128)(2,1)} %slice.82), channel_id=1, source_target_pairs={{0,16},{8,24},{16,0},{24,8},{1,17},{9,25},{17,1},{25,9},{2,18},{10... | collective-permute-start | bytes 2359304 | tf_op jit(solution)/shard_map/ppermute | solution.py:23
  51.3 5.2 %copy-start.2 = (bf16[512,1536]{1,0:T(8,128)(2,1)}, bf16[512,1536]{1,0:T(8,128)(2,1)S(1)}, u32[]{:S(2)}) copy-start(bf16[512,1536]{1,0:T(8,128)(2,1)S(1)} %collective-permute-done.1.refs_2_) | copy-start | bytes 4718596
  52.3 41.8 %collective-permute-start.14 = (bf16[256,1536]{1,0:T(8,128)(2,1)}, bf16[256,1536]{1,0:T(8,128)(2,1)}, u32[]{:S(2)}, u32[]{:S(2)}) collective-permute-start(bf16[256,1536]{1,0:T(8,128)(2,1)} %slice.83), channel_id=1, source_target_pairs={{0,8},{8,0},{16,24},{24,16},{1,9},{9,1},{17,25},{25,17},{2,10},{10... | collective-permute-start | bytes 2359304 | tf_op jit(solution)/shard_map/ppermute | solution.py:23
  57.9 36.2 %copy-start.7 = (s32[2]{0:T(128)}, s32[2]{0:T(128)S(1)}, u32[]{:S(2)}) copy-start(s32[2]{0:T(128)S(1)} %pad_add_fusion.place) | copy-start | bytes 28
  57.9 5.1 %copy-start.6 = (bf16[512,1536]{1,0:T(8,128)(2,1)S(1)}, bf16[512,1536]{1,0:T(8,128)(2,1)}, u32[]{:S(2)}) copy-start(bf16[512,1536]{1,0:T(8,128)(2,1)} %copy-done.5) | copy-start | bytes 4718596
  57.9 5.1 %copy-start.1 = (bf16[512,1536]{1,0:T(8,128)(2,1)S(1)}, bf16[512,1536]{1,0:T(8,128)(2,1)}, u32[]{:S(2)}) copy-start(bf16[512,1536]{1,0:T(8,128)(2,1)} %copy-done) | copy-start | bytes 4718596
  57.9 5.1 %copy-start.3 = (bf16[512,1536]{1,0:T(8,128)(2,1)S(1)}, bf16[512,1536]{1,0:T(8,128)(2,1)}, u32[]{:S(2)}) copy-start(bf16[512,1536]{1,0:T(8,128)(2,1)} %copy-done.2) | copy-start | bytes 4718596
  60.4 21.5 %collective-permute-start.2 = (bf16[528,384]{1,0:T(8,128)(2,1)S(1)}, bf16[528,384]{1,0:T(8,128)(2,1)S(1)}, u32[]{:S(2)}, u32[]{:S(2)}) collective-permute-start(bf16[528,384]{1,0:T(8,128)(2,1)S(1)} %get-tuple-element.15), channel_id=1, source_target_pairs={{0,24},{8,16},{16,8},{24,0},{1,25},{9,17},{17,9},{25,1},{2,26},{10... | collective-permute-start | bytes 1216520 | tf_op jit(solution)/shard_map/ppermute | solution.py:23
  60.6 32.7 %collective-permute-start.3 = (bf16[528,384]{1,0:T(8,128)(2,1)S(1)}, bf16[528,384]{1,0:T(8,128)(2,1)S(1)}, u32[]{:S(2)}, u32[]{:S(2)}) collective-permute-start(bf16[528,384]{1,0:T(8,128)(2,1)S(1)} %get-tuple-element.14), channel_id=1, source_target_pairs={{0,8},{8,0},{16,24},{24,16},{1,9},{9,1},{17,25},{25,17},{2,10},{10... | collective-permute-start | bytes 1216520 | tf_op jit(solution)/shard_map/ppermute | solution.py:23
  61.8 31.4 %collective-permute-start.4 = (bf16[528,384]{1,0:T(8,128)(2,1)S(1)}, bf16[528,384]{1,0:T(8,128)(2,1)S(1)}, u32[]{:S(2)}, u32[]{:S(2)}) collective-permute-start(bf16[528,384]{1,0:T(8,128)(2,1)S(1)} %get-tuple-element.13), channel_id=1, source_target_pairs={{0,16},{8,24},{16,0},{24,8},{1,17},{9,25},{17,1},{25,9},{2,18},{10... | collective-permute-start | bytes 1216520 | tf_op jit(solution)/shard_map/ppermute | solution.py:23
  81.8 11.4 %copy-start.9 = (bf16[528,384]{1,0:T(8,128)(2,1)}, bf16[528,384]{1,0:T(8,128)(2,1)S(1)}, u32[]{:S(2)}) copy-start(bf16[528,384]{1,0:T(8,128)(2,1)S(1)} %collective-permute-done.2.refs_3_.refs_0_) | copy-start | bytes 1216516
  93.2 0.8 copy-start.10
  93.2 0.9 copy-start.11
  103.8 11.9 %collective-permute-start.15 = (bf16[4,5,96,384]{3,2,1,0:T(8,128)(2,1)}, bf16[4,5,96,384]{3,2,1,0:T(8,128)(2,1)}, u32[]{:S(2)}, u32[]{:S(2)}) collective-permute-start(bf16[4,5,96,384]{3,2,1,0:T(8,128)(2,1)} %get-tuple-element.9), channel_id=1, source_target_pairs={{0,1},{1,0},{2,3},{3,2},{4,5},{5,4},{6,7},{7,6},{8,9},{9,8},{10,11... | collective-permute-start | bytes 4423688 | tf_op jit(solution)/shard_map/ppermute | solution.py:23
  113.5 22.3 %collective-permute-start.5 = (bf16[4,3,96,384]{3,2,1,0:T(8,128)(2,1)}, bf16[4,3,96,384]{3,2,1,0:T(8,128)(2,1)S(1)}, u32[]{:S(2)}, u32[]{:S(2)}) collective-permute-start(bf16[4,3,96,384]{3,2,1,0:T(8,128)(2,1)} %after.5), channel_id=1, source_target_pairs={{0,8},{8,0},{16,24},{24,16},{1,9},{9,1},{17,25},{25,17},{2,10},{10... | collective-permute-start | bytes 2654216 | tf_op jit(solution)/shard_map/ppermute | solution.py:23
  115.7 21.1 %collective-permute-start.8 = (bf16[4,3,96,384]{3,2,1,0:T(8,128)(2,1)}, bf16[4,3,96,384]{3,2,1,0:T(8,128)(2,1)S(1)}, u32[]{:S(2)}, u32[]{:S(2)}) collective-permute-start(bf16[4,3,96,384]{3,2,1,0:T(8,128)(2,1)} %after.5), channel_id=1, source_target_pairs={{0,16},{8,24},{16,0},{24,8},{1,17},{9,25},{17,1},{25,9},{2,18},{10... | collective-permute-start | bytes 2654216 | tf_op jit(solution)/shard_map/ppermute | solution.py:23
  117.0 21.2 %collective-permute-start.16 = (bf16[2,5,96,384]{3,2,1,0:T(8,128)(2,1)S(1)}, bf16[2,5,96,384]{3,2,1,0:T(8,128)(2,1)S(1)}, u32[]{:S(2)}, u32[]{:S(2)}) collective-permute-start(bf16[2,5,96,384]{3,2,1,0:T(8,128)(2,1)S(1)} %pad_maximum_fusion), channel_id=1, source_target_pairs={{0,2},{1,3},{2,0},{3,1},{4,6},{5,7},{6,4},{7,5},{8,10},{9,11},{10,... | collective-permute-start | bytes 2211848 | tf_op jit(solution)/shard_map/ppermute | solution.py:23
  135.8 17.0 %copy-start.13 = (bf16[4,3,96,384]{3,2,1,0:T(8,128)(2,1)}, bf16[4,3,96,384]{3,2,1,0:T(8,128)(2,1)S(1)}, u32[]{:S(2)}) copy-start(bf16[4,3,96,384]{3,2,1,0:T(8,128)(2,1)S(1)} %collective-permute-done.5.refs_5_) | copy-start | bytes 2654212
  135.8 15.1 %collective-permute-start.11 = (bf16[4,3,96,384]{3,2,1,0:T(8,128)(2,1)S(1)}, bf16[4,3,96,384]{3,2,1,0:T(8,128)(2,1)S(1)}, u32[]{:S(2)}, u32[]{:S(2)}) collective-permute-start(bf16[4,3,96,384]{3,2,1,0:T(8,128)(2,1)S(1)} %collective-permute-done.5.refs_5_), channel_id=1, source_target_pairs={{0,1},{1,0},{2,3},{3,2},{4,5},{5,4},{6,7},{7,6},{8,9},{9,8},{10,11... | collective-permute-start | bytes 2654216 | tf_op jit(solution)/shard_map/ppermute | solution.py:23
  136.8 16.1 %copy-start.14 = (bf16[4,3,96,384]{3,2,1,0:T(8,128)(2,1)}, bf16[4,3,96,384]{3,2,1,0:T(8,128)(2,1)S(1)}, u32[]{:S(2)}) copy-start(bf16[4,3,96,384]{3,2,1,0:T(8,128)(2,1)S(1)} %collective-permute-done.8.refs_7_) | copy-start | bytes 2654212
  136.8 14.2 %collective-permute-start.12 = (bf16[4,3,96,384]{3,2,1,0:T(8,128)(2,1)S(1)}, bf16[4,3,96,384]{3,2,1,0:T(8,128)(2,1)S(1)}, u32[]{:S(2)}, u32[]{:S(2)}) collective-permute-start(bf16[4,3,96,384]{3,2,1,0:T(8,128)(2,1)S(1)} %collective-permute-done.8.refs_7_), channel_id=1, source_target_pairs={{0,1},{1,0},{2,3},{3,2},{4,5},{5,4},{6,7},{7,6},{8,9},{9,8},{10,11... | collective-permute-start | bytes 2654216 | tf_op jit(solution)/shard_map/ppermute | solution.py:23
  138.0 12.0 %collective-permute-start.9 = (bf16[2,3,96,384]{3,2,1,0:T(8,128)(2,1)S(1)}, bf16[2,3,96,384]{3,2,1,0:T(8,128)(2,1)S(1)}, u32[]{:S(2)}, u32[]{:S(2)}) collective-permute-start(bf16[2,3,96,384]{3,2,1,0:T(8,128)(2,1)S(1)} %slice.81), channel_id=1, source_target_pairs={{0,8},{8,0},{16,24},{24,16},{1,9},{9,1},{17,25},{25,17},{2,10},{10... | collective-permute-start | bytes 1327112 | tf_op jit(solution)/shard_map/ppermute | solution.py:23
  138.2 12.5 %collective-permute-start.6 = (bf16[2,3,96,384]{3,2,1,0:T(8,128)(2,1)S(1)}, bf16[2,3,96,384]{3,2,1,0:T(8,128)(2,1)}, u32[]{:S(2)}, u32[]{:S(2)}) collective-permute-start(bf16[2,3,96,384]{3,2,1,0:T(8,128)(2,1)S(1)} %slice.80), channel_id=1, source_target_pairs={{0,16},{8,24},{16,0},{24,8},{1,17},{9,25},{17,1},{25,9},{2,18},{10... | collective-permute-start | bytes 1327112 | tf_op jit(solution)/shard_map/ppermute | solution.py:23
  139.4 28.0 %collective-permute-start.17 = (bf16[1,5,96,384]{3,2,1,0:T(8,128)(2,1)S(1)}, bf16[1,5,96,384]{3,2,1,0:T(8,128)(2,1)S(1)}, u32[]{:S(2)}, u32[]{:S(2)}) collective-permute-start(bf16[1,5,96,384]{3,2,1,0:T(8,128)(2,1)S(1)} %add_convert_fusion), channel_id=1, source_target_pairs={{0,6},{1,7},{2,4},{3,5},{4,2},{5,3},{6,0},{7,1},{8,14},{9,15},{10,... | collective-permute-start | bytes 1105928 | tf_op jit(solution)/shard_map/ppermute | solution.py:23
  150.0 17.4 %copy-start.12 = (bf16[2,3,96,384]{3,2,1,0:T(8,128)(2,1)}, bf16[2,3,96,384]{3,2,1,0:T(8,128)(2,1)S(1)}, u32[]{:S(2)}) copy-start(bf16[2,3,96,384]{3,2,1,0:T(8,128)(2,1)S(1)} %collective-permute-done.9.refs_3_) | copy-start | bytes 1327108
  150.0 28.4 %collective-permute-start.10 = (bf16[2,3,96,384]{3,2,1,0:T(8,128)(2,1)S(1)}, bf16[2,3,96,384]{3,2,1,0:T(8,128)(2,1)}, u32[]{:S(2)}, u32[]{:S(2)}) collective-permute-start(bf16[2,3,96,384]{3,2,1,0:T(8,128)(2,1)S(1)} %collective-permute-done.9.refs_3_), channel_id=1, source_target_pairs={{0,1},{1,0},{2,3},{3,2},{4,5},{5,4},{6,7},{7,6},{8,9},{9,8},{10,11... | collective-permute-start | bytes 1327112 | tf_op jit(solution)/shard_map/ppermute | solution.py:23
  150.6 27.7 %collective-permute-start.7 = (bf16[2,3,96,384]{3,2,1,0:T(8,128)(2,1)}, bf16[2,3,96,384]{3,2,1,0:T(8,128)(2,1)}, u32[]{:S(2)}, u32[]{:S(2)}) collective-permute-start(bf16[2,3,96,384]{3,2,1,0:T(8,128)(2,1)} %collective-permute-done.6.refs_1_), channel_id=1, source_target_pairs={{0,1},{1,0},{2,3},{3,2},{4,5},{5,4},{6,7},{7,6},{8,9},{9,8},{10,11... | collective-permute-start | bytes 1327112 | tf_op jit(solution)/shard_map/ppermute | solution.py:23
  150.9 0.9 copy-start.15
  151.9 0.9 copy-start.16
Sparse Core Ops, SparseCore 0:
  10.2 28.0 all-gather.4
  41.2 70.8 all-gather.6

commit v7 on v6

--- a/solution.py
+++ b/solution.py
@@ -114,6 +114,33 @@
         scratch_shapes=[pltpu.VMEM((width // LANES, 128, LANES), jnp.float32)],
         compiler_params=pltpu.CompilerParams(vmem_limit_bytes=24 << 20),
         name="act",
+    )(inputs)
+
+
+def slope_kernel(x_ref, out_ref, scratch):
+    width = x_ref.shape[2]
+
+    @pl.loop(0, out_ref.shape[1] // 64)
+    def _(step):
+        start = pl.multiple_of(step * 64, 64)
+        span = pl.ds(pl.multiple_of(2 * start, 128), 128)
+        for c in range(width // LANES):
+            lanes = slice(c * LANES, (c + 1) * LANES)
+            scratch[c] = 0.5 * gelu_slope(x_ref[0, span, lanes].astype(jnp.float32))
+            for parity in range(2):
+                out_ref[parity, pl.ds(start, 64), lanes] = scratch[c, pl.ds(parity, 64, stride=2), :]
+
+
+def half_slope(inputs):
+    fine, width = inputs.shape[1:]
+    return pl.pallas_call(
+        slope_kernel,
+        out_shape=jax.ShapeDtypeStruct((2, fine // 2, width), jnp.float32),
+        in_specs=[pl.BlockSpec(memory_space=pltpu.VMEM)],
+        out_specs=pl.BlockSpec(memory_space=pltpu.VMEM),
+        scratch_shapes=[pltpu.VMEM((width // LANES, 128, LANES), jnp.float32)],
+        compiler_params=pltpu.CompilerParams(vmem_limit_bytes=24 << 20),
+        name="half_slope",
     )(inputs)
 
 
@@ -307,7 +334,7 @@
     return total
 
 
-def gradient_stage(place, grads, run, pieces, begun, inputs, shape, last):
+def gradient_stage(place, grads, run, pieces, slope, begun, shape):
     first_tap, taps = run
     window, block = grads[0].shape
     _, fine, width = shape
@@ -315,71 +342,59 @@
     rows = pieces[0][0].shape[-2]
     planes = width // (2 * rows)
     whole = pieces[0][3] is None
-    distances = list(range(seqs)) if whole else sorted({piece[3] for piece in pieces})
-    depth, planar = len(distances) * block, (2, coarse, width)
-    used = list(range(seqs)) if inputs is not None else distances
-    shown = width // block
-    operands = [grads[d] for d in used] + [piece[0] for piece in pieces]
-    operands += list(begun) if begun else [inputs]
+    depth, planar = seqs * block, (2, coarse, width)
+    last = begun is not None
+    operands = [*grads, *(piece[0] for piece in pieces), slope] + ([begun] if last else [])
 
     def body(place, *refs):
-        own, refs = refs[: len(used)], refs[len(used) :]
+        own, refs = refs[:seqs], refs[seqs:]
         sources, refs = refs[: len(pieces)], refs[len(pieces) :]
-        if begun:
-            begun_ref, slope_ref, out_ref = refs[:3]
-            wv, gv, products, strip, sems, grad_sems, sums, slopes, sum_sems = refs[3:]
-        else:
-            x_ref, out_ref, slope_ref = refs[:3]
-            wv, gv, products, strip, sems, grad_sems, skips, skip_sems = refs[3:]
+        slope_ref, refs = refs[0], refs[1:]
+        if last:
+            begun_ref, refs = refs[0], refs[1:]
+        out_ref, wv, gv, products, slopes, sems, grad_sems, slope_sem = refs[:8]
         me, core = place[0], place[1] % 2
 
-        def kernel_copy(number, k, s=None):
-            array, plane, flip, distance = pieces[number]
-            ref = sources[number]
-            if whole:
-                spot = pl.ds(s * block, block)
-                return pltpu.make_async_copy(
-                    ref.at[:, :, s, k], wv.at[k, :, :, :, spot], sems.at[k, number * seqs + s]
-                )
-            spot = pl.ds(distances.index(distance) * block, block)
-            if flip is None:
-                target = wv.at[k, :, :, :, spot]
-                return pltpu.make_async_copy(ref.at[:, :, k], target, sems.at[k, number])
-            span = pl.ds(plane, array.shape[0])
-            target = wv.at[k, span, core ^ flip, :, spot]
-            return pltpu.make_async_copy(ref.at[:, k], target, sems.at[k, number])
+        def left_of(distance):
+            return pl.multiple_of((me ^ distance) * block, block)
 
         def kernel_copies(k):
-            for number in range(len(pieces)):
-                for s in range(seqs) if whole else (None,):
-                    yield kernel_copy(number, k, s)
-
-        early, late = [], []
-        for slot, distance in enumerate(distances):
-            left = (me ^ distance) * block if whole else slot * block
-            spot = pl.ds(pl.multiple_of(left, block), block)
-            source = own[used.index(distance)]
-            early.append(pltpu.make_async_copy(source, gv.at[:, spot], grad_sems.at[slot]))
-        if begun:
-            late.append(pltpu.make_async_copy(begun_ref, sums, sum_sems.at[0]))
-            late.append(pltpu.make_async_copy(slope_ref, slopes, sum_sems.at[1]))
-        else:
-            for d in used:
-                late.append(pltpu.make_async_copy(own[d], skips.at[me ^ d], skip_sems.at[d]))
-        for copy in early:
-            copy.start()
+            for number, (array, plane, flip, distance) in enumerate(pieces):
+                ref = sources[number]
+                if whole:
+                    for s in range(seqs):
+                        target = wv.at[k, :, :, :, pl.ds(s * block, block)]
+                        yield ref.at[:, :, s, k], target, sems.at[k, number * seqs + s]
+                elif flip is None:
+                    target = wv.at[k, :, :, :, pl.ds(left_of(distance), block)]
+                    yield ref.at[:, :, k], target, sems.at[k, number]
+                else:
+                    span = pl.ds(plane, array.shape[0])
+                    target = wv.at[k, span, core ^ flip, :, pl.ds(left_of(distance), block)]
+                    yield ref.at[:, k], target, sems.at[k, number]
+
+        def grad_copy(d):
+            target = gv.at[:, pl.ds(left_of(d), block)]
+            return pltpu.make_async_copy(own[d], target, grad_sems.at[d])
+
+        late = [pltpu.make_async_copy(slope_ref, slopes, slope_sem)]
+        if last:
+            sums, strip, sum_sem = refs[8:]
+            late.append(pltpu.make_async_copy(begun_ref, sums, sum_sem))
+        for d in range(seqs):
+            grad_copy(d).start()
         for k in range(taps):
             for copy in kernel_copies(k):
-                copy.start()
+                pltpu.make_async_copy(*copy).start()
         for copy in late:
             copy.start()
-        for copy in early:
-            copy.wait()
+        for d in range(seqs):
+            grad_copy(d).wait()
 
         @pl.loop(0, taps)
         def _(k):
             for copy in kernel_copies(k):
-                copy.wait()
+                pltpu.make_async_copy(*copy).wait()
             span = planes // 2 * 2 * rows
             for part in range(2):
                 kernel = wv[k, part * (planes // 2) : (part + 1) * (planes // 2)]
@@ -399,66 +414,44 @@
             spot, span = pl.ds(base, STEP), pl.ds(pl.multiple_of(2 * base, 2 * STEP), 2 * STEP)
             for c in range(width // LANES):
                 lanes = slice(c * LANES, (c + 1) * LANES)
-                if not begun:
-                    strip[c] = 0.5 * gelu_slope(x_ref[0, span, lanes].astype(jnp.float32))
-                    left = c * LANES % block
-                    skip = skips[
-                        c * LANES // block, pl.ds(base, STEP + 2 * HALO), left : left + LANES
-                    ].astype(jnp.float32)
+                if not last:
+                    skip = gv[pl.ds(base, STEP + 2 * HALO), lanes].astype(jnp.float32)
                     skip = 0.5 * skip[HALO : HALO + STEP]
                 for parity in range(2):
                     total = shifted_total(products, first_tap, taps, base, lanes, parity)
-                    if begun:
-                        total = sums[parity, spot, lanes] + total * slopes[parity, spot, lanes]
-                    else:
-                        slope = strip[c, pl.ds(parity, STEP, stride=2), :]
-                        slope_ref[parity, spot, lanes] = slope
-                        total = total * slope + skip
+                    total = total * slopes[parity, spot, lanes]
                     if last:
+                        total = total + sums[parity, spot, lanes]
                         strip[c, pl.ds(parity, STEP, stride=2), :] = total
                     else:
-                        out_ref[parity, spot, lanes] = total
+                        out_ref[parity, spot, lanes] = total + skip
                 if last:
                     out_ref[0, span, lanes] = strip[c].astype(jnp.bfloat16)
 
-    block_of = lambda shape: pl.BlockSpec(shape, lambda i, place: (0, 0, 0))
-    in_specs = [ANYWHERE] * (len(used) + len(pieces))
+    out_shape = jax.ShapeDtypeStruct(shape if last else planar, jnp.bfloat16 if last else jnp.float32)
     scratch = [
         pltpu.VMEM((taps, planes, 2, rows, depth), jnp.bfloat16),
         pltpu.VMEM((window, depth), jnp.bfloat16),
         pltpu.VMEM((taps, window, width), jnp.float32),
-        pltpu.VMEM((width // LANES, 2 * STEP, LANES), jnp.float32),
+        pltpu.VMEM(planar, jnp.float32),
         pltpu.SemaphoreType.DMA((taps, len(pieces) * (seqs if whole else 1))),
-        pltpu.SemaphoreType.DMA((len(distances),)),
+        pltpu.SemaphoreType.DMA((seqs,)),
+        pltpu.SemaphoreType.DMA,
     ]
-    planes_out = jax.ShapeDtypeStruct(planar, jnp.float32)
-    if begun:
-        in_specs += [ANYWHERE] * 2
+    if last:
         scratch += [
             pltpu.VMEM(planar, jnp.float32),
-            pltpu.VMEM(planar, jnp.float32),
-            pltpu.SemaphoreType.DMA((2,)),
+            pltpu.VMEM((width // LANES, 2 * STEP, LANES), jnp.float32),
+            pltpu.SemaphoreType.DMA,
         ]
-    else:
-        in_specs.append(block_of(shape))
-        scratch += [
-            pltpu.VMEM((seqs, window, block), jnp.bfloat16),
-            pltpu.SemaphoreType.DMA((seqs,)),
-        ]
-    if last:
-        out_shape, out_specs = jax.ShapeDtypeStruct(shape, jnp.bfloat16), block_of(shape)
-    elif begun:
-        out_shape, out_specs = planes_out, block_of(planar)
-    else:
-        out_shape, out_specs = [planes_out] * 2, [block_of(planar)] * 2
     return pl.pallas_call(
         body,
         out_shape=out_shape,
         grid_spec=pltpu.PrefetchScalarGridSpec(
             num_scalar_prefetch=1,
             grid=(1,),
-            in_specs=in_specs,
-            out_specs=out_specs,
+            in_specs=[ANYWHERE] * len(operands),
+            out_specs=pl.BlockSpec(out_shape.shape, lambda i, place: (0, 0, 0)),
             scratch_shapes=scratch,
         ),
         compiler_params=pltpu.CompilerParams(vmem_limit_bytes=56 << 20),
@@ -505,13 +498,14 @@
     aligned = block % LANES == 0
 
     first = lax.all_gather(weights[:SPLIT], "rep").reshape(planes, 2, SPLIT, rows, block)
-    last = lax.all_gather(weights[SPLIT:], ("rep", "seq"))
+    last = lax.all_gather(lax.all_gather(weights[SPLIT:], "seq"), "rep")
     last = last.reshape(planes, 2, seqs, taps - SPLIT, rows, block)
+    slope = half_slope(inputs)
 
     act = {0: (activate(inputs),)}
     act.update(gather_near(act[0][0], "seq"))
     near = [act[d][0] for d in act if d]
-    act.update(gather_far(act, "seq"))
+    act.update(gather_far(act, "seq", slope))
     far = [part for d in act if len(act[d]) == 2 for part in act[d]]
 
     trunk = trunk_grad[0]
@@ -526,13 +520,12 @@
     kept = {0: (column,)}
     kept.update(gather_near(column, "seq"))
     kept.update(gather_far(kept, "seq"))
-    soon, rest = [(first, 0, None, 0)], []
+    pieces = [(first, 0, None, 0)]
     for distance, parts in kept.items():
         plane = 0
         for part in parts if distance else ():
-            share = soon if len(parts) == 1 else rest
-            share.append((part, plane, 0, distance))
-            share.append((from_peer(part, "rep", 1), plane, 1, distance))
+            pieces.append((part, plane, 0, distance))
+            pieces.append((from_peer(part, "rep", 1), plane, 1, distance))
             plane += part.shape[0]
 
     zeros = jnp.zeros((1, block), jnp.bfloat16)
@@ -552,13 +545,12 @@
     weight_grad = reduce_line(summed, "rep", planes, 2)
 
     if aligned:
-        stage = functools.partial(gradient_stage, place, grads, shape=inputs.shape)
-        begun, slope = stage((0, SPLIT), soon, None, inputs, last=False)
-        begun = stage((SPLIT, taps - SPLIT), [(last, 0, None, None)], (begun, slope), None, last=False)
-        input_grad = stage((0, SPLIT), rest, (begun, slope), None, last=True)
+        stage = functools.partial(gradient_stage, place, grads, slope=slope, shape=inputs.shape)
+        begun = stage((SPLIT, taps - SPLIT), [(last, 0, None, None)], begun=None)
+        input_grad = stage((0, SPLIT), pieces, begun=begun)
     else:
         kernel = jnp.zeros((planes, 2, seqs, SPLIT, rows, block), jnp.bfloat16)
-        for part, plane, flip, distance in soon + rest:
+        for part, plane, flip, distance in pieces:
             part = part if flip is None else part[:, None]
             spot = (plane, 0 if flip is None else rep % 2 ^ flip, me ^ distance, 0, 0, 0)
             kernel = lax.dynamic_update_slice(kernel, part[:, :, None], spot)

time: 194 us -> 191 us (0.985)
  waiting for transfers between devices: 77.4 us -> 65.9 us
  blocking collectives: 0 us -> 9.99 us
  Pallas kernels: 55.6 us -> 48.3 us
  local copies, waits for them, and re-layouts: 16 us -> 22.8 us
  starting transfers between devices: 22.2 us -> 18.6 us
  other arithmetic: 7.47 us -> 9.8 us
    ppermute x18, waiting for transfers between devices: 77.4 us -> 65.8 us  [from_peer(): return lax.ppermute(value, axis, [(i, i ^ distance) for i in range(peers)])]
    pallas_call x3 -> x2, Pallas kernels: 31.2 us -> 19.8 us  [gradient_stage(): pl.pallas_call(body, out_shape=out_shape, grid_spec=pltpu.PrefetchScalarG...]
    all_gather x0 -> x1, blocking collectives: none -> 9.99 us  [on_device(): last = lax.all_gather(lax.all_gather(weights[SPLIT:], 'seq'), 'rep')]
    ppermute x18, starting transfers between devices: 22.2 us -> 18.5 us  [from_peer(): return lax.ppermute(value, axis, [(i, i ^ distance) for i in range(peers)])]
    slice x4, local copies, waits for them, and re-layouts: 2.08 us -> 5.19 us  [half_of(): return lax.slice_in_dim(piece[0], which * size, (which + 1) * size, axis=0)]
    pallas_call x0 -> x1, Pallas kernels: none -> 2.34 us  [half_slope(): pl.pallas_call(slope_kernel, out_shape=jax.ShapeDtypeStruct((2, fine // 2...]
    concatenate x1, other arithmetic: 2.95 us -> 5.28 us  [on_device(): shifts = jnp.concatenate([later, trunk, earlier], axis=1)]
    slice x1, local copies, waits for them, and re-layouts: 0.51 us -> 2.63 us  [on_device(): later = jnp.concatenate([trunk[1:], zeros])]
  transfers between devices with their start and end apart: 20 -> 20, of which waited for: 6 -> 5; matrix products, arithmetic and copies ran while one was open for 9% -> 13% of each run, Pallas kernels for 25% -> 20%
where the time goes in v7:
time: 191 us; the launch traced here: 190 us
  waiting for transfers between devices  65.9 us (35%)
  Pallas kernels  48.3 us (25%)
  local copies, waits for them, and re-layouts  22.8 us (12%)
  starting transfers between devices  18.6 us (10%)
  between operations  14.3 us (7%)
  blocking collectives  9.99 us (5%)
  other arithmetic  9.8 us (5%)
    ppermute x18, waiting for transfers between devices, from_peer(): return lax.ppermute(value, axis, [(i, i ^ distance) for i in range(peers)])  65.8 us
    pallas_call x2, Pallas kernels, gradient_stage(): pl.pallas_call(body, out_shape=out_shape, grid_spec=pltpu.PrefetchScalarG...  19.8 us
    ppermute x18, starting transfers between devices, from_peer(): return lax.ppermute(value, axis, [(i, i ^ distance) for i in range(peers)])  18.5 us
    pallas_call x1, Pallas kernels, early_terms(): pl.pallas_call(kernel, out_shape=jax.ShapeDtypeStruct((both, columns), jn...  13.9 us
    all_gather x1, blocking collectives, on_device(): last = lax.all_gather(lax.all_gather(weights[SPLIT:], 'seq'), 'rep')  9.99 us
    pallas_call x1, Pallas kernels, late_terms(): pl.pallas_call(kernel, out_shape=(jax.ShapeDtypeStruct(shape, jnp.float32...  9.3 us
    unnamed x34, local copies, waits for them, and re-layouts  6.25 us
    concatenate x1, other arithmetic, on_device(): shifts = jnp.concatenate([later, trunk, earlier], axis=1)  5.28 us
  transfers between devices with their start and end apart: 20, of which 5 were waited for; matrix products, arithmetic and copies ran while one was open for 13% of the time, Pallas kernels for 20%

profile of v7, /device:TPU:9, one launch (start us, length us, event | category | flops | bytes accessed | tf_op | source)
XLA Modules:
  0.0 189.7 jit_solution(8097440947132919328)
XLA Ops:
  7.2 1.8 slice.60
  9.0 0.9 slice.63
  10.0 10.0 %all-gather.1 = bf16[8,96,384]{2,1,0:T(8,128)(2,1)} all-gather(bf16[2,96,384]{2,1,0:T(8,128)(2,1)S(1)} %slice.63), channel_id=3, replica_groups=mesh['seq'=4,'rep'=8] {'seq'}, dimensions={0}, use_global_device_ids=true | all-gather | bytes 737280 | tf_op jit(solution)/shard_map/all_gather | solution.py:501
  20.0 2.9 %act.1.refs_0_ = bf16[512,1536]{1,0:T(8,128)(2,1)} custom-call(bf16[1,1024,768]{2,1,0:T(8,128)(2,1)S(1)} %copy-done.1), custom_call_target="tpu_custom_call" | custom-call | tf_op jit(solution)/shard_map/act/pallas_call | solution.py:109
  22.9 0.2 collective-permute-start
  23.1 1.3 collective-permute-start.1
  24.4 2.3 %half_slope.1.refs_5_.refs_13_.refs_1_ = f32[2,512,768]{2,1,0:T(8,128)S(1)} custom-call(bf16[1,1024,768]{2,1,0:T(8,128)(2,1)S(1)} %copy-done.1), custom_call_target="tpu_custom_call" | custom-call | tf_op jit(solution)/shard_map/half_slope/pallas_call | solution.py:136
  26.8 2.6 %slice_bitcast_fusion.1 = (bf16[2047,384]{1,0:T(8,128)(2,1)}, bf16[2047,384]{1,0:T(8,128)(2,1)}) fusion(bf16[1,2048,384]{2,1,0:T(8,128)(2,1)S(1)} %copy-done.11), kind=kLoop, calls=%fused_computation.7 | loop fusion | bytes 6288384 | tf_op jit(solution)/shard_map/slice | solution.py:532
  29.4 0.1 copy-done
  29.5 27.7 %collective-permute-done.refs_1_ = bf16[512,1536]{1,0:T(8,128)(2,1)S(1)} collective-permute-done((bf16[512,1536]{1,0:T(8,128)(2,1)}, bf16[512,1536]{1,0:T(8,128)(2,1)S(1)}, u32[]{:S(2)}, u32[]{:S(2)}) %collective-permute-start) | collective-permute-done | bytes 1572896 | tf_op jit(solution)/shard_map/ppermute | solution.py:23
  57.2 1.0 slice.82.refs_0_
  58.3 0.4 copy-done.2
  58.6 2.1 %slice.83.refs_0_ = bf16[256,1536]{1,0:T(8,128)(2,1)} slice(bf16[512,1536]{1,0:T(8,128)(2,1)} %collective-permute-done.1.refs_2_), slice={[256:512], [0:1536]} | slice | bytes 1572864 | tf_op jit(solution)/shard_map/slice | solution.py:41
  60.7 1.5 collective-permute-start.14
  62.2 5.3 %fusion.2.shifts_ref = bf16[2048,1152]{1,0:T(8,128)(2,1)} fusion(bf16[2047,384]{1,0:T(8,128)(2,1)} %get-tuple-element.13, bf16[2047,384]{1,0:T(8,128)(2,1)} %get-tuple-element.12, bf16[2048,384]{1,0:T(8,128)(2,1)S(1)} %bitcast.14), kind=kLoop, calls=%fused_computation.4 | loop fusion | flops 23592960 | bytes 9435648 | tf_op jit(solution)/shard_map/concatenate | solution.py:534
  67.5 1.3 pad.6.refs_0_
  68.9 2.4 %constant_dynamic-slice_fusion = (bf16[528,384]{1,0:T(8,128)(2,1)S(1)}, bf16[528,384]{1,0:T(8,128)(2,1)S(1)}, bf16[528,384]{1,0:T(8,128)(2,1)S(1)}, bf16[528,384]{1,0:T(8,128)(2,1)}) fusion(bf16[2064,384]{1,0:T(8,128)(2,1)} %after.6, s32[]{:T(128)S(6)} %select_n.26, s32[]{:T(128)S(6)} %select_n.25, s32[]{:T(128)S(6)} %select_n.24, s32[]{:T(128)S(6)} %select_n.23), kind=kLoop, calls=%fused_computation.14 | loop fusion | bytes 3244048 | tf_op jit(solution)/shard_map/dynamic_slice | solution.py:515
  71.4 1.4 collective-permute-start.2
  72.8 0.1 collective-permute-start.3
  72.9 1.2 collective-permute-start.4
  74.0 13.9 %weight_grad_early.1.early_ref = f32[1536,1152]{1,0:T(8,128)} custom-call(s32[2]{0:T(128)S(1)} %pad_add_fusion.place, bf16[2048,1152]{1,0:T(8,128)(2,1)} %fusion.2.shifts_ref, bf16[512,1536]{1,0:T(8,128)(2,1)} %act.1.refs_0_, bf16[512,1536]{1,0:T(8,128)(2,1)S(1)} %copy-done.3, bf16[512,1536]{1,0:T(8,128)(2,1)} %collective-permute-done.1.refs_2_), custom_call_target="tpu_custom_call" | custom-call | flops 5435817984 | bytes 16777216 | tf_op jit(solution)/shard_map/weight_grad_early/pallas_call | solution.py:195
  88.0 7.7 %collective-permute-done.4.refs_3_ = bf16[528,384]{1,0:T(8,128)(2,1)S(1)} collective-permute-done((bf16[528,384]{1,0:T(8,128)(2,1)S(1)}, bf16[528,384]{1,0:T(8,128)(2,1)S(1)}, u32[]{:S(2)}, u32[]{:S(2)}) %collective-permute-start.4) | collective-permute-done | bytes 405536 | tf_op jit(solution)/shard_map/ppermute | solution.py:23
  95.7 0.7 copy-done.15
  96.4 0.9 copy-done.4
  97.3 0.9 copy-done.6
  98.2 0.5 copy-done.5
  98.7 1.1 copy-done.7
  99.8 9.3 %weight_grad_late.1 = (f32[4,5,96,384]{3,2,1,0:T(8,128)S(1)}, bf16[4,5,96,384]{3,2,1,0:T(8,128)(2,1)}) custom-call(s32[2]{0:T(128)S(1)} %pad_add_fusion.place, bf16[2048,1152]{1,0:T(8,128)(2,1)} %fusion.2.shifts_ref, f32[1536,1152]{1,0:T(8,128)} %weight_grad_early.1.early_ref, bf16[256,1536]{1,0:T(8,128)(2,1)S(1)} %copy-done.5, bf16[256,1536]{1,0:T(8,128)(2,1)S(1)} %copy-done.7), custom_call_target="tpu_custom_call" | custom-call | flops 1811939328 | bytes 16777216 | tf_op jit(solution)/shard_map/weight_grad_late/pallas_call | solution.py:268
  109.1 1.6 copy-done.8
  110.7 3.9 %collective-permute-start.15 = (bf16[4,5,96,384]{3,2,1,0:T(8,128)(2,1)}, bf16[4,5,96,384]{3,2,1,0:T(8,128)(2,1)}, u32[]{:S(2)}, u32[]{:S(2)}) collective-permute-start(bf16[4,5,96,384]{3,2,1,0:T(8,128)(2,1)} %get-tuple-element.5), channel_id=1, source_target_pairs={{0,1},{1,0},{2,3},{3,2},{4,5},{5,4},{6,7},{7,6},{8,9},{9,8},{10,11... | collective-permute-start | bytes 4423688 | tf_op jit(solution)/shard_map/ppermute | solution.py:23
  114.6 2.3 %dynamic-slice_bitcast_fusion.refs_0_ = bf16[4,3,96,384]{3,2,1,0:T(8,128)(2,1)} fusion(bf16[4,2,3,96,384]{4,3,2,1,0:T(8,128)(2,1)} %bitcast.17, s32[]{:T(128)S(6)} %select_n.28), kind=kLoop, calls=%fused_computation.8 | loop fusion | bytes 1769476 | tf_op jit(solution)/shard_map/jit(dynamic_index_in_dim)/squeeze | solution.py:518
  116.9 1.5 collective-permute-start.7
  118.4 1.3 add_convert_fusion.2
  119.7 0.2 collective-permute-start.16
  119.9 18.6 %collective-permute-done.5.refs_5_ = bf16[4,3,96,384]{3,2,1,0:T(8,128)(2,1)} collective-permute-done((bf16[4,3,96,384]{3,2,1,0:T(8,128)(2,1)}, bf16[4,3,96,384]{3,2,1,0:T(8,128)(2,1)}, u32[]{:S(2)}, u32[]{:S(2)}) %collective-permute-start.5) | collective-permute-done | bytes 884768 | tf_op jit(solution)/shard_map/ppermute | solution.py:23
  138.5 1.1 slice.80
  139.6 1.1 slice.81
  140.7 1.5 collective-permute-start.11
  142.2 1.1 add_convert_fusion
  143.3 1.3 collective-permute-start.17
  144.6 1.6 collective-permute-start.6
  146.3 4.4 %collective-permute-done.9.refs_9_ = bf16[2,3,96,384]{3,2,1,0:T(8,128)(2,1)S(1)} collective-permute-done((bf16[2,3,96,384]{3,2,1,0:T(8,128)(2,1)S(1)}, bf16[2,3,96,384]{3,2,1,0:T(8,128)(2,1)S(1)}, u32[]{:S(2)}, u32[]{:S(2)}) %collective-permute-start.9) | collective-permute-done | bytes 442400 | tf_op jit(solution)/shard_map/ppermute | solution.py:23
  150.6 1.6 collective-permute-start.10
  152.2 1.3 collective-permute-start.12
  153.5 7.5 %collective-permute-done.17 = bf16[1,5,96,384]{3,2,1,0:T(8,128)(2,1)S(1)} collective-permute-done((bf16[1,5,96,384]{3,2,1,0:T(8,128)(2,1)S(1)}, bf16[1,5,96,384]{3,2,1,0:T(8,128)(2,1)S(1)}, u32[]{:S(2)}, u32[]{:S(2)}) %collective-permute-start.17) | collective-permute-done | bytes 368672 | tf_op jit(solution)/shard_map/ppermute | solution.py:23
  160.9 2.0 %add_bitcast_fusion = f32[5,96,384]{2,1,0:T(8,128)} fusion(bf16[1,5,96,384]{3,2,1,0:T(8,128)(2,1)S(1)} %collective-permute-done.17, f32[4,5,96,384]{3,2,1,0:T(8,128)S(1)} %copy-done.9, bf16[2,5,96,384]{3,2,1,0:T(8,128)(2,1)S(1)} %collective-permute-done.16, bf16[4,5,96,384]{3,2,1,0:T(8,128)(2,1)} %collective-permute-done.15), kind=kLoop, calls=%fused_computation.10 | loop fusion | flops 1105920 | bytes 2580480 | tf_op jit(solution)/shard_map/add | solution.py:79
  162.9 9.1 %input_grad.2.refs_14_ = f32[2,512,768]{2,1,0:T(8,128)} custom-call(s32[2]{0:T(128)} %copy-done.10, bf16[528,384]{1,0:T(8,128)(2,1)} %get-tuple-element.11.refs_0_, bf16[528,384]{1,0:T(8,128)(2,1)} %copy-done.13, bf16[528,384]{1,0:T(8,128)(2,1)} %copy-done.14, bf16[528,384]{1,0:T(8,128)(2,1)} %copy-done.15, bf16[4,2,4,2,96,384]{5,4,3,2,1,0:T(8,128)(2,1)} %bitcast.16, ...), custom_call_target="tpu_custom_call" | custom-call | flops 2491416576 | bytes 20971520 | tf_op jit(solution)/shard_map/input_grad/pallas_call | solution.py:447
  172.0 10.8 %input_grad.3 = bf16[1,1024,768]{2,1,0:T(8,128)(2,1)} custom-call(s32[2]{0:T(128)} %copy-done.10, bf16[528,384]{1,0:T(8,128)(2,1)} %get-tuple-element.11.refs_0_, bf16[528,384]{1,0:T(8,128)(2,1)} %copy-done.13, bf16[528,384]{1,0:T(8,128)(2,1)} %copy-done.14, bf16[528,384]{1,0:T(8,128)(2,1)} %copy-done.15, bf16[4,2,3,96,384]{4,3,2,1,0:T(8,128)(2,1)} %bitcast.18, ...), custom_call_target="tpu_custom_call" | custom-call | flops 3737124864 | bytes 20971520 | tf_op jit(solution)/shard_map/input_grad/pallas_call | solution.py:447
  (57 shorter events, 0.5 us)
Async XLA Ops:
  7.2 12.8 %copy-start.1 = (bf16[1,1024,768]{2,1,0:T(8,128)(2,1)S(1)}, bf16[1,1024,768]{2,1,0:T(8,128)(2,1)}, u32[]{:S(2)}) copy-start(bf16[1,1024,768]{2,1,0:T(8,128)(2,1)} %x_ref.3) | copy-start | bytes 4718596
  7.2 107.4 %all-gather.6.cloned.1.call-start = ((), (), s32[]{:S(2)}) async-start(), calls=%async_computation | async-start | bytes 1990656 | tf_op jit(solution)/shard_map/all_gather | solution.py:500
  9.0 153.9 %all-gather.8.cloned.1.call-start = ((), (), s32[]{:S(2)}) async-start(), calls=%async_computation.1 | async-start | bytes 5308416 | tf_op jit(solution)/shard_map/all_gather | solution.py:501
  22.9 3.8 %copy-start.11 = (bf16[1,2048,384]{2,1,0:T(8,128)(2,1)S(1)}, bf16[1,2048,384]{2,1,0:T(8,128)(2,1)}, u32[]{:S(2)}) copy-start(bf16[1,2048,384]{2,1,0:T(8,128)(2,1)} %param.4) | copy-start | bytes 4718596
  22.9 34.3 %collective-permute-start = (bf16[512,1536]{1,0:T(8,128)(2,1)}, bf16[512,1536]{1,0:T(8,128)(2,1)S(1)}, u32[]{:S(2)}, u32[]{:S(2)}) collective-permute-start(bf16[512,1536]{1,0:T(8,128)(2,1)} %act.1.refs_0_), channel_id=1, source_target_pairs={{0,8},{8,0},{16,24},{24,16},{1,9},{9,1},{17,25},{25,17},{2,10},{10... | collective-permute-start | bytes 4718600 | tf_op jit(solution)/shard_map/ppermute | solution.py:23
  23.1 35.6 %collective-permute-start.1 = (bf16[512,1536]{1,0:T(8,128)(2,1)}, bf16[512,1536]{1,0:T(8,128)(2,1)}, u32[]{:S(2)}, u32[]{:S(2)}) collective-permute-start(bf16[512,1536]{1,0:T(8,128)(2,1)} %act.1.refs_0_), channel_id=1, source_target_pairs={{0,16},{8,24},{16,0},{24,8},{1,17},{9,25},{17,1},{25,9},{2,18},{10... | collective-permute-start | bytes 4718600 | tf_op jit(solution)/shard_map/ppermute | solution.py:23
  26.7 2.8 %copy-start = (f32[2,512,768]{2,1,0:T(8,128)}, f32[2,512,768]{2,1,0:T(8,128)S(1)}, u32[]{:S(2)}) copy-start(f32[2,512,768]{2,1,0:T(8,128)S(1)} %half_slope.1.refs_5_.refs_13_.refs_1_) | copy-start | bytes 9437188
  57.2 1.4 copy-start.2
  58.6 37.0 %collective-permute-start.13 = (bf16[256,1536]{1,0:T(8,128)(2,1)}, bf16[256,1536]{1,0:T(8,128)(2,1)S(1)}, u32[]{:S(2)}, u32[]{:S(2)}) collective-permute-start(bf16[256,1536]{1,0:T(8,128)(2,1)} %after.8), channel_id=1, source_target_pairs={{0,16},{8,24},{16,0},{24,8},{1,17},{9,25},{17,1},{25,9},{2,18},{10... | collective-permute-start | bytes 2359304 | tf_op jit(solution)/shard_map/ppermute | solution.py:23
  60.7 1.5 copy-start.12
  60.7 36.6 %collective-permute-start.14 = (bf16[256,1536]{1,0:T(8,128)(2,1)}, bf16[256,1536]{1,0:T(8,128)(2,1)S(1)}, u32[]{:S(2)}, u32[]{:S(2)}) collective-permute-start(bf16[256,1536]{1,0:T(8,128)(2,1)} %after.10), channel_id=1, source_target_pairs={{0,8},{8,0},{16,24},{24,16},{1,9},{9,1},{17,25},{25,17},{2,10},{10... | collective-permute-start | bytes 2359304 | tf_op jit(solution)/shard_map/ppermute | solution.py:23
  68.9 29.2 %copy-start.10 = (s32[2]{0:T(128)}, s32[2]{0:T(128)S(1)}, u32[]{:S(2)}) copy-start(s32[2]{0:T(128)S(1)} %pad_add_fusion.place) | copy-start | bytes 28
  68.9 5.1 %copy-start.3 = (bf16[512,1536]{1,0:T(8,128)(2,1)S(1)}, bf16[512,1536]{1,0:T(8,128)(2,1)}, u32[]{:S(2)}) copy-start(bf16[512,1536]{1,0:T(8,128)(2,1)} %copy-done.2) | copy-start | bytes 4718596
  71.4 16.6 %collective-permute-start.2 = (bf16[528,384]{1,0:T(8,128)(2,1)S(1)}, bf16[528,384]{1,0:T(8,128)(2,1)S(1)}, u32[]{:S(2)}, u32[]{:S(2)}) collective-permute-start(bf16[528,384]{1,0:T(8,128)(2,1)S(1)} %get-tuple-element.10), channel_id=1, source_target_pairs={{0,8},{8,0},{16,24},{24,16},{1,9},{9,1},{17,25},{25,17},{2,10},{10... | collective-permute-start | bytes 1216520 | tf_op jit(solution)/shard_map/ppermute | solution.py:23
  72.8 15.2 %collective-permute-start.3 = (bf16[528,384]{1,0:T(8,128)(2,1)S(1)}, bf16[528,384]{1,0:T(8,128)(2,1)S(1)}, u32[]{:S(2)}, u32[]{:S(2)}) collective-permute-start(bf16[528,384]{1,0:T(8,128)(2,1)S(1)} %get-tuple-element.9), channel_id=1, source_target_pairs={{0,16},{8,24},{16,0},{24,8},{1,17},{9,25},{17,1},{25,9},{2,18},{10... | collective-permute-start | bytes 1216520 | tf_op jit(solution)/shard_map/ppermute | solution.py:23
  72.9 22.8 %collective-permute-start.4 = (bf16[528,384]{1,0:T(8,128)(2,1)S(1)}, bf16[528,384]{1,0:T(8,128)(2,1)S(1)}, u32[]{:S(2)}, u32[]{:S(2)}) collective-permute-start(bf16[528,384]{1,0:T(8,128)(2,1)S(1)} %get-tuple-element.8), channel_id=1, source_target_pairs={{0,24},{8,16},{16,8},{24,0},{1,25},{9,17},{17,9},{25,1},{2,26},{10... | collective-permute-start | bytes 1216520 | tf_op jit(solution)/shard_map/ppermute | solution.py:23
  87.9 7.7 %copy-start.13 = (bf16[528,384]{1,0:T(8,128)(2,1)}, bf16[528,384]{1,0:T(8,128)(2,1)S(1)}, u32[]{:S(2)}) copy-start(bf16[528,384]{1,0:T(8,128)(2,1)S(1)} %collective-permute-done.2.refs_1_) | copy-start | bytes 1216516
  88.0 7.7 %copy-start.14 = (bf16[528,384]{1,0:T(8,128)(2,1)}, bf16[528,384]{1,0:T(8,128)(2,1)S(1)}, u32[]{:S(2)}) copy-start(bf16[528,384]{1,0:T(8,128)(2,1)S(1)} %collective-permute-done.3.refs_2_) | copy-start | bytes 1216516
  95.6 0.8 copy-start.15
  96.4 0.9 copy-start.4
  97.3 1.4 copy-start.5
  97.3 0.9 copy-start.6
  98.7 1.1 copy-start.7
  109.1 1.6 copy-start.8
  110.7 7.7 %collective-permute-start.15 = (bf16[4,5,96,384]{3,2,1,0:T(8,128)(2,1)}, bf16[4,5,96,384]{3,2,1,0:T(8,128)(2,1)}, u32[]{:S(2)}, u32[]{:S(2)}) collective-permute-start(bf16[4,5,96,384]{3,2,1,0:T(8,128)(2,1)} %get-tuple-element.5), channel_id=1, source_target_pairs={{0,1},{1,0},{2,3},{3,2},{4,5},{5,4},{6,7},{7,6},{8,9},{9,8},{10,11... | collective-permute-start | bytes 4423688 | tf_op jit(solution)/shard_map/ppermute | solution.py:23
  114.6 3.8 %copy-start.9 = (f32[4,5,96,384]{3,2,1,0:T(8,128)S(1)}, f32[4,5,96,384]{3,2,1,0:T(8,128)}, u32[]{:S(2)}) copy-start(f32[4,5,96,384]{3,2,1,0:T(8,128)} %copy-done.8) | copy-start | bytes 8847364
  116.9 21.6 %collective-permute-start.5 = (bf16[4,3,96,384]{3,2,1,0:T(8,128)(2,1)}, bf16[4,3,96,384]{3,2,1,0:T(8,128)(2,1)}, u32[]{:S(2)}, u32[]{:S(2)}) collective-permute-start(bf16[4,3,96,384]{3,2,1,0:T(8,128)(2,1)} %after.7), channel_id=1, source_target_pairs={{0,8},{8,0},{16,24},{24,16},{1,9},{9,1},{17,25},{25,17},{2,10},{10... | collective-permute-start | bytes 2654216 | tf_op jit(solution)/shard_map/ppermute | solution.py:23
  116.9 22.7 %collective-permute-start.7 = (bf16[4,3,96,384]{3,2,1,0:T(8,128)(2,1)}, bf16[4,3,96,384]{3,2,1,0:T(8,128)(2,1)}, u32[]{:S(2)}, u32[]{:S(2)}) collective-permute-start(bf16[4,3,96,384]{3,2,1,0:T(8,128)(2,1)} %after.7), channel_id=1, source_target_pairs={{0,16},{8,24},{16,0},{24,8},{1,17},{9,25},{17,1},{25,9},{2,18},{10... | collective-permute-start | bytes 2654216 | tf_op jit(solution)/shard_map/ppermute | solution.py:23
  119.7 22.5 %collective-permute-start.16 = (bf16[2,5,96,384]{3,2,1,0:T(8,128)(2,1)S(1)}, bf16[2,5,96,384]{3,2,1,0:T(8,128)(2,1)S(1)}, u32[]{:S(2)}, u32[]{:S(2)}) collective-permute-start(bf16[2,5,96,384]{3,2,1,0:T(8,128)(2,1)S(1)} %pad_maximum_fusion), channel_id=1, source_target_pairs={{0,2},{1,3},{2,0},{3,1},{4,6},{5,7},{6,4},{7,5},{8,10},{9,11},{10,... | collective-permute-start | bytes 2211848 | tf_op jit(solution)/shard_map/ppermute | solution.py:23
  139.6 11.1 %collective-permute-start.9 = (bf16[2,3,96,384]{3,2,1,0:T(8,128)(2,1)S(1)}, bf16[2,3,96,384]{3,2,1,0:T(8,128)(2,1)S(1)}, u32[]{:S(2)}, u32[]{:S(2)}) collective-permute-start(bf16[2,3,96,384]{3,2,1,0:T(8,128)(2,1)S(1)} %slice.80), channel_id=1, source_target_pairs={{0,16},{8,24},{16,0},{24,8},{1,17},{9,25},{17,1},{25,9},{2,18},{10... | collective-permute-start | bytes 1327112 | tf_op jit(solution)/shard_map/ppermute | solution.py:23
  140.7 11.5 %collective-permute-start.11 = (bf16[2,3,96,384]{3,2,1,0:T(8,128)(2,1)S(1)}, bf16[2,3,96,384]{3,2,1,0:T(8,128)(2,1)}, u32[]{:S(2)}, u32[]{:S(2)}) collective-permute-start(bf16[2,3,96,384]{3,2,1,0:T(8,128)(2,1)S(1)} %slice.81), channel_id=1, source_target_pairs={{0,8},{8,0},{16,24},{24,16},{1,9},{9,1},{17,25},{25,17},{2,10},{10... | collective-permute-start | bytes 1327112 | tf_op jit(solution)/shard_map/ppermute | solution.py:23
  143.3 17.6 %collective-permute-start.17 = (bf16[1,5,96,384]{3,2,1,0:T(8,128)(2,1)S(1)}, bf16[1,5,96,384]{3,2,1,0:T(8,128)(2,1)S(1)}, u32[]{:S(2)}, u32[]{:S(2)}) collective-permute-start(bf16[1,5,96,384]{3,2,1,0:T(8,128)(2,1)S(1)} %add_convert_fusion), channel_id=1, source_target_pairs={{0,6},{1,7},{2,4},{3,5},{4,2},{5,3},{6,0},{7,1},{8,14},{9,15},{10,... | collective-permute-start | bytes 1105928 | tf_op jit(solution)/shard_map/ppermute | solution.py:23
  144.6 27.4 %collective-permute-start.6 = (bf16[4,3,96,384]{3,2,1,0:T(8,128)(2,1)}, bf16[4,3,96,384]{3,2,1,0:T(8,128)(2,1)}, u32[]{:S(2)}, u32[]{:S(2)}) collective-permute-start(bf16[4,3,96,384]{3,2,1,0:T(8,128)(2,1)} %collective-permute-done.5.refs_5_), channel_id=1, source_target_pairs={{0,1},{1,0},{2,3},{3,2},{4,5},{5,4},{6,7},{7,6},{8,9},{9,8},{10,11... | collective-permute-start | bytes 2654216 | tf_op jit(solution)/shard_map/ppermute | solution.py:23
  146.3 25.8 %collective-permute-start.8 = (bf16[4,3,96,384]{3,2,1,0:T(8,128)(2,1)}, bf16[4,3,96,384]{3,2,1,0:T(8,128)(2,1)}, u32[]{:S(2)}, u32[]{:S(2)}) collective-permute-start(bf16[4,3,96,384]{3,2,1,0:T(8,128)(2,1)} %collective-permute-done.7.refs_7_), channel_id=1, source_target_pairs={{0,1},{1,0},{2,3},{3,2},{4,5},{5,4},{6,7},{7,6},{8,9},{9,8},{10,11... | collective-permute-start | bytes 2654216 | tf_op jit(solution)/shard_map/ppermute | solution.py:23
  150.6 21.4 %copy-start.16 = (bf16[2,3,96,384]{3,2,1,0:T(8,128)(2,1)}, bf16[2,3,96,384]{3,2,1,0:T(8,128)(2,1)S(1)}, u32[]{:S(2)}) copy-start(bf16[2,3,96,384]{3,2,1,0:T(8,128)(2,1)S(1)} %collective-permute-done.9.refs_9_) | copy-start | bytes 1327108
  150.6 21.4 %collective-permute-start.10 = (bf16[2,3,96,384]{3,2,1,0:T(8,128)(2,1)S(1)}, bf16[2,3,96,384]{3,2,1,0:T(8,128)(2,1)}, u32[]{:S(2)}, u32[]{:S(2)}) collective-permute-start(bf16[2,3,96,384]{3,2,1,0:T(8,128)(2,1)S(1)} %collective-permute-done.9.refs_9_), channel_id=1, source_target_pairs={{0,1},{1,0},{2,3},{3,2},{4,5},{5,4},{6,7},{7,6},{8,9},{9,8},{10,11... | collective-permute-start | bytes 1327112 | tf_op jit(solution)/shard_map/ppermute | solution.py:23
  152.2 19.8 %collective-permute-start.12 = (bf16[2,3,96,384]{3,2,1,0:T(8,128)(2,1)}, bf16[2,3,96,384]{3,2,1,0:T(8,128)(2,1)}, u32[]{:S(2)}, u32[]{:S(2)}) collective-permute-start(bf16[2,3,96,384]{3,2,1,0:T(8,128)(2,1)} %collective-permute-done.11.refs_11_), channel_id=1, source_target_pairs={{0,1},{1,0},{2,3},{3,2},{4,5},{5,4},{6,7},{7,6},{8,9},{9,8},{10,11... | collective-permute-start | bytes 1327112 | tf_op jit(solution)/shard_map/ppermute | solution.py:23
Sparse Core Ops, SparseCore 0:
  10.2 28.0 all-gather.5
  40.0 49.5 all-gather.7

commit v8 on v7

v8 whole, which is shorter than its diff:
```python
import functools
import math

import jax
import jax.numpy as jnp
from jax import lax
from jax.experimental import pallas as pl
from jax.experimental.pallas import tpu as pltpu
from jax.sharding import PartitionSpec as P

LANES = 128
HALO = 32
CHUNKS = 4
FIRST = 80
EDGE = 16
MARGIN = HALO - EDGE
STEP = 64
ROOT = math.sqrt(2.0 / math.pi)
CUBIC = 0.044715
ANYWHERE = pl.BlockSpec(memory_space=pl.ANY)
ROW_OFFSETS = ((1, 1), (0, 1), (0, 0), (-1, 0), (-1, -1))
GRAD_PARTS = ((0, 0), (1, 0), (1, 1), (2, 1), (2, 2))


def from_peer(value, axis, distance):
    peers = lax.axis_size(axis)
    return lax.ppermute(value, axis, [(i, i ^ distance) for i in range(peers)])


def after(value, *earlier):
    return pl.pallas_call(
        lambda *refs: None,
        out_shape=jax.ShapeDtypeStruct(value.shape, value.dtype),
        in_specs=[ANYWHERE] * (1 + len(earlier)),
        out_specs=ANYWHERE,
        input_output_aliases={0: 0},
        name="after",
    )(value, *earlier)


def gather_line(value, axis, count, unit):
    found, mask = {0: value}, count - 1
    while mask:
        for distance in list(found):
            found[distance ^ mask] = from_peer(found[distance], axis, mask * unit)
        mask //= 2
    return [found[distance] for distance in range(count)]


def gelu_slope(x):
    tanh = jnp.tanh(ROOT * (x + CUBIC * (x * x * x)))
    return 0.5 * (1.0 + tanh) + 0.5 * x * (1.0 - tanh * tanh) * (
        ROOT * (1.0 + 3.0 * CUBIC * (x * x))
    )


def messages_kernel(place, x_ref, trunk_ref, beside_ref, below_ref, own_ref, edged, strip, sem):
    coarse, width, block = x_ref.shape[1] // 2, x_ref.shape[2], edged.shape[1]
    length = trunk_ref.shape[1]
    packed = (coarse + 2 * HALO) // CHUNKS
    copy = pltpu.make_async_copy(trunk_ref.at[0], edged.at[pl.ds(HALO, length)], sem)
    copy.start()
    edged[:HALO] = jnp.zeros((HALO, block), jnp.bfloat16)
    edged[HALO + length :] = jnp.zeros((HALO, block), jnp.bfloat16)

    @pl.loop(0, coarse // STEP)
    def _(step):
        start = pl.multiple_of(step * STEP, STEP)
        x = x_ref[0, pl.ds(pl.multiple_of(2 * start, 2 * STEP), 2 * STEP), :].astype(jnp.float32)
        act = x * (0.5 * (1.0 + jnp.tanh(ROOT * (x + CUBIC * (x * x * x)))))
        for c in range(width // LANES):
            strip[c] = act[:, c * LANES : (c + 1) * LANES]
        for parity in range(2):
            for c in range(width // LANES):
                picked = strip[c, pl.ds(parity, STEP, stride=2), :].astype(jnp.bfloat16)
                lanes = slice(parity * width + c * LANES, parity * width + (c + 1) * LANES)
                beside_ref[pl.ds(FIRST + start, STEP), lanes] = picked
                below_ref[pl.ds(start, STEP), lanes] = picked

    copy.wait()

    def pack(out_ref, row, distance, first, last):
        base = (place[0] ^ distance) * coarse
        for q in range(CHUNKS):
            start = pl.multiple_of(base + q * packed + first, 16)
            out_ref[row : row + last - first, q * block : (q + 1) * block] = edged[
                pl.ds(start, last - first), :
            ]

    pack(beside_ref, 0, 3, 0, FIRST)
    pack(beside_ref, FIRST + coarse, 1, 0, packed)
    pack(below_ref, coarse, 3, FIRST, packed)
    pack(below_ref, coarse + packed - FIRST, 2, 0, packed)
    pack(own_ref, 0, 0, 0, packed)


def messages(place, inputs, trunk_grad):
    _, fine, width = inputs.shape
    _, length, block = trunk_grad.shape
    coarse = fine // 2
    packed = (coarse + 2 * HALO) // CHUNKS
    rows = (FIRST + coarse + packed, coarse + packed - FIRST + packed, packed)
    return pl.pallas_call(
        messages_kernel,
        out_shape=[jax.ShapeDtypeStruct((n, 2 * width), jnp.bfloat16) for n in rows],
        grid_spec=pltpu.PrefetchScalarGridSpec(
            num_scalar_prefetch=1,
            grid=(1,),
            in_specs=[pl.BlockSpec(inputs.shape, lambda i, place: (0, 0, 0)), ANYWHERE],
            out_specs=[pl.BlockSpec((n, 2 * width), lambda i, place: (0, 0)) for n in rows],
            scratch_shapes=[
                pltpu.VMEM((length + 2 * HALO, block), jnp.bfloat16),
                pltpu.VMEM((width // LANES, 2 * STEP, LANES), jnp.float32),
                pltpu.SemaphoreType.DMA,
            ],
        ),
        compiler_params=pltpu.CompilerParams(vmem_limit_bytes=32 << 20),
        name="messages",
    )(place, inputs, trunk_grad)


def slope_kernel(x_ref, out_ref, scratch):
    width = x_ref.shape[2]

    @pl.loop(0, out_ref.shape[1] // 64)
    def _(step):
        start = pl.multiple_of(step * 64, 64)
        span = pl.ds(pl.multiple_of(2 * start, 128), 128)
        for c in range(width // LANES):
            lanes = slice(c * LANES, (c + 1) * LANES)
            scratch[c] = 0.5 * gelu_slope(x_ref[0, span, lanes].astype(jnp.float32))
            for parity in range(2):
                out_ref[parity, pl.ds(start, 64), lanes] = scratch[c, pl.ds(parity, 64, stride=2), :]


def half_slope(inputs):
    fine, width = inputs.shape[1:]
    return pl.pallas_call(
        slope_kernel,
        out_shape=jax.ShapeDtypeStruct((2, fine // 2, width), jnp.float32),
        in_specs=[pl.BlockSpec(memory_space=pltpu.VMEM)],
        out_specs=pl.BlockSpec(memory_space=pltpu.VMEM),
        scratch_shapes=[pltpu.VMEM((width // LANES, 128, LANES), jnp.float32)],
        compiler_params=pltpu.CompilerParams(vmem_limit_bytes=24 << 20),
        name="half_slope",
    )(inputs)


def start_act(place, coarse, layout, pieces, shifts_ref, held, shifts, sems, shift_sems):
    copies, row = [], 0
    for i, (distance, first, size, offset) in enumerate(layout):
        start = pl.multiple_of((place[0] ^ distance) * coarse + first, 16)
        spot = pl.ds(row, size)
        source = pieces[i].at[pl.ds(offset, size)]
        copies.append(pltpu.make_async_copy(source, held.at[spot], sems.at[i]))
        copies.append(
            pltpu.make_async_copy(shifts_ref.at[pl.ds(start, size)], shifts.at[spot], shift_sems.at[i])
        )
        row += size
    for copy in copies:
        copy.start()
    return copies


def early_terms(place, layout, pieces, shifts, coarse):
    both, columns = pieces[0].shape[1], shifts.shape[1]
    rows = sum(size for _, _, size, _ in layout)
    tile = 256

    def kernel(place, shifts_ref, *refs):
        pieces, total = refs[: len(layout)], refs[len(layout)]
        held, shifts, sems, shift_sems = refs[len(layout) + 1 :]
        copies = start_act(
            place, coarse, layout, pieces, shifts_ref, held, shifts, sems, shift_sems
        )
        for copy in copies:
            copy.wait()

        @pl.loop(0, both // tile)
        def _(i):
            span = pl.ds(pl.multiple_of(i * tile, tile), tile)
            total[span, :] = lax.dot_general(
                held[:, span], shifts[...], (((0,), (0,)), ((), ())), preferred_element_type=jnp.float32
            )

    return pl.pallas_call(
        kernel,
        out_shape=jax.ShapeDtypeStruct((both, columns), jnp.float32),
        grid_spec=pltpu.PrefetchScalarGridSpec(
            num_scalar_prefetch=1,
            grid=(1,),
            in_specs=[ANYWHERE] * (1 + len(pieces)),
            out_specs=pl.BlockSpec((both, columns), lambda i, place: (0, 0)),
            scratch_shapes=[
                pltpu.VMEM((rows, both), jnp.bfloat16),
                pltpu.VMEM((rows, columns), jnp.bfloat16),
                pltpu.SemaphoreType.DMA((len(pieces),)),
                pltpu.SemaphoreType.DMA((len(pieces),)),
            ],
        ),
        compiler_params=pltpu.CompilerParams(vmem_limit_bytes=48 << 20),
        cost_estimate=pl.CostEstimate(
            flops=2 * rows * both * columns, bytes_accessed=16 << 20, transcendentals=0
        ),
        name="weight_grad_early",
    )(place, shifts, *pieces)


def late_terms(place, layout, pieces, shifts, early, coarse, scale, planes, taps, rows):
    both, columns = early.shape
    width, block = both // 2, columns // 3
    count = sum(size for _, _, size, _ in layout)
    tile = 256
    shape = (planes, taps, rows, block)

    def kernel(place, shifts_ref, early_ref, *refs):
        pieces, (mine_ref, theirs_ref) = refs[: len(layout)], refs[len(layout) : len(layout) + 2]
        held, shifts, total, sems, shift_sems, early_sems = refs[len(layout) + 2 :]
        core, plane = place[1] % 2, place[1] // 2
        copies = start_act(
            place, coarse, layout, pieces, shifts_ref, held, shifts, sems, shift_sems
        )

        def fetch(i):
            span = pl.ds(pl.multiple_of(i * tile, tile), tile)
            return pltpu.make_async_copy(early_ref.at[span], total.at[span], early_sems.at[i])

        for i in range(both // tile):
            fetch(i).start()
        for copy in copies:
            copy.wait()

        @pl.loop(0, both // tile)
        def _(i):
            span = pl.ds(pl.multiple_of(i * tile, tile), tile)
            term = lax.dot_general(
                held[:, span], shifts[...], (((0,), (0,)), ((), ())), preferred_element_type=jnp.float32
            )
            fetch(i).wait()
            total[span, :] += term

        for out_ref, parity, kind in (
            (theirs_ref, 1 - core, jnp.bfloat16),
            (mine_ref, core, jnp.float32),
        ):

            @pl.loop(0, planes)
            def _(j):
                start = ((plane ^ j) * 2 + parity) * rows
                even = pl.ds(pl.multiple_of(start, 16), rows)
                odd = pl.ds(pl.multiple_of(width + start, 16), rows)
                for k, (left, right) in enumerate(GRAD_PARTS):
                    term = total[even, left * block : (left + 1) * block]
                    term += total[odd, right * block : (right + 1) * block]
                    out_ref[j, k] = (scale * term).astype(kind)

    whole = pl.BlockSpec(shape, lambda i, place: (0, 0, 0, 0))
    return pl.pallas_call(
        kernel,
        out_shape=(
            jax.ShapeDtypeStruct(shape, jnp.float32),
            jax.ShapeDtypeStruct(shape, jnp.bfloat16),
        ),
        grid_spec=pltpu.PrefetchScalarGridSpec(
            num_scalar_prefetch=1,
            grid=(1,),
            in_specs=[ANYWHERE] * (2 + len(pieces)),
            out_specs=[whole, whole],
            scratch_shapes=[
                pltpu.VMEM((count, both), jnp.bfloat16),
                pltpu.VMEM((count, columns), jnp.bfloat16),
                pltpu.VMEM((both, columns), jnp.float32),
                pltpu.SemaphoreType.DMA((len(pieces),)),
                pltpu.SemaphoreType.DMA((len(pieces),)),
                pltpu.SemaphoreType.DMA((both // tile,)),
            ],
        ),
        compiler_params=pltpu.CompilerParams(vmem_limit_bytes=48 << 20),
        cost_estimate=pl.CostEstimate(
            flops=2 * count * both * columns, bytes_accessed=16 << 20, transcendentals=0
        ),
        name="weight_grad_late",
    )(place, shifts, early, *pieces)


def shifted_total(products, base, lanes, parity):
    total = None
    for by in (0, 1, -1):
        wanted = [k for k in range(products.shape[0]) if ROW_OFFSETS[k][parity] == by]
        if wanted:
            near = pl.ds(base + MARGIN - 8, STEP + 16)
            part = sum(products[k, near, lanes] for k in wanted)[8 + by : 8 + by + STEP]
            total = part if total is None else total + part
    return total


def gradient_stage(place, windows, pieces, distances, slope, begun, shape):
    _, fine, width = shape
    coarse, seqs = fine // 2, len(windows)
    taps, rows, block = pieces[0][0].shape[1:]
    planes = width // (2 * rows)
    packed = (coarse + 2 * HALO) // CHUNKS
    window, used = CHUNKS * packed, coarse + 2 * MARGIN
    depth, planar = len(distances) * block, (2, coarse, width)
    last = begun is not None
    needed = distances if last else list(range(seqs))
    parts = [(d, *part) for d in needed for part in windows[d]]
    operands = [part[1] for part in parts] + [piece[0] for piece in pieces]
    operands += [slope] + ([begun] if last else [])

    def body(place, *refs):
        own, refs = refs[: len(parts)], refs[len(parts) :]
        sources, refs = refs[: len(pieces)], refs[len(pieces) :]
        slope_ref, refs = refs[0], refs[1:]
        if last:
            begun_ref, refs = refs[0], refs[1:]
        out_ref, wv, gv, products, slopes, sems, grad_sems, slope_sem = refs[:8]
        me, core = place[0], place[1] % 2

        def kernel_copies(k):
            for number, (array, plane, flip, distance) in enumerate(pieces):
                spot = pl.ds(distances.index(distance) * block, block)
                span = pl.ds(plane, array.shape[0])
                target = wv.at[k, span, core ^ flip, :, spot]
                yield sources[number].at[:, k], target, sems.at[k, number]

        def window_copies(target_of, sems):
            for number, (distance, _, row, first, size) in enumerate(parts):
                for q in range(CHUNKS):
                    source = own[number].at[pl.ds(row, size), pl.ds(q * block, block)]
                    target = target_of(distance, pl.ds(q * packed + first, size))
                    if target is not None:
                        yield pltpu.make_async_copy(source, target, sems.at[number, q])

        def into_window(distance, span):
            if distance not in distances:
                return None
            return gv.at[span, pl.ds(distances.index(distance) * block, block)]

        early = list(window_copies(into_window, grad_sems))
        late = [pltpu.make_async_copy(slope_ref, slopes, slope_sem)]
        if last:
            sums, strip, sum_sem = refs[8:]
            late.append(pltpu.make_async_copy(begun_ref, sums, sum_sem))
        else:
            skips, skip_sems = refs[8:]
            late += window_copies(lambda d, span: skips.at[me ^ d, span], skip_sems)
        for copy in early:
            copy.start()
        for k in range(taps):
            for copy in kernel_copies(k):
                pltpu.make_async_copy(*copy).start()
        for copy in late:
            copy.start()
        for copy in early:
            copy.wait()

        @pl.loop(0, taps)
        def _(k):
            for copy in kernel_copies(k):
                pltpu.make_async_copy(*copy).wait()
            half = planes // 2
            for part in range(2):
                kernel = wv[k, part * half : (part + 1) * half].reshape(2 * half * rows, depth)
                lanes = slice(part * 2 * half * rows, (part + 1) * 2 * half * rows)
                products[k, :, lanes] = lax.dot_general(
                    gv[EDGE : EDGE + used],
                    kernel,
                    (((1,), (1,)), ((), ())),
                    preferred_element_type=jnp.float32,
                )

        for copy in late:
            copy.wait()

        @pl.loop(0, coarse // STEP)
        def _(i):
            base = pl.multiple_of(i * STEP, STEP)
            spot, span = pl.ds(base, STEP), pl.ds(pl.multiple_of(2 * base, 2 * STEP), 2 * STEP)
            for c in range(width // LANES):
                lanes = slice(c * LANES, (c + 1) * LANES)
                if not last:
                    left = c * LANES % block
                    skip = skips[c * LANES // block, pl.ds(base + HALO, STEP), left : left + LANES]
                    skip = 0.5 * skip.astype(jnp.float32)
                for parity in range(2):
                    total = shifted_total(products, base, lanes, parity)
                    total = total * slopes[parity, spot, lanes]
                    if last:
                        total = total + sums[parity, spot, lanes]
                        strip[c, pl.ds(parity, STEP, stride=2), :] = total
                    else:
                        out_ref[parity, spot, lanes] = total + skip
                if last:
                    out_ref[0, span, lanes] = strip[c].astype(jnp.bfloat16)

    out_shape = jax.ShapeDtypeStruct(shape if last else planar, jnp.bfloat16 if last else jnp.float32)
    scratch = [
        pltpu.VMEM((taps, planes, 2, rows, depth), jnp.bfloat16),
        pltpu.VMEM((window, depth), jnp.bfloat16),
        pltpu.VMEM((taps, used, width), jnp.float32),
        pltpu.VMEM(planar, jnp.float32),
        pltpu.SemaphoreType.DMA((taps, len(pieces))),
        pltpu.SemaphoreType.DMA((len(parts), CHUNKS)),
        pltpu.SemaphoreType.DMA,
    ]
    if last:
        scratch += [
            pltpu.VMEM(planar, jnp.float32),
            pltpu.VMEM((width // LANES, 2 * STEP, LANES), jnp.float32),
            pltpu.SemaphoreType.DMA,
        ]
    else:
        scratch += [
            pltpu.VMEM((seqs, window, block), jnp.bfloat16),
            pltpu.SemaphoreType.DMA((len(parts), CHUNKS)),
        ]
    return pl.pallas_call(
        body,
        out_shape=out_shape,
        grid_spec=pltpu.PrefetchScalarGridSpec(
            num_scalar_prefetch=1,
            grid=(1,),
            in_specs=[ANYWHERE] * len(operands),
            out_specs=pl.BlockSpec(out_shape.shape, lambda i, place: (0, 0, 0)),
            scratch_shapes=scratch,
        ),
        compiler_params=pltpu.CompilerParams(vmem_limit_bytes=56 << 20),
        cost_estimate=pl.CostEstimate(
            flops=2 * taps * window * width * depth, bytes_accessed=20 << 20, transcendentals=0
        ),
        name="input_grad_late" if last else "input_grad_early",
    )(place, *operands)


def stack_planes(place, line):
    count = len(line)

    def kernel(place, *refs):
        parts, out_ref, sems = refs[:count], refs[count], refs[count + 1]
        copies = [
            pltpu.make_async_copy(parts[j], out_ref.at[place[1] // 2 ^ j], sems.at[j])
            for j in range(count)
        ]
        for copy in copies:
            copy.start()
        for copy in copies:
            copy.wait()

    return pl.pallas_call(
        kernel,
        out_shape=jax.ShapeDtypeStruct((count, *line[0].shape), line[0].dtype),
        grid_spec=pltpu.PrefetchScalarGridSpec(
            num_scalar_prefetch=1,
            grid=(1,),
            in_specs=[ANYWHERE] * count,
            out_specs=ANYWHERE,
            scratch_shapes=[pltpu.SemaphoreType.DMA((count,))],
        ),
        name="stack_planes",
    )(place, *line)


def on_device_square(inputs, trunk_grad, weights):
    seqs, reps = lax.axis_size("seq"), lax.axis_size("rep")
    me, rep = lax.axis_index("seq"), lax.axis_index("rep")
    place = jnp.stack([me, rep]).astype(jnp.int32)
    taps, rows, block = weights.shape
    fine = inputs.shape[1]
    coarse, planes = fine // 2, reps // 2
    packed = (coarse + 2 * HALO) // CHUNKS
    half = coarse // 2

    to_beside, to_below, own_window = messages(place, inputs, trunk_grad)
    beside, below = from_peer(to_beside, "seq", 1), from_peer(to_below, "seq", 2)
    slope = half_slope(inputs)
    line = gather_line(weights, "rep", planes, 2)
    top = after(beside[: FIRST + half], slope, *line[1:])
    bottom = after(below[half : coarse + packed - FIRST], slope, *line[1:])
    far_top, far_bottom = from_peer(top, "seq", 2), from_peer(bottom, "seq", 1)

    column = after(stack_planes(place, line), beside, below)
    kept_beside, kept_below = from_peer(column, "seq", 1), from_peer(column, "seq", 2)
    kept = [
        (column, 0, 0),
        (kept_beside, 0, 1),
        (kept_below, 0, 2),
        (from_peer(kept_beside[: planes // 2], "seq", 2), 0, 3),
        (from_peer(kept_below[planes // 2 :], "seq", 1), planes // 2, 3),
    ]
    pieces = []
    for part, plane, distance in kept:
        pieces.append((part, plane, 0, distance))
        pieces.append((from_peer(part, "rep", 1), plane, 1, distance))

    trunk = trunk_grad[0]
    zeros = jnp.zeros((1, block), jnp.bfloat16)
    later = jnp.concatenate([trunk[1:], zeros])
    earlier = jnp.concatenate([zeros, trunk[:-1]])
    shifts = jnp.concatenate([later, trunk, earlier], axis=1)
    scale = 0.5 * float(fine * seqs * reps) ** (-0.5)
    near_rows = [(0, 0, coarse, FIRST), (1, 0, coarse, FIRST), (2, 0, coarse, 0)]
    far_rows = [(3, 0, half, FIRST), (3, half, half, 0)]
    early = early_terms(place, near_rows, [to_beside, beside, below], shifts, coarse)
    mine, theirs = late_terms(
        place, far_rows, [far_top, far_bottom], shifts, early, coarse, scale, planes, taps, rows
    )
    arrived = from_peer(theirs, "rep", 1)
    weight_grad = mine[0] + arrived[0].astype(jnp.float32)
    for j in range(1, planes):
        leaving = (mine[j] + arrived[j].astype(jnp.float32)).astype(jnp.bfloat16)
        weight_grad = weight_grad + from_peer(leaving, "rep", 2 * j).astype(jnp.float32)

    windows = [
        [(own_window, 0, 0, packed)],
        [(beside, FIRST + coarse, 0, packed)],
        [(below, coarse + packed - FIRST, 0, packed)],
        [(far_top, 0, 0, FIRST), (far_bottom, half, FIRST, packed - FIRST)],
    ]
    stage = functools.partial(gradient_stage, place, windows, slope=slope, shape=inputs.shape)
    soon, rest = ([p for p in pieces if (p[3] == 3) == far] for far in (False, True))
    begun = stage(soon, [0, 1, 2], begun=None)
    input_grad = stage(rest, [3], begun=begun)
    return (input_grad, weight_grad)


def with_halo(value, sides, width):
    for axis, dim in sides:
        peers, length = (lax.axis_size(axis), value.shape[dim])
        up = [(i, (i + 1) % peers) for i in range(peers - 1)]
        down = [(j, i) for i, j in up]
        last = lax.slice_in_dim(value, length - width, length, axis=dim)
        leading = lax.slice_in_dim(value, 0, width, axis=dim)
        before = lax.ppermute(last, axis, up)
        after = lax.ppermute(leading, axis, down)
        value = jnp.concatenate([before, value, after], axis=dim)
    return value


def contract_last(left, right):
    return lax.dot_general(
        left, right, (((1,), (1,)), ((), ())), preferred_element_type=jnp.float32
    )


def contract_first(left, right):
    return lax.dot_general(
        left, right, (((0,), (0,)), ((), ())), preferred_element_type=jnp.float32
    )


def on_device_plain(inputs, trunk_grad, weights):
    taps = weights.shape[0]
    grad = lax.all_to_all(trunk_grad, "seq", split_axis=1, concat_axis=2, tiled=True)
    grad_up = jnp.repeat(grad.astype(jnp.float32) * 0.5, 2, axis=1).astype(jnp.bfloat16)
    rows = grad_up.shape[1]
    padded = with_halo(grad_up, (("seq", 1),), 2)
    shifts = [padded[0, 4 - k : 4 - k + rows] for k in range(taps)]
    inputs_f = inputs[0].astype(jnp.float32)
    act_vals, back = jax.vjp(jax.nn.gelu, inputs_f)
    slope = back(jnp.ones_like(inputs_f))[0]
    act = act_vals.astype(jnp.bfloat16)
    in_width = inputs.shape[2]
    columns = lax.all_gather(weights, "seq", axis=2, tiled=True)
    piece = lax.all_gather(columns, "rep", axis=1, tiled=True)
    result = contract_last(shifts[0], piece[0])
    for project_k in range(1, taps):
        result = result + contract_last(shifts[project_k], piece[project_k])
    input_grad = (result * slope + grad_up[0, :, :in_width].astype(jnp.float32)).astype(
        jnp.bfloat16
    )
    scale_factor = float(rows * lax.axis_size("seq") * lax.axis_size("rep")) ** (-0.5)
    terms = jnp.stack([contract_first(act, shifts[k]) for k in range(taps)]) * scale_factor
    partial_sum = lax.psum_scatter(terms, "rep", scatter_dimension=1, tiled=True)
    weight_grad = lax.psum_scatter(partial_sum, "seq", scatter_dimension=2, tiled=True)
    return (input_grad[None], weight_grad)


def on_device(inputs, trunk_grad, weights):
    square = lax.axis_size("seq") == 4 and lax.axis_size("rep") % 8 == 0
    if square and weights.shape[2] % LANES == 0 and inputs.shape[2] % LANES == 0:
        return on_device_square(inputs, trunk_grad, weights)
    return on_device_plain(inputs, trunk_grad, weights)


def solution(mesh):
    in_specs = (P("rep", "seq", None), P("rep", None, "seq"), P(None, "rep", "seq"))
    out_specs = (P("rep", "seq", None), P(None, "rep", "seq"))
    return jax.shard_map(
        on_device, mesh=mesh, in_specs=in_specs, out_specs=out_specs, check_vma=False
    )
```

time: 191 us -> 235 us (1.23)
  Pallas kernels: 48.3 us -> 98.2 us
  waiting for transfers between devices: 65.9 us -> 85.7 us
  between operations: 14.3 us -> 0.92 us
  blocking collectives: 9.99 us -> 0 us
  local copies, waits for them, and re-layouts: 22.8 us -> 14.4 us
  starting transfers between devices: 18.6 us -> 26 us
  other arithmetic: 9.8 us -> 6.63 us
    pallas_call x1 -> x2, Pallas kernels: 2.92 us -> 49.2 us  [the longest x1 46.5 us: stack_planes(): pl.pallas_call(kernel, out_shape=jax.ShapeDtypeStruct((count, *line[0].sh...]
    ppermute x18 -> x20, waiting for transfers between devices: 65.8 us -> 85.7 us  [from_peer(): return lax.ppermute(value, axis, [(i, i ^ distance) for i in range(peers)])]
    all_gather x1 -> x0, blocking collectives: 9.99 us -> none  [on_device(): last = lax.all_gather(lax.all_gather(weights[SPLIT:], 'seq'), 'rep')]
    ppermute x18 -> x20, starting transfers between devices: 18.5 us -> 26 us  [from_peer(): return lax.ppermute(value, axis, [(i, i ^ distance) for i in range(peers)])]
    slice x7 -> x5, local copies, waits for them, and re-layouts: 10.5 us -> 5.62 us  [the longest x1 2.28 us: on_device_square(): top = after(beside[:FIRST + half], slope, *line[1:])]
    pallas_call x2, Pallas kernels: 19.8 us -> 23 us  [gradient_stage(): pl.pallas_call(body, out_shape=out_shape, grid_spec=pltpu.PrefetchScalarG...]
    unnamed x34 -> x46, local copies, waits for them, and re-layouts: 6.25 us -> 8.8 us
    dynamic_slice x1 -> x0, local copies, waits for them, and re-layouts: 2.43 us -> none  [on_device(): lax.dynamic_slice_in_dim(edged, (me ^ distance) * coarse, coarse + 2 * HA...]
  transfers between devices with their start and end apart: 20 -> 20, of which waited for: 5 -> 8; matrix products, arithmetic and copies ran while one was open for 13% -> 5% of each run, Pallas kernels for 20% -> 37%
where the time goes in v8:
time: 235 us; the launch traced here: 232 us
  Pallas kernels  98.2 us (42%)
  waiting for transfers between devices  85.7 us (36%)
  starting transfers between devices  26 us (11%)
  local copies, waits for them, and re-layouts  14.4 us (6%)
  other arithmetic  6.63 us (3%)
    ppermute x20, waiting for transfers between devices, from_peer(): return lax.ppermute(value, axis, [(i, i ^ distance) for i in range(peers)])  85.7 us
    pallas_call x1, Pallas kernels, stack_planes(): pl.pallas_call(kernel, out_shape=jax.ShapeDtypeStruct((count, *line[0].sh...  46.5 us
    ppermute x20, starting transfers between devices, from_peer(): return lax.ppermute(value, axis, [(i, i ^ distance) for i in range(peers)])  26 us
    pallas_call x2, Pallas kernels, gradient_stage(): pl.pallas_call(body, out_shape=out_shape, grid_spec=pltpu.PrefetchScalarG...  23 us
    pallas_call x1, Pallas kernels, early_terms(): pl.pallas_call(kernel, out_shape=jax.ShapeDtypeStruct((both, columns), jn...  13.4 us
    pallas_call x1, Pallas kernels, late_terms(): pl.pallas_call(kernel, out_shape=(jax.ShapeDtypeStruct(shape, jnp.float32...  10.2 us
    unnamed x46, local copies, waits for them, and re-layouts  8.8 us
    concatenate x1, other arithmetic, on_device_square(): shifts = jnp.concatenate([later, trunk, earlier], axis=1)  5.24 us
  transfers between devices with their start and end apart: 20, of which 8 were waited for; matrix products, arithmetic and copies ran while one was open for 5% of the time, Pallas kernels for 37%

profile of v8, /device:TPU:9, one launch (start us, length us, event | category | flops | bytes accessed | tf_op | source)
XLA Modules:
  0.0 231.9 jit_solution(17488855866877933159)
XLA Ops:
  0.6 0.1 pad_add_fusion.place
  0.7 1.4 copy-done.1
  2.1 1.4 copy-done.6
  3.5 2.8 %messages.1 = (bf16[736,1536]{1,0:T(8,128)(2,1)S(1)}, bf16[720,1536]{1,0:T(8,128)(2,1)S(1)}, bf16[144,1536]{1,0:T(8,128)(2,1)S(1)}) custom-call(s32[2]{0:T(128)S(1)} %pad_add_fusion.place, bf16[1,1024,768]{2,1,0:T(8,128)(2,1)S(1)} %copy-done.6, bf16[1,2048,384]{2,1,0:T(8,128)(2,1)S(1)} %copy-done.1), custom_call_target="tpu_custom_call" | custom-call | tf_op jit(solution)/shard_map/messages/pallas_call | solution.py:103
  6.3 1.3 collective-permute-start
  7.6 1.2 collective-permute-start.5
  8.8 1.3 collective-permute-start.2
  10.1 2.2 collective-permute-start.1
  12.3 2.4 %half_slope.1.refs_1_.refs_11_.refs_6_ = f32[2,512,768]{2,1,0:T(8,128)S(1)} custom-call(bf16[1,1024,768]{2,1,0:T(8,128)(2,1)S(1)} %copy-done.6), custom_call_target="tpu_custom_call" | custom-call | tf_op jit(solution)/shard_map/half_slope/pallas_call | solution.py:138
  14.7 11.7 %collective-permute-done.2.refs_4_.refs_3_ = bf16[5,96,384]{2,1,0:T(8,128)(2,1)S(1)} collective-permute-done((bf16[5,96,384]{2,1,0:T(8,128)(2,1)S(1)}, bf16[5,96,384]{2,1,0:T(8,128)(2,1)S(1)}, u32[]{:S(2)}, u32[]{:S(2)}) %collective-permute-start.2) | collective-permute-done | bytes 368672 | tf_op jit(solution)/shard_map/ppermute | solution.py:27
  26.4 2.1 slice_bitcast_fusion.1
  28.6 27.8 %collective-permute-done.5.refs_2_ = bf16[720,1536]{1,0:T(8,128)(2,1)S(1)} collective-permute-done((bf16[720,1536]{1,0:T(8,128)(2,1)S(1)}, bf16[720,1536]{1,0:T(8,128)(2,1)S(1)}, u32[]{:S(2)}, u32[]{:S(2)}) %collective-permute-start.5) | collective-permute-done | bytes 2211872 | tf_op jit(solution)/shard_map/ppermute | solution.py:27
  56.3 1.3 copy-done.3
  57.7 1.1 slice.65.refs_0_
  58.8 0.7 copy-done.14
  59.5 0.3 collective-permute-start.6
  59.8 2.3 slice.64.refs_0_
  62.0 1.2 collective-permute-start.4
  63.3 0.2 copy-done.2
  63.4 5.2 %fusion.2.shifts_ref = bf16[2048,1152]{1,0:T(8,128)(2,1)} fusion(bf16[2047,384]{1,0:T(8,128)(2,1)} %get-tuple-element.16, bf16[2047,384]{1,0:T(8,128)(2,1)} %get-tuple-element.15, bf16[2048,384]{1,0:T(8,128)(2,1)S(1)} %bitcast.19), kind=kLoop, calls=%fused_computation.4 | loop fusion | flops 23592960 | bytes 9435648 | tf_op jit(solution)/shard_map/concatenate | solution.py:500
  68.7 46.5 %stack_planes.1.refs_0_ = bf16[4,5,96,384]{3,2,1,0:T(8,128)(2,1)} custom-call(s32[2]{0:T(128)} %copy-done.8, bf16[5,96,384]{2,1,0:T(8,128)(2,1)} %refs_0_.1, bf16[5,96,384]{2,1,0:T(8,128)(2,1)} %copy-done.14, bf16[5,96,384]{2,1,0:T(8,128)(2,1)} %collective-permute-done.3.refs_3_.refs_2_, bf16[5,96,384]{2,1,0:T(8,128)(2,1)} %copy-done.13), custom_call_target="tpu_custom_call" | custom-call | tf_op jit(solution)/shard_map/stack_planes/pallas_call | solution.py:450
  115.2 1.3 collective-permute-start.7
  116.5 1.2 collective-permute-start.10
  117.7 1.6 copy-done.11
  119.4 13.4 %weight_grad_early.1.early_ref = f32[1536,1152]{1,0:T(8,128)} custom-call(s32[2]{0:T(128)S(1)} %copy-done.9, bf16[2048,1152]{1,0:T(8,128)(2,1)} %fusion.2.shifts_ref, bf16[736,1536]{1,0:T(8,128)(2,1)S(1)} %copy-done.11, bf16[736,1536]{1,0:T(8,128)(2,1)} %collective-permute-done.refs_1_, bf16[720,1536]{1,0:T(8,128)(2,1)S(1)} %copy-done.4), custom_call_target="tpu_custom_call" | custom-call | flops 5435817984 | bytes 16777216 | tf_op jit(solution)/shard_map/weight_grad_early/pallas_call | solution.py:186
  132.8 10.2 %weight_grad_late.1 = (f32[4,5,96,384]{3,2,1,0:T(8,128)}, bf16[4,5,96,384]{3,2,1,0:T(8,128)(2,1)S(1)}) custom-call(s32[2]{0:T(128)S(1)} %copy-done.9, bf16[2048,1152]{1,0:T(8,128)(2,1)} %fusion.2.shifts_ref, f32[1536,1152]{1,0:T(8,128)} %weight_grad_early.1.early_ref, bf16[336,1536]{1,0:T(8,128)(2,1)S(1)} %collective-permute-done.4.refs_3_.refs_0_, ...), custom_call_target="tpu_custom_call" | custom-call | flops 1811939328 | bytes 16777216 | tf_op jit(solution)/shard_map/weight_grad_late/pallas_call | solution.py:258
  143.0 2.6 %collective-permute-start.16 = (bf16[4,5,96,384]{3,2,1,0:T(8,128)(2,1)S(1)}, bf16[4,5,96,384]{3,2,1,0:T(8,128)(2,1)S(1)}, u32[]{:S(2)}, u32[]{:S(2)}) collective-permute-start(bf16[4,5,96,384]{3,2,1,0:T(8,128)(2,1)S(1)} %get-tuple-element.11), channel_id=1, source_target_pairs={{0,1},{1,0},{2,3},{3,2},{4,5},{5,4},{6,7},{7,6},{8,9},{9,8},{10,11... | collective-permute-start | bytes 4423688 | tf_op jit(solution)/shard_map/ppermute | solution.py:27
  145.7 1.4 collective-permute-done.7.refs_7_
  147.2 1.4 collective-permute-start.8
  148.6 3.2 %collective-permute-start.13 = (bf16[4,5,96,384]{3,2,1,0:T(8,128)(2,1)S(1)}, bf16[4,5,96,384]{3,2,1,0:T(8,128)(2,1)S(1)}, u32[]{:S(2)}, u32[]{:S(2)}) collective-permute-start(bf16[4,5,96,384]{3,2,1,0:T(8,128)(2,1)S(1)} %copy-done.12), channel_id=1, source_target_pairs={{0,1},{1,0},{2,3},{3,2},{4,5},{5,4},{6,7},{7,6},{8,9},{9,8},{10,11... | collective-permute-start | bytes 4423688 | tf_op jit(solution)/shard_map/ppermute | solution.py:27
  151.9 0.5 collective-permute-start.15
  152.5 1.3 collective-permute-start.11
  153.7 0.3 fusion.6
  154.0 10.3 %collective-permute-done.8.refs_2_ = bf16[2,5,96,384]{3,2,1,0:T(8,128)(2,1)S(1)} collective-permute-done((bf16[2,5,96,384]{3,2,1,0:T(8,128)(2,1)S(1)}, bf16[2,5,96,384]{3,2,1,0:T(8,128)(2,1)S(1)}, u32[]{:S(2)}, u32[]{:S(2)}) %collective-permute-start.8) | collective-permute-done | bytes 737312 | tf_op jit(solution)/shard_map/ppermute | solution.py:27
  164.3 1.3 collective-permute-start.19
  165.6 5.0 %collective-permute-done.11.refs_4_ = bf16[2,5,96,384]{3,2,1,0:T(8,128)(2,1)} collective-permute-done((bf16[2,5,96,384]{3,2,1,0:T(8,128)(2,1)S(1)}, bf16[2,5,96,384]{3,2,1,0:T(8,128)(2,1)}, u32[]{:S(2)}, u32[]{:S(2)}) %collective-permute-start.11) | collective-permute-done | bytes 737312 | tf_op jit(solution)/shard_map/ppermute | solution.py:27
  170.7 2.3 collective-permute-start.18
  173.0 16.7 %collective-permute-done.19 = bf16[5,96,384]{2,1,0:T(8,128)(2,1)S(1)} collective-permute-done((bf16[5,96,384]{2,1,0:T(8,128)(2,1)S(1)}, bf16[5,96,384]{2,1,0:T(8,128)(2,1)S(1)}, u32[]{:S(2)}, u32[]{:S(2)}) %collective-permute-start.19) | collective-permute-done | bytes 368672 | tf_op jit(solution)/shard_map/ppermute | solution.py:27
  189.7 6.0 %collective-permute-done.18 = bf16[5,96,384]{2,1,0:T(8,128)(2,1)S(1)} collective-permute-done((bf16[5,96,384]{2,1,0:T(8,128)(2,1)S(1)}, bf16[5,96,384]{2,1,0:T(8,128)(2,1)S(1)}, u32[]{:S(2)}, u32[]{:S(2)}) %collective-permute-start.18) | collective-permute-done | bytes 368672 | tf_op jit(solution)/shard_map/ppermute | solution.py:27
  195.7 2.5 %collective-permute-start.9 = (bf16[2,5,96,384]{3,2,1,0:T(8,128)(2,1)S(1)}, bf16[2,5,96,384]{3,2,1,0:T(8,128)(2,1)}, u32[]{:S(2)}, u32[]{:S(2)}) collective-permute-start(bf16[2,5,96,384]{3,2,1,0:T(8,128)(2,1)S(1)} %collective-permute-done.8.refs_2_), channel_id=1, source_target_pairs={{0,1},{1,0},{2,3},{3,2},{4,5},{5,4},{6,7},{7,6},{8,9},{9,8},{10,11... | collective-permute-start | bytes 2211848 | tf_op jit(solution)/shard_map/ppermute | solution.py:27
  198.2 6.7 %collective-permute-done.17 = bf16[5,96,384]{2,1,0:T(8,128)(2,1)S(1)} collective-permute-done((bf16[5,96,384]{2,1,0:T(8,128)(2,1)S(1)}, bf16[5,96,384]{2,1,0:T(8,128)(2,1)S(1)}, u32[]{:S(2)}, u32[]{:S(2)}) %collective-permute-start.17) | collective-permute-done | bytes 368672 | tf_op jit(solution)/shard_map/ppermute | solution.py:27
  204.9 0.8 collective-permute-start.12
  205.7 1.1 fusion.5
  206.8 1.1 copy-done.18
  207.9 0.5 copy-done.19
  208.3 0.5 copy-done.20
  208.8 14.1 %input_grad_early.1.refs_7_ = f32[2,512,768]{2,1,0:T(8,128)} custom-call(s32[2]{0:T(128)} %copy-done.8, bf16[144,1536]{1,0:T(8,128)(2,1)} %copy-done.7, bf16[736,1536]{1,0:T(8,128)(2,1)} %collective-permute-done.refs_1_, bf16[720,1536]{1,0:T(8,128)(2,1)} %copy-done.3, bf16[336,1536]{1,0:T(8,128)(2,1)} %copy-done.5, ...), custom_call_target="tpu_custom_call" | custom-call | flops 5096079360 | bytes 20971520 | tf_op jit(solution)/shard_map/input_grad_early/pallas_call | solution.py:418
  222.9 9.0 %input_grad_late.1 = bf16[1,1024,768]{2,1,0:T(8,128)(2,1)} custom-call(s32[2]{0:T(128)} %copy-done.8, bf16[336,1536]{1,0:T(8,128)(2,1)} %copy-done.5, bf16[320,1536]{1,0:T(8,128)(2,1)} %collective-permute-done.6.refs_4_.refs_1_, bf16[2,5,96,384]{3,2,1,0:T(8,128)(2,1)} %copy-done.21, bf16[2,5,96,384]{3,2,1,0:T(8,128)(2,1)} %collective-permute-done.9.refs_3_, ...), custom_call_target="tpu_custom_call" | custom-call | flops 1698693120 | bytes 20971520 | tf_op jit(solution)/shard_map/input_grad_late/pallas_call | solution.py:418
  (57 shorter events, 0.3 us)
Async XLA Ops:
  0.7 1.4 copy-start.1
  2.1 1.4 copy-start.6
  3.5 11.2 %copy-start.8 = (s32[2]{0:T(128)}, s32[2]{0:T(128)S(1)}, u32[]{:S(2)}) copy-start(s32[2]{0:T(128)S(1)} %pad_add_fusion.place) | copy-start | bytes 28
  3.5 5.3 %copy-start.22 = (bf16[5,96,384]{2,1,0:T(8,128)(2,1)S(1)}, bf16[5,96,384]{2,1,0:T(8,128)(2,1)}, u32[]{:S(2)}) copy-start(bf16[5,96,384]{2,1,0:T(8,128)(2,1)} %refs_0_.1) | copy-start | bytes 1105924
  6.3 8.4 %copy-start.7 = (bf16[144,1536]{1,0:T(8,128)(2,1)}, bf16[144,1536]{1,0:T(8,128)(2,1)S(1)}, u32[]{:S(2)}) copy-start(bf16[144,1536]{1,0:T(8,128)(2,1)S(1)} %get-tuple-element.9.refs_0_) | copy-start | bytes 1327108
  6.3 8.4 %copy-start.10 = (bf16[736,1536]{1,0:T(8,128)(2,1)}, bf16[736,1536]{1,0:T(8,128)(2,1)S(1)}, u32[]{:S(2)}) copy-start(bf16[736,1536]{1,0:T(8,128)(2,1)S(1)} %get-tuple-element.7.refs_0_) | copy-start | bytes 6782980
  6.3 53.4 %collective-permute-start = (bf16[736,1536]{1,0:T(8,128)(2,1)S(1)}, bf16[736,1536]{1,0:T(8,128)(2,1)}, u32[]{:S(2)}, u32[]{:S(2)}) collective-permute-start(bf16[736,1536]{1,0:T(8,128)(2,1)S(1)} %get-tuple-element.7.refs_0_), channel_id=1, source_target_pairs={{0,8},{8,0},{16,24},{24,16},{1,9},{9,1},{17,25},{25,17},{2,10},{10... | collective-permute-start | bytes 6782984 | tf_op jit(solution)/shard_map/ppermute | solution.py:27
  7.6 48.7 %collective-permute-start.5 = (bf16[720,1536]{1,0:T(8,128)(2,1)S(1)}, bf16[720,1536]{1,0:T(8,128)(2,1)S(1)}, u32[]{:S(2)}, u32[]{:S(2)}) collective-permute-start(bf16[720,1536]{1,0:T(8,128)(2,1)S(1)} %get-tuple-element.8), channel_id=1, source_target_pairs={{0,16},{8,24},{16,0},{24,8},{1,17},{9,25},{17,1},{25,9},{2,18},{10... | collective-permute-start | bytes 6635528 | tf_op jit(solution)/shard_map/ppermute | solution.py:27
  8.8 17.6 %collective-permute-start.2 = (bf16[5,96,384]{2,1,0:T(8,128)(2,1)S(1)}, bf16[5,96,384]{2,1,0:T(8,128)(2,1)S(1)}, u32[]{:S(2)}, u32[]{:S(2)}) collective-permute-start(bf16[5,96,384]{2,1,0:T(8,128)(2,1)S(1)} %copy-done.22), channel_id=1, source_target_pairs={{0,6},{1,7},{2,4},{3,5},{4,2},{5,3},{6,0},{7,1},{8,14},{9,15},{10,... | collective-permute-start | bytes 1105928 | tf_op jit(solution)/shard_map/ppermute | solution.py:27
  10.1 48.6 %collective-permute-start.1 = (bf16[5,96,384]{2,1,0:T(8,128)(2,1)S(1)}, bf16[5,96,384]{2,1,0:T(8,128)(2,1)S(1)}, u32[]{:S(2)}, u32[]{:S(2)}) collective-permute-start(bf16[5,96,384]{2,1,0:T(8,128)(2,1)S(1)} %copy-done.22), channel_id=1, source_target_pairs={{0,2},{1,3},{2,0},{3,1},{4,6},{5,7},{6,4},{7,5},{8,10},{9,11},{10,... | collective-permute-start | bytes 1105928 | tf_op jit(solution)/shard_map/ppermute | solution.py:27
  14.7 13.8 %copy-start = (f32[2,512,768]{2,1,0:T(8,128)}, f32[2,512,768]{2,1,0:T(8,128)S(1)}, u32[]{:S(2)}) copy-start(f32[2,512,768]{2,1,0:T(8,128)S(1)} %half_slope.1.refs_1_.refs_11_.refs_6_) | copy-start | bytes 9437188
  26.4 2.1 copy-start.13
  26.4 32.3 %collective-permute-start.3 = (bf16[5,96,384]{2,1,0:T(8,128)(2,1)S(1)}, bf16[5,96,384]{2,1,0:T(8,128)(2,1)}, u32[]{:S(2)}, u32[]{:S(2)}) collective-permute-start(bf16[5,96,384]{2,1,0:T(8,128)(2,1)S(1)} %collective-permute-done.2.refs_4_.refs_3_), channel_id=1, source_target_pairs={{0,2},{1,3},{2,0},{3,1},{4,6},{5,7},{6,4},{7,5},{8,10},{9,11},{10,... | collective-permute-start | bytes 1105928 | tf_op jit(solution)/shard_map/ppermute | solution.py:27
  56.3 1.3 copy-start.3
  58.8 0.7 copy-start.14
  59.5 73.3 %collective-permute-start.6 = (bf16[320,1536]{1,0:T(8,128)(2,1)}, bf16[320,1536]{1,0:T(8,128)(2,1)}, u32[]{:S(2)}, u32[]{:S(2)}) collective-permute-start(bf16[320,1536]{1,0:T(8,128)(2,1)} %after.4), channel_id=1, source_target_pairs={{0,8},{8,0},{16,24},{24,16},{1,9},{9,1},{17,25},{25,17},{2,10},{10... | collective-permute-start | bytes 2949128 | tf_op jit(solution)/shard_map/ppermute | solution.py:27
  62.0 1.4 copy-start.2
  62.0 70.8 %collective-permute-start.4 = (bf16[336,1536]{1,0:T(8,128)(2,1)}, bf16[336,1536]{1,0:T(8,128)(2,1)S(1)}, u32[]{:S(2)}, u32[]{:S(2)}) collective-permute-start(bf16[336,1536]{1,0:T(8,128)(2,1)} %after.3), channel_id=1, source_target_pairs={{0,16},{8,24},{16,0},{24,8},{1,17},{9,25},{17,1},{25,9},{2,18},{10... | collective-permute-start | bytes 3096584 | tf_op jit(solution)/shard_map/ppermute | solution.py:27
  115.2 2.6 %copy-start.4 = (bf16[720,1536]{1,0:T(8,128)(2,1)S(1)}, bf16[720,1536]{1,0:T(8,128)(2,1)}, u32[]{:S(2)}) copy-start(bf16[720,1536]{1,0:T(8,128)(2,1)} %copy-done.3) | copy-start | bytes 6635524
  115.2 2.5 %copy-start.9 = (s32[2]{0:T(128)S(1)}, s32[2]{0:T(128)}, u32[]{:S(2)}) copy-start(s32[2]{0:T(128)} %copy-done.8) | copy-start | bytes 28
  115.2 31.9 %collective-permute-start.7 = (bf16[4,5,96,384]{3,2,1,0:T(8,128)(2,1)}, bf16[4,5,96,384]{3,2,1,0:T(8,128)(2,1)S(1)}, u32[]{:S(2)}, u32[]{:S(2)}) collective-permute-start(bf16[4,5,96,384]{3,2,1,0:T(8,128)(2,1)} %after.5.refs_5_), channel_id=1, source_target_pairs={{0,8},{8,0},{16,24},{24,16},{1,9},{9,1},{17,25},{25,17},{2,10},{10... | collective-permute-start | bytes 4423688 | tf_op jit(solution)/shard_map/ppermute | solution.py:27
  116.5 35.4 %collective-permute-start.10 = (bf16[4,5,96,384]{3,2,1,0:T(8,128)(2,1)}, bf16[4,5,96,384]{3,2,1,0:T(8,128)(2,1)S(1)}, u32[]{:S(2)}, u32[]{:S(2)}) collective-permute-start(bf16[4,5,96,384]{3,2,1,0:T(8,128)(2,1)} %after.5.refs_5_), channel_id=1, source_target_pairs={{0,16},{8,24},{16,0},{24,8},{1,17},{9,25},{17,1},{25,9},{2,18},{10... | collective-permute-start | bytes 4423688 | tf_op jit(solution)/shard_map/ppermute | solution.py:27
  117.7 1.6 copy-start.11
  132.8 15.8 %copy-start.12 = (bf16[4,5,96,384]{3,2,1,0:T(8,128)(2,1)S(1)}, bf16[4,5,96,384]{3,2,1,0:T(8,128)(2,1)}, u32[]{:S(2)}) copy-start(bf16[4,5,96,384]{3,2,1,0:T(8,128)(2,1)} %after.5.refs_5_) | copy-start | bytes 4423684
  132.8 10.2 %copy-start.5 = (bf16[336,1536]{1,0:T(8,128)(2,1)}, bf16[336,1536]{1,0:T(8,128)(2,1)S(1)}, u32[]{:S(2)}) copy-start(bf16[336,1536]{1,0:T(8,128)(2,1)S(1)} %collective-permute-done.4.refs_3_.refs_0_) | copy-start | bytes 3096580
  143.0 10.7 %copy-start.17 = (f32[4,5,96,384]{3,2,1,0:T(8,128)S(1)}, f32[4,5,96,384]{3,2,1,0:T(8,128)}, u32[]{:S(2)}) copy-start(f32[4,5,96,384]{3,2,1,0:T(8,128)} %get-tuple-element.10) | copy-start | bytes 8847364
  143.0 9.4 %collective-permute-start.16 = (bf16[4,5,96,384]{3,2,1,0:T(8,128)(2,1)S(1)}, bf16[4,5,96,384]{3,2,1,0:T(8,128)(2,1)S(1)}, u32[]{:S(2)}, u32[]{:S(2)}) collective-permute-start(bf16[4,5,96,384]{3,2,1,0:T(8,128)(2,1)S(1)} %get-tuple-element.11), channel_id=1, source_target_pairs={{0,1},{1,0},{2,3},{3,2},{4,5},{5,4},{6,7},{7,6},{8,9},{9,8},{10,11... | collective-permute-start | bytes 4423688 | tf_op jit(solution)/shard_map/ppermute | solution.py:27
  147.1 6.9 %copy-start.15 = (bf16[4,5,96,384]{3,2,1,0:T(8,128)(2,1)}, bf16[4,5,96,384]{3,2,1,0:T(8,128)(2,1)S(1)}, u32[]{:S(2)}) copy-start(bf16[4,5,96,384]{3,2,1,0:T(8,128)(2,1)S(1)} %collective-permute-done.7.refs_7_) | copy-start | bytes 4423684
  147.2 17.2 %collective-permute-start.8 = (bf16[2,5,96,384]{3,2,1,0:T(8,128)(2,1)S(1)}, bf16[2,5,96,384]{3,2,1,0:T(8,128)(2,1)S(1)}, u32[]{:S(2)}, u32[]{:S(2)}) collective-permute-start(bf16[2,5,96,384]{3,2,1,0:T(8,128)(2,1)S(1)} %slice.66), channel_id=1, source_target_pairs={{0,16},{8,24},{16,0},{24,8},{1,17},{9,25},{17,1},{25,9},{2,18},{10... | collective-permute-start | bytes 2211848 | tf_op jit(solution)/shard_map/ppermute | solution.py:27
  148.6 58.1 %collective-permute-start.13 = (bf16[4,5,96,384]{3,2,1,0:T(8,128)(2,1)S(1)}, bf16[4,5,96,384]{3,2,1,0:T(8,128)(2,1)S(1)}, u32[]{:S(2)}, u32[]{:S(2)}) collective-permute-start(bf16[4,5,96,384]{3,2,1,0:T(8,128)(2,1)S(1)} %copy-done.12), channel_id=1, source_target_pairs={{0,1},{1,0},{2,3},{3,2},{4,5},{5,4},{6,7},{7,6},{8,9},{9,8},{10,11... | collective-permute-start | bytes 4423688 | tf_op jit(solution)/shard_map/ppermute | solution.py:27
  151.9 54.9 %collective-permute-start.14 = (bf16[4,5,96,384]{3,2,1,0:T(8,128)(2,1)S(1)}, bf16[4,5,96,384]{3,2,1,0:T(8,128)(2,1)S(1)}, u32[]{:S(2)}, u32[]{:S(2)}) collective-permute-start(bf16[4,5,96,384]{3,2,1,0:T(8,128)(2,1)S(1)} %collective-permute-done.7.refs_7_), channel_id=1, source_target_pairs={{0,1},{1,0},{2,3},{3,2},{4,5},{5,4},{6,7},{7,6},{8,9},{9,8},{10,11... | collective-permute-start | bytes 4423688 | tf_op jit(solution)/shard_map/ppermute | solution.py:27
  151.9 2.2 copy-start.16
  151.9 54.9 %collective-permute-start.15 = (bf16[4,5,96,384]{3,2,1,0:T(8,128)(2,1)S(1)}, bf16[4,5,96,384]{3,2,1,0:T(8,128)(2,1)S(1)}, u32[]{:S(2)}, u32[]{:S(2)}) collective-permute-start(bf16[4,5,96,384]{3,2,1,0:T(8,128)(2,1)S(1)} %collective-permute-done.10.refs_9_), channel_id=1, source_target_pairs={{0,1},{1,0},{2,3},{3,2},{4,5},{5,4},{6,7},{7,6},{8,9},{9,8},{10,11... | collective-permute-start | bytes 4423688 | tf_op jit(solution)/shard_map/ppermute | solution.py:27
  152.5 18.2 %collective-permute-start.11 = (bf16[2,5,96,384]{3,2,1,0:T(8,128)(2,1)S(1)}, bf16[2,5,96,384]{3,2,1,0:T(8,128)(2,1)}, u32[]{:S(2)}, u32[]{:S(2)}) collective-permute-start(bf16[2,5,96,384]{3,2,1,0:T(8,128)(2,1)S(1)} %slice.67), channel_id=1, source_target_pairs={{0,8},{8,0},{16,24},{24,16},{1,9},{9,1},{17,25},{25,17},{2,10},{10... | collective-permute-start | bytes 2211848 | tf_op jit(solution)/shard_map/ppermute | solution.py:27
  164.3 58.6 %copy-start.21 = (bf16[2,5,96,384]{3,2,1,0:T(8,128)(2,1)}, bf16[2,5,96,384]{3,2,1,0:T(8,128)(2,1)S(1)}, u32[]{:S(2)}) copy-start(bf16[2,5,96,384]{3,2,1,0:T(8,128)(2,1)S(1)} %collective-permute-done.8.refs_2_) | copy-start | bytes 2211844
  164.3 25.4 %collective-permute-start.19 = (bf16[5,96,384]{2,1,0:T(8,128)(2,1)S(1)}, bf16[5,96,384]{2,1,0:T(8,128)(2,1)S(1)}, u32[]{:S(2)}, u32[]{:S(2)}) collective-permute-start(bf16[5,96,384]{2,1,0:T(8,128)(2,1)S(1)} %get-tuple-element.13), channel_id=1, source_target_pairs={{0,6},{1,7},{2,4},{3,5},{4,2},{5,3},{6,0},{7,1},{8,14},{9,15},{10,... | collective-permute-start | bytes 1105928 | tf_op jit(solution)/shard_map/ppermute | solution.py:27
  170.7 25.0 %collective-permute-start.18 = (bf16[5,96,384]{2,1,0:T(8,128)(2,1)S(1)}, bf16[5,96,384]{2,1,0:T(8,128)(2,1)S(1)}, u32[]{:S(2)}, u32[]{:S(2)}) collective-permute-start(bf16[5,96,384]{2,1,0:T(8,128)(2,1)S(1)} %get-tuple-element.14), channel_id=1, source_target_pairs={{0,4},{1,5},{2,6},{3,7},{4,0},{5,1},{6,2},{7,3},{8,12},{9,13},{10,... | collective-permute-start | bytes 1105928 | tf_op jit(solution)/shard_map/ppermute | solution.py:27
  189.7 15.1 %collective-permute-start.17 = (bf16[5,96,384]{2,1,0:T(8,128)(2,1)S(1)}, bf16[5,96,384]{2,1,0:T(8,128)(2,1)S(1)}, u32[]{:S(2)}, u32[]{:S(2)}) collective-permute-start(bf16[5,96,384]{2,1,0:T(8,128)(2,1)S(1)} %get-tuple-element.12), channel_id=1, source_target_pairs={{0,2},{1,3},{2,0},{3,1},{4,6},{5,7},{6,4},{7,5},{8,10},{9,11},{10,... | collective-permute-start | bytes 1105928 | tf_op jit(solution)/shard_map/ppermute | solution.py:27
  195.7 27.2 %collective-permute-start.9 = (bf16[2,5,96,384]{3,2,1,0:T(8,128)(2,1)S(1)}, bf16[2,5,96,384]{3,2,1,0:T(8,128)(2,1)}, u32[]{:S(2)}, u32[]{:S(2)}) collective-permute-start(bf16[2,5,96,384]{3,2,1,0:T(8,128)(2,1)S(1)} %collective-permute-done.8.refs_2_), channel_id=1, source_target_pairs={{0,1},{1,0},{2,3},{3,2},{4,5},{5,4},{6,7},{7,6},{8,9},{9,8},{10,11... | collective-permute-start | bytes 2211848 | tf_op jit(solution)/shard_map/ppermute | solution.py:27
  204.9 18.1 %collective-permute-start.12 = (bf16[2,5,96,384]{3,2,1,0:T(8,128)(2,1)}, bf16[2,5,96,384]{3,2,1,0:T(8,128)(2,1)}, u32[]{:S(2)}, u32[]{:S(2)}) collective-permute-start(bf16[2,5,96,384]{3,2,1,0:T(8,128)(2,1)} %collective-permute-done.11.refs_4_), channel_id=1, source_target_pairs={{0,1},{1,0},{2,3},{3,2},{4,5},{5,4},{6,7},{7,6},{8,9},{9,8},{10,11... | collective-permute-start | bytes 2211848 | tf_op jit(solution)/shard_map/ppermute | solution.py:27
  206.7 1.1 copy-start.18
  206.8 1.6 copy-start.19
  206.8 2.1 copy-start.20

commit v9 on v8

--- a/solution.py
+++ b/solution.py
@@ -17,6 +17,7 @@
 STEP = 64
 ROOT = math.sqrt(2.0 / math.pi)
 CUBIC = 0.044715
+SMALL = pl.CostEstimate(flops=1 << 20, bytes_accessed=1 << 16, transcendentals=0)
 ANYWHERE = pl.BlockSpec(memory_space=pl.ANY)
 ROW_OFFSETS = ((1, 1), (0, 1), (0, 0), (-1, 0), (-1, -1))
 GRAD_PARTS = ((0, 0), (1, 0), (1, 1), (2, 1), (2, 2))
@@ -199,9 +200,7 @@
             ],
         ),
         compiler_params=pltpu.CompilerParams(vmem_limit_bytes=48 << 20),
-        cost_estimate=pl.CostEstimate(
-            flops=2 * rows * both * columns, bytes_accessed=16 << 20, transcendentals=0
-        ),
+        cost_estimate=SMALL,
         name="weight_grad_early",
     )(place, shifts, *pieces)
 
@@ -276,9 +275,7 @@
             ],
         ),
         compiler_params=pltpu.CompilerParams(vmem_limit_bytes=48 << 20),
-        cost_estimate=pl.CostEstimate(
-            flops=2 * count * both * columns, bytes_accessed=16 << 20, transcendentals=0
-        ),
+        cost_estimate=SMALL,
         name="weight_grad_late",
     )(place, shifts, early, *pieces)
 
@@ -426,9 +423,7 @@
             scratch_shapes=scratch,
         ),
         compiler_params=pltpu.CompilerParams(vmem_limit_bytes=56 << 20),
-        cost_estimate=pl.CostEstimate(
-            flops=2 * taps * window * width * depth, bytes_accessed=20 << 20, transcendentals=0
-        ),
+        cost_estimate=SMALL,
         name="input_grad_late" if last else "input_grad_early",
     )(place, *operands)
 
@@ -437,26 +432,22 @@
     count = len(line)
 
     def kernel(place, *refs):
-        parts, out_ref, sems = refs[:count], refs[count], refs[count + 1]
-        copies = [
-            pltpu.make_async_copy(parts[j], out_ref.at[place[1] // 2 ^ j], sems.at[j])
-            for j in range(count)
-        ]
-        for copy in copies:
-            copy.start()
-        for copy in copies:
-            copy.wait()
-
+        parts, out_ref = refs[:count], refs[count]
+        for j in range(count):
+            out_ref[place[1] // 2 ^ j] = parts[j][...]
+
+    shape = line[0].shape
     return pl.pallas_call(
         kernel,
-        out_shape=jax.ShapeDtypeStruct((count, *line[0].shape), line[0].dtype),
+        out_shape=jax.ShapeDtypeStruct((count, *shape), line[0].dtype),
         grid_spec=pltpu.PrefetchScalarGridSpec(
             num_scalar_prefetch=1,
             grid=(1,),
-            in_specs=[ANYWHERE] * count,
-            out_specs=ANYWHERE,
-            scratch_shapes=[pltpu.SemaphoreType.DMA((count,))],
+            in_specs=[pl.BlockSpec(shape, lambda i, place: (0, 0, 0))] * count,
+            out_specs=pl.BlockSpec((count, *shape), lambda i, place: (0, 0, 0, 0)),
         ),
+        compiler_params=pltpu.CompilerParams(vmem_limit_bytes=24 << 20),
+        cost_estimate=SMALL,
         name="stack_planes",
     )(place, *line)
 
@@ -474,24 +465,18 @@
     to_beside, to_below, own_window = messages(place, inputs, trunk_grad)
     beside, below = from_peer(to_beside, "seq", 1), from_peer(to_below, "seq", 2)
     slope = half_slope(inputs)
-    line = gather_line(weights, "rep", planes, 2)
-    top = after(beside[: FIRST + half], slope, *line[1:])
-    bottom = after(below[half : coarse + packed - FIRST], slope, *line[1:])
+    column = stack_planes(place, gather_line(weights, "rep", planes, 2))
+    top = after(beside[: FIRST + half], slope, column)
+    bottom = after(below[half : coarse + packed - FIRST], slope, column)
     far_top, far_bottom = from_peer(top, "seq", 2), from_peer(bottom, "seq", 1)
 
-    column = after(stack_planes(place, line), beside, below)
+    column = after(column, beside, below)
     kept_beside, kept_below = from_peer(column, "seq", 1), from_peer(column, "seq", 2)
-    kept = [
-        (column, 0, 0),
-        (kept_beside, 0, 1),
-        (kept_below, 0, 2),
-        (from_peer(kept_beside[: planes // 2], "seq", 2), 0, 3),
-        (from_peer(kept_below[planes // 2 :], "seq", 1), planes // 2, 3),
-    ]
-    pieces = []
-    for part, plane, distance in kept:
-        pieces.append((part, plane, 0, distance))
-        pieces.append((from_peer(part, "rep", 1), plane, 1, distance))
+    far_first = from_peer(kept_beside[: planes // 2], "seq", 2)
+    far_second = from_peer(kept_below[planes // 2 :], "seq", 1)
+    soon, rest = [], []
+    for part, distance in ((column, 0), (kept_beside, 1), (kept_below, 2)):
+        soon += [(part, 0, 0, distance), (from_peer(part, "rep", 1), 0, 1, distance)]
 
     trunk = trunk_grad[0]
     zeros = jnp.zeros((1, block), jnp.bfloat16)
@@ -518,8 +503,10 @@
         [(far_top, 0, 0, FIRST), (far_bottom, half, FIRST, packed - FIRST)],
     ]
     stage = functools.partial(gradient_stage, place, windows, slope=slope, shape=inputs.shape)
-    soon, rest = ([p for p in pieces if (p[3] == 3) == far] for far in (False, True))
     begun = stage(soon, [0, 1, 2], begun=None)
+    for part, plane in ((far_first, 0), (far_second, planes // 2)):
+        part = after(part, begun)
+        rest += [(part, plane, 0, 3), (from_peer(part, "rep", 1), plane, 1, 3)]
     input_grad = stage(rest, [3], begun=begun)
     return (input_grad, weight_grad)
 

time: 235 us -> 201 us (0.86)
  Pallas kernels: 98.2 us -> 53.7 us
  waiting for transfers between devices: 85.7 us -> 95.5 us
  local copies, waits for them, and re-layouts: 14.4 us -> 11.9 us
    pallas_call x1, Pallas kernels: 46.5 us -> 0.68 us  [stack_planes(): pl.pallas_call(kernel, out_shape=jax.ShapeDtypeStruct((count, *shape), li...]
    ppermute x20, waiting for transfers between devices: 85.7 us -> 95.5 us  [from_peer(): return lax.ppermute(value, axis, [(i, i ^ distance) for i in range(peers)])]
    unnamed x46 -> x36, local copies, waits for them, and re-layouts: 8.8 us -> 7.1 us
  transfers between devices with their start and end apart: 20 -> 20, of which waited for: 8 -> 8; matrix products, arithmetic and copies ran while one was open for 5% -> 5% of each run, Pallas kernels for 37% -> 21%
where the time goes in v9:
time: 201 us; the launch traced here: 197 us
  waiting for transfers between devices  95.5 us (48%)
  Pallas kernels  53.7 us (27%)
  starting transfers between devices  28.3 us (14%)
  local copies, waits for them, and re-layouts  11.9 us (6%)
  other arithmetic  7 us (3%)
    ppermute x20, waiting for transfers between devices, from_peer(): return lax.ppermute(value, axis, [(i, i ^ distance) for i in range(peers)])  95.5 us
    ppermute x20, starting transfers between devices, from_peer(): return lax.ppermute(value, axis, [(i, i ^ distance) for i in range(peers)])  28.3 us
    pallas_call x2, Pallas kernels, gradient_stage(): pl.pallas_call(body, out_shape=out_shape, grid_spec=pltpu.PrefetchScalarG...  23 us
    pallas_call x1, Pallas kernels, early_terms(): pl.pallas_call(kernel, out_shape=jax.ShapeDtypeStruct((both, columns), jn...  13.8 us
    pallas_call x1, Pallas kernels, late_terms(): pl.pallas_call(kernel, out_shape=(jax.ShapeDtypeStruct(shape, jnp.float32...  9.82 us
    unnamed x36, local copies, waits for them, and re-layouts  7.1 us
    pallas_call x1, Pallas kernels, messages(): pl.pallas_call(messages_kernel, out_shape=[jax.ShapeDtypeStruct((n, 2 * w...  4.09 us
  transfers between devices with their start and end apart: 20, of which 8 were waited for; matrix products, arithmetic and copies ran while one was open for 5% of the time, Pallas kernels for 21%

profile of v9, /device:TPU:9, one launch (start us, length us, event | category | flops | bytes accessed | tf_op | source)
XLA Modules:
  0.0 197.3 jit_solution(3023805719890555513)
XLA Ops:
  0.6 0.1 pad_add_fusion.place
  0.7 1.4 copy-done.5
  2.1 1.4 copy-done.9
  3.5 4.1 %messages.1 = (bf16[736,1536]{1,0:T(8,128)(2,1)}, bf16[720,1536]{1,0:T(8,128)(2,1)S(1)}, bf16[144,1536]{1,0:T(8,128)(2,1)S(1)}) custom-call(s32[2]{0:T(128)S(1)} %pad_add_fusion.place, bf16[1,1024,768]{2,1,0:T(8,128)(2,1)S(1)} %copy-done.9, bf16[1,2048,384]{2,1,0:T(8,128)(2,1)S(1)} %copy-done.5), custom_call_target="tpu_custom_call" | custom-call | tf_op jit(solution)/shard_map/messages/pallas_call | solution.py:104
  7.6 1.3 collective-permute-start
  8.9 1.2 collective-permute-start.5
  10.2 1.3 collective-permute-start.2
  11.5 2.2 %collective-permute-start.1 = (bf16[5,96,384]{2,1,0:T(8,128)(2,1)S(1)}, bf16[5,96,384]{2,1,0:T(8,128)(2,1)S(1)}, u32[]{:S(2)}, u32[]{:S(2)}) collective-permute-start(bf16[5,96,384]{2,1,0:T(8,128)(2,1)S(1)} %copy-done.11), channel_id=1, source_target_pairs={{0,2},{1,3},{2,0},{3,1},{4,6},{5,7},{6,4},{7,5},{8,10},{9,11},{10,... | collective-permute-start | bytes 1105928 | tf_op jit(solution)/shard_map/ppermute | solution.py:28
  13.6 14.1 %collective-permute-done.2.refs_3_ = bf16[5,96,384]{2,1,0:T(8,128)(2,1)S(1)} collective-permute-done((bf16[5,96,384]{2,1,0:T(8,128)(2,1)S(1)}, bf16[5,96,384]{2,1,0:T(8,128)(2,1)S(1)}, u32[]{:S(2)}, u32[]{:S(2)}) %collective-permute-start.2) | collective-permute-done | bytes 368672 | tf_op jit(solution)/shard_map/ppermute | solution.py:28
  27.8 2.3 %half_slope.1.refs_1_.refs_11_.refs_6_ = f32[2,512,768]{2,1,0:T(8,128)S(1)} custom-call(bf16[1,1024,768]{2,1,0:T(8,128)(2,1)S(1)} %copy-done.9), custom_call_target="tpu_custom_call" | custom-call | tf_op jit(solution)/shard_map/half_slope/pallas_call | solution.py:139
  30.1 1.7 copy-done
  31.8 5.4 %collective-permute-done.3.refs_2_ = bf16[5,96,384]{2,1,0:T(8,128)(2,1)S(1)} collective-permute-done((bf16[5,96,384]{2,1,0:T(8,128)(2,1)S(1)}, bf16[5,96,384]{2,1,0:T(8,128)(2,1)S(1)}, u32[]{:S(2)}, u32[]{:S(2)}) %collective-permute-start.3) | collective-permute-done | bytes 368672 | tf_op jit(solution)/shard_map/ppermute | solution.py:28
  37.2 0.7 stack_planes.1.refs_2_.refs_0_
  37.9 1.1 copy-done.1
  39.0 18.7 %collective-permute-done.5.refs_2_ = bf16[720,1536]{1,0:T(8,128)(2,1)S(1)} collective-permute-done((bf16[720,1536]{1,0:T(8,128)(2,1)S(1)}, bf16[720,1536]{1,0:T(8,128)(2,1)S(1)}, u32[]{:S(2)}, u32[]{:S(2)}) %collective-permute-start.5) | collective-permute-done | bytes 2211872 | tf_op jit(solution)/shard_map/ppermute | solution.py:28
  57.7 1.1 slice.65.refs_0_
  58.7 0.6 copy-done.3
  59.3 2.3 %slice.64.refs_0_ = bf16[336,1536]{1,0:T(8,128)(2,1)} slice(bf16[736,1536]{1,0:T(8,128)(2,1)} %collective-permute-done.refs_1_), slice={[0:336], [0:1536]} | slice | bytes 2064384 | tf_op jit(solution)/shard_map/slice | solution.py:469
  61.6 0.3 collective-permute-start.7
  61.9 1.2 collective-permute-start.11
  63.2 0.5 slice_bitcast_fusion.1
  63.7 1.3 collective-permute-start.6
  65.0 0.2 collective-permute-start.4
  65.2 2.9 %collective-permute-start.9 = (bf16[4,5,96,384]{3,2,1,0:T(8,128)(2,1)S(1)}, bf16[4,5,96,384]{3,2,1,0:T(8,128)(2,1)}, u32[]{:S(2)}, u32[]{:S(2)}) collective-permute-start(bf16[4,5,96,384]{3,2,1,0:T(8,128)(2,1)S(1)} %copy-done.2), channel_id=1, source_target_pairs={{0,1},{1,0},{2,3},{3,2},{4,5},{5,4},{6,7},{7,6},{8,9},{9,8},{10,11... | collective-permute-start | bytes 4423688 | tf_op jit(solution)/shard_map/ppermute | solution.py:28
  68.1 25.8 %collective-permute-done.7.refs_7_ = bf16[4,5,96,384]{3,2,1,0:T(8,128)(2,1)S(1)} collective-permute-done((bf16[4,5,96,384]{3,2,1,0:T(8,128)(2,1)}, bf16[4,5,96,384]{3,2,1,0:T(8,128)(2,1)S(1)}, u32[]{:S(2)}, u32[]{:S(2)}) %collective-permute-start.7) | collective-permute-done | bytes 1474592 | tf_op jit(solution)/shard_map/ppermute | solution.py:28
  93.9 5.0 %collective-permute-start.10 = (bf16[4,5,96,384]{3,2,1,0:T(8,128)(2,1)S(1)}, bf16[4,5,96,384]{3,2,1,0:T(8,128)(2,1)}, u32[]{:S(2)}, u32[]{:S(2)}) collective-permute-start(bf16[4,5,96,384]{3,2,1,0:T(8,128)(2,1)S(1)} %collective-permute-done.7.refs_7_), channel_id=1, source_target_pairs={{0,1},{1,0},{2,3},{3,2},{4,5},{5,4},{6,7},{7,6},{8,9},{9,8},{10,11... | collective-permute-start | bytes 4423688 | tf_op jit(solution)/shard_map/ppermute | solution.py:28
  98.9 0.5 collective-permute-start.12
  99.4 2.9 %fusion.2.shifts_ref = bf16[2048,1152]{1,0:T(8,128)(2,1)} fusion(bf16[2047,384]{1,0:T(8,128)(2,1)S(1)} %get-tuple-element.16, bf16[2047,384]{1,0:T(8,128)(2,1)S(1)} %get-tuple-element.15, bf16[2048,384]{1,0:T(8,128)(2,1)S(1)} %bitcast.19), kind=kLoop, calls=%fused_computation.4 | loop fusion | flops 23592960 | bytes 9435648 | tf_op jit(solution)/shard_map/concatenate | solution.py:485
  102.3 13.8 %weight_grad_early.1.early_ref = f32[1536,1152]{1,0:T(8,128)} custom-call(s32[2]{0:T(128)S(1)} %pad_add_fusion.place, bf16[2048,1152]{1,0:T(8,128)(2,1)} %fusion.2.shifts_ref, bf16[736,1536]{1,0:T(8,128)(2,1)} %get-tuple-element.7.refs_0_, bf16[736,1536]{1,0:T(8,128)(2,1)} %collective-permute-done.refs_1_, bf16[720,1536]{1,0:T(8,128)(2,1)S(1)} %copy-done.4), custom_call_target="tpu_custom_call" | custom-call | flops 1048576 | bytes 65536 | tf_op jit(solution)/shard_map/weight_grad_early/pallas_call | solution.py:187
  116.2 9.8 %weight_grad_late.1 = (f32[4,5,96,384]{3,2,1,0:T(8,128)}, bf16[4,5,96,384]{3,2,1,0:T(8,128)(2,1)S(1)}) custom-call(s32[2]{0:T(128)S(1)} %pad_add_fusion.place, bf16[2048,1152]{1,0:T(8,128)(2,1)} %fusion.2.shifts_ref, f32[1536,1152]{1,0:T(8,128)} %weight_grad_early.1.early_ref, bf16[336,1536]{1,0:T(8,128)(2,1)S(1)} %collective-permute-done.4.refs_3_.refs_0_, ...), custom_call_target="tpu_custom_call" | custom-call | flops 1048576 | bytes 65536 | tf_op jit(solution)/shard_map/weight_grad_late/pallas_call | solution.py:257
  126.0 2.8 %collective-permute-start.16 = (bf16[4,5,96,384]{3,2,1,0:T(8,128)(2,1)S(1)}, bf16[4,5,96,384]{3,2,1,0:T(8,128)(2,1)S(1)}, u32[]{:S(2)}, u32[]{:S(2)}) collective-permute-start(bf16[4,5,96,384]{3,2,1,0:T(8,128)(2,1)S(1)} %get-tuple-element.11), channel_id=1, source_target_pairs={{0,1},{1,0},{2,3},{3,2},{4,5},{5,4},{6,7},{7,6},{8,9},{9,8},{10,11... | collective-permute-start | bytes 4423688 | tf_op jit(solution)/shard_map/ppermute | solution.py:28
  128.9 1.3 collective-permute-start.8
  130.2 0.9 slice.67
  131.2 1.2 collective-permute-start.14
  132.4 14.1 %input_grad_early.1.refs_1_.refs_7_ = f32[2,512,768]{2,1,0:T(8,128)} custom-call(s32[2]{0:T(128)} %copy-done.12, bf16[144,1536]{1,0:T(8,128)(2,1)} %copy-done.10, bf16[736,1536]{1,0:T(8,128)(2,1)} %collective-permute-done.refs_1_, bf16[720,1536]{1,0:T(8,128)(2,1)} %copy-done.3, bf16[336,1536]{1,0:T(8,128)(2,1)} %copy-done.7, bf16[320,1536]{1,0:T(8,128)(2,1)} %copy-done.8, ...), custom_call_target="tpu_custom_call" | custom-call | flops 1048576 | bytes 65536 | tf_op jit(solution)/shard_map/input_grad_early/pallas_call | solution.py:415
  146.5 0.7 collective-permute-done.8.refs_0_
  147.2 0.8 collective-permute-start.13
  148.0 1.3 collective-permute-done.14.refs_0_
  149.3 1.1 collective-permute-start.15
  150.4 1.8 fusion.6
  152.2 1.4 collective-permute-start.19
  153.6 1.1 collective-permute-start.18
  154.7 1.1 collective-permute-start.17
  155.8 22.5 %collective-permute-done.19 = bf16[5,96,384]{2,1,0:T(8,128)(2,1)S(1)} collective-permute-done((bf16[5,96,384]{2,1,0:T(8,128)(2,1)S(1)}, bf16[5,96,384]{2,1,0:T(8,128)(2,1)S(1)}, u32[]{:S(2)}, u32[]{:S(2)}) %collective-permute-start.19) | collective-permute-done | bytes 368672 | tf_op jit(solution)/shard_map/ppermute | solution.py:28
  178.3 7.0 %collective-permute-done.18 = bf16[5,96,384]{2,1,0:T(8,128)(2,1)S(1)} collective-permute-done((bf16[5,96,384]{2,1,0:T(8,128)(2,1)S(1)}, bf16[5,96,384]{2,1,0:T(8,128)(2,1)S(1)}, u32[]{:S(2)}, u32[]{:S(2)}) %collective-permute-start.18) | collective-permute-done | bytes 368672 | tf_op jit(solution)/shard_map/ppermute | solution.py:28
  185.3 2.2 %fusion.5 = f32[5,96,384]{2,1,0:T(8,128)} fusion(bf16[5,96,384]{2,1,0:T(8,128)(2,1)S(1)} %collective-permute-done.19, bf16[5,96,384]{2,1,0:T(8,128)(2,1)S(1)} %collective-permute-done.18, bf16[5,96,384]{2,1,0:T(8,128)(2,1)S(1)} %collective-permute-done.17, f32[4,5,96,384]{3,2,1,0:T(8,128)} %get-tuple-element.10, ...), kind=kLoop, calls=%fused_computation.10 | loop fusion | flops 1474560 | bytes 2949120 | tf_op jit(solution)/shard_map/add | solution.py:497
  187.5 0.9 copy-done.17
  188.4 9.0 %input_grad_late.1 = bf16[1,1024,768]{2,1,0:T(8,128)(2,1)} custom-call(s32[2]{0:T(128)} %copy-done.12, bf16[336,1536]{1,0:T(8,128)(2,1)} %copy-done.7, bf16[320,1536]{1,0:T(8,128)(2,1)} %copy-done.8, bf16[2,5,96,384]{3,2,1,0:T(8,128)(2,1)} %after.8.refs_2_, bf16[2,5,96,384]{3,2,1,0:T(8,128)(2,1)} %collective-permute-done.13.refs_3_, ...), custom_call_target="tpu_custom_call" | custom-call | flops 1048576 | bytes 65536 | tf_op jit(solution)/shard_map/input_grad_late/pallas_call | solution.py:415
  (49 shorter events, 0.2 us)
Async XLA Ops:
  0.7 1.4 copy-start.5
  2.1 1.4 copy-start.9
  3.5 112.6 %copy-start.12 = (s32[2]{0:T(128)}, s32[2]{0:T(128)S(1)}, u32[]{:S(2)}) copy-start(s32[2]{0:T(128)S(1)} %pad_add_fusion.place) | copy-start | bytes 28
  3.5 6.6 %copy-start.11 = (bf16[5,96,384]{2,1,0:T(8,128)(2,1)S(1)}, bf16[5,96,384]{2,1,0:T(8,128)(2,1)}, u32[]{:S(2)}) copy-start(bf16[5,96,384]{2,1,0:T(8,128)(2,1)} %refs_0_.1) | copy-start | bytes 1105924
  7.6 22.5 %copy-start.10 = (bf16[144,1536]{1,0:T(8,128)(2,1)}, bf16[144,1536]{1,0:T(8,128)(2,1)S(1)}, u32[]{:S(2)}) copy-start(bf16[144,1536]{1,0:T(8,128)(2,1)S(1)} %get-tuple-element.9.refs_0_) | copy-start | bytes 1327108
  7.6 51.7 %collective-permute-start = (bf16[736,1536]{1,0:T(8,128)(2,1)}, bf16[736,1536]{1,0:T(8,128)(2,1)}, u32[]{:S(2)}, u32[]{:S(2)}) collective-permute-start(bf16[736,1536]{1,0:T(8,128)(2,1)} %get-tuple-element.7.refs_0_), channel_id=1, source_target_pairs={{0,8},{8,0},{16,24},{24,16},{1,9},{9,1},{17,25},{25,17},{2,10},{10... | collective-permute-start | bytes 6782984 | tf_op jit(solution)/shard_map/ppermute | solution.py:28
  8.9 48.7 %collective-permute-start.5 = (bf16[720,1536]{1,0:T(8,128)(2,1)S(1)}, bf16[720,1536]{1,0:T(8,128)(2,1)S(1)}, u32[]{:S(2)}, u32[]{:S(2)}) collective-permute-start(bf16[720,1536]{1,0:T(8,128)(2,1)S(1)} %get-tuple-element.8), channel_id=1, source_target_pairs={{0,16},{8,24},{16,0},{24,8},{1,17},{9,25},{17,1},{25,9},{2,18},{10... | collective-permute-start | bytes 6635528 | tf_op jit(solution)/shard_map/ppermute | solution.py:28
  10.2 17.6 %collective-permute-start.2 = (bf16[5,96,384]{2,1,0:T(8,128)(2,1)S(1)}, bf16[5,96,384]{2,1,0:T(8,128)(2,1)S(1)}, u32[]{:S(2)}, u32[]{:S(2)}) collective-permute-start(bf16[5,96,384]{2,1,0:T(8,128)(2,1)S(1)} %copy-done.11), channel_id=1, source_target_pairs={{0,6},{1,7},{2,4},{3,5},{4,2},{5,3},{6,0},{7,1},{8,14},{9,15},{10,... | collective-permute-start | bytes 1105928 | tf_op jit(solution)/shard_map/ppermute | solution.py:28
  11.5 20.3 %collective-permute-start.1 = (bf16[5,96,384]{2,1,0:T(8,128)(2,1)S(1)}, bf16[5,96,384]{2,1,0:T(8,128)(2,1)S(1)}, u32[]{:S(2)}, u32[]{:S(2)}) collective-permute-start(bf16[5,96,384]{2,1,0:T(8,128)(2,1)S(1)} %copy-done.11), channel_id=1, source_target_pairs={{0,2},{1,3},{2,0},{3,1},{4,6},{5,7},{6,4},{7,5},{8,10},{9,11},{10,... | collective-permute-start | bytes 1105928 | tf_op jit(solution)/shard_map/ppermute | solution.py:28
  27.8 9.4 %collective-permute-start.3 = (bf16[5,96,384]{2,1,0:T(8,128)(2,1)S(1)}, bf16[5,96,384]{2,1,0:T(8,128)(2,1)S(1)}, u32[]{:S(2)}, u32[]{:S(2)}) collective-permute-start(bf16[5,96,384]{2,1,0:T(8,128)(2,1)S(1)} %collective-permute-done.2.refs_3_), channel_id=1, source_target_pairs={{0,2},{1,3},{2,0},{3,1},{4,6},{5,7},{6,4},{7,5},{8,10},{9,11},{10,... | collective-permute-start | bytes 1105928 | tf_op jit(solution)/shard_map/ppermute | solution.py:28
  30.1 1.7 copy-start
  37.9 1.1 copy-start.1
  57.7 1.7 copy-start.3
  61.6 1.6 copy-start.6
  61.6 2.1 %copy-start.14 = (bf16[320,1536]{1,0:T(8,128)(2,1)S(1)}, bf16[320,1536]{1,0:T(8,128)(2,1)}, u32[]{:S(2)}) copy-start(bf16[320,1536]{1,0:T(8,128)(2,1)} %after.6) | copy-start | bytes 2949124
  61.6 3.4 %copy-start.13 = (bf16[336,1536]{1,0:T(8,128)(2,1)S(1)}, bf16[336,1536]{1,0:T(8,128)(2,1)}, u32[]{:S(2)}) copy-start(bf16[336,1536]{1,0:T(8,128)(2,1)} %after.5) | copy-start | bytes 3096580
  61.6 3.6 %copy-start.2 = (bf16[4,5,96,384]{3,2,1,0:T(8,128)(2,1)S(1)}, bf16[4,5,96,384]{3,2,1,0:T(8,128)(2,1)}, u32[]{:S(2)}) copy-start(bf16[4,5,96,384]{3,2,1,0:T(8,128)(2,1)} %after.7.refs_5_) | copy-start | bytes 4423684
  61.6 32.3 %collective-permute-start.7 = (bf16[4,5,96,384]{3,2,1,0:T(8,128)(2,1)}, bf16[4,5,96,384]{3,2,1,0:T(8,128)(2,1)S(1)}, u32[]{:S(2)}, u32[]{:S(2)}) collective-permute-start(bf16[4,5,96,384]{3,2,1,0:T(8,128)(2,1)} %after.7.refs_5_), channel_id=1, source_target_pairs={{0,8},{8,0},{16,24},{24,16},{1,9},{9,1},{17,25},{25,17},{2,10},{10... | collective-permute-start | bytes 4423688 | tf_op jit(solution)/shard_map/ppermute | solution.py:28
  61.9 36.9 %collective-permute-start.11 = (bf16[4,5,96,384]{3,2,1,0:T(8,128)(2,1)}, bf16[4,5,96,384]{3,2,1,0:T(8,128)(2,1)S(1)}, u32[]{:S(2)}, u32[]{:S(2)}) collective-permute-start(bf16[4,5,96,384]{3,2,1,0:T(8,128)(2,1)} %after.7.refs_5_), channel_id=1, source_target_pairs={{0,16},{8,24},{16,0},{24,8},{1,17},{9,25},{17,1},{25,9},{2,18},{10... | collective-permute-start | bytes 4423688 | tf_op jit(solution)/shard_map/ppermute | solution.py:28
  63.7 52.4 %collective-permute-start.6 = (bf16[320,1536]{1,0:T(8,128)(2,1)S(1)}, bf16[320,1536]{1,0:T(8,128)(2,1)S(1)}, u32[]{:S(2)}, u32[]{:S(2)}) collective-permute-start(bf16[320,1536]{1,0:T(8,128)(2,1)S(1)} %copy-done.14), channel_id=1, source_target_pairs={{0,8},{8,0},{16,24},{24,16},{1,9},{9,1},{17,25},{25,17},{2,10},{10... | collective-permute-start | bytes 2949128 | tf_op jit(solution)/shard_map/ppermute | solution.py:28
  65.0 51.2 %collective-permute-start.4 = (bf16[336,1536]{1,0:T(8,128)(2,1)S(1)}, bf16[336,1536]{1,0:T(8,128)(2,1)S(1)}, u32[]{:S(2)}, u32[]{:S(2)}) collective-permute-start(bf16[336,1536]{1,0:T(8,128)(2,1)S(1)} %copy-done.13), channel_id=1, source_target_pairs={{0,16},{8,24},{16,0},{24,8},{1,17},{9,25},{17,1},{25,9},{2,18},{10... | collective-permute-start | bytes 3096584 | tf_op jit(solution)/shard_map/ppermute | solution.py:28
  65.2 66.0 %collective-permute-start.9 = (bf16[4,5,96,384]{3,2,1,0:T(8,128)(2,1)S(1)}, bf16[4,5,96,384]{3,2,1,0:T(8,128)(2,1)}, u32[]{:S(2)}, u32[]{:S(2)}) collective-permute-start(bf16[4,5,96,384]{3,2,1,0:T(8,128)(2,1)S(1)} %copy-done.2), channel_id=1, source_target_pairs={{0,1},{1,0},{2,3},{3,2},{4,5},{5,4},{6,7},{7,6},{8,9},{9,8},{10,11... | collective-permute-start | bytes 4423688 | tf_op jit(solution)/shard_map/ppermute | solution.py:28
  93.9 34.9 %copy-start.15 = (bf16[4,5,96,384]{3,2,1,0:T(8,128)(2,1)}, bf16[4,5,96,384]{3,2,1,0:T(8,128)(2,1)S(1)}, u32[]{:S(2)}) copy-start(bf16[4,5,96,384]{3,2,1,0:T(8,128)(2,1)S(1)} %collective-permute-done.7.refs_7_) | copy-start | bytes 4423684
  93.9 38.5 %collective-permute-start.10 = (bf16[4,5,96,384]{3,2,1,0:T(8,128)(2,1)S(1)}, bf16[4,5,96,384]{3,2,1,0:T(8,128)(2,1)}, u32[]{:S(2)}, u32[]{:S(2)}) collective-permute-start(bf16[4,5,96,384]{3,2,1,0:T(8,128)(2,1)S(1)} %collective-permute-done.7.refs_7_), channel_id=1, source_target_pairs={{0,1},{1,0},{2,3},{3,2},{4,5},{5,4},{6,7},{7,6},{8,9},{9,8},{10,11... | collective-permute-start | bytes 4423688 | tf_op jit(solution)/shard_map/ppermute | solution.py:28
  98.9 31.4 %copy-start.16 = (bf16[4,5,96,384]{3,2,1,0:T(8,128)(2,1)}, bf16[4,5,96,384]{3,2,1,0:T(8,128)(2,1)S(1)}, u32[]{:S(2)}) copy-start(bf16[4,5,96,384]{3,2,1,0:T(8,128)(2,1)S(1)} %collective-permute-done.11.refs_9_) | copy-start | bytes 4423684
  98.9 33.5 %collective-permute-start.12 = (bf16[4,5,96,384]{3,2,1,0:T(8,128)(2,1)S(1)}, bf16[4,5,96,384]{3,2,1,0:T(8,128)(2,1)}, u32[]{:S(2)}, u32[]{:S(2)}) collective-permute-start(bf16[4,5,96,384]{3,2,1,0:T(8,128)(2,1)S(1)} %collective-permute-done.11.refs_9_), channel_id=1, source_target_pairs={{0,1},{1,0},{2,3},{3,2},{4,5},{5,4},{6,7},{7,6},{8,9},{9,8},{10,11... | collective-permute-start | bytes 4423688 | tf_op jit(solution)/shard_map/ppermute | solution.py:28
  99.4 2.9 %copy-start.4 = (bf16[720,1536]{1,0:T(8,128)(2,1)S(1)}, bf16[720,1536]{1,0:T(8,128)(2,1)}, u32[]{:S(2)}) copy-start(bf16[720,1536]{1,0:T(8,128)(2,1)} %copy-done.3) | copy-start | bytes 6635524
  116.1 9.9 %copy-start.8 = (bf16[320,1536]{1,0:T(8,128)(2,1)}, bf16[320,1536]{1,0:T(8,128)(2,1)S(1)}, u32[]{:S(2)}) copy-start(bf16[320,1536]{1,0:T(8,128)(2,1)S(1)} %collective-permute-done.6.refs_4_.refs_1_) | copy-start | bytes 2949124
  116.1 9.8 %copy-start.7 = (bf16[336,1536]{1,0:T(8,128)(2,1)}, bf16[336,1536]{1,0:T(8,128)(2,1)S(1)}, u32[]{:S(2)}) copy-start(bf16[336,1536]{1,0:T(8,128)(2,1)S(1)} %collective-permute-done.4.refs_3_.refs_0_) | copy-start | bytes 3096580
  126.0 24.4 %collective-permute-start.16 = (bf16[4,5,96,384]{3,2,1,0:T(8,128)(2,1)S(1)}, bf16[4,5,96,384]{3,2,1,0:T(8,128)(2,1)S(1)}, u32[]{:S(2)}, u32[]{:S(2)}) collective-permute-start(bf16[4,5,96,384]{3,2,1,0:T(8,128)(2,1)S(1)} %get-tuple-element.11), channel_id=1, source_target_pairs={{0,1},{1,0},{2,3},{3,2},{4,5},{5,4},{6,7},{7,6},{8,9},{9,8},{10,11... | collective-permute-start | bytes 4423688 | tf_op jit(solution)/shard_map/ppermute | solution.py:28
  128.9 18.3 %collective-permute-start.8 = (bf16[2,5,96,384]{3,2,1,0:T(8,128)(2,1)S(1)}, bf16[2,5,96,384]{3,2,1,0:T(8,128)(2,1)}, u32[]{:S(2)}, u32[]{:S(2)}) collective-permute-start(bf16[2,5,96,384]{3,2,1,0:T(8,128)(2,1)S(1)} %slice.66), channel_id=1, source_target_pairs={{0,16},{8,24},{16,0},{24,8},{1,17},{9,25},{17,1},{25,9},{2,18},{10... | collective-permute-start | bytes 2211848 | tf_op jit(solution)/shard_map/ppermute | solution.py:28
  131.2 18.1 %collective-permute-start.14 = (bf16[2,5,96,384]{3,2,1,0:T(8,128)(2,1)}, bf16[2,5,96,384]{3,2,1,0:T(8,128)(2,1)}, u32[]{:S(2)}, u32[]{:S(2)}) collective-permute-start(bf16[2,5,96,384]{3,2,1,0:T(8,128)(2,1)} %slice.67), channel_id=1, source_target_pairs={{0,8},{8,0},{16,24},{24,16},{1,9},{9,1},{17,25},{25,17},{2,10},{10... | collective-permute-start | bytes 2211848 | tf_op jit(solution)/shard_map/ppermute | solution.py:28
  147.2 40.3 %collective-permute-start.13 = (bf16[2,5,96,384]{3,2,1,0:T(8,128)(2,1)}, bf16[2,5,96,384]{3,2,1,0:T(8,128)(2,1)}, u32[]{:S(2)}, u32[]{:S(2)}) collective-permute-start(bf16[2,5,96,384]{3,2,1,0:T(8,128)(2,1)} %after.8.refs_2_), channel_id=1, source_target_pairs={{0,1},{1,0},{2,3},{3,2},{4,5},{5,4},{6,7},{7,6},{8,9},{9,8},{10,11... | collective-permute-start | bytes 2211848 | tf_op jit(solution)/shard_map/ppermute | solution.py:28
  149.3 38.2 %collective-permute-start.15 = (bf16[2,5,96,384]{3,2,1,0:T(8,128)(2,1)}, bf16[2,5,96,384]{3,2,1,0:T(8,128)(2,1)S(1)}, u32[]{:S(2)}, u32[]{:S(2)}) collective-permute-start(bf16[2,5,96,384]{3,2,1,0:T(8,128)(2,1)} %after.9.refs_4_), channel_id=1, source_target_pairs={{0,1},{1,0},{2,3},{3,2},{4,5},{5,4},{6,7},{7,6},{8,9},{9,8},{10,11... | collective-permute-start | bytes 2211848 | tf_op jit(solution)/shard_map/ppermute | solution.py:28
  152.2 26.1 %collective-permute-start.19 = (bf16[5,96,384]{2,1,0:T(8,128)(2,1)S(1)}, bf16[5,96,384]{2,1,0:T(8,128)(2,1)S(1)}, u32[]{:S(2)}, u32[]{:S(2)}) collective-permute-start(bf16[5,96,384]{2,1,0:T(8,128)(2,1)S(1)} %get-tuple-element.13), channel_id=1, source_target_pairs={{0,6},{1,7},{2,4},{3,5},{4,2},{5,3},{6,0},{7,1},{8,14},{9,15},{10,... | collective-permute-start | bytes 1105928 | tf_op jit(solution)/shard_map/ppermute | solution.py:28
  153.6 31.7 %collective-permute-start.18 = (bf16[5,96,384]{2,1,0:T(8,128)(2,1)S(1)}, bf16[5,96,384]{2,1,0:T(8,128)(2,1)S(1)}, u32[]{:S(2)}, u32[]{:S(2)}) collective-permute-start(bf16[5,96,384]{2,1,0:T(8,128)(2,1)S(1)} %get-tuple-element.14), channel_id=1, source_target_pairs={{0,4},{1,5},{2,6},{3,7},{4,0},{5,1},{6,2},{7,3},{8,12},{9,13},{10,... | collective-permute-start | bytes 1105928 | tf_op jit(solution)/shard_map/ppermute | solution.py:28
  154.7 30.6 %collective-permute-start.17 = (bf16[5,96,384]{2,1,0:T(8,128)(2,1)S(1)}, bf16[5,96,384]{2,1,0:T(8,128)(2,1)S(1)}, u32[]{:S(2)}, u32[]{:S(2)}) collective-permute-start(bf16[5,96,384]{2,1,0:T(8,128)(2,1)S(1)} %get-tuple-element.12), channel_id=1, source_target_pairs={{0,2},{1,3},{2,0},{3,1},{4,6},{5,7},{6,4},{7,5},{8,10},{9,11},{10,... | collective-permute-start | bytes 1105928 | tf_op jit(solution)/shard_map/ppermute | solution.py:28
  187.5 0.9 copy-start.17

commit v10 on v9

--- a/solution.py
+++ b/solution.py
@@ -466,23 +466,20 @@
     beside, below = from_peer(to_beside, "seq", 1), from_peer(to_below, "seq", 2)
     slope = half_slope(inputs)
     column = stack_planes(place, gather_line(weights, "rep", planes, 2))
-    top = after(beside[: FIRST + half], slope, column)
-    bottom = after(below[half : coarse + packed - FIRST], slope, column)
-    far_top, far_bottom = from_peer(top, "seq", 2), from_peer(bottom, "seq", 1)
-
-    column = after(column, beside, below)
-    kept_beside, kept_below = from_peer(column, "seq", 1), from_peer(column, "seq", 2)
-    far_first = from_peer(kept_beside[: planes // 2], "seq", 2)
-    far_second = from_peer(kept_below[planes // 2 :], "seq", 1)
-    soon, rest = [], []
-    for part, distance in ((column, 0), (kept_beside, 1), (kept_below, 2)):
-        soon += [(part, 0, 0, distance), (from_peer(part, "rep", 1), 0, 1, distance)]
-
     trunk = trunk_grad[0]
     zeros = jnp.zeros((1, block), jnp.bfloat16)
     later = jnp.concatenate([trunk[1:], zeros])
     earlier = jnp.concatenate([zeros, trunk[:-1]])
     shifts = jnp.concatenate([later, trunk, earlier], axis=1)
+    top = after(beside[: FIRST + half], slope, column, shifts)
+    bottom = after(below[half : coarse + packed - FIRST], slope, column, shifts)
+    far_top, far_bottom = from_peer(top, "seq", 2), from_peer(bottom, "seq", 1)
+
+    column = after(column, top, bottom)
+    other_column = from_peer(column, "rep", 1)
+    column = after(column, other_column)
+    kept_beside, kept_below = from_peer(column, "seq", 1), from_peer(column, "seq", 2)
+
     scale = 0.5 * float(fine * seqs * reps) ** (-0.5)
     near_rows = [(0, 0, coarse, FIRST), (1, 0, coarse, FIRST), (2, 0, coarse, 0)]
     far_rows = [(3, 0, half, FIRST), (3, half, half, 0)]
@@ -492,9 +489,15 @@
     )
     arrived = from_peer(theirs, "rep", 1)
     weight_grad = mine[0] + arrived[0].astype(jnp.float32)
-    for j in range(1, planes):
-        leaving = (mine[j] + arrived[j].astype(jnp.float32)).astype(jnp.bfloat16)
-        weight_grad = weight_grad + from_peer(leaving, "rep", 2 * j).astype(jnp.float32)
+    leaving = [(mine[j] + arrived[j].astype(jnp.float32)).astype(jnp.bfloat16) for j in range(planes)]
+    summed = [from_peer(leaving[j], "rep", 2 * j) for j in range(1, planes)]
+
+    kept_beside, kept_below = after(kept_beside, early), after(kept_below, early)
+    far_first = from_peer(kept_beside[: planes // 2], "seq", 2)
+    far_second = from_peer(kept_below[planes // 2 :], "seq", 1)
+    soon = [(after(column, *leaving[1:]), 0, 0, 0), (other_column, 0, 1, 0)]
+    for part, distance in ((kept_beside, 1), (kept_below, 2)):
+        soon += [(part, 0, 0, distance), (from_peer(part, "rep", 1), 0, 1, distance)]
 
     windows = [
         [(own_window, 0, 0, packed)],
@@ -503,11 +506,13 @@
         [(far_top, 0, 0, FIRST), (far_bottom, half, FIRST, packed - FIRST)],
     ]
     stage = functools.partial(gradient_stage, place, windows, slope=slope, shape=inputs.shape)
-    begun = stage(soon, [0, 1, 2], begun=None)
+    begun, rest = stage(soon, [0, 1, 2], begun=None), []
     for part, plane in ((far_first, 0), (far_second, planes // 2)):
         part = after(part, begun)
         rest += [(part, plane, 0, 3), (from_peer(part, "rep", 1), plane, 1, 3)]
     input_grad = stage(rest, [3], begun=begun)
+    for part in summed:
+        weight_grad = weight_grad + after(part, input_grad).astype(jnp.float32)
     return (input_grad, weight_grad)
 
 

time: 201 us -> 200 us (level)
  the two profiles are of different devices: /device:TPU:9 before, /device:TPU:0 now
where the time goes in v10:
time: 200 us
  waiting for transfers between devices  97 us (48%)
  Pallas kernels  53.7 us (27%)
  starting transfers between devices  21.7 us (11%)
  local copies, waits for them, and re-layouts  19 us (10%)
  other arithmetic  7.74 us (4%)
    ppermute x20, waiting for transfers between devices, from_peer(): return lax.ppermute(value, axis, [(i, i ^ distance) for i in range(peers)])  97 us
    pallas_call x2, Pallas kernels, gradient_stage(): pl.pallas_call(body, out_shape=out_shape, grid_spec=pltpu.PrefetchScalarG...  23 us
    ppermute x20, starting transfers between devices, from_peer(): return lax.ppermute(value, axis, [(i, i ^ distance) for i in range(peers)])  21.7 us
    pallas_call x1, Pallas kernels, early_terms(): pl.pallas_call(kernel, out_shape=jax.ShapeDtypeStruct((both, columns), jn...  13.8 us
    unnamed x46, local copies, waits for them, and re-layouts  10.8 us
    pallas_call x1, Pallas kernels, late_terms(): pl.pallas_call(kernel, out_shape=(jax.ShapeDtypeStruct(shape, jnp.float32...  9.8 us
    pallas_call x1, Pallas kernels, messages(): pl.pallas_call(messages_kernel, out_shape=[jax.ShapeDtypeStruct((n, 2 * w...  4.1 us
  transfers between devices with their start and end apart: 20, of which 7 were waited for; matrix products, arithmetic and copies ran while one was open for 6% of the time, Pallas kernels for 25%

profile of v10, /device:TPU:0, one launch (start us, length us, event | category | flops | bytes accessed | tf_op | source)
XLA Modules:
  0.0 200.1 jit_solution(13255584657974740713)
XLA Ops:
  0.7 1.4 copy-done.2
  2.1 1.4 copy-done.6
  3.5 4.1 %messages.1 = (bf16[736,1536]{1,0:T(8,128)(2,1)}, bf16[720,1536]{1,0:T(8,128)(2,1)S(1)}, bf16[144,1536]{1,0:T(8,128)(2,1)S(1)}) custom-call(s32[2]{0:T(128)S(1)} %pad_add_fusion.place, bf16[1,1024,768]{2,1,0:T(8,128)(2,1)S(1)} %copy-done.6, bf16[1,2048,384]{2,1,0:T(8,128)(2,1)S(1)} %copy-done.2), custom_call_target="tpu_custom_call" | custom-call | tf_op jit(solution)/shard_map/messages/pallas_call | solution.py:104
  7.6 3.0 %collective-permute-start = (bf16[736,1536]{1,0:T(8,128)(2,1)}, bf16[736,1536]{1,0:T(8,128)(2,1)}, u32[]{:S(2)}, u32[]{:S(2)}) collective-permute-start(bf16[736,1536]{1,0:T(8,128)(2,1)} %get-tuple-element.7.refs_0_), channel_id=1, source_target_pairs={{0,8},{8,0},{16,24},{24,16},{1,9},{9,1},{17,25},{25,17},{2,10},{10... | collective-permute-start | bytes 6782984 | tf_op jit(solution)/shard_map/ppermute | solution.py:28
  10.6 1.5 collective-permute-start.5
  12.2 1.6 collective-permute-start.1
  13.7 2.5 %collective-permute-start.2 = (bf16[5,96,384]{2,1,0:T(8,128)(2,1)S(1)}, bf16[5,96,384]{2,1,0:T(8,128)(2,1)S(1)}, u32[]{:S(2)}, u32[]{:S(2)}) collective-permute-start(bf16[5,96,384]{2,1,0:T(8,128)(2,1)S(1)} %copy-done.8), channel_id=1, source_target_pairs={{0,6},{1,7},{2,4},{3,5},{4,2},{5,3},{6,0},{7,1},{8,14},{9,15},{10,... | collective-permute-start | bytes 1105928 | tf_op jit(solution)/shard_map/ppermute | solution.py:28
  16.2 0.5 slice_bitcast_fusion.1
  16.8 15.2 %collective-permute-done.2.refs_3_ = bf16[5,96,384]{2,1,0:T(8,128)(2,1)S(1)} collective-permute-done((bf16[5,96,384]{2,1,0:T(8,128)(2,1)S(1)}, bf16[5,96,384]{2,1,0:T(8,128)(2,1)S(1)}, u32[]{:S(2)}, u32[]{:S(2)}) %collective-permute-start.2) | collective-permute-done | bytes 368672 | tf_op jit(solution)/shard_map/ppermute | solution.py:28
  32.0 0.6 collective-permute-start.3
  32.5 2.9 %fusion.2.refs_3_.shifts_ref = bf16[2048,1152]{1,0:T(8,128)(2,1)} fusion(bf16[2047,384]{1,0:T(8,128)(2,1)S(1)} %get-tuple-element.16, bf16[2047,384]{1,0:T(8,128)(2,1)S(1)} %get-tuple-element.15, bf16[2048,384]{1,0:T(8,128)(2,1)S(1)} %bitcast.19), kind=kLoop, calls=%fused_computation.4 | loop fusion | flops 23592960 | bytes 9435648 | tf_op jit(solution)/shard_map/concatenate | solution.py:473
  35.5 2.4 %half_slope.1.refs_1_.refs_11_.refs_6_ = f32[2,512,768]{2,1,0:T(8,128)S(1)} custom-call(bf16[1,1024,768]{2,1,0:T(8,128)(2,1)S(1)} %copy-done.6), custom_call_target="tpu_custom_call" | custom-call | tf_op jit(solution)/shard_map/half_slope/pallas_call | solution.py:139
  37.9 1.7 copy-done
  39.5 1.2 collective-permute-done.3.refs_2_
  40.8 0.7 stack_planes.1.refs_2_.refs_0_
  41.5 1.1 copy-done.1
  42.6 17.6 %collective-permute-done.5.refs_2_ = bf16[720,1536]{1,0:T(8,128)(2,1)S(1)} collective-permute-done((bf16[720,1536]{1,0:T(8,128)(2,1)S(1)}, bf16[720,1536]{1,0:T(8,128)(2,1)S(1)}, u32[]{:S(2)}, u32[]{:S(2)}) %collective-permute-start.5) | collective-permute-done | bytes 2211872 | tf_op jit(solution)/shard_map/ppermute | solution.py:28
  60.2 1.1 slice.65.refs_0_
  61.3 2.3 %slice.64.refs_0_ = bf16[336,1536]{1,0:T(8,128)(2,1)} slice(bf16[736,1536]{1,0:T(8,128)(2,1)} %collective-permute-done.refs_1_), slice={[0:336], [0:1536]} | slice | bytes 2064384 | tf_op jit(solution)/shard_map/slice | solution.py:474
  63.6 3.6 %collective-permute-done.7.refs_1_.refs_6_ = bf16[4,5,96,384]{3,2,1,0:T(8,128)(2,1)} collective-permute-done((bf16[4,5,96,384]{3,2,1,0:T(8,128)(2,1)}, bf16[4,5,96,384]{3,2,1,0:T(8,128)(2,1)}, u32[]{:S(2)}, u32[]{:S(2)}) %collective-permute-start.7) | collective-permute-done | bytes 1474592 | tf_op jit(solution)/shard_map/ppermute | solution.py:28
  67.2 0.6 collective-permute-start.8
  67.7 1.5 collective-permute-start.12
  69.3 0.5 collective-permute-start.4
  69.8 1.5 collective-permute-start.6
  71.2 13.8 %weight_grad_early.1.refs_1_.early_ref = f32[1536,1152]{1,0:T(8,128)} custom-call(s32[2]{0:T(128)S(1)} %pad_add_fusion.place, bf16[2048,1152]{1,0:T(8,128)(2,1)} %fusion.2.refs_3_.shifts_ref, bf16[736,1536]{1,0:T(8,128)(2,1)} %get-tuple-element.7.refs_0_, bf16[736,1536]{1,0:T(8,128)(2,1)} %collective-permute-done.refs_1_, ...), custom_call_target="tpu_custom_call" | custom-call | flops 1048576 | bytes 65536 | tf_op jit(solution)/shard_map/weight_grad_early/pallas_call | solution.py:187
  85.0 37.8 %collective-permute-done.6.refs_1_.refs_4_ = bf16[320,1536]{1,0:T(8,128)(2,1)S(1)} collective-permute-done((bf16[320,1536]{1,0:T(8,128)(2,1)}, bf16[320,1536]{1,0:T(8,128)(2,1)S(1)}, u32[]{:S(2)}, u32[]{:S(2)}) %collective-permute-start.6) | collective-permute-done | bytes 983072 | tf_op jit(solution)/shard_map/ppermute | solution.py:28
  122.8 1.3 collective-permute-done.4.refs_0_.refs_3_
  124.1 9.8 %weight_grad_late.1 = (f32[4,5,96,384]{3,2,1,0:T(8,128)}, bf16[4,5,96,384]{3,2,1,0:T(8,128)(2,1)S(1)}) custom-call(s32[2]{0:T(128)S(1)} %pad_add_fusion.place, bf16[2048,1152]{1,0:T(8,128)(2,1)} %fusion.2.refs_3_.shifts_ref, f32[1536,1152]{1,0:T(8,128)} %weight_grad_early.1.refs_1_.early_ref, bf16[336,1536]{1,0:T(8,128)(2,1)S(1)} %collective-permute-done.4.refs_0_.refs_3_, ...), custom_call_target="tpu_custom_call" | custom-call | flops 1048576 | bytes 65536 | tf_op jit(solution)/shard_map/weight_grad_late/pallas_call | solution.py:257
  134.1 0.5 collective-permute-start.11
  134.6 2.2 %slice.66 = bf16[2,5,96,384]{3,2,1,0:T(8,128)(2,1)} slice(bf16[4,5,96,384]{3,2,1,0:T(8,128)(2,1)} %after.16.refs_7_), slice={[0:2], [0:5], [0:96], [0:384]} | slice | bytes 1474560 | tf_op jit(solution)/shard_map/slice | solution.py:496
  136.8 1.5 collective-permute-start.9
  138.4 2.0 %slice.70 = bf16[2,5,96,384]{3,2,1,0:T(8,128)(2,1)} slice(bf16[4,5,96,384]{3,2,1,0:T(8,128)(2,1)} %after.18.refs_9_), slice={[2:4], [0:5], [0:96], [0:384]} | slice | bytes 1474560 | tf_op jit(solution)/shard_map/slice | solution.py:497
  140.4 1.5 collective-permute-start.15
  141.9 2.3 %fusion.8 = (bf16[5,96,384]{2,1,0:T(8,128)(2,1)}, bf16[5,96,384]{2,1,0:T(8,128)(2,1)}, bf16[5,96,384]{2,1,0:T(8,128)(2,1)}) fusion(f32[4,5,96,384]{3,2,1,0:T(8,128)S(1)} %copy-done.13, bf16[4,5,96,384]{3,2,1,0:T(8,128)(2,1)} %collective-permute-done.10), kind=kLoop, calls=%fused_computation.16 | loop fusion | flops 1658880 | bytes 4423680 | tf_op jit(solution)/shard_map/convert_element_type | solution.py:492
  144.2 14.1 %input_grad_early.1.refs_1_.refs_7_ = f32[2,512,768]{2,1,0:T(8,128)} custom-call(s32[2]{0:T(128)} %copy-done.9, bf16[144,1536]{1,0:T(8,128)(2,1)} %copy-done.7, bf16[736,1536]{1,0:T(8,128)(2,1)} %collective-permute-done.refs_1_, bf16[720,1536]{1,0:T(8,128)(2,1)} %copy-done.3, bf16[336,1536]{1,0:T(8,128)(2,1)} %copy-done.4, bf16[320,1536]{1,0:T(8,128)(2,1)} %copy-done.5, ...), custom_call_target="tpu_custom_call" | custom-call | flops 1048576 | bytes 65536 | tf_op jit(solution)/shard_map/input_grad_early/pallas_call | solution.py:415
  158.3 0.9 copy-done.12
  159.2 0.9 copy-done.11
  160.1 0.5 collective-permute-start.16
  160.6 3.6 %collective-permute-start.19 = (bf16[5,96,384]{2,1,0:T(8,128)(2,1)S(1)}, bf16[5,96,384]{2,1,0:T(8,128)(2,1)S(1)}, u32[]{:S(2)}, u32[]{:S(2)}) collective-permute-start(bf16[5,96,384]{2,1,0:T(8,128)(2,1)S(1)} %copy-done.21), channel_id=1, source_target_pairs={{0,6},{1,7},{2,4},{3,5},{4,2},{5,3},{6,0},{7,1},{8,14},{9,15},{10,... | collective-permute-start | bytes 1105928 | tf_op jit(solution)/shard_map/ppermute | solution.py:28
  164.2 0.8 collective-permute-start.17
  165.0 0.9 copy-done.22
  165.9 9.0 %input_grad_late.1.refs_1_ = bf16[1,1024,768]{2,1,0:T(8,128)(2,1)} custom-call(s32[2]{0:T(128)} %copy-done.9, bf16[336,1536]{1,0:T(8,128)(2,1)} %copy-done.4, bf16[320,1536]{1,0:T(8,128)(2,1)} %copy-done.5, bf16[2,5,96,384]{3,2,1,0:T(8,128)(2,1)} %after.19.refs_2_, bf16[2,5,96,384]{3,2,1,0:T(8,128)(2,1)} %collective-permute-done.14.refs_3_, ...), custom_call_target="tpu_custom_call" | custom-call | flops 1048576 | bytes 65536 | tf_op jit(solution)/shard_map/input_grad_late/pallas_call | solution.py:415
  174.9 0.7 copy-done.17
  175.6 20.2 %collective-permute-done.18.refs_0_ = bf16[5,96,384]{2,1,0:T(8,128)(2,1)S(1)} collective-permute-done((bf16[5,96,384]{2,1,0:T(8,128)(2,1)S(1)}, bf16[5,96,384]{2,1,0:T(8,128)(2,1)S(1)}, u32[]{:S(2)}, u32[]{:S(2)}) %collective-permute-start.18) | collective-permute-done | bytes 368672 | tf_op jit(solution)/shard_map/ppermute | solution.py:28
  195.8 0.8 copy-done.15
  196.6 0.7 copy-done.14
  197.3 0.4 copy-done.16
  197.7 2.4 %fusion.5 = f32[5,96,384]{2,1,0:T(8,128)} fusion(bf16[5,96,384]{2,1,0:T(8,128)(2,1)S(1)} %copy-done.18, bf16[5,96,384]{2,1,0:T(8,128)(2,1)S(1)} %copy-done.16, bf16[5,96,384]{2,1,0:T(8,128)(2,1)} %after.21, f32[4,5,96,384]{3,2,1,0:T(8,128)} %get-tuple-element.10, bf16[4,5,96,384]{3,2,1,0:T(8,128)(2,1)} %collective-permute-done.10), kind=kLoop, calls=%fused_computation.10 | loop fusion | flops 1474560 | bytes 2949120 | tf_op jit(solution)/shard_map/add | solution.py:515
  (66 shorter events, 0.4 us)
Async XLA Ops:
  0.7 1.4 copy-start.2
  2.1 1.4 copy-start.6
  3.5 120.6 %copy-start.9 = (s32[2]{0:T(128)}, s32[2]{0:T(128)S(1)}, u32[]{:S(2)}) copy-start(s32[2]{0:T(128)S(1)} %pad_add_fusion.place) | copy-start | bytes 28
  3.5 8.6 %copy-start.8 = (bf16[5,96,384]{2,1,0:T(8,128)(2,1)S(1)}, bf16[5,96,384]{2,1,0:T(8,128)(2,1)}, u32[]{:S(2)}) copy-start(bf16[5,96,384]{2,1,0:T(8,128)(2,1)} %refs_0_.1) | copy-start | bytes 1105924
  7.6 9.1 %copy-start.7 = (bf16[144,1536]{1,0:T(8,128)(2,1)}, bf16[144,1536]{1,0:T(8,128)(2,1)S(1)}, u32[]{:S(2)}) copy-start(bf16[144,1536]{1,0:T(8,128)(2,1)S(1)} %get-tuple-element.9.refs_0_) | copy-start | bytes 1327108
  7.6 53.6 %collective-permute-start = (bf16[736,1536]{1,0:T(8,128)(2,1)}, bf16[736,1536]{1,0:T(8,128)(2,1)}, u32[]{:S(2)}, u32[]{:S(2)}) collective-permute-start(bf16[736,1536]{1,0:T(8,128)(2,1)} %get-tuple-element.7.refs_0_), channel_id=1, source_target_pairs={{0,8},{8,0},{16,24},{24,16},{1,9},{9,1},{17,25},{25,17},{2,10},{10... | collective-permute-start | bytes 6782984 | tf_op jit(solution)/shard_map/ppermute | solution.py:28
  10.6 49.5 %collective-permute-start.5 = (bf16[720,1536]{1,0:T(8,128)(2,1)S(1)}, bf16[720,1536]{1,0:T(8,128)(2,1)S(1)}, u32[]{:S(2)}, u32[]{:S(2)}) collective-permute-start(bf16[720,1536]{1,0:T(8,128)(2,1)S(1)} %get-tuple-element.8), channel_id=1, source_target_pairs={{0,16},{8,24},{16,0},{24,8},{1,17},{9,25},{17,1},{25,9},{2,18},{10... | collective-permute-start | bytes 6635528 | tf_op jit(solution)/shard_map/ppermute | solution.py:28
  12.2 27.3 %collective-permute-start.1 = (bf16[5,96,384]{2,1,0:T(8,128)(2,1)S(1)}, bf16[5,96,384]{2,1,0:T(8,128)(2,1)S(1)}, u32[]{:S(2)}, u32[]{:S(2)}) collective-permute-start(bf16[5,96,384]{2,1,0:T(8,128)(2,1)S(1)} %copy-done.8), channel_id=1, source_target_pairs={{0,2},{1,3},{2,0},{3,1},{4,6},{5,7},{6,4},{7,5},{8,10},{9,11},{10,... | collective-permute-start | bytes 1105928 | tf_op jit(solution)/shard_map/ppermute | solution.py:28
  13.7 18.2 %collective-permute-start.2 = (bf16[5,96,384]{2,1,0:T(8,128)(2,1)S(1)}, bf16[5,96,384]{2,1,0:T(8,128)(2,1)S(1)}, u32[]{:S(2)}, u32[]{:S(2)}) collective-permute-start(bf16[5,96,384]{2,1,0:T(8,128)(2,1)S(1)} %copy-done.8), channel_id=1, source_target_pairs={{0,6},{1,7},{2,4},{3,5},{4,2},{5,3},{6,0},{7,1},{8,14},{9,15},{10,... | collective-permute-start | bytes 1105928 | tf_op jit(solution)/shard_map/ppermute | solution.py:28
  32.0 8.8 %collective-permute-start.3 = (bf16[5,96,384]{2,1,0:T(8,128)(2,1)S(1)}, bf16[5,96,384]{2,1,0:T(8,128)(2,1)S(1)}, u32[]{:S(2)}, u32[]{:S(2)}) collective-permute-start(bf16[5,96,384]{2,1,0:T(8,128)(2,1)S(1)} %collective-permute-done.2.refs_3_), channel_id=1, source_target_pairs={{0,2},{1,3},{2,0},{3,1},{4,6},{5,7},{6,4},{7,5},{8,10},{9,11},{10,... | collective-permute-start | bytes 1105928 | tf_op jit(solution)/shard_map/ppermute | solution.py:28
  37.8 1.7 copy-start
  41.4 1.1 copy-start.1
  60.2 11.0 %copy-start.3 = (bf16[720,1536]{1,0:T(8,128)(2,1)}, bf16[720,1536]{1,0:T(8,128)(2,1)S(1)}, u32[]{:S(2)}) copy-start(bf16[720,1536]{1,0:T(8,128)(2,1)S(1)} %collective-permute-done.5.refs_2_) | copy-start | bytes 6635524
  63.6 5.7 %copy-start.10 = (bf16[336,1536]{1,0:T(8,128)(2,1)S(1)}, bf16[336,1536]{1,0:T(8,128)(2,1)}, u32[]{:S(2)}) copy-start(bf16[336,1536]{1,0:T(8,128)(2,1)} %after.12.refs_1_) | copy-start | bytes 3096580
  63.6 3.6 %collective-permute-start.7 = (bf16[4,5,96,384]{3,2,1,0:T(8,128)(2,1)}, bf16[4,5,96,384]{3,2,1,0:T(8,128)(2,1)}, u32[]{:S(2)}, u32[]{:S(2)}) collective-permute-start(bf16[4,5,96,384]{3,2,1,0:T(8,128)(2,1)} %after.14.refs_0_), channel_id=1, source_target_pairs={{0,1},{1,0},{2,3},{3,2},{4,5},{5,4},{6,7},{7,6},{8,9},{9,8},{10,11... | collective-permute-start | bytes 4423688 | tf_op jit(solution)/shard_map/ppermute | solution.py:28
  67.2 66.9 %collective-permute-start.8 = (bf16[4,5,96,384]{3,2,1,0:T(8,128)(2,1)}, bf16[4,5,96,384]{3,2,1,0:T(8,128)(2,1)}, u32[]{:S(2)}, u32[]{:S(2)}) collective-permute-start(bf16[4,5,96,384]{3,2,1,0:T(8,128)(2,1)} %after.15.refs_0_), channel_id=1, source_target_pairs={{0,8},{8,0},{16,24},{24,16},{1,9},{9,1},{17,25},{25,17},{2,10},{10... | collective-permute-start | bytes 4423688 | tf_op jit(solution)/shard_map/ppermute | solution.py:28
  67.7 66.8 %collective-permute-start.12 = (bf16[4,5,96,384]{3,2,1,0:T(8,128)(2,1)}, bf16[4,5,96,384]{3,2,1,0:T(8,128)(2,1)}, u32[]{:S(2)}, u32[]{:S(2)}) collective-permute-start(bf16[4,5,96,384]{3,2,1,0:T(8,128)(2,1)} %after.15.refs_0_), channel_id=1, source_target_pairs={{0,16},{8,24},{16,0},{24,8},{1,17},{9,25},{17,1},{25,9},{2,18},{10... | collective-permute-start | bytes 4423688 | tf_op jit(solution)/shard_map/ppermute | solution.py:28
  69.3 54.9 %collective-permute-start.4 = (bf16[336,1536]{1,0:T(8,128)(2,1)S(1)}, bf16[336,1536]{1,0:T(8,128)(2,1)S(1)}, u32[]{:S(2)}, u32[]{:S(2)}) collective-permute-start(bf16[336,1536]{1,0:T(8,128)(2,1)S(1)} %copy-done.10), channel_id=1, source_target_pairs={{0,16},{8,24},{16,0},{24,8},{1,17},{9,25},{17,1},{25,9},{2,18},{10... | collective-permute-start | bytes 3096584 | tf_op jit(solution)/shard_map/ppermute | solution.py:28
  69.8 53.0 %collective-permute-start.6 = (bf16[320,1536]{1,0:T(8,128)(2,1)}, bf16[320,1536]{1,0:T(8,128)(2,1)S(1)}, u32[]{:S(2)}, u32[]{:S(2)}) collective-permute-start(bf16[320,1536]{1,0:T(8,128)(2,1)} %after.13.refs_2_), channel_id=1, source_target_pairs={{0,8},{8,0},{16,24},{24,16},{1,9},{9,1},{17,25},{25,17},{2,10},{10... | collective-permute-start | bytes 2949128 | tf_op jit(solution)/shard_map/ppermute | solution.py:28
  122.8 11.1 %copy-start.5 = (bf16[320,1536]{1,0:T(8,128)(2,1)}, bf16[320,1536]{1,0:T(8,128)(2,1)S(1)}, u32[]{:S(2)}) copy-start(bf16[320,1536]{1,0:T(8,128)(2,1)S(1)} %collective-permute-done.6.refs_1_.refs_4_) | copy-start | bytes 2949124
  124.1 9.8 %copy-start.4 = (bf16[336,1536]{1,0:T(8,128)(2,1)}, bf16[336,1536]{1,0:T(8,128)(2,1)S(1)}, u32[]{:S(2)}) copy-start(bf16[336,1536]{1,0:T(8,128)(2,1)S(1)} %collective-permute-done.4.refs_0_.refs_3_) | copy-start | bytes 3096580
  134.0 7.9 %collective-permute-start.10 = (bf16[4,5,96,384]{3,2,1,0:T(8,128)(2,1)S(1)}, bf16[4,5,96,384]{3,2,1,0:T(8,128)(2,1)}, u32[]{:S(2)}, u32[]{:S(2)}) collective-permute-start(bf16[4,5,96,384]{3,2,1,0:T(8,128)(2,1)S(1)} %get-tuple-element.11), channel_id=1, source_target_pairs={{0,1},{1,0},{2,3},{3,2},{4,5},{5,4},{6,7},{7,6},{8,9},{9,8},{10,11... | collective-permute-start | bytes 4423688 | tf_op jit(solution)/shard_map/ppermute | solution.py:28
  134.1 10.2 %collective-permute-start.11 = (bf16[4,5,96,384]{3,2,1,0:T(8,128)(2,1)}, bf16[4,5,96,384]{3,2,1,0:T(8,128)(2,1)}, u32[]{:S(2)}, u32[]{:S(2)}) collective-permute-start(bf16[4,5,96,384]{3,2,1,0:T(8,128)(2,1)} %after.16.refs_7_), channel_id=1, source_target_pairs={{0,1},{1,0},{2,3},{3,2},{4,5},{5,4},{6,7},{7,6},{8,9},{9,8},{10,11... | collective-permute-start | bytes 4423688 | tf_op jit(solution)/shard_map/ppermute | solution.py:28
  134.5 7.3 %copy-start.13 = (f32[4,5,96,384]{3,2,1,0:T(8,128)S(1)}, f32[4,5,96,384]{3,2,1,0:T(8,128)}, u32[]{:S(2)}) copy-start(f32[4,5,96,384]{3,2,1,0:T(8,128)} %get-tuple-element.10) | copy-start | bytes 8847364
  134.5 9.7 %collective-permute-start.13 = (bf16[4,5,96,384]{3,2,1,0:T(8,128)(2,1)}, bf16[4,5,96,384]{3,2,1,0:T(8,128)(2,1)}, u32[]{:S(2)}, u32[]{:S(2)}) collective-permute-start(bf16[4,5,96,384]{3,2,1,0:T(8,128)(2,1)} %after.18.refs_9_), channel_id=1, source_target_pairs={{0,1},{1,0},{2,3},{3,2},{4,5},{5,4},{6,7},{7,6},{8,9},{9,8},{10,11... | collective-permute-start | bytes 4423688 | tf_op jit(solution)/shard_map/ppermute | solution.py:28
  136.8 21.5 %collective-permute-start.9 = (bf16[2,5,96,384]{3,2,1,0:T(8,128)(2,1)}, bf16[2,5,96,384]{3,2,1,0:T(8,128)(2,1)S(1)}, u32[]{:S(2)}, u32[]{:S(2)}) collective-permute-start(bf16[2,5,96,384]{3,2,1,0:T(8,128)(2,1)} %slice.66), channel_id=1, source_target_pairs={{0,16},{8,24},{16,0},{24,8},{1,17},{9,25},{17,1},{25,9},{2,18},{10... | collective-permute-start | bytes 2211848 | tf_op jit(solution)/shard_map/ppermute | solution.py:28
  140.4 18.8 %collective-permute-start.15 = (bf16[2,5,96,384]{3,2,1,0:T(8,128)(2,1)}, bf16[2,5,96,384]{3,2,1,0:T(8,128)(2,1)S(1)}, u32[]{:S(2)}, u32[]{:S(2)}) collective-permute-start(bf16[2,5,96,384]{3,2,1,0:T(8,128)(2,1)} %slice.70), channel_id=1, source_target_pairs={{0,8},{8,0},{16,24},{24,16},{1,9},{9,1},{17,25},{25,17},{2,10},{10... | collective-permute-start | bytes 2211848 | tf_op jit(solution)/shard_map/ppermute | solution.py:28
  158.3 0.9 copy-start.12
  159.2 1.4 copy-start.21
  159.2 5.0 %copy-start.20 = (bf16[5,96,384]{2,1,0:T(8,128)(2,1)S(1)}, bf16[5,96,384]{2,1,0:T(8,128)(2,1)}, u32[]{:S(2)}) copy-start(bf16[5,96,384]{2,1,0:T(8,128)(2,1)} %get-tuple-element.13.refs_2_) | copy-start | bytes 1105924
  159.2 5.0 %copy-start.19 = (bf16[5,96,384]{2,1,0:T(8,128)(2,1)S(1)}, bf16[5,96,384]{2,1,0:T(8,128)(2,1)}, u32[]{:S(2)}) copy-start(bf16[5,96,384]{2,1,0:T(8,128)(2,1)} %get-tuple-element.14.refs_1_) | copy-start | bytes 1105924
  159.2 5.8 %collective-permute-start.14 = (bf16[2,5,96,384]{3,2,1,0:T(8,128)(2,1)}, bf16[2,5,96,384]{3,2,1,0:T(8,128)(2,1)}, u32[]{:S(2)}, u32[]{:S(2)}) collective-permute-start(bf16[2,5,96,384]{3,2,1,0:T(8,128)(2,1)} %after.19.refs_2_), channel_id=1, source_target_pairs={{0,1},{1,0},{2,3},{3,2},{4,5},{5,4},{6,7},{7,6},{8,9},{9,8},{10,11... | collective-permute-start | bytes 2211848 | tf_op jit(solution)/shard_map/ppermute | solution.py:28
  159.2 0.9 copy-start.11
  160.1 4.9 %collective-permute-start.16 = (bf16[2,5,96,384]{3,2,1,0:T(8,128)(2,1)}, bf16[2,5,96,384]{3,2,1,0:T(8,128)(2,1)S(1)}, u32[]{:S(2)}, u32[]{:S(2)}) collective-permute-start(bf16[2,5,96,384]{3,2,1,0:T(8,128)(2,1)} %after.20.refs_4_), channel_id=1, source_target_pairs={{0,1},{1,0},{2,3},{3,2},{4,5},{5,4},{6,7},{7,6},{8,9},{9,8},{10,11... | collective-permute-start | bytes 2211848 | tf_op jit(solution)/shard_map/ppermute | solution.py:28
  160.6 14.2 %collective-permute-start.19 = (bf16[5,96,384]{2,1,0:T(8,128)(2,1)S(1)}, bf16[5,96,384]{2,1,0:T(8,128)(2,1)S(1)}, u32[]{:S(2)}, u32[]{:S(2)}) collective-permute-start(bf16[5,96,384]{2,1,0:T(8,128)(2,1)S(1)} %copy-done.21), channel_id=1, source_target_pairs={{0,6},{1,7},{2,4},{3,5},{4,2},{5,3},{6,0},{7,1},{8,14},{9,15},{10,... | collective-permute-start | bytes 1105928 | tf_op jit(solution)/shard_map/ppermute | solution.py:28
  164.2 31.6 %collective-permute-start.18 = (bf16[5,96,384]{2,1,0:T(8,128)(2,1)S(1)}, bf16[5,96,384]{2,1,0:T(8,128)(2,1)S(1)}, u32[]{:S(2)}, u32[]{:S(2)}) collective-permute-start(bf16[5,96,384]{2,1,0:T(8,128)(2,1)S(1)} %copy-done.20), channel_id=1, source_target_pairs={{0,4},{1,5},{2,6},{3,7},{4,0},{5,1},{6,2},{7,3},{8,12},{9,13},{10,... | collective-permute-start | bytes 1105928 | tf_op jit(solution)/shard_map/ppermute | solution.py:28
  164.2 32.4 %collective-permute-start.17 = (bf16[5,96,384]{2,1,0:T(8,128)(2,1)S(1)}, bf16[5,96,384]{2,1,0:T(8,128)(2,1)S(1)}, u32[]{:S(2)}, u32[]{:S(2)}) collective-permute-start(bf16[5,96,384]{2,1,0:T(8,128)(2,1)S(1)} %copy-done.19), channel_id=1, source_target_pairs={{0,2},{1,3},{2,0},{3,1},{4,6},{5,7},{6,4},{7,5},{8,10},{9,11},{10,... | collective-permute-start | bytes 1105928 | tf_op jit(solution)/shard_map/ppermute | solution.py:28
  165.0 0.9 copy-start.22
  174.9 0.7 copy-start.17
  175.6 21.7 %copy-start.18 = (bf16[5,96,384]{2,1,0:T(8,128)(2,1)S(1)}, bf16[5,96,384]{2,1,0:T(8,128)(2,1)}, u32[]{:S(2)}) copy-start(bf16[5,96,384]{2,1,0:T(8,128)(2,1)} %after.23) | copy-start | bytes 1105924
  195.8 0.8 copy-start.15
  196.6 1.1 copy-start.16
  196.6 0.7 copy-start.14

commit v11 on v10

--- a/solution.py
+++ b/solution.py
@@ -15,6 +15,7 @@
 EDGE = 16
 MARGIN = HALO - EDGE
 STEP = 64
+SPLIT = 3
 ROOT = math.sqrt(2.0 / math.pi)
 CUBIC = 0.044715
 SMALL = pl.CostEstimate(flops=1 << 20, bytes_accessed=1 << 16, transcendentals=0)
@@ -280,10 +281,10 @@
     )(place, shifts, early, *pieces)
 
 
-def shifted_total(products, base, lanes, parity):
+def shifted_total(products, first_tap, base, lanes, parity):
     total = None
     for by in (0, 1, -1):
-        wanted = [k for k in range(products.shape[0]) if ROW_OFFSETS[k][parity] == by]
+        wanted = [k for k in range(products.shape[0]) if ROW_OFFSETS[first_tap + k][parity] == by]
         if wanted:
             near = pl.ds(base + MARGIN - 8, STEP + 16)
             part = sum(products[k, near, lanes] for k in wanted)[8 + by : 8 + by + STEP]
@@ -291,25 +292,25 @@
     return total
 
 
-def gradient_stage(place, windows, pieces, distances, slope, begun, shape):
+def gradient_stage(place, windows, first_tap, pieces, distances, slope, begun, shape, last=False):
     _, fine, width = shape
     coarse, seqs = fine // 2, len(windows)
-    taps, rows, block = pieces[0][0].shape[1:]
+    taps, rows, block = pieces[0][0].shape[-3:]
     planes = width // (2 * rows)
     packed = (coarse + 2 * HALO) // CHUNKS
     window, used = CHUNKS * packed, coarse + 2 * MARGIN
     depth, planar = len(distances) * block, (2, coarse, width)
-    last = begun is not None
-    needed = distances if last else list(range(seqs))
+    first = begun is None
+    needed = list(range(seqs)) if first else distances
     parts = [(d, *part) for d in needed for part in windows[d]]
     operands = [part[1] for part in parts] + [piece[0] for piece in pieces]
-    operands += [slope] + ([begun] if last else [])
+    operands += [slope] + ([] if first else [begun])
 
     def body(place, *refs):
         own, refs = refs[: len(parts)], refs[len(parts) :]
         sources, refs = refs[: len(pieces)], refs[len(pieces) :]
         slope_ref, refs = refs[0], refs[1:]
-        if last:
+        if not first:
             begun_ref, refs = refs[0], refs[1:]
         out_ref, wv, gv, products, slopes, sems, grad_sems, slope_sem = refs[:8]
         me, core = place[0], place[1] % 2
@@ -319,7 +320,9 @@
                 spot = pl.ds(distances.index(distance) * block, block)
                 span = pl.ds(plane, array.shape[0])
                 target = wv.at[k, span, core ^ flip, :, spot]
-                yield sources[number].at[:, k], target, sems.at[k, number]
+                source = sources[number]
+                source = source.at[:, k] if len(array.shape) == 4 else source.at[:, distance, k]
+                yield source, target, sems.at[k, number]
 
         def window_copies(target_of, sems):
             for number, (distance, _, row, first, size) in enumerate(parts):
@@ -336,7 +339,7 @@
 
         early = list(window_copies(into_window, grad_sems))
         late = [pltpu.make_async_copy(slope_ref, slopes, slope_sem)]
-        if last:
+        if not first:
             sums, strip, sum_sem = refs[8:]
             late.append(pltpu.make_async_copy(begun_ref, sums, sum_sem))
         else:
@@ -376,18 +379,18 @@
             spot, span = pl.ds(base, STEP), pl.ds(pl.multiple_of(2 * base, 2 * STEP), 2 * STEP)
             for c in range(width // LANES):
                 lanes = slice(c * LANES, (c + 1) * LANES)
-                if not last:
+                if first:
                     left = c * LANES % block
                     skip = skips[c * LANES // block, pl.ds(base + HALO, STEP), left : left + LANES]
                     skip = 0.5 * skip.astype(jnp.float32)
                 for parity in range(2):
-                    total = shifted_total(products, base, lanes, parity)
+                    total = shifted_total(products, first_tap, base, lanes, parity)
                     total = total * slopes[parity, spot, lanes]
+                    total = total + (skip if first else sums[parity, spot, lanes])
                     if last:
-                        total = total + sums[parity, spot, lanes]
                         strip[c, pl.ds(parity, STEP, stride=2), :] = total
                     else:
-                        out_ref[parity, spot, lanes] = total + skip
+                        out_ref[parity, spot, lanes] = total
                 if last:
                     out_ref[0, span, lanes] = strip[c].astype(jnp.bfloat16)
 
@@ -401,7 +404,7 @@
         pltpu.SemaphoreType.DMA((len(parts), CHUNKS)),
         pltpu.SemaphoreType.DMA,
     ]
-    if last:
+    if not first:
         scratch += [
             pltpu.VMEM(planar, jnp.float32),
             pltpu.VMEM((width // LANES, 2 * STEP, LANES), jnp.float32),
@@ -424,7 +427,7 @@
         ),
         compiler_params=pltpu.CompilerParams(vmem_limit_bytes=56 << 20),
         cost_estimate=SMALL,
-        name="input_grad_late" if last else "input_grad_early",
+        name="input_grad",
     )(place, *operands)
 
 
@@ -443,8 +446,8 @@
         grid_spec=pltpu.PrefetchScalarGridSpec(
             num_scalar_prefetch=1,
             grid=(1,),
-            in_specs=[pl.BlockSpec(shape, lambda i, place: (0, 0, 0))] * count,
-            out_specs=pl.BlockSpec((count, *shape), lambda i, place: (0, 0, 0, 0)),
+            in_specs=[pl.BlockSpec(shape, lambda i, place: (0,) * len(shape))] * count,
+            out_specs=pl.BlockSpec((count, *shape), lambda i, place: (0,) * (1 + len(shape))),
         ),
         compiler_params=pltpu.CompilerParams(vmem_limit_bytes=24 << 20),
         cost_estimate=SMALL,
@@ -465,19 +468,21 @@
     to_beside, to_below, own_window = messages(place, inputs, trunk_grad)
     beside, below = from_peer(to_beside, "seq", 1), from_peer(to_below, "seq", 2)
     slope = half_slope(inputs)
-    column = stack_planes(place, gather_line(weights, "rep", planes, 2))
+    last_taps = weights[SPLIT:]
+    across = [last_taps] + [from_peer(last_taps, "seq", d) for d in range(1, seqs)]
+    column = stack_planes(place, gather_line(weights[:SPLIT], "rep", planes, 2))
+    lines = stack_planes(place, gather_line(jnp.stack(across), "rep", planes, 2))
     trunk = trunk_grad[0]
     zeros = jnp.zeros((1, block), jnp.bfloat16)
     later = jnp.concatenate([trunk[1:], zeros])
     earlier = jnp.concatenate([zeros, trunk[:-1]])
     shifts = jnp.concatenate([later, trunk, earlier], axis=1)
-    top = after(beside[: FIRST + half], slope, column, shifts)
-    bottom = after(below[half : coarse + packed - FIRST], slope, column, shifts)
+    top = after(beside[: FIRST + half], slope, column, lines, shifts)
+    bottom = after(below[half : coarse + packed - FIRST], slope, column, lines, shifts)
     far_top, far_bottom = from_peer(top, "seq", 2), from_peer(bottom, "seq", 1)
 
-    column = after(column, top, bottom)
-    other_column = from_peer(column, "rep", 1)
-    column = after(column, other_column)
+    other_column, other_lines = from_peer(column, "rep", 1), from_peer(lines, "rep", 1)
+    column = after(column, far_top, far_bottom)
     kept_beside, kept_below = from_peer(column, "seq", 1), from_peer(column, "seq", 2)
 
     scale = 0.5 * float(fine * seqs * reps) ** (-0.5)
@@ -506,11 +511,13 @@
         [(far_top, 0, 0, FIRST), (far_bottom, half, FIRST, packed - FIRST)],
     ]
     stage = functools.partial(gradient_stage, place, windows, slope=slope, shape=inputs.shape)
-    begun, rest = stage(soon, [0, 1, 2], begun=None), []
+    crossed = [(part, 0, flip, d) for flip, part in enumerate((lines, other_lines)) for d in range(seqs)]
+    begun = stage(SPLIT, crossed, list(range(seqs)), begun=None)
+    begun, rest = stage(0, soon, [0, 1, 2], begun=begun), []
     for part, plane in ((far_first, 0), (far_second, planes // 2)):
-        part = after(part, begun)
+        part = after(part, begun, *summed)
         rest += [(part, plane, 0, 3), (from_peer(part, "rep", 1), plane, 1, 3)]
-    input_grad = stage(rest, [3], begun=begun)
+    input_grad = stage(0, rest, [3], begun=begun, last=True)
     for part in summed:
         weight_grad = weight_grad + after(part, input_grad).astype(jnp.float32)
     return (input_grad, weight_grad)

time: 200 us -> 244 us (1.22)
  the two profiles are of different devices: /device:TPU:0 before, /device:TPU:9 now
where the time goes in v11:
time: 244 us; the launch traced here: 243 us
  waiting for transfers between devices  119 us (49%)
  Pallas kernels  58.8 us (24%)
  starting transfers between devices  30.6 us (13%)
  local copies, waits for them, and re-layouts  25.2 us (10%)
  other arithmetic  8.62 us (4%)
    ppermute x27, waiting for transfers between devices, from_peer(): return lax.ppermute(value, axis, [(i, i ^ distance) for i in range(peers)])  119 us
    ppermute x27, starting transfers between devices, from_peer(): return lax.ppermute(value, axis, [(i, i ^ distance) for i in range(peers)])  30.6 us
    pallas_call x3, Pallas kernels, gradient_stage(): pl.pallas_call(body, out_shape=out_shape, grid_spec=pltpu.PrefetchScalarG...  26.7 us
    unnamed x52, local copies, waits for them, and re-layouts  18.9 us
    pallas_call x1, Pallas kernels, early_terms(): pl.pallas_call(kernel, out_shape=jax.ShapeDtypeStruct((both, columns), jn...  13.4 us
    pallas_call x1, Pallas kernels, late_terms(): pl.pallas_call(kernel, out_shape=(jax.ShapeDtypeStruct(shape, jnp.float32...  10.8 us
  transfers between devices with their start and end apart: 27, of which 10 were waited for; matrix products, arithmetic and copies ran while one was open for 5% of the time, Pallas kernels for 20%

profile of v11, /device:TPU:9, one launch (start us, length us, event | category | flops | bytes accessed | tf_op | source)
XLA Modules:
  0.0 243.2 jit_solution(6387123618390557624)
XLA Ops:
  0.7 1.4 copy-done.7
  2.1 1.4 copy-done.8
  3.5 4.1 %messages.1 = (bf16[736,1536]{1,0:T(8,128)(2,1)S(1)}, bf16[720,1536]{1,0:T(8,128)(2,1)}, bf16[144,1536]{1,0:T(8,128)(2,1)S(1)}) custom-call(s32[2]{0:T(128)S(1)} %pad_add_fusion.place, bf16[1,1024,768]{2,1,0:T(8,128)(2,1)S(1)} %copy-done.8, bf16[1,2048,384]{2,1,0:T(8,128)(2,1)S(1)} %copy-done.7), custom_call_target="tpu_custom_call" | custom-call | tf_op jit(solution)/shard_map/messages/pallas_call | solution.py:105
  7.7 1.3 collective-permute-start
  9.0 1.2 collective-permute-start.11
  10.5 1.2 collective-permute-start.5
  11.8 1.2 collective-permute-start.4
  13.0 48.9 %collective-permute-done.6 = bf16[2,96,384]{2,1,0:T(8,128)(2,1)S(1)} collective-permute-done((bf16[2,96,384]{2,1,0:T(8,128)(2,1)S(1)}, bf16[2,96,384]{2,1,0:T(8,128)(2,1)S(1)}, u32[]{:S(2)}, u32[]{:S(2)}) %collective-permute-start.6) | collective-permute-done | bytes 147488 | tf_op jit(solution)/shard_map/ppermute | solution.py:29
  61.9 2.2 collective-permute-done.5
  64.2 1.4 collective-permute-start.8
  65.6 2.3 collective-permute-start.1
  68.4 17.5 %collective-permute-done.1.refs_1_ = bf16[3,96,384]{2,1,0:T(8,128)(2,1)S(1)} collective-permute-done((bf16[3,96,384]{2,1,0:T(8,128)(2,1)S(1)}, bf16[3,96,384]{2,1,0:T(8,128)(2,1)S(1)}, u32[]{:S(2)}, u32[]{:S(2)}) %collective-permute-start.1) | collective-permute-done | bytes 221216 | tf_op jit(solution)/shard_map/ppermute | solution.py:29
  85.9 2.7 %collective-permute-start.7 = (bf16[4,2,96,384]{3,2,1,0:T(8,128)(2,1)S(1)}, bf16[4,2,96,384]{3,2,1,0:T(8,128)(2,1)S(1)}, u32[]{:S(2)}, u32[]{:S(2)}) collective-permute-start(bf16[4,2,96,384]{3,2,1,0:T(8,128)(2,1)S(1)} %pad_maximum_fusion.refs_0_), channel_id=1, source_target_pairs={{0,2},{1,3},{2,0},{3,1},{4,6},{5,7},{6,4},{7,5},{8,10},{9,11},{10,... | collective-permute-start | bytes 1769480 | tf_op jit(solution)/shard_map/ppermute | solution.py:29
  88.6 12.0 %collective-permute-done.2.refs_3_ = bf16[3,96,384]{2,1,0:T(8,128)(2,1)S(1)} collective-permute-done((bf16[3,96,384]{2,1,0:T(8,128)(2,1)S(1)}, bf16[3,96,384]{2,1,0:T(8,128)(2,1)S(1)}, u32[]{:S(2)}, u32[]{:S(2)}) %collective-permute-start.2) | collective-permute-done | bytes 221216 | tf_op jit(solution)/shard_map/ppermute | solution.py:29
  100.7 1.5 collective-permute-start.9
  102.1 3.0 %fusion.2.refs_4_.shifts_ref = bf16[2048,1152]{1,0:T(8,128)(2,1)} fusion(bf16[2047,384]{1,0:T(8,128)(2,1)S(1)} %get-tuple-element.16, bf16[2047,384]{1,0:T(8,128)(2,1)S(1)} %get-tuple-element.15, bf16[2048,384]{1,0:T(8,128)(2,1)S(1)} %bitcast.24), kind=kLoop, calls=%fused_computation.4 | loop fusion | flops 23592960 | bytes 9435648 | tf_op jit(solution)/shard_map/concatenate | solution.py:479
  105.1 2.3 half_slope.1.refs_1_.refs_13_.refs_9_.refs_6_
  107.5 1.6 copy-done.2
  110.7 9.0 %collective-permute-done.9.refs_2_ = bf16[4,2,96,384]{3,2,1,0:T(8,128)(2,1)S(1)} collective-permute-done((bf16[4,2,96,384]{3,2,1,0:T(8,128)(2,1)S(1)}, bf16[4,2,96,384]{3,2,1,0:T(8,128)(2,1)S(1)}, u32[]{:S(2)}, u32[]{:S(2)}) %collective-permute-start.9) | collective-permute-done | bytes 589856 | tf_op jit(solution)/shard_map/ppermute | solution.py:29
  120.4 1.4 copy-done
  121.8 1.5 copy-done.13
  123.3 1.0 slice.72.refs_0_
  124.3 1.2 collective-permute-start.10
  125.6 1.0 slice.73.refs_0_
  126.6 1.4 copy-done.5
  128.0 1.2 collective-permute-start.12
  129.2 2.5 %collective-permute-start.16 = (bf16[4,3,96,384]{3,2,1,0:T(8,128)(2,1)S(1)}, bf16[4,3,96,384]{3,2,1,0:T(8,128)(2,1)S(1)}, u32[]{:S(2)}, u32[]{:S(2)}) collective-permute-start(bf16[4,3,96,384]{3,2,1,0:T(8,128)(2,1)S(1)} %copy-done.4), channel_id=1, source_target_pairs={{0,1},{1,0},{2,3},{3,2},{4,5},{5,4},{6,7},{7,6},{8,9},{9,8},{10,11... | collective-permute-start | bytes 2654216 | tf_op jit(solution)/shard_map/ppermute | solution.py:29
  132.2 1.6 collective-permute-done.16.refs_4_
  134.7 14.6 %collective-permute-done.12.refs_2_.refs_1_.refs_4_ = bf16[320,1536]{1,0:T(8,128)(2,1)} collective-permute-done((bf16[320,1536]{1,0:T(8,128)(2,1)}, bf16[320,1536]{1,0:T(8,128)(2,1)}, u32[]{:S(2)}, u32[]{:S(2)}) %collective-permute-start.12) | collective-permute-done | bytes 983072 | tf_op jit(solution)/shard_map/ppermute | solution.py:29
  149.3 1.3 collective-permute-start.13
  150.8 1.6 copy-done.6
  152.5 1.6 copy-done.10
  154.1 13.4 %weight_grad_early.1.refs_1_.early_ref = f32[1536,1152]{1,0:T(8,128)} custom-call(s32[2]{0:T(128)S(1)} %pad_add_fusion.place, bf16[2048,1152]{1,0:T(8,128)(2,1)} %fusion.2.refs_4_.shifts_ref, bf16[736,1536]{1,0:T(8,128)(2,1)S(1)} %copy-done.10, bf16[736,1536]{1,0:T(8,128)(2,1)} %copy-done.13, bf16[720,1536]{1,0:T(8,128)(2,1)S(1)} %copy-done.6), custom_call_target="tpu_custom_call" | custom-call | flops 1048576 | bytes 65536 | tf_op jit(solution)/shard_map/weight_grad_early/pallas_call | solution.py:188
  167.5 10.8 %weight_grad_late.1 = (f32[4,5,96,384]{3,2,1,0:T(8,128)}, bf16[4,5,96,384]{3,2,1,0:T(8,128)(2,1)}) custom-call(s32[2]{0:T(128)S(1)} %pad_add_fusion.place, bf16[2048,1152]{1,0:T(8,128)(2,1)} %fusion.2.refs_4_.shifts_ref, f32[1536,1152]{1,0:T(8,128)} %weight_grad_early.1.refs_1_.early_ref, bf16[336,1536]{1,0:T(8,128)(2,1)} %collective-permute-done.10.refs_1_.refs_0_.refs_3_, ...), custom_call_target="tpu_custom_call" | custom-call | flops 1048576 | bytes 65536 | tf_op jit(solution)/shard_map/weight_grad_late/pallas_call | solution.py:258
  178.3 3.7 %collective-permute-start.15 = (bf16[4,5,96,384]{3,2,1,0:T(8,128)(2,1)}, bf16[4,5,96,384]{3,2,1,0:T(8,128)(2,1)}, u32[]{:S(2)}, u32[]{:S(2)}) collective-permute-start(bf16[4,5,96,384]{3,2,1,0:T(8,128)(2,1)} %get-tuple-element.11), channel_id=1, source_target_pairs={{0,1},{1,0},{2,3},{3,2},{4,5},{5,4},{6,7},{7,6},{8,9},{9,8},{10,11... | collective-permute-start | bytes 4423688 | tf_op jit(solution)/shard_map/ppermute | solution.py:29
  183.5 1.8 slice.74
  185.3 1.8 slice.78
  187.2 1.2 collective-permute-start.14
  188.7 3.0 %fusion.8 = (bf16[5,96,384]{2,1,0:T(8,128)(2,1)}, bf16[5,96,384]{2,1,0:T(8,128)(2,1)}, bf16[5,96,384]{2,1,0:T(8,128)(2,1)}) fusion(f32[4,5,96,384]{3,2,1,0:T(8,128)} %get-tuple-element.10, bf16[4,5,96,384]{3,2,1,0:T(8,128)(2,1)} %collective-permute-done.15), kind=kLoop, calls=%fused_computation.17 | loop fusion | flops 1658880 | bytes 4423680 | tf_op jit(solution)/shard_map/convert_element_type | solution.py:497
  191.6 2.2 collective-permute-start.21
  194.7 1.3 collective-permute-start.23
  196.0 9.9 %input_grad.3.refs_10_ = f32[2,512,768]{2,1,0:T(8,128)} custom-call(s32[2]{0:T(128)} %copy-done.12, bf16[144,1536]{1,0:T(8,128)(2,1)} %copy-done.11, bf16[736,1536]{1,0:T(8,128)(2,1)} %copy-done.13, bf16[720,1536]{1,0:T(8,128)(2,1)} %copy-done.5, bf16[336,1536]{1,0:T(8,128)(2,1)} %collective-permute-done.10.refs_1_.refs_0_.refs_3_, ...), custom_call_target="tpu_custom_call" | custom-call | flops 1048576 | bytes 65536 | tf_op jit(solution)/shard_map/input_grad/pallas_call | solution.py:418
  205.9 10.0 %input_grad.4.refs_1_.refs_7_ = f32[2,512,768]{2,1,0:T(8,128)} custom-call(s32[2]{0:T(128)} %copy-done.12, bf16[144,1536]{1,0:T(8,128)(2,1)} %copy-done.11, bf16[736,1536]{1,0:T(8,128)(2,1)} %copy-done.13, bf16[720,1536]{1,0:T(8,128)(2,1)} %copy-done.5, bf16[4,3,96,384]{3,2,1,0:T(8,128)(2,1)} %after.15.refs_3_, bf16[4,3,96,384]{3,2,1,0:T(8,128)(2,1)} %copy-done.21, ...), custom_call_target="tpu_custom_call" | custom-call | flops 1048576 | bytes 65536 | tf_op jit(solution)/shard_map/input_grad/pallas_call | solution.py:418
  216.0 11.1 %collective-permute-done.23.refs_4_.refs_0_ = bf16[5,96,384]{2,1,0:T(8,128)(2,1)S(1)} collective-permute-done((bf16[5,96,384]{2,1,0:T(8,128)(2,1)}, bf16[5,96,384]{2,1,0:T(8,128)(2,1)S(1)}, u32[]{:S(2)}, u32[]{:S(2)}) %collective-permute-start.23) | collective-permute-done | bytes 368672 | tf_op jit(solution)/shard_map/ppermute | solution.py:29
  227.8 1.5 collective-permute-start.24
  230.9 1.2 collective-permute-done.26.refs_5_
  232.9 6.8 %input_grad.5.refs_1_ = bf16[1,1024,768]{2,1,0:T(8,128)(2,1)} custom-call(s32[2]{0:T(128)} %copy-done.12, bf16[336,1536]{1,0:T(8,128)(2,1)} %collective-permute-done.10.refs_1_.refs_0_.refs_3_, bf16[320,1536]{1,0:T(8,128)(2,1)} %collective-permute-done.12.refs_2_.refs_1_.refs_4_, bf16[2,3,96,384]{3,2,1,0:T(8,128)(2,1)} %after.17.refs_2_, ...), custom_call_target="tpu_custom_call" | custom-call | flops 1048576 | bytes 65536 | tf_op jit(solution)/shard_map/input_grad/pallas_call | solution.py:418
  240.7 2.5 %fusion.5 = f32[5,96,384]{2,1,0:T(8,128)} fusion(bf16[5,96,384]{2,1,0:T(8,128)(2,1)S(1)} %copy-done.17, bf16[5,96,384]{2,1,0:T(8,128)(2,1)} %after.20, bf16[5,96,384]{2,1,0:T(8,128)(2,1)} %after.19, f32[4,5,96,384]{3,2,1,0:T(8,128)} %get-tuple-element.10, bf16[4,5,96,384]{3,2,1,0:T(8,128)(2,1)} %collective-permute-done.15), kind=kLoop, calls=%fused_computation.10 | loop fusion | flops 1474560 | bytes 2949120 | tf_op jit(solution)/shard_map/add | solution.py:522
  (90 shorter events, 11.7 us)
Async XLA Ops:
  0.7 1.4 copy-start.7
  2.1 1.4 copy-start.8
  3.5 164.0 %copy-start.12 = (s32[2]{0:T(128)}, s32[2]{0:T(128)S(1)}, u32[]{:S(2)}) copy-start(s32[2]{0:T(128)S(1)} %pad_add_fusion.place) | copy-start | bytes 28
  3.5 6.7 %copy-start.25 = (bf16[5,96,384]{2,1,0:T(8,128)(2,1)S(1)}, bf16[5,96,384]{2,1,0:T(8,128)(2,1)}, u32[]{:S(2)}) copy-start(bf16[5,96,384]{2,1,0:T(8,128)(2,1)} %param.5) | copy-start | bytes 1105924
  7.7 60.7 %copy-start.9 = (bf16[736,1536]{1,0:T(8,128)(2,1)}, bf16[736,1536]{1,0:T(8,128)(2,1)S(1)}, u32[]{:S(2)}) copy-start(bf16[736,1536]{1,0:T(8,128)(2,1)S(1)} %get-tuple-element.7.refs_0_) | copy-start | bytes 6782980
  7.7 60.7 %copy-start.11 = (bf16[144,1536]{1,0:T(8,128)(2,1)}, bf16[144,1536]{1,0:T(8,128)(2,1)S(1)}, u32[]{:S(2)}) copy-start(bf16[144,1536]{1,0:T(8,128)(2,1)S(1)} %get-tuple-element.9.refs_0_) | copy-start | bytes 1327108
  7.7 114.1 %collective-permute-start = (bf16[736,1536]{1,0:T(8,128)(2,1)S(1)}, bf16[736,1536]{1,0:T(8,128)(2,1)S(1)}, u32[]{:S(2)}, u32[]{:S(2)}) collective-permute-start(bf16[736,1536]{1,0:T(8,128)(2,1)S(1)} %get-tuple-element.7.refs_0_), channel_id=1, source_target_pairs={{0,8},{8,0},{16,24},{24,16},{1,9},{9,1},{17,25},{25,17},{2,10},{10... | collective-permute-start | bytes 6782984 | tf_op jit(solution)/shard_map/ppermute | solution.py:29
  9.0 116.6 %collective-permute-start.11 = (bf16[720,1536]{1,0:T(8,128)(2,1)}, bf16[720,1536]{1,0:T(8,128)(2,1)S(1)}, u32[]{:S(2)}, u32[]{:S(2)}) collective-permute-start(bf16[720,1536]{1,0:T(8,128)(2,1)} %get-tuple-element.8), channel_id=1, source_target_pairs={{0,16},{8,24},{16,0},{24,8},{1,17},{9,25},{17,1},{25,9},{2,18},{10... | collective-permute-start | bytes 6635528 | tf_op jit(solution)/shard_map/ppermute | solution.py:29
  10.2 51.6 %collective-permute-start.6 = (bf16[2,96,384]{2,1,0:T(8,128)(2,1)S(1)}, bf16[2,96,384]{2,1,0:T(8,128)(2,1)S(1)}, u32[]{:S(2)}, u32[]{:S(2)}) collective-permute-start(bf16[2,96,384]{2,1,0:T(8,128)(2,1)S(1)} %get-tuple-element.18), channel_id=1, source_target_pairs={{0,24},{8,16},{16,8},{24,0},{1,25},{9,17},{17,9},{25,1},{2,26},{10... | collective-permute-start | bytes 442376 | tf_op jit(solution)/shard_map/ppermute | solution.py:29
  10.5 53.6 %collective-permute-start.5 = (bf16[2,96,384]{2,1,0:T(8,128)(2,1)S(1)}, bf16[2,96,384]{2,1,0:T(8,128)(2,1)S(1)}, u32[]{:S(2)}, u32[]{:S(2)}) collective-permute-start(bf16[2,96,384]{2,1,0:T(8,128)(2,1)S(1)} %get-tuple-element.18), channel_id=1, source_target_pairs={{0,16},{8,24},{16,0},{24,8},{1,17},{9,25},{17,1},{25,9},{2,18},{10... | collective-permute-start | bytes 442376 | tf_op jit(solution)/shard_map/ppermute | solution.py:29
  11.8 52.3 %collective-permute-start.4 = (bf16[2,96,384]{2,1,0:T(8,128)(2,1)S(1)}, bf16[2,96,384]{2,1,0:T(8,128)(2,1)S(1)}, u32[]{:S(2)}, u32[]{:S(2)}) collective-permute-start(bf16[2,96,384]{2,1,0:T(8,128)(2,1)S(1)} %get-tuple-element.18), channel_id=1, source_target_pairs={{0,8},{8,0},{16,24},{24,16},{1,9},{9,1},{17,25},{25,17},{2,10},{10... | collective-permute-start | bytes 442376 | tf_op jit(solution)/shard_map/ppermute | solution.py:29
  64.2 36.5 %collective-permute-start.8 = (bf16[4,2,96,384]{3,2,1,0:T(8,128)(2,1)S(1)}, bf16[4,2,96,384]{3,2,1,0:T(8,128)(2,1)S(1)}, u32[]{:S(2)}, u32[]{:S(2)}) collective-permute-start(bf16[4,2,96,384]{3,2,1,0:T(8,128)(2,1)S(1)} %pad_maximum_fusion.refs_0_), channel_id=1, source_target_pairs={{0,6},{1,7},{2,4},{3,5},{4,2},{5,3},{6,0},{7,1},{8,14},{9,15},{10,... | collective-permute-start | bytes 1769480 | tf_op jit(solution)/shard_map/ppermute | solution.py:29
  65.6 20.3 %collective-permute-start.1 = (bf16[3,96,384]{2,1,0:T(8,128)(2,1)S(1)}, bf16[3,96,384]{2,1,0:T(8,128)(2,1)S(1)}, u32[]{:S(2)}, u32[]{:S(2)}) collective-permute-start(bf16[3,96,384]{2,1,0:T(8,128)(2,1)S(1)} %slice.55.refs_0_), channel_id=1, source_target_pairs={{0,2},{1,3},{2,0},{3,1},{4,6},{5,7},{6,4},{7,5},{8,10},{9,11},{10,... | collective-permute-start | bytes 663560 | tf_op jit(solution)/shard_map/ppermute | solution.py:29
  67.8 32.8 %collective-permute-start.2 = (bf16[3,96,384]{2,1,0:T(8,128)(2,1)S(1)}, bf16[3,96,384]{2,1,0:T(8,128)(2,1)S(1)}, u32[]{:S(2)}, u32[]{:S(2)}) collective-permute-start(bf16[3,96,384]{2,1,0:T(8,128)(2,1)S(1)} %slice.55.refs_0_), channel_id=1, source_target_pairs={{0,6},{1,7},{2,4},{3,5},{4,2},{5,3},{6,0},{7,1},{8,14},{9,15},{10,... | collective-permute-start | bytes 663560 | tf_op jit(solution)/shard_map/ppermute | solution.py:29
  85.9 24.7 %collective-permute-start.7 = (bf16[4,2,96,384]{3,2,1,0:T(8,128)(2,1)S(1)}, bf16[4,2,96,384]{3,2,1,0:T(8,128)(2,1)S(1)}, u32[]{:S(2)}, u32[]{:S(2)}) collective-permute-start(bf16[4,2,96,384]{3,2,1,0:T(8,128)(2,1)S(1)} %pad_maximum_fusion.refs_0_), channel_id=1, source_target_pairs={{0,2},{1,3},{2,0},{3,1},{4,6},{5,7},{6,4},{7,5},{8,10},{9,11},{10,... | collective-permute-start | bytes 1769480 | tf_op jit(solution)/shard_map/ppermute | solution.py:29
  100.7 8.4 %collective-permute-start.3 = (bf16[3,96,384]{2,1,0:T(8,128)(2,1)S(1)}, bf16[3,96,384]{2,1,0:T(8,128)(2,1)S(1)}, u32[]{:S(2)}, u32[]{:S(2)}) collective-permute-start(bf16[3,96,384]{2,1,0:T(8,128)(2,1)S(1)} %collective-permute-done.2.refs_3_), channel_id=1, source_target_pairs={{0,2},{1,3},{2,0},{3,1},{4,6},{5,7},{6,4},{7,5},{8,10},{9,11},{10,... | collective-permute-start | bytes 663560 | tf_op jit(solution)/shard_map/ppermute | solution.py:29
  100.7 19.0 %collective-permute-start.9 = (bf16[4,2,96,384]{3,2,1,0:T(8,128)(2,1)S(1)}, bf16[4,2,96,384]{3,2,1,0:T(8,128)(2,1)S(1)}, u32[]{:S(2)}, u32[]{:S(2)}) collective-permute-start(bf16[4,2,96,384]{3,2,1,0:T(8,128)(2,1)S(1)} %collective-permute-done.8.refs_3_), channel_id=1, source_target_pairs={{0,2},{1,3},{2,0},{3,1},{4,6},{5,7},{6,4},{7,5},{8,10},{9,11},{10,... | collective-permute-start | bytes 1769480 | tf_op jit(solution)/shard_map/ppermute | solution.py:29
  107.5 1.6 copy-start.2
  109.7 0.9 copy-start.3
  120.4 1.4 copy-start
  121.8 1.5 copy-start.13
  124.3 25.0 %collective-permute-start.10 = (bf16[336,1536]{1,0:T(8,128)(2,1)}, bf16[336,1536]{1,0:T(8,128)(2,1)}, u32[]{:S(2)}, u32[]{:S(2)}) collective-permute-start(bf16[336,1536]{1,0:T(8,128)(2,1)} %after.11), channel_id=1, source_target_pairs={{0,16},{8,24},{16,0},{24,8},{1,17},{9,25},{17,1},{25,9},{2,18},{10... | collective-permute-start | bytes 3096584 | tf_op jit(solution)/shard_map/ppermute | solution.py:29
  126.6 1.4 copy-start.5
  128.0 1.2 copy-start.4
  128.0 3.7 %copy-start.1 = (bf16[4,4,2,96,384]{4,3,2,1,0:T(8,128)(2,1)S(1)}, bf16[4,4,2,96,384]{4,3,2,1,0:T(8,128)(2,1)}, u32[]{:S(2)}) copy-start(bf16[4,4,2,96,384]{4,3,2,1,0:T(8,128)(2,1)} %copy-done) | copy-start | bytes 7077892
  128.0 21.3 %collective-permute-start.12 = (bf16[320,1536]{1,0:T(8,128)(2,1)}, bf16[320,1536]{1,0:T(8,128)(2,1)}, u32[]{:S(2)}, u32[]{:S(2)}) collective-permute-start(bf16[320,1536]{1,0:T(8,128)(2,1)} %after.12), channel_id=1, source_target_pairs={{0,8},{8,0},{16,24},{24,16},{1,9},{9,1},{17,25},{25,17},{2,10},{10... | collective-permute-start | bytes 2949128 | tf_op jit(solution)/shard_map/ppermute | solution.py:29
  129.2 4.5 %collective-permute-start.16 = (bf16[4,3,96,384]{3,2,1,0:T(8,128)(2,1)S(1)}, bf16[4,3,96,384]{3,2,1,0:T(8,128)(2,1)S(1)}, u32[]{:S(2)}, u32[]{:S(2)}) collective-permute-start(bf16[4,3,96,384]{3,2,1,0:T(8,128)(2,1)S(1)} %copy-done.4), channel_id=1, source_target_pairs={{0,1},{1,0},{2,3},{3,2},{4,5},{5,4},{6,7},{7,6},{8,9},{9,8},{10,11... | collective-permute-start | bytes 2654216 | tf_op jit(solution)/shard_map/ppermute | solution.py:29
  131.7 59.9 %collective-permute-start.20 = (bf16[4,4,2,96,384]{4,3,2,1,0:T(8,128)(2,1)S(1)}, bf16[4,4,2,96,384]{4,3,2,1,0:T(8,128)(2,1)}, u32[]{:S(2)}, u32[]{:S(2)}) collective-permute-start(bf16[4,4,2,96,384]{4,3,2,1,0:T(8,128)(2,1)S(1)} %copy-done.1), channel_id=1, source_target_pairs={{0,1},{1,0},{2,3},{3,2},{4,5},{5,4},{6,7},{7,6},{8,9},{9,8},{10,11... | collective-permute-start | bytes 7077896 | tf_op jit(solution)/shard_map/ppermute | solution.py:29
  149.3 32.8 %collective-permute-start.13 = (bf16[4,3,96,384]{3,2,1,0:T(8,128)(2,1)}, bf16[4,3,96,384]{3,2,1,0:T(8,128)(2,1)}, u32[]{:S(2)}, u32[]{:S(2)}) collective-permute-start(bf16[4,3,96,384]{3,2,1,0:T(8,128)(2,1)} %after.13.refs_0_), channel_id=1, source_target_pairs={{0,8},{8,0},{16,24},{24,16},{1,9},{9,1},{17,25},{25,17},{2,10},{10... | collective-permute-start | bytes 2654216 | tf_op jit(solution)/shard_map/ppermute | solution.py:29
  150.6 31.6 %collective-permute-start.18 = (bf16[4,3,96,384]{3,2,1,0:T(8,128)(2,1)}, bf16[4,3,96,384]{3,2,1,0:T(8,128)(2,1)S(1)}, u32[]{:S(2)}, u32[]{:S(2)}) collective-permute-start(bf16[4,3,96,384]{3,2,1,0:T(8,128)(2,1)} %after.13.refs_0_), channel_id=1, source_target_pairs={{0,16},{8,24},{16,0},{24,8},{1,17},{9,25},{17,1},{25,9},{2,18},{10... | collective-permute-start | bytes 2654216 | tf_op jit(solution)/shard_map/ppermute | solution.py:29
  150.8 1.6 copy-start.6
  152.5 1.6 copy-start.10
  178.3 10.1 %collective-permute-start.15 = (bf16[4,5,96,384]{3,2,1,0:T(8,128)(2,1)}, bf16[4,5,96,384]{3,2,1,0:T(8,128)(2,1)}, u32[]{:S(2)}, u32[]{:S(2)}) collective-permute-start(bf16[4,5,96,384]{3,2,1,0:T(8,128)(2,1)} %get-tuple-element.11), channel_id=1, source_target_pairs={{0,1},{1,0},{2,3},{3,2},{4,5},{5,4},{6,7},{7,6},{8,9},{9,8},{10,11... | collective-permute-start | bytes 4423688 | tf_op jit(solution)/shard_map/ppermute | solution.py:29
  182.1 11.7 %collective-permute-start.17 = (bf16[4,3,96,384]{3,2,1,0:T(8,128)(2,1)}, bf16[4,3,96,384]{3,2,1,0:T(8,128)(2,1)}, u32[]{:S(2)}, u32[]{:S(2)}) collective-permute-start(bf16[4,3,96,384]{3,2,1,0:T(8,128)(2,1)} %after.14.refs_5_), channel_id=1, source_target_pairs={{0,1},{1,0},{2,3},{3,2},{4,5},{5,4},{6,7},{7,6},{8,9},{9,8},{10,11... | collective-permute-start | bytes 2654216 | tf_op jit(solution)/shard_map/ppermute | solution.py:29
  183.1 10.7 %collective-permute-start.19 = (bf16[4,3,96,384]{3,2,1,0:T(8,128)(2,1)}, bf16[4,3,96,384]{3,2,1,0:T(8,128)(2,1)S(1)}, u32[]{:S(2)}, u32[]{:S(2)}) collective-permute-start(bf16[4,3,96,384]{3,2,1,0:T(8,128)(2,1)} %after.16.refs_7_), channel_id=1, source_target_pairs={{0,1},{1,0},{2,3},{3,2},{4,5},{5,4},{6,7},{7,6},{8,9},{9,8},{10,11... | collective-permute-start | bytes 2654216 | tf_op jit(solution)/shard_map/ppermute | solution.py:29
  187.2 28.7 %collective-permute-start.14 = (bf16[2,3,96,384]{3,2,1,0:T(8,128)(2,1)}, bf16[2,3,96,384]{3,2,1,0:T(8,128)(2,1)S(1)}, u32[]{:S(2)}, u32[]{:S(2)}) collective-permute-start(bf16[2,3,96,384]{3,2,1,0:T(8,128)(2,1)} %slice.74), channel_id=1, source_target_pairs={{0,16},{8,24},{16,0},{24,8},{1,17},{9,25},{17,1},{25,9},{2,18},{10... | collective-permute-start | bytes 1327112 | tf_op jit(solution)/shard_map/ppermute | solution.py:29
  188.4 40.9 %collective-permute-start.25 = (bf16[2,3,96,384]{3,2,1,0:T(8,128)(2,1)}, bf16[2,3,96,384]{3,2,1,0:T(8,128)(2,1)S(1)}, u32[]{:S(2)}, u32[]{:S(2)}) collective-permute-start(bf16[2,3,96,384]{3,2,1,0:T(8,128)(2,1)} %slice.78), channel_id=1, source_target_pairs={{0,8},{8,0},{16,24},{24,16},{1,9},{9,1},{17,25},{25,17},{2,10},{10... | collective-permute-start | bytes 1327112 | tf_op jit(solution)/shard_map/ppermute | solution.py:29
  191.6 24.3 %collective-permute-start.21 = (bf16[5,96,384]{2,1,0:T(8,128)(2,1)}, bf16[5,96,384]{2,1,0:T(8,128)(2,1)S(1)}, u32[]{:S(2)}, u32[]{:S(2)}) collective-permute-start(bf16[5,96,384]{2,1,0:T(8,128)(2,1)} %get-tuple-element.14.refs_1_), channel_id=1, source_target_pairs={{0,2},{1,3},{2,0},{3,1},{4,6},{5,7},{6,4},{7,5},{8,10},{9,11},{10,... | collective-permute-start | bytes 1105928 | tf_op jit(solution)/shard_map/ppermute | solution.py:29
  193.8 22.1 %collective-permute-start.22 = (bf16[5,96,384]{2,1,0:T(8,128)(2,1)}, bf16[5,96,384]{2,1,0:T(8,128)(2,1)S(1)}, u32[]{:S(2)}, u32[]{:S(2)}) collective-permute-start(bf16[5,96,384]{2,1,0:T(8,128)(2,1)} %get-tuple-element.13.refs_2_), channel_id=1, source_target_pairs={{0,4},{1,5},{2,6},{3,7},{4,0},{5,1},{6,2},{7,3},{8,12},{9,13},{10,... | collective-permute-start | bytes 1105928 | tf_op jit(solution)/shard_map/ppermute | solution.py:29
  193.8 0.9 copy-start.22
  194.7 32.4 %collective-permute-start.23 = (bf16[5,96,384]{2,1,0:T(8,128)(2,1)}, bf16[5,96,384]{2,1,0:T(8,128)(2,1)S(1)}, u32[]{:S(2)}, u32[]{:S(2)}) collective-permute-start(bf16[5,96,384]{2,1,0:T(8,128)(2,1)} %get-tuple-element.12.refs_3_), channel_id=1, source_target_pairs={{0,6},{1,7},{2,4},{3,5},{4,2},{5,3},{6,0},{7,1},{8,14},{9,15},{10,... | collective-permute-start | bytes 1105928 | tf_op jit(solution)/shard_map/ppermute | solution.py:29
  215.9 11.2 %copy-start.20 = (bf16[2,3,96,384]{3,2,1,0:T(8,128)(2,1)}, bf16[2,3,96,384]{3,2,1,0:T(8,128)(2,1)S(1)}, u32[]{:S(2)}) copy-start(bf16[2,3,96,384]{3,2,1,0:T(8,128)(2,1)S(1)} %collective-permute-done.14.refs_0_) | copy-start | bytes 1327108
  215.9 11.2 %copy-start.14 = (bf16[5,96,384]{2,1,0:T(8,128)(2,1)}, bf16[5,96,384]{2,1,0:T(8,128)(2,1)S(1)}, u32[]{:S(2)}) copy-start(bf16[5,96,384]{2,1,0:T(8,128)(2,1)S(1)} %collective-permute-done.21.refs_2_.refs_0_) | copy-start | bytes 1105924
  216.0 11.2 %copy-start.15 = (bf16[5,96,384]{2,1,0:T(8,128)(2,1)}, bf16[5,96,384]{2,1,0:T(8,128)(2,1)S(1)}, u32[]{:S(2)}) copy-start(bf16[5,96,384]{2,1,0:T(8,128)(2,1)S(1)} %collective-permute-done.22.refs_3_.refs_0_) | copy-start | bytes 1105924
  227.8 3.1 %collective-permute-start.24 = (bf16[2,3,96,384]{3,2,1,0:T(8,128)(2,1)}, bf16[2,3,96,384]{3,2,1,0:T(8,128)(2,1)S(1)}, u32[]{:S(2)}, u32[]{:S(2)}) collective-permute-start(bf16[2,3,96,384]{3,2,1,0:T(8,128)(2,1)} %after.17.refs_2_), channel_id=1, source_target_pairs={{0,1},{1,0},{2,3},{3,2},{4,5},{5,4},{6,7},{7,6},{8,9},{9,8},{10,11... | collective-permute-start | bytes 1327112 | tf_op jit(solution)/shard_map/ppermute | solution.py:29
  230.1 2.0 collective-permute-start.26
  230.9 1.2 copy-start.23
  239.7 1.0 copy-start.17
  (5 other events, 4.1 us)

commit v12 on v11

--- a/solution.py
+++ b/solution.py
@@ -465,11 +465,12 @@
     packed = (coarse + 2 * HALO) // CHUNKS
     half = coarse // 2
 
+    last_taps = weights[SPLIT:]
+    across = [last_taps] + [from_peer(last_taps, "seq", d) for d in range(1, seqs)]
     to_beside, to_below, own_window = messages(place, inputs, trunk_grad)
+    to_beside, to_below = after(to_beside, *across[1:]), after(to_below, *across[1:])
     beside, below = from_peer(to_beside, "seq", 1), from_peer(to_below, "seq", 2)
     slope = half_slope(inputs)
-    last_taps = weights[SPLIT:]
-    across = [last_taps] + [from_peer(last_taps, "seq", d) for d in range(1, seqs)]
     column = stack_planes(place, gather_line(weights[:SPLIT], "rep", planes, 2))
     lines = stack_planes(place, gather_line(jnp.stack(across), "rep", planes, 2))
     trunk = trunk_grad[0]
@@ -481,14 +482,16 @@
     bottom = after(below[half : coarse + packed - FIRST], slope, column, lines, shifts)
     far_top, far_bottom = from_peer(top, "seq", 2), from_peer(bottom, "seq", 1)
 
-    other_column, other_lines = from_peer(column, "rep", 1), from_peer(lines, "rep", 1)
-    column = after(column, far_top, far_bottom)
-    kept_beside, kept_below = from_peer(column, "seq", 1), from_peer(column, "seq", 2)
-
     scale = 0.5 * float(fine * seqs * reps) ** (-0.5)
     near_rows = [(0, 0, coarse, FIRST), (1, 0, coarse, FIRST), (2, 0, coarse, 0)]
     far_rows = [(3, 0, half, FIRST), (3, half, half, 0)]
     early = early_terms(place, near_rows, [to_beside, beside, below], shifts, coarse)
+    far_top, far_bottom = after(far_top, early), after(far_bottom, early)
+
+    other_column, other_lines = from_peer(column, "rep", 1), from_peer(lines, "rep", 1)
+    column = after(column, far_top, far_bottom)
+    kept_beside, kept_below = from_peer(column, "seq", 1), from_peer(column, "seq", 2)
+
     mine, theirs = late_terms(
         place, far_rows, [far_top, far_bottom], shifts, early, coarse, scale, planes, taps, rows
     )

time: 244 us -> 197 us (0.81)
  the two profiles are of different devices: /device:TPU:9 before, /device:TPU:0 now
where the time goes in v12:
time: 197 us
  waiting for transfers between devices  60.5 us (31%)
  Pallas kernels  57.1 us (29%)
  starting transfers between devices  38.6 us (20%)
  local copies, waits for them, and re-layouts  31.4 us (16%)
  other arithmetic  8.48 us (4%)
    ppermute x27, waiting for transfers between devices, from_peer(): return lax.ppermute(value, axis, [(i, i ^ distance) for i in range(peers)])  60.5 us
    ppermute x27, starting transfers between devices, from_peer(): return lax.ppermute(value, axis, [(i, i ^ distance) for i in range(peers)])  38.6 us
    pallas_call x3, Pallas kernels, gradient_stage(): pl.pallas_call(body, out_shape=out_shape, grid_spec=pltpu.PrefetchScalarG...  26.6 us
    unnamed x68, local copies, waits for them, and re-layouts  23 us
    pallas_call x1, Pallas kernels, early_terms(): pl.pallas_call(kernel, out_shape=jax.ShapeDtypeStruct((both, columns), jn...  13.4 us
    pallas_call x1, Pallas kernels, late_terms(): pl.pallas_call(kernel, out_shape=(jax.ShapeDtypeStruct(shape, jnp.float32...  10.6 us
  transfers between devices with their start and end apart: 27, of which 9 were waited for; matrix products, arithmetic and copies ran while one was open for 7% of the time, Pallas kernels for 26%

profile of v12, /device:TPU:0, one launch (start us, length us, event | category | flops | bytes accessed | tf_op | source)
XLA Modules:
  0.0 197.0 jit_solution(17991203227882435811)
XLA Ops:
  0.6 0.9 slice_bitcast_fusion.2
  1.6 4.0 %collective-permute-start.2 = (bf16[2,96,384]{2,1,0:T(8,128)(2,1)S(1)}, bf16[2,96,384]{2,1,0:T(8,128)(2,1)S(1)}, u32[]{:S(2)}, u32[]{:S(2)}) collective-permute-start(bf16[2,96,384]{2,1,0:T(8,128)(2,1)S(1)} %get-tuple-element.18), channel_id=1, source_target_pairs={{0,24},{8,16},{16,8},{24,0},{1,25},{9,17},{17,9},{25,1},{2,26},{10... | collective-permute-start | bytes 442376 | tf_op jit(solution)/shard_map/ppermute | solution.py:29
  6.3 1.4 copy-done.7
  7.7 1.4 copy-done.11
  9.1 2.8 %messages.1 = (bf16[736,1536]{1,0:T(8,128)(2,1)S(1)}, bf16[720,1536]{1,0:T(8,128)(2,1)S(1)}, bf16[144,1536]{1,0:T(8,128)(2,1)S(1)}) custom-call(s32[2]{0:T(128)S(1)} %pad_add_fusion.place, bf16[1,1024,768]{2,1,0:T(8,128)(2,1)S(1)} %copy-done.11, bf16[1,2048,384]{2,1,0:T(8,128)(2,1)S(1)} %copy-done.7), custom_call_target="tpu_custom_call" | custom-call | tf_op jit(solution)/shard_map/messages/pallas_call | solution.py:105
  11.8 1.4 copy-done.9
  13.2 1.4 copy-done.13
  14.6 0.8 copy-done.14
  16.1 1.9 collective-permute-start.3
  18.1 1.6 collective-permute-start.11
  19.8 3.7 %collective-permute-start.8 = (bf16[4,2,96,384]{3,2,1,0:T(8,128)(2,1)S(1)}, bf16[4,2,96,384]{3,2,1,0:T(8,128)(2,1)S(1)}, u32[]{:S(2)}, u32[]{:S(2)}) collective-permute-start(bf16[4,2,96,384]{3,2,1,0:T(8,128)(2,1)S(1)} %pad_maximum_fusion.refs_0_), channel_id=1, source_target_pairs={{0,6},{1,7},{2,4},{3,5},{4,2},{5,3},{6,0},{7,1},{8,14},{9,15},{10,... | collective-permute-start | bytes 1769480 | tf_op jit(solution)/shard_map/ppermute | solution.py:29
  24.3 18.3 %collective-permute-done.5.refs_3_ = bf16[3,96,384]{2,1,0:T(8,128)(2,1)S(1)} collective-permute-done((bf16[3,96,384]{2,1,0:T(8,128)(2,1)S(1)}, bf16[3,96,384]{2,1,0:T(8,128)(2,1)S(1)}, u32[]{:S(2)}, u32[]{:S(2)}) %collective-permute-start.5) | collective-permute-done | bytes 221216 | tf_op jit(solution)/shard_map/ppermute | solution.py:29
  42.6 14.6 %collective-permute-start.7 = (bf16[4,2,96,384]{3,2,1,0:T(8,128)(2,1)S(1)}, bf16[4,2,96,384]{3,2,1,0:T(8,128)(2,1)S(1)}, u32[]{:S(2)}, u32[]{:S(2)}) collective-permute-start(bf16[4,2,96,384]{3,2,1,0:T(8,128)(2,1)S(1)} %pad_maximum_fusion.refs_0_), channel_id=1, source_target_pairs={{0,2},{1,3},{2,0},{3,1},{4,6},{5,7},{6,4},{7,5},{8,10},{9,11},{10,... | collective-permute-start | bytes 1769480 | tf_op jit(solution)/shard_map/ppermute | solution.py:29
  57.2 2.0 %collective-permute-start.9 = (bf16[4,2,96,384]{3,2,1,0:T(8,128)(2,1)S(1)}, bf16[4,2,96,384]{3,2,1,0:T(8,128)(2,1)S(1)}, u32[]{:S(2)}, u32[]{:S(2)}) collective-permute-start(bf16[4,2,96,384]{3,2,1,0:T(8,128)(2,1)S(1)} %collective-permute-done.8.refs_3_), channel_id=1, source_target_pairs={{0,2},{1,3},{2,0},{3,1},{4,6},{5,7},{6,4},{7,5},{8,10},{9,11},{10,... | collective-permute-start | bytes 1769480 | tf_op jit(solution)/shard_map/ppermute | solution.py:29
  59.2 3.0 %fusion.2.refs_4_.shifts_ref = bf16[2048,1152]{1,0:T(8,128)(2,1)} fusion(bf16[2047,384]{1,0:T(8,128)(2,1)S(1)} %get-tuple-element.16, bf16[2047,384]{1,0:T(8,128)(2,1)S(1)} %get-tuple-element.15, bf16[2048,384]{1,0:T(8,128)(2,1)S(1)} %bitcast.24), kind=kLoop, calls=%fused_computation.4 | loop fusion | flops 23592960 | bytes 9435648 | tf_op jit(solution)/shard_map/concatenate | solution.py:480
  62.2 2.4 %half_slope.1.refs_1_.refs_13_.refs_9_.refs_6_ = f32[2,512,768]{2,1,0:T(8,128)S(1)} custom-call(bf16[1,1024,768]{2,1,0:T(8,128)(2,1)S(1)} %copy-done.12), custom_call_target="tpu_custom_call" | custom-call | tf_op jit(solution)/shard_map/half_slope/pallas_call | solution.py:140
  64.6 1.6 copy-done.2
  66.2 10.0 %collective-permute-done.6.refs_2_ = bf16[3,96,384]{2,1,0:T(8,128)(2,1)S(1)} collective-permute-done((bf16[3,96,384]{2,1,0:T(8,128)(2,1)S(1)}, bf16[3,96,384]{2,1,0:T(8,128)(2,1)S(1)}, u32[]{:S(2)}, u32[]{:S(2)}) %collective-permute-start.6) | collective-permute-done | bytes 221216 | tf_op jit(solution)/shard_map/ppermute | solution.py:29
  76.8 0.9 copy-done.3
  77.8 9.5 %collective-permute-done.9.refs_2_ = bf16[4,2,96,384]{3,2,1,0:T(8,128)(2,1)S(1)} collective-permute-done((bf16[4,2,96,384]{3,2,1,0:T(8,128)(2,1)S(1)}, bf16[4,2,96,384]{3,2,1,0:T(8,128)(2,1)S(1)}, u32[]{:S(2)}, u32[]{:S(2)}) %collective-permute-start.9) | collective-permute-done | bytes 589856 | tf_op jit(solution)/shard_map/ppermute | solution.py:29
  88.0 1.4 copy-done
  89.4 2.2 %slice.72.refs_0_ = bf16[336,1536]{1,0:T(8,128)(2,1)} slice(bf16[736,1536]{1,0:T(8,128)(2,1)} %collective-permute-done.3.refs_1_), slice={[0:336], [0:1536]} | slice | bytes 2064384 | tf_op jit(solution)/shard_map/slice | solution.py:481
  91.7 1.2 collective-permute-start.10
  92.9 1.0 slice.73.refs_0_
  93.9 1.4 copy-done.5
  97.2 1.6 copy-done.6
  98.9 1.6 copy-done.10
  100.5 13.4 %weight_grad_early.1.refs_1_.early_ref = f32[1536,1152]{1,0:T(8,128)} custom-call(s32[2]{0:T(128)S(1)} %pad_add_fusion.place, bf16[2048,1152]{1,0:T(8,128)(2,1)} %fusion.2.refs_4_.shifts_ref, bf16[736,1536]{1,0:T(8,128)(2,1)S(1)} %copy-done.10, bf16[736,1536]{1,0:T(8,128)(2,1)} %collective-permute-done.3.refs_1_, bf16[720,1536]{1,0:T(8,128)(2,1)S(1)} %copy-done.6), custom_call_target="tpu_custom_call" | custom-call | flops 1048576 | bytes 65536 | tf_op jit(solution)/shard_map/weight_grad_early/pallas_call | solution.py:188
  113.9 3.7 %collective-permute-done.12.refs_0_ = bf16[320,1536]{1,0:T(8,128)(2,1)} collective-permute-done((bf16[320,1536]{1,0:T(8,128)(2,1)}, bf16[320,1536]{1,0:T(8,128)(2,1)}, u32[]{:S(2)}, u32[]{:S(2)}) %collective-permute-start.12) | collective-permute-done | bytes 983072 | tf_op jit(solution)/shard_map/ppermute | solution.py:29
  117.6 0.9 collective-permute-start.18
  119.0 10.6 %weight_grad_late.1 = (f32[4,5,96,384]{3,2,1,0:T(8,128)}, bf16[4,5,96,384]{3,2,1,0:T(8,128)(2,1)}) custom-call(s32[2]{0:T(128)S(1)} %pad_add_fusion.place, bf16[2048,1152]{1,0:T(8,128)(2,1)} %fusion.2.refs_4_.shifts_ref, f32[1536,1152]{1,0:T(8,128)} %weight_grad_early.1.refs_1_.early_ref, bf16[336,1536]{1,0:T(8,128)(2,1)} %after.18.refs_1_.refs_0_.refs_3_, ...), custom_call_target="tpu_custom_call" | custom-call | flops 1048576 | bytes 65536 | tf_op jit(solution)/shard_map/weight_grad_late/pallas_call | solution.py:258
  129.7 7.2 %collective-permute-done.18.refs_0_ = bf16[4,3,96,384]{3,2,1,0:T(8,128)(2,1)} collective-permute-done((bf16[4,3,96,384]{3,2,1,0:T(8,128)(2,1)}, bf16[4,3,96,384]{3,2,1,0:T(8,128)(2,1)}, u32[]{:S(2)}, u32[]{:S(2)}) %collective-permute-start.18) | collective-permute-done | bytes 884768 | tf_op jit(solution)/shard_map/ppermute | solution.py:29
  137.3 0.9 copy-done.21
  138.3 1.8 slice.78
  140.1 1.8 slice.74
  142.5 1.1 collective-permute-start.14
  143.6 3.0 %fusion.8 = (bf16[5,96,384]{2,1,0:T(8,128)(2,1)}, bf16[5,96,384]{2,1,0:T(8,128)(2,1)}, bf16[5,96,384]{2,1,0:T(8,128)(2,1)}) fusion(f32[4,5,96,384]{3,2,1,0:T(8,128)} %get-tuple-element.10, bf16[4,5,96,384]{3,2,1,0:T(8,128)(2,1)} %collective-permute-done.15), kind=kLoop, calls=%fused_computation.17 | loop fusion | flops 1658880 | bytes 4423680 | tf_op jit(solution)/shard_map/convert_element_type | solution.py:500
  146.6 0.9 collective-permute-start.23
  147.5 1.8 collective-permute-start.22
  149.3 0.9 copy-done.30
  150.2 1.7 collective-permute-start.21
  151.9 9.9 %input_grad.3.refs_10_ = f32[2,512,768]{2,1,0:T(8,128)} custom-call(s32[2]{0:T(128)} %copy-done.15, bf16[144,1536]{1,0:T(8,128)(2,1)} %copy-done.14, bf16[736,1536]{1,0:T(8,128)(2,1)} %collective-permute-done.3.refs_1_, bf16[720,1536]{1,0:T(8,128)(2,1)} %copy-done.5, bf16[336,1536]{1,0:T(8,128)(2,1)} %after.18.refs_1_.refs_0_.refs_3_, ...), custom_call_target="tpu_custom_call" | custom-call | flops 1048576 | bytes 65536 | tf_op jit(solution)/shard_map/input_grad/pallas_call | solution.py:418
  161.8 10.0 %input_grad.4.refs_1_.refs_7_ = f32[2,512,768]{2,1,0:T(8,128)} custom-call(s32[2]{0:T(128)} %copy-done.15, bf16[144,1536]{1,0:T(8,128)(2,1)} %copy-done.14, bf16[736,1536]{1,0:T(8,128)(2,1)} %collective-permute-done.3.refs_1_, bf16[720,1536]{1,0:T(8,128)(2,1)} %copy-done.5, bf16[4,3,96,384]{3,2,1,0:T(8,128)(2,1)} %after.23.refs_3_, ...), custom_call_target="tpu_custom_call" | custom-call | flops 1048576 | bytes 65536 | tf_op jit(solution)/shard_map/input_grad/pallas_call | solution.py:418
  171.8 9.8 %collective-permute-done.22.refs_3_.refs_0_ = bf16[5,96,384]{2,1,0:T(8,128)(2,1)S(1)} collective-permute-done((bf16[5,96,384]{2,1,0:T(8,128)(2,1)}, bf16[5,96,384]{2,1,0:T(8,128)(2,1)S(1)}, u32[]{:S(2)}, u32[]{:S(2)}) %collective-permute-start.22) | collective-permute-done | bytes 368672 | tf_op jit(solution)/shard_map/ppermute | solution.py:29
  185.1 0.9 collective-permute-done.26.refs_5_
  186.8 6.7 %input_grad.5.refs_1_ = bf16[1,1024,768]{2,1,0:T(8,128)(2,1)} custom-call(s32[2]{0:T(128)} %copy-done.15, bf16[336,1536]{1,0:T(8,128)(2,1)} %after.18.refs_1_.refs_0_.refs_3_, bf16[320,1536]{1,0:T(8,128)(2,1)} %after.20.refs_2_.refs_1_.refs_4_, bf16[2,3,96,384]{3,2,1,0:T(8,128)(2,1)} %after.25.refs_2_, bf16[2,3,96,384]{3,2,1,0:T(8,128)(2,1)} %copy-done.31, ...), custom_call_target="tpu_custom_call" | custom-call | flops 1048576 | bytes 65536 | tf_op jit(solution)/shard_map/input_grad/pallas_call | solution.py:418
  193.5 0.9 copy-done.17
  194.6 2.4 %fusion.5 = f32[5,96,384]{2,1,0:T(8,128)} fusion(bf16[5,96,384]{2,1,0:T(8,128)(2,1)S(1)} %copy-done.17, bf16[5,96,384]{2,1,0:T(8,128)(2,1)S(1)} %copy-done.19, bf16[5,96,384]{2,1,0:T(8,128)(2,1)} %after.27, f32[4,5,96,384]{3,2,1,0:T(8,128)} %get-tuple-element.10, bf16[4,5,96,384]{3,2,1,0:T(8,128)(2,1)} %collective-permute-done.15), kind=kLoop, calls=%fused_computation.10 | loop fusion | flops 1474560 | bytes 2949120 | tf_op jit(solution)/shard_map/add | solution.py:525
  (110 shorter events, 11.9 us)
Async XLA Ops:
  1.6 13.8 %collective-permute-start.2 = (bf16[2,96,384]{2,1,0:T(8,128)(2,1)S(1)}, bf16[2,96,384]{2,1,0:T(8,128)(2,1)S(1)}, u32[]{:S(2)}, u32[]{:S(2)}) collective-permute-start(bf16[2,96,384]{2,1,0:T(8,128)(2,1)S(1)} %get-tuple-element.18), channel_id=1, source_target_pairs={{0,24},{8,16},{16,8},{24,0},{1,25},{9,17},{17,9},{25,1},{2,26},{10... | collective-permute-start | bytes 442376 | tf_op jit(solution)/shard_map/ppermute | solution.py:29
  5.5 9.9 %collective-permute-start.1 = (bf16[2,96,384]{2,1,0:T(8,128)(2,1)S(1)}, bf16[2,96,384]{2,1,0:T(8,128)(2,1)S(1)}, u32[]{:S(2)}, u32[]{:S(2)}) collective-permute-start(bf16[2,96,384]{2,1,0:T(8,128)(2,1)S(1)} %get-tuple-element.18), channel_id=1, source_target_pairs={{0,16},{8,24},{16,0},{24,8},{1,17},{9,25},{17,1},{25,9},{2,18},{10... | collective-permute-start | bytes 442376 | tf_op jit(solution)/shard_map/ppermute | solution.py:29
  6.0 9.4 %collective-permute-start = (bf16[2,96,384]{2,1,0:T(8,128)(2,1)S(1)}, bf16[2,96,384]{2,1,0:T(8,128)(2,1)S(1)}, u32[]{:S(2)}, u32[]{:S(2)}) collective-permute-start(bf16[2,96,384]{2,1,0:T(8,128)(2,1)S(1)} %get-tuple-element.18), channel_id=1, source_target_pairs={{0,8},{8,0},{16,24},{24,16},{1,9},{9,1},{17,25},{25,17},{2,10},{10... | collective-permute-start | bytes 442376 | tf_op jit(solution)/shard_map/ppermute | solution.py:29
  6.2 1.4 copy-start.7
  7.7 1.4 copy-start.11
  9.1 109.9 %copy-start.15 = (s32[2]{0:T(128)}, s32[2]{0:T(128)S(1)}, u32[]{:S(2)}) copy-start(s32[2]{0:T(128)S(1)} %pad_add_fusion.place) | copy-start | bytes 28
  11.8 1.4 copy-start.9
  13.2 1.4 copy-start.13
  16.1 73.3 %collective-permute-start.3 = (bf16[736,1536]{1,0:T(8,128)(2,1)}, bf16[736,1536]{1,0:T(8,128)(2,1)}, u32[]{:S(2)}, u32[]{:S(2)}) collective-permute-start(bf16[736,1536]{1,0:T(8,128)(2,1)} %after.15.refs_0_), channel_id=1, source_target_pairs={{0,8},{8,0},{16,24},{24,16},{1,9},{9,1},{17,25},{25,17},{2,10},{10... | collective-permute-start | bytes 6782984 | tf_op jit(solution)/shard_map/ppermute | solution.py:29
  18.0 1.6 copy-start.25
  18.0 1.6 copy-start.27
  18.0 1.6 copy-start.29
  18.0 5.4 %copy-start.33 = (bf16[5,96,384]{2,1,0:T(8,128)(2,1)S(1)}, bf16[5,96,384]{2,1,0:T(8,128)(2,1)}, u32[]{:S(2)}) copy-start(bf16[5,96,384]{2,1,0:T(8,128)(2,1)} %param.5) | copy-start | bytes 1105924
  18.1 5.7 %copy-start.8 = (bf16[1,2048,384]{2,1,0:T(8,128)(2,1)S(1)}, bf16[1,2048,384]{2,1,0:T(8,128)(2,1)}, u32[]{:S(2)}) copy-start(bf16[1,2048,384]{2,1,0:T(8,128)(2,1)} %trunk_ref.1) | copy-start | bytes 4718596
  18.1 74.8 %collective-permute-start.11 = (bf16[720,1536]{1,0:T(8,128)(2,1)}, bf16[720,1536]{1,0:T(8,128)(2,1)S(1)}, u32[]{:S(2)}, u32[]{:S(2)}) collective-permute-start(bf16[720,1536]{1,0:T(8,128)(2,1)} %after.17), channel_id=1, source_target_pairs={{0,16},{8,24},{16,0},{24,8},{1,17},{9,25},{17,1},{25,9},{2,18},{10... | collective-permute-start | bytes 6635528 | tf_op jit(solution)/shard_map/ppermute | solution.py:29
  19.8 37.5 %collective-permute-start.8 = (bf16[4,2,96,384]{3,2,1,0:T(8,128)(2,1)S(1)}, bf16[4,2,96,384]{3,2,1,0:T(8,128)(2,1)S(1)}, u32[]{:S(2)}, u32[]{:S(2)}) collective-permute-start(bf16[4,2,96,384]{3,2,1,0:T(8,128)(2,1)S(1)} %pad_maximum_fusion.refs_0_), channel_id=1, source_target_pairs={{0,6},{1,7},{2,4},{3,5},{4,2},{5,3},{6,0},{7,1},{8,14},{9,15},{10,... | collective-permute-start | bytes 1769480 | tf_op jit(solution)/shard_map/ppermute | solution.py:29
  23.5 19.1 %collective-permute-start.5 = (bf16[3,96,384]{2,1,0:T(8,128)(2,1)S(1)}, bf16[3,96,384]{2,1,0:T(8,128)(2,1)S(1)}, u32[]{:S(2)}, u32[]{:S(2)}) collective-permute-start(bf16[3,96,384]{2,1,0:T(8,128)(2,1)S(1)} %slice.56.refs_0_), channel_id=1, source_target_pairs={{0,6},{1,7},{2,4},{3,5},{4,2},{5,3},{6,0},{7,1},{8,14},{9,15},{10,... | collective-permute-start | bytes 663560 | tf_op jit(solution)/shard_map/ppermute | solution.py:29
  23.7 33.4 %collective-permute-start.4 = (bf16[3,96,384]{2,1,0:T(8,128)(2,1)S(1)}, bf16[3,96,384]{2,1,0:T(8,128)(2,1)S(1)}, u32[]{:S(2)}, u32[]{:S(2)}) collective-permute-start(bf16[3,96,384]{2,1,0:T(8,128)(2,1)S(1)} %slice.56.refs_0_), channel_id=1, source_target_pairs={{0,2},{1,3},{2,0},{3,1},{4,6},{5,7},{6,4},{7,5},{8,10},{9,11},{10,... | collective-permute-start | bytes 663560 | tf_op jit(solution)/shard_map/ppermute | solution.py:29
  42.6 35.2 %collective-permute-start.7 = (bf16[4,2,96,384]{3,2,1,0:T(8,128)(2,1)S(1)}, bf16[4,2,96,384]{3,2,1,0:T(8,128)(2,1)S(1)}, u32[]{:S(2)}, u32[]{:S(2)}) collective-permute-start(bf16[4,2,96,384]{3,2,1,0:T(8,128)(2,1)S(1)} %pad_maximum_fusion.refs_0_), channel_id=1, source_target_pairs={{0,2},{1,3},{2,0},{3,1},{4,6},{5,7},{6,4},{7,5},{8,10},{9,11},{10,... | collective-permute-start | bytes 1769480 | tf_op jit(solution)/shard_map/ppermute | solution.py:29
  57.2 19.0 %collective-permute-start.6 = (bf16[3,96,384]{2,1,0:T(8,128)(2,1)S(1)}, bf16[3,96,384]{2,1,0:T(8,128)(2,1)S(1)}, u32[]{:S(2)}, u32[]{:S(2)}) collective-permute-start(bf16[3,96,384]{2,1,0:T(8,128)(2,1)S(1)} %collective-permute-done.5.refs_3_), channel_id=1, source_target_pairs={{0,2},{1,3},{2,0},{3,1},{4,6},{5,7},{6,4},{7,5},{8,10},{9,11},{10,... | collective-permute-start | bytes 663560 | tf_op jit(solution)/shard_map/ppermute | solution.py:29
  57.2 30.0 %collective-permute-start.9 = (bf16[4,2,96,384]{3,2,1,0:T(8,128)(2,1)S(1)}, bf16[4,2,96,384]{3,2,1,0:T(8,128)(2,1)S(1)}, u32[]{:S(2)}, u32[]{:S(2)}) collective-permute-start(bf16[4,2,96,384]{3,2,1,0:T(8,128)(2,1)S(1)} %collective-permute-done.8.refs_3_), channel_id=1, source_target_pairs={{0,2},{1,3},{2,0},{3,1},{4,6},{5,7},{6,4},{7,5},{8,10},{9,11},{10,... | collective-permute-start | bytes 1769480 | tf_op jit(solution)/shard_map/ppermute | solution.py:29
  59.2 3.0 %copy-start.12 = (bf16[1,1024,768]{2,1,0:T(8,128)(2,1)S(1)}, bf16[1,1024,768]{2,1,0:T(8,128)(2,1)}, u32[]{:S(2)}) copy-start(bf16[1,1024,768]{2,1,0:T(8,128)(2,1)} %x_ref.3) | copy-start | bytes 4718596
  64.6 1.7 copy-start.2
  88.0 1.4 copy-start
  91.7 25.9 %collective-permute-start.10 = (bf16[336,1536]{1,0:T(8,128)(2,1)}, bf16[336,1536]{1,0:T(8,128)(2,1)}, u32[]{:S(2)}, u32[]{:S(2)}) collective-permute-start(bf16[336,1536]{1,0:T(8,128)(2,1)} %after.16), channel_id=1, source_target_pairs={{0,16},{8,24},{16,0},{24,8},{1,17},{9,25},{17,1},{25,9},{2,18},{10... | collective-permute-start | bytes 3096584 | tf_op jit(solution)/shard_map/ppermute | solution.py:29
  93.9 1.4 copy-start.5
  95.3 1.2 copy-start.4
  95.3 1.9 copy-start.1
  95.3 22.3 %collective-permute-start.12 = (bf16[320,1536]{1,0:T(8,128)(2,1)}, bf16[320,1536]{1,0:T(8,128)(2,1)}, u32[]{:S(2)}, u32[]{:S(2)}) collective-permute-start(bf16[320,1536]{1,0:T(8,128)(2,1)} %after.19), channel_id=1, source_target_pairs={{0,8},{8,0},{16,24},{24,16},{1,9},{9,1},{17,25},{25,17},{2,10},{10... | collective-permute-start | bytes 2949128 | tf_op jit(solution)/shard_map/ppermute | solution.py:29
  96.5 21.1 %collective-permute-start.16 = (bf16[4,3,96,384]{3,2,1,0:T(8,128)(2,1)S(1)}, bf16[4,3,96,384]{3,2,1,0:T(8,128)(2,1)}, u32[]{:S(2)}, u32[]{:S(2)}) collective-permute-start(bf16[4,3,96,384]{3,2,1,0:T(8,128)(2,1)S(1)} %copy-done.4), channel_id=1, source_target_pairs={{0,1},{1,0},{2,3},{3,2},{4,5},{5,4},{6,7},{7,6},{8,9},{9,8},{10,11... | collective-permute-start | bytes 2654216 | tf_op jit(solution)/shard_map/ppermute | solution.py:29
  97.2 49.3 %collective-permute-start.20 = (bf16[4,4,2,96,384]{4,3,2,1,0:T(8,128)(2,1)S(1)}, bf16[4,4,2,96,384]{4,3,2,1,0:T(8,128)(2,1)}, u32[]{:S(2)}, u32[]{:S(2)}) collective-permute-start(bf16[4,4,2,96,384]{4,3,2,1,0:T(8,128)(2,1)S(1)} %copy-done.1), channel_id=1, source_target_pairs={{0,1},{1,0},{2,3},{3,2},{4,5},{5,4},{6,7},{7,6},{8,9},{9,8},{10,11... | collective-permute-start | bytes 7077896 | tf_op jit(solution)/shard_map/ppermute | solution.py:29
  97.2 1.6 copy-start.6
  98.9 1.6 copy-start.10
  117.6 19.3 %collective-permute-start.18 = (bf16[4,3,96,384]{3,2,1,0:T(8,128)(2,1)}, bf16[4,3,96,384]{3,2,1,0:T(8,128)(2,1)}, u32[]{:S(2)}, u32[]{:S(2)}) collective-permute-start(bf16[4,3,96,384]{3,2,1,0:T(8,128)(2,1)} %after.21.refs_0_), channel_id=1, source_target_pairs={{0,16},{8,24},{16,0},{24,8},{1,17},{9,25},{17,1},{25,9},{2,18},{10... | collective-permute-start | bytes 2654216 | tf_op jit(solution)/shard_map/ppermute | solution.py:29
  118.4 18.8 %collective-permute-start.13 = (bf16[4,3,96,384]{3,2,1,0:T(8,128)(2,1)}, bf16[4,3,96,384]{3,2,1,0:T(8,128)(2,1)S(1)}, u32[]{:S(2)}, u32[]{:S(2)}) collective-permute-start(bf16[4,3,96,384]{3,2,1,0:T(8,128)(2,1)} %after.21.refs_0_), channel_id=1, source_target_pairs={{0,8},{8,0},{16,24},{24,16},{1,9},{9,1},{17,25},{25,17},{2,10},{10... | collective-permute-start | bytes 2654216 | tf_op jit(solution)/shard_map/ppermute | solution.py:29
  129.6 12.8 %collective-permute-start.15 = (bf16[4,5,96,384]{3,2,1,0:T(8,128)(2,1)}, bf16[4,5,96,384]{3,2,1,0:T(8,128)(2,1)}, u32[]{:S(2)}, u32[]{:S(2)}) collective-permute-start(bf16[4,5,96,384]{3,2,1,0:T(8,128)(2,1)} %get-tuple-element.11), channel_id=1, source_target_pairs={{0,1},{1,0},{2,3},{3,2},{4,5},{5,4},{6,7},{7,6},{8,9},{9,8},{10,11... | collective-permute-start | bytes 4423688 | tf_op jit(solution)/shard_map/ppermute | solution.py:29
  136.9 10.6 %collective-permute-start.19 = (bf16[4,3,96,384]{3,2,1,0:T(8,128)(2,1)}, bf16[4,3,96,384]{3,2,1,0:T(8,128)(2,1)}, u32[]{:S(2)}, u32[]{:S(2)}) collective-permute-start(bf16[4,3,96,384]{3,2,1,0:T(8,128)(2,1)} %after.24.refs_7_), channel_id=1, source_target_pairs={{0,1},{1,0},{2,3},{3,2},{4,5},{5,4},{6,7},{7,6},{8,9},{9,8},{10,11... | collective-permute-start | bytes 2654216 | tf_op jit(solution)/shard_map/ppermute | solution.py:29
  138.2 11.1 %collective-permute-start.17 = (bf16[4,3,96,384]{3,2,1,0:T(8,128)(2,1)}, bf16[4,3,96,384]{3,2,1,0:T(8,128)(2,1)S(1)}, u32[]{:S(2)}, u32[]{:S(2)}) collective-permute-start(bf16[4,3,96,384]{3,2,1,0:T(8,128)(2,1)} %after.22.refs_5_), channel_id=1, source_target_pairs={{0,1},{1,0},{2,3},{3,2},{4,5},{5,4},{6,7},{7,6},{8,9},{9,8},{10,11... | collective-permute-start | bytes 2654216 | tf_op jit(solution)/shard_map/ppermute | solution.py:29
  141.9 41.2 %collective-permute-start.25 = (bf16[2,3,96,384]{3,2,1,0:T(8,128)(2,1)}, bf16[2,3,96,384]{3,2,1,0:T(8,128)(2,1)S(1)}, u32[]{:S(2)}, u32[]{:S(2)}) collective-permute-start(bf16[2,3,96,384]{3,2,1,0:T(8,128)(2,1)} %slice.78), channel_id=1, source_target_pairs={{0,8},{8,0},{16,24},{24,16},{1,9},{9,1},{17,25},{25,17},{2,10},{10... | collective-permute-start | bytes 1327112 | tf_op jit(solution)/shard_map/ppermute | solution.py:29
  142.5 29.3 %collective-permute-start.14 = (bf16[2,3,96,384]{3,2,1,0:T(8,128)(2,1)}, bf16[2,3,96,384]{3,2,1,0:T(8,128)(2,1)S(1)}, u32[]{:S(2)}, u32[]{:S(2)}) collective-permute-start(bf16[2,3,96,384]{3,2,1,0:T(8,128)(2,1)} %slice.74), channel_id=1, source_target_pairs={{0,16},{8,24},{16,0},{24,8},{1,17},{9,25},{17,1},{25,9},{2,18},{10... | collective-permute-start | bytes 1327112 | tf_op jit(solution)/shard_map/ppermute | solution.py:29
  146.6 25.2 %collective-permute-start.23 = (bf16[5,96,384]{2,1,0:T(8,128)(2,1)}, bf16[5,96,384]{2,1,0:T(8,128)(2,1)S(1)}, u32[]{:S(2)}, u32[]{:S(2)}) collective-permute-start(bf16[5,96,384]{2,1,0:T(8,128)(2,1)} %get-tuple-element.12.refs_3_), channel_id=1, source_target_pairs={{0,6},{1,7},{2,4},{3,5},{4,2},{5,3},{6,0},{7,1},{8,14},{9,15},{10,... | collective-permute-start | bytes 1105928 | tf_op jit(solution)/shard_map/ppermute | solution.py:29
  147.5 34.1 %collective-permute-start.22 = (bf16[5,96,384]{2,1,0:T(8,128)(2,1)}, bf16[5,96,384]{2,1,0:T(8,128)(2,1)S(1)}, u32[]{:S(2)}, u32[]{:S(2)}) collective-permute-start(bf16[5,96,384]{2,1,0:T(8,128)(2,1)} %get-tuple-element.13.refs_2_), channel_id=1, source_target_pairs={{0,4},{1,5},{2,6},{3,7},{4,0},{5,1},{6,2},{7,3},{8,12},{9,13},{10,... | collective-permute-start | bytes 1105928 | tf_op jit(solution)/shard_map/ppermute | solution.py:29
  150.2 31.4 %collective-permute-start.21 = (bf16[5,96,384]{2,1,0:T(8,128)(2,1)}, bf16[5,96,384]{2,1,0:T(8,128)(2,1)S(1)}, u32[]{:S(2)}, u32[]{:S(2)}) collective-permute-start(bf16[5,96,384]{2,1,0:T(8,128)(2,1)} %get-tuple-element.14.refs_1_), channel_id=1, source_target_pairs={{0,2},{1,3},{2,0},{3,1},{4,6},{5,7},{6,4},{7,5},{8,10},{9,11},{10,... | collective-permute-start | bytes 1105928 | tf_op jit(solution)/shard_map/ppermute | solution.py:29
  171.8 9.8 %copy-start.23 = (bf16[2,3,96,384]{3,2,1,0:T(8,128)(2,1)}, bf16[2,3,96,384]{3,2,1,0:T(8,128)(2,1)S(1)}, u32[]{:S(2)}) copy-start(bf16[2,3,96,384]{3,2,1,0:T(8,128)(2,1)S(1)} %collective-permute-done.14.refs_0_) | copy-start | bytes 1327108
  171.8 9.8 %copy-start.16 = (bf16[5,96,384]{2,1,0:T(8,128)(2,1)}, bf16[5,96,384]{2,1,0:T(8,128)(2,1)S(1)}, u32[]{:S(2)}) copy-start(bf16[5,96,384]{2,1,0:T(8,128)(2,1)S(1)} %collective-permute-done.23.refs_4_.refs_0_) | copy-start | bytes 1105924
  183.1 2.0 %collective-permute-start.24 = (bf16[2,3,96,384]{3,2,1,0:T(8,128)(2,1)}, bf16[2,3,96,384]{3,2,1,0:T(8,128)(2,1)S(1)}, u32[]{:S(2)}, u32[]{:S(2)}) collective-permute-start(bf16[2,3,96,384]{3,2,1,0:T(8,128)(2,1)} %after.25.refs_2_), channel_id=1, source_target_pairs={{0,1},{1,0},{2,3},{3,2},{4,5},{5,4},{6,7},{7,6},{8,9},{9,8},{10,11... | collective-permute-start | bytes 1327112 | tf_op jit(solution)/shard_map/ppermute | solution.py:29
  183.9 2.1 %collective-permute-start.26 = (bf16[2,3,96,384]{3,2,1,0:T(8,128)(2,1)}, bf16[2,3,96,384]{3,2,1,0:T(8,128)(2,1)S(1)}, u32[]{:S(2)}, u32[]{:S(2)}) collective-permute-start(bf16[2,3,96,384]{3,2,1,0:T(8,128)(2,1)} %after.26.refs_4_), channel_id=1, source_target_pairs={{0,1},{1,0},{2,3},{3,2},{4,5},{5,4},{6,7},{7,6},{8,9},{9,8},{10,11... | collective-permute-start | bytes 1327112 | tf_op jit(solution)/shard_map/ppermute | solution.py:29
  193.5 1.1 copy-start.19
  (13 other events, 10.6 us)

commit v13 on v10

--- a/solution.py
+++ b/solution.py
@@ -10,11 +10,10 @@
 
 LANES = 128
 HALO = 32
-CHUNKS = 4
-FIRST = 80
 EDGE = 16
 MARGIN = HALO - EDGE
 STEP = 64
+SPLIT = 3
 ROOT = math.sqrt(2.0 / math.pi)
 CUBIC = 0.044715
 SMALL = pl.CostEstimate(flops=1 << 20, bytes_accessed=1 << 16, transcendentals=0)
@@ -55,16 +54,10 @@
     )
 
 
-def messages_kernel(place, x_ref, trunk_ref, beside_ref, below_ref, own_ref, edged, strip, sem):
-    coarse, width, block = x_ref.shape[1] // 2, x_ref.shape[2], edged.shape[1]
-    length = trunk_ref.shape[1]
-    packed = (coarse + 2 * HALO) // CHUNKS
-    copy = pltpu.make_async_copy(trunk_ref.at[0], edged.at[pl.ds(HALO, length)], sem)
-    copy.start()
-    edged[:HALO] = jnp.zeros((HALO, block), jnp.bfloat16)
-    edged[HALO + length :] = jnp.zeros((HALO, block), jnp.bfloat16)
-
-    @pl.loop(0, coarse // STEP)
+def act_kernel(x_ref, out_ref, strip):
+    width = x_ref.shape[2]
+
+    @pl.loop(0, out_ref.shape[0] // STEP)
     def _(step):
         start = pl.multiple_of(step * STEP, STEP)
         x = x_ref[0, pl.ds(pl.multiple_of(2 * start, 2 * STEP), 2 * STEP), :].astype(jnp.float32)
@@ -74,50 +67,79 @@
         for parity in range(2):
             for c in range(width // LANES):
                 picked = strip[c, pl.ds(parity, STEP, stride=2), :].astype(jnp.bfloat16)
-                lanes = slice(parity * width + c * LANES, parity * width + (c + 1) * LANES)
-                beside_ref[pl.ds(FIRST + start, STEP), lanes] = picked
-                below_ref[pl.ds(start, STEP), lanes] = picked
-
-    copy.wait()
-
-    def pack(out_ref, row, distance, first, last):
-        base = (place[0] ^ distance) * coarse
-        for q in range(CHUNKS):
-            start = pl.multiple_of(base + q * packed + first, 16)
-            out_ref[row : row + last - first, q * block : (q + 1) * block] = edged[
-                pl.ds(start, last - first), :
-            ]
-
-    pack(beside_ref, 0, 3, 0, FIRST)
-    pack(beside_ref, FIRST + coarse, 1, 0, packed)
-    pack(below_ref, coarse, 3, FIRST, packed)
-    pack(below_ref, coarse + packed - FIRST, 2, 0, packed)
-    pack(own_ref, 0, 0, 0, packed)
-
-
-def messages(place, inputs, trunk_grad):
-    _, fine, width = inputs.shape
-    _, length, block = trunk_grad.shape
-    coarse = fine // 2
-    packed = (coarse + 2 * HALO) // CHUNKS
-    rows = (FIRST + coarse + packed, coarse + packed - FIRST + packed, packed)
-    return pl.pallas_call(
-        messages_kernel,
-        out_shape=[jax.ShapeDtypeStruct((n, 2 * width), jnp.bfloat16) for n in rows],
+                left = parity * width + c * LANES
+                out_ref[pl.ds(start, STEP), left : left + LANES] = picked
+
+
+def activate(inputs):
+    fine, width = inputs.shape[1:]
+    return pl.pallas_call(
+        act_kernel,
+        out_shape=jax.ShapeDtypeStruct((fine // 2, 2 * width), jnp.bfloat16),
+        in_specs=[pl.BlockSpec(memory_space=pltpu.VMEM)],
+        out_specs=pl.BlockSpec(memory_space=pltpu.VMEM),
+        scratch_shapes=[pltpu.VMEM((width // LANES, 2 * STEP, LANES), jnp.float32)],
+        compiler_params=pltpu.CompilerParams(vmem_limit_bytes=24 << 20),
+        cost_estimate=SMALL,
+        name="act",
+    )(inputs)
+
+
+def kernel_messages(place, line, trunk_grad, coarse):
+    taps, rows, block = line[0].shape
+    planes, length = len(line), trunk_grad.shape[1]
+    window = (coarse + 2 * HALO) // rows
+    half = planes // 2
+
+    def kernel(place, *refs):
+        parts, trunk_ref = refs[:planes], refs[planes]
+        beside_ref, below_ref, own_ref, edged, sem = refs[planes + 1 :]
+        copy = pltpu.make_async_copy(trunk_ref.at[0], edged.at[pl.ds(HALO, length)], sem)
+        copy.start()
+        edged[:HALO] = jnp.zeros((HALO, block), jnp.bfloat16)
+        edged[HALO + length :] = jnp.zeros((HALO, block), jnp.bfloat16)
+        for j in range(planes):
+            plane = place[1] // 2 ^ j
+            for k in range(taps):
+                spot = (plane // half * taps + k) * half + plane % half
+                beside_ref[window // 2 + spot] = parts[j][k]
+                below_ref[spot] = parts[j][k]
+        copy.wait()
+
+        def cut(out_ref, spot, distance, first, last):
+            base = (place[0] ^ distance) * coarse
+            for b in range(first, last):
+                out_ref[spot + b - first] = edged[pl.ds(pl.multiple_of(base + b * rows, 16), rows), :]
+
+        cut(beside_ref, 0, 3, 0, window // 2)
+        cut(beside_ref, window // 2 + planes * taps, 1, 0, window)
+        cut(below_ref, planes * taps, 3, window // 2, window)
+        cut(below_ref, planes * taps + window // 2, 2, 0, window)
+        cut(own_ref, 0, 0, 0, window)
+
+    count = window // 2 + planes * taps + window
+    return pl.pallas_call(
+        kernel,
+        out_shape=[
+            jax.ShapeDtypeStruct((n, rows, block), jnp.bfloat16) for n in (count, count, window)
+        ],
         grid_spec=pltpu.PrefetchScalarGridSpec(
             num_scalar_prefetch=1,
             grid=(1,),
-            in_specs=[pl.BlockSpec(inputs.shape, lambda i, place: (0, 0, 0)), ANYWHERE],
-            out_specs=[pl.BlockSpec((n, 2 * width), lambda i, place: (0, 0)) for n in rows],
+            in_specs=[pl.BlockSpec(line[0].shape, lambda i, place: (0, 0, 0))] * planes + [ANYWHERE],
+            out_specs=[
+                pl.BlockSpec((n, rows, block), lambda i, place: (0, 0, 0))
+                for n in (count, count, window)
+            ],
             scratch_shapes=[
                 pltpu.VMEM((length + 2 * HALO, block), jnp.bfloat16),
-                pltpu.VMEM((width // LANES, 2 * STEP, LANES), jnp.float32),
                 pltpu.SemaphoreType.DMA,
             ],
         ),
         compiler_params=pltpu.CompilerParams(vmem_limit_bytes=32 << 20),
-        name="messages",
-    )(place, inputs, trunk_grad)
+        cost_estimate=SMALL,
+        name="kernel_messages",
+    )(place, *line, trunk_grad)
 
 
 def slope_kernel(x_ref, out_ref, scratch):
@@ -291,13 +313,13 @@
     return total
 
 
-def gradient_stage(place, windows, pieces, distances, slope, begun, shape):
+def gradient_stage(place, windows, taps, pieces, distances, slope, begun, shape):
     _, fine, width = shape
     coarse, seqs = fine // 2, len(windows)
-    taps, rows, block = pieces[0][0].shape[1:]
+    rows, block = pieces[0][0].shape[-2:]
     planes = width // (2 * rows)
-    packed = (coarse + 2 * HALO) // CHUNKS
-    window, used = CHUNKS * packed, coarse + 2 * MARGIN
+    half = planes // 2
+    window, used = coarse + 2 * HALO, coarse + 2 * MARGIN
     depth, planar = len(distances) * block, (2, coarse, width)
     last = begun is not None
     needed = distances if last else list(range(seqs))
@@ -314,20 +336,30 @@
         out_ref, wv, gv, products, slopes, sems, grad_sems, slope_sem = refs[:8]
         me, core = place[0], place[1] % 2
 
-        def kernel_copies(k):
-            for number, (array, plane, flip, distance) in enumerate(pieces):
+        def kernel_copies(first):
+            for number, (array, start, plane, count, flip, distance) in enumerate(pieces):
                 spot = pl.ds(distances.index(distance) * block, block)
-                span = pl.ds(plane, array.shape[0])
-                target = wv.at[k, span, core ^ flip, :, spot]
-                yield sources[number].at[:, k], target, sems.at[k, number]
+                if first != (start is not None):
+                    continue
+                for k in range(SPLIT if first else taps - SPLIT):
+                    for h in range(count // half):
+                        span = pl.ds(plane + h * half, half)
+                        if first:
+                            source = sources[number].at[pl.ds(start + (h * SPLIT + k) * half, half)]
+                        else:
+                            source = sources[number].at[span, distance, k]
+                        tap = k if first else SPLIT + k
+                        target = wv.at[tap, span, core ^ flip, :, spot]
+                        sem = sems.at[tap, number, h]
+                        yield tap, pltpu.make_async_copy(source, target, sem)
 
         def window_copies(target_of, sems):
-            for number, (distance, _, row, first, size) in enumerate(parts):
-                for q in range(CHUNKS):
-                    source = own[number].at[pl.ds(row, size), pl.ds(q * block, block)]
-                    target = target_of(distance, pl.ds(q * packed + first, size))
+            for number, (distance, _, start, first, count) in enumerate(parts):
+                for b in range(count):
+                    target = target_of(distance, pl.ds((first + b) * rows, rows))
                     if target is not None:
-                        yield pltpu.make_async_copy(source, target, sems.at[number, q])
+                        source = own[number].at[start + b]
+                        yield pltpu.make_async_copy(source, target, sems.at[number, b])
 
         def into_window(distance, span):
             if distance not in distances:
@@ -344,19 +376,17 @@
             late += window_copies(lambda d, span: skips.at[me ^ d, span], skip_sems)
         for copy in early:
             copy.start()
-        for k in range(taps):
-            for copy in kernel_copies(k):
-                pltpu.make_async_copy(*copy).start()
+        arriving = sorted([*kernel_copies(True), *kernel_copies(False)], key=lambda pair: pair[0])
+        for _, copy in arriving:
+            copy.start()
         for copy in late:
             copy.start()
         for copy in early:
             copy.wait()
-
-        @pl.loop(0, taps)
-        def _(k):
-            for copy in kernel_copies(k):
-                pltpu.make_async_copy(*copy).wait()
-            half = planes // 2
+        for k in range(taps):
+            for tap, copy in arriving:
+                if tap == k:
+                    copy.wait()
             for part in range(2):
                 kernel = wv[k, part * half : (part + 1) * half].reshape(2 * half * rows, depth)
                 lanes = slice(part * 2 * half * rows, (part + 1) * 2 * half * rows)
@@ -383,11 +413,11 @@
                 for parity in range(2):
                     total = shifted_total(products, base, lanes, parity)
                     total = total * slopes[parity, spot, lanes]
+                    total = total + (sums[parity, spot, lanes] if last else skip)
                     if last:
-                        total = total + sums[parity, spot, lanes]
                         strip[c, pl.ds(parity, STEP, stride=2), :] = total
                     else:
-                        out_ref[parity, spot, lanes] = total + skip
+                        out_ref[parity, spot, lanes] = total
                 if last:
                     out_ref[0, span, lanes] = strip[c].astype(jnp.bfloat16)
 
@@ -397,8 +427,8 @@
         pltpu.VMEM((window, depth), jnp.bfloat16),
         pltpu.VMEM((taps, used, width), jnp.float32),
         pltpu.VMEM(planar, jnp.float32),
-        pltpu.SemaphoreType.DMA((taps, len(pieces))),
-        pltpu.SemaphoreType.DMA((len(parts), CHUNKS)),
+        pltpu.SemaphoreType.DMA((taps, len(pieces), 2)),
+        pltpu.SemaphoreType.DMA((len(parts), window // rows)),
         pltpu.SemaphoreType.DMA,
     ]
     if last:
@@ -410,7 +440,7 @@
     else:
         scratch += [
             pltpu.VMEM((seqs, window, block), jnp.bfloat16),
-            pltpu.SemaphoreType.DMA((len(parts), CHUNKS)),
+            pltpu.SemaphoreType.DMA((len(parts), window // rows)),
         ]
     return pl.pallas_call(
         body,
@@ -424,7 +454,7 @@
         ),
         compiler_params=pltpu.CompilerParams(vmem_limit_bytes=56 << 20),
         cost_estimate=SMALL,
-        name="input_grad_late" if last else "input_grad_early",
+        name="input_grad",
     )(place, *operands)
 
 
@@ -443,8 +473,8 @@
         grid_spec=pltpu.PrefetchScalarGridSpec(
             num_scalar_prefetch=1,
             grid=(1,),
-            in_specs=[pl.BlockSpec(shape, lambda i, place: (0, 0, 0))] * count,
-            out_specs=pl.BlockSpec((count, *shape), lambda i, place: (0, 0, 0, 0)),
+            in_specs=[pl.BlockSpec(shape, lambda i, place: (0,) * len(shape))] * count,
+            out_specs=pl.BlockSpec((count, *shape), lambda i, place: (0,) * (1 + len(shape))),
         ),
         compiler_params=pltpu.CompilerParams(vmem_limit_bytes=24 << 20),
         cost_estimate=SMALL,
@@ -459,31 +489,39 @@
     taps, rows, block = weights.shape
     fine = inputs.shape[1]
     coarse, planes = fine // 2, reps // 2
-    packed = (coarse + 2 * HALO) // CHUNKS
     half = coarse // 2
 
-    to_beside, to_below, own_window = messages(place, inputs, trunk_grad)
-    beside, below = from_peer(to_beside, "seq", 1), from_peer(to_below, "seq", 2)
+    last_taps = weights[SPLIT:]
+    across = [last_taps] + [from_peer(last_taps, "seq", d) for d in range(1, seqs)]
+
+    act = after(activate(inputs), *across[1:])
+    beside, below = from_peer(act, "seq", 1), from_peer(act, "seq", 2)
     slope = half_slope(inputs)
-    column = stack_planes(place, gather_line(weights, "rep", planes, 2))
+    line = gather_line(weights[:SPLIT], "rep", planes, 2)
+    line_across = gather_line(after(jnp.stack(across), *line[1:]), "rep", planes, 2)
     trunk = trunk_grad[0]
     zeros = jnp.zeros((1, block), jnp.bfloat16)
     later = jnp.concatenate([trunk[1:], zeros])
     earlier = jnp.concatenate([zeros, trunk[:-1]])
     shifts = jnp.concatenate([later, trunk, earlier], axis=1)
-    top = after(beside[: FIRST + half], slope, column, shifts)
-    bottom = after(below[half : coarse + packed - FIRST], slope, column, shifts)
+    to_beside, to_below, own_window = kernel_messages(place, line, trunk_grad, coarse)
+    ready = (slope, shifts, to_beside, line_across[1], line_across[planes - 1])
+    top, bottom = after(beside[:half], *ready), after(below[half:], *ready)
     far_top, far_bottom = from_peer(top, "seq", 2), from_peer(bottom, "seq", 1)
 
-    column = after(column, top, bottom)
-    other_column = from_peer(column, "rep", 1)
-    column = after(column, other_column)
-    kept_beside, kept_below = from_peer(column, "seq", 1), from_peer(column, "seq", 2)
-
     scale = 0.5 * float(fine * seqs * reps) ** (-0.5)
-    near_rows = [(0, 0, coarse, FIRST), (1, 0, coarse, FIRST), (2, 0, coarse, 0)]
-    far_rows = [(3, 0, half, FIRST), (3, half, half, 0)]
-    early = early_terms(place, near_rows, [to_beside, beside, below], shifts, coarse)
+    near_rows = [(d, 0, coarse, 0) for d in range(3)]
+    far_rows = [(3, 0, half, 0), (3, half, half, 0)]
+    early = early_terms(place, near_rows, [act, beside, below], shifts, coarse)
+    far_top, far_bottom = after(far_top, early), after(far_bottom, early)
+
+    lines = stack_planes(place, line_across)
+    to_beside, to_below = (
+        after(message, far_top, far_bottom, lines) for message in (to_beside, to_below)
+    )
+    kept_beside, kept_below = from_peer(to_beside, "seq", 1), from_peer(to_below, "seq", 2)
+    other_column, other_lines = from_peer(to_below, "rep", 1), from_peer(lines, "rep", 1)
+
     mine, theirs = late_terms(
         place, far_rows, [far_top, far_bottom], shifts, early, coarse, scale, planes, taps, rows
     )
@@ -492,24 +530,36 @@
     leaving = [(mine[j] + arrived[j].astype(jnp.float32)).astype(jnp.bfloat16) for j in range(planes)]
     summed = [from_peer(leaving[j], "rep", 2 * j) for j in range(1, planes)]
 
-    kept_beside, kept_below = after(kept_beside, early), after(kept_below, early)
-    far_first = from_peer(kept_beside[: planes // 2], "seq", 2)
-    far_second = from_peer(kept_below[planes // 2 :], "seq", 1)
-    soon = [(after(column, *leaving[1:]), 0, 0, 0), (other_column, 0, 1, 0)]
-    for part, distance in ((kept_beside, 1), (kept_below, 2)):
-        soon += [(part, 0, 0, distance), (from_peer(part, "rep", 1), 0, 1, distance)]
-
+    window = (coarse + 2 * HALO) // rows
+    count, side = planes * SPLIT, window // 2
+    kept_beside, kept_below = after(kept_beside, *leaving[1:]), after(kept_below, *leaving[1:])
+    far_first = from_peer(kept_beside[: side + count // 2], "seq", 2)
+    far_second = from_peer(kept_below[count // 2 : count + side], "seq", 1)
     windows = [
-        [(own_window, 0, 0, packed)],
-        [(beside, FIRST + coarse, 0, packed)],
-        [(below, coarse + packed - FIRST, 0, packed)],
-        [(far_top, 0, 0, FIRST), (far_bottom, half, FIRST, packed - FIRST)],
+        [(own_window, 0, 0, window)],
+        [(kept_beside, side + count, 0, window)],
+        [(kept_below, count + side, 0, window)],
+        [(far_first, 0, 0, side), (far_second, count // 2, side, side)],
     ]
-    stage = functools.partial(gradient_stage, place, windows, slope=slope, shape=inputs.shape)
-    begun, rest = stage(soon, [0, 1, 2], begun=None), []
-    for part, plane in ((far_first, 0), (far_second, planes // 2)):
-        part = after(part, begun)
-        rest += [(part, plane, 0, 3), (from_peer(part, "rep", 1), plane, 1, 3)]
+
+    stage = functools.partial(
+        gradient_stage, place, windows, taps, slope=slope, shape=inputs.shape
+    )
+    soon = [(to_below, 0, 0, planes, 0, 0), (other_column, 0, 0, planes, 1, 0)]
+    for part, start, distance in ((kept_beside, side, 1), (kept_below, 0, 2)):
+        soon.append((part, start, 0, planes, 0, distance))
+        soon.append((from_peer(part, "rep", 1), start, 0, planes, 1, distance))
+    crossed = [
+        (part, None, 0, planes, flip, d)
+        for flip, part in enumerate((lines, other_lines))
+        for d in range(seqs)
+    ]
+    begun = stage(soon + [piece for piece in crossed if piece[-1] < 3], [0, 1, 2], begun=None)
+    rest = [piece for piece in crossed if piece[-1] == 3]
+    for part, start, plane in ((far_first, side, 0), (far_second, 0, planes // 2)):
+        part = after(part, begun, *summed)
+        rest.append((part, start, plane, planes // 2, 0, 3))
+        rest.append((from_peer(part, "rep", 1), start, plane, planes // 2, 1, 3))
     input_grad = stage(rest, [3], begun=begun)
     for part in summed:
         weight_grad = weight_grad + after(part, input_grad).astype(jnp.float32)

time: 200 us -> 213 us (1.065)
  the two profiles are of different devices: /device:TPU:0 before, /device:TPU:9 now
where the time goes in v13:
time: 213 us; the launch traced here: 212 us
  waiting for transfers between devices  86.3 us (41%)
  Pallas kernels  54 us (25%)
  local copies, waits for them, and re-layouts  33.6 us (16%)
  starting transfers between devices  25.1 us (12%)
  other arithmetic  11.7 us (5%)
    ppermute x27, waiting for transfers between devices, from_peer(): return lax.ppermute(value, axis, [(i, i ^ distance) for i in range(peers)])  86.3 us
    ppermute x27, starting transfers between devices, from_peer(): return lax.ppermute(value, axis, [(i, i ^ distance) for i in range(peers)])  25.1 us
    pallas_call x2, Pallas kernels, gradient_stage(): pl.pallas_call(body, out_shape=out_shape, grid_spec=pltpu.PrefetchScalarG...  24.7 us
    unnamed x92, local copies, waits for them, and re-layouts  23.1 us
    pallas_call x1, Pallas kernels, early_terms(): pl.pallas_call(kernel, out_shape=jax.ShapeDtypeStruct((both, columns), jn...  13.9 us
    pallas_call x1, Pallas kernels, late_terms(): pl.pallas_call(kernel, out_shape=(jax.ShapeDtypeStruct(shape, jnp.float32...  9.51 us
    concatenate x1, other arithmetic, on_device_square(): shifts = jnp.concatenate([later, trunk, earlier], axis=1)  5.41 us
  transfers between devices with their start and end apart: 27, of which 10 were waited for; matrix products, arithmetic and copies ran while one was open for 10% of the time, Pallas kernels for 21%

profile of v13, /device:TPU:9, one launch (start us, length us, event | category | flops | bytes accessed | tf_op | source)
XLA Modules:
  0.0 211.8 jit_solution(10893584834005956889)
XLA Ops:
  1.6 1.4 collective-permute-start.1
  3.9 1.3 collective-permute-start.3
  5.2 1.2 collective-permute-start.4
  6.6 2.2 %collective-permute-start = (bf16[3,96,384]{2,1,0:T(8,128)(2,1)S(1)}, bf16[3,96,384]{2,1,0:T(8,128)(2,1)S(1)}, u32[]{:S(2)}, u32[]{:S(2)}) collective-permute-start(bf16[3,96,384]{2,1,0:T(8,128)(2,1)S(1)} %slice.54.refs_0_), channel_id=1, source_target_pairs={{0,2},{1,3},{2,0},{3,1},{4,6},{5,7},{6,4},{7,5},{8,10},{9,11},{10,... | collective-permute-start | bytes 663560 | tf_op jit(solution)/shard_map/ppermute | solution.py:27
  8.8 1.4 copy-done.8
  10.2 1.8 act.1.refs_0_
  12.0 1.1 copy-done.3
  14.5 1.2 collective-permute-start.6
  15.7 1.2 collective-permute-start.10
  17.0 2.1 slice_bitcast_fusion.1
  20.0 2.1 collective-permute-done.2.refs_2_
  22.9 5.4 %fusion.2.refs_2_.shifts_ref = bf16[2048,1152]{1,0:T(8,128)(2,1)} fusion(bf16[2047,384]{1,0:T(8,128)(2,1)} %get-tuple-element.16, bf16[2047,384]{1,0:T(8,128)(2,1)} %get-tuple-element.15, bf16[2048,384]{1,0:T(8,128)(2,1)S(1)} %bitcast.24), kind=kLoop, calls=%fused_computation.4 | loop fusion | flops 23592960 | bytes 9435648 | tf_op jit(solution)/shard_map/concatenate | solution.py:506
  28.3 2.3 %half_slope.1.refs_1_.refs_17_.refs_8_ = f32[2,512,768]{2,1,0:T(8,128)S(1)} custom-call(bf16[1,1024,768]{2,1,0:T(8,128)(2,1)S(1)} %copy-done.9), custom_call_target="tpu_custom_call" | custom-call | tf_op jit(solution)/shard_map/half_slope/pallas_call | solution.py:161
  30.7 1.6 copy-done.1
  34.4 1.2 copy-done.5
  35.6 1.2 copy-done.10
  36.8 11.9 %collective-permute-done.6.refs_1_ = bf16[512,1536]{1,0:T(8,128)(2,1)} collective-permute-done((bf16[512,1536]{1,0:T(8,128)(2,1)}, bf16[512,1536]{1,0:T(8,128)(2,1)}, u32[]{:S(2)}, u32[]{:S(2)}) %collective-permute-start.6) | collective-permute-done | bytes 1572896 | tf_op jit(solution)/shard_map/ppermute | solution.py:27
  48.6 2.1 slice.72.refs_0_
  51.7 1.2 collective-permute-start.9
  53.0 2.1 slice.73.refs_0_
  55.1 1.2 collective-permute-start.11
  56.3 11.4 %collective-permute-done.12.refs_2_ = bf16[4,2,96,384]{3,2,1,0:T(8,128)(2,1)S(1)} collective-permute-done((bf16[4,2,96,384]{3,2,1,0:T(8,128)(2,1)S(1)}, bf16[4,2,96,384]{3,2,1,0:T(8,128)(2,1)S(1)}, u32[]{:S(2)}, u32[]{:S(2)}) %collective-permute-start.12) | collective-permute-done | bytes 589856 | tf_op jit(solution)/shard_map/ppermute | solution.py:27
  67.7 1.1 copy-done.11
  68.7 1.1 copy-done.13
  69.8 1.1 copy-done.16
  71.6 4.4 %collective-permute-start.18 = (bf16[4,4,2,96,384]{4,3,2,1,0:T(8,128)(2,1)S(1)}, bf16[4,4,2,96,384]{4,3,2,1,0:T(8,128)(2,1)}, u32[]{:S(2)}, u32[]{:S(2)}) collective-permute-start(bf16[4,4,2,96,384]{4,3,2,1,0:T(8,128)(2,1)S(1)} %stack_planes.1.refs_3_.refs_11_.refs_12_.refs_13_.refs_2_), channel_id=1, source_target_pairs={{0,1},{1,0},{2,3},{3,2},{4,5},{5,4},{6,7},{7,6},{8,9},{9,8},{10,11... | collective-permute-start | bytes 7077896 | tf_op jit(solution)/shard_map/ppermute | solution.py:27
  76.1 13.9 %weight_grad_early.1.refs_1_.early_ref = f32[1536,1152]{1,0:T(8,128)} custom-call(s32[2]{0:T(128)S(1)} %pad_add_fusion.place, bf16[2048,1152]{1,0:T(8,128)(2,1)} %fusion.2.refs_2_.shifts_ref, bf16[512,1536]{1,0:T(8,128)(2,1)S(1)} %copy-done.4, bf16[512,1536]{1,0:T(8,128)(2,1)} %collective-permute-done.6.refs_1_, ...), custom_call_target="tpu_custom_call" | custom-call | flops 1048576 | bytes 65536 | tf_op jit(solution)/shard_map/weight_grad_early/pallas_call | solution.py:209
  90.9 1.1 copy-done.7
  92.0 9.5 %weight_grad_late.1 = (f32[4,5,96,384]{3,2,1,0:T(8,128)S(1)}, bf16[4,5,96,384]{3,2,1,0:T(8,128)(2,1)}) custom-call(s32[2]{0:T(128)S(1)} %pad_add_fusion.place, bf16[2048,1152]{1,0:T(8,128)(2,1)} %fusion.2.refs_2_.shifts_ref, f32[1536,1152]{1,0:T(8,128)} %weight_grad_early.1.refs_1_.early_ref, bf16[256,1536]{1,0:T(8,128)(2,1)S(1)} %copy-done.7, ...), custom_call_target="tpu_custom_call" | custom-call | flops 1048576 | bytes 65536 | tf_op jit(solution)/shard_map/weight_grad_late/pallas_call | solution.py:279
  101.5 1.6 copy-done.17
  103.1 1.0 collective-permute-start.13
  105.5 1.3 collective-permute-done.14
  106.7 3.0 %fusion.8 = (bf16[5,96,384]{2,1,0:T(8,128)(2,1)}, bf16[5,96,384]{2,1,0:T(8,128)(2,1)}, bf16[5,96,384]{2,1,0:T(8,128)(2,1)}) fusion(f32[4,5,96,384]{3,2,1,0:T(8,128)} %copy-done.17, bf16[4,5,96,384]{3,2,1,0:T(8,128)(2,1)} %collective-permute-done.14), kind=kLoop, calls=%fused_computation.17 | loop fusion | flops 1658880 | bytes 4423680 | tf_op jit(solution)/shard_map/convert_element_type | solution.py:530
  109.7 28.7 %collective-permute-done.13.refs_0_ = bf16[21,96,384]{2,1,0:T(8,128)(2,1)} collective-permute-done((bf16[21,96,384]{2,1,0:T(8,128)(2,1)}, bf16[21,96,384]{2,1,0:T(8,128)(2,1)}, u32[]{:S(2)}, u32[]{:S(2)}) %collective-permute-start.13) | collective-permute-done | bytes 1548320 | tf_op jit(solution)/shard_map/ppermute | solution.py:27
  138.4 1.4 collective-permute-start.20
  139.8 1.1 collective-permute-start.21
  140.9 1.2 slice.77
  142.0 1.2 slice.78
  144.9 14.8 %collective-permute-done.15.refs_3_.refs_0_ = bf16[9,96,384]{2,1,0:T(8,128)(2,1)S(1)} collective-permute-done((bf16[9,96,384]{2,1,0:T(8,128)(2,1)S(1)}, bf16[9,96,384]{2,1,0:T(8,128)(2,1)S(1)}, u32[]{:S(2)}, u32[]{:S(2)}) %collective-permute-start.15) | collective-permute-done | bytes 663584 | tf_op jit(solution)/shard_map/ppermute | solution.py:27
  159.8 1.2 collective-permute-start.24
  162.8 1.1 copy-done.36
  163.9 15.2 %input_grad.2.refs_1_.refs_9_ = f32[2,512,768]{2,1,0:T(8,128)} custom-call(s32[2]{0:T(128)} %copy-done.25, bf16[6,96,384]{2,1,0:T(8,128)(2,1)} %copy-done.24, bf16[21,96,384]{2,1,0:T(8,128)(2,1)} %after.22.refs_1_.refs_7_, bf16[21,96,384]{2,1,0:T(8,128)(2,1)} %after.24.refs_2_.refs_9_, bf16[9,96,384]{2,1,0:T(8,128)(2,1)} %copy-done.26, ...), custom_call_target="tpu_custom_call" | custom-call | flops 1048576 | bytes 65536 | tf_op jit(solution)/shard_map/input_grad/pallas_call | solution.py:445
  179.1 4.7 %collective-permute-done.23.refs_3_.refs_0_ = bf16[5,96,384]{2,1,0:T(8,128)(2,1)S(1)} collective-permute-done((bf16[5,96,384]{2,1,0:T(8,128)(2,1)S(1)}, bf16[5,96,384]{2,1,0:T(8,128)(2,1)S(1)}, u32[]{:S(2)}, u32[]{:S(2)}) %collective-permute-start.23) | collective-permute-done | bytes 368672 | tf_op jit(solution)/shard_map/ppermute | solution.py:27
  183.8 8.7 %collective-permute-done.24.refs_4_.refs_0_ = bf16[5,96,384]{2,1,0:T(8,128)(2,1)S(1)} collective-permute-done((bf16[5,96,384]{2,1,0:T(8,128)(2,1)S(1)}, bf16[5,96,384]{2,1,0:T(8,128)(2,1)S(1)}, u32[]{:S(2)}, u32[]{:S(2)}) %collective-permute-start.24) | collective-permute-done | bytes 368672 | tf_op jit(solution)/shard_map/ppermute | solution.py:27
  193.2 1.7 collective-permute-start.25
  194.9 1.9 collective-permute-done.25.refs_5_
  198.7 9.5 %input_grad.3.refs_1_ = bf16[1,1024,768]{2,1,0:T(8,128)(2,1)} custom-call(s32[2]{0:T(128)} %copy-done.25, bf16[9,96,384]{2,1,0:T(8,128)(2,1)} %copy-done.26, bf16[9,96,384]{2,1,0:T(8,128)(2,1)} %copy-done.27, bf16[4,4,2,96,384]{4,3,2,1,0:T(8,128)(2,1)} %copy-done, bf16[4,4,2,96,384]{4,3,2,1,0:T(8,128)(2,1)} %collective-permute-done.18.refs_14_.refs_15_.refs_16_.refs_3_, ...), custom_call_target="tpu_custom_call" | custom-call | flops 1048576 | bytes 65536 | tf_op jit(solution)/shard_map/input_grad/pallas_call | solution.py:445
  209.4 2.4 %fusion.5 = f32[5,96,384]{2,1,0:T(8,128)} fusion(bf16[5,96,384]{2,1,0:T(8,128)(2,1)S(1)} %copy-done.32, bf16[5,96,384]{2,1,0:T(8,128)(2,1)S(1)} %copy-done.30, bf16[5,96,384]{2,1,0:T(8,128)(2,1)} %after.27, f32[4,5,96,384]{3,2,1,0:T(8,128)} %copy-done.17, bf16[4,5,96,384]{3,2,1,0:T(8,128)(2,1)} %collective-permute-done.14), kind=kLoop, calls=%fused_computation.10 | loop fusion | flops 1474560 | bytes 2949120 | tf_op jit(solution)/shard_map/add | solution.py:565
  (133 shorter events, 18.4 us)
Async XLA Ops:
  1.6 15.4 %collective-permute-start.1 = (bf16[3,96,384]{2,1,0:T(8,128)(2,1)S(1)}, bf16[3,96,384]{2,1,0:T(8,128)(2,1)S(1)}, u32[]{:S(2)}, u32[]{:S(2)}) collective-permute-start(bf16[3,96,384]{2,1,0:T(8,128)(2,1)S(1)} %slice.54.refs_0_), channel_id=1, source_target_pairs={{0,6},{1,7},{2,4},{3,5},{4,2},{5,3},{6,0},{7,1},{8,14},{9,15},{10,... | collective-permute-start | bytes 663560 | tf_op jit(solution)/shard_map/ppermute | solution.py:27
  3.9 9.2 %collective-permute-start.3 = (bf16[2,96,384]{2,1,0:T(8,128)(2,1)S(1)}, bf16[2,96,384]{2,1,0:T(8,128)(2,1)S(1)}, u32[]{:S(2)}, u32[]{:S(2)}) collective-permute-start(bf16[2,96,384]{2,1,0:T(8,128)(2,1)S(1)} %get-tuple-element.18), channel_id=1, source_target_pairs={{0,8},{8,0},{16,24},{24,16},{1,9},{9,1},{17,25},{25,17},{2,10},{10... | collective-permute-start | bytes 442376 | tf_op jit(solution)/shard_map/ppermute | solution.py:27
  5.2 8.0 %collective-permute-start.4 = (bf16[2,96,384]{2,1,0:T(8,128)(2,1)S(1)}, bf16[2,96,384]{2,1,0:T(8,128)(2,1)S(1)}, u32[]{:S(2)}, u32[]{:S(2)}) collective-permute-start(bf16[2,96,384]{2,1,0:T(8,128)(2,1)S(1)} %get-tuple-element.18), channel_id=1, source_target_pairs={{0,16},{8,24},{16,0},{24,8},{1,17},{9,25},{17,1},{25,9},{2,18},{10... | collective-permute-start | bytes 442376 | tf_op jit(solution)/shard_map/ppermute | solution.py:27
  6.4 6.7 %collective-permute-start.5 = (bf16[2,96,384]{2,1,0:T(8,128)(2,1)S(1)}, bf16[2,96,384]{2,1,0:T(8,128)(2,1)S(1)}, u32[]{:S(2)}, u32[]{:S(2)}) collective-permute-start(bf16[2,96,384]{2,1,0:T(8,128)(2,1)S(1)} %get-tuple-element.18), channel_id=1, source_target_pairs={{0,24},{8,16},{16,8},{24,0},{1,25},{9,17},{17,9},{25,1},{2,26},{10... | collective-permute-start | bytes 442376 | tf_op jit(solution)/shard_map/ppermute | solution.py:27
  6.6 13.4 %collective-permute-start = (bf16[3,96,384]{2,1,0:T(8,128)(2,1)S(1)}, bf16[3,96,384]{2,1,0:T(8,128)(2,1)S(1)}, u32[]{:S(2)}, u32[]{:S(2)}) collective-permute-start(bf16[3,96,384]{2,1,0:T(8,128)(2,1)S(1)} %slice.54.refs_0_), channel_id=1, source_target_pairs={{0,2},{1,3},{2,0},{3,1},{4,6},{5,7},{6,4},{7,5},{8,10},{9,11},{10,... | collective-permute-start | bytes 663560 | tf_op jit(solution)/shard_map/ppermute | solution.py:27
  13.1 3.9 %copy-start.2 = (bf16[1,2048,384]{2,1,0:T(8,128)(2,1)S(1)}, bf16[1,2048,384]{2,1,0:T(8,128)(2,1)}, u32[]{:S(2)}) copy-start(bf16[1,2048,384]{2,1,0:T(8,128)(2,1)} %refs_4_.1) | copy-start | bytes 4718596
  14.5 4.6 %copy-start.40 = (bf16[2,96,384]{2,1,0:T(8,128)(2,1)S(1)}, bf16[2,96,384]{2,1,0:T(8,128)(2,1)}, u32[]{:S(2)}) copy-start(bf16[2,96,384]{2,1,0:T(8,128)(2,1)} %copy-done.39) | copy-start | bytes 442372
  14.5 4.6 %copy-start.42 = (bf16[2,96,384]{2,1,0:T(8,128)(2,1)S(1)}, bf16[2,96,384]{2,1,0:T(8,128)(2,1)}, u32[]{:S(2)}) copy-start(bf16[2,96,384]{2,1,0:T(8,128)(2,1)} %copy-done.41) | copy-start | bytes 442372
  14.5 4.6 %copy-start.44 = (bf16[2,96,384]{2,1,0:T(8,128)(2,1)S(1)}, bf16[2,96,384]{2,1,0:T(8,128)(2,1)}, u32[]{:S(2)}) copy-start(bf16[2,96,384]{2,1,0:T(8,128)(2,1)} %copy-done.43) | copy-start | bytes 442372
  14.5 34.1 %collective-permute-start.6 = (bf16[512,1536]{1,0:T(8,128)(2,1)}, bf16[512,1536]{1,0:T(8,128)(2,1)}, u32[]{:S(2)}, u32[]{:S(2)}) collective-permute-start(bf16[512,1536]{1,0:T(8,128)(2,1)} %after.15.refs_0_), channel_id=1, source_target_pairs={{0,8},{8,0},{16,24},{24,16},{1,9},{9,1},{17,25},{25,17},{2,10},{10... | collective-permute-start | bytes 4718600 | tf_op jit(solution)/shard_map/ppermute | solution.py:27
  15.7 37.2 %collective-permute-start.10 = (bf16[512,1536]{1,0:T(8,128)(2,1)}, bf16[512,1536]{1,0:T(8,128)(2,1)}, u32[]{:S(2)}, u32[]{:S(2)}) collective-permute-start(bf16[512,1536]{1,0:T(8,128)(2,1)} %after.15.refs_0_), channel_id=1, source_target_pairs={{0,16},{8,24},{16,0},{24,8},{1,17},{9,25},{17,1},{25,9},{2,18},{10... | collective-permute-start | bytes 4718600 | tf_op jit(solution)/shard_map/ppermute | solution.py:27
  17.0 2.1 %copy-start.18 = (bf16[3,96,384]{2,1,0:T(8,128)(2,1)}, bf16[3,96,384]{2,1,0:T(8,128)(2,1)S(1)}, u32[]{:S(2)}) copy-start(bf16[3,96,384]{2,1,0:T(8,128)(2,1)S(1)} %collective-permute-done.1.refs_3_) | copy-start | bytes 663556
  17.0 5.2 %collective-permute-start.2 = (bf16[3,96,384]{2,1,0:T(8,128)(2,1)S(1)}, bf16[3,96,384]{2,1,0:T(8,128)(2,1)S(1)}, u32[]{:S(2)}, u32[]{:S(2)}) collective-permute-start(bf16[3,96,384]{2,1,0:T(8,128)(2,1)S(1)} %collective-permute-done.1.refs_3_), channel_id=1, source_target_pairs={{0,2},{1,3},{2,0},{3,1},{4,6},{5,7},{6,4},{7,5},{8,10},{9,11},{10,... | collective-permute-start | bytes 663560 | tf_op jit(solution)/shard_map/ppermute | solution.py:27
  20.0 2.1 %copy-start.20 = (bf16[3,96,384]{2,1,0:T(8,128)(2,1)}, bf16[3,96,384]{2,1,0:T(8,128)(2,1)S(1)}, u32[]{:S(2)}) copy-start(bf16[3,96,384]{2,1,0:T(8,128)(2,1)S(1)} %collective-permute-done.refs_1_) | copy-start | bytes 663556
  22.9 27.8 %collective-permute-start.7 = (bf16[4,2,96,384]{3,2,1,0:T(8,128)(2,1)}, bf16[4,2,96,384]{3,2,1,0:T(8,128)(2,1)S(1)}, u32[]{:S(2)}, u32[]{:S(2)}) collective-permute-start(bf16[4,2,96,384]{3,2,1,0:T(8,128)(2,1)} %after.16.refs_0_), channel_id=1, source_target_pairs={{0,2},{1,3},{2,0},{3,1},{4,6},{5,7},{6,4},{7,5},{8,10},{9,11},{10,... | collective-permute-start | bytes 1769480 | tf_op jit(solution)/shard_map/ppermute | solution.py:27
  22.9 27.8 %collective-permute-start.8 = (bf16[4,2,96,384]{3,2,1,0:T(8,128)(2,1)}, bf16[4,2,96,384]{3,2,1,0:T(8,128)(2,1)S(1)}, u32[]{:S(2)}, u32[]{:S(2)}) collective-permute-start(bf16[4,2,96,384]{3,2,1,0:T(8,128)(2,1)} %after.16.refs_0_), channel_id=1, source_target_pairs={{0,6},{1,7},{2,4},{3,5},{4,2},{5,3},{6,0},{7,1},{8,14},{9,15},{10,... | collective-permute-start | bytes 1769480 | tf_op jit(solution)/shard_map/ppermute | solution.py:27
  22.9 5.4 %copy-start.9 = (bf16[1,1024,768]{2,1,0:T(8,128)(2,1)S(1)}, bf16[1,1024,768]{2,1,0:T(8,128)(2,1)}, u32[]{:S(2)}) copy-start(bf16[1,1024,768]{2,1,0:T(8,128)(2,1)} %x_ref.3) | copy-start | bytes 4718596
  28.3 4.1 %copy-start.19 = (bf16[3,96,384]{2,1,0:T(8,128)(2,1)S(1)}, bf16[3,96,384]{2,1,0:T(8,128)(2,1)}, u32[]{:S(2)}) copy-start(bf16[3,96,384]{2,1,0:T(8,128)(2,1)} %copy-done.18) | copy-start | bytes 663556
  28.3 4.1 %copy-start.21 = (bf16[3,96,384]{2,1,0:T(8,128)(2,1)S(1)}, bf16[3,96,384]{2,1,0:T(8,128)(2,1)}, u32[]{:S(2)}) copy-start(bf16[3,96,384]{2,1,0:T(8,128)(2,1)} %copy-done.20) | copy-start | bytes 663556
  30.7 1.6 copy-start.1
  33.3 57.5 %copy-start.25 = (s32[2]{0:T(128)}, s32[2]{0:T(128)S(1)}, u32[]{:S(2)}) copy-start(s32[2]{0:T(128)S(1)} %pad_add_fusion.place) | copy-start | bytes 28
  36.8 13.9 %copy-start.24 = (bf16[6,96,384]{2,1,0:T(8,128)(2,1)}, bf16[6,96,384]{2,1,0:T(8,128)(2,1)S(1)}, u32[]{:S(2)}) copy-start(bf16[6,96,384]{2,1,0:T(8,128)(2,1)S(1)} %get-tuple-element.11.refs_0_) | copy-start | bytes 1327108
  51.7 38.2 %collective-permute-start.9 = (bf16[256,1536]{1,0:T(8,128)(2,1)}, bf16[256,1536]{1,0:T(8,128)(2,1)S(1)}, u32[]{:S(2)}, u32[]{:S(2)}) collective-permute-start(bf16[256,1536]{1,0:T(8,128)(2,1)} %after.17), channel_id=1, source_target_pairs={{0,16},{8,24},{16,0},{24,8},{1,17},{9,25},{17,1},{25,9},{2,18},{10... | collective-permute-start | bytes 2359304 | tf_op jit(solution)/shard_map/ppermute | solution.py:27
  55.1 21.0 %copy-start.4 = (bf16[512,1536]{1,0:T(8,128)(2,1)S(1)}, bf16[512,1536]{1,0:T(8,128)(2,1)}, u32[]{:S(2)}) copy-start(bf16[512,1536]{1,0:T(8,128)(2,1)} %after.15.refs_0_) | copy-start | bytes 4718596
  55.1 35.8 %collective-permute-start.11 = (bf16[256,1536]{1,0:T(8,128)(2,1)}, bf16[256,1536]{1,0:T(8,128)(2,1)}, u32[]{:S(2)}, u32[]{:S(2)}) collective-permute-start(bf16[256,1536]{1,0:T(8,128)(2,1)} %after.19), channel_id=1, source_target_pairs={{0,8},{8,0},{16,24},{24,16},{1,9},{9,1},{17,25},{25,17},{2,10},{10... | collective-permute-start | bytes 2359304 | tf_op jit(solution)/shard_map/ppermute | solution.py:27
  56.3 11.4 %collective-permute-start.12 = (bf16[4,2,96,384]{3,2,1,0:T(8,128)(2,1)S(1)}, bf16[4,2,96,384]{3,2,1,0:T(8,128)(2,1)S(1)}, u32[]{:S(2)}, u32[]{:S(2)}) collective-permute-start(bf16[4,2,96,384]{3,2,1,0:T(8,128)(2,1)S(1)} %copy-done.15), channel_id=1, source_target_pairs={{0,2},{1,3},{2,0},{3,1},{4,6},{5,7},{6,4},{7,5},{8,10},{9,11},{10,... | collective-permute-start | bytes 1769480 | tf_op jit(solution)/shard_map/ppermute | solution.py:27
  71.6 18.4 %copy-start = (bf16[4,4,2,96,384]{4,3,2,1,0:T(8,128)(2,1)}, bf16[4,4,2,96,384]{4,3,2,1,0:T(8,128)(2,1)S(1)}, u32[]{:S(2)}) copy-start(bf16[4,4,2,96,384]{4,3,2,1,0:T(8,128)(2,1)S(1)} %stack_planes.1.refs_3_.refs_11_.refs_12_.refs_13_.refs_2_) | copy-start | bytes 7077892
  71.6 71.9 %collective-permute-start.18 = (bf16[4,4,2,96,384]{4,3,2,1,0:T(8,128)(2,1)S(1)}, bf16[4,4,2,96,384]{4,3,2,1,0:T(8,128)(2,1)}, u32[]{:S(2)}, u32[]{:S(2)}) collective-permute-start(bf16[4,4,2,96,384]{4,3,2,1,0:T(8,128)(2,1)S(1)} %stack_planes.1.refs_3_.refs_11_.refs_12_.refs_13_.refs_2_), channel_id=1, source_target_pairs={{0,1},{1,0},{2,3},{3,2},{4,5},{5,4},{6,7},{7,6},{8,9},{9,8},{10,11... | collective-permute-start | bytes 7077896 | tf_op jit(solution)/shard_map/ppermute | solution.py:27
  103.1 3.6 %collective-permute-start.14 = (bf16[4,5,96,384]{3,2,1,0:T(8,128)(2,1)}, bf16[4,5,96,384]{3,2,1,0:T(8,128)(2,1)}, u32[]{:S(2)}, u32[]{:S(2)}) collective-permute-start(bf16[4,5,96,384]{3,2,1,0:T(8,128)(2,1)} %get-tuple-element.9), channel_id=1, source_target_pairs={{0,1},{1,0},{2,3},{3,2},{4,5},{5,4},{6,7},{7,6},{8,9},{9,8},{10,11... | collective-permute-start | bytes 4423688 | tf_op jit(solution)/shard_map/ppermute | solution.py:27
  103.1 35.2 %collective-permute-start.13 = (bf16[21,96,384]{2,1,0:T(8,128)(2,1)}, bf16[21,96,384]{2,1,0:T(8,128)(2,1)}, u32[]{:S(2)}, u32[]{:S(2)}) collective-permute-start(bf16[21,96,384]{2,1,0:T(8,128)(2,1)} %after.21), channel_id=1, source_target_pairs={{0,8},{8,0},{16,24},{24,16},{1,9},{9,1},{17,25},{25,17},{2,10},{10... | collective-permute-start | bytes 4644872 | tf_op jit(solution)/shard_map/ppermute | solution.py:27
  104.2 35.6 %collective-permute-start.16 = (bf16[21,96,384]{2,1,0:T(8,128)(2,1)}, bf16[21,96,384]{2,1,0:T(8,128)(2,1)}, u32[]{:S(2)}, u32[]{:S(2)}) collective-permute-start(bf16[21,96,384]{2,1,0:T(8,128)(2,1)} %after.23.refs_5_), channel_id=1, source_target_pairs={{0,16},{8,24},{16,0},{24,8},{1,17},{9,25},{17,1},{25,9},{2,18},{10... | collective-permute-start | bytes 4644872 | tf_op jit(solution)/shard_map/ppermute | solution.py:27
  104.5 39.4 %collective-permute-start.19 = (bf16[21,96,384]{2,1,0:T(8,128)(2,1)}, bf16[21,96,384]{2,1,0:T(8,128)(2,1)}, u32[]{:S(2)}, u32[]{:S(2)}) collective-permute-start(bf16[21,96,384]{2,1,0:T(8,128)(2,1)} %after.23.refs_5_), channel_id=1, source_target_pairs={{0,1},{1,0},{2,3},{3,2},{4,5},{5,4},{6,7},{7,6},{8,9},{9,8},{10,11... | collective-permute-start | bytes 4644872 | tf_op jit(solution)/shard_map/ppermute | solution.py:27
  138.4 24.4 %collective-permute-start.20 = (bf16[21,96,384]{2,1,0:T(8,128)(2,1)}, bf16[21,96,384]{2,1,0:T(8,128)(2,1)}, u32[]{:S(2)}, u32[]{:S(2)}) collective-permute-start(bf16[21,96,384]{2,1,0:T(8,128)(2,1)} %after.22.refs_1_.refs_7_), channel_id=1, source_target_pairs={{0,1},{1,0},{2,3},{3,2},{4,5},{5,4},{6,7},{7,6},{8,9},{9,8},{10,11... | collective-permute-start | bytes 4644872 | tf_op jit(solution)/shard_map/ppermute | solution.py:27
  139.7 4.1 %copy-start.35 = (bf16[5,96,384]{2,1,0:T(8,128)(2,1)S(1)}, bf16[5,96,384]{2,1,0:T(8,128)(2,1)}, u32[]{:S(2)}) copy-start(bf16[5,96,384]{2,1,0:T(8,128)(2,1)} %get-tuple-element.14.refs_1_) | copy-start | bytes 1105924
  139.7 20.0 %copy-start.34 = (bf16[5,96,384]{2,1,0:T(8,128)(2,1)S(1)}, bf16[5,96,384]{2,1,0:T(8,128)(2,1)}, u32[]{:S(2)}) copy-start(bf16[5,96,384]{2,1,0:T(8,128)(2,1)} %get-tuple-element.13.refs_2_) | copy-start | bytes 1105924
  139.8 20.0 %copy-start.33 = (bf16[5,96,384]{2,1,0:T(8,128)(2,1)S(1)}, bf16[5,96,384]{2,1,0:T(8,128)(2,1)}, u32[]{:S(2)}) copy-start(bf16[5,96,384]{2,1,0:T(8,128)(2,1)} %get-tuple-element.12.refs_3_) | copy-start | bytes 1105924
  139.8 23.0 %collective-permute-start.21 = (bf16[21,96,384]{2,1,0:T(8,128)(2,1)}, bf16[21,96,384]{2,1,0:T(8,128)(2,1)S(1)}, u32[]{:S(2)}, u32[]{:S(2)}) collective-permute-start(bf16[21,96,384]{2,1,0:T(8,128)(2,1)} %after.24.refs_2_.refs_9_), channel_id=1, source_target_pairs={{0,1},{1,0},{2,3},{3,2},{4,5},{5,4},{6,7},{7,6},{8,9},{9,8},{10,11... | collective-permute-start | bytes 4644872 | tf_op jit(solution)/shard_map/ppermute | solution.py:27
  143.2 16.5 %collective-permute-start.15 = (bf16[9,96,384]{2,1,0:T(8,128)(2,1)S(1)}, bf16[9,96,384]{2,1,0:T(8,128)(2,1)S(1)}, u32[]{:S(2)}, u32[]{:S(2)}) collective-permute-start(bf16[9,96,384]{2,1,0:T(8,128)(2,1)S(1)} %slice.77), channel_id=1, source_target_pairs={{0,16},{8,24},{16,0},{24,8},{1,17},{9,25},{17,1},{25,9},{2,18},{10... | collective-permute-start | bytes 1990664 | tf_op jit(solution)/shard_map/ppermute | solution.py:27
  143.6 16.2 %collective-permute-start.17 = (bf16[9,96,384]{2,1,0:T(8,128)(2,1)S(1)}, bf16[9,96,384]{2,1,0:T(8,128)(2,1)S(1)}, u32[]{:S(2)}, u32[]{:S(2)}) collective-permute-start(bf16[9,96,384]{2,1,0:T(8,128)(2,1)S(1)} %slice.78), channel_id=1, source_target_pairs={{0,8},{8,0},{16,24},{24,16},{1,9},{9,1},{17,25},{25,17},{2,10},{10... | collective-permute-start | bytes 1990664 | tf_op jit(solution)/shard_map/ppermute | solution.py:27
  143.9 35.2 %collective-permute-start.22 = (bf16[5,96,384]{2,1,0:T(8,128)(2,1)S(1)}, bf16[5,96,384]{2,1,0:T(8,128)(2,1)S(1)}, u32[]{:S(2)}, u32[]{:S(2)}) collective-permute-start(bf16[5,96,384]{2,1,0:T(8,128)(2,1)S(1)} %copy-done.35), channel_id=1, source_target_pairs={{0,2},{1,3},{2,0},{3,1},{4,6},{5,7},{6,4},{7,5},{8,10},{9,11},{10,... | collective-permute-start | bytes 1105928 | tf_op jit(solution)/shard_map/ppermute | solution.py:27
  159.7 3.0 %copy-start.26 = (bf16[9,96,384]{2,1,0:T(8,128)(2,1)}, bf16[9,96,384]{2,1,0:T(8,128)(2,1)S(1)}, u32[]{:S(2)}) copy-start(bf16[9,96,384]{2,1,0:T(8,128)(2,1)S(1)} %collective-permute-done.15.refs_3_.refs_0_) | copy-start | bytes 1990660
  159.7 24.0 %collective-permute-start.23 = (bf16[5,96,384]{2,1,0:T(8,128)(2,1)S(1)}, bf16[5,96,384]{2,1,0:T(8,128)(2,1)S(1)}, u32[]{:S(2)}, u32[]{:S(2)}) collective-permute-start(bf16[5,96,384]{2,1,0:T(8,128)(2,1)S(1)} %copy-done.34), channel_id=1, source_target_pairs={{0,4},{1,5},{2,6},{3,7},{4,0},{5,1},{6,2},{7,3},{8,12},{9,13},{10,... | collective-permute-start | bytes 1105928 | tf_op jit(solution)/shard_map/ppermute | solution.py:27
  159.7 3.0 %copy-start.27 = (bf16[9,96,384]{2,1,0:T(8,128)(2,1)}, bf16[9,96,384]{2,1,0:T(8,128)(2,1)S(1)}, u32[]{:S(2)}) copy-start(bf16[9,96,384]{2,1,0:T(8,128)(2,1)S(1)} %collective-permute-done.17.refs_4_.refs_1_) | copy-start | bytes 1990660
  159.8 32.7 %collective-permute-start.24 = (bf16[5,96,384]{2,1,0:T(8,128)(2,1)S(1)}, bf16[5,96,384]{2,1,0:T(8,128)(2,1)S(1)}, u32[]{:S(2)}, u32[]{:S(2)}) collective-permute-start(bf16[5,96,384]{2,1,0:T(8,128)(2,1)S(1)} %copy-done.33), channel_id=1, source_target_pairs={{0,6},{1,7},{2,4},{3,5},{4,2},{5,3},{6,0},{7,1},{8,14},{9,15},{10,... | collective-permute-start | bytes 1105928 | tf_op jit(solution)/shard_map/ppermute | solution.py:27
  179.1 13.4 %copy-start.28 = (bf16[5,96,384]{2,1,0:T(8,128)(2,1)}, bf16[5,96,384]{2,1,0:T(8,128)(2,1)S(1)}, u32[]{:S(2)}) copy-start(bf16[5,96,384]{2,1,0:T(8,128)(2,1)S(1)} %collective-permute-done.22.refs_2_.refs_0_) | copy-start | bytes 1105924
  183.8 8.7 %copy-start.29 = (bf16[5,96,384]{2,1,0:T(8,128)(2,1)}, bf16[5,96,384]{2,1,0:T(8,128)(2,1)S(1)}, u32[]{:S(2)}) copy-start(bf16[5,96,384]{2,1,0:T(8,128)(2,1)S(1)} %collective-permute-done.23.refs_3_.refs_0_) | copy-start | bytes 1105924
  193.2 3.7 %collective-permute-start.25 = (bf16[9,96,384]{2,1,0:T(8,128)(2,1)}, bf16[9,96,384]{2,1,0:T(8,128)(2,1)S(1)}, u32[]{:S(2)}, u32[]{:S(2)}) collective-permute-start(bf16[9,96,384]{2,1,0:T(8,128)(2,1)} %after.25.refs_4_), channel_id=1, source_target_pairs={{0,1},{1,0},{2,3},{3,2},{4,5},{5,4},{6,7},{7,6},{8,9},{9,8},{10,11... | collective-permute-start | bytes 1990664 | tf_op jit(solution)/shard_map/ppermute | solution.py:27
  194.9 2.9 %collective-permute-start.26 = (bf16[9,96,384]{2,1,0:T(8,128)(2,1)}, bf16[9,96,384]{2,1,0:T(8,128)(2,1)S(1)}, u32[]{:S(2)}, u32[]{:S(2)}) collective-permute-start(bf16[9,96,384]{2,1,0:T(8,128)(2,1)} %after.26.refs_6_), channel_id=1, source_target_pairs={{0,1},{1,0},{2,3},{3,2},{4,5},{5,4},{6,7},{7,6},{8,9},{9,8},{10,11... | collective-permute-start | bytes 1990664 | tf_op jit(solution)/shard_map/ppermute | solution.py:27
  (24 other events, 24.4 us)

commit v14 on v13

--- a/solution.py
+++ b/solution.py
@@ -513,11 +513,12 @@
     near_rows = [(d, 0, coarse, 0) for d in range(3)]
     far_rows = [(3, 0, half, 0), (3, half, half, 0)]
     early = early_terms(place, near_rows, [act, beside, below], shifts, coarse)
-    far_top, far_bottom = after(far_top, early), after(far_bottom, early)
-
+    line_across[2] = after(line_across[2], early)
     lines = stack_planes(place, line_across)
+    far_top, far_bottom = after(far_top, early, lines), after(far_bottom, early, lines)
+
     to_beside, to_below = (
-        after(message, far_top, far_bottom, lines) for message in (to_beside, to_below)
+        after(message, far_top, far_bottom) for message in (to_beside, to_below)
     )
     kept_beside, kept_below = from_peer(to_beside, "seq", 1), from_peer(to_below, "seq", 2)
     other_column, other_lines = from_peer(to_below, "rep", 1), from_peer(lines, "rep", 1)
@@ -532,7 +533,7 @@
 
     window = (coarse + 2 * HALO) // rows
     count, side = planes * SPLIT, window // 2
-    kept_beside, kept_below = after(kept_beside, *leaving[1:]), after(kept_below, *leaving[1:])
+    kept_beside, kept_below = after(kept_beside, *summed), after(kept_below, *summed)
     far_first = from_peer(kept_beside[: side + count // 2], "seq", 2)
     far_second = from_peer(kept_below[count // 2 : count + side], "seq", 1)
     windows = [
@@ -557,7 +558,7 @@
     begun = stage(soon + [piece for piece in crossed if piece[-1] < 3], [0, 1, 2], begun=None)
     rest = [piece for piece in crossed if piece[-1] == 3]
     for part, start, plane in ((far_first, side, 0), (far_second, 0, planes // 2)):
-        part = after(part, begun, *summed)
+        part = after(part, begun)
         rest.append((part, start, plane, planes // 2, 0, 3))
         rest.append((from_peer(part, "rep", 1), start, plane, planes // 2, 1, 3))
     input_grad = stage(rest, [3], begun=begun)

time: 213 us -> 217 us (1.019)
  waiting for transfers between devices: 86.3 us -> 90.1 us
    ppermute x27, waiting for transfers between devices: 86.3 us -> 90.1 us  [from_peer(): return lax.ppermute(value, axis, [(i, i ^ distance) for i in range(peers)])]
    unnamed x92 -> x84, local copies, waits for them, and re-layouts: 23.1 us -> 23 us
  transfers between devices with their start and end apart: 27 -> 27, of which waited for: 10 -> 9; matrix products, arithmetic and copies ran while one was open for 10% -> 9% of each run, Pallas kernels for 21% -> 10%
where the time goes in v14:
time: 217 us; the launch traced here: 216 us
  waiting for transfers between devices  90.1 us (42%)
  Pallas kernels  55.8 us (26%)
  local copies, waits for them, and re-layouts  33.5 us (15%)
  starting transfers between devices  25.1 us (12%)
  other arithmetic  11 us (5%)
    ppermute x27, waiting for transfers between devices, from_peer(): return lax.ppermute(value, axis, [(i, i ^ distance) for i in range(peers)])  90.1 us
    ppermute x27, starting transfers between devices, from_peer(): return lax.ppermute(value, axis, [(i, i ^ distance) for i in range(peers)])  25.1 us
    pallas_call x2, Pallas kernels, gradient_stage(): pl.pallas_call(body, out_shape=out_shape, grid_spec=pltpu.PrefetchScalarG...  24.6 us
    unnamed x84, local copies, waits for them, and re-layouts  23 us
    pallas_call x1, Pallas kernels, early_terms(): pl.pallas_call(kernel, out_shape=jax.ShapeDtypeStruct((both, columns), jn...  13.8 us
    pallas_call x1, Pallas kernels, late_terms(): pl.pallas_call(kernel, out_shape=(jax.ShapeDtypeStruct(shape, jnp.float32...  9.3 us
    concatenate x1, other arithmetic, on_device_square(): shifts = jnp.concatenate([later, trunk, earlier], axis=1)  5.41 us
  transfers between devices with their start and end apart: 27, of which 9 were waited for; matrix products, arithmetic and copies ran while one was open for 9% of the time, Pallas kernels for 10%

profile of v14, /device:TPU:9, one launch (start us, length us, event | category | flops | bytes accessed | tf_op | source)
XLA Modules:
  0.0 216.5 jit_solution(18368947044941818079)
XLA Ops:
  0.6 1.0 slice.54.refs_0_
  1.6 1.4 collective-permute-start.1
  3.9 1.3 collective-permute-start.3
  5.2 1.2 collective-permute-start.4
  6.6 2.2 %collective-permute-start = (bf16[3,96,384]{2,1,0:T(8,128)(2,1)S(1)}, bf16[3,96,384]{2,1,0:T(8,128)(2,1)S(1)}, u32[]{:S(2)}, u32[]{:S(2)}) collective-permute-start(bf16[3,96,384]{2,1,0:T(8,128)(2,1)S(1)} %slice.54.refs_0_), channel_id=1, source_target_pairs={{0,2},{1,3},{2,0},{3,1},{4,6},{5,7},{6,4},{7,5},{8,10},{9,11},{10,... | collective-permute-start | bytes 663560 | tf_op jit(solution)/shard_map/ppermute | solution.py:27
  8.8 1.4 copy-done.11
  10.2 1.8 act.1.refs_0_
  12.0 1.1 copy-done.4
  14.5 1.2 collective-permute-start.6
  15.7 1.2 collective-permute-start.10
  17.0 2.1 slice_bitcast_fusion.1
  20.0 2.1 collective-permute-done.2.refs_2_
  22.9 5.4 %fusion.2.refs_2_.shifts_ref = bf16[2048,1152]{1,0:T(8,128)(2,1)} fusion(bf16[2047,384]{1,0:T(8,128)(2,1)} %get-tuple-element.16, bf16[2047,384]{1,0:T(8,128)(2,1)} %get-tuple-element.15, bf16[2048,384]{1,0:T(8,128)(2,1)S(1)} %bitcast.24), kind=kLoop, calls=%fused_computation.4 | loop fusion | flops 23592960 | bytes 9435648 | tf_op jit(solution)/shard_map/concatenate | solution.py:506
  28.3 2.3 %half_slope.1.refs_1_.refs_17_.refs_8_ = f32[2,512,768]{2,1,0:T(8,128)S(1)} custom-call(bf16[1,1024,768]{2,1,0:T(8,128)(2,1)S(1)} %copy-done.12), custom_call_target="tpu_custom_call" | custom-call | tf_op jit(solution)/shard_map/half_slope/pallas_call | solution.py:161
  30.7 1.6 copy-done.2
  33.3 2.2 kernel_messages.1
  35.5 1.1 copy-done.6
  36.6 12.0 %collective-permute-done.6.refs_1_ = bf16[512,1536]{1,0:T(8,128)(2,1)} collective-permute-done((bf16[512,1536]{1,0:T(8,128)(2,1)}, bf16[512,1536]{1,0:T(8,128)(2,1)}, u32[]{:S(2)}, u32[]{:S(2)}) %collective-permute-start.6) | collective-permute-done | bytes 1572896 | tf_op jit(solution)/shard_map/ppermute | solution.py:27
  48.6 2.1 slice.72.refs_0_
  51.7 1.2 collective-permute-start.9
  53.0 2.1 slice.73.refs_0_
  55.1 1.2 collective-permute-start.12
  56.5 13.8 %weight_grad_early.1.refs_1_.early_ref = f32[1536,1152]{1,0:T(8,128)} custom-call(s32[2]{0:T(128)S(1)} %pad_add_fusion.place, bf16[2048,1152]{1,0:T(8,128)(2,1)} %fusion.2.refs_2_.shifts_ref, bf16[512,1536]{1,0:T(8,128)(2,1)S(1)} %copy-done.5, bf16[512,1536]{1,0:T(8,128)(2,1)} %collective-permute-done.6.refs_1_, ...), custom_call_target="tpu_custom_call" | custom-call | flops 1048576 | bytes 65536 | tf_op jit(solution)/shard_map/weight_grad_early/pallas_call | solution.py:209
  70.3 1.0 copy-done.13
  71.7 1.8 stack_planes.1.refs_2_.refs_11_.refs_12_.refs_13_
  73.5 1.4 copy-done
  77.2 1.1 copy-done.10
  78.4 9.3 %weight_grad_late.1 = (f32[4,5,96,384]{3,2,1,0:T(8,128)S(1)}, bf16[4,5,96,384]{3,2,1,0:T(8,128)(2,1)}) custom-call(s32[2]{0:T(128)S(1)} %pad_add_fusion.place, bf16[2048,1152]{1,0:T(8,128)(2,1)} %fusion.2.refs_2_.shifts_ref, f32[1536,1152]{1,0:T(8,128)} %weight_grad_early.1.refs_1_.early_ref, bf16[256,1536]{1,0:T(8,128)(2,1)S(1)} %copy-done.8, ...), custom_call_target="tpu_custom_call" | custom-call | flops 1048576 | bytes 65536 | tf_op jit(solution)/shard_map/weight_grad_late/pallas_call | solution.py:279
  87.7 1.6 copy-done.18
  89.3 3.6 %collective-permute-start.14 = (bf16[4,5,96,384]{3,2,1,0:T(8,128)(2,1)}, bf16[4,5,96,384]{3,2,1,0:T(8,128)(2,1)}, u32[]{:S(2)}, u32[]{:S(2)}) collective-permute-start(bf16[4,5,96,384]{3,2,1,0:T(8,128)(2,1)} %get-tuple-element.9), channel_id=1, source_target_pairs={{0,1},{1,0},{2,3},{3,2},{4,5},{5,4},{6,7},{7,6},{8,9},{9,8},{10,11... | collective-permute-start | bytes 4423688 | tf_op jit(solution)/shard_map/ppermute | solution.py:27
  94.5 1.0 copy-done.1
  96.2 2.1 fusion.8
  98.3 1.5 collective-permute-start.15
  99.8 28.9 %collective-permute-done.13.refs_0_ = bf16[21,96,384]{2,1,0:T(8,128)(2,1)} collective-permute-done((bf16[21,96,384]{2,1,0:T(8,128)(2,1)}, bf16[21,96,384]{2,1,0:T(8,128)(2,1)}, u32[]{:S(2)}, u32[]{:S(2)}) %collective-permute-start.13) | collective-permute-done | bytes 1548320 | tf_op jit(solution)/shard_map/ppermute | solution.py:27
  129.6 16.5 %collective-permute-done.17.refs_3_.refs_0_ = bf16[5,96,384]{2,1,0:T(8,128)(2,1)} collective-permute-done((bf16[5,96,384]{2,1,0:T(8,128)(2,1)S(1)}, bf16[5,96,384]{2,1,0:T(8,128)(2,1)}, u32[]{:S(2)}, u32[]{:S(2)}) %collective-permute-start.17) | collective-permute-done | bytes 368672 | tf_op jit(solution)/shard_map/ppermute | solution.py:27
  146.1 1.7 collective-permute-start.23
  147.9 1.2 slice.77
  149.0 1.1 collective-permute-start.18
  150.1 1.2 slice.78
  151.3 13.8 %collective-permute-done.18.refs_3_.refs_0_ = bf16[9,96,384]{2,1,0:T(8,128)(2,1)S(1)} collective-permute-done((bf16[9,96,384]{2,1,0:T(8,128)(2,1)S(1)}, bf16[9,96,384]{2,1,0:T(8,128)(2,1)S(1)}, u32[]{:S(2)}, u32[]{:S(2)}) %collective-permute-start.18) | collective-permute-done | bytes 663584 | tf_op jit(solution)/shard_map/ppermute | solution.py:27
  166.9 13.4 %collective-permute-done.20.refs_4_.refs_1_ = bf16[9,96,384]{2,1,0:T(8,128)(2,1)S(1)} collective-permute-done((bf16[9,96,384]{2,1,0:T(8,128)(2,1)S(1)}, bf16[9,96,384]{2,1,0:T(8,128)(2,1)S(1)}, u32[]{:S(2)}, u32[]{:S(2)}) %collective-permute-start.20) | collective-permute-done | bytes 663584 | tf_op jit(solution)/shard_map/ppermute | solution.py:27
  181.3 1.0 copy-done.32
  182.3 15.1 %input_grad.2.refs_1_.refs_9_ = f32[2,512,768]{2,1,0:T(8,128)} custom-call(s32[2]{0:T(128)} %copy-done.26, bf16[6,96,384]{2,1,0:T(8,128)(2,1)} %copy-done.25, bf16[21,96,384]{2,1,0:T(8,128)(2,1)} %after.24.refs_1_.refs_7_, bf16[21,96,384]{2,1,0:T(8,128)(2,1)} %after.26.refs_2_.refs_9_, bf16[9,96,384]{2,1,0:T(8,128)(2,1)} %copy-done.27, ...), custom_call_target="tpu_custom_call" | custom-call | flops 1048576 | bytes 65536 | tf_op jit(solution)/shard_map/input_grad/pallas_call | solution.py:445
  197.4 2.3 %collective-permute-start.25 = (bf16[9,96,384]{2,1,0:T(8,128)(2,1)}, bf16[9,96,384]{2,1,0:T(8,128)(2,1)S(1)}, u32[]{:S(2)}, u32[]{:S(2)}) collective-permute-start(bf16[9,96,384]{2,1,0:T(8,128)(2,1)} %after.27.refs_4_), channel_id=1, source_target_pairs={{0,1},{1,0},{2,3},{3,2},{4,5},{5,4},{6,7},{7,6},{8,9},{9,8},{10,11... | collective-permute-start | bytes 1990664 | tf_op jit(solution)/shard_map/ppermute | solution.py:27
  199.8 1.9 collective-permute-done.25.refs_5_
  203.5 9.5 %input_grad.3.refs_1_ = bf16[1,1024,768]{2,1,0:T(8,128)(2,1)} custom-call(s32[2]{0:T(128)} %copy-done.26, bf16[9,96,384]{2,1,0:T(8,128)(2,1)} %copy-done.27, bf16[9,96,384]{2,1,0:T(8,128)(2,1)} %copy-done.28, bf16[4,4,2,96,384]{4,3,2,1,0:T(8,128)(2,1)} %copy-done, bf16[4,4,2,96,384]{4,3,2,1,0:T(8,128)(2,1)} %collective-permute-done.21.refs_14_.refs_15_.refs_16_.refs_3_, ...), custom_call_target="tpu_custom_call" | custom-call | flops 1048576 | bytes 65536 | tf_op jit(solution)/shard_map/input_grad/pallas_call | solution.py:445
  213.0 1.0 copy-done.31
  214.0 2.5 %fusion.5 = f32[5,96,384]{2,1,0:T(8,128)} fusion(bf16[5,96,384]{2,1,0:T(8,128)(2,1)} %after.31, bf16[5,96,384]{2,1,0:T(8,128)(2,1)S(1)} %copy-done.31, bf16[5,96,384]{2,1,0:T(8,128)(2,1)} %after.29, f32[4,5,96,384]{3,2,1,0:T(8,128)} %copy-done.18, bf16[4,5,96,384]{3,2,1,0:T(8,128)(2,1)} %collective-permute-done.14), kind=kLoop, calls=%fused_computation.10 | loop fusion | flops 1474560 | bytes 2949120 | tf_op jit(solution)/shard_map/add | solution.py:566
  (126 shorter events, 17.0 us)
Async XLA Ops:
  1.6 15.4 %collective-permute-start.1 = (bf16[3,96,384]{2,1,0:T(8,128)(2,1)S(1)}, bf16[3,96,384]{2,1,0:T(8,128)(2,1)S(1)}, u32[]{:S(2)}, u32[]{:S(2)}) collective-permute-start(bf16[3,96,384]{2,1,0:T(8,128)(2,1)S(1)} %slice.54.refs_0_), channel_id=1, source_target_pairs={{0,6},{1,7},{2,4},{3,5},{4,2},{5,3},{6,0},{7,1},{8,14},{9,15},{10,... | collective-permute-start | bytes 663560 | tf_op jit(solution)/shard_map/ppermute | solution.py:27
  3.9 9.2 %collective-permute-start.3 = (bf16[2,96,384]{2,1,0:T(8,128)(2,1)S(1)}, bf16[2,96,384]{2,1,0:T(8,128)(2,1)S(1)}, u32[]{:S(2)}, u32[]{:S(2)}) collective-permute-start(bf16[2,96,384]{2,1,0:T(8,128)(2,1)S(1)} %get-tuple-element.18), channel_id=1, source_target_pairs={{0,8},{8,0},{16,24},{24,16},{1,9},{9,1},{17,25},{25,17},{2,10},{10... | collective-permute-start | bytes 442376 | tf_op jit(solution)/shard_map/ppermute | solution.py:27
  5.2 8.0 %collective-permute-start.4 = (bf16[2,96,384]{2,1,0:T(8,128)(2,1)S(1)}, bf16[2,96,384]{2,1,0:T(8,128)(2,1)S(1)}, u32[]{:S(2)}, u32[]{:S(2)}) collective-permute-start(bf16[2,96,384]{2,1,0:T(8,128)(2,1)S(1)} %get-tuple-element.18), channel_id=1, source_target_pairs={{0,16},{8,24},{16,0},{24,8},{1,17},{9,25},{17,1},{25,9},{2,18},{10... | collective-permute-start | bytes 442376 | tf_op jit(solution)/shard_map/ppermute | solution.py:27
  6.4 6.7 %collective-permute-start.5 = (bf16[2,96,384]{2,1,0:T(8,128)(2,1)S(1)}, bf16[2,96,384]{2,1,0:T(8,128)(2,1)S(1)}, u32[]{:S(2)}, u32[]{:S(2)}) collective-permute-start(bf16[2,96,384]{2,1,0:T(8,128)(2,1)S(1)} %get-tuple-element.18), channel_id=1, source_target_pairs={{0,24},{8,16},{16,8},{24,0},{1,25},{9,17},{17,9},{25,1},{2,26},{10... | collective-permute-start | bytes 442376 | tf_op jit(solution)/shard_map/ppermute | solution.py:27
  6.6 13.4 %collective-permute-start = (bf16[3,96,384]{2,1,0:T(8,128)(2,1)S(1)}, bf16[3,96,384]{2,1,0:T(8,128)(2,1)S(1)}, u32[]{:S(2)}, u32[]{:S(2)}) collective-permute-start(bf16[3,96,384]{2,1,0:T(8,128)(2,1)S(1)} %slice.54.refs_0_), channel_id=1, source_target_pairs={{0,2},{1,3},{2,0},{3,1},{4,6},{5,7},{6,4},{7,5},{8,10},{9,11},{10,... | collective-permute-start | bytes 663560 | tf_op jit(solution)/shard_map/ppermute | solution.py:27
  8.8 1.4 copy-start.11
  13.1 3.8 %copy-start.3 = (bf16[1,2048,384]{2,1,0:T(8,128)(2,1)S(1)}, bf16[1,2048,384]{2,1,0:T(8,128)(2,1)}, u32[]{:S(2)}) copy-start(bf16[1,2048,384]{2,1,0:T(8,128)(2,1)} %refs_4_.1) | copy-start | bytes 4718596
  14.5 4.6 %copy-start.36 = (bf16[2,96,384]{2,1,0:T(8,128)(2,1)S(1)}, bf16[2,96,384]{2,1,0:T(8,128)(2,1)}, u32[]{:S(2)}) copy-start(bf16[2,96,384]{2,1,0:T(8,128)(2,1)} %copy-done.35) | copy-start | bytes 442372
  14.5 4.6 %copy-start.38 = (bf16[2,96,384]{2,1,0:T(8,128)(2,1)S(1)}, bf16[2,96,384]{2,1,0:T(8,128)(2,1)}, u32[]{:S(2)}) copy-start(bf16[2,96,384]{2,1,0:T(8,128)(2,1)} %copy-done.37) | copy-start | bytes 442372
  14.5 4.6 %copy-start.40 = (bf16[2,96,384]{2,1,0:T(8,128)(2,1)S(1)}, bf16[2,96,384]{2,1,0:T(8,128)(2,1)}, u32[]{:S(2)}) copy-start(bf16[2,96,384]{2,1,0:T(8,128)(2,1)} %copy-done.39) | copy-start | bytes 442372
  14.5 34.1 %collective-permute-start.6 = (bf16[512,1536]{1,0:T(8,128)(2,1)}, bf16[512,1536]{1,0:T(8,128)(2,1)}, u32[]{:S(2)}, u32[]{:S(2)}) collective-permute-start(bf16[512,1536]{1,0:T(8,128)(2,1)} %after.16.refs_0_), channel_id=1, source_target_pairs={{0,8},{8,0},{16,24},{24,16},{1,9},{9,1},{17,25},{25,17},{2,10},{10... | collective-permute-start | bytes 4718600 | tf_op jit(solution)/shard_map/ppermute | solution.py:27
  15.7 37.3 %collective-permute-start.10 = (bf16[512,1536]{1,0:T(8,128)(2,1)}, bf16[512,1536]{1,0:T(8,128)(2,1)}, u32[]{:S(2)}, u32[]{:S(2)}) collective-permute-start(bf16[512,1536]{1,0:T(8,128)(2,1)} %after.16.refs_0_), channel_id=1, source_target_pairs={{0,16},{8,24},{16,0},{24,8},{1,17},{9,25},{17,1},{25,9},{2,18},{10... | collective-permute-start | bytes 4718600 | tf_op jit(solution)/shard_map/ppermute | solution.py:27
  17.0 2.1 copy-start.19
  17.0 5.2 %collective-permute-start.2 = (bf16[3,96,384]{2,1,0:T(8,128)(2,1)S(1)}, bf16[3,96,384]{2,1,0:T(8,128)(2,1)S(1)}, u32[]{:S(2)}, u32[]{:S(2)}) collective-permute-start(bf16[3,96,384]{2,1,0:T(8,128)(2,1)S(1)} %collective-permute-done.1.refs_3_), channel_id=1, source_target_pairs={{0,2},{1,3},{2,0},{3,1},{4,6},{5,7},{6,4},{7,5},{8,10},{9,11},{10,... | collective-permute-start | bytes 663560 | tf_op jit(solution)/shard_map/ppermute | solution.py:27
  20.0 2.1 copy-start.21
  22.8 27.9 %collective-permute-start.7 = (bf16[4,2,96,384]{3,2,1,0:T(8,128)(2,1)}, bf16[4,2,96,384]{3,2,1,0:T(8,128)(2,1)S(1)}, u32[]{:S(2)}, u32[]{:S(2)}) collective-permute-start(bf16[4,2,96,384]{3,2,1,0:T(8,128)(2,1)} %after.17.refs_0_), channel_id=1, source_target_pairs={{0,2},{1,3},{2,0},{3,1},{4,6},{5,7},{6,4},{7,5},{8,10},{9,11},{10,... | collective-permute-start | bytes 1769480 | tf_op jit(solution)/shard_map/ppermute | solution.py:27
  22.9 27.8 %collective-permute-start.8 = (bf16[4,2,96,384]{3,2,1,0:T(8,128)(2,1)}, bf16[4,2,96,384]{3,2,1,0:T(8,128)(2,1)S(1)}, u32[]{:S(2)}, u32[]{:S(2)}) collective-permute-start(bf16[4,2,96,384]{3,2,1,0:T(8,128)(2,1)} %after.17.refs_0_), channel_id=1, source_target_pairs={{0,6},{1,7},{2,4},{3,5},{4,2},{5,3},{6,0},{7,1},{8,14},{9,15},{10,... | collective-permute-start | bytes 1769480 | tf_op jit(solution)/shard_map/ppermute | solution.py:27
  22.9 5.4 %copy-start.12 = (bf16[1,1024,768]{2,1,0:T(8,128)(2,1)S(1)}, bf16[1,1024,768]{2,1,0:T(8,128)(2,1)}, u32[]{:S(2)}) copy-start(bf16[1,1024,768]{2,1,0:T(8,128)(2,1)} %x_ref.3) | copy-start | bytes 4718596
  28.3 4.1 %copy-start.20 = (bf16[3,96,384]{2,1,0:T(8,128)(2,1)S(1)}, bf16[3,96,384]{2,1,0:T(8,128)(2,1)}, u32[]{:S(2)}) copy-start(bf16[3,96,384]{2,1,0:T(8,128)(2,1)} %copy-done.19) | copy-start | bytes 663556
  28.3 4.1 %copy-start.22 = (bf16[3,96,384]{2,1,0:T(8,128)(2,1)S(1)}, bf16[3,96,384]{2,1,0:T(8,128)(2,1)}, u32[]{:S(2)}) copy-start(bf16[3,96,384]{2,1,0:T(8,128)(2,1)} %copy-done.21) | copy-start | bytes 663556
  30.6 1.6 copy-start.2
  33.3 43.4 %copy-start.26 = (s32[2]{0:T(128)}, s32[2]{0:T(128)S(1)}, u32[]{:S(2)}) copy-start(s32[2]{0:T(128)S(1)} %pad_add_fusion.place) | copy-start | bytes 28
  36.6 14.1 %copy-start.25 = (bf16[6,96,384]{2,1,0:T(8,128)(2,1)}, bf16[6,96,384]{2,1,0:T(8,128)(2,1)S(1)}, u32[]{:S(2)}) copy-start(bf16[6,96,384]{2,1,0:T(8,128)(2,1)S(1)} %get-tuple-element.11.refs_0_) | copy-start | bytes 1327108
  51.7 23.2 %collective-permute-start.9 = (bf16[256,1536]{1,0:T(8,128)(2,1)}, bf16[256,1536]{1,0:T(8,128)(2,1)S(1)}, u32[]{:S(2)}, u32[]{:S(2)}) collective-permute-start(bf16[256,1536]{1,0:T(8,128)(2,1)} %after.18), channel_id=1, source_target_pairs={{0,16},{8,24},{16,0},{24,8},{1,17},{9,25},{17,1},{25,9},{2,18},{10... | collective-permute-start | bytes 2359304 | tf_op jit(solution)/shard_map/ppermute | solution.py:27
  55.1 1.4 copy-start.5
  55.1 20.7 %collective-permute-start.12 = (bf16[256,1536]{1,0:T(8,128)(2,1)}, bf16[256,1536]{1,0:T(8,128)(2,1)S(1)}, u32[]{:S(2)}, u32[]{:S(2)}) collective-permute-start(bf16[256,1536]{1,0:T(8,128)(2,1)} %after.21), channel_id=1, source_target_pairs={{0,8},{8,0},{16,24},{24,16},{1,9},{9,1},{17,25},{25,17},{2,10},{10... | collective-permute-start | bytes 2359304 | tf_op jit(solution)/shard_map/ppermute | solution.py:27
  56.3 14.0 %collective-permute-start.11 = (bf16[4,2,96,384]{3,2,1,0:T(8,128)(2,1)}, bf16[4,2,96,384]{3,2,1,0:T(8,128)(2,1)}, u32[]{:S(2)}, u32[]{:S(2)}) collective-permute-start(bf16[4,2,96,384]{3,2,1,0:T(8,128)(2,1)} %copy-done.16), channel_id=1, source_target_pairs={{0,2},{1,3},{2,0},{3,1},{4,6},{5,7},{6,4},{7,5},{8,10},{9,11},{10,... | collective-permute-start | bytes 1769480 | tf_op jit(solution)/shard_map/ppermute | solution.py:27
  70.3 1.4 copy-start.17
  75.8 1.4 copy-start.8
  87.7 1.6 copy-start.18
  89.3 6.9 %collective-permute-start.14 = (bf16[4,5,96,384]{3,2,1,0:T(8,128)(2,1)}, bf16[4,5,96,384]{3,2,1,0:T(8,128)(2,1)}, u32[]{:S(2)}, u32[]{:S(2)}) collective-permute-start(bf16[4,5,96,384]{3,2,1,0:T(8,128)(2,1)} %get-tuple-element.9), channel_id=1, source_target_pairs={{0,1},{1,0},{2,3},{3,2},{4,5},{5,4},{6,7},{7,6},{8,9},{9,8},{10,11... | collective-permute-start | bytes 4423688 | tf_op jit(solution)/shard_map/ppermute | solution.py:27
  92.9 35.8 %collective-permute-start.13 = (bf16[21,96,384]{2,1,0:T(8,128)(2,1)}, bf16[21,96,384]{2,1,0:T(8,128)(2,1)}, u32[]{:S(2)}, u32[]{:S(2)}) collective-permute-start(bf16[21,96,384]{2,1,0:T(8,128)(2,1)} %after.23), channel_id=1, source_target_pairs={{0,8},{8,0},{16,24},{24,16},{1,9},{9,1},{17,25},{25,17},{2,10},{10... | collective-permute-start | bytes 4644872 | tf_op jit(solution)/shard_map/ppermute | solution.py:27
  93.8 1.7 copy-start.1
  93.8 54.0 %collective-permute-start.19 = (bf16[21,96,384]{2,1,0:T(8,128)(2,1)}, bf16[21,96,384]{2,1,0:T(8,128)(2,1)}, u32[]{:S(2)}, u32[]{:S(2)}) collective-permute-start(bf16[21,96,384]{2,1,0:T(8,128)(2,1)} %after.25.refs_5_), channel_id=1, source_target_pairs={{0,16},{8,24},{16,0},{24,8},{1,17},{9,25},{17,1},{25,9},{2,18},{10... | collective-permute-start | bytes 4644872 | tf_op jit(solution)/shard_map/ppermute | solution.py:27
  95.4 85.7 %collective-permute-start.21 = (bf16[4,4,2,96,384]{4,3,2,1,0:T(8,128)(2,1)S(1)}, bf16[4,4,2,96,384]{4,3,2,1,0:T(8,128)(2,1)}, u32[]{:S(2)}, u32[]{:S(2)}) collective-permute-start(bf16[4,4,2,96,384]{4,3,2,1,0:T(8,128)(2,1)S(1)} %copy-done.1), channel_id=1, source_target_pairs={{0,1},{1,0},{2,3},{3,2},{4,5},{5,4},{6,7},{7,6},{8,9},{9,8},{10,11... | collective-permute-start | bytes 7077896 | tf_op jit(solution)/shard_map/ppermute | solution.py:27
  98.3 30.5 %collective-permute-start.15 = (bf16[5,96,384]{2,1,0:T(8,128)(2,1)S(1)}, bf16[5,96,384]{2,1,0:T(8,128)(2,1)S(1)}, u32[]{:S(2)}, u32[]{:S(2)}) collective-permute-start(bf16[5,96,384]{2,1,0:T(8,128)(2,1)S(1)} %get-tuple-element.14), channel_id=1, source_target_pairs={{0,2},{1,3},{2,0},{3,1},{4,6},{5,7},{6,4},{7,5},{8,10},{9,11},{10,... | collective-permute-start | bytes 1105928 | tf_op jit(solution)/shard_map/ppermute | solution.py:27
  99.8 29.8 %collective-permute-start.16 = (bf16[5,96,384]{2,1,0:T(8,128)(2,1)S(1)}, bf16[5,96,384]{2,1,0:T(8,128)(2,1)S(1)}, u32[]{:S(2)}, u32[]{:S(2)}) collective-permute-start(bf16[5,96,384]{2,1,0:T(8,128)(2,1)S(1)} %get-tuple-element.13), channel_id=1, source_target_pairs={{0,4},{1,5},{2,6},{3,7},{4,0},{5,1},{6,2},{7,3},{8,12},{9,13},{10,... | collective-permute-start | bytes 1105928 | tf_op jit(solution)/shard_map/ppermute | solution.py:27
  128.7 17.3 %collective-permute-start.17 = (bf16[5,96,384]{2,1,0:T(8,128)(2,1)S(1)}, bf16[5,96,384]{2,1,0:T(8,128)(2,1)}, u32[]{:S(2)}, u32[]{:S(2)}) collective-permute-start(bf16[5,96,384]{2,1,0:T(8,128)(2,1)S(1)} %get-tuple-element.12), channel_id=1, source_target_pairs={{0,6},{1,7},{2,4},{3,5},{4,2},{5,3},{6,0},{7,1},{8,14},{9,15},{10,... | collective-permute-start | bytes 1105928 | tf_op jit(solution)/shard_map/ppermute | solution.py:27
  128.7 17.3 %copy-start.29 = (bf16[5,96,384]{2,1,0:T(8,128)(2,1)}, bf16[5,96,384]{2,1,0:T(8,128)(2,1)S(1)}, u32[]{:S(2)}) copy-start(bf16[5,96,384]{2,1,0:T(8,128)(2,1)S(1)} %collective-permute-done.15.refs_1_.refs_0_) | copy-start | bytes 1105924
  128.7 52.4 %collective-permute-start.22 = (bf16[21,96,384]{2,1,0:T(8,128)(2,1)}, bf16[21,96,384]{2,1,0:T(8,128)(2,1)}, u32[]{:S(2)}, u32[]{:S(2)}) collective-permute-start(bf16[21,96,384]{2,1,0:T(8,128)(2,1)} %after.25.refs_5_), channel_id=1, source_target_pairs={{0,1},{1,0},{2,3},{3,2},{4,5},{5,4},{6,7},{7,6},{8,9},{9,8},{10,11... | collective-permute-start | bytes 4644872 | tf_op jit(solution)/shard_map/ppermute | solution.py:27
  129.6 16.5 %copy-start.30 = (bf16[5,96,384]{2,1,0:T(8,128)(2,1)}, bf16[5,96,384]{2,1,0:T(8,128)(2,1)S(1)}, u32[]{:S(2)}) copy-start(bf16[5,96,384]{2,1,0:T(8,128)(2,1)S(1)} %collective-permute-done.16.refs_2_.refs_0_) | copy-start | bytes 1105924
  146.1 35.1 %collective-permute-start.23 = (bf16[21,96,384]{2,1,0:T(8,128)(2,1)}, bf16[21,96,384]{2,1,0:T(8,128)(2,1)}, u32[]{:S(2)}, u32[]{:S(2)}) collective-permute-start(bf16[21,96,384]{2,1,0:T(8,128)(2,1)} %after.24.refs_1_.refs_7_), channel_id=1, source_target_pairs={{0,1},{1,0},{2,3},{3,2},{4,5},{5,4},{6,7},{7,6},{8,9},{9,8},{10,11... | collective-permute-start | bytes 4644872 | tf_op jit(solution)/shard_map/ppermute | solution.py:27
  147.8 33.4 %collective-permute-start.24 = (bf16[21,96,384]{2,1,0:T(8,128)(2,1)}, bf16[21,96,384]{2,1,0:T(8,128)(2,1)S(1)}, u32[]{:S(2)}, u32[]{:S(2)}) collective-permute-start(bf16[21,96,384]{2,1,0:T(8,128)(2,1)} %after.26.refs_2_.refs_9_), channel_id=1, source_target_pairs={{0,1},{1,0},{2,3},{3,2},{4,5},{5,4},{6,7},{7,6},{8,9},{9,8},{10,11... | collective-permute-start | bytes 4644872 | tf_op jit(solution)/shard_map/ppermute | solution.py:27
  149.0 16.1 %collective-permute-start.18 = (bf16[9,96,384]{2,1,0:T(8,128)(2,1)S(1)}, bf16[9,96,384]{2,1,0:T(8,128)(2,1)S(1)}, u32[]{:S(2)}, u32[]{:S(2)}) collective-permute-start(bf16[9,96,384]{2,1,0:T(8,128)(2,1)S(1)} %slice.77), channel_id=1, source_target_pairs={{0,16},{8,24},{16,0},{24,8},{1,17},{9,25},{17,1},{25,9},{2,18},{10... | collective-permute-start | bytes 1990664 | tf_op jit(solution)/shard_map/ppermute | solution.py:27
  165.1 16.0 %copy-start.27 = (bf16[9,96,384]{2,1,0:T(8,128)(2,1)}, bf16[9,96,384]{2,1,0:T(8,128)(2,1)S(1)}, u32[]{:S(2)}) copy-start(bf16[9,96,384]{2,1,0:T(8,128)(2,1)S(1)} %collective-permute-done.18.refs_3_.refs_0_) | copy-start | bytes 1990660
  165.1 15.1 %collective-permute-start.20 = (bf16[9,96,384]{2,1,0:T(8,128)(2,1)S(1)}, bf16[9,96,384]{2,1,0:T(8,128)(2,1)S(1)}, u32[]{:S(2)}, u32[]{:S(2)}) collective-permute-start(bf16[9,96,384]{2,1,0:T(8,128)(2,1)S(1)} %slice.78), channel_id=1, source_target_pairs={{0,8},{8,0},{16,24},{24,16},{1,9},{9,1},{17,25},{25,17},{2,10},{10... | collective-permute-start | bytes 1990664 | tf_op jit(solution)/shard_map/ppermute | solution.py:27
  197.4 4.2 %collective-permute-start.25 = (bf16[9,96,384]{2,1,0:T(8,128)(2,1)}, bf16[9,96,384]{2,1,0:T(8,128)(2,1)S(1)}, u32[]{:S(2)}, u32[]{:S(2)}) collective-permute-start(bf16[9,96,384]{2,1,0:T(8,128)(2,1)} %after.27.refs_4_), channel_id=1, source_target_pairs={{0,1},{1,0},{2,3},{3,2},{4,5},{5,4},{6,7},{7,6},{8,9},{9,8},{10,11... | collective-permute-start | bytes 1990664 | tf_op jit(solution)/shard_map/ppermute | solution.py:27
  199.7 2.9 %collective-permute-start.26 = (bf16[9,96,384]{2,1,0:T(8,128)(2,1)}, bf16[9,96,384]{2,1,0:T(8,128)(2,1)S(1)}, u32[]{:S(2)}, u32[]{:S(2)}) collective-permute-start(bf16[9,96,384]{2,1,0:T(8,128)(2,1)} %after.28.refs_6_), channel_id=1, source_target_pairs={{0,1},{1,0},{2,3},{3,2},{4,5},{5,4},{6,7},{7,6},{8,9},{9,8},{10,11... | collective-permute-start | bytes 1990664 | tf_op jit(solution)/shard_map/ppermute | solution.py:27
  (20 other events, 19.4 us)

commit v15 on v14

--- a/solution.py
+++ b/solution.py
@@ -235,8 +235,8 @@
     shape = (planes, taps, rows, block)
 
     def kernel(place, shifts_ref, early_ref, *refs):
-        pieces, (mine_ref, theirs_ref) = refs[: len(layout)], refs[len(layout) : len(layout) + 2]
-        held, shifts, total, sems, shift_sems, early_sems = refs[len(layout) + 2 :]
+        pieces, (mine_ref, *theirs_refs) = refs[: len(layout)], refs[len(layout) : len(layout) + 3]
+        held, shifts, total, sems, shift_sems, early_sems = refs[len(layout) + 3 :]
         core, plane = place[1] % 2, place[1] // 2
         copies = start_act(
             place, coarse, layout, pieces, shifts_ref, held, shifts, sems, shift_sems
@@ -260,33 +260,40 @@
             fetch(i).wait()
             total[span, :] += term
 
-        for out_ref, parity, kind in (
-            (theirs_ref, 1 - core, jnp.bfloat16),
-            (mine_ref, core, jnp.float32),
-        ):
-
-            @pl.loop(0, planes)
-            def _(j):
-                start = ((plane ^ j) * 2 + parity) * rows
-                even = pl.ds(pl.multiple_of(start, 16), rows)
-                odd = pl.ds(pl.multiple_of(width + start, 16), rows)
-                for k, (left, right) in enumerate(GRAD_PARTS):
-                    term = total[even, left * block : (left + 1) * block]
-                    term += total[odd, right * block : (right + 1) * block]
-                    out_ref[j, k] = (scale * term).astype(kind)
-
+        def finish(out_ref, at, j, parity, kind):
+            start = ((plane ^ j) * 2 + parity) * rows
+            even = pl.ds(pl.multiple_of(start, 16), rows)
+            odd = pl.ds(pl.multiple_of(width + start, 16), rows)
+            for k, (left, right) in enumerate(GRAD_PARTS):
+                term = total[even, left * block : (left + 1) * block]
+                term += total[odd, right * block : (right + 1) * block]
+                out_ref[at, k] = (scale * term).astype(kind)
+
+        for which, out_ref in enumerate(theirs_refs):
+
+            @pl.loop(0, planes // 2)
+            def _(at):
+                finish(out_ref, at, at + which * (planes // 2), 1 - core, jnp.bfloat16)
+
+        @pl.loop(0, planes)
+        def _(j):
+            finish(mine_ref, j, j, core, jnp.float32)
+
+    half_shape = (planes // 2, *shape[1:])
     whole = pl.BlockSpec(shape, lambda i, place: (0, 0, 0, 0))
+    half = pl.BlockSpec(half_shape, lambda i, place: (0, 0, 0, 0))
     return pl.pallas_call(
         kernel,
         out_shape=(
             jax.ShapeDtypeStruct(shape, jnp.float32),
-            jax.ShapeDtypeStruct(shape, jnp.bfloat16),
+            jax.ShapeDtypeStruct(half_shape, jnp.bfloat16),
+            jax.ShapeDtypeStruct(half_shape, jnp.bfloat16),
         ),
         grid_spec=pltpu.PrefetchScalarGridSpec(
             num_scalar_prefetch=1,
             grid=(1,),
             in_specs=[ANYWHERE] * (2 + len(pieces)),
-            out_specs=[whole, whole],
+            out_specs=[whole, half, half],
             scratch_shapes=[
                 pltpu.VMEM((count, both), jnp.bfloat16),
                 pltpu.VMEM((count, columns), jnp.bfloat16),
@@ -523,13 +530,17 @@
     kept_beside, kept_below = from_peer(to_beside, "seq", 1), from_peer(to_below, "seq", 2)
     other_column, other_lines = from_peer(to_below, "rep", 1), from_peer(lines, "rep", 1)
 
-    mine, theirs = late_terms(
+    mine, *theirs = late_terms(
         place, far_rows, [far_top, far_bottom], shifts, early, coarse, scale, planes, taps, rows
     )
-    arrived = from_peer(theirs, "rep", 1)
-    weight_grad = mine[0] + arrived[0].astype(jnp.float32)
-    leaving = [(mine[j] + arrived[j].astype(jnp.float32)).astype(jnp.bfloat16) for j in range(planes)]
-    summed = [from_peer(leaving[j], "rep", 2 * j) for j in range(1, planes)]
+    arrived = [from_peer(part, "rep", 1) for part in theirs]
+    pairs = []
+    for j in range(planes):
+        part = arrived[j // (planes // 2)][j % (planes // 2)]
+        pairs.append(mine[j] + part.astype(jnp.float32))
+    weight_grad = pairs[0]
+    leaving = [after(part.astype(jnp.bfloat16), other_column, other_lines) for part in pairs[1:]]
+    summed = [from_peer(leaving[j - 1], "rep", 2 * j) for j in range(1, planes)]
 
     window = (coarse + 2 * HALO) // rows
     count, side = planes * SPLIT, window // 2

time: 217 us -> 203 us (0.935)
  waiting for transfers between devices: 90.1 us -> 77.4 us
  starting transfers between devices: 25.1 us -> 29.8 us
  local copies, waits for them, and re-layouts: 33.5 us -> 29.5 us
    ppermute x27 -> x28, waiting for transfers between devices: 90.1 us -> 77.4 us  [from_peer(): return lax.ppermute(value, axis, [(i, i ^ distance) for i in range(peers)])]
    ppermute x27 -> x28, starting transfers between devices: 25.1 us -> 29.8 us  [from_peer(): return lax.ppermute(value, axis, [(i, i ^ distance) for i in range(peers)])]
    unnamed x84 -> x76, local copies, waits for them, and re-layouts: 23 us -> 20.3 us
    concatenate x1, other arithmetic: 5.41 us -> 2.97 us  [on_device_square(): shifts = jnp.concatenate([later, trunk, earlier], axis=1)]
  transfers between devices with their start and end apart: 27 -> 28, of which waited for: 9 -> 12; matrix products, arithmetic and copies ran while one was open for 9% -> 8% of each run, Pallas kernels for 10% -> 15%
where the time goes in v15:
time: 203 us; the launch traced here: 202 us
  waiting for transfers between devices  77.4 us (38%)
  Pallas kernels  55.2 us (27%)
  starting transfers between devices  29.8 us (15%)
  local copies, waits for them, and re-layouts  29.5 us (15%)
  other arithmetic  9.44 us (5%)
    ppermute x28, waiting for transfers between devices, from_peer(): return lax.ppermute(value, axis, [(i, i ^ distance) for i in range(peers)])  77.4 us
    ppermute x28, starting transfers between devices, from_peer(): return lax.ppermute(value, axis, [(i, i ^ distance) for i in range(peers)])  29.8 us
    pallas_call x2, Pallas kernels, gradient_stage(): pl.pallas_call(body, out_shape=out_shape, grid_spec=pltpu.PrefetchScalarG...  24.6 us
    unnamed x76, local copies, waits for them, and re-layouts  20.3 us
    pallas_call x1, Pallas kernels, early_terms(): pl.pallas_call(kernel, out_shape=jax.ShapeDtypeStruct((both, columns), jn...  13.8 us
    pallas_call x1, Pallas kernels, late_terms(): pl.pallas_call(kernel, out_shape=(jax.ShapeDtypeStruct(shape, jnp.float32...  9.26 us
    slice x2, local copies, waits for them, and re-layouts, on_device_square(): top, bottom = (after(beside[:half], *ready), after(below[half:], *ready))  4.3 us
  transfers between devices with their start and end apart: 28, of which 12 were waited for; matrix products, arithmetic and copies ran while one was open for 8% of the time, Pallas kernels for 15%

profile of v15, /device:TPU:9, one launch (start us, length us, event | category | flops | bytes accessed | tf_op | source)
XLA Modules:
  0.0 202.2 jit_solution(4967485266295995337)
XLA Ops:
  0.6 1.1 slice.54.refs_0_
  1.7 1.4 collective-permute-start.1
  4.0 1.3 collective-permute-start.3
  5.3 1.2 collective-permute-start.4
  6.7 2.2 %collective-permute-start = (bf16[3,96,384]{2,1,0:T(8,128)(2,1)S(1)}, bf16[3,96,384]{2,1,0:T(8,128)(2,1)S(1)}, u32[]{:S(2)}, u32[]{:S(2)}) collective-permute-start(bf16[3,96,384]{2,1,0:T(8,128)(2,1)S(1)} %slice.54.refs_0_), channel_id=1, source_target_pairs={{0,2},{1,3},{2,0},{3,1},{4,6},{5,7},{6,4},{7,5},{8,10},{9,11},{10,... | collective-permute-start | bytes 663560 | tf_op jit(solution)/shard_map/ppermute | solution.py:27
  8.9 4.1 %collective-permute-done.1.refs_3_ = bf16[3,96,384]{2,1,0:T(8,128)(2,1)S(1)} collective-permute-done((bf16[3,96,384]{2,1,0:T(8,128)(2,1)S(1)}, bf16[3,96,384]{2,1,0:T(8,128)(2,1)S(1)}, u32[]{:S(2)}, u32[]{:S(2)}) %collective-permute-start.1) | collective-permute-done | bytes 221216 | tf_op jit(solution)/shard_map/ppermute | solution.py:27
  14.9 4.3 %collective-permute-done.2.refs_2_ = bf16[3,96,384]{2,1,0:T(8,128)(2,1)S(1)} collective-permute-done((bf16[3,96,384]{2,1,0:T(8,128)(2,1)S(1)}, bf16[3,96,384]{2,1,0:T(8,128)(2,1)S(1)}, u32[]{:S(2)}, u32[]{:S(2)}) %collective-permute-start.2) | collective-permute-done | bytes 221216 | tf_op jit(solution)/shard_map/ppermute | solution.py:27
  19.9 1.7 collective-permute-start.8
  21.6 1.8 act.1.refs_0_
  23.4 1.1 copy-done.3
  24.5 1.2 collective-permute-start.6
  25.7 1.2 collective-permute-start.10
  27.5 3.2 %collective-permute-start.7 = (bf16[4,2,96,384]{3,2,1,0:T(8,128)(2,1)}, bf16[4,2,96,384]{3,2,1,0:T(8,128)(2,1)}, u32[]{:S(2)}, u32[]{:S(2)}) collective-permute-start(bf16[4,2,96,384]{3,2,1,0:T(8,128)(2,1)} %after.20.refs_0_), channel_id=1, source_target_pairs={{0,2},{1,3},{2,0},{3,1},{4,6},{5,7},{6,4},{7,5},{8,10},{9,11},{10,... | collective-permute-start | bytes 1769480 | tf_op jit(solution)/shard_map/ppermute | solution.py:27
  30.6 15.7 %collective-permute-done.8.refs_5_.refs_3_ = bf16[4,2,96,384]{3,2,1,0:T(8,128)(2,1)} collective-permute-done((bf16[4,2,96,384]{3,2,1,0:T(8,128)(2,1)}, bf16[4,2,96,384]{3,2,1,0:T(8,128)(2,1)}, u32[]{:S(2)}, u32[]{:S(2)}) %collective-permute-start.8) | collective-permute-done | bytes 589856 | tf_op jit(solution)/shard_map/ppermute | solution.py:27
  46.4 3.0 %fusion.2.refs_2_.shifts_ref = bf16[2048,1152]{1,0:T(8,128)(2,1)} fusion(bf16[2047,384]{1,0:T(8,128)(2,1)S(1)} %get-tuple-element.18, bf16[2047,384]{1,0:T(8,128)(2,1)S(1)} %get-tuple-element.17, bf16[2048,384]{1,0:T(8,128)(2,1)S(1)} %bitcast.24), kind=kLoop, calls=%fused_computation.4 | loop fusion | flops 23592960 | bytes 9435648 | tf_op jit(solution)/shard_map/concatenate | solution.py:513
  49.3 2.3 %half_slope.1.refs_1_.refs_17_.refs_8_ = f32[2,512,768]{2,1,0:T(8,128)S(1)} custom-call(bf16[1,1024,768]{2,1,0:T(8,128)(2,1)S(1)} %copy-done.8), custom_call_target="tpu_custom_call" | custom-call | tf_op jit(solution)/shard_map/half_slope/pallas_call | solution.py:161
  51.7 1.6 copy-done.1
  56.2 1.0 kernel_messages.1
  57.2 1.1 copy-done.5
  58.3 1.1 copy-done.9
  60.2 2.1 %slice.72.refs_0_ = bf16[256,1536]{1,0:T(8,128)(2,1)} slice(bf16[512,1536]{1,0:T(8,128)(2,1)} %collective-permute-done.6.refs_1_), slice={[0:256], [0:1536]} | slice | bytes 1572864 | tf_op jit(solution)/shard_map/slice | solution.py:516
  62.4 1.2 collective-permute-start.9
  63.6 2.2 %slice.73.refs_0_ = bf16[256,1536]{1,0:T(8,128)(2,1)} slice(bf16[512,1536]{1,0:T(8,128)(2,1)} %collective-permute-done.10.refs_2_), slice={[256:512], [0:1536]} | slice | bytes 1572864 | tf_op jit(solution)/shard_map/slice | solution.py:516
  65.8 1.2 collective-permute-start.12
  67.2 13.8 %weight_grad_early.1.refs_1_.early_ref = f32[1536,1152]{1,0:T(8,128)} custom-call(s32[2]{0:T(128)S(1)} %pad_add_fusion.place, bf16[2048,1152]{1,0:T(8,128)(2,1)} %fusion.2.refs_2_.shifts_ref, bf16[512,1536]{1,0:T(8,128)(2,1)S(1)} %copy-done.4, bf16[512,1536]{1,0:T(8,128)(2,1)} %collective-permute-done.6.refs_1_, ...), custom_call_target="tpu_custom_call" | custom-call | flops 1048576 | bytes 65536 | tf_op jit(solution)/shard_map/weight_grad_early/pallas_call | solution.py:209
  81.0 2.4 %stack_planes.1.refs_2_.refs_11_.refs_12_.refs_13_ = bf16[4,4,2,96,384]{4,3,2,1,0:T(8,128)(2,1)S(1)} custom-call(s32[2]{0:T(128)S(1)} %pad_add_fusion.place, bf16[4,2,96,384]{3,2,1,0:T(8,128)(2,1)} %after.20.refs_0_, bf16[4,2,96,384]{3,2,1,0:T(8,128)(2,1)} %collective-permute-done.7.refs_4_.refs_1_, bf16[4,2,96,384]{3,2,1,0:T(8,128)(2,1)} %after.22.refs_2_, ...), custom_call_target="tpu_custom_call" | custom-call | flops 1048576 | bytes 65536 | tf_op jit(solution)/shard_map/stack_planes/pallas_call | solution.py:477
  83.4 2.9 %collective-permute-start.16 = (bf16[4,4,2,96,384]{4,3,2,1,0:T(8,128)(2,1)S(1)}, bf16[4,4,2,96,384]{4,3,2,1,0:T(8,128)(2,1)}, u32[]{:S(2)}, u32[]{:S(2)}) collective-permute-start(bf16[4,4,2,96,384]{4,3,2,1,0:T(8,128)(2,1)S(1)} %stack_planes.1.refs_2_.refs_11_.refs_12_.refs_13_), channel_id=1, source_target_pairs={{0,1},{1,0},{2,3},{3,2},{4,5},{5,4},{6,7},{7,6},{8,9},{9,8},{10,11... | collective-permute-start | bytes 7077896 | tf_op jit(solution)/shard_map/ppermute | solution.py:27
  87.2 1.1 copy-done.7
  88.3 9.3 %weight_grad_late.1 = (f32[4,5,96,384]{3,2,1,0:T(8,128)S(1)}, bf16[2,5,96,384]{3,2,1,0:T(8,128)(2,1)S(1)}, bf16[2,5,96,384]{3,2,1,0:T(8,128)(2,1)}) custom-call(s32[2]{0:T(128)S(1)} %pad_add_fusion.place, bf16[2048,1152]{1,0:T(8,128)(2,1)} %fusion.2.refs_2_.shifts_ref, f32[1536,1152]{1,0:T(8,128)} %weight_grad_early.1.refs_1_.early_ref, ...), custom_call_target="tpu_custom_call" | custom-call | flops 1048576 | bytes 65536 | tf_op jit(solution)/shard_map/weight_grad_late/pallas_call | solution.py:285
  97.6 1.6 copy-done.10
  100.1 1.3 collective-permute-start.18
  101.4 1.1 collective-permute-start.13
  104.0 2.5 %collective-permute-done.14 = bf16[2,5,96,384]{3,2,1,0:T(8,128)(2,1)S(1)} collective-permute-done((bf16[2,5,96,384]{3,2,1,0:T(8,128)(2,1)S(1)}, bf16[2,5,96,384]{3,2,1,0:T(8,128)(2,1)S(1)}, u32[]{:S(2)}, u32[]{:S(2)}) %collective-permute-start.14) | collective-permute-done | bytes 737312 | tf_op jit(solution)/shard_map/ppermute | solution.py:27
  106.5 3.1 %fusion.8 = (bf16[5,96,384]{2,1,0:T(8,128)(2,1)}, bf16[5,96,384]{2,1,0:T(8,128)(2,1)}, bf16[5,96,384]{2,1,0:T(8,128)(2,1)}) fusion(f32[4,5,96,384]{3,2,1,0:T(8,128)} %copy-done.10, bf16[2,5,96,384]{3,2,1,0:T(8,128)(2,1)} %collective-permute-done.18, bf16[2,5,96,384]{3,2,1,0:T(8,128)(2,1)S(1)} %collective-permute-done.14), kind=kLoop, calls=%fused_computation.17 | loop fusion | flops 1658880 | bytes 4423680 | tf_op jit(solution)/shard_map/convert_element_type | solution.py:542
  109.7 2.1 %collective-permute-start.17 = (bf16[5,96,384]{2,1,0:T(8,128)(2,1)}, bf16[5,96,384]{2,1,0:T(8,128)(2,1)S(1)}, u32[]{:S(2)}, u32[]{:S(2)}) collective-permute-start(bf16[5,96,384]{2,1,0:T(8,128)(2,1)} %after.28), channel_id=1, source_target_pairs={{0,2},{1,3},{2,0},{3,1},{4,6},{5,7},{6,4},{7,5},{8,10},{9,11},{10,... | collective-permute-start | bytes 1105928 | tf_op jit(solution)/shard_map/ppermute | solution.py:27
  113.1 23.6 %collective-permute-done.13.refs_0_ = bf16[21,96,384]{2,1,0:T(8,128)(2,1)} collective-permute-done((bf16[21,96,384]{2,1,0:T(8,128)(2,1)}, bf16[21,96,384]{2,1,0:T(8,128)(2,1)}, u32[]{:S(2)}, u32[]{:S(2)}) %collective-permute-start.13) | collective-permute-done | bytes 1548320 | tf_op jit(solution)/shard_map/ppermute | solution.py:27
  136.7 8.7 %collective-permute-done.20.refs_3_.refs_0_ = bf16[5,96,384]{2,1,0:T(8,128)(2,1)S(1)} collective-permute-done((bf16[5,96,384]{2,1,0:T(8,128)(2,1)}, bf16[5,96,384]{2,1,0:T(8,128)(2,1)S(1)}, u32[]{:S(2)}, u32[]{:S(2)}) %collective-permute-start.20) | collective-permute-done | bytes 368672 | tf_op jit(solution)/shard_map/ppermute | solution.py:27
  146.1 1.2 collective-permute-start.24
  147.4 1.2 slice.77
  149.0 1.2 slice.78
  150.2 1.0 collective-permute-start.23
  151.2 13.5 %collective-permute-done.21.refs_3_.refs_0_ = bf16[9,96,384]{2,1,0:T(8,128)(2,1)S(1)} collective-permute-done((bf16[9,96,384]{2,1,0:T(8,128)(2,1)S(1)}, bf16[9,96,384]{2,1,0:T(8,128)(2,1)S(1)}, u32[]{:S(2)}, u32[]{:S(2)}) %collective-permute-start.21) | collective-permute-done | bytes 663584 | tf_op jit(solution)/shard_map/ppermute | solution.py:27
  167.0 1.0 copy-done.28
  168.5 15.1 %input_grad.2.refs_1_.refs_9_ = f32[2,512,768]{2,1,0:T(8,128)} custom-call(s32[2]{0:T(128)} %copy-done.18, bf16[6,96,384]{2,1,0:T(8,128)(2,1)} %copy-done.17, bf16[21,96,384]{2,1,0:T(8,128)(2,1)} %after.31.refs_1_.refs_7_, bf16[21,96,384]{2,1,0:T(8,128)(2,1)} %after.32.refs_2_.refs_9_, bf16[9,96,384]{2,1,0:T(8,128)(2,1)} %copy-done.21, ...), custom_call_target="tpu_custom_call" | custom-call | flops 1048576 | bytes 65536 | tf_op jit(solution)/shard_map/input_grad/pallas_call | solution.py:452
  183.6 1.7 collective-permute-start.26
  185.4 1.9 collective-permute-done.26.refs_5_
  189.1 9.5 %input_grad.3.refs_1_ = bf16[1,1024,768]{2,1,0:T(8,128)(2,1)} custom-call(s32[2]{0:T(128)} %copy-done.18, bf16[9,96,384]{2,1,0:T(8,128)(2,1)} %copy-done.21, bf16[9,96,384]{2,1,0:T(8,128)(2,1)} %copy-done.22, bf16[4,4,2,96,384]{4,3,2,1,0:T(8,128)(2,1)} %copy-done, ...), custom_call_target="tpu_custom_call" | custom-call | flops 1048576 | bytes 65536 | tf_op jit(solution)/shard_map/input_grad/pallas_call | solution.py:452
  199.9 2.3 %fusion.5 = f32[5,96,384]{2,1,0:T(8,128)} fusion(bf16[5,96,384]{2,1,0:T(8,128)(2,1)S(1)} %copy-done.27, bf16[5,96,384]{2,1,0:T(8,128)(2,1)S(1)} %copy-done.25, bf16[5,96,384]{2,1,0:T(8,128)(2,1)} %after.35, f32[4,5,96,384]{3,2,1,0:T(8,128)} %copy-done.10, bf16[2,5,96,384]{3,2,1,0:T(8,128)(2,1)S(1)} %copy-done.31), kind=kLoop, calls=%fused_computation.10 | loop fusion | flops 1474560 | bytes 2949120 | tf_op jit(solution)/shard_map/add | solution.py:577
  (123 shorter events, 19.9 us)
Async XLA Ops:
  0.6 21.0 %copy-start.8 = (bf16[1,1024,768]{2,1,0:T(8,128)(2,1)S(1)}, bf16[1,1024,768]{2,1,0:T(8,128)(2,1)}, u32[]{:S(2)}) copy-start(bf16[1,1024,768]{2,1,0:T(8,128)(2,1)} %x_ref.3) | copy-start | bytes 4718596
  1.7 11.3 %collective-permute-start.1 = (bf16[3,96,384]{2,1,0:T(8,128)(2,1)S(1)}, bf16[3,96,384]{2,1,0:T(8,128)(2,1)S(1)}, u32[]{:S(2)}, u32[]{:S(2)}) collective-permute-start(bf16[3,96,384]{2,1,0:T(8,128)(2,1)S(1)} %slice.54.refs_0_), channel_id=1, source_target_pairs={{0,6},{1,7},{2,4},{3,5},{4,2},{5,3},{6,0},{7,1},{8,14},{9,15},{10,... | collective-permute-start | bytes 663560 | tf_op jit(solution)/shard_map/ppermute | solution.py:27
  4.0 9.0 %collective-permute-start.3 = (bf16[2,96,384]{2,1,0:T(8,128)(2,1)S(1)}, bf16[2,96,384]{2,1,0:T(8,128)(2,1)S(1)}, u32[]{:S(2)}, u32[]{:S(2)}) collective-permute-start(bf16[2,96,384]{2,1,0:T(8,128)(2,1)S(1)} %get-tuple-element.20), channel_id=1, source_target_pairs={{0,8},{8,0},{16,24},{24,16},{1,9},{9,1},{17,25},{25,17},{2,10},{10... | collective-permute-start | bytes 442376 | tf_op jit(solution)/shard_map/ppermute | solution.py:27
  5.3 7.7 %collective-permute-start.4 = (bf16[2,96,384]{2,1,0:T(8,128)(2,1)S(1)}, bf16[2,96,384]{2,1,0:T(8,128)(2,1)S(1)}, u32[]{:S(2)}, u32[]{:S(2)}) collective-permute-start(bf16[2,96,384]{2,1,0:T(8,128)(2,1)S(1)} %get-tuple-element.20), channel_id=1, source_target_pairs={{0,16},{8,24},{16,0},{24,8},{1,17},{9,25},{17,1},{25,9},{2,18},{10... | collective-permute-start | bytes 442376 | tf_op jit(solution)/shard_map/ppermute | solution.py:27
  6.5 6.5 %collective-permute-start.5 = (bf16[2,96,384]{2,1,0:T(8,128)(2,1)S(1)}, bf16[2,96,384]{2,1,0:T(8,128)(2,1)S(1)}, u32[]{:S(2)}, u32[]{:S(2)}) collective-permute-start(bf16[2,96,384]{2,1,0:T(8,128)(2,1)S(1)} %get-tuple-element.20), channel_id=1, source_target_pairs={{0,24},{8,16},{16,8},{24,0},{1,25},{9,17},{17,9},{25,1},{2,26},{10... | collective-permute-start | bytes 442376 | tf_op jit(solution)/shard_map/ppermute | solution.py:27
  6.7 8.2 %collective-permute-start = (bf16[3,96,384]{2,1,0:T(8,128)(2,1)S(1)}, bf16[3,96,384]{2,1,0:T(8,128)(2,1)S(1)}, u32[]{:S(2)}, u32[]{:S(2)}) collective-permute-start(bf16[3,96,384]{2,1,0:T(8,128)(2,1)S(1)} %slice.54.refs_0_), channel_id=1, source_target_pairs={{0,2},{1,3},{2,0},{3,1},{4,6},{5,7},{6,4},{7,5},{8,10},{9,11},{10,... | collective-permute-start | bytes 663560 | tf_op jit(solution)/shard_map/ppermute | solution.py:27
  13.0 6.2 %copy-start.11 = (bf16[3,96,384]{2,1,0:T(8,128)(2,1)}, bf16[3,96,384]{2,1,0:T(8,128)(2,1)S(1)}, u32[]{:S(2)}) copy-start(bf16[3,96,384]{2,1,0:T(8,128)(2,1)S(1)} %collective-permute-done.1.refs_3_) | copy-start | bytes 663556
  13.0 6.2 %collective-permute-start.2 = (bf16[3,96,384]{2,1,0:T(8,128)(2,1)S(1)}, bf16[3,96,384]{2,1,0:T(8,128)(2,1)S(1)}, u32[]{:S(2)}, u32[]{:S(2)}) collective-permute-start(bf16[3,96,384]{2,1,0:T(8,128)(2,1)S(1)} %collective-permute-done.1.refs_3_), channel_id=1, source_target_pairs={{0,2},{1,3},{2,0},{3,1},{4,6},{5,7},{6,4},{7,5},{8,10},{9,11},{10,... | collective-permute-start | bytes 663560 | tf_op jit(solution)/shard_map/ppermute | solution.py:27
  13.0 10.4 %copy-start.34 = (bf16[2,96,384]{2,1,0:T(8,128)(2,1)}, bf16[2,96,384]{2,1,0:T(8,128)(2,1)S(1)}, u32[]{:S(2)}) copy-start(bf16[2,96,384]{2,1,0:T(8,128)(2,1)S(1)} %collective-permute-done.3.refs_1_) | copy-start | bytes 442372
  13.0 8.6 %copy-start.35 = (bf16[2,96,384]{2,1,0:T(8,128)(2,1)}, bf16[2,96,384]{2,1,0:T(8,128)(2,1)S(1)}, u32[]{:S(2)}) copy-start(bf16[2,96,384]{2,1,0:T(8,128)(2,1)S(1)} %collective-permute-done.4.refs_2_) | copy-start | bytes 442372
  13.1 8.5 %copy-start.36 = (bf16[2,96,384]{2,1,0:T(8,128)(2,1)}, bf16[2,96,384]{2,1,0:T(8,128)(2,1)S(1)}, u32[]{:S(2)}) copy-start(bf16[2,96,384]{2,1,0:T(8,128)(2,1)S(1)} %collective-permute-done.5.refs_3_) | copy-start | bytes 442372
  14.9 4.3 %copy-start.13 = (bf16[3,96,384]{2,1,0:T(8,128)(2,1)}, bf16[3,96,384]{2,1,0:T(8,128)(2,1)S(1)}, u32[]{:S(2)}) copy-start(bf16[3,96,384]{2,1,0:T(8,128)(2,1)S(1)} %collective-permute-done.refs_1_) | copy-start | bytes 663556
  19.9 26.4 %collective-permute-start.8 = (bf16[4,2,96,384]{3,2,1,0:T(8,128)(2,1)}, bf16[4,2,96,384]{3,2,1,0:T(8,128)(2,1)}, u32[]{:S(2)}, u32[]{:S(2)}) collective-permute-start(bf16[4,2,96,384]{3,2,1,0:T(8,128)(2,1)} %after.20.refs_0_), channel_id=1, source_target_pairs={{0,6},{1,7},{2,4},{3,5},{4,2},{5,3},{6,0},{7,1},{8,14},{9,15},{10,... | collective-permute-start | bytes 1769480 | tf_op jit(solution)/shard_map/ppermute | solution.py:27
  24.5 2.4 %copy-start.2 = (bf16[1,2048,384]{2,1,0:T(8,128)(2,1)S(1)}, bf16[1,2048,384]{2,1,0:T(8,128)(2,1)}, u32[]{:S(2)}) copy-start(bf16[1,2048,384]{2,1,0:T(8,128)(2,1)} %refs_4_.1) | copy-start | bytes 4718596
  24.5 35.7 %collective-permute-start.6 = (bf16[512,1536]{1,0:T(8,128)(2,1)}, bf16[512,1536]{1,0:T(8,128)(2,1)}, u32[]{:S(2)}, u32[]{:S(2)}) collective-permute-start(bf16[512,1536]{1,0:T(8,128)(2,1)} %after.19.refs_0_), channel_id=1, source_target_pairs={{0,8},{8,0},{16,24},{24,16},{1,9},{9,1},{17,25},{25,17},{2,10},{10... | collective-permute-start | bytes 4718600 | tf_op jit(solution)/shard_map/ppermute | solution.py:27
  25.7 37.9 %collective-permute-start.10 = (bf16[512,1536]{1,0:T(8,128)(2,1)}, bf16[512,1536]{1,0:T(8,128)(2,1)}, u32[]{:S(2)}, u32[]{:S(2)}) collective-permute-start(bf16[512,1536]{1,0:T(8,128)(2,1)} %after.19.refs_0_), channel_id=1, source_target_pairs={{0,16},{8,24},{16,0},{24,8},{1,17},{9,25},{17,1},{25,9},{2,18},{10... | collective-permute-start | bytes 4718600 | tf_op jit(solution)/shard_map/ppermute | solution.py:27
  27.5 34.9 %collective-permute-start.7 = (bf16[4,2,96,384]{3,2,1,0:T(8,128)(2,1)}, bf16[4,2,96,384]{3,2,1,0:T(8,128)(2,1)}, u32[]{:S(2)}, u32[]{:S(2)}) collective-permute-start(bf16[4,2,96,384]{3,2,1,0:T(8,128)(2,1)} %after.20.refs_0_), channel_id=1, source_target_pairs={{0,2},{1,3},{2,0},{3,1},{4,6},{5,7},{6,4},{7,5},{8,10},{9,11},{10,... | collective-permute-start | bytes 1769480 | tf_op jit(solution)/shard_map/ppermute | solution.py:27
  46.4 34.6 %collective-permute-start.11 = (bf16[4,2,96,384]{3,2,1,0:T(8,128)(2,1)}, bf16[4,2,96,384]{3,2,1,0:T(8,128)(2,1)}, u32[]{:S(2)}, u32[]{:S(2)}) collective-permute-start(bf16[4,2,96,384]{3,2,1,0:T(8,128)(2,1)} %collective-permute-done.8.refs_5_.refs_3_), channel_id=1, source_target_pairs={{0,2},{1,3},{2,0},{3,1},{4,6},{5,7},{6,4},{7,5},{8,10},{9,11},{10,... | collective-permute-start | bytes 1769480 | tf_op jit(solution)/shard_map/ppermute | solution.py:27
  51.7 1.6 copy-start.1
  56.2 31.0 %copy-start.18 = (s32[2]{0:T(128)}, s32[2]{0:T(128)S(1)}, u32[]{:S(2)}) copy-start(s32[2]{0:T(128)S(1)} %pad_add_fusion.place) | copy-start | bytes 28
  62.4 23.9 %collective-permute-start.9 = (bf16[256,1536]{1,0:T(8,128)(2,1)}, bf16[256,1536]{1,0:T(8,128)(2,1)S(1)}, u32[]{:S(2)}, u32[]{:S(2)}) collective-permute-start(bf16[256,1536]{1,0:T(8,128)(2,1)} %after.21), channel_id=1, source_target_pairs={{0,16},{8,24},{16,0},{24,8},{1,17},{9,25},{17,1},{25,9},{2,18},{10... | collective-permute-start | bytes 2359304 | tf_op jit(solution)/shard_map/ppermute | solution.py:27
  65.8 1.4 copy-start.4
  65.8 21.4 %collective-permute-start.12 = (bf16[256,1536]{1,0:T(8,128)(2,1)}, bf16[256,1536]{1,0:T(8,128)(2,1)}, u32[]{:S(2)}, u32[]{:S(2)}) collective-permute-start(bf16[256,1536]{1,0:T(8,128)(2,1)} %after.24), channel_id=1, source_target_pairs={{0,8},{8,0},{16,24},{24,16},{1,9},{9,1},{17,25},{25,17},{2,10},{10... | collective-permute-start | bytes 2359304 | tf_op jit(solution)/shard_map/ppermute | solution.py:27
  83.4 2.9 %copy-start = (bf16[4,4,2,96,384]{4,3,2,1,0:T(8,128)(2,1)}, bf16[4,4,2,96,384]{4,3,2,1,0:T(8,128)(2,1)S(1)}, u32[]{:S(2)}) copy-start(bf16[4,4,2,96,384]{4,3,2,1,0:T(8,128)(2,1)S(1)} %stack_planes.1.refs_2_.refs_11_.refs_12_.refs_13_) | copy-start | bytes 7077892
  83.4 26.3 %collective-permute-start.16 = (bf16[4,4,2,96,384]{4,3,2,1,0:T(8,128)(2,1)S(1)}, bf16[4,4,2,96,384]{4,3,2,1,0:T(8,128)(2,1)}, u32[]{:S(2)}, u32[]{:S(2)}) collective-permute-start(bf16[4,4,2,96,384]{4,3,2,1,0:T(8,128)(2,1)S(1)} %stack_planes.1.refs_2_.refs_11_.refs_12_.refs_13_), channel_id=1, source_target_pairs={{0,1},{1,0},{2,3},{3,2},{4,5},{5,4},{6,7},{7,6},{8,9},{9,8},{10,11... | collective-permute-start | bytes 7077896 | tf_op jit(solution)/shard_map/ppermute | solution.py:27
  97.6 1.6 copy-start.10
  100.1 3.5 %collective-permute-start.18 = (bf16[2,5,96,384]{3,2,1,0:T(8,128)(2,1)}, bf16[2,5,96,384]{3,2,1,0:T(8,128)(2,1)}, u32[]{:S(2)}, u32[]{:S(2)}) collective-permute-start(bf16[2,5,96,384]{3,2,1,0:T(8,128)(2,1)} %get-tuple-element.12), channel_id=1, source_target_pairs={{0,1},{1,0},{2,3},{3,2},{4,5},{5,4},{6,7},{7,6},{8,9},{9,8},{10,11... | collective-permute-start | bytes 2211848 | tf_op jit(solution)/shard_map/ppermute | solution.py:27
  101.4 2.2 %copy-start.20 = (bf16[2,5,96,384]{3,2,1,0:T(8,128)(2,1)S(1)}, bf16[2,5,96,384]{3,2,1,0:T(8,128)(2,1)}, u32[]{:S(2)}) copy-start(bf16[2,5,96,384]{3,2,1,0:T(8,128)(2,1)} %copy-done.19) | copy-start | bytes 2211844
  101.4 8.2 %collective-permute-start.15 = (bf16[21,96,384]{2,1,0:T(8,128)(2,1)}, bf16[21,96,384]{2,1,0:T(8,128)(2,1)}, u32[]{:S(2)}, u32[]{:S(2)}) collective-permute-start(bf16[21,96,384]{2,1,0:T(8,128)(2,1)} %after.27.refs_5_), channel_id=1, source_target_pairs={{0,1},{1,0},{2,3},{3,2},{4,5},{5,4},{6,7},{7,6},{8,9},{9,8},{10,11... | collective-permute-start | bytes 4644872 | tf_op jit(solution)/shard_map/ppermute | solution.py:27
  101.4 35.2 %collective-permute-start.13 = (bf16[21,96,384]{2,1,0:T(8,128)(2,1)}, bf16[21,96,384]{2,1,0:T(8,128)(2,1)}, u32[]{:S(2)}, u32[]{:S(2)}) collective-permute-start(bf16[21,96,384]{2,1,0:T(8,128)(2,1)} %after.26), channel_id=1, source_target_pairs={{0,8},{8,0},{16,24},{24,16},{1,9},{9,1},{17,25},{25,17},{2,10},{10... | collective-permute-start | bytes 4644872 | tf_op jit(solution)/shard_map/ppermute | solution.py:27
  102.5 44.8 %collective-permute-start.22 = (bf16[21,96,384]{2,1,0:T(8,128)(2,1)}, bf16[21,96,384]{2,1,0:T(8,128)(2,1)}, u32[]{:S(2)}, u32[]{:S(2)}) collective-permute-start(bf16[21,96,384]{2,1,0:T(8,128)(2,1)} %after.27.refs_5_), channel_id=1, source_target_pairs={{0,16},{8,24},{16,0},{24,8},{1,17},{9,25},{17,1},{25,9},{2,18},{10... | collective-permute-start | bytes 4644872 | tf_op jit(solution)/shard_map/ppermute | solution.py:27
  103.6 2.9 %collective-permute-start.14 = (bf16[2,5,96,384]{3,2,1,0:T(8,128)(2,1)S(1)}, bf16[2,5,96,384]{3,2,1,0:T(8,128)(2,1)S(1)}, u32[]{:S(2)}, u32[]{:S(2)}) collective-permute-start(bf16[2,5,96,384]{3,2,1,0:T(8,128)(2,1)S(1)} %copy-done.20), channel_id=1, source_target_pairs={{0,1},{1,0},{2,3},{3,2},{4,5},{5,4},{6,7},{7,6},{8,9},{9,8},{10,11... | collective-permute-start | bytes 2211848 | tf_op jit(solution)/shard_map/ppermute | solution.py:27
  106.5 3.1 %copy-start.30 = (bf16[2,5,96,384]{3,2,1,0:T(8,128)(2,1)}, bf16[2,5,96,384]{3,2,1,0:T(8,128)(2,1)S(1)}, u32[]{:S(2)}) copy-start(bf16[2,5,96,384]{3,2,1,0:T(8,128)(2,1)S(1)} %collective-permute-done.14) | copy-start | bytes 2211844
  109.7 27.0 %collective-permute-start.17 = (bf16[5,96,384]{2,1,0:T(8,128)(2,1)}, bf16[5,96,384]{2,1,0:T(8,128)(2,1)S(1)}, u32[]{:S(2)}, u32[]{:S(2)}) collective-permute-start(bf16[5,96,384]{2,1,0:T(8,128)(2,1)} %after.28), channel_id=1, source_target_pairs={{0,2},{1,3},{2,0},{3,1},{4,6},{5,7},{6,4},{7,5},{8,10},{9,11},{10,... | collective-permute-start | bytes 1105928 | tf_op jit(solution)/shard_map/ppermute | solution.py:27
  111.8 24.9 %collective-permute-start.19 = (bf16[5,96,384]{2,1,0:T(8,128)(2,1)}, bf16[5,96,384]{2,1,0:T(8,128)(2,1)S(1)}, u32[]{:S(2)}, u32[]{:S(2)}) collective-permute-start(bf16[5,96,384]{2,1,0:T(8,128)(2,1)} %after.29), channel_id=1, source_target_pairs={{0,4},{1,5},{2,6},{3,7},{4,0},{5,1},{6,2},{7,3},{8,12},{9,13},{10,... | collective-permute-start | bytes 1105928 | tf_op jit(solution)/shard_map/ppermute | solution.py:27
  112.8 32.6 %collective-permute-start.20 = (bf16[5,96,384]{2,1,0:T(8,128)(2,1)}, bf16[5,96,384]{2,1,0:T(8,128)(2,1)S(1)}, u32[]{:S(2)}, u32[]{:S(2)}) collective-permute-start(bf16[5,96,384]{2,1,0:T(8,128)(2,1)} %after.30), channel_id=1, source_target_pairs={{0,6},{1,7},{2,4},{3,5},{4,2},{5,3},{6,0},{7,1},{8,14},{9,15},{10,... | collective-permute-start | bytes 1105928 | tf_op jit(solution)/shard_map/ppermute | solution.py:27
  136.7 8.7 %copy-start.23 = (bf16[5,96,384]{2,1,0:T(8,128)(2,1)}, bf16[5,96,384]{2,1,0:T(8,128)(2,1)S(1)}, u32[]{:S(2)}) copy-start(bf16[5,96,384]{2,1,0:T(8,128)(2,1)S(1)} %collective-permute-done.17.refs_1_.refs_0_) | copy-start | bytes 1105924
  136.7 8.7 %copy-start.24 = (bf16[5,96,384]{2,1,0:T(8,128)(2,1)}, bf16[5,96,384]{2,1,0:T(8,128)(2,1)S(1)}, u32[]{:S(2)}) copy-start(bf16[5,96,384]{2,1,0:T(8,128)(2,1)S(1)} %collective-permute-done.19.refs_2_.refs_0_) | copy-start | bytes 1105924
  146.1 20.7 %collective-permute-start.24 = (bf16[21,96,384]{2,1,0:T(8,128)(2,1)}, bf16[21,96,384]{2,1,0:T(8,128)(2,1)S(1)}, u32[]{:S(2)}, u32[]{:S(2)}) collective-permute-start(bf16[21,96,384]{2,1,0:T(8,128)(2,1)} %after.31.refs_1_.refs_7_), channel_id=1, source_target_pairs={{0,1},{1,0},{2,3},{3,2},{4,5},{5,4},{6,7},{7,6},{8,9},{9,8},{10,11... | collective-permute-start | bytes 4644872 | tf_op jit(solution)/shard_map/ppermute | solution.py:27
  147.3 19.5 %collective-permute-start.25 = (bf16[21,96,384]{2,1,0:T(8,128)(2,1)}, bf16[21,96,384]{2,1,0:T(8,128)(2,1)S(1)}, u32[]{:S(2)}, u32[]{:S(2)}) collective-permute-start(bf16[21,96,384]{2,1,0:T(8,128)(2,1)} %after.32.refs_2_.refs_9_), channel_id=1, source_target_pairs={{0,1},{1,0},{2,3},{3,2},{4,5},{5,4},{6,7},{7,6},{8,9},{9,8},{10,11... | collective-permute-start | bytes 4644872 | tf_op jit(solution)/shard_map/ppermute | solution.py:27
  148.6 16.1 %collective-permute-start.21 = (bf16[9,96,384]{2,1,0:T(8,128)(2,1)S(1)}, bf16[9,96,384]{2,1,0:T(8,128)(2,1)S(1)}, u32[]{:S(2)}, u32[]{:S(2)}) collective-permute-start(bf16[9,96,384]{2,1,0:T(8,128)(2,1)S(1)} %slice.77), channel_id=1, source_target_pairs={{0,16},{8,24},{16,0},{24,8},{1,17},{9,25},{17,1},{25,9},{2,18},{10... | collective-permute-start | bytes 1990664 | tf_op jit(solution)/shard_map/ppermute | solution.py:27
  150.2 15.8 %collective-permute-start.23 = (bf16[9,96,384]{2,1,0:T(8,128)(2,1)S(1)}, bf16[9,96,384]{2,1,0:T(8,128)(2,1)S(1)}, u32[]{:S(2)}, u32[]{:S(2)}) collective-permute-start(bf16[9,96,384]{2,1,0:T(8,128)(2,1)S(1)} %slice.78), channel_id=1, source_target_pairs={{0,8},{8,0},{16,24},{24,16},{1,9},{9,1},{17,25},{25,17},{2,10},{10... | collective-permute-start | bytes 1990664 | tf_op jit(solution)/shard_map/ppermute | solution.py:27
  164.7 2.2 %copy-start.21 = (bf16[9,96,384]{2,1,0:T(8,128)(2,1)}, bf16[9,96,384]{2,1,0:T(8,128)(2,1)S(1)}, u32[]{:S(2)}) copy-start(bf16[9,96,384]{2,1,0:T(8,128)(2,1)S(1)} %collective-permute-done.21.refs_3_.refs_0_) | copy-start | bytes 1990660
  166.9 1.6 copy-start.29
  183.6 3.6 %collective-permute-start.26 = (bf16[9,96,384]{2,1,0:T(8,128)(2,1)}, bf16[9,96,384]{2,1,0:T(8,128)(2,1)S(1)}, u32[]{:S(2)}, u32[]{:S(2)}) collective-permute-start(bf16[9,96,384]{2,1,0:T(8,128)(2,1)} %after.33.refs_4_), channel_id=1, source_target_pairs={{0,1},{1,0},{2,3},{3,2},{4,5},{5,4},{6,7},{7,6},{8,9},{9,8},{10,11... | collective-permute-start | bytes 1990664 | tf_op jit(solution)/shard_map/ppermute | solution.py:27
  185.3 2.9 %collective-permute-start.27 = (bf16[9,96,384]{2,1,0:T(8,128)(2,1)}, bf16[9,96,384]{2,1,0:T(8,128)(2,1)S(1)}, u32[]{:S(2)}, u32[]{:S(2)}) collective-permute-start(bf16[9,96,384]{2,1,0:T(8,128)(2,1)} %after.34.refs_6_), channel_id=1, source_target_pairs={{0,1},{1,0},{2,3},{3,2},{4,5},{5,4},{6,7},{7,6},{8,9},{9,8},{10,11... | collective-permute-start | bytes 1990664 | tf_op jit(solution)/shard_map/ppermute | solution.py:27
  198.6 1.2 copy-start.31
  198.6 1.3 copy-start.25
  (17 other events, 16.3 us)

commit v16 on v15

--- a/solution.py
+++ b/solution.py
@@ -21,11 +21,9 @@
 ROW_OFFSETS = ((1, 1), (0, 1), (0, 0), (-1, 0), (-1, -1))
 GRAD_PARTS = ((0, 0), (1, 0), (1, 1), (2, 1), (2, 2))
 
-
 def from_peer(value, axis, distance):
     peers = lax.axis_size(axis)
     return lax.ppermute(value, axis, [(i, i ^ distance) for i in range(peers)])
-
 
 def after(value, *earlier):
     return pl.pallas_call(
@@ -37,7 +35,6 @@
         name="after",
     )(value, *earlier)
 
-
 def gather_line(value, axis, count, unit):
     found, mask = {0: value}, count - 1
     while mask:
@@ -46,13 +43,11 @@
         mask //= 2
     return [found[distance] for distance in range(count)]
 
-
 def gelu_slope(x):
     tanh = jnp.tanh(ROOT * (x + CUBIC * (x * x * x)))
     return 0.5 * (1.0 + tanh) + 0.5 * x * (1.0 - tanh * tanh) * (
         ROOT * (1.0 + 3.0 * CUBIC * (x * x))
     )
-
 
 def act_kernel(x_ref, out_ref, strip):
     width = x_ref.shape[2]
@@ -70,7 +65,6 @@
                 left = parity * width + c * LANES
                 out_ref[pl.ds(start, STEP), left : left + LANES] = picked
 
-
 def activate(inputs):
     fine, width = inputs.shape[1:]
     return pl.pallas_call(
@@ -83,7 +77,6 @@
         cost_estimate=SMALL,
         name="act",
     )(inputs)
-
 
 def kernel_messages(place, line, trunk_grad, coarse):
     taps, rows, block = line[0].shape
@@ -141,7 +134,6 @@
         name="kernel_messages",
     )(place, *line, trunk_grad)
 
-
 def slope_kernel(x_ref, out_ref, scratch):
     width = x_ref.shape[2]
 
@@ -155,7 +147,6 @@
             for parity in range(2):
                 out_ref[parity, pl.ds(start, 64), lanes] = scratch[c, pl.ds(parity, 64, stride=2), :]
 
-
 def half_slope(inputs):
     fine, width = inputs.shape[1:]
     return pl.pallas_call(
@@ -167,7 +158,6 @@
         compiler_params=pltpu.CompilerParams(vmem_limit_bytes=24 << 20),
         name="half_slope",
     )(inputs)
-
 
 def start_act(place, coarse, layout, pieces, shifts_ref, held, shifts, sems, shift_sems):
     copies, row = [], 0
@@ -183,7 +173,6 @@
     for copy in copies:
         copy.start()
     return copies
-
 
 def early_terms(place, layout, pieces, shifts, coarse):
     both, columns = pieces[0].shape[1], shifts.shape[1]
@@ -225,7 +214,6 @@
         cost_estimate=SMALL,
         name="weight_grad_early",
     )(place, shifts, *pieces)
-
 
 def late_terms(place, layout, pieces, shifts, early, coarse, scale, planes, taps, rows):
     both, columns = early.shape
@@ -308,7 +296,6 @@
         name="weight_grad_late",
     )(place, shifts, early, *pieces)
 
-
 def shifted_total(products, base, lanes, parity):
     total = None
     for by in (0, 1, -1):
@@ -319,28 +306,26 @@
             total = part if total is None else total + part
     return total
 
-
 def gradient_stage(place, windows, taps, pieces, distances, slope, begun, shape):
     _, fine, width = shape
-    coarse, seqs = fine // 2, len(windows)
+    coarse, seqs = fine // 2, lax.axis_size("seq")
     rows, block = pieces[0][0].shape[-2:]
     planes = width // (2 * rows)
     half = planes // 2
     window, used = coarse + 2 * HALO, coarse + 2 * MARGIN
     depth, planar = len(distances) * block, (2, coarse, width)
     last = begun is not None
-    needed = distances if last else list(range(seqs))
+    needed = list(range(seqs)) if last else distances
     parts = [(d, *part) for d in needed for part in windows[d]]
     operands = [part[1] for part in parts] + [piece[0] for piece in pieces]
-    operands += [slope] + ([begun] if last else [])
+    operands += [slope, begun] if last else []
 
     def body(place, *refs):
         own, refs = refs[: len(parts)], refs[len(parts) :]
         sources, refs = refs[: len(pieces)], refs[len(pieces) :]
-        slope_ref, refs = refs[0], refs[1:]
         if last:
-            begun_ref, refs = refs[0], refs[1:]
-        out_ref, wv, gv, products, slopes, sems, grad_sems, slope_sem = refs[:8]
+            (slope_ref, begun_ref), refs = refs[:2], refs[2:]
+        out_ref, wv, gv, products, sems, grad_sems = refs[:6]
         me, core = place[0], place[1] % 2
 
         def kernel_copies(first):
@@ -374,12 +359,11 @@
             return gv.at[span, pl.ds(distances.index(distance) * block, block)]
 
         early = list(window_copies(into_window, grad_sems))
-        late = [pltpu.make_async_copy(slope_ref, slopes, slope_sem)]
+        late = []
         if last:
-            sums, strip, sum_sem = refs[8:]
-            late.append(pltpu.make_async_copy(begun_ref, sums, sum_sem))
-        else:
-            skips, skip_sems = refs[8:]
+            sums, slopes, strip, skips, sum_sems, skip_sems = refs[6:]
+            late.append(pltpu.make_async_copy(begun_ref, sums, sum_sems.at[0]))
+            late.append(pltpu.make_async_copy(slope_ref, slopes, sum_sems.at[1]))
             late += window_copies(lambda d, span: skips.at[me ^ d, span], skip_sems)
         for copy in early:
             copy.start()
@@ -413,16 +397,15 @@
             spot, span = pl.ds(base, STEP), pl.ds(pl.multiple_of(2 * base, 2 * STEP), 2 * STEP)
             for c in range(width // LANES):
                 lanes = slice(c * LANES, (c + 1) * LANES)
-                if not last:
+                if last:
                     left = c * LANES % block
                     skip = skips[c * LANES // block, pl.ds(base + HALO, STEP), left : left + LANES]
                     skip = 0.5 * skip.astype(jnp.float32)
                 for parity in range(2):
                     total = shifted_total(products, base, lanes, parity)
-                    total = total * slopes[parity, spot, lanes]
-                    total = total + (sums[parity, spot, lanes] if last else skip)
                     if last:
-                        strip[c, pl.ds(parity, STEP, stride=2), :] = total
+                        total = (total + sums[parity, spot, lanes]) * slopes[parity, spot, lanes]
+                        strip[c, pl.ds(parity, STEP, stride=2), :] = total + skip
                     else:
                         out_ref[parity, spot, lanes] = total
                 if last:
@@ -433,20 +416,16 @@
         pltpu.VMEM((taps, planes, 2, rows, depth), jnp.bfloat16),
         pltpu.VMEM((window, depth), jnp.bfloat16),
         pltpu.VMEM((taps, used, width), jnp.float32),
-        pltpu.VMEM(planar, jnp.float32),
         pltpu.SemaphoreType.DMA((taps, len(pieces), 2)),
         pltpu.SemaphoreType.DMA((len(parts), window // rows)),
-        pltpu.SemaphoreType.DMA,
     ]
     if last:
         scratch += [
             pltpu.VMEM(planar, jnp.float32),
+            pltpu.VMEM(planar, jnp.float32),
             pltpu.VMEM((width // LANES, 2 * STEP, LANES), jnp.float32),
-            pltpu.SemaphoreType.DMA,
-        ]
-    else:
-        scratch += [
             pltpu.VMEM((seqs, window, block), jnp.bfloat16),
+            pltpu.SemaphoreType.DMA((2,)),
             pltpu.SemaphoreType.DMA((len(parts), window // rows)),
         ]
     return pl.pallas_call(
@@ -464,7 +443,6 @@
         name="input_grad",
     )(place, *operands)
 
-
 def stack_planes(place, line):
     count = len(line)
 
@@ -488,7 +466,6 @@
         name="stack_planes",
     )(place, *line)
 
-
 def on_device_square(inputs, trunk_grad, weights):
     seqs, reps = lax.axis_size("seq"), lax.axis_size("rep")
     me, rep = lax.axis_index("seq"), lax.axis_index("rep")
@@ -504,15 +481,16 @@
     act = after(activate(inputs), *across[1:])
     beside, below = from_peer(act, "seq", 1), from_peer(act, "seq", 2)
     slope = half_slope(inputs)
-    line = gather_line(weights[:SPLIT], "rep", planes, 2)
-    line_across = gather_line(after(jnp.stack(across), *line[1:]), "rep", planes, 2)
+    line_across = gather_line(after(jnp.stack(across), act), "rep", planes, 2)
+    crossing = (line_across[1], line_across[planes - 1])
+    line = gather_line(after(weights[:SPLIT], *crossing), "rep", planes, 2)
     trunk = trunk_grad[0]
     zeros = jnp.zeros((1, block), jnp.bfloat16)
     later = jnp.concatenate([trunk[1:], zeros])
     earlier = jnp.concatenate([zeros, trunk[:-1]])
     shifts = jnp.concatenate([later, trunk, earlier], axis=1)
     to_beside, to_below, own_window = kernel_messages(place, line, trunk_grad, coarse)
-    ready = (slope, shifts, to_beside, line_across[1], line_across[planes - 1])
+    ready = (slope, shifts, line[1], line[planes - 1], *crossing)
     top, bottom = after(beside[:half], *ready), after(below[half:], *ready)
     far_top, far_bottom = from_peer(top, "seq", 2), from_peer(bottom, "seq", 1)
 
@@ -544,19 +522,16 @@
 
     window = (coarse + 2 * HALO) // rows
     count, side = planes * SPLIT, window // 2
-    kept_beside, kept_below = after(kept_beside, *summed), after(kept_below, *summed)
-    far_first = from_peer(kept_beside[: side + count // 2], "seq", 2)
-    far_second = from_peer(kept_below[count // 2 : count + side], "seq", 1)
+    far_first = after(kept_beside[: side + count // 2], *leaving)
+    far_second = after(kept_below[count // 2 : count + side], *leaving)
+    far_first, far_second = from_peer(far_first, "seq", 2), from_peer(far_second, "seq", 1)
+
     windows = [
         [(own_window, 0, 0, window)],
         [(kept_beside, side + count, 0, window)],
         [(kept_below, count + side, 0, window)],
-        [(far_first, 0, 0, side), (far_second, count // 2, side, side)],
     ]
-
-    stage = functools.partial(
-        gradient_stage, place, windows, taps, slope=slope, shape=inputs.shape
-    )
+    stage = functools.partial(gradient_stage, place, taps=taps, slope=slope, shape=inputs.shape)
     soon = [(to_below, 0, 0, planes, 0, 0), (other_column, 0, 0, planes, 1, 0)]
     for part, start, distance in ((kept_beside, side, 1), (kept_below, 0, 2)):
         soon.append((part, start, 0, planes, 0, distance))
@@ -566,17 +541,18 @@
         for flip, part in enumerate((lines, other_lines))
         for d in range(seqs)
     ]
-    begun = stage(soon + [piece for piece in crossed if piece[-1] < 3], [0, 1, 2], begun=None)
+    near = [piece for piece in crossed if piece[-1] < 3]
+    begun = stage(windows, pieces=soon + near, distances=[0, 1, 2], begun=None)
+    far_first, far_second = after(far_first, begun), after(far_second, begun)
+    windows.append([(far_first, 0, 0, side), (far_second, count // 2, side, side)])
     rest = [piece for piece in crossed if piece[-1] == 3]
     for part, start, plane in ((far_first, side, 0), (far_second, 0, planes // 2)):
-        part = after(part, begun)
         rest.append((part, start, plane, planes // 2, 0, 3))
         rest.append((from_peer(part, "rep", 1), start, plane, planes // 2, 1, 3))
-    input_grad = stage(rest, [3], begun=begun)
+    input_grad = stage(windows, pieces=rest, distances=[3], begun=begun)
     for part in summed:
         weight_grad = weight_grad + after(part, input_grad).astype(jnp.float32)
     return (input_grad, weight_grad)
-
 
 def with_halo(value, sides, width):
     for axis, dim in sides:
@@ -590,18 +566,15 @@
         value = jnp.concatenate([before, value, after], axis=dim)
     return value
 
-
 def contract_last(left, right):
     return lax.dot_general(
         left, right, (((1,), (1,)), ((), ())), preferred_element_type=jnp.float32
     )
 
-
 def contract_first(left, right):
     return lax.dot_general(
         left, right, (((0,), (0,)), ((), ())), preferred_element_type=jnp.float32
     )
-
 
 def on_device_plain(inputs, trunk_grad, weights):
     taps = weights.shape[0]
@@ -629,13 +602,11 @@
     weight_grad = lax.psum_scatter(partial_sum, "seq", scatter_dimension=2, tiled=True)
     return (input_grad[None], weight_grad)
 
-
 def on_device(inputs, trunk_grad, weights):
     square = lax.axis_size("seq") == 4 and lax.axis_size("rep") % 8 == 0
     if square and weights.shape[2] % LANES == 0 and inputs.shape[2] % LANES == 0:
         return on_device_square(inputs, trunk_grad, weights)
     return on_device_plain(inputs, trunk_grad, weights)
-
 
 def solution(mesh):
     in_specs = (P("rep", "seq", None), P("rep", None, "seq"), P(None, "rep", "seq"))

time: 203 us -> 205 us (level)
  waiting for transfers between devices: 77.4 us -> 71.2 us
  starting transfers between devices: 29.8 us -> 32.6 us
    ppermute x28, waiting for transfers between devices: 77.4 us -> 71.2 us  [from_peer(): return lax.ppermute(value, axis, [(i, i ^ distance) for i in range(peers)])]
    ppermute x28, starting transfers between devices: 29.8 us -> 32.6 us  [from_peer(): return lax.ppermute(value, axis, [(i, i ^ distance) for i in range(peers)])]
    concatenate x1, other arithmetic: 2.97 us -> 5.38 us  [on_device_square(): shifts = jnp.concatenate([later, trunk, earlier], axis=1)]
  transfers between devices with their start and end apart: 28 -> 28, of which waited for: 12 -> 8; matrix products, arithmetic and copies ran while one was open for 8% -> 9% of each run, Pallas kernels for 15% -> 28%
where the time goes in v16:
time: 205 us; the launch traced here: 203 us
  waiting for transfers between devices  71.2 us (35%)
  Pallas kernels  56.9 us (28%)
  starting transfers between devices  32.6 us (16%)
  local copies, waits for them, and re-layouts  31.5 us (15%)
  other arithmetic  9.86 us (5%)
    ppermute x28, waiting for transfers between devices, from_peer(): return lax.ppermute(value, axis, [(i, i ^ distance) for i in range(peers)])  71.2 us
    ppermute x28, starting transfers between devices, from_peer(): return lax.ppermute(value, axis, [(i, i ^ distance) for i in range(peers)])  32.6 us
    pallas_call x2, Pallas kernels, gradient_stage(): pl.pallas_call(body, out_shape=out_shape, grid_spec=pltpu.PrefetchScalarG...  26.2 us
    unnamed x76, local copies, waits for them, and re-layouts  19.6 us
    pallas_call x1, Pallas kernels, early_terms(): pl.pallas_call(kernel, out_shape=jax.ShapeDtypeStruct((both, columns), jn...  13.8 us
    pallas_call x1, Pallas kernels, late_terms(): pl.pallas_call(kernel, out_shape=(jax.ShapeDtypeStruct(shape, jnp.float32...  8.56 us
    concatenate x1, other arithmetic, on_device_square(): shifts = jnp.concatenate([later, trunk, earlier], axis=1)  5.38 us
    slice x2, local copies, waits for them, and re-layouts, on_device_square(): top, bottom = (after(beside[:half], *ready), after(below[half:], *ready))  4.14 us
  transfers between devices with their start and end apart: 28, of which 8 were waited for; matrix products, arithmetic and copies ran while one was open for 9% of the time, Pallas kernels for 28%

profile of v16, /device:TPU:9, one launch (start us, length us, event | category | flops | bytes accessed | tf_op | source)
XLA Modules:
  0.0 203.0 jit_solution(14063839624132749167)
XLA Ops:
  0.6 0.9 slice_bitcast_fusion.2
  1.6 1.3 collective-permute-start
  2.8 1.2 collective-permute-start.1
  4.3 1.4 copy-done.6
  5.7 1.8 act.1.refs_0_
  7.5 1.1 copy-done.4
  8.6 2.0 %collective-permute-done.2.refs_3_ = bf16[2,96,384]{2,1,0:T(8,128)(2,1)S(1)} collective-permute-done((bf16[2,96,384]{2,1,0:T(8,128)(2,1)S(1)}, bf16[2,96,384]{2,1,0:T(8,128)(2,1)S(1)}, u32[]{:S(2)}, u32[]{:S(2)}) %collective-permute-start.2) | collective-permute-done | bytes 147488 | tf_op jit(solution)/shard_map/ppermute | solution.py:26
  11.6 1.4 collective-permute-start.4
  13.0 2.2 %collective-permute-start.3 = (bf16[4,2,96,384]{3,2,1,0:T(8,128)(2,1)}, bf16[4,2,96,384]{3,2,1,0:T(8,128)(2,1)}, u32[]{:S(2)}, u32[]{:S(2)}) collective-permute-start(bf16[4,2,96,384]{3,2,1,0:T(8,128)(2,1)} %after.21.refs_0_), channel_id=1, source_target_pairs={{0,2},{1,3},{2,0},{3,1},{4,6},{5,7},{6,4},{7,5},{8,10},{9,11},{10,... | collective-permute-start | bytes 1769480 | tf_op jit(solution)/shard_map/ppermute | solution.py:26
  16.1 1.0 collective-permute-start.8
  17.2 2.1 %slice_bitcast_fusion.1 = (bf16[2047,384]{1,0:T(8,128)(2,1)}, bf16[2047,384]{1,0:T(8,128)(2,1)}) fusion(bf16[1,2048,384]{2,1,0:T(8,128)(2,1)S(1)} %copy-done.3), kind=kLoop, calls=%fused_computation.7 | loop fusion | bytes 6288384 | tf_op jit(solution)/shard_map/slice | solution.py:489
  19.3 19.7 %collective-permute-done.4.refs_2_.refs_6_.refs_3_ = bf16[4,2,96,384]{3,2,1,0:T(8,128)(2,1)} collective-permute-done((bf16[4,2,96,384]{3,2,1,0:T(8,128)(2,1)}, bf16[4,2,96,384]{3,2,1,0:T(8,128)(2,1)}, u32[]{:S(2)}, u32[]{:S(2)}) %collective-permute-start.4) | collective-permute-done | bytes 589856 | tf_op jit(solution)/shard_map/ppermute | solution.py:26
  39.0 1.0 collective-permute-done.3.refs_1_.refs_5_
  40.0 2.1 %collective-permute-start.5 = (bf16[3,96,384]{2,1,0:T(8,128)(2,1)}, bf16[3,96,384]{2,1,0:T(8,128)(2,1)}, u32[]{:S(2)}, u32[]{:S(2)}) collective-permute-start(bf16[3,96,384]{2,1,0:T(8,128)(2,1)} %after.22.refs_0_), channel_id=1, source_target_pairs={{0,2},{1,3},{2,0},{3,1},{4,6},{5,7},{6,4},{7,5},{8,10},{9,11},{10,... | collective-permute-start | bytes 663560 | tf_op jit(solution)/shard_map/ppermute | solution.py:26
  42.1 5.4 %fusion.2.refs_2_.shifts_ref = bf16[2048,1152]{1,0:T(8,128)(2,1)} fusion(bf16[2047,384]{1,0:T(8,128)(2,1)} %get-tuple-element.18, bf16[2047,384]{1,0:T(8,128)(2,1)} %get-tuple-element.17, bf16[2048,384]{1,0:T(8,128)(2,1)S(1)} %bitcast.24), kind=kLoop, calls=%fused_computation.4 | loop fusion | flops 23592960 | bytes 9435648 | tf_op jit(solution)/shard_map/concatenate | solution.py:491
  47.4 2.3 %half_slope.1.refs_1_.refs_11_ = f32[2,512,768]{2,1,0:T(8,128)S(1)} custom-call(bf16[1,1024,768]{2,1,0:T(8,128)(2,1)S(1)} %copy-done.7), custom_call_target="tpu_custom_call" | custom-call | tf_op jit(solution)/shard_map/half_slope/pallas_call | solution.py:152
  49.8 1.6 copy-done.2
  51.4 2.1 %slice.73.refs_0_ = bf16[256,1536]{1,0:T(8,128)(2,1)} slice(bf16[512,1536]{1,0:T(8,128)(2,1)} %collective-permute-done.10.refs_2_), slice={[256:512], [0:1536]} | slice | bytes 1572864 | tf_op jit(solution)/shard_map/slice | solution.py:494
  54.2 1.0 collective-permute-start.12
  55.2 2.1 %slice.72.refs_0_ = bf16[256,1536]{1,0:T(8,128)(2,1)} slice(bf16[512,1536]{1,0:T(8,128)(2,1)} %collective-permute-done.8.refs_1_), slice={[0:256], [0:1536]} | slice | bytes 1572864 | tf_op jit(solution)/shard_map/slice | solution.py:494
  57.7 1.5 collective-permute-start.7
  59.2 15.4 %collective-permute-done.7.refs_2_ = bf16[3,96,384]{2,1,0:T(8,128)(2,1)} collective-permute-done((bf16[3,96,384]{2,1,0:T(8,128)(2,1)}, bf16[3,96,384]{2,1,0:T(8,128)(2,1)}, u32[]{:S(2)}, u32[]{:S(2)}) %collective-permute-start.7) | collective-permute-done | bytes 221216 | tf_op jit(solution)/shard_map/ppermute | solution.py:26
  75.6 2.0 %kernel_messages.1 = (bf16[21,96,384]{2,1,0:T(8,128)(2,1)S(1)}, bf16[21,96,384]{2,1,0:T(8,128)(2,1)S(1)}, bf16[6,96,384]{2,1,0:T(8,128)(2,1)S(1)}) custom-call(s32[2]{0:T(128)S(1)} %pad_add_fusion.place, bf16[3,96,384]{2,1,0:T(8,128)(2,1)S(1)} %copy-done.12, bf16[3,96,384]{2,1,0:T(8,128)(2,1)} %collective-permute-done.5.refs_1_.refs_3_, ...), custom_call_target="tpu_custom_call" | custom-call | flops 1048576 | bytes 65536 | tf_op jit(solution)/shard_map/kernel_messages/pallas_call | solution.py:114
  77.6 1.1 copy-done.8
  79.6 1.1 copy-done.16
  80.7 13.8 %weight_grad_early.1.refs_1_.early_ref = f32[1536,1152]{1,0:T(8,128)} custom-call(s32[2]{0:T(128)S(1)} %pad_add_fusion.place, bf16[2048,1152]{1,0:T(8,128)(2,1)} %fusion.2.refs_2_.shifts_ref, bf16[512,1536]{1,0:T(8,128)(2,1)S(1)} %copy-done.5, bf16[512,1536]{1,0:T(8,128)(2,1)} %collective-permute-done.8.refs_1_, ...), custom_call_target="tpu_custom_call" | custom-call | flops 1048576 | bytes 65536 | tf_op jit(solution)/shard_map/weight_grad_early/pallas_call | solution.py:198
  94.5 1.0 copy-done.10
  95.6 2.2 %stack_planes.1.refs_2_.refs_9_.refs_10_.refs_11_.refs_5_ = bf16[4,4,2,96,384]{4,3,2,1,0:T(8,128)(2,1)S(1)} custom-call(s32[2]{0:T(128)S(1)} %pad_add_fusion.place, bf16[4,2,96,384]{3,2,1,0:T(8,128)(2,1)S(1)} %copy-done.10, bf16[4,2,96,384]{3,2,1,0:T(8,128)(2,1)} %collective-permute-done.3.refs_1_.refs_5_, bf16[4,2,96,384]{3,2,1,0:T(8,128)(2,1)} %after.24.refs_2_, ...), custom_call_target="tpu_custom_call" | custom-call | flops 1048576 | bytes 65536 | tf_op jit(solution)/shard_map/stack_planes/pallas_call | solution.py:455
  97.8 1.4 copy-done
  99.2 1.0 collective-permute-start.14
  101.1 4.1 %collective-permute-start.17 = (bf16[4,4,2,96,384]{4,3,2,1,0:T(8,128)(2,1)S(1)}, bf16[4,4,2,96,384]{4,3,2,1,0:T(8,128)(2,1)S(1)}, u32[]{:S(2)}, u32[]{:S(2)}) collective-permute-start(bf16[4,4,2,96,384]{4,3,2,1,0:T(8,128)(2,1)S(1)} %copy-done.1), channel_id=1, source_target_pairs={{0,1},{1,0},{2,3},{3,2},{4,5},{5,4},{6,7},{7,6},{8,9},{9,8},{10,11... | collective-permute-start | bytes 7077896 | tf_op jit(solution)/shard_map/ppermute | solution.py:26
  105.2 8.6 %weight_grad_late.1 = (f32[4,5,96,384]{3,2,1,0:T(8,128)S(1)}, bf16[2,5,96,384]{3,2,1,0:T(8,128)(2,1)S(1)}, bf16[2,5,96,384]{3,2,1,0:T(8,128)(2,1)S(1)}) custom-call(s32[2]{0:T(128)S(1)} %pad_add_fusion.place, bf16[2048,1152]{1,0:T(8,128)(2,1)} %fusion.2.refs_2_.shifts_ref, f32[1536,1152]{1,0:T(8,128)} %weight_grad_early.1.refs_1_.early_ref, ...), custom_call_target="tpu_custom_call" | custom-call | flops 1048576 | bytes 65536 | tf_op jit(solution)/shard_map/weight_grad_late/pallas_call | solution.py:273
  114.4 1.7 collective-permute-done.15
  116.2 14.9 %collective-permute-done.14.refs_2_.refs_7_ = bf16[21,96,384]{2,1,0:T(8,128)(2,1)} collective-permute-done((bf16[21,96,384]{2,1,0:T(8,128)(2,1)}, bf16[21,96,384]{2,1,0:T(8,128)(2,1)}, u32[]{:S(2)}, u32[]{:S(2)}) %collective-permute-start.14) | collective-permute-done | bytes 1548320 | tf_op jit(solution)/shard_map/ppermute | solution.py:26
  131.1 4.7 %collective-permute-start.21 = (bf16[21,96,384]{2,1,0:T(8,128)(2,1)}, bf16[21,96,384]{2,1,0:T(8,128)(2,1)}, u32[]{:S(2)}, u32[]{:S(2)}) collective-permute-start(bf16[21,96,384]{2,1,0:T(8,128)(2,1)} %collective-permute-done.14.refs_2_.refs_7_), channel_id=1, source_target_pairs={{0,1},{1,0},{2,3},{3,2},{4,5},{5,4},{6,7},{7,6},{8,9},{9,8},{10,11... | collective-permute-start | bytes 4644872 | tf_op jit(solution)/shard_map/ppermute | solution.py:26
  135.9 1.0 collective-permute-start.20
  136.8 1.2 fusion.8
  138.0 2.0 slice.78.refs_0_
  140.0 1.1 copy-done.19
  141.2 1.5 copy-done.18
  143.5 2.0 slice.74.refs_0_
  145.5 1.4 collective-permute-start.19
  146.9 14.4 %input_grad.2.refs_1_.refs_12_ = f32[2,512,768]{2,1,0:T(8,128)} custom-call(s32[2]{0:T(128)} %copy-done.17, bf16[6,96,384]{2,1,0:T(8,128)(2,1)} %copy-done.15, bf16[21,96,384]{2,1,0:T(8,128)(2,1)} %collective-permute-done.13.refs_1_.refs_5_, bf16[21,96,384]{2,1,0:T(8,128)(2,1)} %collective-permute-done.14.refs_2_.refs_7_, ...), custom_call_target="tpu_custom_call" | custom-call | flops 1048576 | bytes 65536 | tf_op jit(solution)/shard_map/input_grad/pallas_call | solution.py:431
  164.2 4.3 %collective-permute-start.26 = (bf16[5,96,384]{2,1,0:T(8,128)(2,1)S(1)}, bf16[5,96,384]{2,1,0:T(8,128)(2,1)S(1)}, u32[]{:S(2)}, u32[]{:S(2)}) collective-permute-start(bf16[5,96,384]{2,1,0:T(8,128)(2,1)S(1)} %copy-done.23), channel_id=1, source_target_pairs={{0,4},{1,5},{2,6},{3,7},{4,0},{5,1},{6,2},{7,3},{8,12},{9,13},{10,... | collective-permute-start | bytes 1105928 | tf_op jit(solution)/shard_map/ppermute | solution.py:26
  170.2 11.8 %input_grad.3.refs_1_ = bf16[1,1024,768]{2,1,0:T(8,128)(2,1)} custom-call(s32[2]{0:T(128)} %copy-done.17, bf16[6,96,384]{2,1,0:T(8,128)(2,1)} %copy-done.15, bf16[21,96,384]{2,1,0:T(8,128)(2,1)} %collective-permute-done.13.refs_1_.refs_5_, bf16[21,96,384]{2,1,0:T(8,128)(2,1)} %collective-permute-done.14.refs_2_.refs_7_, ...), custom_call_target="tpu_custom_call" | custom-call | flops 1048576 | bytes 65536 | tf_op jit(solution)/shard_map/input_grad/pallas_call | solution.py:431
  182.8 9.3 %collective-permute-done.26.refs_0_ = bf16[5,96,384]{2,1,0:T(8,128)(2,1)S(1)} collective-permute-done((bf16[5,96,384]{2,1,0:T(8,128)(2,1)S(1)}, bf16[5,96,384]{2,1,0:T(8,128)(2,1)S(1)}, u32[]{:S(2)}, u32[]{:S(2)}) %collective-permute-start.26) | collective-permute-done | bytes 368672 | tf_op jit(solution)/shard_map/ppermute | solution.py:26
  192.8 7.2 %collective-permute-done.27.refs_0_ = bf16[5,96,384]{2,1,0:T(8,128)(2,1)S(1)} collective-permute-done((bf16[5,96,384]{2,1,0:T(8,128)(2,1)S(1)}, bf16[5,96,384]{2,1,0:T(8,128)(2,1)S(1)}, u32[]{:S(2)}, u32[]{:S(2)}) %collective-permute-start.27) | collective-permute-done | bytes 368672 | tf_op jit(solution)/shard_map/ppermute | solution.py:26
  200.7 2.3 %fusion.5 = f32[5,96,384]{2,1,0:T(8,128)} fusion(bf16[5,96,384]{2,1,0:T(8,128)(2,1)} %after.39, bf16[5,96,384]{2,1,0:T(8,128)(2,1)S(1)} %copy-done.27, bf16[5,96,384]{2,1,0:T(8,128)(2,1)S(1)} %copy-done.29, f32[4,5,96,384]{3,2,1,0:T(8,128)} %copy-done.11, bf16[2,5,96,384]{3,2,1,0:T(8,128)(2,1)S(1)} %copy-done.31), kind=kLoop, calls=%fused_computation.10 | loop fusion | flops 1474560 | bytes 2949120 | tf_op jit(solution)/shard_map/add | solution.py:554
  (124 shorter events, 14.3 us)
Async XLA Ops:
  1.6 7.0 %collective-permute-start = (bf16[2,96,384]{2,1,0:T(8,128)(2,1)S(1)}, bf16[2,96,384]{2,1,0:T(8,128)(2,1)S(1)}, u32[]{:S(2)}, u32[]{:S(2)}) collective-permute-start(bf16[2,96,384]{2,1,0:T(8,128)(2,1)S(1)} %get-tuple-element.20), channel_id=1, source_target_pairs={{0,8},{8,0},{16,24},{24,16},{1,9},{9,1},{17,25},{25,17},{2,10},{10... | collective-permute-start | bytes 442376 | tf_op jit(solution)/shard_map/ppermute | solution.py:26
  2.8 5.8 %collective-permute-start.1 = (bf16[2,96,384]{2,1,0:T(8,128)(2,1)S(1)}, bf16[2,96,384]{2,1,0:T(8,128)(2,1)S(1)}, u32[]{:S(2)}, u32[]{:S(2)}) collective-permute-start(bf16[2,96,384]{2,1,0:T(8,128)(2,1)S(1)} %get-tuple-element.20), channel_id=1, source_target_pairs={{0,16},{8,24},{16,0},{24,8},{1,17},{9,25},{17,1},{25,9},{2,18},{10... | collective-permute-start | bytes 442376 | tf_op jit(solution)/shard_map/ppermute | solution.py:26
  4.1 6.6 %collective-permute-start.2 = (bf16[2,96,384]{2,1,0:T(8,128)(2,1)S(1)}, bf16[2,96,384]{2,1,0:T(8,128)(2,1)S(1)}, u32[]{:S(2)}, u32[]{:S(2)}) collective-permute-start(bf16[2,96,384]{2,1,0:T(8,128)(2,1)S(1)} %get-tuple-element.20), channel_id=1, source_target_pairs={{0,24},{8,16},{16,8},{24,0},{1,25},{9,17},{17,9},{25,1},{2,26},{10... | collective-permute-start | bytes 442376 | tf_op jit(solution)/shard_map/ppermute | solution.py:26
  8.6 3.0 %copy-start.34 = (bf16[2,96,384]{2,1,0:T(8,128)(2,1)}, bf16[2,96,384]{2,1,0:T(8,128)(2,1)S(1)}, u32[]{:S(2)}) copy-start(bf16[2,96,384]{2,1,0:T(8,128)(2,1)S(1)} %collective-permute-done.refs_1_) | copy-start | bytes 442372
  8.6 3.0 %copy-start.35 = (bf16[2,96,384]{2,1,0:T(8,128)(2,1)}, bf16[2,96,384]{2,1,0:T(8,128)(2,1)S(1)}, u32[]{:S(2)}) copy-start(bf16[2,96,384]{2,1,0:T(8,128)(2,1)S(1)} %collective-permute-done.1.refs_2_) | copy-start | bytes 442372
  11.6 3.6 %copy-start.37 = (bf16[5,96,384]{2,1,0:T(8,128)(2,1)S(1)}, bf16[5,96,384]{2,1,0:T(8,128)(2,1)}, u32[]{:S(2)}) copy-start(bf16[5,96,384]{2,1,0:T(8,128)(2,1)} %param.5) | copy-start | bytes 1105924
  11.6 4.3 %copy-start.5 = (bf16[512,1536]{1,0:T(8,128)(2,1)S(1)}, bf16[512,1536]{1,0:T(8,128)(2,1)}, u32[]{:S(2)}) copy-start(bf16[512,1536]{1,0:T(8,128)(2,1)} %after.20.refs_1_.refs_0_) | copy-start | bytes 4718596
  11.6 5.5 %copy-start.3 = (bf16[1,2048,384]{2,1,0:T(8,128)(2,1)S(1)}, bf16[1,2048,384]{2,1,0:T(8,128)(2,1)}, u32[]{:S(2)}) copy-start(bf16[1,2048,384]{2,1,0:T(8,128)(2,1)} %refs_4_.1) | copy-start | bytes 4718596
  11.6 27.3 %collective-permute-start.4 = (bf16[4,2,96,384]{3,2,1,0:T(8,128)(2,1)}, bf16[4,2,96,384]{3,2,1,0:T(8,128)(2,1)}, u32[]{:S(2)}, u32[]{:S(2)}) collective-permute-start(bf16[4,2,96,384]{3,2,1,0:T(8,128)(2,1)} %after.21.refs_0_), channel_id=1, source_target_pairs={{0,6},{1,7},{2,4},{3,5},{4,2},{5,3},{6,0},{7,1},{8,14},{9,15},{10,... | collective-permute-start | bytes 1769480 | tf_op jit(solution)/shard_map/ppermute | solution.py:26
  13.0 26.9 %collective-permute-start.3 = (bf16[4,2,96,384]{3,2,1,0:T(8,128)(2,1)}, bf16[4,2,96,384]{3,2,1,0:T(8,128)(2,1)}, u32[]{:S(2)}, u32[]{:S(2)}) collective-permute-start(bf16[4,2,96,384]{3,2,1,0:T(8,128)(2,1)} %after.21.refs_0_), channel_id=1, source_target_pairs={{0,2},{1,3},{2,0},{3,1},{4,6},{5,7},{6,4},{7,5},{8,10},{9,11},{10,... | collective-permute-start | bytes 1769480 | tf_op jit(solution)/shard_map/ppermute | solution.py:26
  15.9 35.5 %collective-permute-start.10 = (bf16[512,1536]{1,0:T(8,128)(2,1)S(1)}, bf16[512,1536]{1,0:T(8,128)(2,1)}, u32[]{:S(2)}, u32[]{:S(2)}) collective-permute-start(bf16[512,1536]{1,0:T(8,128)(2,1)S(1)} %copy-done.5), channel_id=1, source_target_pairs={{0,16},{8,24},{16,0},{24,8},{1,17},{9,25},{17,1},{25,9},{2,18},{10... | collective-permute-start | bytes 4718600 | tf_op jit(solution)/shard_map/ppermute | solution.py:26
  16.1 39.1 %collective-permute-start.8 = (bf16[512,1536]{1,0:T(8,128)(2,1)S(1)}, bf16[512,1536]{1,0:T(8,128)(2,1)}, u32[]{:S(2)}, u32[]{:S(2)}) collective-permute-start(bf16[512,1536]{1,0:T(8,128)(2,1)S(1)} %copy-done.5), channel_id=1, source_target_pairs={{0,8},{8,0},{16,24},{24,16},{1,9},{9,1},{17,25},{25,17},{2,10},{10... | collective-permute-start | bytes 4718600 | tf_op jit(solution)/shard_map/ppermute | solution.py:26
  40.0 13.5 %collective-permute-start.6 = (bf16[3,96,384]{2,1,0:T(8,128)(2,1)}, bf16[3,96,384]{2,1,0:T(8,128)(2,1)S(1)}, u32[]{:S(2)}, u32[]{:S(2)}) collective-permute-start(bf16[3,96,384]{2,1,0:T(8,128)(2,1)} %after.22.refs_0_), channel_id=1, source_target_pairs={{0,6},{1,7},{2,4},{3,5},{4,2},{5,3},{6,0},{7,1},{8,14},{9,15},{10,... | collective-permute-start | bytes 663560 | tf_op jit(solution)/shard_map/ppermute | solution.py:26
  40.0 13.5 %collective-permute-start.5 = (bf16[3,96,384]{2,1,0:T(8,128)(2,1)}, bf16[3,96,384]{2,1,0:T(8,128)(2,1)}, u32[]{:S(2)}, u32[]{:S(2)}) collective-permute-start(bf16[3,96,384]{2,1,0:T(8,128)(2,1)} %after.22.refs_0_), channel_id=1, source_target_pairs={{0,2},{1,3},{2,0},{3,1},{4,6},{5,7},{6,4},{7,5},{8,10},{9,11},{10,... | collective-permute-start | bytes 663560 | tf_op jit(solution)/shard_map/ppermute | solution.py:26
  42.1 5.4 %copy-start.7 = (bf16[1,1024,768]{2,1,0:T(8,128)(2,1)S(1)}, bf16[1,1024,768]{2,1,0:T(8,128)(2,1)}, u32[]{:S(2)}) copy-start(bf16[1,1024,768]{2,1,0:T(8,128)(2,1)} %x_ref.3) | copy-start | bytes 4718596
  49.8 1.6 copy-start.2
  54.2 45.0 %collective-permute-start.12 = (bf16[256,1536]{1,0:T(8,128)(2,1)}, bf16[256,1536]{1,0:T(8,128)(2,1)}, u32[]{:S(2)}, u32[]{:S(2)}) collective-permute-start(bf16[256,1536]{1,0:T(8,128)(2,1)} %after.26), channel_id=1, source_target_pairs={{0,8},{8,0},{16,24},{24,16},{1,9},{9,1},{17,25},{25,17},{2,10},{10... | collective-permute-start | bytes 2359304 | tf_op jit(solution)/shard_map/ppermute | solution.py:26
  57.3 17.4 %copy-start.12 = (bf16[3,96,384]{2,1,0:T(8,128)(2,1)S(1)}, bf16[3,96,384]{2,1,0:T(8,128)(2,1)}, u32[]{:S(2)}) copy-start(bf16[3,96,384]{2,1,0:T(8,128)(2,1)} %after.22.refs_0_) | copy-start | bytes 663556
  57.3 41.9 %collective-permute-start.9 = (bf16[256,1536]{1,0:T(8,128)(2,1)}, bf16[256,1536]{1,0:T(8,128)(2,1)}, u32[]{:S(2)}, u32[]{:S(2)}) collective-permute-start(bf16[256,1536]{1,0:T(8,128)(2,1)} %after.23), channel_id=1, source_target_pairs={{0,16},{8,24},{16,0},{24,8},{1,17},{9,25},{17,1},{25,9},{2,18},{10... | collective-permute-start | bytes 2359304 | tf_op jit(solution)/shard_map/ppermute | solution.py:26
  57.6 36.9 %collective-permute-start.11 = (bf16[4,2,96,384]{3,2,1,0:T(8,128)(2,1)}, bf16[4,2,96,384]{3,2,1,0:T(8,128)(2,1)}, u32[]{:S(2)}, u32[]{:S(2)}) collective-permute-start(bf16[4,2,96,384]{3,2,1,0:T(8,128)(2,1)} %collective-permute-done.4.refs_2_.refs_6_.refs_3_), channel_id=1, source_target_pairs={{0,2},{1,3},{2,0},{3,1},{4,6},{5,7},{6,4},{7,5},{8,10},{9,11},{10,... | collective-permute-start | bytes 1769480 | tf_op jit(solution)/shard_map/ppermute | solution.py:26
  57.7 17.0 %collective-permute-start.7 = (bf16[3,96,384]{2,1,0:T(8,128)(2,1)}, bf16[3,96,384]{2,1,0:T(8,128)(2,1)}, u32[]{:S(2)}, u32[]{:S(2)}) collective-permute-start(bf16[3,96,384]{2,1,0:T(8,128)(2,1)} %copy-done.13), channel_id=1, source_target_pairs={{0,2},{1,3},{2,0},{3,1},{4,6},{5,7},{6,4},{7,5},{8,10},{9,11},{10,... | collective-permute-start | bytes 663560 | tf_op jit(solution)/shard_map/ppermute | solution.py:26
  59.2 46.0 %copy-start.17 = (s32[2]{0:T(128)}, s32[2]{0:T(128)S(1)}, u32[]{:S(2)}) copy-start(s32[2]{0:T(128)S(1)} %pad_add_fusion.place) | copy-start | bytes 28
  99.2 1.9 copy-start.1
  99.2 31.9 %collective-permute-start.14 = (bf16[21,96,384]{2,1,0:T(8,128)(2,1)}, bf16[21,96,384]{2,1,0:T(8,128)(2,1)}, u32[]{:S(2)}, u32[]{:S(2)}) collective-permute-start(bf16[21,96,384]{2,1,0:T(8,128)(2,1)} %after.29.refs_3_), channel_id=1, source_target_pairs={{0,16},{8,24},{16,0},{24,8},{1,17},{9,25},{17,1},{25,9},{2,18},{10... | collective-permute-start | bytes 4644872 | tf_op jit(solution)/shard_map/ppermute | solution.py:26
  100.2 13.7 %copy-start.9 = (bf16[21,96,384]{2,1,0:T(8,128)(2,1)S(1)}, bf16[21,96,384]{2,1,0:T(8,128)(2,1)}, u32[]{:S(2)}) copy-start(bf16[21,96,384]{2,1,0:T(8,128)(2,1)} %after.29.refs_3_) | copy-start | bytes 4644868
  100.2 35.6 %collective-permute-start.13 = (bf16[21,96,384]{2,1,0:T(8,128)(2,1)}, bf16[21,96,384]{2,1,0:T(8,128)(2,1)}, u32[]{:S(2)}, u32[]{:S(2)}) collective-permute-start(bf16[21,96,384]{2,1,0:T(8,128)(2,1)} %after.28), channel_id=1, source_target_pairs={{0,8},{8,0},{16,24},{24,16},{1,9},{9,1},{17,25},{25,17},{2,10},{10... | collective-permute-start | bytes 4644872 | tf_op jit(solution)/shard_map/ppermute | solution.py:26
  101.1 39.0 %collective-permute-start.17 = (bf16[4,4,2,96,384]{4,3,2,1,0:T(8,128)(2,1)S(1)}, bf16[4,4,2,96,384]{4,3,2,1,0:T(8,128)(2,1)S(1)}, u32[]{:S(2)}, u32[]{:S(2)}) collective-permute-start(bf16[4,4,2,96,384]{4,3,2,1,0:T(8,128)(2,1)S(1)} %copy-done.1), channel_id=1, source_target_pairs={{0,1},{1,0},{2,3},{3,2},{4,5},{5,4},{6,7},{7,6},{8,9},{9,8},{10,11... | collective-permute-start | bytes 7077896 | tf_op jit(solution)/shard_map/ppermute | solution.py:26
  113.8 26.2 %copy-start.11 = (f32[4,5,96,384]{3,2,1,0:T(8,128)}, f32[4,5,96,384]{3,2,1,0:T(8,128)S(1)}, u32[]{:S(2)}) copy-start(f32[4,5,96,384]{3,2,1,0:T(8,128)S(1)} %get-tuple-element.11) | copy-start | bytes 8847364
  113.8 2.3 %collective-permute-start.15 = (bf16[2,5,96,384]{3,2,1,0:T(8,128)(2,1)S(1)}, bf16[2,5,96,384]{3,2,1,0:T(8,128)(2,1)S(1)}, u32[]{:S(2)}, u32[]{:S(2)}) collective-permute-start(bf16[2,5,96,384]{3,2,1,0:T(8,128)(2,1)S(1)} %get-tuple-element.12), channel_id=1, source_target_pairs={{0,1},{1,0},{2,3},{3,2},{4,5},{5,4},{6,7},{7,6},{8,9},{9,8},{10,11... | collective-permute-start | bytes 2211848 | tf_op jit(solution)/shard_map/ppermute | solution.py:26
  113.9 26.1 %collective-permute-start.16 = (bf16[21,96,384]{2,1,0:T(8,128)(2,1)S(1)}, bf16[21,96,384]{2,1,0:T(8,128)(2,1)S(1)}, u32[]{:S(2)}, u32[]{:S(2)}) collective-permute-start(bf16[21,96,384]{2,1,0:T(8,128)(2,1)S(1)} %copy-done.9), channel_id=1, source_target_pairs={{0,1},{1,0},{2,3},{3,2},{4,5},{5,4},{6,7},{7,6},{8,9},{9,8},{10,11... | collective-permute-start | bytes 4644872 | tf_op jit(solution)/shard_map/ppermute | solution.py:26
  116.1 24.0 %copy-start.30 = (bf16[2,5,96,384]{3,2,1,0:T(8,128)(2,1)}, bf16[2,5,96,384]{3,2,1,0:T(8,128)(2,1)S(1)}, u32[]{:S(2)}) copy-start(bf16[2,5,96,384]{3,2,1,0:T(8,128)(2,1)S(1)} %collective-permute-done.15) | copy-start | bytes 2211844
  116.1 20.7 %collective-permute-start.18 = (bf16[2,5,96,384]{3,2,1,0:T(8,128)(2,1)S(1)}, bf16[2,5,96,384]{3,2,1,0:T(8,128)(2,1)S(1)}, u32[]{:S(2)}, u32[]{:S(2)}) collective-permute-start(bf16[2,5,96,384]{3,2,1,0:T(8,128)(2,1)S(1)} %get-tuple-element.13), channel_id=1, source_target_pairs={{0,1},{1,0},{2,3},{3,2},{4,5},{5,4},{6,7},{7,6},{8,9},{9,8},{10,11... | collective-permute-start | bytes 2211848 | tf_op jit(solution)/shard_map/ppermute | solution.py:26
  131.1 15.8 %collective-permute-start.21 = (bf16[21,96,384]{2,1,0:T(8,128)(2,1)}, bf16[21,96,384]{2,1,0:T(8,128)(2,1)}, u32[]{:S(2)}, u32[]{:S(2)}) collective-permute-start(bf16[21,96,384]{2,1,0:T(8,128)(2,1)} %collective-permute-done.14.refs_2_.refs_7_), channel_id=1, source_target_pairs={{0,1},{1,0},{2,3},{3,2},{4,5},{5,4},{6,7},{7,6},{8,9},{9,8},{10,11... | collective-permute-start | bytes 4644872 | tf_op jit(solution)/shard_map/ppermute | solution.py:26
  135.9 11.0 %collective-permute-start.20 = (bf16[21,96,384]{2,1,0:T(8,128)(2,1)}, bf16[21,96,384]{2,1,0:T(8,128)(2,1)}, u32[]{:S(2)}, u32[]{:S(2)}) collective-permute-start(bf16[21,96,384]{2,1,0:T(8,128)(2,1)} %collective-permute-done.13.refs_1_.refs_5_), channel_id=1, source_target_pairs={{0,1},{1,0},{2,3},{3,2},{4,5},{5,4},{6,7},{7,6},{8,9},{9,8},{10,11... | collective-permute-start | bytes 4644872 | tf_op jit(solution)/shard_map/ppermute | solution.py:26
  141.2 1.5 copy-start.18
  142.6 18.6 %collective-permute-start.22 = (bf16[9,96,384]{2,1,0:T(8,128)(2,1)}, bf16[9,96,384]{2,1,0:T(8,128)(2,1)S(1)}, u32[]{:S(2)}, u32[]{:S(2)}) collective-permute-start(bf16[9,96,384]{2,1,0:T(8,128)(2,1)} %after.35), channel_id=1, source_target_pairs={{0,8},{8,0},{16,24},{24,16},{1,9},{9,1},{17,25},{25,17},{2,10},{10... | collective-permute-start | bytes 1990664 | tf_op jit(solution)/shard_map/ppermute | solution.py:26
  145.5 17.2 %collective-permute-start.19 = (bf16[9,96,384]{2,1,0:T(8,128)(2,1)}, bf16[9,96,384]{2,1,0:T(8,128)(2,1)S(1)}, u32[]{:S(2)}, u32[]{:S(2)}) collective-permute-start(bf16[9,96,384]{2,1,0:T(8,128)(2,1)} %after.33), channel_id=1, source_target_pairs={{0,16},{8,24},{16,0},{24,8},{1,17},{9,25},{17,1},{25,9},{2,18},{10... | collective-permute-start | bytes 1990664 | tf_op jit(solution)/shard_map/ppermute | solution.py:26
  162.1 1.8 copy-start.22
  162.1 2.1 %copy-start.23 = (bf16[5,96,384]{2,1,0:T(8,128)(2,1)S(1)}, bf16[5,96,384]{2,1,0:T(8,128)(2,1)}, u32[]{:S(2)}) copy-start(bf16[5,96,384]{2,1,0:T(8,128)(2,1)} %after.31.refs_2_) | copy-start | bytes 1105924
  162.1 6.4 %copy-start.24 = (bf16[5,96,384]{2,1,0:T(8,128)(2,1)S(1)}, bf16[5,96,384]{2,1,0:T(8,128)(2,1)}, u32[]{:S(2)}) copy-start(bf16[5,96,384]{2,1,0:T(8,128)(2,1)} %after.32.refs_3_) | copy-start | bytes 1105924
  162.1 6.4 %collective-permute-start.24 = (bf16[9,96,384]{2,1,0:T(8,128)(2,1)}, bf16[9,96,384]{2,1,0:T(8,128)(2,1)S(1)}, u32[]{:S(2)}, u32[]{:S(2)}) collective-permute-start(bf16[9,96,384]{2,1,0:T(8,128)(2,1)} %after.36.refs_4_.refs_9_), channel_id=1, source_target_pairs={{0,1},{1,0},{2,3},{3,2},{4,5},{5,4},{6,7},{7,6},{8,9},{9,8},{10,11... | collective-permute-start | bytes 1990664 | tf_op jit(solution)/shard_map/ppermute | solution.py:26
  163.5 5.0 %collective-permute-start.23 = (bf16[9,96,384]{2,1,0:T(8,128)(2,1)}, bf16[9,96,384]{2,1,0:T(8,128)(2,1)S(1)}, u32[]{:S(2)}, u32[]{:S(2)}) collective-permute-start(bf16[9,96,384]{2,1,0:T(8,128)(2,1)} %after.34.refs_3_.refs_7_), channel_id=1, source_target_pairs={{0,1},{1,0},{2,3},{3,2},{4,5},{5,4},{6,7},{7,6},{8,9},{9,8},{10,11... | collective-permute-start | bytes 1990664 | tf_op jit(solution)/shard_map/ppermute | solution.py:26
  163.9 18.1 %collective-permute-start.25 = (bf16[5,96,384]{2,1,0:T(8,128)(2,1)S(1)}, bf16[5,96,384]{2,1,0:T(8,128)(2,1)S(1)}, u32[]{:S(2)}, u32[]{:S(2)}) collective-permute-start(bf16[5,96,384]{2,1,0:T(8,128)(2,1)S(1)} %copy-done.22), channel_id=1, source_target_pairs={{0,2},{1,3},{2,0},{3,1},{4,6},{5,7},{6,4},{7,5},{8,10},{9,11},{10,... | collective-permute-start | bytes 1105928 | tf_op jit(solution)/shard_map/ppermute | solution.py:26
  164.2 27.9 %collective-permute-start.26 = (bf16[5,96,384]{2,1,0:T(8,128)(2,1)S(1)}, bf16[5,96,384]{2,1,0:T(8,128)(2,1)S(1)}, u32[]{:S(2)}, u32[]{:S(2)}) collective-permute-start(bf16[5,96,384]{2,1,0:T(8,128)(2,1)S(1)} %copy-done.23), channel_id=1, source_target_pairs={{0,4},{1,5},{2,6},{3,7},{4,0},{5,1},{6,2},{7,3},{8,12},{9,13},{10,... | collective-permute-start | bytes 1105928 | tf_op jit(solution)/shard_map/ppermute | solution.py:26
  168.5 31.4 %collective-permute-start.27 = (bf16[5,96,384]{2,1,0:T(8,128)(2,1)S(1)}, bf16[5,96,384]{2,1,0:T(8,128)(2,1)S(1)}, u32[]{:S(2)}, u32[]{:S(2)}) collective-permute-start(bf16[5,96,384]{2,1,0:T(8,128)(2,1)S(1)} %copy-done.24), channel_id=1, source_target_pairs={{0,6},{1,7},{2,4},{3,5},{4,2},{5,3},{6,0},{7,1},{8,14},{9,15},{10,... | collective-permute-start | bytes 1105928 | tf_op jit(solution)/shard_map/ppermute | solution.py:26
  182.8 17.9 %copy-start.29 = (bf16[5,96,384]{2,1,0:T(8,128)(2,1)S(1)}, bf16[5,96,384]{2,1,0:T(8,128)(2,1)}, u32[]{:S(2)}) copy-start(bf16[5,96,384]{2,1,0:T(8,128)(2,1)} %after.37) | copy-start | bytes 1105924
  182.8 17.9 %copy-start.31 = (bf16[2,5,96,384]{3,2,1,0:T(8,128)(2,1)S(1)}, bf16[2,5,96,384]{3,2,1,0:T(8,128)(2,1)}, u32[]{:S(2)}) copy-start(bf16[2,5,96,384]{3,2,1,0:T(8,128)(2,1)} %copy-done.30) | copy-start | bytes 2211844
  192.8 7.9 %copy-start.27 = (bf16[5,96,384]{2,1,0:T(8,128)(2,1)S(1)}, bf16[5,96,384]{2,1,0:T(8,128)(2,1)}, u32[]{:S(2)}) copy-start(bf16[5,96,384]{2,1,0:T(8,128)(2,1)} %after.38) | copy-start | bytes 1105924
  (18 other events, 17.4 us)

commit v17 on v16

--- a/solution.py
+++ b/solution.py
@@ -481,16 +481,16 @@
     act = after(activate(inputs), *across[1:])
     beside, below = from_peer(act, "seq", 1), from_peer(act, "seq", 2)
     slope = half_slope(inputs)
-    line_across = gather_line(after(jnp.stack(across), act), "rep", planes, 2)
+    line = gather_line(weights[:SPLIT], "rep", planes, 2)
+    line_across = gather_line(after(jnp.stack(across), act, *line[1:]), "rep", planes, 2)
     crossing = (line_across[1], line_across[planes - 1])
-    line = gather_line(after(weights[:SPLIT], *crossing), "rep", planes, 2)
     trunk = trunk_grad[0]
     zeros = jnp.zeros((1, block), jnp.bfloat16)
     later = jnp.concatenate([trunk[1:], zeros])
     earlier = jnp.concatenate([zeros, trunk[:-1]])
     shifts = jnp.concatenate([later, trunk, earlier], axis=1)
     to_beside, to_below, own_window = kernel_messages(place, line, trunk_grad, coarse)
-    ready = (slope, shifts, line[1], line[planes - 1], *crossing)
+    ready = (slope, shifts, to_beside, *crossing)
     top, bottom = after(beside[:half], *ready), after(below[half:], *ready)
     far_top, far_bottom = from_peer(top, "seq", 2), from_peer(bottom, "seq", 1)
 
@@ -543,7 +543,7 @@
     ]
     near = [piece for piece in crossed if piece[-1] < 3]
     begun = stage(windows, pieces=soon + near, distances=[0, 1, 2], begun=None)
-    far_first, far_second = after(far_first, begun), after(far_second, begun)
+    far_first, far_second = after(far_first, begun, *summed), after(far_second, begun, *summed)
     windows.append([(far_first, 0, 0, side), (far_second, count // 2, side, side)])
     rest = [piece for piece in crossed if piece[-1] == 3]
     for part, start, plane in ((far_first, side, 0), (far_second, 0, planes // 2)):

time: 205 us -> 186 us (0.907)
  the two profiles are of different devices: /device:TPU:9 before, /device:TPU:0 now
where the time goes in v17:
time: 186 us
  waiting for transfers between devices  57.9 us (31%)
  Pallas kernels  55 us (30%)
  local copies, waits for them, and re-layouts  36.6 us (20%)
  starting transfers between devices  25.2 us (14%)
  other arithmetic  9.8 us (5%)
    ppermute x28, waiting for transfers between devices, from_peer(): return lax.ppermute(value, axis, [(i, i ^ distance) for i in range(peers)])  57.9 us
    pallas_call x2, Pallas kernels, gradient_stage(): pl.pallas_call(body, out_shape=out_shape, grid_spec=pltpu.PrefetchScalarG...  25.9 us
    ppermute x28, starting transfers between devices, from_peer(): return lax.ppermute(value, axis, [(i, i ^ distance) for i in range(peers)])  25.2 us
    unnamed x102, local copies, waits for them, and re-layouts  24.4 us
    pallas_call x1, Pallas kernels, early_terms(): pl.pallas_call(kernel, out_shape=jax.ShapeDtypeStruct((both, columns), jn...  13.8 us
    pallas_call x1, Pallas kernels, late_terms(): pl.pallas_call(kernel, out_shape=(jax.ShapeDtypeStruct(shape, jnp.float32...  8.37 us
    concatenate x1, other arithmetic, on_device_square(): shifts = jnp.concatenate([later, trunk, earlier], axis=1)  5.42 us
    slice x2, local copies, waits for them, and re-layouts, on_device_square(): top, bottom = (after(beside[:half], *ready), after(below[half:], *ready))  4.17 us
  transfers between devices with their start and end apart: 28, of which 9 were waited for; matrix products, arithmetic and copies ran while one was open for 10% of the time, Pallas kernels for 23%

profile of v17, /device:TPU:0, one launch (start us, length us, event | category | flops | bytes accessed | tf_op | source)
XLA Modules:
  0.0 185.6 jit_solution(18129278313022978621)
XLA Ops:
  0.6 1.0 slice.54.refs_0_
  1.6 5.1 %collective-permute-start.1 = (bf16[3,96,384]{2,1,0:T(8,128)(2,1)S(1)}, bf16[3,96,384]{2,1,0:T(8,128)(2,1)S(1)}, u32[]{:S(2)}, u32[]{:S(2)}) collective-permute-start(bf16[3,96,384]{2,1,0:T(8,128)(2,1)S(1)} %slice.54.refs_0_), channel_id=1, source_target_pairs={{0,6},{1,7},{2,4},{3,5},{4,2},{5,3},{6,0},{7,1},{8,14},{9,15},{10,... | collective-permute-start | bytes 663560 | tf_op jit(solution)/shard_map/ppermute | solution.py:26
  7.6 1.6 collective-permute-start.3
  9.2 1.5 collective-permute-start.4
  11.2 1.4 copy-done.11
  12.6 1.8 act.1.refs_0_
  14.4 1.1 copy-done.4
  15.5 2.0 %collective-permute-done.4.refs_2_ = bf16[2,96,384]{2,1,0:T(8,128)(2,1)S(1)} collective-permute-done((bf16[2,96,384]{2,1,0:T(8,128)(2,1)S(1)}, bf16[2,96,384]{2,1,0:T(8,128)(2,1)S(1)}, u32[]{:S(2)}, u32[]{:S(2)}) %collective-permute-start.4) | collective-permute-done | bytes 147488 | tf_op jit(solution)/shard_map/ppermute | solution.py:26
  18.8 1.4 collective-permute-start.10
  20.8 1.2 collective-permute-start.2
  22.0 2.1 %slice_bitcast_fusion.1 = (bf16[2047,384]{1,0:T(8,128)(2,1)}, bf16[2047,384]{1,0:T(8,128)(2,1)}) fusion(bf16[1,2048,384]{2,1,0:T(8,128)(2,1)S(1)} %copy-done.3), kind=kLoop, calls=%fused_computation.7 | loop fusion | bytes 6288384 | tf_op jit(solution)/shard_map/slice | solution.py:489
  25.0 1.7 collective-permute-done.2.refs_2_.refs_3_
  27.7 1.3 collective-permute-start.7
  29.0 5.4 %fusion.2.refs_2_.shifts_ref = bf16[2048,1152]{1,0:T(8,128)(2,1)} fusion(bf16[2047,384]{1,0:T(8,128)(2,1)} %get-tuple-element.18, bf16[2047,384]{1,0:T(8,128)(2,1)} %get-tuple-element.17, bf16[2048,384]{1,0:T(8,128)(2,1)S(1)} %bitcast.24), kind=kLoop, calls=%fused_computation.4 | loop fusion | flops 23592960 | bytes 9435648 | tf_op jit(solution)/shard_map/concatenate | solution.py:491
  34.5 2.3 %half_slope.1.refs_1_.refs_11_ = f32[2,512,768]{2,1,0:T(8,128)S(1)} custom-call(bf16[1,1024,768]{2,1,0:T(8,128)(2,1)S(1)} %copy-done.12), custom_call_target="tpu_custom_call" | custom-call | tf_op jit(solution)/shard_map/half_slope/pallas_call | solution.py:152
  36.8 1.6 copy-done.2
  39.5 1.0 kernel_messages.1
  40.5 1.2 copy-done.6
  41.7 1.1 copy-done.13
  42.8 10.5 %collective-permute-done.10.refs_2_ = bf16[512,1536]{1,0:T(8,128)(2,1)} collective-permute-done((bf16[512,1536]{1,0:T(8,128)(2,1)}, bf16[512,1536]{1,0:T(8,128)(2,1)}, u32[]{:S(2)}, u32[]{:S(2)}) %collective-permute-start.10) | collective-permute-done | bytes 1572896 | tf_op jit(solution)/shard_map/ppermute | solution.py:26
  53.3 2.1 %slice.73.refs_0_ = bf16[256,1536]{1,0:T(8,128)(2,1)} slice(bf16[512,1536]{1,0:T(8,128)(2,1)} %collective-permute-done.10.refs_2_), slice={[256:512], [0:1536]} | slice | bytes 1572864 | tf_op jit(solution)/shard_map/slice | solution.py:494
  56.5 1.3 collective-permute-start.12
  57.8 2.1 %slice.72.refs_0_ = bf16[256,1536]{1,0:T(8,128)(2,1)} slice(bf16[512,1536]{1,0:T(8,128)(2,1)} %collective-permute-done.6.refs_1_), slice={[0:256], [0:1536]} | slice | bytes 1572864 | tf_op jit(solution)/shard_map/slice | solution.py:494
  60.6 1.7 collective-permute-start.11
  62.3 13.8 %weight_grad_early.1.refs_1_.early_ref = f32[1536,1152]{1,0:T(8,128)} custom-call(s32[2]{0:T(128)S(1)} %pad_add_fusion.place, bf16[2048,1152]{1,0:T(8,128)(2,1)} %fusion.2.refs_2_.shifts_ref, bf16[512,1536]{1,0:T(8,128)(2,1)S(1)} %copy-done.5, bf16[512,1536]{1,0:T(8,128)(2,1)} %collective-permute-done.6.refs_1_, ...), custom_call_target="tpu_custom_call" | custom-call | flops 1048576 | bytes 65536 | tf_op jit(solution)/shard_map/weight_grad_early/pallas_call | solution.py:198
  76.2 1.0 copy-done.15
  77.6 1.8 stack_planes.1.refs_2_.refs_9_.refs_10_.refs_11_.refs_5_
  79.4 1.4 copy-done
  80.8 1.0 copy-done.7
  84.5 1.1 copy-done.10
  85.6 8.4 %weight_grad_late.1 = (f32[4,5,96,384]{3,2,1,0:T(8,128)S(1)}, bf16[2,5,96,384]{3,2,1,0:T(8,128)(2,1)S(1)}, bf16[2,5,96,384]{3,2,1,0:T(8,128)(2,1)S(1)}) custom-call(s32[2]{0:T(128)S(1)} %pad_add_fusion.place, bf16[2048,1152]{1,0:T(8,128)(2,1)} %fusion.2.refs_2_.shifts_ref, f32[1536,1152]{1,0:T(8,128)} %weight_grad_early.1.refs_1_.early_ref, ...), custom_call_target="tpu_custom_call" | custom-call | flops 1048576 | bytes 65536 | tf_op jit(solution)/shard_map/weight_grad_late/pallas_call | solution.py:273
  94.6 20.8 %collective-permute-done.14.refs_2_.refs_7_ = bf16[21,96,384]{2,1,0:T(8,128)(2,1)} collective-permute-done((bf16[21,96,384]{2,1,0:T(8,128)(2,1)}, bf16[21,96,384]{2,1,0:T(8,128)(2,1)}, u32[]{:S(2)}, u32[]{:S(2)}) %collective-permute-start.14) | collective-permute-done | bytes 1548320 | tf_op jit(solution)/shard_map/ppermute | solution.py:26
  116.2 4.7 %collective-permute-done.18 = bf16[2,5,96,384]{3,2,1,0:T(8,128)(2,1)S(1)} collective-permute-done((bf16[2,5,96,384]{3,2,1,0:T(8,128)(2,1)S(1)}, bf16[2,5,96,384]{3,2,1,0:T(8,128)(2,1)S(1)}, u32[]{:S(2)}, u32[]{:S(2)}) %collective-permute-start.18) | collective-permute-done | bytes 737312 | tf_op jit(solution)/shard_map/ppermute | solution.py:26
  120.9 1.1 fusion.8
  122.0 2.0 %slice.78.refs_0_ = bf16[9,96,384]{2,1,0:T(8,128)(2,1)} slice(bf16[21,96,384]{2,1,0:T(8,128)(2,1)} %collective-permute-done.14.refs_2_.refs_7_), slice={[6:15], [0:96], [0:384]} | slice | bytes 1327104 | tf_op jit(solution)/shard_map/slice | solution.py:526
  124.0 1.1 copy-done.30
  125.2 1.5 copy-done.29
  127.2 2.0 %slice.74.refs_0_ = bf16[9,96,384]{2,1,0:T(8,128)(2,1)} slice(bf16[21,96,384]{2,1,0:T(8,128)(2,1)} %collective-permute-done.13.refs_1_.refs_5_), slice={[0:9], [0:96], [0:384]} | slice | bytes 1327104 | tf_op jit(solution)/shard_map/slice | solution.py:525
  129.8 1.8 collective-permute-start.24
  131.5 1.2 collective-permute-start.23
  132.7 1.5 collective-permute-start.22
  134.2 14.2 %input_grad.2.refs_1_.refs_12_ = f32[2,512,768]{2,1,0:T(8,128)} custom-call(s32[2]{0:T(128)} %copy-done.28, bf16[6,96,384]{2,1,0:T(8,128)(2,1)} %copy-done.21, bf16[21,96,384]{2,1,0:T(8,128)(2,1)} %collective-permute-done.13.refs_1_.refs_5_, bf16[21,96,384]{2,1,0:T(8,128)(2,1)} %collective-permute-done.14.refs_2_.refs_7_, ...), custom_call_target="tpu_custom_call" | custom-call | flops 1048576 | bytes 65536 | tf_op jit(solution)/shard_map/input_grad/pallas_call | solution.py:431
  148.4 16.0 %collective-permute-done.23.refs_3_.refs_0_ = bf16[5,96,384]{2,1,0:T(8,128)(2,1)S(1)} collective-permute-done((bf16[5,96,384]{2,1,0:T(8,128)(2,1)S(1)}, bf16[5,96,384]{2,1,0:T(8,128)(2,1)S(1)}, u32[]{:S(2)}, u32[]{:S(2)}) %collective-permute-start.23) | collective-permute-done | bytes 368672 | tf_op jit(solution)/shard_map/ppermute | solution.py:26
  167.5 1.0 collective-permute-done.27.refs_10_
  168.5 1.0 collective-permute-done.26.refs_8_
  170.3 11.6 %input_grad.3.refs_1_ = bf16[1,1024,768]{2,1,0:T(8,128)(2,1)} custom-call(s32[2]{0:T(128)} %copy-done.28, bf16[6,96,384]{2,1,0:T(8,128)(2,1)} %copy-done.21, bf16[21,96,384]{2,1,0:T(8,128)(2,1)} %collective-permute-done.13.refs_1_.refs_5_, bf16[21,96,384]{2,1,0:T(8,128)(2,1)} %collective-permute-done.14.refs_2_.refs_7_, ...), custom_call_target="tpu_custom_call" | custom-call | flops 1048576 | bytes 65536 | tf_op jit(solution)/shard_map/input_grad/pallas_call | solution.py:431
  182.0 0.9 copy-done.40
  183.3 2.3 %fusion.5 = f32[5,96,384]{2,1,0:T(8,128)} fusion(bf16[5,96,384]{2,1,0:T(8,128)(2,1)} %after.37, bf16[5,96,384]{2,1,0:T(8,128)(2,1)S(1)} %copy-done.38, bf16[5,96,384]{2,1,0:T(8,128)(2,1)S(1)} %copy-done.40, f32[4,5,96,384]{3,2,1,0:T(8,128)} %copy-done.20, bf16[2,5,96,384]{3,2,1,0:T(8,128)(2,1)S(1)} %copy-done.42), kind=kLoop, calls=%fused_computation.10 | loop fusion | flops 1474560 | bytes 2949120 | tf_op jit(solution)/shard_map/add | solution.py:554
  (149 shorter events, 17.9 us)
Async XLA Ops:
  1.6 19.2 %collective-permute-start.1 = (bf16[3,96,384]{2,1,0:T(8,128)(2,1)S(1)}, bf16[3,96,384]{2,1,0:T(8,128)(2,1)S(1)}, u32[]{:S(2)}, u32[]{:S(2)}) collective-permute-start(bf16[3,96,384]{2,1,0:T(8,128)(2,1)S(1)} %slice.54.refs_0_), channel_id=1, source_target_pairs={{0,6},{1,7},{2,4},{3,5},{4,2},{5,3},{6,0},{7,1},{8,14},{9,15},{10,... | collective-permute-start | bytes 663560 | tf_op jit(solution)/shard_map/ppermute | solution.py:26
  7.6 7.9 %collective-permute-start.3 = (bf16[2,96,384]{2,1,0:T(8,128)(2,1)S(1)}, bf16[2,96,384]{2,1,0:T(8,128)(2,1)S(1)}, u32[]{:S(2)}, u32[]{:S(2)}) collective-permute-start(bf16[2,96,384]{2,1,0:T(8,128)(2,1)S(1)} %get-tuple-element.20), channel_id=1, source_target_pairs={{0,8},{8,0},{16,24},{24,16},{1,9},{9,1},{17,25},{25,17},{2,10},{10... | collective-permute-start | bytes 442376 | tf_op jit(solution)/shard_map/ppermute | solution.py:26
  9.2 8.3 %collective-permute-start.4 = (bf16[2,96,384]{2,1,0:T(8,128)(2,1)S(1)}, bf16[2,96,384]{2,1,0:T(8,128)(2,1)S(1)}, u32[]{:S(2)}, u32[]{:S(2)}) collective-permute-start(bf16[2,96,384]{2,1,0:T(8,128)(2,1)S(1)} %get-tuple-element.20), channel_id=1, source_target_pairs={{0,16},{8,24},{16,0},{24,8},{1,17},{9,25},{17,1},{25,9},{2,18},{10... | collective-permute-start | bytes 442376 | tf_op jit(solution)/shard_map/ppermute | solution.py:26
  10.7 6.8 %collective-permute-start.5 = (bf16[2,96,384]{2,1,0:T(8,128)(2,1)S(1)}, bf16[2,96,384]{2,1,0:T(8,128)(2,1)S(1)}, u32[]{:S(2)}, u32[]{:S(2)}) collective-permute-start(bf16[2,96,384]{2,1,0:T(8,128)(2,1)S(1)} %get-tuple-element.20), channel_id=1, source_target_pairs={{0,24},{8,16},{16,8},{24,0},{1,25},{9,17},{17,9},{25,1},{2,26},{10... | collective-permute-start | bytes 442376 | tf_op jit(solution)/shard_map/ppermute | solution.py:26
  11.2 13.8 %collective-permute-start = (bf16[3,96,384]{2,1,0:T(8,128)(2,1)S(1)}, bf16[3,96,384]{2,1,0:T(8,128)(2,1)S(1)}, u32[]{:S(2)}, u32[]{:S(2)}) collective-permute-start(bf16[3,96,384]{2,1,0:T(8,128)(2,1)S(1)} %slice.54.refs_0_), channel_id=1, source_target_pairs={{0,2},{1,3},{2,0},{3,1},{4,6},{5,7},{6,4},{7,5},{8,10},{9,11},{10,... | collective-permute-start | bytes 663560 | tf_op jit(solution)/shard_map/ppermute | solution.py:26
  15.5 6.4 %copy-start.3 = (bf16[1,2048,384]{2,1,0:T(8,128)(2,1)S(1)}, bf16[1,2048,384]{2,1,0:T(8,128)(2,1)}, u32[]{:S(2)}) copy-start(bf16[1,2048,384]{2,1,0:T(8,128)(2,1)} %refs_4_.1) | copy-start | bytes 4718596
  15.5 2.0 %copy-start.45 = (bf16[2,96,384]{2,1,0:T(8,128)(2,1)}, bf16[2,96,384]{2,1,0:T(8,128)(2,1)S(1)}, u32[]{:S(2)}) copy-start(bf16[2,96,384]{2,1,0:T(8,128)(2,1)S(1)} %collective-permute-done.3.refs_1_) | copy-start | bytes 442372
  18.8 5.3 %copy-start.46 = (bf16[2,96,384]{2,1,0:T(8,128)(2,1)S(1)}, bf16[2,96,384]{2,1,0:T(8,128)(2,1)}, u32[]{:S(2)}) copy-start(bf16[2,96,384]{2,1,0:T(8,128)(2,1)} %copy-done.45) | copy-start | bytes 442372
  18.8 5.3 %copy-start.48 = (bf16[2,96,384]{2,1,0:T(8,128)(2,1)S(1)}, bf16[2,96,384]{2,1,0:T(8,128)(2,1)}, u32[]{:S(2)}) copy-start(bf16[2,96,384]{2,1,0:T(8,128)(2,1)} %copy-done.47) | copy-start | bytes 442372
  18.8 5.3 %copy-start.50 = (bf16[2,96,384]{2,1,0:T(8,128)(2,1)S(1)}, bf16[2,96,384]{2,1,0:T(8,128)(2,1)}, u32[]{:S(2)}) copy-start(bf16[2,96,384]{2,1,0:T(8,128)(2,1)} %copy-done.49) | copy-start | bytes 442372
  18.8 34.4 %collective-permute-start.10 = (bf16[512,1536]{1,0:T(8,128)(2,1)}, bf16[512,1536]{1,0:T(8,128)(2,1)}, u32[]{:S(2)}, u32[]{:S(2)}) collective-permute-start(bf16[512,1536]{1,0:T(8,128)(2,1)} %after.19.refs_1_.refs_0_), channel_id=1, source_target_pairs={{0,16},{8,24},{16,0},{24,8},{1,17},{9,25},{17,1},{25,9},{2,18},{10... | collective-permute-start | bytes 4718600 | tf_op jit(solution)/shard_map/ppermute | solution.py:26
  20.2 37.5 %collective-permute-start.6 = (bf16[512,1536]{1,0:T(8,128)(2,1)}, bf16[512,1536]{1,0:T(8,128)(2,1)}, u32[]{:S(2)}, u32[]{:S(2)}) collective-permute-start(bf16[512,1536]{1,0:T(8,128)(2,1)} %after.19.refs_1_.refs_0_), channel_id=1, source_target_pairs={{0,8},{8,0},{16,24},{24,16},{1,9},{9,1},{17,25},{25,17},{2,10},{10... | collective-permute-start | bytes 4718600 | tf_op jit(solution)/shard_map/ppermute | solution.py:26
  20.8 3.3 %copy-start.22 = (bf16[3,96,384]{2,1,0:T(8,128)(2,1)}, bf16[3,96,384]{2,1,0:T(8,128)(2,1)S(1)}, u32[]{:S(2)}) copy-start(bf16[3,96,384]{2,1,0:T(8,128)(2,1)S(1)} %collective-permute-done.1.refs_3_.refs_4_) | copy-start | bytes 663556
  20.8 5.9 %collective-permute-start.2 = (bf16[3,96,384]{2,1,0:T(8,128)(2,1)S(1)}, bf16[3,96,384]{2,1,0:T(8,128)(2,1)S(1)}, u32[]{:S(2)}, u32[]{:S(2)}) collective-permute-start(bf16[3,96,384]{2,1,0:T(8,128)(2,1)S(1)} %collective-permute-done.1.refs_3_.refs_4_), channel_id=1, source_target_pairs={{0,2},{1,3},{2,0},{3,1},{4,6},{5,7},{6,4},{7,5},{8,10},{9,11},{10,... | collective-permute-start | bytes 663560 | tf_op jit(solution)/shard_map/ppermute | solution.py:26
  27.4 27.9 %collective-permute-start.8 = (bf16[4,2,96,384]{3,2,1,0:T(8,128)(2,1)}, bf16[4,2,96,384]{3,2,1,0:T(8,128)(2,1)S(1)}, u32[]{:S(2)}, u32[]{:S(2)}) collective-permute-start(bf16[4,2,96,384]{3,2,1,0:T(8,128)(2,1)} %after.20.refs_0_), channel_id=1, source_target_pairs={{0,6},{1,7},{2,4},{3,5},{4,2},{5,3},{6,0},{7,1},{8,14},{9,15},{10,... | collective-permute-start | bytes 1769480 | tf_op jit(solution)/shard_map/ppermute | solution.py:26
  27.7 27.6 %collective-permute-start.7 = (bf16[4,2,96,384]{3,2,1,0:T(8,128)(2,1)}, bf16[4,2,96,384]{3,2,1,0:T(8,128)(2,1)S(1)}, u32[]{:S(2)}, u32[]{:S(2)}) collective-permute-start(bf16[4,2,96,384]{3,2,1,0:T(8,128)(2,1)} %after.20.refs_0_), channel_id=1, source_target_pairs={{0,2},{1,3},{2,0},{3,1},{4,6},{5,7},{6,4},{7,5},{8,10},{9,11},{10,... | collective-permute-start | bytes 1769480 | tf_op jit(solution)/shard_map/ppermute | solution.py:26
  29.0 5.4 %copy-start.12 = (bf16[1,1024,768]{2,1,0:T(8,128)(2,1)S(1)}, bf16[1,1024,768]{2,1,0:T(8,128)(2,1)}, u32[]{:S(2)}) copy-start(bf16[1,1024,768]{2,1,0:T(8,128)(2,1)} %x_ref.3) | copy-start | bytes 4718596
  34.4 4.1 %copy-start.23 = (bf16[3,96,384]{2,1,0:T(8,128)(2,1)S(1)}, bf16[3,96,384]{2,1,0:T(8,128)(2,1)}, u32[]{:S(2)}) copy-start(bf16[3,96,384]{2,1,0:T(8,128)(2,1)} %copy-done.22) | copy-start | bytes 663556
  34.4 4.1 %copy-start.25 = (bf16[3,96,384]{2,1,0:T(8,128)(2,1)S(1)}, bf16[3,96,384]{2,1,0:T(8,128)(2,1)}, u32[]{:S(2)}) copy-start(bf16[3,96,384]{2,1,0:T(8,128)(2,1)} %copy-done.24) | copy-start | bytes 663556
  39.4 44.9 %copy-start.28 = (s32[2]{0:T(128)}, s32[2]{0:T(128)S(1)}, u32[]{:S(2)}) copy-start(s32[2]{0:T(128)S(1)} %pad_add_fusion.place) | copy-start | bytes 28
  42.8 12.6 %copy-start.21 = (bf16[6,96,384]{2,1,0:T(8,128)(2,1)}, bf16[6,96,384]{2,1,0:T(8,128)(2,1)S(1)}, u32[]{:S(2)}) copy-start(bf16[6,96,384]{2,1,0:T(8,128)(2,1)S(1)} %get-tuple-element.8.refs_0_) | copy-start | bytes 1327108
  56.5 24.4 %collective-permute-start.12 = (bf16[256,1536]{1,0:T(8,128)(2,1)}, bf16[256,1536]{1,0:T(8,128)(2,1)S(1)}, u32[]{:S(2)}, u32[]{:S(2)}) collective-permute-start(bf16[256,1536]{1,0:T(8,128)(2,1)} %after.24), channel_id=1, source_target_pairs={{0,8},{8,0},{16,24},{24,16},{1,9},{9,1},{17,25},{25,17},{2,10},{10... | collective-permute-start | bytes 2359304 | tf_op jit(solution)/shard_map/ppermute | solution.py:26
  59.9 2.4 %copy-start.5 = (bf16[512,1536]{1,0:T(8,128)(2,1)S(1)}, bf16[512,1536]{1,0:T(8,128)(2,1)}, u32[]{:S(2)}) copy-start(bf16[512,1536]{1,0:T(8,128)(2,1)} %after.19.refs_1_.refs_0_) | copy-start | bytes 4718596
  59.9 21.9 %collective-permute-start.9 = (bf16[256,1536]{1,0:T(8,128)(2,1)}, bf16[256,1536]{1,0:T(8,128)(2,1)S(1)}, u32[]{:S(2)}, u32[]{:S(2)}) collective-permute-start(bf16[256,1536]{1,0:T(8,128)(2,1)} %after.21), channel_id=1, source_target_pairs={{0,16},{8,24},{16,0},{24,8},{1,17},{9,25},{17,1},{25,9},{2,18},{10... | collective-permute-start | bytes 2359304 | tf_op jit(solution)/shard_map/ppermute | solution.py:26
  60.6 15.6 %collective-permute-start.11 = (bf16[4,2,96,384]{3,2,1,0:T(8,128)(2,1)}, bf16[4,2,96,384]{3,2,1,0:T(8,128)(2,1)}, u32[]{:S(2)}, u32[]{:S(2)}) collective-permute-start(bf16[4,2,96,384]{3,2,1,0:T(8,128)(2,1)} %copy-done.16), channel_id=1, source_target_pairs={{0,2},{1,3},{2,0},{3,1},{4,6},{5,7},{6,4},{7,5},{8,10},{9,11},{10,... | collective-permute-start | bytes 1769480 | tf_op jit(solution)/shard_map/ppermute | solution.py:26
  82.7 1.8 copy-start.8
  82.7 32.8 %collective-permute-start.14 = (bf16[21,96,384]{2,1,0:T(8,128)(2,1)}, bf16[21,96,384]{2,1,0:T(8,128)(2,1)}, u32[]{:S(2)}, u32[]{:S(2)}) collective-permute-start(bf16[21,96,384]{2,1,0:T(8,128)(2,1)} %after.27.refs_3_), channel_id=1, source_target_pairs={{0,16},{8,24},{16,0},{24,8},{1,17},{9,25},{17,1},{25,9},{2,18},{10... | collective-permute-start | bytes 4644872 | tf_op jit(solution)/shard_map/ppermute | solution.py:26
  83.2 32.5 %collective-permute-start.13 = (bf16[21,96,384]{2,1,0:T(8,128)(2,1)}, bf16[21,96,384]{2,1,0:T(8,128)(2,1)}, u32[]{:S(2)}, u32[]{:S(2)}) collective-permute-start(bf16[21,96,384]{2,1,0:T(8,128)(2,1)} %after.26), channel_id=1, source_target_pairs={{0,8},{8,0},{16,24},{24,16},{1,9},{9,1},{17,25},{25,17},{2,10},{10... | collective-permute-start | bytes 4644872 | tf_op jit(solution)/shard_map/ppermute | solution.py:26
  84.3 39.7 %collective-permute-start.17 = (bf16[4,4,2,96,384]{4,3,2,1,0:T(8,128)(2,1)S(1)}, bf16[4,4,2,96,384]{4,3,2,1,0:T(8,128)(2,1)S(1)}, u32[]{:S(2)}, u32[]{:S(2)}) collective-permute-start(bf16[4,4,2,96,384]{4,3,2,1,0:T(8,128)(2,1)S(1)} %copy-done.1), channel_id=1, source_target_pairs={{0,1},{1,0},{2,3},{3,2},{4,5},{5,4},{6,7},{7,6},{8,9},{9,8},{10,11... | collective-permute-start | bytes 7077896 | tf_op jit(solution)/shard_map/ppermute | solution.py:26
  85.6 8.8 %copy-start.14 = (bf16[21,96,384]{2,1,0:T(8,128)(2,1)S(1)}, bf16[21,96,384]{2,1,0:T(8,128)(2,1)}, u32[]{:S(2)}) copy-start(bf16[21,96,384]{2,1,0:T(8,128)(2,1)} %after.27.refs_3_) | copy-start | bytes 4644868
  94.0 30.0 %copy-start.20 = (f32[4,5,96,384]{3,2,1,0:T(8,128)}, f32[4,5,96,384]{3,2,1,0:T(8,128)S(1)}, u32[]{:S(2)}) copy-start(f32[4,5,96,384]{3,2,1,0:T(8,128)S(1)} %get-tuple-element.11) | copy-start | bytes 8847364
  94.0 21.9 %collective-permute-start.15 = (bf16[2,5,96,384]{3,2,1,0:T(8,128)(2,1)S(1)}, bf16[2,5,96,384]{3,2,1,0:T(8,128)(2,1)S(1)}, u32[]{:S(2)}, u32[]{:S(2)}) collective-permute-start(bf16[2,5,96,384]{3,2,1,0:T(8,128)(2,1)S(1)} %get-tuple-element.12), channel_id=1, source_target_pairs={{0,1},{1,0},{2,3},{3,2},{4,5},{5,4},{6,7},{7,6},{8,9},{9,8},{10,11... | collective-permute-start | bytes 2211848 | tf_op jit(solution)/shard_map/ppermute | solution.py:26
  94.4 29.6 %collective-permute-start.16 = (bf16[21,96,384]{2,1,0:T(8,128)(2,1)S(1)}, bf16[21,96,384]{2,1,0:T(8,128)(2,1)S(1)}, u32[]{:S(2)}, u32[]{:S(2)}) collective-permute-start(bf16[21,96,384]{2,1,0:T(8,128)(2,1)S(1)} %copy-done.14), channel_id=1, source_target_pairs={{0,1},{1,0},{2,3},{3,2},{4,5},{5,4},{6,7},{7,6},{8,9},{9,8},{10,11... | collective-permute-start | bytes 4644872 | tf_op jit(solution)/shard_map/ppermute | solution.py:26
  115.4 16.1 %collective-permute-start.21 = (bf16[21,96,384]{2,1,0:T(8,128)(2,1)}, bf16[21,96,384]{2,1,0:T(8,128)(2,1)}, u32[]{:S(2)}, u32[]{:S(2)}) collective-permute-start(bf16[21,96,384]{2,1,0:T(8,128)(2,1)} %collective-permute-done.14.refs_2_.refs_7_), channel_id=1, source_target_pairs={{0,1},{1,0},{2,3},{3,2},{4,5},{5,4},{6,7},{7,6},{8,9},{9,8},{10,11... | collective-permute-start | bytes 4644872 | tf_op jit(solution)/shard_map/ppermute | solution.py:26
  115.6 17.0 %collective-permute-start.20 = (bf16[21,96,384]{2,1,0:T(8,128)(2,1)}, bf16[21,96,384]{2,1,0:T(8,128)(2,1)}, u32[]{:S(2)}, u32[]{:S(2)}) collective-permute-start(bf16[21,96,384]{2,1,0:T(8,128)(2,1)} %collective-permute-done.13.refs_1_.refs_5_), channel_id=1, source_target_pairs={{0,1},{1,0},{2,3},{3,2},{4,5},{5,4},{6,7},{7,6},{8,9},{9,8},{10,11... | collective-permute-start | bytes 4644872 | tf_op jit(solution)/shard_map/ppermute | solution.py:26
  115.9 8.1 %copy-start.41 = (bf16[2,5,96,384]{3,2,1,0:T(8,128)(2,1)}, bf16[2,5,96,384]{3,2,1,0:T(8,128)(2,1)S(1)}, u32[]{:S(2)}) copy-start(bf16[2,5,96,384]{3,2,1,0:T(8,128)(2,1)S(1)} %collective-permute-done.15) | copy-start | bytes 2211844
  115.9 5.0 %collective-permute-start.18 = (bf16[2,5,96,384]{3,2,1,0:T(8,128)(2,1)S(1)}, bf16[2,5,96,384]{3,2,1,0:T(8,128)(2,1)S(1)}, u32[]{:S(2)}, u32[]{:S(2)}) collective-permute-start(bf16[2,5,96,384]{3,2,1,0:T(8,128)(2,1)S(1)} %get-tuple-element.13), channel_id=1, source_target_pairs={{0,1},{1,0},{2,3},{3,2},{4,5},{5,4},{6,7},{7,6},{8,9},{9,8},{10,11... | collective-permute-start | bytes 2211848 | tf_op jit(solution)/shard_map/ppermute | solution.py:26
  126.6 3.1 %copy-start.35 = (bf16[5,96,384]{2,1,0:T(8,128)(2,1)S(1)}, bf16[5,96,384]{2,1,0:T(8,128)(2,1)}, u32[]{:S(2)}) copy-start(bf16[5,96,384]{2,1,0:T(8,128)(2,1)} %after.30.refs_3_) | copy-start | bytes 1105924
  126.6 4.9 %copy-start.34 = (bf16[5,96,384]{2,1,0:T(8,128)(2,1)S(1)}, bf16[5,96,384]{2,1,0:T(8,128)(2,1)}, u32[]{:S(2)}) copy-start(bf16[5,96,384]{2,1,0:T(8,128)(2,1)} %after.29.refs_2_) | copy-start | bytes 1105924
  126.6 6.1 %copy-start.33 = (bf16[5,96,384]{2,1,0:T(8,128)(2,1)S(1)}, bf16[5,96,384]{2,1,0:T(8,128)(2,1)}, u32[]{:S(2)}) copy-start(bf16[5,96,384]{2,1,0:T(8,128)(2,1)} %after.28.refs_1_) | copy-start | bytes 1105924
  126.6 37.8 %collective-permute-start.25 = (bf16[9,96,384]{2,1,0:T(8,128)(2,1)}, bf16[9,96,384]{2,1,0:T(8,128)(2,1)S(1)}, u32[]{:S(2)}, u32[]{:S(2)}) collective-permute-start(bf16[9,96,384]{2,1,0:T(8,128)(2,1)} %after.33), channel_id=1, source_target_pairs={{0,8},{8,0},{16,24},{24,16},{1,9},{9,1},{17,25},{25,17},{2,10},{10... | collective-permute-start | bytes 1990664 | tf_op jit(solution)/shard_map/ppermute | solution.py:26
  129.2 36.9 %collective-permute-start.19 = (bf16[9,96,384]{2,1,0:T(8,128)(2,1)}, bf16[9,96,384]{2,1,0:T(8,128)(2,1)S(1)}, u32[]{:S(2)}, u32[]{:S(2)}) collective-permute-start(bf16[9,96,384]{2,1,0:T(8,128)(2,1)} %after.31), channel_id=1, source_target_pairs={{0,16},{8,24},{16,0},{24,8},{1,17},{9,25},{17,1},{25,9},{2,18},{10... | collective-permute-start | bytes 1990664 | tf_op jit(solution)/shard_map/ppermute | solution.py:26
  129.8 18.6 %collective-permute-start.24 = (bf16[5,96,384]{2,1,0:T(8,128)(2,1)S(1)}, bf16[5,96,384]{2,1,0:T(8,128)(2,1)S(1)}, u32[]{:S(2)}, u32[]{:S(2)}) collective-permute-start(bf16[5,96,384]{2,1,0:T(8,128)(2,1)S(1)} %copy-done.35), channel_id=1, source_target_pairs={{0,6},{1,7},{2,4},{3,5},{4,2},{5,3},{6,0},{7,1},{8,14},{9,15},{10,... | collective-permute-start | bytes 1105928 | tf_op jit(solution)/shard_map/ppermute | solution.py:26
  131.5 32.9 %collective-permute-start.23 = (bf16[5,96,384]{2,1,0:T(8,128)(2,1)S(1)}, bf16[5,96,384]{2,1,0:T(8,128)(2,1)S(1)}, u32[]{:S(2)}, u32[]{:S(2)}) collective-permute-start(bf16[5,96,384]{2,1,0:T(8,128)(2,1)S(1)} %copy-done.34), channel_id=1, source_target_pairs={{0,4},{1,5},{2,6},{3,7},{4,0},{5,1},{6,2},{7,3},{8,12},{9,13},{10,... | collective-permute-start | bytes 1105928 | tf_op jit(solution)/shard_map/ppermute | solution.py:26
  132.7 31.7 %collective-permute-start.22 = (bf16[5,96,384]{2,1,0:T(8,128)(2,1)S(1)}, bf16[5,96,384]{2,1,0:T(8,128)(2,1)S(1)}, u32[]{:S(2)}, u32[]{:S(2)}) collective-permute-start(bf16[5,96,384]{2,1,0:T(8,128)(2,1)S(1)} %copy-done.33), channel_id=1, source_target_pairs={{0,2},{1,3},{2,0},{3,1},{4,6},{5,7},{6,4},{7,5},{8,10},{9,11},{10,... | collective-permute-start | bytes 1105928 | tf_op jit(solution)/shard_map/ppermute | solution.py:26
  148.4 16.0 %copy-start.36 = (bf16[5,96,384]{2,1,0:T(8,128)(2,1)}, bf16[5,96,384]{2,1,0:T(8,128)(2,1)S(1)}, u32[]{:S(2)}) copy-start(bf16[5,96,384]{2,1,0:T(8,128)(2,1)S(1)} %collective-permute-done.24.refs_4_.refs_0_) | copy-start | bytes 1105924
  166.1 2.3 %collective-permute-start.27 = (bf16[9,96,384]{2,1,0:T(8,128)(2,1)}, bf16[9,96,384]{2,1,0:T(8,128)(2,1)S(1)}, u32[]{:S(2)}, u32[]{:S(2)}) collective-permute-start(bf16[9,96,384]{2,1,0:T(8,128)(2,1)} %after.34.refs_4_.refs_9_), channel_id=1, source_target_pairs={{0,1},{1,0},{2,3},{3,2},{4,5},{5,4},{6,7},{7,6},{8,9},{9,8},{10,11... | collective-permute-start | bytes 1990664 | tf_op jit(solution)/shard_map/ppermute | solution.py:26
  167.0 2.5 %collective-permute-start.26 = (bf16[9,96,384]{2,1,0:T(8,128)(2,1)}, bf16[9,96,384]{2,1,0:T(8,128)(2,1)S(1)}, u32[]{:S(2)}, u32[]{:S(2)}) collective-permute-start(bf16[9,96,384]{2,1,0:T(8,128)(2,1)} %after.32.refs_3_.refs_7_), channel_id=1, source_target_pairs={{0,1},{1,0},{2,3},{3,2},{4,5},{5,4},{6,7},{7,6},{8,9},{9,8},{10,11... | collective-permute-start | bytes 1990664 | tf_op jit(solution)/shard_map/ppermute | solution.py:26
  (31 other events, 34.2 us)

commit v18 on v17

--- a/solution.py
+++ b/solution.py
@@ -35,6 +35,20 @@
         name="after",
     )(value, *earlier)
 
+def reduce_line(blocks, axis, count, unit):
+    held, masks = [[0]], []
+    while count > 1:
+        masks.append(count - 1)
+        held.append(held[-1] + [d ^ masks[-1] for d in held[-1]])
+        count //= 2
+    blocks, steps = dict(enumerate(blocks)), []
+    for mask, keep in reversed(list(zip(masks, held))):
+        leaving = jnp.stack([blocks[d ^ mask].astype(jnp.bfloat16) for d in keep])
+        steps.append(from_peer(leaving, axis, mask * unit))
+        blocks = {d: blocks[d] + steps[-1][n].astype(jnp.float32) for n, d in enumerate(keep)}
+    return blocks[0], steps
+
+
 def gather_line(value, axis, count, unit):
     found, mask = {0: value}, count - 1
     while mask:
@@ -86,17 +100,28 @@
 
     def kernel(place, *refs):
         parts, trunk_ref = refs[:planes], refs[planes]
-        beside_ref, below_ref, own_ref, edged, sem = refs[planes + 1 :]
+        beside_first, beside_second, below_first, below_second, own_ref, edged, sem = refs[planes + 1 :]
         copy = pltpu.make_async_copy(trunk_ref.at[0], edged.at[pl.ds(HALO, length)], sem)
         copy.start()
         edged[:HALO] = jnp.zeros((HALO, block), jnp.bfloat16)
         edged[HALO + length :] = jnp.zeros((HALO, block), jnp.bfloat16)
         for j in range(planes):
             plane = place[1] // 2 ^ j
+            which = plane // half
             for k in range(taps):
-                spot = (plane // half * taps + k) * half + plane % half
-                beside_ref[window // 2 + spot] = parts[j][k]
-                below_ref[spot] = parts[j][k]
+                spot = k * half + plane % half
+                own_ref[which * taps * half + spot] = parts[j][k]
+
+                @pl.when(which == 0)
+                def _():
+                    beside_first[window // 2 + spot] = parts[j][k]
+                    below_second[spot] = parts[j][k]
+
+                @pl.when(which == 1)
+                def _():
+                    beside_second[spot] = parts[j][k]
+                    below_first[spot] = parts[j][k]
+
         copy.wait()
 
         def cut(out_ref, spot, distance, first, last):
@@ -104,17 +129,18 @@
             for b in range(first, last):
                 out_ref[spot + b - first] = edged[pl.ds(pl.multiple_of(base + b * rows, 16), rows), :]
 
-        cut(beside_ref, 0, 3, 0, window // 2)
-        cut(beside_ref, window // 2 + planes * taps, 1, 0, window)
-        cut(below_ref, planes * taps, 3, window // 2, window)
-        cut(below_ref, planes * taps + window // 2, 2, 0, window)
-        cut(own_ref, 0, 0, 0, window)
-
-    count = window // 2 + planes * taps + window
+        cut(beside_first, 0, 3, 0, window // 2)
+        cut(beside_second, half * taps, 1, 0, window)
+        cut(below_first, half * taps, 3, window // 2, window)
+        cut(below_second, half * taps, 2, 0, window)
+        cut(own_ref, planes * taps, 0, 0, window)
+
+    first, second = half * taps + window // 2, half * taps + window
+    counts = (first, second, first, second, planes * taps + window)
     return pl.pallas_call(
         kernel,
         out_shape=[
-            jax.ShapeDtypeStruct((n, rows, block), jnp.bfloat16) for n in (count, count, window)
+            jax.ShapeDtypeStruct((n, rows, block), jnp.bfloat16) for n in counts
         ],
         grid_spec=pltpu.PrefetchScalarGridSpec(
             num_scalar_prefetch=1,
@@ -122,7 +148,7 @@
             in_specs=[pl.BlockSpec(line[0].shape, lambda i, place: (0, 0, 0))] * planes + [ANYWHERE],
             out_specs=[
                 pl.BlockSpec((n, rows, block), lambda i, place: (0, 0, 0))
-                for n in (count, count, window)
+                for n in counts
             ],
             scratch_shapes=[
                 pltpu.VMEM((length + 2 * HALO, block), jnp.bfloat16),
@@ -223,8 +249,8 @@
     shape = (planes, taps, rows, block)
 
     def kernel(place, shifts_ref, early_ref, *refs):
-        pieces, (mine_ref, *theirs_refs) = refs[: len(layout)], refs[len(layout) : len(layout) + 3]
-        held, shifts, total, sems, shift_sems, early_sems = refs[len(layout) + 3 :]
+        pieces, (mine_ref, theirs_ref) = refs[: len(layout)], refs[len(layout) : len(layout) + 2]
+        held, shifts, total, sems, shift_sems, early_sems = refs[len(layout) + 2 :]
         core, plane = place[1] % 2, place[1] // 2
         copies = start_act(
             place, coarse, layout, pieces, shifts_ref, held, shifts, sems, shift_sems
@@ -248,40 +274,33 @@
             fetch(i).wait()
             total[span, :] += term
 
-        def finish(out_ref, at, j, parity, kind):
-            start = ((plane ^ j) * 2 + parity) * rows
-            even = pl.ds(pl.multiple_of(start, 16), rows)
-            odd = pl.ds(pl.multiple_of(width + start, 16), rows)
-            for k, (left, right) in enumerate(GRAD_PARTS):
-                term = total[even, left * block : (left + 1) * block]
-                term += total[odd, right * block : (right + 1) * block]
-                out_ref[at, k] = (scale * term).astype(kind)
-
-        for which, out_ref in enumerate(theirs_refs):
-
-            @pl.loop(0, planes // 2)
-            def _(at):
-                finish(out_ref, at, at + which * (planes // 2), 1 - core, jnp.bfloat16)
-
-        @pl.loop(0, planes)
-        def _(j):
-            finish(mine_ref, j, j, core, jnp.float32)
-
-    half_shape = (planes // 2, *shape[1:])
+        for out_ref, parity, kind in (
+            (theirs_ref, 1 - core, jnp.bfloat16),
+            (mine_ref, core, jnp.float32),
+        ):
+
+            @pl.loop(0, planes)
+            def _(j):
+                start = ((plane ^ j) * 2 + parity) * rows
+                even = pl.ds(pl.multiple_of(start, 16), rows)
+                odd = pl.ds(pl.multiple_of(width + start, 16), rows)
+                for k, (left, right) in enumerate(GRAD_PARTS):
+                    term = total[even, left * block : (left + 1) * block]
+                    term += total[odd, right * block : (right + 1) * block]
+                    out_ref[j, k] = (scale * term).astype(kind)
+
     whole = pl.BlockSpec(shape, lambda i, place: (0, 0, 0, 0))
-    half = pl.BlockSpec(half_shape, lambda i, place: (0, 0, 0, 0))
     return pl.pallas_call(
         kernel,
         out_shape=(
             jax.ShapeDtypeStruct(shape, jnp.float32),
-            jax.ShapeDtypeStruct(half_shape, jnp.bfloat16),
-            jax.ShapeDtypeStruct(half_shape, jnp.bfloat16),
+            jax.ShapeDtypeStruct(shape, jnp.bfloat16),
         ),
         grid_spec=pltpu.PrefetchScalarGridSpec(
             num_scalar_prefetch=1,
             grid=(1,),
             in_specs=[ANYWHERE] * (2 + len(pieces)),
-            out_specs=[whole, half, half],
+            out_specs=[whole, whole],
             scratch_shapes=[
                 pltpu.VMEM((count, both), jnp.bfloat16),
                 pltpu.VMEM((count, columns), jnp.bfloat16),
@@ -489,8 +508,8 @@
     later = jnp.concatenate([trunk[1:], zeros])
     earlier = jnp.concatenate([zeros, trunk[:-1]])
     shifts = jnp.concatenate([later, trunk, earlier], axis=1)
-    to_beside, to_below, own_window = kernel_messages(place, line, trunk_grad, coarse)
-    ready = (slope, shifts, to_beside, *crossing)
+    *outgoing, own = kernel_messages(place, line, trunk_grad, coarse)
+    ready = (slope, shifts, own, *crossing)
     top, bottom = after(beside[:half], *ready), after(below[half:], *ready)
     far_top, far_bottom = from_peer(top, "seq", 2), from_peer(bottom, "seq", 1)
 
@@ -502,40 +521,29 @@
     lines = stack_planes(place, line_across)
     far_top, far_bottom = after(far_top, early, lines), after(far_bottom, early, lines)
 
-    to_beside, to_below = (
-        after(message, far_top, far_bottom) for message in (to_beside, to_below)
-    )
-    kept_beside, kept_below = from_peer(to_beside, "seq", 1), from_peer(to_below, "seq", 2)
-    other_column, other_lines = from_peer(to_below, "rep", 1), from_peer(lines, "rep", 1)
-
-    mine, *theirs = late_terms(
+    outgoing = [after(message, far_top, far_bottom) for message in outgoing]
+    kept = [from_peer(message, "seq", d) for message, d in zip(outgoing, (1, 1, 2, 2))]
+    other_own, other_lines = from_peer(own, "rep", 1), from_peer(lines, "rep", 1)
+
+    mine, theirs = late_terms(
         place, far_rows, [far_top, far_bottom], shifts, early, coarse, scale, planes, taps, rows
     )
-    arrived = [from_peer(part, "rep", 1) for part in theirs]
-    pairs = []
-    for j in range(planes):
-        part = arrived[j // (planes // 2)][j % (planes // 2)]
-        pairs.append(mine[j] + part.astype(jnp.float32))
-    weight_grad = pairs[0]
-    leaving = [after(part.astype(jnp.bfloat16), other_column, other_lines) for part in pairs[1:]]
-    summed = [from_peer(leaving[j - 1], "rep", 2 * j) for j in range(1, planes)]
+    arrived = from_peer(theirs, "rep", 1)
+    pairs = [mine[j] + arrived[j].astype(jnp.float32) for j in range(planes)]
+    weight_grad, steps = reduce_line(pairs, "rep", planes, 2)
 
     window = (coarse + 2 * HALO) // rows
-    count, side = planes * SPLIT, window // 2
-    far_first = after(kept_beside[: side + count // 2], *leaving)
-    far_second = after(kept_below[count // 2 : count + side], *leaving)
-    far_first, far_second = from_peer(far_first, "seq", 2), from_peer(far_second, "seq", 1)
-
-    windows = [
-        [(own_window, 0, 0, window)],
-        [(kept_beside, side + count, 0, window)],
-        [(kept_below, count + side, 0, window)],
-    ]
+    count, side = planes * SPLIT // 2, window // 2
+    far_first, far_second = from_peer(kept[0], "seq", 2), from_peer(kept[2], "seq", 1)
+
+    windows = [[(own, 2 * count, 0, window)], [(kept[1], count, 0, window)], [(kept[3], count, 0, window)]]
     stage = functools.partial(gradient_stage, place, taps=taps, slope=slope, shape=inputs.shape)
-    soon = [(to_below, 0, 0, planes, 0, 0), (other_column, 0, 0, planes, 1, 0)]
-    for part, start, distance in ((kept_beside, side, 1), (kept_below, 0, 2)):
-        soon.append((part, start, 0, planes, 0, distance))
-        soon.append((from_peer(part, "rep", 1), start, 0, planes, 1, distance))
+    soon = [(after(own, *steps[:1]), 0, 0, planes, 0, 0), (other_own, 0, 0, planes, 1, 0)]
+    for part, start, plane, distance in zip(
+        kept, (side, 0, 0, 0), (0, planes // 2, planes // 2, 0), (1, 1, 2, 2)
+    ):
+        soon.append((part, start, plane, planes // 2, 0, distance))
+        soon.append((from_peer(part, "rep", 1), start, plane, planes // 2, 1, distance))
     crossed = [
         (part, None, 0, planes, flip, d)
         for flip, part in enumerate((lines, other_lines))
@@ -543,16 +551,15 @@
     ]
     near = [piece for piece in crossed if piece[-1] < 3]
     begun = stage(windows, pieces=soon + near, distances=[0, 1, 2], begun=None)
-    far_first, far_second = after(far_first, begun, *summed), after(far_second, begun, *summed)
-    windows.append([(far_first, 0, 0, side), (far_second, count // 2, side, side)])
+    far_first, far_second = after(far_first, begun, *steps), after(far_second, begun, *steps)
+    windows.append([(far_first, 0, 0, side), (far_second, count, side, side)])
     rest = [piece for piece in crossed if piece[-1] == 3]
     for part, start, plane in ((far_first, side, 0), (far_second, 0, planes // 2)):
         rest.append((part, start, plane, planes // 2, 0, 3))
         rest.append((from_peer(part, "rep", 1), start, plane, planes // 2, 1, 3))
     input_grad = stage(windows, pieces=rest, distances=[3], begun=begun)
-    for part in summed:
-        weight_grad = weight_grad + after(part, input_grad).astype(jnp.float32)
     return (input_grad, weight_grad)
+
 
 def with_halo(value, sides, width):
     for axis, dim in sides:

time: 186 us -> 175 us (0.941)
  the two profiles are of different devices: /device:TPU:0 before, /device:TPU:9 now
where the time goes in v18:
time: 175 us; the launch traced here: 172 us
  Pallas kernels  58.8 us (34%)
  waiting for transfers between devices  43 us (25%)
  local copies, waits for them, and re-layouts  30.4 us (17%)
  starting transfers between devices  27 us (15%)
  other arithmetic  11.7 us (7%)
    ppermute x30, waiting for transfers between devices, from_peer(): return lax.ppermute(value, axis, [(i, i ^ distance) for i in range(peers)])  43 us
    pallas_call x2, Pallas kernels, gradient_stage(): pl.pallas_call(body, out_shape=out_shape, grid_spec=pltpu.PrefetchScalarG...  27.2 us
    ppermute x30, starting transfers between devices, from_peer(): return lax.ppermute(value, axis, [(i, i ^ distance) for i in range(peers)])  27 us
    unnamed x87, local copies, waits for them, and re-layouts  22.2 us
    pallas_call x1, Pallas kernels, early_terms(): pl.pallas_call(kernel, out_shape=jax.ShapeDtypeStruct((both, columns), jn...  13.8 us
    pallas_call x1, Pallas kernels, late_terms(): pl.pallas_call(kernel, out_shape=(jax.ShapeDtypeStruct(shape, jnp.float32...  9.39 us
    concatenate x1, other arithmetic, on_device_square(): shifts = jnp.concatenate([later, trunk, earlier], axis=1)  5.4 us
    slice x2, local copies, waits for them, and re-layouts, on_device_square(): top, bottom = (after(beside[:half], *ready), after(below[half:], *ready))  4.19 us
  transfers between devices with their start and end apart: 30, of which 6 were waited for; matrix products, arithmetic and copies ran while one was open for 12% of the time, Pallas kernels for 27%

profile of v18, /device:TPU:9, one launch (start us, length us, event | category | flops | bytes accessed | tf_op | source)
XLA Modules:
  0.0 172.2 jit_solution(17231113266622364185)
XLA Ops:
  0.6 1.0 slice.54.refs_0_
  1.6 1.4 collective-permute-start.1
  3.0 0.9 slice_bitcast_fusion.2
  3.9 1.3 collective-permute-start.3
  5.2 1.2 collective-permute-start.4
  6.6 2.2 %collective-permute-start = (bf16[3,96,384]{2,1,0:T(8,128)(2,1)S(1)}, bf16[3,96,384]{2,1,0:T(8,128)(2,1)S(1)}, u32[]{:S(2)}, u32[]{:S(2)}) collective-permute-start(bf16[3,96,384]{2,1,0:T(8,128)(2,1)S(1)} %slice.54.refs_0_), channel_id=1, source_target_pairs={{0,2},{1,3},{2,0},{3,1},{4,6},{5,7},{6,4},{7,5},{8,10},{9,11},{10,... | collective-permute-start | bytes 663560 | tf_op jit(solution)/shard_map/ppermute | solution.py:26
  8.8 1.4 copy-done.10
  10.2 1.8 %act.1.refs_0_ = bf16[512,1536]{1,0:T(8,128)(2,1)S(1)} custom-call(bf16[1,1024,768]{2,1,0:T(8,128)(2,1)S(1)} %copy-done.10), custom_call_target="tpu_custom_call" | custom-call | flops 1048576 | bytes 65536 | tf_op jit(solution)/shard_map/act/pallas_call | solution.py:84
  12.0 1.1 copy-done.8
  14.5 1.2 collective-permute-start.10
  15.7 1.2 collective-permute-start.6
  17.0 2.1 %slice_bitcast_fusion.1 = (bf16[2047,384]{1,0:T(8,128)(2,1)}, bf16[2047,384]{1,0:T(8,128)(2,1)}) fusion(bf16[1,2048,384]{2,1,0:T(8,128)(2,1)S(1)} %copy-done.7), kind=kLoop, calls=%fused_computation.7 | loop fusion | bytes 6288384 | tf_op jit(solution)/shard_map/slice | solution.py:508
  19.1 0.9 pad_maximum_fusion.1.refs_0_
  20.0 2.1 %collective-permute-done.2.refs_2_.refs_3_ = bf16[3,96,384]{2,1,0:T(8,128)(2,1)S(1)} collective-permute-done((bf16[3,96,384]{2,1,0:T(8,128)(2,1)S(1)}, bf16[3,96,384]{2,1,0:T(8,128)(2,1)S(1)}, u32[]{:S(2)}, u32[]{:S(2)}) %collective-permute-start.2) | collective-permute-done | bytes 221216 | tf_op jit(solution)/shard_map/ppermute | solution.py:26
  23.2 5.4 %fusion.2.refs_2_.shifts_ref = bf16[2048,1152]{1,0:T(8,128)(2,1)} fusion(bf16[2047,384]{1,0:T(8,128)(2,1)} %get-tuple-element.19, bf16[2047,384]{1,0:T(8,128)(2,1)} %get-tuple-element.18, bf16[2048,384]{1,0:T(8,128)(2,1)S(1)} %bitcast.14), kind=kLoop, calls=%fused_computation.4 | loop fusion | flops 23592960 | bytes 9435648 | tf_op jit(solution)/shard_map/concatenate | solution.py:510
  28.6 2.3 %half_slope.1.refs_1_.refs_11_ = f32[2,512,768]{2,1,0:T(8,128)S(1)} custom-call(bf16[1,1024,768]{2,1,0:T(8,128)(2,1)S(1)} %copy-done.11), custom_call_target="tpu_custom_call" | custom-call | tf_op jit(solution)/shard_map/half_slope/pallas_call | solution.py:178
  30.9 1.6 copy-done.2
  32.6 0.9 copy-done.25
  33.6 2.5 %kernel_messages.1 = (bf16[9,96,384]{2,1,0:T(8,128)(2,1)S(1)}, bf16[12,96,384]{2,1,0:T(8,128)(2,1)S(1)}, bf16[9,96,384]{2,1,0:T(8,128)(2,1)S(1)}, bf16[12,96,384]{2,1,0:T(8,128)(2,1)S(1)}, bf16[18,96,384]{2,1,0:T(8,128)(2,1)}) custom-call(s32[2]{0:T(128)S(1)} %pad_add_fusion.place, bf16[3,96,384]{2,1,0:T(8,128)(2,1)S(1)} %slice.54.refs_0_, ...), custom_call_target="tpu_custom_call" | custom-call | flops 1048576 | bytes 65536 | tf_op jit(solution)/shard_map/kernel_messages/pallas_call | solution.py:140
  36.1 0.9 copy-done.19
  37.0 0.9 copy-done.27
  37.9 10.7 %collective-permute-done.10.refs_2_ = bf16[512,1536]{1,0:T(8,128)(2,1)} collective-permute-done((bf16[512,1536]{1,0:T(8,128)(2,1)}, bf16[512,1536]{1,0:T(8,128)(2,1)}, u32[]{:S(2)}, u32[]{:S(2)}) %collective-permute-start.10) | collective-permute-done | bytes 1572896 | tf_op jit(solution)/shard_map/ppermute | solution.py:26
  48.6 2.1 %slice.73.refs_0_ = bf16[256,1536]{1,0:T(8,128)(2,1)} slice(bf16[512,1536]{1,0:T(8,128)(2,1)} %collective-permute-done.10.refs_2_), slice={[256:512], [0:1536]} | slice | bytes 1572864 | tf_op jit(solution)/shard_map/slice | solution.py:513
  51.7 1.2 collective-permute-start.12
  52.9 2.1 %slice.72.refs_0_ = bf16[256,1536]{1,0:T(8,128)(2,1)} slice(bf16[512,1536]{1,0:T(8,128)(2,1)} %collective-permute-done.6.refs_1_), slice={[0:256], [0:1536]} | slice | bytes 1572864 | tf_op jit(solution)/shard_map/slice | solution.py:513
  55.1 1.2 collective-permute-start.9
  56.3 3.8 %collective-permute-start.19 = (bf16[18,96,384]{2,1,0:T(8,128)(2,1)}, bf16[18,96,384]{2,1,0:T(8,128)(2,1)}, u32[]{:S(2)}, u32[]{:S(2)}) collective-permute-start(bf16[18,96,384]{2,1,0:T(8,128)(2,1)} %get-tuple-element.9.refs_3_.refs_0_), channel_id=1, source_target_pairs={{0,1},{1,0},{2,3},{3,2},{4,5},{5,4},{6,7},{7,6},{8,9},{9,8},{10,11... | collective-permute-start | bytes 3981320 | tf_op jit(solution)/shard_map/ppermute | solution.py:26
  60.2 13.8 %weight_grad_early.1.refs_1_.early_ref = f32[1536,1152]{1,0:T(8,128)} custom-call(s32[2]{0:T(128)S(1)} %pad_add_fusion.place, bf16[2048,1152]{1,0:T(8,128)(2,1)} %fusion.2.refs_2_.shifts_ref, bf16[512,1536]{1,0:T(8,128)(2,1)S(1)} %copy-done.9, bf16[512,1536]{1,0:T(8,128)(2,1)} %collective-permute-done.6.refs_1_, ...), custom_call_target="tpu_custom_call" | custom-call | flops 1048576 | bytes 65536 | tf_op jit(solution)/shard_map/weight_grad_early/pallas_call | solution.py:224
  74.0 1.0 copy-done.13
  75.4 1.8 %stack_planes.1.refs_2_.refs_13_.refs_14_.refs_15_.refs_5_ = bf16[4,4,2,96,384]{4,3,2,1,0:T(8,128)(2,1)S(1)} custom-call(s32[2]{0:T(128)S(1)} %pad_add_fusion.place, bf16[4,2,96,384]{3,2,1,0:T(8,128)(2,1)S(1)} %copy-done.16, bf16[4,2,96,384]{3,2,1,0:T(8,128)(2,1)S(1)} %copy-done.15, bf16[4,2,96,384]{3,2,1,0:T(8,128)(2,1)} %after.17.refs_2_, ...), custom_call_target="tpu_custom_call" | custom-call | flops 1048576 | bytes 65536 | tf_op jit(solution)/shard_map/stack_planes/pallas_call | solution.py:474
  77.2 1.4 copy-done
  81.0 1.1 copy-done.6
  82.1 9.4 %weight_grad_late.1 = (f32[4,5,96,384]{3,2,1,0:T(8,128)S(1)}, bf16[4,5,96,384]{3,2,1,0:T(8,128)(2,1)}) custom-call(s32[2]{0:T(128)S(1)} %pad_add_fusion.place, bf16[2048,1152]{1,0:T(8,128)(2,1)} %fusion.2.refs_2_.shifts_ref, f32[1536,1152]{1,0:T(8,128)} %weight_grad_early.1.refs_1_.early_ref, bf16[256,1536]{1,0:T(8,128)(2,1)S(1)} %copy-done.6, ...), custom_call_target="tpu_custom_call" | custom-call | flops 1048576 | bytes 65536 | tf_op jit(solution)/shard_map/weight_grad_late/pallas_call | solution.py:293
  91.5 1.6 copy-done.17
  93.6 1.1 collective-permute-start.22
  95.4 15.1 %collective-permute-done.22.refs_9_ = bf16[9,96,384]{2,1,0:T(8,128)(2,1)} collective-permute-done((bf16[9,96,384]{2,1,0:T(8,128)(2,1)}, bf16[9,96,384]{2,1,0:T(8,128)(2,1)}, u32[]{:S(2)}, u32[]{:S(2)}) %collective-permute-start.22) | collective-permute-done | bytes 663584 | tf_op jit(solution)/shard_map/ppermute | solution.py:26
  110.8 1.4 collective-permute-start.23
  112.2 1.7 add_convert_fusion.2
  114.0 1.5 collective-permute-start.18
  115.5 13.9 %collective-permute-done.14.refs_2_.refs_11_ = bf16[12,96,384]{2,1,0:T(8,128)(2,1)} collective-permute-done((bf16[12,96,384]{2,1,0:T(8,128)(2,1)}, bf16[12,96,384]{2,1,0:T(8,128)(2,1)}, u32[]{:S(2)}, u32[]{:S(2)}) %collective-permute-start.14) | collective-permute-done | bytes 884768 | tf_op jit(solution)/shard_map/ppermute | solution.py:26
  130.8 2.1 %collective-permute-start.24 = (bf16[12,96,384]{2,1,0:T(8,128)(2,1)}, bf16[12,96,384]{2,1,0:T(8,128)(2,1)}, u32[]{:S(2)}, u32[]{:S(2)}) collective-permute-start(bf16[12,96,384]{2,1,0:T(8,128)(2,1)} %collective-permute-done.14.refs_2_.refs_11_), channel_id=1, source_target_pairs={{0,1},{1,0},{2,3},{3,2},{4,5},{5,4},{6,7},{7,6},{8,9},{9,8},{10,11... | collective-permute-start | bytes 2654216 | tf_op jit(solution)/shard_map/ppermute | solution.py:26
  133.2 1.2 collective-permute-start.16
  134.5 1.3 add_convert_fusion
  135.9 2.5 %copy.29.refs_0_ = bf16[18,96,384]{2,1,0:T(8,128)(2,1)} copy(bf16[18,96,384]{2,1,0:T(8,128)(2,1)} %get-tuple-element.9.refs_3_.refs_0_) | data formatting | bytes 2654208
  138.4 14.8 %input_grad.2.refs_1_.refs_12_ = f32[2,512,768]{2,1,0:T(8,128)} custom-call(s32[2]{0:T(128)} %copy-done.28, bf16[18,96,384]{2,1,0:T(8,128)(2,1)} %get-tuple-element.9.refs_3_.refs_0_, bf16[12,96,384]{2,1,0:T(8,128)(2,1)} %collective-permute-done.13.refs_1_.refs_7_, bf16[12,96,384]{2,1,0:T(8,128)(2,1)} %collective-permute-done.14.refs_2_.refs_11_, ...), custom_call_target="tpu_custom_call" | custom-call | flops 1048576 | bytes 65536 | tf_op jit(solution)/shard_map/input_grad/pallas_call | solution.py:450
  154.0 1.5 collective-permute-start.29
  155.6 2.2 %add_bitcast_fusion = f32[5,96,384]{2,1,0:T(8,128)} fusion(bf16[1,5,96,384]{3,2,1,0:T(8,128)(2,1)S(1)} %copy-done.32, f32[4,5,96,384]{3,2,1,0:T(8,128)} %copy-done.17, bf16[2,5,96,384]{3,2,1,0:T(8,128)(2,1)S(1)} %copy-done.30, bf16[4,5,96,384]{3,2,1,0:T(8,128)(2,1)} %collective-permute-done.17), kind=kLoop, calls=%fused_computation.9 | loop fusion | flops 1105920 | bytes 2580480 | tf_op jit(solution)/shard_map/add | solution.py:48
  159.6 12.4 %input_grad.3 = bf16[1,1024,768]{2,1,0:T(8,128)(2,1)} custom-call(s32[2]{0:T(128)} %copy-done.28, bf16[18,96,384]{2,1,0:T(8,128)(2,1)} %get-tuple-element.9.refs_3_.refs_0_, bf16[12,96,384]{2,1,0:T(8,128)(2,1)} %collective-permute-done.13.refs_1_.refs_7_, bf16[12,96,384]{2,1,0:T(8,128)(2,1)} %collective-permute-done.14.refs_2_.refs_11_, ...), custom_call_target="tpu_custom_call" | custom-call | flops 1048576 | bytes 65536 | tf_op jit(solution)/shard_map/input_grad/pallas_call | solution.py:450
  (133 shorter events, 12.3 us)
Async XLA Ops:
  1.6 15.4 %collective-permute-start.1 = (bf16[3,96,384]{2,1,0:T(8,128)(2,1)S(1)}, bf16[3,96,384]{2,1,0:T(8,128)(2,1)S(1)}, u32[]{:S(2)}, u32[]{:S(2)}) collective-permute-start(bf16[3,96,384]{2,1,0:T(8,128)(2,1)S(1)} %slice.54.refs_0_), channel_id=1, source_target_pairs={{0,6},{1,7},{2,4},{3,5},{4,2},{5,3},{6,0},{7,1},{8,14},{9,15},{10,... | collective-permute-start | bytes 663560 | tf_op jit(solution)/shard_map/ppermute | solution.py:26
  3.9 9.2 %collective-permute-start.3 = (bf16[2,96,384]{2,1,0:T(8,128)(2,1)S(1)}, bf16[2,96,384]{2,1,0:T(8,128)(2,1)S(1)}, u32[]{:S(2)}, u32[]{:S(2)}) collective-permute-start(bf16[2,96,384]{2,1,0:T(8,128)(2,1)S(1)} %get-tuple-element.21), channel_id=1, source_target_pairs={{0,8},{8,0},{16,24},{24,16},{1,9},{9,1},{17,25},{25,17},{2,10},{10... | collective-permute-start | bytes 442376 | tf_op jit(solution)/shard_map/ppermute | solution.py:26
  5.2 8.0 %collective-permute-start.4 = (bf16[2,96,384]{2,1,0:T(8,128)(2,1)S(1)}, bf16[2,96,384]{2,1,0:T(8,128)(2,1)S(1)}, u32[]{:S(2)}, u32[]{:S(2)}) collective-permute-start(bf16[2,96,384]{2,1,0:T(8,128)(2,1)S(1)} %get-tuple-element.21), channel_id=1, source_target_pairs={{0,16},{8,24},{16,0},{24,8},{1,17},{9,25},{17,1},{25,9},{2,18},{10... | collective-permute-start | bytes 442376 | tf_op jit(solution)/shard_map/ppermute | solution.py:26
  6.4 6.7 %collective-permute-start.5 = (bf16[2,96,384]{2,1,0:T(8,128)(2,1)S(1)}, bf16[2,96,384]{2,1,0:T(8,128)(2,1)S(1)}, u32[]{:S(2)}, u32[]{:S(2)}) collective-permute-start(bf16[2,96,384]{2,1,0:T(8,128)(2,1)S(1)} %get-tuple-element.21), channel_id=1, source_target_pairs={{0,24},{8,16},{16,8},{24,0},{1,25},{9,17},{17,9},{25,1},{2,26},{10... | collective-permute-start | bytes 442376 | tf_op jit(solution)/shard_map/ppermute | solution.py:26
  6.6 13.4 %collective-permute-start = (bf16[3,96,384]{2,1,0:T(8,128)(2,1)S(1)}, bf16[3,96,384]{2,1,0:T(8,128)(2,1)S(1)}, u32[]{:S(2)}, u32[]{:S(2)}) collective-permute-start(bf16[3,96,384]{2,1,0:T(8,128)(2,1)S(1)} %slice.54.refs_0_), channel_id=1, source_target_pairs={{0,2},{1,3},{2,0},{3,1},{4,6},{5,7},{6,4},{7,5},{8,10},{9,11},{10,... | collective-permute-start | bytes 663560 | tf_op jit(solution)/shard_map/ppermute | solution.py:26
  13.1 3.8 %copy-start.7 = (bf16[1,2048,384]{2,1,0:T(8,128)(2,1)S(1)}, bf16[1,2048,384]{2,1,0:T(8,128)(2,1)}, u32[]{:S(2)}) copy-start(bf16[1,2048,384]{2,1,0:T(8,128)(2,1)} %refs_4_.1) | copy-start | bytes 4718596
  14.5 4.6 %copy-start.38 = (bf16[2,96,384]{2,1,0:T(8,128)(2,1)S(1)}, bf16[2,96,384]{2,1,0:T(8,128)(2,1)}, u32[]{:S(2)}) copy-start(bf16[2,96,384]{2,1,0:T(8,128)(2,1)} %copy-done.37) | copy-start | bytes 442372
  14.5 4.6 %copy-start.40 = (bf16[2,96,384]{2,1,0:T(8,128)(2,1)S(1)}, bf16[2,96,384]{2,1,0:T(8,128)(2,1)}, u32[]{:S(2)}) copy-start(bf16[2,96,384]{2,1,0:T(8,128)(2,1)} %copy-done.39) | copy-start | bytes 442372
  14.5 4.6 %copy-start.42 = (bf16[2,96,384]{2,1,0:T(8,128)(2,1)S(1)}, bf16[2,96,384]{2,1,0:T(8,128)(2,1)}, u32[]{:S(2)}) copy-start(bf16[2,96,384]{2,1,0:T(8,128)(2,1)} %copy-done.41) | copy-start | bytes 442372
  14.5 34.1 %collective-permute-start.10 = (bf16[512,1536]{1,0:T(8,128)(2,1)}, bf16[512,1536]{1,0:T(8,128)(2,1)}, u32[]{:S(2)}, u32[]{:S(2)}) collective-permute-start(bf16[512,1536]{1,0:T(8,128)(2,1)} %after.14.refs_1_.refs_0_), channel_id=1, source_target_pairs={{0,16},{8,24},{16,0},{24,8},{1,17},{9,25},{17,1},{25,9},{2,18},{10... | collective-permute-start | bytes 4718600 | tf_op jit(solution)/shard_map/ppermute | solution.py:26
  15.7 37.2 %collective-permute-start.6 = (bf16[512,1536]{1,0:T(8,128)(2,1)}, bf16[512,1536]{1,0:T(8,128)(2,1)}, u32[]{:S(2)}, u32[]{:S(2)}) collective-permute-start(bf16[512,1536]{1,0:T(8,128)(2,1)} %after.14.refs_1_.refs_0_), channel_id=1, source_target_pairs={{0,8},{8,0},{16,24},{24,16},{1,9},{9,1},{17,25},{25,17},{2,10},{10... | collective-permute-start | bytes 4718600 | tf_op jit(solution)/shard_map/ppermute | solution.py:26
  16.9 2.1 %copy-start.20 = (bf16[3,96,384]{2,1,0:T(8,128)(2,1)}, bf16[3,96,384]{2,1,0:T(8,128)(2,1)S(1)}, u32[]{:S(2)}) copy-start(bf16[3,96,384]{2,1,0:T(8,128)(2,1)S(1)} %collective-permute-done.1.refs_3_.refs_4_) | copy-start | bytes 663556
  17.0 5.2 %collective-permute-start.2 = (bf16[3,96,384]{2,1,0:T(8,128)(2,1)S(1)}, bf16[3,96,384]{2,1,0:T(8,128)(2,1)S(1)}, u32[]{:S(2)}, u32[]{:S(2)}) collective-permute-start(bf16[3,96,384]{2,1,0:T(8,128)(2,1)S(1)} %collective-permute-done.1.refs_3_.refs_4_), channel_id=1, source_target_pairs={{0,2},{1,3},{2,0},{3,1},{4,6},{5,7},{6,4},{7,5},{8,10},{9,11},{10,... | collective-permute-start | bytes 663560 | tf_op jit(solution)/shard_map/ppermute | solution.py:26
  20.0 2.1 %copy-start.22 = (bf16[3,96,384]{2,1,0:T(8,128)(2,1)}, bf16[3,96,384]{2,1,0:T(8,128)(2,1)S(1)}, u32[]{:S(2)}) copy-start(bf16[3,96,384]{2,1,0:T(8,128)(2,1)S(1)} %collective-permute-done.refs_1_.refs_2_) | copy-start | bytes 663556
  22.8 27.9 %collective-permute-start.8 = (bf16[4,2,96,384]{3,2,1,0:T(8,128)(2,1)}, bf16[4,2,96,384]{3,2,1,0:T(8,128)(2,1)S(1)}, u32[]{:S(2)}, u32[]{:S(2)}) collective-permute-start(bf16[4,2,96,384]{3,2,1,0:T(8,128)(2,1)} %after.15.refs_0_), channel_id=1, source_target_pairs={{0,6},{1,7},{2,4},{3,5},{4,2},{5,3},{6,0},{7,1},{8,14},{9,15},{10,... | collective-permute-start | bytes 1769480 | tf_op jit(solution)/shard_map/ppermute | solution.py:26
  22.8 27.9 %collective-permute-start.7 = (bf16[4,2,96,384]{3,2,1,0:T(8,128)(2,1)}, bf16[4,2,96,384]{3,2,1,0:T(8,128)(2,1)S(1)}, u32[]{:S(2)}, u32[]{:S(2)}) collective-permute-start(bf16[4,2,96,384]{3,2,1,0:T(8,128)(2,1)} %after.15.refs_0_), channel_id=1, source_target_pairs={{0,2},{1,3},{2,0},{3,1},{4,6},{5,7},{6,4},{7,5},{8,10},{9,11},{10,... | collective-permute-start | bytes 1769480 | tf_op jit(solution)/shard_map/ppermute | solution.py:26
  23.2 5.4 %copy-start.11 = (bf16[1,1024,768]{2,1,0:T(8,128)(2,1)S(1)}, bf16[1,1024,768]{2,1,0:T(8,128)(2,1)}, u32[]{:S(2)}) copy-start(bf16[1,1024,768]{2,1,0:T(8,128)(2,1)} %x_ref.3) | copy-start | bytes 4718596
  28.6 4.1 %copy-start.21 = (bf16[3,96,384]{2,1,0:T(8,128)(2,1)S(1)}, bf16[3,96,384]{2,1,0:T(8,128)(2,1)}, u32[]{:S(2)}) copy-start(bf16[3,96,384]{2,1,0:T(8,128)(2,1)} %copy-done.20) | copy-start | bytes 663556
  28.6 4.1 %copy-start.23 = (bf16[3,96,384]{2,1,0:T(8,128)(2,1)S(1)}, bf16[3,96,384]{2,1,0:T(8,128)(2,1)}, u32[]{:S(2)}) copy-start(bf16[3,96,384]{2,1,0:T(8,128)(2,1)} %copy-done.22) | copy-start | bytes 663556
  30.9 1.6 copy-start.2
  33.6 46.8 %copy-start.28 = (s32[2]{0:T(128)}, s32[2]{0:T(128)S(1)}, u32[]{:S(2)}) copy-start(s32[2]{0:T(128)S(1)} %pad_add_fusion.place) | copy-start | bytes 28
  37.9 12.8 %copy-start.18 = (bf16[12,96,384]{2,1,0:T(8,128)(2,1)}, bf16[12,96,384]{2,1,0:T(8,128)(2,1)S(1)}, u32[]{:S(2)}) copy-start(bf16[12,96,384]{2,1,0:T(8,128)(2,1)S(1)} %get-tuple-element.10.refs_0_) | copy-start | bytes 2654212
  37.9 12.8 %copy-start.26 = (bf16[9,96,384]{2,1,0:T(8,128)(2,1)}, bf16[9,96,384]{2,1,0:T(8,128)(2,1)S(1)}, u32[]{:S(2)}) copy-start(bf16[9,96,384]{2,1,0:T(8,128)(2,1)S(1)} %get-tuple-element.12.refs_0_) | copy-start | bytes 1990660
  51.7 26.9 %collective-permute-start.12 = (bf16[256,1536]{1,0:T(8,128)(2,1)}, bf16[256,1536]{1,0:T(8,128)(2,1)S(1)}, u32[]{:S(2)}, u32[]{:S(2)}) collective-permute-start(bf16[256,1536]{1,0:T(8,128)(2,1)} %after.19), channel_id=1, source_target_pairs={{0,8},{8,0},{16,24},{24,16},{1,9},{9,1},{17,25},{25,17},{2,10},{10... | collective-permute-start | bytes 2359304 | tf_op jit(solution)/shard_map/ppermute | solution.py:26
  55.1 5.1 %copy-start.9 = (bf16[512,1536]{1,0:T(8,128)(2,1)S(1)}, bf16[512,1536]{1,0:T(8,128)(2,1)}, u32[]{:S(2)}) copy-start(bf16[512,1536]{1,0:T(8,128)(2,1)} %after.14.refs_1_.refs_0_) | copy-start | bytes 4718596
  55.1 24.5 %collective-permute-start.9 = (bf16[256,1536]{1,0:T(8,128)(2,1)}, bf16[256,1536]{1,0:T(8,128)(2,1)S(1)}, u32[]{:S(2)}, u32[]{:S(2)}) collective-permute-start(bf16[256,1536]{1,0:T(8,128)(2,1)} %after.16), channel_id=1, source_target_pairs={{0,16},{8,24},{16,0},{24,8},{1,17},{9,25},{17,1},{25,9},{2,18},{10... | collective-permute-start | bytes 2359304 | tf_op jit(solution)/shard_map/ppermute | solution.py:26
  56.3 17.7 %collective-permute-start.11 = (bf16[4,2,96,384]{3,2,1,0:T(8,128)(2,1)}, bf16[4,2,96,384]{3,2,1,0:T(8,128)(2,1)}, u32[]{:S(2)}, u32[]{:S(2)}) collective-permute-start(bf16[4,2,96,384]{3,2,1,0:T(8,128)(2,1)} %copy-done.12), channel_id=1, source_target_pairs={{0,2},{1,3},{2,0},{3,1},{4,6},{5,7},{6,4},{7,5},{8,10},{9,11},{10,... | collective-permute-start | bytes 1769480 | tf_op jit(solution)/shard_map/ppermute | solution.py:26
  56.3 38.8 %collective-permute-start.19 = (bf16[18,96,384]{2,1,0:T(8,128)(2,1)}, bf16[18,96,384]{2,1,0:T(8,128)(2,1)}, u32[]{:S(2)}, u32[]{:S(2)}) collective-permute-start(bf16[18,96,384]{2,1,0:T(8,128)(2,1)} %get-tuple-element.9.refs_3_.refs_0_), channel_id=1, source_target_pairs={{0,1},{1,0},{2,3},{3,2},{4,5},{5,4},{6,7},{7,6},{8,9},{9,8},{10,11... | collective-permute-start | bytes 3981320 | tf_op jit(solution)/shard_map/ppermute | solution.py:26
  82.1 11.0 %copy-start.1 = (bf16[4,4,2,96,384]{4,3,2,1,0:T(8,128)(2,1)S(1)}, bf16[4,4,2,96,384]{4,3,2,1,0:T(8,128)(2,1)}, u32[]{:S(2)}) copy-start(bf16[4,4,2,96,384]{4,3,2,1,0:T(8,128)(2,1)} %copy-done) | copy-start | bytes 7077892
  93.1 17.7 %collective-permute-start.17 = (bf16[4,5,96,384]{3,2,1,0:T(8,128)(2,1)}, bf16[4,5,96,384]{3,2,1,0:T(8,128)(2,1)}, u32[]{:S(2)}, u32[]{:S(2)}) collective-permute-start(bf16[4,5,96,384]{3,2,1,0:T(8,128)(2,1)} %get-tuple-element.14), channel_id=1, source_target_pairs={{0,1},{1,0},{2,3},{3,2},{4,5},{5,4},{6,7},{7,6},{8,9},{9,8},{10,11... | collective-permute-start | bytes 4423688 | tf_op jit(solution)/shard_map/ppermute | solution.py:26
  93.1 42.7 %collective-permute-start.25 = (bf16[4,4,2,96,384]{4,3,2,1,0:T(8,128)(2,1)S(1)}, bf16[4,4,2,96,384]{4,3,2,1,0:T(8,128)(2,1)}, u32[]{:S(2)}, u32[]{:S(2)}) collective-permute-start(bf16[4,4,2,96,384]{4,3,2,1,0:T(8,128)(2,1)S(1)} %copy-done.1), channel_id=1, source_target_pairs={{0,1},{1,0},{2,3},{3,2},{4,5},{5,4},{6,7},{7,6},{8,9},{9,8},{10,11... | collective-permute-start | bytes 7077896 | tf_op jit(solution)/shard_map/ppermute | solution.py:26
  93.6 16.8 %collective-permute-start.22 = (bf16[9,96,384]{2,1,0:T(8,128)(2,1)}, bf16[9,96,384]{2,1,0:T(8,128)(2,1)}, u32[]{:S(2)}, u32[]{:S(2)}) collective-permute-start(bf16[9,96,384]{2,1,0:T(8,128)(2,1)} %after.25), channel_id=1, source_target_pairs={{0,16},{8,24},{16,0},{24,8},{1,17},{9,25},{17,1},{25,9},{2,18},{10... | collective-permute-start | bytes 1990664 | tf_op jit(solution)/shard_map/ppermute | solution.py:26
  94.7 34.7 %collective-permute-start.14 = (bf16[12,96,384]{2,1,0:T(8,128)(2,1)}, bf16[12,96,384]{2,1,0:T(8,128)(2,1)}, u32[]{:S(2)}, u32[]{:S(2)}) collective-permute-start(bf16[12,96,384]{2,1,0:T(8,128)(2,1)} %after.22), channel_id=1, source_target_pairs={{0,16},{8,24},{16,0},{24,8},{1,17},{9,25},{17,1},{25,9},{2,18},{10... | collective-permute-start | bytes 2654216 | tf_op jit(solution)/shard_map/ppermute | solution.py:26
  95.1 18.9 %collective-permute-start.15 = (bf16[9,96,384]{2,1,0:T(8,128)(2,1)}, bf16[9,96,384]{2,1,0:T(8,128)(2,1)}, u32[]{:S(2)}, u32[]{:S(2)}) collective-permute-start(bf16[9,96,384]{2,1,0:T(8,128)(2,1)} %after.23), channel_id=1, source_target_pairs={{0,8},{8,0},{16,24},{24,16},{1,9},{9,1},{17,25},{25,17},{2,10},{10... | collective-permute-start | bytes 1990664 | tf_op jit(solution)/shard_map/ppermute | solution.py:26
  110.5 20.3 %collective-permute-start.13 = (bf16[12,96,384]{2,1,0:T(8,128)(2,1)}, bf16[12,96,384]{2,1,0:T(8,128)(2,1)}, u32[]{:S(2)}, u32[]{:S(2)}) collective-permute-start(bf16[12,96,384]{2,1,0:T(8,128)(2,1)} %after.21), channel_id=1, source_target_pairs={{0,8},{8,0},{16,24},{24,16},{1,9},{9,1},{17,25},{25,17},{2,10},{10... | collective-permute-start | bytes 2654216 | tf_op jit(solution)/shard_map/ppermute | solution.py:26
  110.8 22.1 %collective-permute-start.23 = (bf16[9,96,384]{2,1,0:T(8,128)(2,1)}, bf16[9,96,384]{2,1,0:T(8,128)(2,1)S(1)}, u32[]{:S(2)}, u32[]{:S(2)}) collective-permute-start(bf16[9,96,384]{2,1,0:T(8,128)(2,1)} %collective-permute-done.22.refs_9_), channel_id=1, source_target_pairs={{0,1},{1,0},{2,3},{3,2},{4,5},{5,4},{6,7},{7,6},{8,9},{9,8},{10,11... | collective-permute-start | bytes 1990664 | tf_op jit(solution)/shard_map/ppermute | solution.py:26
  114.0 19.2 %collective-permute-start.18 = (bf16[2,5,96,384]{3,2,1,0:T(8,128)(2,1)S(1)}, bf16[2,5,96,384]{3,2,1,0:T(8,128)(2,1)S(1)}, u32[]{:S(2)}, u32[]{:S(2)}) collective-permute-start(bf16[2,5,96,384]{3,2,1,0:T(8,128)(2,1)S(1)} %pad_maximum_fusion), channel_id=1, source_target_pairs={{0,2},{1,3},{2,0},{3,1},{4,6},{5,7},{6,4},{7,5},{8,10},{9,11},{10,... | collective-permute-start | bytes 2211848 | tf_op jit(solution)/shard_map/ppermute | solution.py:26
  129.4 3.5 %collective-permute-start.20 = (bf16[9,96,384]{2,1,0:T(8,128)(2,1)}, bf16[9,96,384]{2,1,0:T(8,128)(2,1)S(1)}, u32[]{:S(2)}, u32[]{:S(2)}) collective-permute-start(bf16[9,96,384]{2,1,0:T(8,128)(2,1)} %collective-permute-done.15.refs_5_), channel_id=1, source_target_pairs={{0,1},{1,0},{2,3},{3,2},{4,5},{5,4},{6,7},{7,6},{8,9},{9,8},{10,11... | collective-permute-start | bytes 1990664 | tf_op jit(solution)/shard_map/ppermute | solution.py:26
  130.8 7.7 %collective-permute-start.24 = (bf16[12,96,384]{2,1,0:T(8,128)(2,1)}, bf16[12,96,384]{2,1,0:T(8,128)(2,1)}, u32[]{:S(2)}, u32[]{:S(2)}) collective-permute-start(bf16[12,96,384]{2,1,0:T(8,128)(2,1)} %collective-permute-done.14.refs_2_.refs_11_), channel_id=1, source_target_pairs={{0,1},{1,0},{2,3},{3,2},{4,5},{5,4},{6,7},{7,6},{8,9},{9,8},{10,11... | collective-permute-start | bytes 2654216 | tf_op jit(solution)/shard_map/ppermute | solution.py:26
  132.9 2.9 %copy-start.33 = (bf16[9,96,384]{2,1,0:T(8,128)(2,1)}, bf16[9,96,384]{2,1,0:T(8,128)(2,1)S(1)}, u32[]{:S(2)}) copy-start(bf16[9,96,384]{2,1,0:T(8,128)(2,1)S(1)} %collective-permute-done.23.refs_10_) | copy-start | bytes 1990660
  132.9 5.6 %collective-permute-start.21 = (bf16[12,96,384]{2,1,0:T(8,128)(2,1)}, bf16[12,96,384]{2,1,0:T(8,128)(2,1)}, u32[]{:S(2)}, u32[]{:S(2)}) collective-permute-start(bf16[12,96,384]{2,1,0:T(8,128)(2,1)} %collective-permute-done.13.refs_1_.refs_7_), channel_id=1, source_target_pairs={{0,1},{1,0},{2,3},{3,2},{4,5},{5,4},{6,7},{7,6},{8,9},{9,8},{10,11... | collective-permute-start | bytes 2654216 | tf_op jit(solution)/shard_map/ppermute | solution.py:26
  132.9 2.9 %copy-start.34 = (bf16[9,96,384]{2,1,0:T(8,128)(2,1)}, bf16[9,96,384]{2,1,0:T(8,128)(2,1)S(1)}, u32[]{:S(2)}) copy-start(bf16[9,96,384]{2,1,0:T(8,128)(2,1)S(1)} %collective-permute-done.20.refs_6_) | copy-start | bytes 1990660
  132.9 20.3 %collective-permute-start.27 = (bf16[9,96,384]{2,1,0:T(8,128)(2,1)}, bf16[9,96,384]{2,1,0:T(8,128)(2,1)}, u32[]{:S(2)}, u32[]{:S(2)}) collective-permute-start(bf16[9,96,384]{2,1,0:T(8,128)(2,1)} %collective-permute-done.22.refs_9_), channel_id=1, source_target_pairs={{0,8},{8,0},{16,24},{24,16},{1,9},{9,1},{17,25},{25,17},{2,10},{10... | collective-permute-start | bytes 1990664 | tf_op jit(solution)/shard_map/ppermute | solution.py:26
  133.2 5.2 %copy-start.29 = (bf16[2,5,96,384]{3,2,1,0:T(8,128)(2,1)}, bf16[2,5,96,384]{3,2,1,0:T(8,128)(2,1)S(1)}, u32[]{:S(2)}) copy-start(bf16[2,5,96,384]{3,2,1,0:T(8,128)(2,1)S(1)} %collective-permute-done.18.refs_1_.refs_2_) | copy-start | bytes 2211844
  133.2 22.3 %collective-permute-start.16 = (bf16[9,96,384]{2,1,0:T(8,128)(2,1)}, bf16[9,96,384]{2,1,0:T(8,128)(2,1)}, u32[]{:S(2)}, u32[]{:S(2)}) collective-permute-start(bf16[9,96,384]{2,1,0:T(8,128)(2,1)} %collective-permute-done.15.refs_5_), channel_id=1, source_target_pairs={{0,16},{8,24},{16,0},{24,8},{1,17},{9,25},{17,1},{25,9},{2,18},{10... | collective-permute-start | bytes 1990664 | tf_op jit(solution)/shard_map/ppermute | solution.py:26
  135.8 17.4 %collective-permute-start.26 = (bf16[1,5,96,384]{3,2,1,0:T(8,128)(2,1)S(1)}, bf16[1,5,96,384]{3,2,1,0:T(8,128)(2,1)S(1)}, u32[]{:S(2)}, u32[]{:S(2)}) collective-permute-start(bf16[1,5,96,384]{3,2,1,0:T(8,128)(2,1)S(1)} %add_convert_fusion), channel_id=1, source_target_pairs={{0,6},{1,7},{2,4},{3,5},{4,2},{5,3},{6,0},{7,1},{8,14},{9,15},{10,... | collective-permute-start | bytes 1105928 | tf_op jit(solution)/shard_map/ppermute | solution.py:26
  154.0 3.8 %collective-permute-start.29 = (bf16[9,96,384]{2,1,0:T(8,128)(2,1)}, bf16[9,96,384]{2,1,0:T(8,128)(2,1)S(1)}, u32[]{:S(2)}, u32[]{:S(2)}) collective-permute-start(bf16[9,96,384]{2,1,0:T(8,128)(2,1)} %after.27.refs_4_.refs_9_), channel_id=1, source_target_pairs={{0,1},{1,0},{2,3},{3,2},{4,5},{5,4},{6,7},{7,6},{8,9},{9,8},{10,11... | collective-permute-start | bytes 1990664 | tf_op jit(solution)/shard_map/ppermute | solution.py:26
  155.5 2.9 %collective-permute-start.28 = (bf16[9,96,384]{2,1,0:T(8,128)(2,1)}, bf16[9,96,384]{2,1,0:T(8,128)(2,1)S(1)}, u32[]{:S(2)}, u32[]{:S(2)}) collective-permute-start(bf16[9,96,384]{2,1,0:T(8,128)(2,1)} %after.26.refs_3_.refs_7_), channel_id=1, source_target_pairs={{0,1},{1,0},{2,3},{3,2},{4,5},{5,4},{6,7},{7,6},{8,9},{9,8},{10,11... | collective-permute-start | bytes 1990664 | tf_op jit(solution)/shard_map/ppermute | solution.py:26
  (25 other events, 26.6 us)

commit v19 on v18

--- a/solution.py
+++ b/solution.py
@@ -249,8 +249,11 @@
     shape = (planes, taps, rows, block)
 
     def kernel(place, shifts_ref, early_ref, *refs):
-        pieces, (mine_ref, theirs_ref) = refs[: len(layout)], refs[len(layout) : len(layout) + 2]
-        held, shifts, total, sems, shift_sems, early_sems = refs[len(layout) + 2 :]
+        pieces, (mine_ref, *theirs_refs) = (
+            refs[: len(layout)],
+            refs[len(layout) : len(layout) + 1 + planes],
+        )
+        held, shifts, total, sems, shift_sems, early_sems = refs[len(layout) + 1 + planes :]
         core, plane = place[1] % 2, place[1] // 2
         copies = start_act(
             place, coarse, layout, pieces, shifts_ref, held, shifts, sems, shift_sems
@@ -274,33 +277,41 @@
             fetch(i).wait()
             total[span, :] += term
 
-        for out_ref, parity, kind in (
-            (theirs_ref, 1 - core, jnp.bfloat16),
-            (mine_ref, core, jnp.float32),
-        ):
-
-            @pl.loop(0, planes)
-            def _(j):
-                start = ((plane ^ j) * 2 + parity) * rows
-                even = pl.ds(pl.multiple_of(start, 16), rows)
-                odd = pl.ds(pl.multiple_of(width + start, 16), rows)
-                for k, (left, right) in enumerate(GRAD_PARTS):
-                    term = total[even, left * block : (left + 1) * block]
-                    term += total[odd, right * block : (right + 1) * block]
-                    out_ref[j, k] = (scale * term).astype(kind)
+        def finish(j, parity, store):
+            start = ((plane ^ j) * 2 + parity) * rows
+            even = pl.ds(pl.multiple_of(start, 16), rows)
+            odd = pl.ds(pl.multiple_of(width + start, 16), rows)
+            for k, (left, right) in enumerate(GRAD_PARTS):
+                term = total[even, left * block : (left + 1) * block]
+                term += total[odd, right * block : (right + 1) * block]
+                store(k, scale * term)
+
+        for j in range(planes):
+
+            def leave(k, term):
+                theirs_refs[j][k] = term.astype(jnp.bfloat16)
+
+            finish(j, 1 - core, leave)
+
+        @pl.loop(0, planes)
+        def _(j):
+            def keep(k, term):
+                mine_ref[j, k] = term
+
+            finish(j, core, keep)
 
     whole = pl.BlockSpec(shape, lambda i, place: (0, 0, 0, 0))
     return pl.pallas_call(
         kernel,
         out_shape=(
             jax.ShapeDtypeStruct(shape, jnp.float32),
-            jax.ShapeDtypeStruct(shape, jnp.bfloat16),
+            *[jax.ShapeDtypeStruct(shape[1:], jnp.bfloat16)] * planes,
         ),
         grid_spec=pltpu.PrefetchScalarGridSpec(
             num_scalar_prefetch=1,
             grid=(1,),
             in_specs=[ANYWHERE] * (2 + len(pieces)),
-            out_specs=[whole, whole],
+            out_specs=[whole] + [pl.BlockSpec(shape[1:], lambda i, place: (0, 0, 0))] * planes,
             scratch_shapes=[
                 pltpu.VMEM((count, both), jnp.bfloat16),
                 pltpu.VMEM((count, columns), jnp.bfloat16),
@@ -521,14 +532,14 @@
     lines = stack_planes(place, line_across)
     far_top, far_bottom = after(far_top, early, lines), after(far_bottom, early, lines)
 
-    outgoing = [after(message, far_top, far_bottom) for message in outgoing]
+    other_own, other_lines = from_peer(own, "rep", 1), from_peer(lines, "rep", 1)
+    outgoing = [after(message, far_top, far_bottom, other_own, other_lines) for message in outgoing]
     kept = [from_peer(message, "seq", d) for message, d in zip(outgoing, (1, 1, 2, 2))]
-    other_own, other_lines = from_peer(own, "rep", 1), from_peer(lines, "rep", 1)
-
-    mine, theirs = late_terms(
+
+    mine, *theirs = late_terms(
         place, far_rows, [far_top, far_bottom], shifts, early, coarse, scale, planes, taps, rows
     )
-    arrived = from_peer(theirs, "rep", 1)
+    arrived = [from_peer(part, "rep", 1) for part in theirs]
     pairs = [mine[j] + arrived[j].astype(jnp.float32) for j in range(planes)]
     weight_grad, steps = reduce_line(pairs, "rep", planes, 2)
 

time: 175 us -> 207 us (1.18)
  waiting for transfers between devices: 43 us -> 75.3 us
  local copies, waits for them, and re-layouts: 30.4 us -> 21.7 us
  starting transfers between devices: 27 us -> 33.2 us
    ppermute x30 -> x33, waiting for transfers between devices: 43 us -> 75.3 us  [from_peer(): return lax.ppermute(value, axis, [(i, i ^ distance) for i in range(peers)])]
    unnamed x87 -> x55, local copies, waits for them, and re-layouts: 22.2 us -> 14.4 us
    ppermute x30 -> x33, starting transfers between devices: 27 us -> 33.2 us  [from_peer(): return lax.ppermute(value, axis, [(i, i ^ distance) for i in range(peers)])]
    another operation x1 -> x3, other arithmetic: 0.09 us -> 3.18 us  [reduce_line(): leaving = jnp.stack([blocks[d ^ mask].astype(jnp.bfloat16) for d in keep])]
    convert_element_type x2 -> x0, other arithmetic: 3.02 us -> none  [reduce_line(): leaving = jnp.stack([blocks[d ^ mask].astype(jnp.bfloat16) for d in keep])]
    concatenate x1, other arithmetic: 5.4 us -> 2.96 us  [on_device_square(): shifts = jnp.concatenate([later, trunk, earlier], axis=1)]
  transfers between devices with their start and end apart: 30 -> 33, of which waited for: 6 -> 10; matrix products, arithmetic and copies ran while one was open for 12% -> 10% of each run, Pallas kernels for 27% -> 22%
where the time goes in v19:
time: 207 us; the launch traced here: 202 us
  waiting for transfers between devices  75.3 us (36%)
  Pallas kernels  60.7 us (29%)
  starting transfers between devices  33.2 us (16%)
  local copies, waits for them, and re-layouts  21.7 us (10%)
  other arithmetic  10.5 us (5%)
    ppermute x33, waiting for transfers between devices, from_peer(): return lax.ppermute(value, axis, [(i, i ^ distance) for i in range(peers)])  75.3 us
    ppermute x33, starting transfers between devices, from_peer(): return lax.ppermute(value, axis, [(i, i ^ distance) for i in range(peers)])  33.2 us
    pallas_call x2, Pallas kernels, gradient_stage(): pl.pallas_call(body, out_shape=out_shape, grid_spec=pltpu.PrefetchScalarG...  27.3 us
    unnamed x55, local copies, waits for them, and re-layouts  14.4 us
    pallas_call x1, Pallas kernels, early_terms(): pl.pallas_call(kernel, out_shape=jax.ShapeDtypeStruct((both, columns), jn...  13.8 us
    pallas_call x1, Pallas kernels, late_terms(): pl.pallas_call(kernel, out_shape=(jax.ShapeDtypeStruct(shape, jnp.float32...  9.24 us
    slice x2, local copies, waits for them, and re-layouts, on_device_square(): top, bottom = (after(beside[:half], *ready), after(below[half:], *ready))  4.18 us
  transfers between devices with their start and end apart: 33, of which 10 were waited for; matrix products, arithmetic and copies ran while one was open for 10% of the time, Pallas kernels for 22%

profile of v19, /device:TPU:9, one launch (start us, length us, event | category | flops | bytes accessed | tf_op | source)
XLA Modules:
  0.0 202.5 jit_solution(9230791947676381774)
XLA Ops:
  0.6 1.0 slice.42.refs_0_
  1.6 1.4 collective-permute-start.1
  3.0 1.6 slice_bitcast_fusion.4
  4.5 1.2 collective-permute-start.3
  5.8 1.2 collective-permute-start.4
  7.2 2.2 %collective-permute-start = (bf16[3,96,384]{2,1,0:T(8,128)(2,1)S(1)}, bf16[3,96,384]{2,1,0:T(8,128)(2,1)}, u32[]{:S(2)}, u32[]{:S(2)}) collective-permute-start(bf16[3,96,384]{2,1,0:T(8,128)(2,1)S(1)} %slice.42.refs_0_), channel_id=1, source_target_pairs={{0,2},{1,3},{2,0},{3,1},{4,6},{5,7},{6,4},{7,5},{8,10},{9,11},{10,... | collective-permute-start | bytes 663560 | tf_op jit(solution)/shard_map/ppermute | solution.py:26
  9.4 3.6 %collective-permute-done.1.refs_3_.refs_4_ = bf16[3,96,384]{2,1,0:T(8,128)(2,1)} collective-permute-done((bf16[3,96,384]{2,1,0:T(8,128)(2,1)S(1)}, bf16[3,96,384]{2,1,0:T(8,128)(2,1)}, u32[]{:S(2)}, u32[]{:S(2)}) %collective-permute-start.1) | collective-permute-done | bytes 221216 | tf_op jit(solution)/shard_map/ppermute | solution.py:26
  13.0 1.4 copy-done.8
  14.4 1.8 act.1.refs_0_
  16.2 1.1 copy-done.6
  18.7 2.2 %pad_maximum_fusion.1.refs_0_ = bf16[4,2,96,384]{3,2,1,0:T(8,128)(2,1)} fusion(bf16[1,2,96,384]{3,2,1,0:T(8,128)(2,1)} %bitcast.56, bf16[1,2,96,384]{3,2,1,0:T(8,128)(2,1)} %bitcast.55, bf16[1,2,96,384]{3,2,1,0:T(8,128)(2,1)} %bitcast.54, bf16[1,2,96,384]{3,2,1,0:T(8,128)(2,1)} %get-tuple-element.26), kind=kLoop, calls=%fused_computation.19 | loop fusion | flops 884736 | bytes 1179648 | tf_op jit(solution)/shard_map/stack | solution.py:515
  20.9 1.2 collective-permute-start.8
  22.1 1.2 collective-permute-start.10
  23.3 1.2 collective-permute-start.6
  25.1 2.4 %collective-permute-start.7 = (bf16[4,2,96,384]{3,2,1,0:T(8,128)(2,1)}, bf16[4,2,96,384]{3,2,1,0:T(8,128)(2,1)}, u32[]{:S(2)}, u32[]{:S(2)}) collective-permute-start(bf16[4,2,96,384]{3,2,1,0:T(8,128)(2,1)} %after.15.refs_0_), channel_id=1, source_target_pairs={{0,2},{1,3},{2,0},{3,1},{4,6},{5,7},{6,4},{7,5},{8,10},{9,11},{10,... | collective-permute-start | bytes 1769480 | tf_op jit(solution)/shard_map/ppermute | solution.py:26
  27.5 19.9 %collective-permute-done.8.refs_5_.refs_3_ = bf16[4,2,96,384]{3,2,1,0:T(8,128)(2,1)} collective-permute-done((bf16[4,2,96,384]{3,2,1,0:T(8,128)(2,1)}, bf16[4,2,96,384]{3,2,1,0:T(8,128)(2,1)}, u32[]{:S(2)}, u32[]{:S(2)}) %collective-permute-start.8) | collective-permute-done | bytes 589856 | tf_op jit(solution)/shard_map/ppermute | solution.py:26
  47.4 3.0 %fusion.2.refs_2_.shifts_ref = bf16[2048,1152]{1,0:T(8,128)(2,1)} fusion(bf16[2047,384]{1,0:T(8,128)(2,1)S(1)} %get-tuple-element.25, bf16[2047,384]{1,0:T(8,128)(2,1)S(1)} %get-tuple-element.24, bf16[2048,384]{1,0:T(8,128)(2,1)S(1)} %bitcast.53), kind=kLoop, calls=%fused_computation.4 | loop fusion | flops 23592960 | bytes 9435648 | tf_op jit(solution)/shard_map/concatenate | solution.py:521
  50.4 5.8 %collective-permute-done.10.refs_2_ = bf16[512,1536]{1,0:T(8,128)(2,1)} collective-permute-done((bf16[512,1536]{1,0:T(8,128)(2,1)S(1)}, bf16[512,1536]{1,0:T(8,128)(2,1)}, u32[]{:S(2)}, u32[]{:S(2)}) %collective-permute-start.10) | collective-permute-done | bytes 1572896 | tf_op jit(solution)/shard_map/ppermute | solution.py:26
  56.2 1.0 collective-permute-done.6.refs_1_
  57.2 13.8 %weight_grad_early.1.refs_1_.early_ref = f32[1536,1152]{1,0:T(8,128)} custom-call(s32[2]{0:T(128)S(1)} %pad_add_fusion.place, bf16[2048,1152]{1,0:T(8,128)(2,1)} %fusion.2.refs_2_.shifts_ref, bf16[512,1536]{1,0:T(8,128)(2,1)S(1)} %copy-done.7, bf16[512,1536]{1,0:T(8,128)(2,1)} %collective-permute-done.6.refs_1_, ...), custom_call_target="tpu_custom_call" | custom-call | flops 1048576 | bytes 65536 | tf_op jit(solution)/shard_map/weight_grad_early/pallas_call | solution.py:224
  71.1 2.6 %stack_planes.1.refs_2_.refs_13_.refs_14_.refs_15_.refs_5_ = bf16[4,4,2,96,384]{4,3,2,1,0:T(8,128)(2,1)S(1)} custom-call(s32[2]{0:T(128)S(1)} %pad_add_fusion.place, bf16[4,2,96,384]{3,2,1,0:T(8,128)(2,1)} %after.15.refs_0_, bf16[4,2,96,384]{3,2,1,0:T(8,128)(2,1)} %collective-permute-done.7.refs_4_.refs_1_, bf16[4,2,96,384]{3,2,1,0:T(8,128)(2,1)} %after.17.refs_2_, ...), custom_call_target="tpu_custom_call" | custom-call | flops 1048576 | bytes 65536 | tf_op jit(solution)/shard_map/stack_planes/pallas_call | solution.py:485
  73.8 3.1 %collective-permute-start.14 = (bf16[4,4,2,96,384]{4,3,2,1,0:T(8,128)(2,1)S(1)}, bf16[4,4,2,96,384]{4,3,2,1,0:T(8,128)(2,1)}, u32[]{:S(2)}, u32[]{:S(2)}) collective-permute-start(bf16[4,4,2,96,384]{4,3,2,1,0:T(8,128)(2,1)S(1)} %stack_planes.1.refs_2_.refs_13_.refs_14_.refs_15_.refs_5_), channel_id=1, source_target_pairs={{0,1},{1,0},{2,3},{3,2},{4,5},{5,4},{6,7},{7,6},{8,9},{9,8},{10,11... | collective-permute-start | bytes 7077896 | tf_op jit(solution)/shard_map/ppermute | solution.py:26
  76.9 3.6 %kernel_messages.1 = (bf16[9,96,384]{2,1,0:T(8,128)(2,1)S(1)}, bf16[12,96,384]{2,1,0:T(8,128)(2,1)S(1)}, bf16[9,96,384]{2,1,0:T(8,128)(2,1)S(1)}, bf16[12,96,384]{2,1,0:T(8,128)(2,1)S(1)}, bf16[18,96,384]{2,1,0:T(8,128)(2,1)}) custom-call(s32[2]{0:T(128)S(1)} %pad_add_fusion.place, bf16[3,96,384]{2,1,0:T(8,128)(2,1)S(1)} %slice.42.refs_0_, ...), custom_call_target="tpu_custom_call" | custom-call | flops 1048576 | bytes 65536 | tf_op jit(solution)/shard_map/kernel_messages/pallas_call | solution.py:140
  80.8 2.3 %half_slope.1.refs_1_.refs_11_ = f32[2,512,768]{2,1,0:T(8,128)S(1)} custom-call(bf16[1,1024,768]{2,1,0:T(8,128)(2,1)S(1)} %copy-done.9), custom_call_target="tpu_custom_call" | custom-call | tf_op jit(solution)/shard_map/half_slope/pallas_call | solution.py:178
  83.2 1.6 copy-done.1
  84.8 2.1 %slice.57.refs_0_ = bf16[256,1536]{1,0:T(8,128)(2,1)} slice(bf16[512,1536]{1,0:T(8,128)(2,1)} %collective-permute-done.10.refs_2_), slice={[256:512], [0:1536]} | slice | bytes 1572864 | tf_op jit(solution)/shard_map/slice | solution.py:524
  86.9 1.2 collective-permute-start.12
  88.0 2.1 %slice.56.refs_0_ = bf16[256,1536]{1,0:T(8,128)(2,1)} slice(bf16[512,1536]{1,0:T(8,128)(2,1)} %collective-permute-done.6.refs_1_), slice={[0:256], [0:1536]} | slice | bytes 1572864 | tf_op jit(solution)/shard_map/slice | solution.py:524
  90.4 15.6 %collective-permute-done.12.refs_0_ = bf16[256,1536]{1,0:T(8,128)(2,1)S(1)} collective-permute-done((bf16[256,1536]{1,0:T(8,128)(2,1)}, bf16[256,1536]{1,0:T(8,128)(2,1)S(1)}, u32[]{:S(2)}, u32[]{:S(2)}) %collective-permute-start.12) | collective-permute-done | bytes 786464 | tf_op jit(solution)/shard_map/ppermute | solution.py:26
  106.0 0.9 copy-done.2
  106.9 2.0 %collective-permute-done.9.refs_0_ = bf16[256,1536]{1,0:T(8,128)(2,1)} collective-permute-done((bf16[256,1536]{1,0:T(8,128)(2,1)}, bf16[256,1536]{1,0:T(8,128)(2,1)}, u32[]{:S(2)}, u32[]{:S(2)}) %collective-permute-start.9) | collective-permute-done | bytes 786464 | tf_op jit(solution)/shard_map/ppermute | solution.py:26
  109.0 9.2 %weight_grad_late.1 = (f32[4,5,96,384]{3,2,1,0:T(8,128)S(1)}, bf16[5,96,384]{2,1,0:T(8,128)(2,1)S(1)}, bf16[5,96,384]{2,1,0:T(8,128)(2,1)}, bf16[5,96,384]{2,1,0:T(8,128)(2,1)}, bf16[5,96,384]{2,1,0:T(8,128)(2,1)S(1)}) custom-call(s32[2]{0:T(128)S(1)} %pad_add_fusion.place, bf16[2048,1152]{1,0:T(8,128)(2,1)} %fusion.2.refs_2_.shifts_ref, ...), custom_call_target="tpu_custom_call" | custom-call | flops 1048576 | bytes 65536 | tf_op jit(solution)/shard_map/weight_grad_late/pallas_call | solution.py:304
  118.2 1.5 copy-done.10
  121.3 1.5 collective-permute-start.19
  125.4 1.2 collective-permute-start.15
  126.6 1.3 fusion.7
  127.9 2.4 %collective-permute-start.21 = (bf16[2,5,96,384]{3,2,1,0:T(8,128)(2,1)S(1)}, bf16[2,5,96,384]{3,2,1,0:T(8,128)(2,1)S(1)}, u32[]{:S(2)}, u32[]{:S(2)}) collective-permute-start(bf16[2,5,96,384]{3,2,1,0:T(8,128)(2,1)S(1)} %pad_maximum_fusion), channel_id=1, source_target_pairs={{0,2},{1,3},{2,0},{3,1},{4,6},{5,7},{6,4},{7,5},{8,10},{9,11},{10,... | collective-permute-start | bytes 2211848 | tf_op jit(solution)/shard_map/ppermute | solution.py:26
  130.4 8.8 %collective-permute-done.24.refs_9_ = bf16[9,96,384]{2,1,0:T(8,128)(2,1)} collective-permute-done((bf16[9,96,384]{2,1,0:T(8,128)(2,1)}, bf16[9,96,384]{2,1,0:T(8,128)(2,1)}, u32[]{:S(2)}, u32[]{:S(2)}) %collective-permute-start.24) | collective-permute-done | bytes 663584 | tf_op jit(solution)/shard_map/ppermute | solution.py:26
  139.1 2.3 %collective-permute-start.25 = (bf16[9,96,384]{2,1,0:T(8,128)(2,1)}, bf16[9,96,384]{2,1,0:T(8,128)(2,1)}, u32[]{:S(2)}, u32[]{:S(2)}) collective-permute-start(bf16[9,96,384]{2,1,0:T(8,128)(2,1)} %collective-permute-done.24.refs_9_), channel_id=1, source_target_pairs={{0,1},{1,0},{2,3},{3,2},{4,5},{5,4},{6,7},{7,6},{8,9},{9,8},{10,11... | collective-permute-start | bytes 1990664 | tf_op jit(solution)/shard_map/ppermute | solution.py:26
  142.3 15.8 %collective-permute-done.16.refs_2_.refs_11_ = bf16[12,96,384]{2,1,0:T(8,128)(2,1)} collective-permute-done((bf16[12,96,384]{2,1,0:T(8,128)(2,1)}, bf16[12,96,384]{2,1,0:T(8,128)(2,1)}, u32[]{:S(2)}, u32[]{:S(2)}) %collective-permute-start.16) | collective-permute-done | bytes 884768 | tf_op jit(solution)/shard_map/ppermute | solution.py:26
  158.1 1.3 collective-permute-start.26
  162.0 1.8 fusion.9
  164.2 2.5 %copy.29.refs_0_ = bf16[18,96,384]{2,1,0:T(8,128)(2,1)} copy(bf16[18,96,384]{2,1,0:T(8,128)(2,1)} %get-tuple-element.12.refs_3_.refs_0_) | data formatting | bytes 2654208
  166.7 14.8 %input_grad.2.refs_1_.refs_12_ = f32[2,512,768]{2,1,0:T(8,128)} custom-call(s32[2]{0:T(128)} %copy-done.16, bf16[18,96,384]{2,1,0:T(8,128)(2,1)} %get-tuple-element.12.refs_3_.refs_0_, bf16[12,96,384]{2,1,0:T(8,128)(2,1)} %collective-permute-done.15.refs_1_.refs_7_, bf16[12,96,384]{2,1,0:T(8,128)(2,1)} %collective-permute-done.16.refs_2_.refs_11_, ...), custom_call_target="tpu_custom_call" | custom-call | flops 1048576 | bytes 65536 | tf_op jit(solution)/shard_map/input_grad/pallas_call | solution.py:461
  182.3 1.4 collective-permute-start.31
  184.7 2.1 %collective-permute-done.32 = bf16[5,96,384]{2,1,0:T(8,128)(2,1)S(1)} collective-permute-done((bf16[5,96,384]{2,1,0:T(8,128)(2,1)S(1)}, bf16[5,96,384]{2,1,0:T(8,128)(2,1)S(1)}, u32[]{:S(2)}, u32[]{:S(2)}) %collective-permute-start.32) | collective-permute-done | bytes 368672 | tf_op jit(solution)/shard_map/ppermute | solution.py:26
  186.8 2.1 %convert_add_fusion = f32[5,96,384]{2,1,0:T(8,128)} fusion(bf16[5,96,384]{2,1,0:T(8,128)(2,1)S(1)} %collective-permute-done.32, f32[4,5,96,384]{3,2,1,0:T(8,128)S(1)} %copy-done.11, bf16[2,5,96,384]{3,2,1,0:T(8,128)(2,1)} %copy-done.21, bf16[1,5,96,384]{3,2,1,0:T(8,128)(2,1)} %copy-done.22), kind=kLoop, calls=%fused_computation.9 | loop fusion | flops 1105920 | bytes 2580480 | tf_op jit(solution)/shard_map/add | solution.py:48
  189.8 12.5 %input_grad.3 = bf16[1,1024,768]{2,1,0:T(8,128)(2,1)} custom-call(s32[2]{0:T(128)} %copy-done.16, bf16[18,96,384]{2,1,0:T(8,128)(2,1)} %get-tuple-element.12.refs_3_.refs_0_, bf16[12,96,384]{2,1,0:T(8,128)(2,1)} %collective-permute-done.15.refs_1_.refs_7_, bf16[12,96,384]{2,1,0:T(8,128)(2,1)} %collective-permute-done.16.refs_2_.refs_11_, ...), custom_call_target="tpu_custom_call" | custom-call | flops 1048576 | bytes 65536 | tf_op jit(solution)/shard_map/input_grad/pallas_call | solution.py:461
  (107 shorter events, 13.4 us)
Async XLA Ops:
  1.6 11.4 %collective-permute-start.1 = (bf16[3,96,384]{2,1,0:T(8,128)(2,1)S(1)}, bf16[3,96,384]{2,1,0:T(8,128)(2,1)}, u32[]{:S(2)}, u32[]{:S(2)}) collective-permute-start(bf16[3,96,384]{2,1,0:T(8,128)(2,1)S(1)} %slice.42.refs_0_), channel_id=1, source_target_pairs={{0,6},{1,7},{2,4},{3,5},{4,2},{5,3},{6,0},{7,1},{8,14},{9,15},{10,... | collective-permute-start | bytes 663560 | tf_op jit(solution)/shard_map/ppermute | solution.py:26
  4.5 12.8 %collective-permute-start.3 = (bf16[2,96,384]{2,1,0:T(8,128)(2,1)S(1)}, bf16[2,96,384]{2,1,0:T(8,128)(2,1)S(1)}, u32[]{:S(2)}, u32[]{:S(2)}) collective-permute-start(bf16[2,96,384]{2,1,0:T(8,128)(2,1)S(1)} %get-tuple-element.27), channel_id=1, source_target_pairs={{0,8},{8,0},{16,24},{24,16},{1,9},{9,1},{17,25},{25,17},{2,10},{10... | collective-permute-start | bytes 442376 | tf_op jit(solution)/shard_map/ppermute | solution.py:26
  5.8 11.6 %collective-permute-start.4 = (bf16[2,96,384]{2,1,0:T(8,128)(2,1)S(1)}, bf16[2,96,384]{2,1,0:T(8,128)(2,1)S(1)}, u32[]{:S(2)}, u32[]{:S(2)}) collective-permute-start(bf16[2,96,384]{2,1,0:T(8,128)(2,1)S(1)} %get-tuple-element.27), channel_id=1, source_target_pairs={{0,16},{8,24},{16,0},{24,8},{1,17},{9,25},{17,1},{25,9},{2,18},{10... | collective-permute-start | bytes 442376 | tf_op jit(solution)/shard_map/ppermute | solution.py:26
  7.0 10.4 %collective-permute-start.5 = (bf16[2,96,384]{2,1,0:T(8,128)(2,1)S(1)}, bf16[2,96,384]{2,1,0:T(8,128)(2,1)S(1)}, u32[]{:S(2)}, u32[]{:S(2)}) collective-permute-start(bf16[2,96,384]{2,1,0:T(8,128)(2,1)S(1)} %get-tuple-element.27), channel_id=1, source_target_pairs={{0,24},{8,16},{16,8},{24,0},{1,25},{9,17},{17,9},{25,1},{2,26},{10... | collective-permute-start | bytes 442376 | tf_op jit(solution)/shard_map/ppermute | solution.py:26
  7.2 13.7 %collective-permute-start = (bf16[3,96,384]{2,1,0:T(8,128)(2,1)S(1)}, bf16[3,96,384]{2,1,0:T(8,128)(2,1)}, u32[]{:S(2)}, u32[]{:S(2)}) collective-permute-start(bf16[3,96,384]{2,1,0:T(8,128)(2,1)S(1)} %slice.42.refs_0_), channel_id=1, source_target_pairs={{0,2},{1,3},{2,0},{3,1},{4,6},{5,7},{6,4},{7,5},{8,10},{9,11},{10,... | collective-permute-start | bytes 663560 | tf_op jit(solution)/shard_map/ppermute | solution.py:26
  13.0 7.9 %collective-permute-start.2 = (bf16[3,96,384]{2,1,0:T(8,128)(2,1)}, bf16[3,96,384]{2,1,0:T(8,128)(2,1)}, u32[]{:S(2)}, u32[]{:S(2)}) collective-permute-start(bf16[3,96,384]{2,1,0:T(8,128)(2,1)} %collective-permute-done.1.refs_3_.refs_4_), channel_id=1, source_target_pairs={{0,2},{1,3},{2,0},{3,1},{4,6},{5,7},{6,4},{7,5},{8,10},{9,11},{10,... | collective-permute-start | bytes 663560 | tf_op jit(solution)/shard_map/ppermute | solution.py:26
  18.7 3.4 %copy-start.7 = (bf16[512,1536]{1,0:T(8,128)(2,1)S(1)}, bf16[512,1536]{1,0:T(8,128)(2,1)}, u32[]{:S(2)}) copy-start(bf16[512,1536]{1,0:T(8,128)(2,1)} %after.14.refs_1_.refs_0_) | copy-start | bytes 4718596
  18.7 5.8 %copy-start.4 = (bf16[1,2048,384]{2,1,0:T(8,128)(2,1)S(1)}, bf16[1,2048,384]{2,1,0:T(8,128)(2,1)}, u32[]{:S(2)}) copy-start(bf16[1,2048,384]{2,1,0:T(8,128)(2,1)} %refs_4_.1) | copy-start | bytes 4718596
  20.9 26.5 %collective-permute-start.8 = (bf16[4,2,96,384]{3,2,1,0:T(8,128)(2,1)}, bf16[4,2,96,384]{3,2,1,0:T(8,128)(2,1)}, u32[]{:S(2)}, u32[]{:S(2)}) collective-permute-start(bf16[4,2,96,384]{3,2,1,0:T(8,128)(2,1)} %after.15.refs_0_), channel_id=1, source_target_pairs={{0,6},{1,7},{2,4},{3,5},{4,2},{5,3},{6,0},{7,1},{8,14},{9,15},{10,... | collective-permute-start | bytes 1769480 | tf_op jit(solution)/shard_map/ppermute | solution.py:26
  22.1 34.2 %collective-permute-start.10 = (bf16[512,1536]{1,0:T(8,128)(2,1)S(1)}, bf16[512,1536]{1,0:T(8,128)(2,1)}, u32[]{:S(2)}, u32[]{:S(2)}) collective-permute-start(bf16[512,1536]{1,0:T(8,128)(2,1)S(1)} %copy-done.7), channel_id=1, source_target_pairs={{0,16},{8,24},{16,0},{24,8},{1,17},{9,25},{17,1},{25,9},{2,18},{10... | collective-permute-start | bytes 4718600 | tf_op jit(solution)/shard_map/ppermute | solution.py:26
  23.3 33.9 %collective-permute-start.6 = (bf16[512,1536]{1,0:T(8,128)(2,1)S(1)}, bf16[512,1536]{1,0:T(8,128)(2,1)}, u32[]{:S(2)}, u32[]{:S(2)}) collective-permute-start(bf16[512,1536]{1,0:T(8,128)(2,1)S(1)} %copy-done.7), channel_id=1, source_target_pairs={{0,8},{8,0},{16,24},{24,16},{1,9},{9,1},{17,25},{25,17},{2,10},{10... | collective-permute-start | bytes 4718600 | tf_op jit(solution)/shard_map/ppermute | solution.py:26
  25.1 46.0 %collective-permute-start.7 = (bf16[4,2,96,384]{3,2,1,0:T(8,128)(2,1)}, bf16[4,2,96,384]{3,2,1,0:T(8,128)(2,1)}, u32[]{:S(2)}, u32[]{:S(2)}) collective-permute-start(bf16[4,2,96,384]{3,2,1,0:T(8,128)(2,1)} %after.15.refs_0_), channel_id=1, source_target_pairs={{0,2},{1,3},{2,0},{3,1},{4,6},{5,7},{6,4},{7,5},{8,10},{9,11},{10,... | collective-permute-start | bytes 1769480 | tf_op jit(solution)/shard_map/ppermute | solution.py:26
  47.4 23.7 %collective-permute-start.11 = (bf16[4,2,96,384]{3,2,1,0:T(8,128)(2,1)}, bf16[4,2,96,384]{3,2,1,0:T(8,128)(2,1)}, u32[]{:S(2)}, u32[]{:S(2)}) collective-permute-start(bf16[4,2,96,384]{3,2,1,0:T(8,128)(2,1)} %collective-permute-done.8.refs_5_.refs_3_), channel_id=1, source_target_pairs={{0,2},{1,3},{2,0},{3,1},{4,6},{5,7},{6,4},{7,5},{8,10},{9,11},{10,... | collective-permute-start | bytes 1769480 | tf_op jit(solution)/shard_map/ppermute | solution.py:26
  50.4 58.5 %copy-start.16 = (s32[2]{0:T(128)}, s32[2]{0:T(128)S(1)}, u32[]{:S(2)}) copy-start(s32[2]{0:T(128)S(1)} %pad_add_fusion.place) | copy-start | bytes 28
  71.1 5.8 %copy-start.5 = (bf16[1,2048,384]{2,1,0:T(8,128)(2,1)S(1)}, bf16[1,2048,384]{2,1,0:T(8,128)(2,1)}, u32[]{:S(2)}) copy-start(bf16[1,2048,384]{2,1,0:T(8,128)(2,1)} %refs_4_.1) | copy-start | bytes 4718596
  71.1 9.7 %copy-start.9 = (bf16[1,1024,768]{2,1,0:T(8,128)(2,1)S(1)}, bf16[1,1024,768]{2,1,0:T(8,128)(2,1)}, u32[]{:S(2)}) copy-start(bf16[1,1024,768]{2,1,0:T(8,128)(2,1)} %x_ref.3) | copy-start | bytes 4718596
  73.8 9.4 %copy-start = (bf16[4,4,2,96,384]{4,3,2,1,0:T(8,128)(2,1)}, bf16[4,4,2,96,384]{4,3,2,1,0:T(8,128)(2,1)S(1)}, u32[]{:S(2)}) copy-start(bf16[4,4,2,96,384]{4,3,2,1,0:T(8,128)(2,1)S(1)} %stack_planes.1.refs_2_.refs_13_.refs_14_.refs_15_.refs_5_) | copy-start | bytes 7077892
  73.8 49.0 %collective-permute-start.14 = (bf16[4,4,2,96,384]{4,3,2,1,0:T(8,128)(2,1)S(1)}, bf16[4,4,2,96,384]{4,3,2,1,0:T(8,128)(2,1)}, u32[]{:S(2)}, u32[]{:S(2)}) collective-permute-start(bf16[4,4,2,96,384]{4,3,2,1,0:T(8,128)(2,1)S(1)} %stack_planes.1.refs_2_.refs_13_.refs_14_.refs_15_.refs_5_), channel_id=1, source_target_pairs={{0,1},{1,0},{2,3},{3,2},{4,5},{5,4},{6,7},{7,6},{8,9},{9,8},{10,11... | collective-permute-start | bytes 7077896 | tf_op jit(solution)/shard_map/ppermute | solution.py:26
  80.5 2.7 %copy-start.12 = (bf16[12,96,384]{2,1,0:T(8,128)(2,1)}, bf16[12,96,384]{2,1,0:T(8,128)(2,1)S(1)}, u32[]{:S(2)}) copy-start(bf16[12,96,384]{2,1,0:T(8,128)(2,1)S(1)} %get-tuple-element.13.refs_0_) | copy-start | bytes 2654212
  80.5 2.7 %copy-start.13 = (bf16[12,96,384]{2,1,0:T(8,128)(2,1)}, bf16[12,96,384]{2,1,0:T(8,128)(2,1)S(1)}, u32[]{:S(2)}) copy-start(bf16[12,96,384]{2,1,0:T(8,128)(2,1)S(1)} %get-tuple-element.14.refs_0_) | copy-start | bytes 2654212
  80.5 2.7 %copy-start.14 = (bf16[9,96,384]{2,1,0:T(8,128)(2,1)}, bf16[9,96,384]{2,1,0:T(8,128)(2,1)S(1)}, u32[]{:S(2)}) copy-start(bf16[9,96,384]{2,1,0:T(8,128)(2,1)S(1)} %get-tuple-element.15.refs_0_) | copy-start | bytes 1990660
  80.5 2.7 %copy-start.15 = (bf16[9,96,384]{2,1,0:T(8,128)(2,1)}, bf16[9,96,384]{2,1,0:T(8,128)(2,1)S(1)}, u32[]{:S(2)}) copy-start(bf16[9,96,384]{2,1,0:T(8,128)(2,1)S(1)} %get-tuple-element.19.refs_0_) | copy-start | bytes 1990660
  80.5 42.2 %collective-permute-start.13 = (bf16[18,96,384]{2,1,0:T(8,128)(2,1)}, bf16[18,96,384]{2,1,0:T(8,128)(2,1)}, u32[]{:S(2)}, u32[]{:S(2)}) collective-permute-start(bf16[18,96,384]{2,1,0:T(8,128)(2,1)} %get-tuple-element.12.refs_3_.refs_0_), channel_id=1, source_target_pairs={{0,1},{1,0},{2,3},{3,2},{4,5},{5,4},{6,7},{7,6},{8,9},{9,8},{10,11... | collective-permute-start | bytes 3981320 | tf_op jit(solution)/shard_map/ppermute | solution.py:26
  83.2 1.6 copy-start.1
  86.9 19.1 %collective-permute-start.12 = (bf16[256,1536]{1,0:T(8,128)(2,1)}, bf16[256,1536]{1,0:T(8,128)(2,1)S(1)}, u32[]{:S(2)}, u32[]{:S(2)}) collective-permute-start(bf16[256,1536]{1,0:T(8,128)(2,1)} %after.19), channel_id=1, source_target_pairs={{0,8},{8,0},{16,24},{24,16},{1,9},{9,1},{17,25},{25,17},{2,10},{10... | collective-permute-start | bytes 2359304 | tf_op jit(solution)/shard_map/ppermute | solution.py:26
  90.1 18.8 %collective-permute-start.9 = (bf16[256,1536]{1,0:T(8,128)(2,1)}, bf16[256,1536]{1,0:T(8,128)(2,1)}, u32[]{:S(2)}, u32[]{:S(2)}) collective-permute-start(bf16[256,1536]{1,0:T(8,128)(2,1)} %after.16), channel_id=1, source_target_pairs={{0,16},{8,24},{16,0},{24,8},{1,17},{9,25},{17,1},{25,9},{2,18},{10... | collective-permute-start | bytes 2359304 | tf_op jit(solution)/shard_map/ppermute | solution.py:26
  106.9 2.1 %copy-start.3 = (bf16[256,1536]{1,0:T(8,128)(2,1)S(1)}, bf16[256,1536]{1,0:T(8,128)(2,1)}, u32[]{:S(2)}) copy-start(bf16[256,1536]{1,0:T(8,128)(2,1)} %after.20.refs_2_.refs_1_) | copy-start | bytes 2359300
  118.2 1.6 copy-start.10
  121.3 3.3 %collective-permute-start.19 = (bf16[5,96,384]{2,1,0:T(8,128)(2,1)}, bf16[5,96,384]{2,1,0:T(8,128)(2,1)}, u32[]{:S(2)}, u32[]{:S(2)}) collective-permute-start(bf16[5,96,384]{2,1,0:T(8,128)(2,1)} %get-tuple-element.17), channel_id=1, source_target_pairs={{0,1},{1,0},{2,3},{3,2},{4,5},{5,4},{6,7},{7,6},{8,9},{9,8},{10,11... | collective-permute-start | bytes 1105928 | tf_op jit(solution)/shard_map/ppermute | solution.py:26
  122.7 2.7 %collective-permute-start.20 = (bf16[5,96,384]{2,1,0:T(8,128)(2,1)}, bf16[5,96,384]{2,1,0:T(8,128)(2,1)}, u32[]{:S(2)}, u32[]{:S(2)}) collective-permute-start(bf16[5,96,384]{2,1,0:T(8,128)(2,1)} %get-tuple-element.18), channel_id=1, source_target_pairs={{0,1},{1,0},{2,3},{3,2},{4,5},{5,4},{6,7},{7,6},{8,9},{9,8},{10,11... | collective-permute-start | bytes 1105928 | tf_op jit(solution)/shard_map/ppermute | solution.py:26
  122.8 16.4 %collective-permute-start.24 = (bf16[9,96,384]{2,1,0:T(8,128)(2,1)}, bf16[9,96,384]{2,1,0:T(8,128)(2,1)}, u32[]{:S(2)}, u32[]{:S(2)}) collective-permute-start(bf16[9,96,384]{2,1,0:T(8,128)(2,1)} %after.25), channel_id=1, source_target_pairs={{0,16},{8,24},{16,0},{24,8},{1,17},{9,25},{17,1},{25,9},{2,18},{10... | collective-permute-start | bytes 1990664 | tf_op jit(solution)/shard_map/ppermute | solution.py:26
  123.7 4.2 %collective-permute-start.27 = (bf16[5,96,384]{2,1,0:T(8,128)(2,1)S(1)}, bf16[5,96,384]{2,1,0:T(8,128)(2,1)}, u32[]{:S(2)}, u32[]{:S(2)}) collective-permute-start(bf16[5,96,384]{2,1,0:T(8,128)(2,1)S(1)} %copy-done.20), channel_id=1, source_target_pairs={{0,1},{1,0},{2,3},{3,2},{4,5},{5,4},{6,7},{7,6},{8,9},{9,8},{10,11... | collective-permute-start | bytes 1105928 | tf_op jit(solution)/shard_map/ppermute | solution.py:26
  124.2 17.2 %collective-permute-start.17 = (bf16[9,96,384]{2,1,0:T(8,128)(2,1)}, bf16[9,96,384]{2,1,0:T(8,128)(2,1)}, u32[]{:S(2)}, u32[]{:S(2)}) collective-permute-start(bf16[9,96,384]{2,1,0:T(8,128)(2,1)} %after.23), channel_id=1, source_target_pairs={{0,8},{8,0},{16,24},{24,16},{1,9},{9,1},{17,25},{25,17},{2,10},{10... | collective-permute-start | bytes 1990664 | tf_op jit(solution)/shard_map/ppermute | solution.py:26
  124.6 2.0 copy-start.11
  124.6 33.5 %collective-permute-start.16 = (bf16[12,96,384]{2,1,0:T(8,128)(2,1)}, bf16[12,96,384]{2,1,0:T(8,128)(2,1)}, u32[]{:S(2)}, u32[]{:S(2)}) collective-permute-start(bf16[12,96,384]{2,1,0:T(8,128)(2,1)} %after.22), channel_id=1, source_target_pairs={{0,16},{8,24},{16,0},{24,8},{1,17},{9,25},{17,1},{25,9},{2,18},{10... | collective-permute-start | bytes 2654216 | tf_op jit(solution)/shard_map/ppermute | solution.py:26
  125.4 34.7 %collective-permute-start.15 = (bf16[12,96,384]{2,1,0:T(8,128)(2,1)}, bf16[12,96,384]{2,1,0:T(8,128)(2,1)}, u32[]{:S(2)}, u32[]{:S(2)}) collective-permute-start(bf16[12,96,384]{2,1,0:T(8,128)(2,1)} %after.21), channel_id=1, source_target_pairs={{0,8},{8,0},{16,24},{24,16},{1,9},{9,1},{17,25},{25,17},{2,10},{10... | collective-permute-start | bytes 2654216 | tf_op jit(solution)/shard_map/ppermute | solution.py:26
  127.9 32.9 %collective-permute-start.21 = (bf16[2,5,96,384]{3,2,1,0:T(8,128)(2,1)S(1)}, bf16[2,5,96,384]{3,2,1,0:T(8,128)(2,1)S(1)}, u32[]{:S(2)}, u32[]{:S(2)}) collective-permute-start(bf16[2,5,96,384]{3,2,1,0:T(8,128)(2,1)S(1)} %pad_maximum_fusion), channel_id=1, source_target_pairs={{0,2},{1,3},{2,0},{3,1},{4,6},{5,7},{6,4},{7,5},{8,10},{9,11},{10,... | collective-permute-start | bytes 2211848 | tf_op jit(solution)/shard_map/ppermute | solution.py:26
  139.1 22.0 %collective-permute-start.25 = (bf16[9,96,384]{2,1,0:T(8,128)(2,1)}, bf16[9,96,384]{2,1,0:T(8,128)(2,1)}, u32[]{:S(2)}, u32[]{:S(2)}) collective-permute-start(bf16[9,96,384]{2,1,0:T(8,128)(2,1)} %collective-permute-done.24.refs_9_), channel_id=1, source_target_pairs={{0,1},{1,0},{2,3},{3,2},{4,5},{5,4},{6,7},{7,6},{8,9},{9,8},{10,11... | collective-permute-start | bytes 1990664 | tf_op jit(solution)/shard_map/ppermute | solution.py:26
  141.4 22.4 %collective-permute-start.22 = (bf16[9,96,384]{2,1,0:T(8,128)(2,1)}, bf16[9,96,384]{2,1,0:T(8,128)(2,1)}, u32[]{:S(2)}, u32[]{:S(2)}) collective-permute-start(bf16[9,96,384]{2,1,0:T(8,128)(2,1)} %collective-permute-done.17.refs_5_), channel_id=1, source_target_pairs={{0,1},{1,0},{2,3},{3,2},{4,5},{5,4},{6,7},{7,6},{8,9},{9,8},{10,11... | collective-permute-start | bytes 1990664 | tf_op jit(solution)/shard_map/ppermute | solution.py:26
  158.1 8.6 %collective-permute-start.26 = (bf16[12,96,384]{2,1,0:T(8,128)(2,1)}, bf16[12,96,384]{2,1,0:T(8,128)(2,1)}, u32[]{:S(2)}, u32[]{:S(2)}) collective-permute-start(bf16[12,96,384]{2,1,0:T(8,128)(2,1)} %collective-permute-done.16.refs_2_.refs_11_), channel_id=1, source_target_pairs={{0,1},{1,0},{2,3},{3,2},{4,5},{5,4},{6,7},{7,6},{8,9},{9,8},{10,11... | collective-permute-start | bytes 2654216 | tf_op jit(solution)/shard_map/ppermute | solution.py:26
  160.1 6.7 %collective-permute-start.23 = (bf16[12,96,384]{2,1,0:T(8,128)(2,1)}, bf16[12,96,384]{2,1,0:T(8,128)(2,1)}, u32[]{:S(2)}, u32[]{:S(2)}) collective-permute-start(bf16[12,96,384]{2,1,0:T(8,128)(2,1)} %collective-permute-done.15.refs_1_.refs_7_), channel_id=1, source_target_pairs={{0,1},{1,0},{2,3},{3,2},{4,5},{5,4},{6,7},{7,6},{8,9},{9,8},{10,11... | collective-permute-start | bytes 2654216 | tf_op jit(solution)/shard_map/ppermute | solution.py:26
  160.8 20.7 %collective-permute-start.29 = (bf16[9,96,384]{2,1,0:T(8,128)(2,1)}, bf16[9,96,384]{2,1,0:T(8,128)(2,1)}, u32[]{:S(2)}, u32[]{:S(2)}) collective-permute-start(bf16[9,96,384]{2,1,0:T(8,128)(2,1)} %collective-permute-done.24.refs_9_), channel_id=1, source_target_pairs={{0,8},{8,0},{16,24},{24,16},{1,9},{9,1},{17,25},{25,17},{2,10},{10... | collective-permute-start | bytes 1990664 | tf_op jit(solution)/shard_map/ppermute | solution.py:26
  161.2 22.5 %collective-permute-start.18 = (bf16[9,96,384]{2,1,0:T(8,128)(2,1)}, bf16[9,96,384]{2,1,0:T(8,128)(2,1)}, u32[]{:S(2)}, u32[]{:S(2)}) collective-permute-start(bf16[9,96,384]{2,1,0:T(8,128)(2,1)} %collective-permute-done.17.refs_5_), channel_id=1, source_target_pairs={{0,16},{8,24},{16,0},{24,8},{1,17},{9,25},{17,1},{25,9},{2,18},{10... | collective-permute-start | bytes 1990664 | tf_op jit(solution)/shard_map/ppermute | solution.py:26
  163.8 17.7 %collective-permute-start.28 = (bf16[1,5,96,384]{3,2,1,0:T(8,128)(2,1)}, bf16[1,5,96,384]{3,2,1,0:T(8,128)(2,1)S(1)}, u32[]{:S(2)}, u32[]{:S(2)}) collective-permute-start(bf16[1,5,96,384]{3,2,1,0:T(8,128)(2,1)} %fusion.9), channel_id=1, source_target_pairs={{0,6},{1,7},{2,4},{3,5},{4,2},{5,3},{6,0},{7,1},{8,14},{9,15},{10,... | collective-permute-start | bytes 1105928 | tf_op jit(solution)/shard_map/ppermute | solution.py:26
  182.3 1.5 copy-start.18
  182.3 6.6 %collective-permute-start.31 = (bf16[9,96,384]{2,1,0:T(8,128)(2,1)}, bf16[9,96,384]{2,1,0:T(8,128)(2,1)}, u32[]{:S(2)}, u32[]{:S(2)}) collective-permute-start(bf16[9,96,384]{2,1,0:T(8,128)(2,1)} %after.27.refs_4_.refs_9_), channel_id=1, source_target_pairs={{0,1},{1,0},{2,3},{3,2},{4,5},{5,4},{6,7},{7,6},{8,9},{9,8},{10,11... | collective-permute-start | bytes 1990664 | tf_op jit(solution)/shard_map/ppermute | solution.py:26
  183.7 5.2 %collective-permute-start.30 = (bf16[9,96,384]{2,1,0:T(8,128)(2,1)}, bf16[9,96,384]{2,1,0:T(8,128)(2,1)S(1)}, u32[]{:S(2)}, u32[]{:S(2)}) collective-permute-start(bf16[9,96,384]{2,1,0:T(8,128)(2,1)} %after.26.refs_3_.refs_7_), channel_id=1, source_target_pairs={{0,1},{1,0},{2,3},{3,2},{4,5},{5,4},{6,7},{7,6},{8,9},{9,8},{10,11... | collective-permute-start | bytes 1990664 | tf_op jit(solution)/shard_map/ppermute | solution.py:26
  183.8 3.0 %collective-permute-start.32 = (bf16[5,96,384]{2,1,0:T(8,128)(2,1)S(1)}, bf16[5,96,384]{2,1,0:T(8,128)(2,1)S(1)}, u32[]{:S(2)}, u32[]{:S(2)}) collective-permute-start(bf16[5,96,384]{2,1,0:T(8,128)(2,1)S(1)} %copy-done.18), channel_id=1, source_target_pairs={{0,1},{1,0},{2,3},{3,2},{4,5},{5,4},{6,7},{7,6},{8,9},{9,8},{10,11... | collective-permute-start | bytes 1105928 | tf_op jit(solution)/shard_map/ppermute | solution.py:26
  (12 other events, 10.8 us)

commit v20 on v17

--- a/solution.py
+++ b/solution.py
@@ -34,6 +34,20 @@
         input_output_aliases={0: 0},
         name="after",
     )(value, *earlier)
+
+def reduce_line(blocks, axis, count, unit):
+    held, masks = [[0]], []
+    while count > 1:
+        masks.append(count - 1)
+        held.append(held[-1] + [d ^ masks[-1] for d in held[-1]])
+        count //= 2
+    blocks, steps = dict(enumerate(blocks)), []
+    for mask, keep in reversed(list(zip(masks, held))):
+        leaving = jnp.stack([blocks[d ^ mask].astype(jnp.bfloat16) for d in keep])
+        steps.append(from_peer(leaving, axis, mask * unit))
+        blocks = {d: blocks[d] + steps[-1][n].astype(jnp.float32) for n, d in enumerate(keep)}
+    return blocks[0], steps
+
 
 def gather_line(value, axis, count, unit):
     found, mask = {0: value}, count - 1
@@ -516,15 +530,12 @@
     for j in range(planes):
         part = arrived[j // (planes // 2)][j % (planes // 2)]
         pairs.append(mine[j] + part.astype(jnp.float32))
-    weight_grad = pairs[0]
-    leaving = [after(part.astype(jnp.bfloat16), other_column, other_lines) for part in pairs[1:]]
-    summed = [from_peer(leaving[j - 1], "rep", 2 * j) for j in range(1, planes)]
+    weight_grad, steps = reduce_line(pairs, "rep", planes, 2)
 
     window = (coarse + 2 * HALO) // rows
     count, side = planes * SPLIT, window // 2
-    far_first = after(kept_beside[: side + count // 2], *leaving)
-    far_second = after(kept_below[count // 2 : count + side], *leaving)
-    far_first, far_second = from_peer(far_first, "seq", 2), from_peer(far_second, "seq", 1)
+    far_first = from_peer(kept_beside[: side + count // 2], "seq", 2)
+    far_second = from_peer(kept_below[count // 2 : count + side], "seq", 1)
 
     windows = [
         [(own_window, 0, 0, window)],
@@ -543,16 +554,15 @@
     ]
     near = [piece for piece in crossed if piece[-1] < 3]
     begun = stage(windows, pieces=soon + near, distances=[0, 1, 2], begun=None)
-    far_first, far_second = after(far_first, begun, *summed), after(far_second, begun, *summed)
+    far_first, far_second = after(far_first, begun, *steps[:1]), after(far_second, begun, *steps[:1])
     windows.append([(far_first, 0, 0, side), (far_second, count // 2, side, side)])
     rest = [piece for piece in crossed if piece[-1] == 3]
     for part, start, plane in ((far_first, side, 0), (far_second, 0, planes // 2)):
         rest.append((part, start, plane, planes // 2, 0, 3))
         rest.append((from_peer(part, "rep", 1), start, plane, planes // 2, 1, 3))
     input_grad = stage(windows, pieces=rest, distances=[3], begun=begun)
-    for part in summed:
-        weight_grad = weight_grad + after(part, input_grad).astype(jnp.float32)
     return (input_grad, weight_grad)
+
 
 def with_halo(value, sides, width):
     for axis, dim in sides:

time: 186 us -> 174 us (0.935)
  the two profiles are of different devices: /device:TPU:0 before, /device:TPU:9 now
where the time goes in v20:
time: 174 us; the launch traced here: 173 us
  Pallas kernels  55.1 us (32%)
  waiting for transfers between devices  46.8 us (27%)
  local copies, waits for them, and re-layouts  31.8 us (18%)
  starting transfers between devices  26.9 us (15%)
  other arithmetic  10.8 us (6%)
    ppermute x27, waiting for transfers between devices, from_peer(): return lax.ppermute(value, axis, [(i, i ^ distance) for i in range(peers)])  46.8 us
    ppermute x27, starting transfers between devices, from_peer(): return lax.ppermute(value, axis, [(i, i ^ distance) for i in range(peers)])  26.9 us
    pallas_call x2, Pallas kernels, gradient_stage(): pl.pallas_call(body, out_shape=out_shape, grid_spec=pltpu.PrefetchScalarG...  26.2 us
    unnamed x90, local copies, waits for them, and re-layouts  21.4 us
    pallas_call x1, Pallas kernels, early_terms(): pl.pallas_call(kernel, out_shape=jax.ShapeDtypeStruct((both, columns), jn...  13.8 us
    pallas_call x1, Pallas kernels, late_terms(): pl.pallas_call(kernel, out_shape=(jax.ShapeDtypeStruct(shape, jnp.float32...  8.19 us
    concatenate x1, other arithmetic, on_device_square(): shifts = jnp.concatenate([later, trunk, earlier], axis=1)  5.4 us
    slice x2, local copies, waits for them, and re-layouts, on_device_square(): top, bottom = (after(beside[:half], *ready), after(below[half:], *ready))  4.15 us
  transfers between devices with their start and end apart: 27, of which 5 were waited for; matrix products, arithmetic and copies ran while one was open for 12% of the time, Pallas kernels for 25%

profile of v20, /device:TPU:9, one launch (start us, length us, event | category | flops | bytes accessed | tf_op | source)
XLA Modules:
  0.0 172.5 jit_solution(1306037749537122242)
XLA Ops:
  0.6 1.0 slice.60.refs_0_
  1.6 1.4 collective-permute-start.1
  3.0 0.9 slice_bitcast_fusion.2
  3.9 1.3 collective-permute-start.3
  5.2 1.2 collective-permute-start.4
  6.6 2.2 %collective-permute-start = (bf16[3,96,384]{2,1,0:T(8,128)(2,1)S(1)}, bf16[3,96,384]{2,1,0:T(8,128)(2,1)S(1)}, u32[]{:S(2)}, u32[]{:S(2)}) collective-permute-start(bf16[3,96,384]{2,1,0:T(8,128)(2,1)S(1)} %slice.60.refs_0_), channel_id=1, source_target_pairs={{0,2},{1,3},{2,0},{3,1},{4,6},{5,7},{6,4},{7,5},{8,10},{9,11},{10,... | collective-permute-start | bytes 663560 | tf_op jit(solution)/shard_map/ppermute | solution.py:26
  8.8 1.4 copy-done.11
  10.2 1.8 %act.1.refs_0_ = bf16[512,1536]{1,0:T(8,128)(2,1)S(1)} custom-call(bf16[1,1024,768]{2,1,0:T(8,128)(2,1)S(1)} %copy-done.11), custom_call_target="tpu_custom_call" | custom-call | flops 1048576 | bytes 65536 | tf_op jit(solution)/shard_map/act/pallas_call | solution.py:84
  12.0 1.1 copy-done.4
  14.5 1.2 collective-permute-start.10
  15.8 1.2 collective-permute-start.6
  17.0 2.1 %slice_bitcast_fusion.1 = (bf16[2047,384]{1,0:T(8,128)(2,1)}, bf16[2047,384]{1,0:T(8,128)(2,1)}) fusion(bf16[1,2048,384]{2,1,0:T(8,128)(2,1)S(1)} %copy-done.3), kind=kLoop, calls=%fused_computation.7 | loop fusion | bytes 6288384 | tf_op jit(solution)/shard_map/slice | solution.py:503
  20.0 2.1 %collective-permute-done.2.refs_2_.refs_3_ = bf16[3,96,384]{2,1,0:T(8,128)(2,1)S(1)} collective-permute-done((bf16[3,96,384]{2,1,0:T(8,128)(2,1)S(1)}, bf16[3,96,384]{2,1,0:T(8,128)(2,1)S(1)}, u32[]{:S(2)}, u32[]{:S(2)}) %collective-permute-start.2) | collective-permute-done | bytes 221216 | tf_op jit(solution)/shard_map/ppermute | solution.py:26
  23.2 5.4 %fusion.2.refs_2_.shifts_ref = bf16[2048,1152]{1,0:T(8,128)(2,1)} fusion(bf16[2047,384]{1,0:T(8,128)(2,1)} %get-tuple-element.17, bf16[2047,384]{1,0:T(8,128)(2,1)} %get-tuple-element.16, bf16[2048,384]{1,0:T(8,128)(2,1)S(1)} %bitcast.14), kind=kLoop, calls=%fused_computation.4 | loop fusion | flops 23592960 | bytes 9435648 | tf_op jit(solution)/shard_map/concatenate | solution.py:505
  28.6 2.3 %half_slope.1.refs_1_.refs_11_ = f32[2,512,768]{2,1,0:T(8,128)S(1)} custom-call(bf16[1,1024,768]{2,1,0:T(8,128)(2,1)S(1)} %copy-done.12), custom_call_target="tpu_custom_call" | custom-call | tf_op jit(solution)/shard_map/half_slope/pallas_call | solution.py:166
  31.0 1.6 copy-done.2
  32.7 0.9 copy-done.28
  33.6 1.0 kernel_messages.1
  34.6 1.1 copy-done.6
  35.8 1.2 copy-done.13
  36.9 11.7 %collective-permute-done.10.refs_2_ = bf16[512,1536]{1,0:T(8,128)(2,1)} collective-permute-done((bf16[512,1536]{1,0:T(8,128)(2,1)}, bf16[512,1536]{1,0:T(8,128)(2,1)}, u32[]{:S(2)}, u32[]{:S(2)}) %collective-permute-start.10) | collective-permute-done | bytes 1572896 | tf_op jit(solution)/shard_map/ppermute | solution.py:26
  48.6 2.1 %slice.81.refs_0_ = bf16[256,1536]{1,0:T(8,128)(2,1)} slice(bf16[512,1536]{1,0:T(8,128)(2,1)} %collective-permute-done.10.refs_2_), slice={[256:512], [0:1536]} | slice | bytes 1572864 | tf_op jit(solution)/shard_map/slice | solution.py:508
  51.8 1.2 collective-permute-start.12
  53.0 2.1 %slice.80.refs_0_ = bf16[256,1536]{1,0:T(8,128)(2,1)} slice(bf16[512,1536]{1,0:T(8,128)(2,1)} %collective-permute-done.6.refs_1_), slice={[0:256], [0:1536]} | slice | bytes 1572864 | tf_op jit(solution)/shard_map/slice | solution.py:508
  55.1 1.2 collective-permute-start.9
  56.5 13.8 %weight_grad_early.1.refs_1_.early_ref = f32[1536,1152]{1,0:T(8,128)} custom-call(s32[2]{0:T(128)S(1)} %pad_add_fusion.place, bf16[2048,1152]{1,0:T(8,128)(2,1)} %fusion.2.refs_2_.shifts_ref, bf16[512,1536]{1,0:T(8,128)(2,1)S(1)} %copy-done.5, bf16[512,1536]{1,0:T(8,128)(2,1)} %collective-permute-done.6.refs_1_, ...), custom_call_target="tpu_custom_call" | custom-call | flops 1048576 | bytes 65536 | tf_op jit(solution)/shard_map/weight_grad_early/pallas_call | solution.py:212
  70.4 1.0 copy-done.15
  71.8 1.8 %stack_planes.1.refs_2_.refs_9_.refs_10_.refs_11_.refs_5_ = bf16[4,4,2,96,384]{4,3,2,1,0:T(8,128)(2,1)S(1)} custom-call(s32[2]{0:T(128)S(1)} %pad_add_fusion.place, bf16[4,2,96,384]{3,2,1,0:T(8,128)(2,1)S(1)} %copy-done.15, bf16[4,2,96,384]{3,2,1,0:T(8,128)(2,1)S(1)} %copy-done.19, bf16[4,2,96,384]{3,2,1,0:T(8,128)(2,1)} %after.14.refs_2_, ...), custom_call_target="tpu_custom_call" | custom-call | flops 1048576 | bytes 65536 | tf_op jit(solution)/shard_map/stack_planes/pallas_call | solution.py:469
  73.6 1.4 copy-done
  76.8 1.2 collective-permute-start.14
  78.5 4.1 %collective-permute-start.19 = (bf16[4,4,2,96,384]{4,3,2,1,0:T(8,128)(2,1)S(1)}, bf16[4,4,2,96,384]{4,3,2,1,0:T(8,128)(2,1)S(1)}, u32[]{:S(2)}, u32[]{:S(2)}) collective-permute-start(bf16[4,4,2,96,384]{4,3,2,1,0:T(8,128)(2,1)S(1)} %copy-done.1), channel_id=1, source_target_pairs={{0,1},{1,0},{2,3},{3,2},{4,5},{5,4},{6,7},{7,6},{8,9},{9,8},{10,11... | collective-permute-start | bytes 7077896 | tf_op jit(solution)/shard_map/ppermute | solution.py:26
  82.6 1.1 copy-done.10
  83.7 8.2 %weight_grad_late.1 = (f32[4,5,96,384]{3,2,1,0:T(8,128)S(1)}, bf16[2,5,96,384]{3,2,1,0:T(8,128)(2,1)S(1)}, bf16[2,5,96,384]{3,2,1,0:T(8,128)(2,1)S(1)}) custom-call(s32[2]{0:T(128)S(1)} %pad_add_fusion.place, bf16[2048,1152]{1,0:T(8,128)(2,1)} %fusion.2.refs_2_.shifts_ref, f32[1536,1152]{1,0:T(8,128)} %weight_grad_early.1.refs_1_.early_ref, ...), custom_call_target="tpu_custom_call" | custom-call | flops 1048576 | bytes 65536 | tf_op jit(solution)/shard_map/weight_grad_late/pallas_call | solution.py:287
  92.5 1.7 collective-permute-done.20
  94.3 14.5 %collective-permute-done.14.refs_2_.refs_7_ = bf16[21,96,384]{2,1,0:T(8,128)(2,1)} collective-permute-done((bf16[21,96,384]{2,1,0:T(8,128)(2,1)}, bf16[21,96,384]{2,1,0:T(8,128)(2,1)}, u32[]{:S(2)}, u32[]{:S(2)}) %collective-permute-start.14) | collective-permute-done | bytes 1548320 | tf_op jit(solution)/shard_map/ppermute | solution.py:26
  108.8 4.6 %collective-permute-start.18 = (bf16[21,96,384]{2,1,0:T(8,128)(2,1)}, bf16[21,96,384]{2,1,0:T(8,128)(2,1)S(1)}, u32[]{:S(2)}, u32[]{:S(2)}) collective-permute-start(bf16[21,96,384]{2,1,0:T(8,128)(2,1)} %collective-permute-done.14.refs_2_.refs_7_), channel_id=1, source_target_pairs={{0,1},{1,0},{2,3},{3,2},{4,5},{5,4},{6,7},{7,6},{8,9},{9,8},{10,11... | collective-permute-start | bytes 4644872 | tf_op jit(solution)/shard_map/ppermute | solution.py:26
  113.4 1.1 collective-permute-start.17
  114.7 1.0 pad_maximum_fusion
  116.3 1.2 slice.85
  117.8 1.1 slice.82
  119.8 1.1 copy-done.34
  121.0 1.1 copy-done.35
  122.1 14.4 %input_grad.2.refs_1_.refs_12_ = f32[2,512,768]{2,1,0:T(8,128)} custom-call(s32[2]{0:T(128)} %copy-done.29, bf16[6,96,384]{2,1,0:T(8,128)(2,1)} %copy-done.22, bf16[21,96,384]{2,1,0:T(8,128)(2,1)} %copy-done.31, bf16[21,96,384]{2,1,0:T(8,128)(2,1)} %collective-permute-done.14.refs_2_.refs_7_, bf16[21,96,384]{2,1,0:T(8,128)(2,1)} %after.19.refs_3_, ...), custom_call_target="tpu_custom_call" | custom-call | flops 1048576 | bytes 65536 | tf_op jit(solution)/shard_map/input_grad/pallas_call | solution.py:445
  137.4 1.0 collective-permute-start.25
  139.3 1.2 add_convert_fusion
  140.9 16.7 %collective-permute-done.26 = bf16[1,5,96,384]{3,2,1,0:T(8,128)(2,1)S(1)} collective-permute-done((bf16[1,5,96,384]{3,2,1,0:T(8,128)(2,1)S(1)}, bf16[1,5,96,384]{3,2,1,0:T(8,128)(2,1)S(1)}, u32[]{:S(2)}, u32[]{:S(2)}) %collective-permute-start.26) | collective-permute-done | bytes 368672 | tf_op jit(solution)/shard_map/ppermute | solution.py:26
  157.6 2.1 %add_bitcast_fusion = f32[5,96,384]{2,1,0:T(8,128)} fusion(bf16[1,5,96,384]{3,2,1,0:T(8,128)(2,1)S(1)} %collective-permute-done.26, f32[4,5,96,384]{3,2,1,0:T(8,128)S(1)} %copy-done.21, bf16[2,5,96,384]{3,2,1,0:T(8,128)(2,1)} %copy-done.32, bf16[2,5,96,384]{3,2,1,0:T(8,128)(2,1)} %copy-done.36), kind=kLoop, calls=%fused_computation.9 | loop fusion | flops 1105920 | bytes 2580480 | tf_op jit(solution)/shard_map/add | solution.py:48
  160.6 11.8 %input_grad.3 = bf16[1,1024,768]{2,1,0:T(8,128)(2,1)} custom-call(s32[2]{0:T(128)} %copy-done.29, bf16[6,96,384]{2,1,0:T(8,128)(2,1)} %copy-done.22, bf16[21,96,384]{2,1,0:T(8,128)(2,1)} %copy-done.31, bf16[21,96,384]{2,1,0:T(8,128)(2,1)} %collective-permute-done.14.refs_2_.refs_7_, bf16[9,96,384]{2,1,0:T(8,128)(2,1)} %after.20.refs_3_.refs_7_, ...), custom_call_target="tpu_custom_call" | custom-call | flops 1048576 | bytes 65536 | tf_op jit(solution)/shard_map/input_grad/pallas_call | solution.py:445
  (129 shorter events, 13.3 us)
Async XLA Ops:
  1.6 15.4 %collective-permute-start.1 = (bf16[3,96,384]{2,1,0:T(8,128)(2,1)S(1)}, bf16[3,96,384]{2,1,0:T(8,128)(2,1)S(1)}, u32[]{:S(2)}, u32[]{:S(2)}) collective-permute-start(bf16[3,96,384]{2,1,0:T(8,128)(2,1)S(1)} %slice.60.refs_0_), channel_id=1, source_target_pairs={{0,6},{1,7},{2,4},{3,5},{4,2},{5,3},{6,0},{7,1},{8,14},{9,15},{10,... | collective-permute-start | bytes 663560 | tf_op jit(solution)/shard_map/ppermute | solution.py:26
  3.9 9.2 %collective-permute-start.3 = (bf16[2,96,384]{2,1,0:T(8,128)(2,1)S(1)}, bf16[2,96,384]{2,1,0:T(8,128)(2,1)S(1)}, u32[]{:S(2)}, u32[]{:S(2)}) collective-permute-start(bf16[2,96,384]{2,1,0:T(8,128)(2,1)S(1)} %get-tuple-element.19), channel_id=1, source_target_pairs={{0,8},{8,0},{16,24},{24,16},{1,9},{9,1},{17,25},{25,17},{2,10},{10... | collective-permute-start | bytes 442376 | tf_op jit(solution)/shard_map/ppermute | solution.py:26
  5.2 8.0 %collective-permute-start.4 = (bf16[2,96,384]{2,1,0:T(8,128)(2,1)S(1)}, bf16[2,96,384]{2,1,0:T(8,128)(2,1)S(1)}, u32[]{:S(2)}, u32[]{:S(2)}) collective-permute-start(bf16[2,96,384]{2,1,0:T(8,128)(2,1)S(1)} %get-tuple-element.19), channel_id=1, source_target_pairs={{0,16},{8,24},{16,0},{24,8},{1,17},{9,25},{17,1},{25,9},{2,18},{10... | collective-permute-start | bytes 442376 | tf_op jit(solution)/shard_map/ppermute | solution.py:26
  6.4 6.7 %collective-permute-start.5 = (bf16[2,96,384]{2,1,0:T(8,128)(2,1)S(1)}, bf16[2,96,384]{2,1,0:T(8,128)(2,1)S(1)}, u32[]{:S(2)}, u32[]{:S(2)}) collective-permute-start(bf16[2,96,384]{2,1,0:T(8,128)(2,1)S(1)} %get-tuple-element.19), channel_id=1, source_target_pairs={{0,24},{8,16},{16,8},{24,0},{1,25},{9,17},{17,9},{25,1},{2,26},{10... | collective-permute-start | bytes 442376 | tf_op jit(solution)/shard_map/ppermute | solution.py:26
  6.6 13.4 %collective-permute-start = (bf16[3,96,384]{2,1,0:T(8,128)(2,1)S(1)}, bf16[3,96,384]{2,1,0:T(8,128)(2,1)S(1)}, u32[]{:S(2)}, u32[]{:S(2)}) collective-permute-start(bf16[3,96,384]{2,1,0:T(8,128)(2,1)S(1)} %slice.60.refs_0_), channel_id=1, source_target_pairs={{0,2},{1,3},{2,0},{3,1},{4,6},{5,7},{6,4},{7,5},{8,10},{9,11},{10,... | collective-permute-start | bytes 663560 | tf_op jit(solution)/shard_map/ppermute | solution.py:26
  13.1 3.8 %copy-start.3 = (bf16[1,2048,384]{2,1,0:T(8,128)(2,1)S(1)}, bf16[1,2048,384]{2,1,0:T(8,128)(2,1)}, u32[]{:S(2)}) copy-start(bf16[1,2048,384]{2,1,0:T(8,128)(2,1)} %refs_4_.1) | copy-start | bytes 4718596
  14.5 4.6 %copy-start.40 = (bf16[2,96,384]{2,1,0:T(8,128)(2,1)S(1)}, bf16[2,96,384]{2,1,0:T(8,128)(2,1)}, u32[]{:S(2)}) copy-start(bf16[2,96,384]{2,1,0:T(8,128)(2,1)} %copy-done.39) | copy-start | bytes 442372
  14.5 4.6 %copy-start.42 = (bf16[2,96,384]{2,1,0:T(8,128)(2,1)S(1)}, bf16[2,96,384]{2,1,0:T(8,128)(2,1)}, u32[]{:S(2)}) copy-start(bf16[2,96,384]{2,1,0:T(8,128)(2,1)} %copy-done.41) | copy-start | bytes 442372
  14.5 4.6 %copy-start.44 = (bf16[2,96,384]{2,1,0:T(8,128)(2,1)S(1)}, bf16[2,96,384]{2,1,0:T(8,128)(2,1)}, u32[]{:S(2)}) copy-start(bf16[2,96,384]{2,1,0:T(8,128)(2,1)} %copy-done.43) | copy-start | bytes 442372
  14.5 34.1 %collective-permute-start.10 = (bf16[512,1536]{1,0:T(8,128)(2,1)}, bf16[512,1536]{1,0:T(8,128)(2,1)}, u32[]{:S(2)}, u32[]{:S(2)}) collective-permute-start(bf16[512,1536]{1,0:T(8,128)(2,1)} %after.11.refs_1_.refs_0_), channel_id=1, source_target_pairs={{0,16},{8,24},{16,0},{24,8},{1,17},{9,25},{17,1},{25,9},{2,18},{10... | collective-permute-start | bytes 4718600 | tf_op jit(solution)/shard_map/ppermute | solution.py:26
  15.8 37.3 %collective-permute-start.6 = (bf16[512,1536]{1,0:T(8,128)(2,1)}, bf16[512,1536]{1,0:T(8,128)(2,1)}, u32[]{:S(2)}, u32[]{:S(2)}) collective-permute-start(bf16[512,1536]{1,0:T(8,128)(2,1)} %after.11.refs_1_.refs_0_), channel_id=1, source_target_pairs={{0,8},{8,0},{16,24},{24,16},{1,9},{9,1},{17,25},{25,17},{2,10},{10... | collective-permute-start | bytes 4718600 | tf_op jit(solution)/shard_map/ppermute | solution.py:26
  17.0 2.1 %copy-start.23 = (bf16[3,96,384]{2,1,0:T(8,128)(2,1)}, bf16[3,96,384]{2,1,0:T(8,128)(2,1)S(1)}, u32[]{:S(2)}) copy-start(bf16[3,96,384]{2,1,0:T(8,128)(2,1)S(1)} %collective-permute-done.1.refs_3_.refs_4_) | copy-start | bytes 663556
  17.0 5.2 %collective-permute-start.2 = (bf16[3,96,384]{2,1,0:T(8,128)(2,1)S(1)}, bf16[3,96,384]{2,1,0:T(8,128)(2,1)S(1)}, u32[]{:S(2)}, u32[]{:S(2)}) collective-permute-start(bf16[3,96,384]{2,1,0:T(8,128)(2,1)S(1)} %collective-permute-done.1.refs_3_.refs_4_), channel_id=1, source_target_pairs={{0,2},{1,3},{2,0},{3,1},{4,6},{5,7},{6,4},{7,5},{8,10},{9,11},{10,... | collective-permute-start | bytes 663560 | tf_op jit(solution)/shard_map/ppermute | solution.py:26
  20.0 2.1 %copy-start.25 = (bf16[3,96,384]{2,1,0:T(8,128)(2,1)}, bf16[3,96,384]{2,1,0:T(8,128)(2,1)S(1)}, u32[]{:S(2)}) copy-start(bf16[3,96,384]{2,1,0:T(8,128)(2,1)S(1)} %collective-permute-done.refs_1_.refs_2_) | copy-start | bytes 663556
  22.8 27.9 %collective-permute-start.8 = (bf16[4,2,96,384]{3,2,1,0:T(8,128)(2,1)}, bf16[4,2,96,384]{3,2,1,0:T(8,128)(2,1)S(1)}, u32[]{:S(2)}, u32[]{:S(2)}) collective-permute-start(bf16[4,2,96,384]{3,2,1,0:T(8,128)(2,1)} %after.12.refs_0_), channel_id=1, source_target_pairs={{0,6},{1,7},{2,4},{3,5},{4,2},{5,3},{6,0},{7,1},{8,14},{9,15},{10,... | collective-permute-start | bytes 1769480 | tf_op jit(solution)/shard_map/ppermute | solution.py:26
  22.8 27.9 %collective-permute-start.7 = (bf16[4,2,96,384]{3,2,1,0:T(8,128)(2,1)}, bf16[4,2,96,384]{3,2,1,0:T(8,128)(2,1)S(1)}, u32[]{:S(2)}, u32[]{:S(2)}) collective-permute-start(bf16[4,2,96,384]{3,2,1,0:T(8,128)(2,1)} %after.12.refs_0_), channel_id=1, source_target_pairs={{0,2},{1,3},{2,0},{3,1},{4,6},{5,7},{6,4},{7,5},{8,10},{9,11},{10,... | collective-permute-start | bytes 1769480 | tf_op jit(solution)/shard_map/ppermute | solution.py:26
  23.2 5.4 %copy-start.12 = (bf16[1,1024,768]{2,1,0:T(8,128)(2,1)S(1)}, bf16[1,1024,768]{2,1,0:T(8,128)(2,1)}, u32[]{:S(2)}) copy-start(bf16[1,1024,768]{2,1,0:T(8,128)(2,1)} %x_ref.3) | copy-start | bytes 4718596
  28.6 4.1 %copy-start.24 = (bf16[3,96,384]{2,1,0:T(8,128)(2,1)S(1)}, bf16[3,96,384]{2,1,0:T(8,128)(2,1)}, u32[]{:S(2)}) copy-start(bf16[3,96,384]{2,1,0:T(8,128)(2,1)} %copy-done.23) | copy-start | bytes 663556
  28.6 4.1 %copy-start.26 = (bf16[3,96,384]{2,1,0:T(8,128)(2,1)S(1)}, bf16[3,96,384]{2,1,0:T(8,128)(2,1)}, u32[]{:S(2)}) copy-start(bf16[3,96,384]{2,1,0:T(8,128)(2,1)} %copy-done.25) | copy-start | bytes 663556
  33.6 49.0 %copy-start.29 = (s32[2]{0:T(128)}, s32[2]{0:T(128)S(1)}, u32[]{:S(2)}) copy-start(s32[2]{0:T(128)S(1)} %pad_add_fusion.place) | copy-start | bytes 28
  36.9 13.8 %copy-start.22 = (bf16[6,96,384]{2,1,0:T(8,128)(2,1)}, bf16[6,96,384]{2,1,0:T(8,128)(2,1)S(1)}, u32[]{:S(2)}) copy-start(bf16[6,96,384]{2,1,0:T(8,128)(2,1)S(1)} %get-tuple-element.8.refs_0_) | copy-start | bytes 1327108
  51.8 23.2 %collective-permute-start.12 = (bf16[256,1536]{1,0:T(8,128)(2,1)}, bf16[256,1536]{1,0:T(8,128)(2,1)S(1)}, u32[]{:S(2)}, u32[]{:S(2)}) collective-permute-start(bf16[256,1536]{1,0:T(8,128)(2,1)} %after.16), channel_id=1, source_target_pairs={{0,8},{8,0},{16,24},{24,16},{1,9},{9,1},{17,25},{25,17},{2,10},{10... | collective-permute-start | bytes 2359304 | tf_op jit(solution)/shard_map/ppermute | solution.py:26
  55.1 20.8 %collective-permute-start.9 = (bf16[256,1536]{1,0:T(8,128)(2,1)}, bf16[256,1536]{1,0:T(8,128)(2,1)S(1)}, u32[]{:S(2)}, u32[]{:S(2)}) collective-permute-start(bf16[256,1536]{1,0:T(8,128)(2,1)} %after.13), channel_id=1, source_target_pairs={{0,16},{8,24},{16,0},{24,8},{1,17},{9,25},{17,1},{25,9},{2,18},{10... | collective-permute-start | bytes 2359304 | tf_op jit(solution)/shard_map/ppermute | solution.py:26
  56.4 14.0 %collective-permute-start.11 = (bf16[4,2,96,384]{3,2,1,0:T(8,128)(2,1)}, bf16[4,2,96,384]{3,2,1,0:T(8,128)(2,1)}, u32[]{:S(2)}, u32[]{:S(2)}) collective-permute-start(bf16[4,2,96,384]{3,2,1,0:T(8,128)(2,1)} %copy-done.16), channel_id=1, source_target_pairs={{0,2},{1,3},{2,0},{3,1},{4,6},{5,7},{6,4},{7,5},{8,10},{9,11},{10,... | collective-permute-start | bytes 1769480 | tf_op jit(solution)/shard_map/ppermute | solution.py:26
  76.8 1.7 copy-start.1
  76.8 5.7 %copy-start.8 = (bf16[256,1536]{1,0:T(8,128)(2,1)S(1)}, bf16[256,1536]{1,0:T(8,128)(2,1)}, u32[]{:S(2)}) copy-start(bf16[256,1536]{1,0:T(8,128)(2,1)} %after.17.refs_2_.refs_1_) | copy-start | bytes 2359300
  76.8 32.0 %collective-permute-start.14 = (bf16[21,96,384]{2,1,0:T(8,128)(2,1)}, bf16[21,96,384]{2,1,0:T(8,128)(2,1)}, u32[]{:S(2)}, u32[]{:S(2)}) collective-permute-start(bf16[21,96,384]{2,1,0:T(8,128)(2,1)} %after.19.refs_3_), channel_id=1, source_target_pairs={{0,16},{8,24},{16,0},{24,8},{1,17},{9,25},{17,1},{25,9},{2,18},{10... | collective-permute-start | bytes 4644872 | tf_op jit(solution)/shard_map/ppermute | solution.py:26
  78.0 35.4 %collective-permute-start.13 = (bf16[21,96,384]{2,1,0:T(8,128)(2,1)}, bf16[21,96,384]{2,1,0:T(8,128)(2,1)S(1)}, u32[]{:S(2)}, u32[]{:S(2)}) collective-permute-start(bf16[21,96,384]{2,1,0:T(8,128)(2,1)} %after.18), channel_id=1, source_target_pairs={{0,8},{8,0},{16,24},{24,16},{1,9},{9,1},{17,25},{25,17},{2,10},{10... | collective-permute-start | bytes 4644872 | tf_op jit(solution)/shard_map/ppermute | solution.py:26
  78.5 40.4 %collective-permute-start.19 = (bf16[4,4,2,96,384]{4,3,2,1,0:T(8,128)(2,1)S(1)}, bf16[4,4,2,96,384]{4,3,2,1,0:T(8,128)(2,1)S(1)}, u32[]{:S(2)}, u32[]{:S(2)}) collective-permute-start(bf16[4,4,2,96,384]{4,3,2,1,0:T(8,128)(2,1)S(1)} %copy-done.1), channel_id=1, source_target_pairs={{0,1},{1,0},{2,3},{3,2},{4,5},{5,4},{6,7},{7,6},{8,9},{9,8},{10,11... | collective-permute-start | bytes 7077896 | tf_op jit(solution)/shard_map/ppermute | solution.py:26
  83.7 8.3 %copy-start.14 = (bf16[21,96,384]{2,1,0:T(8,128)(2,1)S(1)}, bf16[21,96,384]{2,1,0:T(8,128)(2,1)}, u32[]{:S(2)}) copy-start(bf16[21,96,384]{2,1,0:T(8,128)(2,1)} %after.19.refs_3_) | copy-start | bytes 4644868
  91.9 25.6 %copy-start.20 = (f32[4,5,96,384]{3,2,1,0:T(8,128)}, f32[4,5,96,384]{3,2,1,0:T(8,128)S(1)}, u32[]{:S(2)}) copy-start(f32[4,5,96,384]{3,2,1,0:T(8,128)S(1)} %get-tuple-element.11) | copy-start | bytes 8847364
  91.9 2.3 %collective-permute-start.20 = (bf16[2,5,96,384]{3,2,1,0:T(8,128)(2,1)S(1)}, bf16[2,5,96,384]{3,2,1,0:T(8,128)(2,1)S(1)}, u32[]{:S(2)}, u32[]{:S(2)}) collective-permute-start(bf16[2,5,96,384]{3,2,1,0:T(8,128)(2,1)S(1)} %get-tuple-element.12), channel_id=1, source_target_pairs={{0,1},{1,0},{2,3},{3,2},{4,5},{5,4},{6,7},{7,6},{8,9},{9,8},{10,11... | collective-permute-start | bytes 2211848 | tf_op jit(solution)/shard_map/ppermute | solution.py:26
  92.0 25.5 %collective-permute-start.16 = (bf16[21,96,384]{2,1,0:T(8,128)(2,1)S(1)}, bf16[21,96,384]{2,1,0:T(8,128)(2,1)S(1)}, u32[]{:S(2)}, u32[]{:S(2)}) collective-permute-start(bf16[21,96,384]{2,1,0:T(8,128)(2,1)S(1)} %copy-done.14), channel_id=1, source_target_pairs={{0,1},{1,0},{2,3},{3,2},{4,5},{5,4},{6,7},{7,6},{8,9},{9,8},{10,11... | collective-permute-start | bytes 4644872 | tf_op jit(solution)/shard_map/ppermute | solution.py:26
  94.2 23.3 %copy-start.36 = (bf16[2,5,96,384]{3,2,1,0:T(8,128)(2,1)}, bf16[2,5,96,384]{3,2,1,0:T(8,128)(2,1)S(1)}, u32[]{:S(2)}) copy-start(bf16[2,5,96,384]{3,2,1,0:T(8,128)(2,1)S(1)} %collective-permute-done.20) | copy-start | bytes 2211844
  94.2 20.3 %collective-permute-start.21 = (bf16[2,5,96,384]{3,2,1,0:T(8,128)(2,1)S(1)}, bf16[2,5,96,384]{3,2,1,0:T(8,128)(2,1)S(1)}, u32[]{:S(2)}, u32[]{:S(2)}) collective-permute-start(bf16[2,5,96,384]{3,2,1,0:T(8,128)(2,1)S(1)} %get-tuple-element.13), channel_id=1, source_target_pairs={{0,1},{1,0},{2,3},{3,2},{4,5},{5,4},{6,7},{7,6},{8,9},{9,8},{10,11... | collective-permute-start | bytes 2211848 | tf_op jit(solution)/shard_map/ppermute | solution.py:26
  108.8 11.0 %collective-permute-start.18 = (bf16[21,96,384]{2,1,0:T(8,128)(2,1)}, bf16[21,96,384]{2,1,0:T(8,128)(2,1)S(1)}, u32[]{:S(2)}, u32[]{:S(2)}) collective-permute-start(bf16[21,96,384]{2,1,0:T(8,128)(2,1)} %collective-permute-done.14.refs_2_.refs_7_), channel_id=1, source_target_pairs={{0,1},{1,0},{2,3},{3,2},{4,5},{5,4},{6,7},{7,6},{8,9},{9,8},{10,11... | collective-permute-start | bytes 4644872 | tf_op jit(solution)/shard_map/ppermute | solution.py:26
  113.4 4.4 %copy-start.31 = (bf16[21,96,384]{2,1,0:T(8,128)(2,1)}, bf16[21,96,384]{2,1,0:T(8,128)(2,1)S(1)}, u32[]{:S(2)}) copy-start(bf16[21,96,384]{2,1,0:T(8,128)(2,1)S(1)} %collective-permute-done.13.refs_1_.refs_5_) | copy-start | bytes 4644868
  113.4 6.4 %collective-permute-start.17 = (bf16[21,96,384]{2,1,0:T(8,128)(2,1)S(1)}, bf16[21,96,384]{2,1,0:T(8,128)(2,1)S(1)}, u32[]{:S(2)}, u32[]{:S(2)}) collective-permute-start(bf16[21,96,384]{2,1,0:T(8,128)(2,1)S(1)} %collective-permute-done.13.refs_1_.refs_5_), channel_id=1, source_target_pairs={{0,1},{1,0},{2,3},{3,2},{4,5},{5,4},{6,7},{7,6},{8,9},{9,8},{10,11... | collective-permute-start | bytes 4644872 | tf_op jit(solution)/shard_map/ppermute | solution.py:26
  114.5 5.3 %copy-start.37 = (bf16[2,5,96,384]{3,2,1,0:T(8,128)(2,1)}, bf16[2,5,96,384]{3,2,1,0:T(8,128)(2,1)S(1)}, u32[]{:S(2)}) copy-start(bf16[2,5,96,384]{3,2,1,0:T(8,128)(2,1)S(1)} %collective-permute-done.21) | copy-start | bytes 2211844
  115.7 20.9 %collective-permute-start.22 = (bf16[2,5,96,384]{3,2,1,0:T(8,128)(2,1)}, bf16[2,5,96,384]{3,2,1,0:T(8,128)(2,1)S(1)}, u32[]{:S(2)}, u32[]{:S(2)}) collective-permute-start(bf16[2,5,96,384]{3,2,1,0:T(8,128)(2,1)} %pad_maximum_fusion), channel_id=1, source_target_pairs={{0,2},{1,3},{2,0},{3,1},{4,6},{5,7},{6,4},{7,5},{8,10},{9,11},{10,... | collective-permute-start | bytes 2211848 | tf_op jit(solution)/shard_map/ppermute | solution.py:26
  117.5 2.3 %copy-start.33 = (bf16[21,96,384]{2,1,0:T(8,128)(2,1)}, bf16[21,96,384]{2,1,0:T(8,128)(2,1)S(1)}, u32[]{:S(2)}) copy-start(bf16[21,96,384]{2,1,0:T(8,128)(2,1)S(1)} %collective-permute-done.16.refs_4_) | copy-start | bytes 4644868
  117.5 19.1 %collective-permute-start.23 = (bf16[9,96,384]{2,1,0:T(8,128)(2,1)S(1)}, bf16[9,96,384]{2,1,0:T(8,128)(2,1)}, u32[]{:S(2)}, u32[]{:S(2)}) collective-permute-start(bf16[9,96,384]{2,1,0:T(8,128)(2,1)S(1)} %slice.85), channel_id=1, source_target_pairs={{0,8},{8,0},{16,24},{24,16},{1,9},{9,1},{17,25},{25,17},{2,10},{10... | collective-permute-start | bytes 1990664 | tf_op jit(solution)/shard_map/ppermute | solution.py:26
  118.9 3.2 %copy-start.30 = (bf16[4,4,2,96,384]{4,3,2,1,0:T(8,128)(2,1)}, bf16[4,4,2,96,384]{4,3,2,1,0:T(8,128)(2,1)S(1)}, u32[]{:S(2)}) copy-start(bf16[4,4,2,96,384]{4,3,2,1,0:T(8,128)(2,1)S(1)} %collective-permute-done.19.refs_12_.refs_13_.refs_14_.refs_6_) | copy-start | bytes 7077892
  118.9 19.5 %collective-permute-start.15 = (bf16[9,96,384]{2,1,0:T(8,128)(2,1)}, bf16[9,96,384]{2,1,0:T(8,128)(2,1)}, u32[]{:S(2)}, u32[]{:S(2)}) collective-permute-start(bf16[9,96,384]{2,1,0:T(8,128)(2,1)} %slice.82), channel_id=1, source_target_pairs={{0,16},{8,24},{16,0},{24,8},{1,17},{9,25},{17,1},{25,9},{2,18},{10... | collective-permute-start | bytes 1990664 | tf_op jit(solution)/shard_map/ppermute | solution.py:26
  137.4 1.8 %copy-start.21 = (f32[4,5,96,384]{3,2,1,0:T(8,128)S(1)}, f32[4,5,96,384]{3,2,1,0:T(8,128)}, u32[]{:S(2)}) copy-start(f32[4,5,96,384]{3,2,1,0:T(8,128)} %copy-done.20) | copy-start | bytes 8847364
  137.4 22.3 %collective-permute-start.25 = (bf16[9,96,384]{2,1,0:T(8,128)(2,1)}, bf16[9,96,384]{2,1,0:T(8,128)(2,1)}, u32[]{:S(2)}, u32[]{:S(2)}) collective-permute-start(bf16[9,96,384]{2,1,0:T(8,128)(2,1)} %after.21.refs_4_.refs_9_), channel_id=1, source_target_pairs={{0,1},{1,0},{2,3},{3,2},{4,5},{5,4},{6,7},{7,6},{8,9},{9,8},{10,11... | collective-permute-start | bytes 1990664 | tf_op jit(solution)/shard_map/ppermute | solution.py:26
  138.4 21.4 %collective-permute-start.24 = (bf16[9,96,384]{2,1,0:T(8,128)(2,1)}, bf16[9,96,384]{2,1,0:T(8,128)(2,1)S(1)}, u32[]{:S(2)}, u32[]{:S(2)}) collective-permute-start(bf16[9,96,384]{2,1,0:T(8,128)(2,1)} %after.20.refs_3_.refs_7_), channel_id=1, source_target_pairs={{0,1},{1,0},{2,3},{3,2},{4,5},{5,4},{6,7},{7,6},{8,9},{9,8},{10,11... | collective-permute-start | bytes 1990664 | tf_op jit(solution)/shard_map/ppermute | solution.py:26
  140.5 17.2 %collective-permute-start.26 = (bf16[1,5,96,384]{3,2,1,0:T(8,128)(2,1)S(1)}, bf16[1,5,96,384]{3,2,1,0:T(8,128)(2,1)S(1)}, u32[]{:S(2)}, u32[]{:S(2)}) collective-permute-start(bf16[1,5,96,384]{3,2,1,0:T(8,128)(2,1)S(1)} %add_convert_fusion), channel_id=1, source_target_pairs={{0,6},{1,7},{2,4},{3,5},{4,2},{5,3},{6,0},{7,1},{8,14},{9,15},{10,... | collective-permute-start | bytes 1105928 | tf_op jit(solution)/shard_map/ppermute | solution.py:26
  (24 other events, 25.6 us)

commit v21 on v20

--- a/solution.py
+++ b/solution.py
@@ -45,7 +45,8 @@
     for mask, keep in reversed(list(zip(masks, held))):
         leaving = jnp.stack([blocks[d ^ mask].astype(jnp.bfloat16) for d in keep])
         steps.append(from_peer(leaving, axis, mask * unit))
-        blocks = {d: blocks[d] + steps[-1][n].astype(jnp.float32) for n, d in enumerate(keep)}
+        if mask != masks[0]:
+            blocks = {d: blocks[d] + steps[-1][n].astype(jnp.float32) for n, d in enumerate(keep)}
     return blocks[0], steps
 
 
@@ -561,6 +562,7 @@
         rest.append((part, start, plane, planes // 2, 0, 3))
         rest.append((from_peer(part, "rep", 1), start, plane, planes // 2, 1, 3))
     input_grad = stage(windows, pieces=rest, distances=[3], begun=begun)
+    weight_grad = weight_grad + after(steps[-1], input_grad)[0].astype(jnp.float32)
     return (input_grad, weight_grad)
 
 

time: 174 us -> 162 us (0.931)
  waiting for transfers between devices: 46.8 us -> 34.2 us
    ppermute x27, waiting for transfers between devices: 46.8 us -> 34.2 us  [from_peer(): return lax.ppermute(value, axis, [(i, i ^ distance) for i in range(peers)])]
    unnamed x90 -> x92, local copies, waits for them, and re-layouts: 21.4 us -> 22.1 us
  transfers between devices with their start and end apart: 27 -> 27, of which waited for: 5 -> 6; matrix products, arithmetic and copies ran while one was open for 12% -> 11% of each run, Pallas kernels for 25% -> 34%
where the time goes in v21:
time: 162 us; the launch traced here: 161 us
  Pallas kernels  55.1 us (34%)
  waiting for transfers between devices  34.2 us (21%)
  local copies, waits for them, and re-layouts  32.5 us (20%)
  starting transfers between devices  26.9 us (17%)
  other arithmetic  10.9 us (7%)
    ppermute x27, waiting for transfers between devices, from_peer(): return lax.ppermute(value, axis, [(i, i ^ distance) for i in range(peers)])  34.2 us
    ppermute x27, starting transfers between devices, from_peer(): return lax.ppermute(value, axis, [(i, i ^ distance) for i in range(peers)])  26.9 us
    pallas_call x2, Pallas kernels, gradient_stage(): pl.pallas_call(body, out_shape=out_shape, grid_spec=pltpu.PrefetchScalarG...  26.2 us
    unnamed x92, local copies, waits for them, and re-layouts  22.1 us
    pallas_call x1, Pallas kernels, early_terms(): pl.pallas_call(kernel, out_shape=jax.ShapeDtypeStruct((both, columns), jn...  13.8 us
    pallas_call x1, Pallas kernels, late_terms(): pl.pallas_call(kernel, out_shape=(jax.ShapeDtypeStruct(shape, jnp.float32...  8.19 us
    concatenate x1, other arithmetic, on_device_square(): shifts = jnp.concatenate([later, trunk, earlier], axis=1)  5.4 us
    slice x2, local copies, waits for them, and re-layouts, on_device_square(): top, bottom = (after(beside[:half], *ready), after(below[half:], *ready))  4.18 us
  transfers between devices with their start and end apart: 27, of which 6 were waited for; matrix products, arithmetic and copies ran while one was open for 11% of the time, Pallas kernels for 34%

profile of v21, /device:TPU:9, one launch (start us, length us, event | category | flops | bytes accessed | tf_op | source)
XLA Modules:
  0.0 160.6 jit_solution(2568795312953848515)
XLA Ops:
  0.6 1.0 slice.60.refs_0_
  1.6 1.4 collective-permute-start.1
  3.0 0.9 slice_bitcast_fusion.2
  3.9 1.3 collective-permute-start.3
  5.2 1.2 collective-permute-start.4
  6.6 2.2 %collective-permute-start = (bf16[3,96,384]{2,1,0:T(8,128)(2,1)S(1)}, bf16[3,96,384]{2,1,0:T(8,128)(2,1)S(1)}, u32[]{:S(2)}, u32[]{:S(2)}) collective-permute-start(bf16[3,96,384]{2,1,0:T(8,128)(2,1)S(1)} %slice.60.refs_0_), channel_id=1, source_target_pairs={{0,2},{1,3},{2,0},{3,1},{4,6},{5,7},{6,4},{7,5},{8,10},{9,11},{10,... | collective-permute-start | bytes 663560 | tf_op jit(solution)/shard_map/ppermute | solution.py:26
  8.8 1.4 copy-done.11
  10.2 1.8 %act.1.refs_0_ = bf16[512,1536]{1,0:T(8,128)(2,1)S(1)} custom-call(bf16[1,1024,768]{2,1,0:T(8,128)(2,1)S(1)} %copy-done.11), custom_call_target="tpu_custom_call" | custom-call | flops 1048576 | bytes 65536 | tf_op jit(solution)/shard_map/act/pallas_call | solution.py:85
  12.0 1.1 copy-done.4
  14.5 1.2 collective-permute-start.10
  15.7 1.2 collective-permute-start.6
  17.0 2.1 %slice_bitcast_fusion.1 = (bf16[2047,384]{1,0:T(8,128)(2,1)}, bf16[2047,384]{1,0:T(8,128)(2,1)}) fusion(bf16[1,2048,384]{2,1,0:T(8,128)(2,1)S(1)} %copy-done.3), kind=kLoop, calls=%fused_computation.7 | loop fusion | bytes 6288384 | tf_op jit(solution)/shard_map/slice | solution.py:504
  20.0 2.1 %collective-permute-done.2.refs_2_.refs_3_ = bf16[3,96,384]{2,1,0:T(8,128)(2,1)S(1)} collective-permute-done((bf16[3,96,384]{2,1,0:T(8,128)(2,1)S(1)}, bf16[3,96,384]{2,1,0:T(8,128)(2,1)S(1)}, u32[]{:S(2)}, u32[]{:S(2)}) %collective-permute-start.2) | collective-permute-done | bytes 221216 | tf_op jit(solution)/shard_map/ppermute | solution.py:26
  23.2 5.4 %fusion.2.refs_2_.shifts_ref = bf16[2048,1152]{1,0:T(8,128)(2,1)} fusion(bf16[2047,384]{1,0:T(8,128)(2,1)} %get-tuple-element.17, bf16[2047,384]{1,0:T(8,128)(2,1)} %get-tuple-element.16, bf16[2048,384]{1,0:T(8,128)(2,1)S(1)} %bitcast.14), kind=kLoop, calls=%fused_computation.4 | loop fusion | flops 23592960 | bytes 9435648 | tf_op jit(solution)/shard_map/concatenate | solution.py:506
  28.6 2.3 %half_slope.1.refs_1_.refs_11_ = f32[2,512,768]{2,1,0:T(8,128)S(1)} custom-call(bf16[1,1024,768]{2,1,0:T(8,128)(2,1)S(1)} %copy-done.12), custom_call_target="tpu_custom_call" | custom-call | tf_op jit(solution)/shard_map/half_slope/pallas_call | solution.py:167
  30.9 1.6 %copy-done.2 = f32[2,512,768]{2,1,0:T(8,128)} copy-done((f32[2,512,768]{2,1,0:T(8,128)}, f32[2,512,768]{2,1,0:T(8,128)S(1)}, u32[]{:S(2)}) %copy-start.2) | copy-done | bytes 3145752
  32.6 0.9 copy-done.28
  33.6 1.0 kernel_messages.1
  34.6 1.1 copy-done.6
  35.7 1.2 copy-done.13
  36.9 11.7 %collective-permute-done.10.refs_2_ = bf16[512,1536]{1,0:T(8,128)(2,1)} collective-permute-done((bf16[512,1536]{1,0:T(8,128)(2,1)}, bf16[512,1536]{1,0:T(8,128)(2,1)}, u32[]{:S(2)}, u32[]{:S(2)}) %collective-permute-start.10) | collective-permute-done | bytes 1572896 | tf_op jit(solution)/shard_map/ppermute | solution.py:26
  48.6 2.1 %slice.81.refs_0_ = bf16[256,1536]{1,0:T(8,128)(2,1)} slice(bf16[512,1536]{1,0:T(8,128)(2,1)} %collective-permute-done.10.refs_2_), slice={[256:512], [0:1536]} | slice | bytes 1572864 | tf_op jit(solution)/shard_map/slice | solution.py:509
  51.8 1.2 collective-permute-start.12
  53.0 2.1 %slice.80.refs_0_ = bf16[256,1536]{1,0:T(8,128)(2,1)} slice(bf16[512,1536]{1,0:T(8,128)(2,1)} %collective-permute-done.6.refs_1_), slice={[0:256], [0:1536]} | slice | bytes 1572864 | tf_op jit(solution)/shard_map/slice | solution.py:509
  55.1 1.2 collective-permute-start.9
  56.5 13.8 %weight_grad_early.1.refs_1_.early_ref = f32[1536,1152]{1,0:T(8,128)} custom-call(s32[2]{0:T(128)S(1)} %pad_add_fusion.place, bf16[2048,1152]{1,0:T(8,128)(2,1)} %fusion.2.refs_2_.shifts_ref, bf16[512,1536]{1,0:T(8,128)(2,1)S(1)} %copy-done.5, bf16[512,1536]{1,0:T(8,128)(2,1)} %collective-permute-done.6.refs_1_, ...), custom_call_target="tpu_custom_call" | custom-call | flops 1048576 | bytes 65536 | tf_op jit(solution)/shard_map/weight_grad_early/pallas_call | solution.py:213
  70.4 1.0 copy-done.15
  71.8 1.8 %stack_planes.1.refs_2_.refs_9_.refs_10_.refs_11_.refs_5_ = bf16[4,4,2,96,384]{4,3,2,1,0:T(8,128)(2,1)S(1)} custom-call(s32[2]{0:T(128)S(1)} %pad_add_fusion.place, bf16[4,2,96,384]{3,2,1,0:T(8,128)(2,1)S(1)} %copy-done.15, bf16[4,2,96,384]{3,2,1,0:T(8,128)(2,1)S(1)} %copy-done.19, bf16[4,2,96,384]{3,2,1,0:T(8,128)(2,1)} %after.15.refs_2_, ...), custom_call_target="tpu_custom_call" | custom-call | flops 1048576 | bytes 65536 | tf_op jit(solution)/shard_map/stack_planes/pallas_call | solution.py:470
  73.6 1.4 copy-done
  76.8 1.2 collective-permute-start.14
  78.5 4.1 %collective-permute-start.19 = (bf16[4,4,2,96,384]{4,3,2,1,0:T(8,128)(2,1)S(1)}, bf16[4,4,2,96,384]{4,3,2,1,0:T(8,128)(2,1)S(1)}, u32[]{:S(2)}, u32[]{:S(2)}) collective-permute-start(bf16[4,4,2,96,384]{4,3,2,1,0:T(8,128)(2,1)S(1)} %copy-done.1), channel_id=1, source_target_pairs={{0,1},{1,0},{2,3},{3,2},{4,5},{5,4},{6,7},{7,6},{8,9},{9,8},{10,11... | collective-permute-start | bytes 7077896 | tf_op jit(solution)/shard_map/ppermute | solution.py:26
  82.6 1.1 copy-done.10
  83.7 8.2 %weight_grad_late.1 = (f32[4,5,96,384]{3,2,1,0:T(8,128)S(1)}, bf16[2,5,96,384]{3,2,1,0:T(8,128)(2,1)S(1)}, bf16[2,5,96,384]{3,2,1,0:T(8,128)(2,1)S(1)}) custom-call(s32[2]{0:T(128)S(1)} %pad_add_fusion.place, bf16[2048,1152]{1,0:T(8,128)(2,1)} %fusion.2.refs_2_.shifts_ref, f32[1536,1152]{1,0:T(8,128)} %weight_grad_early.1.refs_1_.early_ref, ...), custom_call_target="tpu_custom_call" | custom-call | flops 1048576 | bytes 65536 | tf_op jit(solution)/shard_map/weight_grad_late/pallas_call | solution.py:288
  92.5 1.7 %collective-permute-done.20 = bf16[2,5,96,384]{3,2,1,0:T(8,128)(2,1)S(1)} collective-permute-done((bf16[2,5,96,384]{3,2,1,0:T(8,128)(2,1)S(1)}, bf16[2,5,96,384]{3,2,1,0:T(8,128)(2,1)S(1)}, u32[]{:S(2)}, u32[]{:S(2)}) %collective-permute-start.20) | collective-permute-done | bytes 737312 | tf_op jit(solution)/shard_map/ppermute | solution.py:26
  94.4 14.4 %collective-permute-done.14.refs_2_.refs_7_ = bf16[21,96,384]{2,1,0:T(8,128)(2,1)} collective-permute-done((bf16[21,96,384]{2,1,0:T(8,128)(2,1)}, bf16[21,96,384]{2,1,0:T(8,128)(2,1)}, u32[]{:S(2)}, u32[]{:S(2)}) %collective-permute-start.14) | collective-permute-done | bytes 1548320 | tf_op jit(solution)/shard_map/ppermute | solution.py:26
  108.8 4.6 %collective-permute-start.18 = (bf16[21,96,384]{2,1,0:T(8,128)(2,1)}, bf16[21,96,384]{2,1,0:T(8,128)(2,1)S(1)}, u32[]{:S(2)}, u32[]{:S(2)}) collective-permute-start(bf16[21,96,384]{2,1,0:T(8,128)(2,1)} %collective-permute-done.14.refs_2_.refs_7_), channel_id=1, source_target_pairs={{0,1},{1,0},{2,3},{3,2},{4,5},{5,4},{6,7},{7,6},{8,9},{9,8},{10,11... | collective-permute-start | bytes 4644872 | tf_op jit(solution)/shard_map/ppermute | solution.py:26
  113.4 1.1 collective-permute-start.17
  114.7 0.9 pad_maximum_fusion
  116.3 1.2 slice.85
  117.8 1.1 slice.82
  119.9 1.1 copy-done.34
  121.0 1.1 copy-done.35
  122.1 14.4 %input_grad.2.refs_1_.refs_12_ = f32[2,512,768]{2,1,0:T(8,128)} custom-call(s32[2]{0:T(128)} %copy-done.29, bf16[6,96,384]{2,1,0:T(8,128)(2,1)} %copy-done.22, bf16[21,96,384]{2,1,0:T(8,128)(2,1)} %copy-done.31, bf16[21,96,384]{2,1,0:T(8,128)(2,1)} %collective-permute-done.14.refs_2_.refs_7_, bf16[21,96,384]{2,1,0:T(8,128)(2,1)} %after.20.refs_3_, ...), custom_call_target="tpu_custom_call" | custom-call | flops 1048576 | bytes 65536 | tf_op jit(solution)/shard_map/input_grad/pallas_call | solution.py:446
  137.4 1.0 collective-permute-start.25
  139.2 1.2 add_convert_fusion
  142.1 11.8 %input_grad.3.refs_1_ = bf16[1,1024,768]{2,1,0:T(8,128)(2,1)} custom-call(s32[2]{0:T(128)} %copy-done.29, bf16[6,96,384]{2,1,0:T(8,128)(2,1)} %copy-done.22, bf16[21,96,384]{2,1,0:T(8,128)(2,1)} %copy-done.31, bf16[21,96,384]{2,1,0:T(8,128)(2,1)} %collective-permute-done.14.refs_2_.refs_7_, bf16[9,96,384]{2,1,0:T(8,128)(2,1)} %after.21.refs_3_.refs_7_, ...), custom_call_target="tpu_custom_call" | custom-call | flops 1048576 | bytes 65536 | tf_op jit(solution)/shard_map/input_grad/pallas_call | solution.py:446
  153.9 3.7 %collective-permute-done.26.refs_0_ = bf16[1,5,96,384]{3,2,1,0:T(8,128)(2,1)S(1)} collective-permute-done((bf16[1,5,96,384]{3,2,1,0:T(8,128)(2,1)S(1)}, bf16[1,5,96,384]{3,2,1,0:T(8,128)(2,1)S(1)}, u32[]{:S(2)}, u32[]{:S(2)}) %collective-permute-start.26) | collective-permute-done | bytes 368672 | tf_op jit(solution)/shard_map/ppermute | solution.py:26
  158.4 2.2 %add_bitcast_fusion = f32[5,96,384]{2,1,0:T(8,128)} fusion(bf16[1,5,96,384]{3,2,1,0:T(8,128)(2,1)} %after.23, f32[4,5,96,384]{3,2,1,0:T(8,128)S(1)} %copy-done.21, bf16[2,5,96,384]{3,2,1,0:T(8,128)(2,1)} %copy-done.32, bf16[2,5,96,384]{3,2,1,0:T(8,128)(2,1)} %copy-done.37), kind=kLoop, calls=%fused_computation.9 | loop fusion | flops 1105920 | bytes 2580480 | tf_op jit(solution)/shard_map/add | solution.py:565
  (132 shorter events, 14.3 us)
Async XLA Ops:
  1.6 15.4 %collective-permute-start.1 = (bf16[3,96,384]{2,1,0:T(8,128)(2,1)S(1)}, bf16[3,96,384]{2,1,0:T(8,128)(2,1)S(1)}, u32[]{:S(2)}, u32[]{:S(2)}) collective-permute-start(bf16[3,96,384]{2,1,0:T(8,128)(2,1)S(1)} %slice.60.refs_0_), channel_id=1, source_target_pairs={{0,6},{1,7},{2,4},{3,5},{4,2},{5,3},{6,0},{7,1},{8,14},{9,15},{10,... | collective-permute-start | bytes 663560 | tf_op jit(solution)/shard_map/ppermute | solution.py:26
  3.9 9.2 %collective-permute-start.3 = (bf16[2,96,384]{2,1,0:T(8,128)(2,1)S(1)}, bf16[2,96,384]{2,1,0:T(8,128)(2,1)S(1)}, u32[]{:S(2)}, u32[]{:S(2)}) collective-permute-start(bf16[2,96,384]{2,1,0:T(8,128)(2,1)S(1)} %get-tuple-element.19), channel_id=1, source_target_pairs={{0,8},{8,0},{16,24},{24,16},{1,9},{9,1},{17,25},{25,17},{2,10},{10... | collective-permute-start | bytes 442376 | tf_op jit(solution)/shard_map/ppermute | solution.py:26
  5.2 8.0 %collective-permute-start.4 = (bf16[2,96,384]{2,1,0:T(8,128)(2,1)S(1)}, bf16[2,96,384]{2,1,0:T(8,128)(2,1)S(1)}, u32[]{:S(2)}, u32[]{:S(2)}) collective-permute-start(bf16[2,96,384]{2,1,0:T(8,128)(2,1)S(1)} %get-tuple-element.19), channel_id=1, source_target_pairs={{0,16},{8,24},{16,0},{24,8},{1,17},{9,25},{17,1},{25,9},{2,18},{10... | collective-permute-start | bytes 442376 | tf_op jit(solution)/shard_map/ppermute | solution.py:26
  6.4 6.7 %collective-permute-start.5 = (bf16[2,96,384]{2,1,0:T(8,128)(2,1)S(1)}, bf16[2,96,384]{2,1,0:T(8,128)(2,1)S(1)}, u32[]{:S(2)}, u32[]{:S(2)}) collective-permute-start(bf16[2,96,384]{2,1,0:T(8,128)(2,1)S(1)} %get-tuple-element.19), channel_id=1, source_target_pairs={{0,24},{8,16},{16,8},{24,0},{1,25},{9,17},{17,9},{25,1},{2,26},{10... | collective-permute-start | bytes 442376 | tf_op jit(solution)/shard_map/ppermute | solution.py:26
  6.6 13.4 %collective-permute-start = (bf16[3,96,384]{2,1,0:T(8,128)(2,1)S(1)}, bf16[3,96,384]{2,1,0:T(8,128)(2,1)S(1)}, u32[]{:S(2)}, u32[]{:S(2)}) collective-permute-start(bf16[3,96,384]{2,1,0:T(8,128)(2,1)S(1)} %slice.60.refs_0_), channel_id=1, source_target_pairs={{0,2},{1,3},{2,0},{3,1},{4,6},{5,7},{6,4},{7,5},{8,10},{9,11},{10,... | collective-permute-start | bytes 663560 | tf_op jit(solution)/shard_map/ppermute | solution.py:26
  13.1 3.8 %copy-start.3 = (bf16[1,2048,384]{2,1,0:T(8,128)(2,1)S(1)}, bf16[1,2048,384]{2,1,0:T(8,128)(2,1)}, u32[]{:S(2)}) copy-start(bf16[1,2048,384]{2,1,0:T(8,128)(2,1)} %refs_4_.1) | copy-start | bytes 4718596
  14.5 4.6 %copy-start.41 = (bf16[2,96,384]{2,1,0:T(8,128)(2,1)S(1)}, bf16[2,96,384]{2,1,0:T(8,128)(2,1)}, u32[]{:S(2)}) copy-start(bf16[2,96,384]{2,1,0:T(8,128)(2,1)} %copy-done.40) | copy-start | bytes 442372
  14.5 4.6 %copy-start.43 = (bf16[2,96,384]{2,1,0:T(8,128)(2,1)S(1)}, bf16[2,96,384]{2,1,0:T(8,128)(2,1)}, u32[]{:S(2)}) copy-start(bf16[2,96,384]{2,1,0:T(8,128)(2,1)} %copy-done.42) | copy-start | bytes 442372
  14.5 4.6 %copy-start.45 = (bf16[2,96,384]{2,1,0:T(8,128)(2,1)S(1)}, bf16[2,96,384]{2,1,0:T(8,128)(2,1)}, u32[]{:S(2)}) copy-start(bf16[2,96,384]{2,1,0:T(8,128)(2,1)} %copy-done.44) | copy-start | bytes 442372
  14.5 34.1 %collective-permute-start.10 = (bf16[512,1536]{1,0:T(8,128)(2,1)}, bf16[512,1536]{1,0:T(8,128)(2,1)}, u32[]{:S(2)}, u32[]{:S(2)}) collective-permute-start(bf16[512,1536]{1,0:T(8,128)(2,1)} %after.12.refs_1_.refs_0_), channel_id=1, source_target_pairs={{0,16},{8,24},{16,0},{24,8},{1,17},{9,25},{17,1},{25,9},{2,18},{10... | collective-permute-start | bytes 4718600 | tf_op jit(solution)/shard_map/ppermute | solution.py:26
  15.7 37.3 %collective-permute-start.6 = (bf16[512,1536]{1,0:T(8,128)(2,1)}, bf16[512,1536]{1,0:T(8,128)(2,1)}, u32[]{:S(2)}, u32[]{:S(2)}) collective-permute-start(bf16[512,1536]{1,0:T(8,128)(2,1)} %after.12.refs_1_.refs_0_), channel_id=1, source_target_pairs={{0,8},{8,0},{16,24},{24,16},{1,9},{9,1},{17,25},{25,17},{2,10},{10... | collective-permute-start | bytes 4718600 | tf_op jit(solution)/shard_map/ppermute | solution.py:26
  16.9 2.1 %copy-start.23 = (bf16[3,96,384]{2,1,0:T(8,128)(2,1)}, bf16[3,96,384]{2,1,0:T(8,128)(2,1)S(1)}, u32[]{:S(2)}) copy-start(bf16[3,96,384]{2,1,0:T(8,128)(2,1)S(1)} %collective-permute-done.1.refs_3_.refs_4_) | copy-start | bytes 663556
  17.0 5.2 %collective-permute-start.2 = (bf16[3,96,384]{2,1,0:T(8,128)(2,1)S(1)}, bf16[3,96,384]{2,1,0:T(8,128)(2,1)S(1)}, u32[]{:S(2)}, u32[]{:S(2)}) collective-permute-start(bf16[3,96,384]{2,1,0:T(8,128)(2,1)S(1)} %collective-permute-done.1.refs_3_.refs_4_), channel_id=1, source_target_pairs={{0,2},{1,3},{2,0},{3,1},{4,6},{5,7},{6,4},{7,5},{8,10},{9,11},{10,... | collective-permute-start | bytes 663560 | tf_op jit(solution)/shard_map/ppermute | solution.py:26
  20.0 2.1 %copy-start.25 = (bf16[3,96,384]{2,1,0:T(8,128)(2,1)}, bf16[3,96,384]{2,1,0:T(8,128)(2,1)S(1)}, u32[]{:S(2)}) copy-start(bf16[3,96,384]{2,1,0:T(8,128)(2,1)S(1)} %collective-permute-done.refs_1_.refs_2_) | copy-start | bytes 663556
  22.8 27.9 %collective-permute-start.8 = (bf16[4,2,96,384]{3,2,1,0:T(8,128)(2,1)}, bf16[4,2,96,384]{3,2,1,0:T(8,128)(2,1)S(1)}, u32[]{:S(2)}, u32[]{:S(2)}) collective-permute-start(bf16[4,2,96,384]{3,2,1,0:T(8,128)(2,1)} %after.13.refs_0_), channel_id=1, source_target_pairs={{0,6},{1,7},{2,4},{3,5},{4,2},{5,3},{6,0},{7,1},{8,14},{9,15},{10,... | collective-permute-start | bytes 1769480 | tf_op jit(solution)/shard_map/ppermute | solution.py:26
  22.8 27.9 %collective-permute-start.7 = (bf16[4,2,96,384]{3,2,1,0:T(8,128)(2,1)}, bf16[4,2,96,384]{3,2,1,0:T(8,128)(2,1)S(1)}, u32[]{:S(2)}, u32[]{:S(2)}) collective-permute-start(bf16[4,2,96,384]{3,2,1,0:T(8,128)(2,1)} %after.13.refs_0_), channel_id=1, source_target_pairs={{0,2},{1,3},{2,0},{3,1},{4,6},{5,7},{6,4},{7,5},{8,10},{9,11},{10,... | collective-permute-start | bytes 1769480 | tf_op jit(solution)/shard_map/ppermute | solution.py:26
  23.2 5.4 %copy-start.12 = (bf16[1,1024,768]{2,1,0:T(8,128)(2,1)S(1)}, bf16[1,1024,768]{2,1,0:T(8,128)(2,1)}, u32[]{:S(2)}) copy-start(bf16[1,1024,768]{2,1,0:T(8,128)(2,1)} %x_ref.3) | copy-start | bytes 4718596
  28.6 4.1 %copy-start.24 = (bf16[3,96,384]{2,1,0:T(8,128)(2,1)S(1)}, bf16[3,96,384]{2,1,0:T(8,128)(2,1)}, u32[]{:S(2)}) copy-start(bf16[3,96,384]{2,1,0:T(8,128)(2,1)} %copy-done.23) | copy-start | bytes 663556
  28.6 4.1 %copy-start.26 = (bf16[3,96,384]{2,1,0:T(8,128)(2,1)S(1)}, bf16[3,96,384]{2,1,0:T(8,128)(2,1)}, u32[]{:S(2)}) copy-start(bf16[3,96,384]{2,1,0:T(8,128)(2,1)} %copy-done.25) | copy-start | bytes 663556
  33.6 49.0 %copy-start.29 = (s32[2]{0:T(128)}, s32[2]{0:T(128)S(1)}, u32[]{:S(2)}) copy-start(s32[2]{0:T(128)S(1)} %pad_add_fusion.place) | copy-start | bytes 28
  36.9 13.8 %copy-start.22 = (bf16[6,96,384]{2,1,0:T(8,128)(2,1)}, bf16[6,96,384]{2,1,0:T(8,128)(2,1)S(1)}, u32[]{:S(2)}) copy-start(bf16[6,96,384]{2,1,0:T(8,128)(2,1)S(1)} %get-tuple-element.8.refs_0_) | copy-start | bytes 1327108
  51.8 23.2 %collective-permute-start.12 = (bf16[256,1536]{1,0:T(8,128)(2,1)}, bf16[256,1536]{1,0:T(8,128)(2,1)S(1)}, u32[]{:S(2)}, u32[]{:S(2)}) collective-permute-start(bf16[256,1536]{1,0:T(8,128)(2,1)} %after.17), channel_id=1, source_target_pairs={{0,8},{8,0},{16,24},{24,16},{1,9},{9,1},{17,25},{25,17},{2,10},{10... | collective-permute-start | bytes 2359304 | tf_op jit(solution)/shard_map/ppermute | solution.py:26
  55.1 20.8 %collective-permute-start.9 = (bf16[256,1536]{1,0:T(8,128)(2,1)}, bf16[256,1536]{1,0:T(8,128)(2,1)S(1)}, u32[]{:S(2)}, u32[]{:S(2)}) collective-permute-start(bf16[256,1536]{1,0:T(8,128)(2,1)} %after.14), channel_id=1, source_target_pairs={{0,16},{8,24},{16,0},{24,8},{1,17},{9,25},{17,1},{25,9},{2,18},{10... | collective-permute-start | bytes 2359304 | tf_op jit(solution)/shard_map/ppermute | solution.py:26
  56.4 14.0 %collective-permute-start.11 = (bf16[4,2,96,384]{3,2,1,0:T(8,128)(2,1)}, bf16[4,2,96,384]{3,2,1,0:T(8,128)(2,1)}, u32[]{:S(2)}, u32[]{:S(2)}) collective-permute-start(bf16[4,2,96,384]{3,2,1,0:T(8,128)(2,1)} %copy-done.16), channel_id=1, source_target_pairs={{0,2},{1,3},{2,0},{3,1},{4,6},{5,7},{6,4},{7,5},{8,10},{9,11},{10,... | collective-permute-start | bytes 1769480 | tf_op jit(solution)/shard_map/ppermute | solution.py:26
  76.8 1.7 %copy-start.1 = (bf16[4,4,2,96,384]{4,3,2,1,0:T(8,128)(2,1)S(1)}, bf16[4,4,2,96,384]{4,3,2,1,0:T(8,128)(2,1)}, u32[]{:S(2)}) copy-start(bf16[4,4,2,96,384]{4,3,2,1,0:T(8,128)(2,1)} %copy-done) | copy-start | bytes 7077892
  76.8 5.8 %copy-start.8 = (bf16[256,1536]{1,0:T(8,128)(2,1)S(1)}, bf16[256,1536]{1,0:T(8,128)(2,1)}, u32[]{:S(2)}) copy-start(bf16[256,1536]{1,0:T(8,128)(2,1)} %after.18.refs_2_.refs_1_) | copy-start | bytes 2359300
  76.8 32.0 %collective-permute-start.14 = (bf16[21,96,384]{2,1,0:T(8,128)(2,1)}, bf16[21,96,384]{2,1,0:T(8,128)(2,1)}, u32[]{:S(2)}, u32[]{:S(2)}) collective-permute-start(bf16[21,96,384]{2,1,0:T(8,128)(2,1)} %after.20.refs_3_), channel_id=1, source_target_pairs={{0,16},{8,24},{16,0},{24,8},{1,17},{9,25},{17,1},{25,9},{2,18},{10... | collective-permute-start | bytes 4644872 | tf_op jit(solution)/shard_map/ppermute | solution.py:26
  78.1 35.4 %collective-permute-start.13 = (bf16[21,96,384]{2,1,0:T(8,128)(2,1)}, bf16[21,96,384]{2,1,0:T(8,128)(2,1)S(1)}, u32[]{:S(2)}, u32[]{:S(2)}) collective-permute-start(bf16[21,96,384]{2,1,0:T(8,128)(2,1)} %after.19), channel_id=1, source_target_pairs={{0,8},{8,0},{16,24},{24,16},{1,9},{9,1},{17,25},{25,17},{2,10},{10... | collective-permute-start | bytes 4644872 | tf_op jit(solution)/shard_map/ppermute | solution.py:26
  78.5 40.4 %collective-permute-start.19 = (bf16[4,4,2,96,384]{4,3,2,1,0:T(8,128)(2,1)S(1)}, bf16[4,4,2,96,384]{4,3,2,1,0:T(8,128)(2,1)S(1)}, u32[]{:S(2)}, u32[]{:S(2)}) collective-permute-start(bf16[4,4,2,96,384]{4,3,2,1,0:T(8,128)(2,1)S(1)} %copy-done.1), channel_id=1, source_target_pairs={{0,1},{1,0},{2,3},{3,2},{4,5},{5,4},{6,7},{7,6},{8,9},{9,8},{10,11... | collective-permute-start | bytes 7077896 | tf_op jit(solution)/shard_map/ppermute | solution.py:26
  83.7 8.3 %copy-start.14 = (bf16[21,96,384]{2,1,0:T(8,128)(2,1)S(1)}, bf16[21,96,384]{2,1,0:T(8,128)(2,1)}, u32[]{:S(2)}) copy-start(bf16[21,96,384]{2,1,0:T(8,128)(2,1)} %after.20.refs_3_) | copy-start | bytes 4644868
  91.9 25.5 %copy-start.20 = (f32[4,5,96,384]{3,2,1,0:T(8,128)}, f32[4,5,96,384]{3,2,1,0:T(8,128)S(1)}, u32[]{:S(2)}) copy-start(f32[4,5,96,384]{3,2,1,0:T(8,128)S(1)} %get-tuple-element.11) | copy-start | bytes 8847364
  91.9 2.3 %collective-permute-start.20 = (bf16[2,5,96,384]{3,2,1,0:T(8,128)(2,1)S(1)}, bf16[2,5,96,384]{3,2,1,0:T(8,128)(2,1)S(1)}, u32[]{:S(2)}, u32[]{:S(2)}) collective-permute-start(bf16[2,5,96,384]{3,2,1,0:T(8,128)(2,1)S(1)} %get-tuple-element.12), channel_id=1, source_target_pairs={{0,1},{1,0},{2,3},{3,2},{4,5},{5,4},{6,7},{7,6},{8,9},{9,8},{10,11... | collective-permute-start | bytes 2211848 | tf_op jit(solution)/shard_map/ppermute | solution.py:26
  92.0 25.4 %collective-permute-start.16 = (bf16[21,96,384]{2,1,0:T(8,128)(2,1)S(1)}, bf16[21,96,384]{2,1,0:T(8,128)(2,1)S(1)}, u32[]{:S(2)}, u32[]{:S(2)}) collective-permute-start(bf16[21,96,384]{2,1,0:T(8,128)(2,1)S(1)} %copy-done.14), channel_id=1, source_target_pairs={{0,1},{1,0},{2,3},{3,2},{4,5},{5,4},{6,7},{7,6},{8,9},{9,8},{10,11... | collective-permute-start | bytes 4644872 | tf_op jit(solution)/shard_map/ppermute | solution.py:26
  94.2 23.2 %copy-start.37 = (bf16[2,5,96,384]{3,2,1,0:T(8,128)(2,1)}, bf16[2,5,96,384]{3,2,1,0:T(8,128)(2,1)S(1)}, u32[]{:S(2)}) copy-start(bf16[2,5,96,384]{3,2,1,0:T(8,128)(2,1)S(1)} %collective-permute-done.20) | copy-start | bytes 2211844
  94.2 20.3 %collective-permute-start.21 = (bf16[2,5,96,384]{3,2,1,0:T(8,128)(2,1)S(1)}, bf16[2,5,96,384]{3,2,1,0:T(8,128)(2,1)S(1)}, u32[]{:S(2)}, u32[]{:S(2)}) collective-permute-start(bf16[2,5,96,384]{3,2,1,0:T(8,128)(2,1)S(1)} %get-tuple-element.13), channel_id=1, source_target_pairs={{0,1},{1,0},{2,3},{3,2},{4,5},{5,4},{6,7},{7,6},{8,9},{9,8},{10,11... | collective-permute-start | bytes 2211848 | tf_op jit(solution)/shard_map/ppermute | solution.py:26
  108.8 11.0 %collective-permute-start.18 = (bf16[21,96,384]{2,1,0:T(8,128)(2,1)}, bf16[21,96,384]{2,1,0:T(8,128)(2,1)S(1)}, u32[]{:S(2)}, u32[]{:S(2)}) collective-permute-start(bf16[21,96,384]{2,1,0:T(8,128)(2,1)} %collective-permute-done.14.refs_2_.refs_7_), channel_id=1, source_target_pairs={{0,1},{1,0},{2,3},{3,2},{4,5},{5,4},{6,7},{7,6},{8,9},{9,8},{10,11... | collective-permute-start | bytes 4644872 | tf_op jit(solution)/shard_map/ppermute | solution.py:26
  113.4 4.4 %copy-start.31 = (bf16[21,96,384]{2,1,0:T(8,128)(2,1)}, bf16[21,96,384]{2,1,0:T(8,128)(2,1)S(1)}, u32[]{:S(2)}) copy-start(bf16[21,96,384]{2,1,0:T(8,128)(2,1)S(1)} %collective-permute-done.13.refs_1_.refs_5_) | copy-start | bytes 4644868
  113.4 6.4 %collective-permute-start.17 = (bf16[21,96,384]{2,1,0:T(8,128)(2,1)S(1)}, bf16[21,96,384]{2,1,0:T(8,128)(2,1)S(1)}, u32[]{:S(2)}, u32[]{:S(2)}) collective-permute-start(bf16[21,96,384]{2,1,0:T(8,128)(2,1)S(1)} %collective-permute-done.13.refs_1_.refs_5_), channel_id=1, source_target_pairs={{0,1},{1,0},{2,3},{3,2},{4,5},{5,4},{6,7},{7,6},{8,9},{9,8},{10,11... | collective-permute-start | bytes 4644872 | tf_op jit(solution)/shard_map/ppermute | solution.py:26
  114.6 5.3 %copy-start.38 = (bf16[2,5,96,384]{3,2,1,0:T(8,128)(2,1)}, bf16[2,5,96,384]{3,2,1,0:T(8,128)(2,1)S(1)}, u32[]{:S(2)}) copy-start(bf16[2,5,96,384]{3,2,1,0:T(8,128)(2,1)S(1)} %collective-permute-done.21) | copy-start | bytes 2211844
  115.7 20.9 %collective-permute-start.22 = (bf16[2,5,96,384]{3,2,1,0:T(8,128)(2,1)}, bf16[2,5,96,384]{3,2,1,0:T(8,128)(2,1)S(1)}, u32[]{:S(2)}, u32[]{:S(2)}) collective-permute-start(bf16[2,5,96,384]{3,2,1,0:T(8,128)(2,1)} %pad_maximum_fusion), channel_id=1, source_target_pairs={{0,2},{1,3},{2,0},{3,1},{4,6},{5,7},{6,4},{7,5},{8,10},{9,11},{10,... | collective-permute-start | bytes 2211848 | tf_op jit(solution)/shard_map/ppermute | solution.py:26
  117.5 2.4 %copy-start.33 = (bf16[21,96,384]{2,1,0:T(8,128)(2,1)}, bf16[21,96,384]{2,1,0:T(8,128)(2,1)S(1)}, u32[]{:S(2)}) copy-start(bf16[21,96,384]{2,1,0:T(8,128)(2,1)S(1)} %collective-permute-done.16.refs_4_) | copy-start | bytes 4644868
  117.5 19.1 %collective-permute-start.23 = (bf16[9,96,384]{2,1,0:T(8,128)(2,1)S(1)}, bf16[9,96,384]{2,1,0:T(8,128)(2,1)}, u32[]{:S(2)}, u32[]{:S(2)}) collective-permute-start(bf16[9,96,384]{2,1,0:T(8,128)(2,1)S(1)} %slice.85), channel_id=1, source_target_pairs={{0,8},{8,0},{16,24},{24,16},{1,9},{9,1},{17,25},{25,17},{2,10},{10... | collective-permute-start | bytes 1990664 | tf_op jit(solution)/shard_map/ppermute | solution.py:26
  118.9 3.2 %copy-start.30 = (bf16[4,4,2,96,384]{4,3,2,1,0:T(8,128)(2,1)}, bf16[4,4,2,96,384]{4,3,2,1,0:T(8,128)(2,1)S(1)}, u32[]{:S(2)}) copy-start(bf16[4,4,2,96,384]{4,3,2,1,0:T(8,128)(2,1)S(1)} %collective-permute-done.19.refs_12_.refs_13_.refs_14_.refs_6_) | copy-start | bytes 7077892
  118.9 19.5 %collective-permute-start.15 = (bf16[9,96,384]{2,1,0:T(8,128)(2,1)}, bf16[9,96,384]{2,1,0:T(8,128)(2,1)}, u32[]{:S(2)}, u32[]{:S(2)}) collective-permute-start(bf16[9,96,384]{2,1,0:T(8,128)(2,1)} %slice.82), channel_id=1, source_target_pairs={{0,16},{8,24},{16,0},{24,8},{1,17},{9,25},{17,1},{25,9},{2,18},{10... | collective-permute-start | bytes 1990664 | tf_op jit(solution)/shard_map/ppermute | solution.py:26
  137.4 1.8 %copy-start.21 = (f32[4,5,96,384]{3,2,1,0:T(8,128)S(1)}, f32[4,5,96,384]{3,2,1,0:T(8,128)}, u32[]{:S(2)}) copy-start(f32[4,5,96,384]{3,2,1,0:T(8,128)} %copy-done.20) | copy-start | bytes 8847364
  137.4 3.5 %collective-permute-start.25 = (bf16[9,96,384]{2,1,0:T(8,128)(2,1)}, bf16[9,96,384]{2,1,0:T(8,128)(2,1)}, u32[]{:S(2)}, u32[]{:S(2)}) collective-permute-start(bf16[9,96,384]{2,1,0:T(8,128)(2,1)} %after.22.refs_4_.refs_9_), channel_id=1, source_target_pairs={{0,1},{1,0},{2,3},{3,2},{4,5},{5,4},{6,7},{7,6},{8,9},{9,8},{10,11... | collective-permute-start | bytes 1990664 | tf_op jit(solution)/shard_map/ppermute | solution.py:26
  138.4 2.9 %collective-permute-start.24 = (bf16[9,96,384]{2,1,0:T(8,128)(2,1)}, bf16[9,96,384]{2,1,0:T(8,128)(2,1)S(1)}, u32[]{:S(2)}, u32[]{:S(2)}) collective-permute-start(bf16[9,96,384]{2,1,0:T(8,128)(2,1)} %after.21.refs_3_.refs_7_), channel_id=1, source_target_pairs={{0,1},{1,0},{2,3},{3,2},{4,5},{5,4},{6,7},{7,6},{8,9},{9,8},{10,11... | collective-permute-start | bytes 1990664 | tf_op jit(solution)/shard_map/ppermute | solution.py:26
  140.5 17.2 %collective-permute-start.26 = (bf16[1,5,96,384]{3,2,1,0:T(8,128)(2,1)S(1)}, bf16[1,5,96,384]{3,2,1,0:T(8,128)(2,1)S(1)}, u32[]{:S(2)}, u32[]{:S(2)}) collective-permute-start(bf16[1,5,96,384]{3,2,1,0:T(8,128)(2,1)S(1)} %add_convert_fusion), channel_id=1, source_target_pairs={{0,6},{1,7},{2,4},{3,5},{4,2},{5,3},{6,0},{7,1},{8,14},{9,15},{10,... | collective-permute-start | bytes 1105928 | tf_op jit(solution)/shard_map/ppermute | solution.py:26
  (25 other events, 26.3 us)

commit v22 on v21

--- a/solution.py
+++ b/solution.py
@@ -13,7 +13,7 @@
 EDGE = 16
 MARGIN = HALO - EDGE
 STEP = 64
-SPLIT = 3
+SPLIT = 2
 ROOT = math.sqrt(2.0 / math.pi)
 CUBIC = 0.044715
 SMALL = pl.CostEstimate(flops=1 << 20, bytes_accessed=1 << 16, transcendentals=0)
@@ -189,14 +189,14 @@
         copy.start()
     return copies
 
-def early_terms(place, layout, pieces, shifts, coarse):
+def early_terms(place, layout, pieces, shifts, coarse, earlier):
     both, columns = pieces[0].shape[1], shifts.shape[1]
     rows = sum(size for _, _, size, _ in layout)
     tile = 256
 
     def kernel(place, shifts_ref, *refs):
-        pieces, total = refs[: len(layout)], refs[len(layout)]
-        held, shifts, sems, shift_sems = refs[len(layout) + 1 :]
+        pieces, total = refs[: len(layout)], refs[len(layout) + len(earlier)]
+        held, shifts, sems, shift_sems = refs[len(layout) + len(earlier) + 1 :]
         copies = start_act(
             place, coarse, layout, pieces, shifts_ref, held, shifts, sems, shift_sems
         )
@@ -216,7 +216,7 @@
         grid_spec=pltpu.PrefetchScalarGridSpec(
             num_scalar_prefetch=1,
             grid=(1,),
-            in_specs=[ANYWHERE] * (1 + len(pieces)),
+            in_specs=[ANYWHERE] * (1 + len(pieces) + len(earlier)),
             out_specs=pl.BlockSpec((both, columns), lambda i, place: (0, 0)),
             scratch_shapes=[
                 pltpu.VMEM((rows, both), jnp.bfloat16),
@@ -228,9 +228,9 @@
         compiler_params=pltpu.CompilerParams(vmem_limit_bytes=48 << 20),
         cost_estimate=SMALL,
         name="weight_grad_early",
-    )(place, shifts, *pieces)
-
-def late_terms(place, layout, pieces, shifts, early, coarse, scale, planes, taps, rows):
+    )(place, shifts, *pieces, *earlier)
+
+def late_terms(place, layout, pieces, shifts, early, coarse, scale, planes, taps, rows, earlier):
     both, columns = early.shape
     width, block = both // 2, columns // 3
     count = sum(size for _, _, size, _ in layout)
@@ -238,8 +238,9 @@
     shape = (planes, taps, rows, block)
 
     def kernel(place, shifts_ref, early_ref, *refs):
-        pieces, (mine_ref, *theirs_refs) = refs[: len(layout)], refs[len(layout) : len(layout) + 3]
-        held, shifts, total, sems, shift_sems, early_sems = refs[len(layout) + 3 :]
+        pieces, refs = refs[: len(layout)], refs[len(layout) + len(earlier) :]
+        mine_ref, *theirs_refs = refs[:3]
+        held, shifts, total, sems, shift_sems, early_sems = refs[3:]
         core, plane = place[1] % 2, place[1] // 2
         copies = start_act(
             place, coarse, layout, pieces, shifts_ref, held, shifts, sems, shift_sems
@@ -295,7 +296,7 @@
         grid_spec=pltpu.PrefetchScalarGridSpec(
             num_scalar_prefetch=1,
             grid=(1,),
-            in_specs=[ANYWHERE] * (2 + len(pieces)),
+            in_specs=[ANYWHERE] * (2 + len(pieces) + len(earlier)),
             out_specs=[whole, half, half],
             scratch_shapes=[
                 pltpu.VMEM((count, both), jnp.bfloat16),
@@ -309,7 +310,7 @@
         compiler_params=pltpu.CompilerParams(vmem_limit_bytes=48 << 20),
         cost_estimate=SMALL,
         name="weight_grad_late",
-    )(place, shifts, early, *pieces)
+    )(place, shifts, early, *pieces, *earlier)
 
 def shifted_total(products, base, lanes, parity):
     total = None
@@ -505,17 +506,17 @@
     earlier = jnp.concatenate([zeros, trunk[:-1]])
     shifts = jnp.concatenate([later, trunk, earlier], axis=1)
     to_beside, to_below, own_window = kernel_messages(place, line, trunk_grad, coarse)
-    ready = (slope, shifts, to_beside, *crossing)
+    ready = (slope, shifts, to_beside)
     top, bottom = after(beside[:half], *ready), after(below[half:], *ready)
     far_top, far_bottom = from_peer(top, "seq", 2), from_peer(bottom, "seq", 1)
 
     scale = 0.5 * float(fine * seqs * reps) ** (-0.5)
     near_rows = [(d, 0, coarse, 0) for d in range(3)]
     far_rows = [(3, 0, half, 0), (3, half, half, 0)]
-    early = early_terms(place, near_rows, [act, beside, below], shifts, coarse)
+    early = early_terms(place, near_rows, [act, beside, below], shifts, coarse, crossing)
     line_across[2] = after(line_across[2], early)
     lines = stack_planes(place, line_across)
-    far_top, far_bottom = after(far_top, early, lines), after(far_bottom, early, lines)
+    far_top, far_bottom = after(far_top, early), after(far_bottom, early)
 
     to_beside, to_below = (
         after(message, far_top, far_bottom) for message in (to_beside, to_below)
@@ -524,7 +525,17 @@
     other_column, other_lines = from_peer(to_below, "rep", 1), from_peer(lines, "rep", 1)
 
     mine, *theirs = late_terms(
-        place, far_rows, [far_top, far_bottom], shifts, early, coarse, scale, planes, taps, rows
+        place,
+        far_rows,
+        [far_top, far_bottom],
+        shifts,
+        early,
+        coarse,
+        scale,
+        planes,
+        taps,
+        rows,
+        [line_across[2]],
     )
     arrived = [from_peer(part, "rep", 1) for part in theirs]
     pairs = []

time: 162 us -> 178 us (1.099)
  waiting for transfers between devices: 34.2 us -> 56.3 us
  local copies, waits for them, and re-layouts: 32.5 us -> 21.7 us
  Pallas kernels: 55.1 us -> 58.7 us
    ppermute x27, waiting for transfers between devices: 34.2 us -> 56.3 us  [from_peer(): return lax.ppermute(value, axis, [(i, i ^ distance) for i in range(peers)])]
    unnamed x92 -> x52, local copies, waits for them, and re-layouts: 22.1 us -> 11.6 us
    concatenate x1, other arithmetic: 5.4 us -> 2.98 us  [on_device_square(): shifts = jnp.concatenate([later, trunk, earlier], axis=1)]
    pallas_call x1, Pallas kernels: 8.19 us -> 10.2 us  [late_terms(): pl.pallas_call(kernel, out_shape=(jax.ShapeDtypeStruct(shape, jnp.float32...]
    convert_element_type x2, other arithmetic: 1.39 us -> 3.33 us  [reduce_line(): leaving = jnp.stack([blocks[d ^ mask].astype(jnp.bfloat16) for d in keep])]
  transfers between devices with their start and end apart: 27 -> 27, of which waited for: 6 -> 5; matrix products, arithmetic and copies ran while one was open for 11% -> 10% of each run, Pallas kernels for 34% -> 33%
where the time goes in v22:
time: 178 us; the launch traced here: 177 us
  Pallas kernels  58.7 us (33%)
  waiting for transfers between devices  56.3 us (32%)
  starting transfers between devices  27.6 us (16%)
  local copies, waits for them, and re-layouts  21.7 us (12%)
  other arithmetic  12 us (7%)
    ppermute x27, waiting for transfers between devices, from_peer(): return lax.ppermute(value, axis, [(i, i ^ distance) for i in range(peers)])  56.3 us
    ppermute x27, starting transfers between devices, from_peer(): return lax.ppermute(value, axis, [(i, i ^ distance) for i in range(peers)])  27.6 us
    pallas_call x2, Pallas kernels, gradient_stage(): pl.pallas_call(body, out_shape=out_shape, grid_spec=pltpu.PrefetchScalarG...  25.8 us
    pallas_call x1, Pallas kernels, early_terms(): pl.pallas_call(kernel, out_shape=jax.ShapeDtypeStruct((both, columns), jn...  13.8 us
    unnamed x52, local copies, waits for them, and re-layouts  11.6 us
    pallas_call x1, Pallas kernels, late_terms(): pl.pallas_call(kernel, out_shape=(jax.ShapeDtypeStruct(shape, jnp.float32...  10.2 us
    slice x2, local copies, waits for them, and re-layouts, on_device_square(): top, bottom = (after(beside[:half], *ready), after(below[half:], *ready))  4.15 us
  transfers between devices with their start and end apart: 27, of which 5 were waited for; matrix products, arithmetic and copies ran while one was open for 10% of the time, Pallas kernels for 33%

profile of v22, /device:TPU:9, one launch (start us, length us, event | category | flops | bytes accessed | tf_op | source)
XLA Modules:
  0.0 177.2 jit_solution(11262749962915525484)
XLA Ops:
  0.6 1.7 slice_bitcast_fusion.2
  2.3 1.2 collective-permute-start.3
  3.5 1.2 collective-permute-start.4
  4.9 0.9 slice.60.refs_0_
  5.9 1.4 collective-permute-start.1
  7.2 2.2 %collective-permute-start = (bf16[2,96,384]{2,1,0:T(8,128)(2,1)S(1)}, bf16[2,96,384]{2,1,0:T(8,128)(2,1)}, u32[]{:S(2)}, u32[]{:S(2)}) collective-permute-start(bf16[2,96,384]{2,1,0:T(8,128)(2,1)S(1)} %slice.60.refs_0_), channel_id=1, source_target_pairs={{0,2},{1,3},{2,0},{3,1},{4,6},{5,7},{6,4},{7,5},{8,10},{9,11},{10,... | collective-permute-start | bytes 442376 | tf_op jit(solution)/shard_map/ppermute | solution.py:26
  9.4 4.1 %collective-permute-done.1.refs_3_.refs_4_ = bf16[2,96,384]{2,1,0:T(8,128)(2,1)S(1)} collective-permute-done((bf16[2,96,384]{2,1,0:T(8,128)(2,1)S(1)}, bf16[2,96,384]{2,1,0:T(8,128)(2,1)S(1)}, u32[]{:S(2)}, u32[]{:S(2)}) %collective-permute-start.1) | collective-permute-done | bytes 147488 | tf_op jit(solution)/shard_map/ppermute | solution.py:26
  13.5 1.5 copy-done.6
  15.0 1.8 act.1.refs_0_
  16.7 1.1 copy-done.3
  19.3 2.5 %pad_maximum_fusion.refs_0_ = bf16[4,3,96,384]{3,2,1,0:T(8,128)(2,1)} fusion(bf16[1,3,96,384]{3,2,1,0:T(8,128)(2,1)} %bitcast.17, bf16[1,3,96,384]{3,2,1,0:T(8,128)(2,1)} %bitcast.16, bf16[1,3,96,384]{3,2,1,0:T(8,128)(2,1)} %bitcast.15, bf16[1,3,96,384]{3,2,1,0:T(8,128)(2,1)} %get-tuple-element.18), kind=kLoop, calls=%fused_computation.8 | loop fusion | flops 1327104 | bytes 1769472 | tf_op jit(solution)/shard_map/stack | solution.py:501
  21.8 1.0 collective-permute-start.10
  22.8 1.2 collective-permute-start.6
  24.0 1.2 collective-permute-start.8
  25.8 1.0 collective-permute-start.9
  26.8 33.9 %collective-permute-done.10.refs_4_.refs_3_ = bf16[4,3,96,384]{3,2,1,0:T(8,128)(2,1)} collective-permute-done((bf16[4,3,96,384]{3,2,1,0:T(8,128)(2,1)}, bf16[4,3,96,384]{3,2,1,0:T(8,128)(2,1)}, u32[]{:S(2)}, u32[]{:S(2)}) %collective-permute-start.10) | collective-permute-done | bytes 884768 | tf_op jit(solution)/shard_map/ppermute | solution.py:26
  60.7 3.0 %fusion.2.refs_2_.shifts_ref = bf16[2048,1152]{1,0:T(8,128)(2,1)} fusion(bf16[2047,384]{1,0:T(8,128)(2,1)S(1)} %get-tuple-element.17, bf16[2047,384]{1,0:T(8,128)(2,1)S(1)} %get-tuple-element.16, bf16[2048,384]{1,0:T(8,128)(2,1)S(1)} %bitcast.14), kind=kLoop, calls=%fused_computation.4 | loop fusion | flops 23592960 | bytes 9435648 | tf_op jit(solution)/shard_map/concatenate | solution.py:507
  63.7 2.4 %half_slope.1.refs_1_.refs_11_ = f32[2,512,768]{2,1,0:T(8,128)S(1)} custom-call(bf16[1,1024,768]{2,1,0:T(8,128)(2,1)S(1)} %copy-done.7), custom_call_target="tpu_custom_call" | custom-call | tf_op jit(solution)/shard_map/half_slope/pallas_call | solution.py:167
  66.1 1.7 copy-done.1
  67.8 1.9 %kernel_messages.1 = (bf16[17,96,384]{2,1,0:T(8,128)(2,1)S(1)}, bf16[17,96,384]{2,1,0:T(8,128)(2,1)S(1)}, bf16[6,96,384]{2,1,0:T(8,128)(2,1)S(1)}) custom-call(s32[2]{0:T(128)S(1)} %pad_add_fusion.place, bf16[2,96,384]{2,1,0:T(8,128)(2,1)S(1)} %slice.60.refs_0_, bf16[2,96,384]{2,1,0:T(8,128)(2,1)} %collective-permute-done.refs_1_.refs_2_, ...), custom_call_target="tpu_custom_call" | custom-call | flops 1048576 | bytes 65536 | tf_op jit(solution)/shard_map/kernel_messages/pallas_call | solution.py:129
  69.8 1.0 copy-done.5
  70.8 1.0 copy-done.8
  72.6 2.1 %slice.81.refs_0_ = bf16[256,1536]{1,0:T(8,128)(2,1)} slice(bf16[512,1536]{1,0:T(8,128)(2,1)} %collective-permute-done.8.refs_2_), slice={[256:512], [0:1536]} | slice | bytes 1572864 | tf_op jit(solution)/shard_map/slice | solution.py:510
  74.7 1.2 collective-permute-start.11
  75.9 2.1 %slice.80.refs_0_ = bf16[256,1536]{1,0:T(8,128)(2,1)} slice(bf16[512,1536]{1,0:T(8,128)(2,1)} %collective-permute-done.6.refs_1_), slice={[0:256], [0:1536]} | slice | bytes 1572864 | tf_op jit(solution)/shard_map/slice | solution.py:510
  78.0 1.2 collective-permute-start.7
  79.2 13.8 %weight_grad_early.1.refs_1_.early_ref = f32[1536,1152]{1,0:T(8,128)} custom-call(s32[2]{0:T(128)S(1)} %pad_add_fusion.place, bf16[2048,1152]{1,0:T(8,128)(2,1)} %fusion.2.refs_2_.shifts_ref, bf16[512,1536]{1,0:T(8,128)(2,1)S(1)} %copy-done.4, bf16[512,1536]{1,0:T(8,128)(2,1)} %collective-permute-done.6.refs_1_, ...), custom_call_target="tpu_custom_call" | custom-call | flops 1048576 | bytes 65536 | tf_op jit(solution)/shard_map/weight_grad_early/pallas_call | solution.py:213
  93.1 2.8 %stack_planes.1.refs_9_.refs_10_.refs_11_.refs_5_ = bf16[4,4,3,96,384]{4,3,2,1,0:T(8,128)(2,1)S(1)} custom-call(s32[2]{0:T(128)S(1)} %pad_add_fusion.place, bf16[4,3,96,384]{3,2,1,0:T(8,128)(2,1)} %after.14.refs_0_, bf16[4,3,96,384]{3,2,1,0:T(8,128)(2,1)} %collective-permute-done.9.refs_3_.refs_1_, bf16[4,3,96,384]{3,2,1,0:T(8,128)(2,1)} %after.20.refs_2_, ...), custom_call_target="tpu_custom_call" | custom-call | flops 1048576 | bytes 65536 | tf_op jit(solution)/shard_map/stack_planes/pallas_call | solution.py:471
  95.9 2.9 %collective-permute-start.19 = (bf16[4,4,3,96,384]{4,3,2,1,0:T(8,128)(2,1)S(1)}, bf16[4,4,3,96,384]{4,3,2,1,0:T(8,128)(2,1)}, u32[]{:S(2)}, u32[]{:S(2)}) collective-permute-start(bf16[4,4,3,96,384]{4,3,2,1,0:T(8,128)(2,1)S(1)} %stack_planes.1.refs_9_.refs_10_.refs_11_.refs_5_), channel_id=1, source_target_pairs={{0,1},{1,0},{2,3},{3,2},{4,5},{5,4},{6,7},{7,6},{8,9},{9,8},{10,11... | collective-permute-start | bytes 10616840 | tf_op jit(solution)/shard_map/ppermute | solution.py:26
  99.6 10.2 %weight_grad_late.1 = (f32[4,5,96,384]{3,2,1,0:T(8,128)}, bf16[2,5,96,384]{3,2,1,0:T(8,128)(2,1)S(1)}, bf16[2,5,96,384]{3,2,1,0:T(8,128)(2,1)S(1)}) custom-call(s32[2]{0:T(128)S(1)} %pad_add_fusion.place, bf16[2048,1152]{1,0:T(8,128)(2,1)} %fusion.2.refs_2_.shifts_ref, f32[1536,1152]{1,0:T(8,128)} %weight_grad_early.1.refs_1_.early_ref, ...), custom_call_target="tpu_custom_call" | custom-call | flops 1048576 | bytes 65536 | tf_op jit(solution)/shard_map/weight_grad_late/pallas_call | solution.py:289
  109.8 2.2 %collective-permute-start.20 = (bf16[2,5,96,384]{3,2,1,0:T(8,128)(2,1)S(1)}, bf16[2,5,96,384]{3,2,1,0:T(8,128)(2,1)S(1)}, u32[]{:S(2)}, u32[]{:S(2)}) collective-permute-start(bf16[2,5,96,384]{3,2,1,0:T(8,128)(2,1)S(1)} %get-tuple-element.12), channel_id=1, source_target_pairs={{0,1},{1,0},{2,3},{3,2},{4,5},{5,4},{6,7},{7,6},{8,9},{9,8},{10,11... | collective-permute-start | bytes 2211848 | tf_op jit(solution)/shard_map/ppermute | solution.py:26
  112.1 1.8 collective-permute-done.20
  114.3 12.4 %collective-permute-done.13.refs_2_.refs_7_ = bf16[17,96,384]{2,1,0:T(8,128)(2,1)} collective-permute-done((bf16[17,96,384]{2,1,0:T(8,128)(2,1)}, bf16[17,96,384]{2,1,0:T(8,128)(2,1)}, u32[]{:S(2)}, u32[]{:S(2)}) %collective-permute-start.13) | collective-permute-done | bytes 1253408 | tf_op jit(solution)/shard_map/ppermute | solution.py:26
  126.7 2.5 %collective-permute-start.17 = (bf16[17,96,384]{2,1,0:T(8,128)(2,1)}, bf16[17,96,384]{2,1,0:T(8,128)(2,1)S(1)}, u32[]{:S(2)}, u32[]{:S(2)}) collective-permute-start(bf16[17,96,384]{2,1,0:T(8,128)(2,1)} %collective-permute-done.13.refs_2_.refs_7_), channel_id=1, source_target_pairs={{0,1},{1,0},{2,3},{3,2},{4,5},{5,4},{6,7},{7,6},{8,9},{9,8},{10,11... | collective-permute-start | bytes 3760136 | tf_op jit(solution)/shard_map/ppermute | solution.py:26
  129.3 2.1 %add_convert_fusion.2 = (bf16[1,5,96,384]{3,2,1,0:T(8,128)(2,1)S(1)}, bf16[1,5,96,384]{3,2,1,0:T(8,128)(2,1)S(1)}) fusion(f32[4,5,96,384]{3,2,1,0:T(8,128)} %get-tuple-element.11, bf16[2,5,96,384]{3,2,1,0:T(8,128)(2,1)S(1)} %collective-permute-done.20, bf16[2,5,96,384]{3,2,1,0:T(8,128)(2,1)S(1)} %collective-permute-done.21), kind=kLoop, calls=%fused_computation.13 | loop fusion | flops 1105920 | bytes 2949120 | tf_op jit(solution)/shard_map/convert_element_type | solution.py:46
  131.5 0.9 pad_maximum_fusion.1
  132.4 1.7 collective-permute-start.22
  134.1 1.9 %slice.85 = bf16[7,96,384]{2,1,0:T(8,128)(2,1)} slice(bf16[17,96,384]{2,1,0:T(8,128)(2,1)} %collective-permute-done.13.refs_2_.refs_7_), slice={[4:11], [0:96], [0:384]} | slice | bytes 1032192 | tf_op jit(solution)/shard_map/slice | solution.py:550
  136.2 1.0 slice.82
  137.2 0.9 collective-permute-start.14
  138.3 0.9 copy-done.19
  139.2 14.2 %input_grad.2.refs_1_.refs_12_ = f32[2,512,768]{2,1,0:T(8,128)} custom-call(s32[2]{0:T(128)} %copy-done.13, bf16[6,96,384]{2,1,0:T(8,128)(2,1)} %copy-done.10, bf16[17,96,384]{2,1,0:T(8,128)(2,1)} %copy-done.14, bf16[17,96,384]{2,1,0:T(8,128)(2,1)} %collective-permute-done.13.refs_2_.refs_7_, bf16[17,96,384]{2,1,0:T(8,128)(2,1)} %after.19.refs_3_, ...), custom_call_target="tpu_custom_call" | custom-call | flops 1048576 | bytes 65536 | tf_op jit(solution)/shard_map/input_grad/pallas_call | solution.py:447
  153.4 1.3 collective-permute-start.25
  155.3 1.2 add_convert_fusion
  156.5 1.2 collective-permute-start.26
  158.5 11.6 %input_grad.3.refs_1_ = bf16[1,1024,768]{2,1,0:T(8,128)(2,1)} custom-call(s32[2]{0:T(128)} %copy-done.13, bf16[6,96,384]{2,1,0:T(8,128)(2,1)} %copy-done.10, bf16[17,96,384]{2,1,0:T(8,128)(2,1)} %copy-done.14, bf16[17,96,384]{2,1,0:T(8,128)(2,1)} %collective-permute-done.13.refs_2_.refs_7_, bf16[7,96,384]{2,1,0:T(8,128)(2,1)} %after.21.refs_3_.refs_7_, ...), custom_call_target="tpu_custom_call" | custom-call | flops 1048576 | bytes 65536 | tf_op jit(solution)/shard_map/input_grad/pallas_call | solution.py:447
  170.2 4.1 %collective-permute-done.26.refs_0_ = bf16[1,5,96,384]{3,2,1,0:T(8,128)(2,1)S(1)} collective-permute-done((bf16[1,5,96,384]{3,2,1,0:T(8,128)(2,1)S(1)}, bf16[1,5,96,384]{3,2,1,0:T(8,128)(2,1)S(1)}, u32[]{:S(2)}, u32[]{:S(2)}) %collective-permute-start.26) | collective-permute-done | bytes 368672 | tf_op jit(solution)/shard_map/ppermute | solution.py:26
  175.0 2.2 %add_bitcast_fusion = f32[5,96,384]{2,1,0:T(8,128)} fusion(bf16[1,5,96,384]{3,2,1,0:T(8,128)(2,1)} %after.23, f32[4,5,96,384]{3,2,1,0:T(8,128)S(1)} %copy-done.15, bf16[2,5,96,384]{3,2,1,0:T(8,128)(2,1)} %collective-permute-done.22.refs_2_, bf16[2,5,96,384]{3,2,1,0:T(8,128)(2,1)} %copy-done.23), kind=kLoop, calls=%fused_computation.10 | loop fusion | flops 1105920 | bytes 2580480 | tf_op jit(solution)/shard_map/add | solution.py:576
  (92 shorter events, 6.8 us)
Async XLA Ops:
  2.3 15.6 %collective-permute-start.3 = (bf16[3,96,384]{2,1,0:T(8,128)(2,1)S(1)}, bf16[3,96,384]{2,1,0:T(8,128)(2,1)S(1)}, u32[]{:S(2)}, u32[]{:S(2)}) collective-permute-start(bf16[3,96,384]{2,1,0:T(8,128)(2,1)S(1)} %get-tuple-element.19), channel_id=1, source_target_pairs={{0,8},{8,0},{16,24},{24,16},{1,9},{9,1},{17,25},{25,17},{2,10},{10... | collective-permute-start | bytes 663560 | tf_op jit(solution)/shard_map/ppermute | solution.py:26
  3.5 14.4 %collective-permute-start.4 = (bf16[3,96,384]{2,1,0:T(8,128)(2,1)S(1)}, bf16[3,96,384]{2,1,0:T(8,128)(2,1)S(1)}, u32[]{:S(2)}, u32[]{:S(2)}) collective-permute-start(bf16[3,96,384]{2,1,0:T(8,128)(2,1)S(1)} %get-tuple-element.19), channel_id=1, source_target_pairs={{0,16},{8,24},{16,0},{24,8},{1,17},{9,25},{17,1},{25,9},{2,18},{10... | collective-permute-start | bytes 663560 | tf_op jit(solution)/shard_map/ppermute | solution.py:26
  4.7 13.2 %collective-permute-start.5 = (bf16[3,96,384]{2,1,0:T(8,128)(2,1)S(1)}, bf16[3,96,384]{2,1,0:T(8,128)(2,1)S(1)}, u32[]{:S(2)}, u32[]{:S(2)}) collective-permute-start(bf16[3,96,384]{2,1,0:T(8,128)(2,1)S(1)} %get-tuple-element.19), channel_id=1, source_target_pairs={{0,24},{8,16},{16,8},{24,0},{1,25},{9,17},{17,9},{25,1},{2,26},{10... | collective-permute-start | bytes 663560 | tf_op jit(solution)/shard_map/ppermute | solution.py:26
  5.9 7.6 %collective-permute-start.1 = (bf16[2,96,384]{2,1,0:T(8,128)(2,1)S(1)}, bf16[2,96,384]{2,1,0:T(8,128)(2,1)S(1)}, u32[]{:S(2)}, u32[]{:S(2)}) collective-permute-start(bf16[2,96,384]{2,1,0:T(8,128)(2,1)S(1)} %slice.60.refs_0_), channel_id=1, source_target_pairs={{0,6},{1,7},{2,4},{3,5},{4,2},{5,3},{6,0},{7,1},{8,14},{9,15},{10,... | collective-permute-start | bytes 442376 | tf_op jit(solution)/shard_map/ppermute | solution.py:26
  7.2 14.6 %collective-permute-start = (bf16[2,96,384]{2,1,0:T(8,128)(2,1)S(1)}, bf16[2,96,384]{2,1,0:T(8,128)(2,1)}, u32[]{:S(2)}, u32[]{:S(2)}) collective-permute-start(bf16[2,96,384]{2,1,0:T(8,128)(2,1)S(1)} %slice.60.refs_0_), channel_id=1, source_target_pairs={{0,2},{1,3},{2,0},{3,1},{4,6},{5,7},{6,4},{7,5},{8,10},{9,11},{10,... | collective-permute-start | bytes 442376 | tf_op jit(solution)/shard_map/ppermute | solution.py:26
  13.5 5.8 %copy-start.11 = (bf16[2,96,384]{2,1,0:T(8,128)(2,1)}, bf16[2,96,384]{2,1,0:T(8,128)(2,1)S(1)}, u32[]{:S(2)}) copy-start(bf16[2,96,384]{2,1,0:T(8,128)(2,1)S(1)} %collective-permute-done.1.refs_3_.refs_4_) | copy-start | bytes 442372
  13.5 8.3 %collective-permute-start.2 = (bf16[2,96,384]{2,1,0:T(8,128)(2,1)S(1)}, bf16[2,96,384]{2,1,0:T(8,128)(2,1)}, u32[]{:S(2)}, u32[]{:S(2)}) collective-permute-start(bf16[2,96,384]{2,1,0:T(8,128)(2,1)S(1)} %collective-permute-done.1.refs_3_.refs_4_), channel_id=1, source_target_pairs={{0,2},{1,3},{2,0},{3,1},{4,6},{5,7},{6,4},{7,5},{8,10},{9,11},{10,... | collective-permute-start | bytes 442376 | tf_op jit(solution)/shard_map/ppermute | solution.py:26
  13.5 1.5 copy-start.6
  16.7 1.1 copy-start.3
  19.3 3.5 %copy-start.4 = (bf16[512,1536]{1,0:T(8,128)(2,1)S(1)}, bf16[512,1536]{1,0:T(8,128)(2,1)}, u32[]{:S(2)}) copy-start(bf16[512,1536]{1,0:T(8,128)(2,1)} %after.12.refs_1_.refs_0_) | copy-start | bytes 4718596
  19.3 6.0 %copy-start.2 = (bf16[1,2048,384]{2,1,0:T(8,128)(2,1)S(1)}, bf16[1,2048,384]{2,1,0:T(8,128)(2,1)}, u32[]{:S(2)}) copy-start(bf16[1,2048,384]{2,1,0:T(8,128)(2,1)} %refs_4_.1) | copy-start | bytes 4718596
  21.8 38.9 %collective-permute-start.10 = (bf16[4,3,96,384]{3,2,1,0:T(8,128)(2,1)}, bf16[4,3,96,384]{3,2,1,0:T(8,128)(2,1)}, u32[]{:S(2)}, u32[]{:S(2)}) collective-permute-start(bf16[4,3,96,384]{3,2,1,0:T(8,128)(2,1)} %after.14.refs_0_), channel_id=1, source_target_pairs={{0,6},{1,7},{2,4},{3,5},{4,2},{5,3},{6,0},{7,1},{8,14},{9,15},{10,... | collective-permute-start | bytes 2654216 | tf_op jit(solution)/shard_map/ppermute | solution.py:26
  22.8 53.1 %collective-permute-start.6 = (bf16[512,1536]{1,0:T(8,128)(2,1)S(1)}, bf16[512,1536]{1,0:T(8,128)(2,1)}, u32[]{:S(2)}, u32[]{:S(2)}) collective-permute-start(bf16[512,1536]{1,0:T(8,128)(2,1)S(1)} %copy-done.4), channel_id=1, source_target_pairs={{0,8},{8,0},{16,24},{24,16},{1,9},{9,1},{17,25},{25,17},{2,10},{10... | collective-permute-start | bytes 4718600 | tf_op jit(solution)/shard_map/ppermute | solution.py:26
  24.0 48.6 %collective-permute-start.8 = (bf16[512,1536]{1,0:T(8,128)(2,1)S(1)}, bf16[512,1536]{1,0:T(8,128)(2,1)}, u32[]{:S(2)}, u32[]{:S(2)}) collective-permute-start(bf16[512,1536]{1,0:T(8,128)(2,1)S(1)} %copy-done.4), channel_id=1, source_target_pairs={{0,16},{8,24},{16,0},{24,8},{1,17},{9,25},{17,1},{25,9},{2,18},{10... | collective-permute-start | bytes 4718600 | tf_op jit(solution)/shard_map/ppermute | solution.py:26
  25.8 53.4 %collective-permute-start.9 = (bf16[4,3,96,384]{3,2,1,0:T(8,128)(2,1)}, bf16[4,3,96,384]{3,2,1,0:T(8,128)(2,1)}, u32[]{:S(2)}, u32[]{:S(2)}) collective-permute-start(bf16[4,3,96,384]{3,2,1,0:T(8,128)(2,1)} %after.14.refs_0_), channel_id=1, source_target_pairs={{0,2},{1,3},{2,0},{3,1},{4,6},{5,7},{6,4},{7,5},{8,10},{9,11},{10,... | collective-permute-start | bytes 2654216 | tf_op jit(solution)/shard_map/ppermute | solution.py:26
  60.7 32.3 %collective-permute-start.18 = (bf16[4,3,96,384]{3,2,1,0:T(8,128)(2,1)}, bf16[4,3,96,384]{3,2,1,0:T(8,128)(2,1)}, u32[]{:S(2)}, u32[]{:S(2)}) collective-permute-start(bf16[4,3,96,384]{3,2,1,0:T(8,128)(2,1)} %collective-permute-done.10.refs_4_.refs_3_), channel_id=1, source_target_pairs={{0,2},{1,3},{2,0},{3,1},{4,6},{5,7},{6,4},{7,5},{8,10},{9,11},{10,... | collective-permute-start | bytes 2654216 | tf_op jit(solution)/shard_map/ppermute | solution.py:26
  60.7 3.0 %copy-start.7 = (bf16[1,1024,768]{2,1,0:T(8,128)(2,1)S(1)}, bf16[1,1024,768]{2,1,0:T(8,128)(2,1)}, u32[]{:S(2)}) copy-start(bf16[1,1024,768]{2,1,0:T(8,128)(2,1)} %x_ref.3) | copy-start | bytes 4718596
  63.7 4.1 %copy-start.12 = (bf16[2,96,384]{2,1,0:T(8,128)(2,1)S(1)}, bf16[2,96,384]{2,1,0:T(8,128)(2,1)}, u32[]{:S(2)}) copy-start(bf16[2,96,384]{2,1,0:T(8,128)(2,1)} %copy-done.11) | copy-start | bytes 442372
  66.1 1.7 copy-start.1
  67.8 31.8 %copy-start.13 = (s32[2]{0:T(128)}, s32[2]{0:T(128)S(1)}, u32[]{:S(2)}) copy-start(s32[2]{0:T(128)S(1)} %pad_add_fusion.place) | copy-start | bytes 28
  69.8 1.0 copy-start.5
  70.8 1.0 copy-start.8
  74.7 24.1 %collective-permute-start.11 = (bf16[256,1536]{1,0:T(8,128)(2,1)}, bf16[256,1536]{1,0:T(8,128)(2,1)}, u32[]{:S(2)}, u32[]{:S(2)}) collective-permute-start(bf16[256,1536]{1,0:T(8,128)(2,1)} %after.16), channel_id=1, source_target_pairs={{0,8},{8,0},{16,24},{24,16},{1,9},{9,1},{17,25},{25,17},{2,10},{10... | collective-permute-start | bytes 2359304 | tf_op jit(solution)/shard_map/ppermute | solution.py:26
  78.0 20.8 %collective-permute-start.7 = (bf16[256,1536]{1,0:T(8,128)(2,1)}, bf16[256,1536]{1,0:T(8,128)(2,1)}, u32[]{:S(2)}, u32[]{:S(2)}) collective-permute-start(bf16[256,1536]{1,0:T(8,128)(2,1)} %after.13), channel_id=1, source_target_pairs={{0,16},{8,24},{16,0},{24,8},{1,17},{9,25},{17,1},{25,9},{2,18},{10... | collective-permute-start | bytes 2359304 | tf_op jit(solution)/shard_map/ppermute | solution.py:26
  95.9 3.0 %copy-start = (bf16[4,4,3,96,384]{4,3,2,1,0:T(8,128)(2,1)}, bf16[4,4,3,96,384]{4,3,2,1,0:T(8,128)(2,1)S(1)}, u32[]{:S(2)}) copy-start(bf16[4,4,3,96,384]{4,3,2,1,0:T(8,128)(2,1)S(1)} %stack_planes.1.refs_9_.refs_10_.refs_11_.refs_5_) | copy-start | bytes 10616836
  95.9 42.3 %collective-permute-start.19 = (bf16[4,4,3,96,384]{4,3,2,1,0:T(8,128)(2,1)S(1)}, bf16[4,4,3,96,384]{4,3,2,1,0:T(8,128)(2,1)}, u32[]{:S(2)}, u32[]{:S(2)}) collective-permute-start(bf16[4,4,3,96,384]{4,3,2,1,0:T(8,128)(2,1)S(1)} %stack_planes.1.refs_9_.refs_10_.refs_11_.refs_5_), channel_id=1, source_target_pairs={{0,1},{1,0},{2,3},{3,2},{4,5},{5,4},{6,7},{7,6},{8,9},{9,8},{10,11... | collective-permute-start | bytes 10616840 | tf_op jit(solution)/shard_map/ppermute | solution.py:26
  98.9 27.8 %collective-permute-start.13 = (bf16[17,96,384]{2,1,0:T(8,128)(2,1)}, bf16[17,96,384]{2,1,0:T(8,128)(2,1)}, u32[]{:S(2)}, u32[]{:S(2)}) collective-permute-start(bf16[17,96,384]{2,1,0:T(8,128)(2,1)} %after.19.refs_3_), channel_id=1, source_target_pairs={{0,16},{8,24},{16,0},{24,8},{1,17},{9,25},{17,1},{25,9},{2,18},{10... | collective-permute-start | bytes 3760136 | tf_op jit(solution)/shard_map/ppermute | solution.py:26
  99.2 14.7 %copy-start.9 = (bf16[17,96,384]{2,1,0:T(8,128)(2,1)S(1)}, bf16[17,96,384]{2,1,0:T(8,128)(2,1)}, u32[]{:S(2)}) copy-start(bf16[17,96,384]{2,1,0:T(8,128)(2,1)} %after.19.refs_3_) | copy-start | bytes 3760132
  99.2 30.1 %collective-permute-start.12 = (bf16[17,96,384]{2,1,0:T(8,128)(2,1)}, bf16[17,96,384]{2,1,0:T(8,128)(2,1)S(1)}, u32[]{:S(2)}, u32[]{:S(2)}) collective-permute-start(bf16[17,96,384]{2,1,0:T(8,128)(2,1)} %after.18), channel_id=1, source_target_pairs={{0,8},{8,0},{16,24},{24,16},{1,9},{9,1},{17,25},{25,17},{2,10},{10... | collective-permute-start | bytes 3760136 | tf_op jit(solution)/shard_map/ppermute | solution.py:26
  109.8 4.1 %collective-permute-start.20 = (bf16[2,5,96,384]{3,2,1,0:T(8,128)(2,1)S(1)}, bf16[2,5,96,384]{3,2,1,0:T(8,128)(2,1)S(1)}, u32[]{:S(2)}, u32[]{:S(2)}) collective-permute-start(bf16[2,5,96,384]{3,2,1,0:T(8,128)(2,1)S(1)} %get-tuple-element.12), channel_id=1, source_target_pairs={{0,1},{1,0},{2,3},{3,2},{4,5},{5,4},{6,7},{7,6},{8,9},{9,8},{10,11... | collective-permute-start | bytes 2211848 | tf_op jit(solution)/shard_map/ppermute | solution.py:26
  112.0 17.3 %collective-permute-start.21 = (bf16[2,5,96,384]{3,2,1,0:T(8,128)(2,1)S(1)}, bf16[2,5,96,384]{3,2,1,0:T(8,128)(2,1)S(1)}, u32[]{:S(2)}, u32[]{:S(2)}) collective-permute-start(bf16[2,5,96,384]{3,2,1,0:T(8,128)(2,1)S(1)} %get-tuple-element.13), channel_id=1, source_target_pairs={{0,1},{1,0},{2,3},{3,2},{4,5},{5,4},{6,7},{7,6},{8,9},{9,8},{10,11... | collective-permute-start | bytes 2211848 | tf_op jit(solution)/shard_map/ppermute | solution.py:26
  113.9 23.3 %copy-start.23 = (bf16[2,5,96,384]{3,2,1,0:T(8,128)(2,1)}, bf16[2,5,96,384]{3,2,1,0:T(8,128)(2,1)S(1)}, u32[]{:S(2)}) copy-start(bf16[2,5,96,384]{3,2,1,0:T(8,128)(2,1)S(1)} %collective-permute-done.20) | copy-start | bytes 2211844
  113.9 22.1 %collective-permute-start.15 = (bf16[17,96,384]{2,1,0:T(8,128)(2,1)S(1)}, bf16[17,96,384]{2,1,0:T(8,128)(2,1)S(1)}, u32[]{:S(2)}, u32[]{:S(2)}) collective-permute-start(bf16[17,96,384]{2,1,0:T(8,128)(2,1)S(1)} %copy-done.9), channel_id=1, source_target_pairs={{0,1},{1,0},{2,3},{3,2},{4,5},{5,4},{6,7},{7,6},{8,9},{9,8},{10,11... | collective-permute-start | bytes 3760136 | tf_op jit(solution)/shard_map/ppermute | solution.py:26
  126.7 10.5 %collective-permute-start.17 = (bf16[17,96,384]{2,1,0:T(8,128)(2,1)}, bf16[17,96,384]{2,1,0:T(8,128)(2,1)S(1)}, u32[]{:S(2)}, u32[]{:S(2)}) collective-permute-start(bf16[17,96,384]{2,1,0:T(8,128)(2,1)} %collective-permute-done.13.refs_2_.refs_7_), channel_id=1, source_target_pairs={{0,1},{1,0},{2,3},{3,2},{4,5},{5,4},{6,7},{7,6},{8,9},{9,8},{10,11... | collective-permute-start | bytes 3760136 | tf_op jit(solution)/shard_map/ppermute | solution.py:26
  129.2 8.0 %copy-start.14 = (bf16[17,96,384]{2,1,0:T(8,128)(2,1)}, bf16[17,96,384]{2,1,0:T(8,128)(2,1)S(1)}, u32[]{:S(2)}) copy-start(bf16[17,96,384]{2,1,0:T(8,128)(2,1)S(1)} %collective-permute-done.12.refs_1_.refs_5_) | copy-start | bytes 3760132
  129.2 9.0 %collective-permute-start.16 = (bf16[17,96,384]{2,1,0:T(8,128)(2,1)S(1)}, bf16[17,96,384]{2,1,0:T(8,128)(2,1)S(1)}, u32[]{:S(2)}, u32[]{:S(2)}) collective-permute-start(bf16[17,96,384]{2,1,0:T(8,128)(2,1)S(1)} %collective-permute-done.12.refs_1_.refs_5_), channel_id=1, source_target_pairs={{0,1},{1,0},{2,3},{3,2},{4,5},{5,4},{6,7},{7,6},{8,9},{9,8},{10,11... | collective-permute-start | bytes 3760136 | tf_op jit(solution)/shard_map/ppermute | solution.py:26
  129.3 7.9 %copy-start.24 = (bf16[2,5,96,384]{3,2,1,0:T(8,128)(2,1)}, bf16[2,5,96,384]{3,2,1,0:T(8,128)(2,1)S(1)}, u32[]{:S(2)}) copy-start(bf16[2,5,96,384]{3,2,1,0:T(8,128)(2,1)S(1)} %collective-permute-done.21) | copy-start | bytes 2211844
  132.4 21.0 %collective-permute-start.22 = (bf16[2,5,96,384]{3,2,1,0:T(8,128)(2,1)}, bf16[2,5,96,384]{3,2,1,0:T(8,128)(2,1)}, u32[]{:S(2)}, u32[]{:S(2)}) collective-permute-start(bf16[2,5,96,384]{3,2,1,0:T(8,128)(2,1)} %pad_maximum_fusion.1), channel_id=1, source_target_pairs={{0,2},{1,3},{2,0},{3,1},{4,6},{5,7},{6,4},{7,5},{8,10},{9,11},{10,... | collective-permute-start | bytes 2211848 | tf_op jit(solution)/shard_map/ppermute | solution.py:26
  136.0 2.2 %copy-start.17 = (bf16[17,96,384]{2,1,0:T(8,128)(2,1)}, bf16[17,96,384]{2,1,0:T(8,128)(2,1)S(1)}, u32[]{:S(2)}) copy-start(bf16[17,96,384]{2,1,0:T(8,128)(2,1)S(1)} %collective-permute-done.15.refs_4_) | copy-start | bytes 3760132
  136.0 17.4 %collective-permute-start.23 = (bf16[7,96,384]{2,1,0:T(8,128)(2,1)}, bf16[7,96,384]{2,1,0:T(8,128)(2,1)}, u32[]{:S(2)}, u32[]{:S(2)}) collective-permute-start(bf16[7,96,384]{2,1,0:T(8,128)(2,1)} %slice.85), channel_id=1, source_target_pairs={{0,8},{8,0},{16,24},{24,16},{1,9},{9,1},{17,25},{25,17},{2,10},{10... | collective-permute-start | bytes 1548296 | tf_op jit(solution)/shard_map/ppermute | solution.py:26
  137.2 1.1 copy-start.18
  137.2 17.5 %collective-permute-start.14 = (bf16[7,96,384]{2,1,0:T(8,128)(2,1)}, bf16[7,96,384]{2,1,0:T(8,128)(2,1)}, u32[]{:S(2)}, u32[]{:S(2)}) collective-permute-start(bf16[7,96,384]{2,1,0:T(8,128)(2,1)} %slice.82), channel_id=1, source_target_pairs={{0,16},{8,24},{16,0},{24,8},{1,17},{9,25},{17,1},{25,9},{2,18},{10... | collective-permute-start | bytes 1548296 | tf_op jit(solution)/shard_map/ppermute | solution.py:26
  138.2 1.0 copy-start.19
  153.4 1.8 %copy-start.15 = (f32[4,5,96,384]{3,2,1,0:T(8,128)S(1)}, f32[4,5,96,384]{3,2,1,0:T(8,128)}, u32[]{:S(2)}) copy-start(f32[4,5,96,384]{3,2,1,0:T(8,128)} %get-tuple-element.11) | copy-start | bytes 8847364
  153.4 4.3 %collective-permute-start.25 = (bf16[7,96,384]{2,1,0:T(8,128)(2,1)}, bf16[7,96,384]{2,1,0:T(8,128)(2,1)}, u32[]{:S(2)}, u32[]{:S(2)}) collective-permute-start(bf16[7,96,384]{2,1,0:T(8,128)(2,1)} %after.22.refs_4_.refs_9_), channel_id=1, source_target_pairs={{0,1},{1,0},{2,3},{3,2},{4,5},{5,4},{6,7},{7,6},{8,9},{9,8},{10,11... | collective-permute-start | bytes 1548296 | tf_op jit(solution)/shard_map/ppermute | solution.py:26
  154.7 3.0 %collective-permute-start.24 = (bf16[7,96,384]{2,1,0:T(8,128)(2,1)}, bf16[7,96,384]{2,1,0:T(8,128)(2,1)S(1)}, u32[]{:S(2)}, u32[]{:S(2)}) collective-permute-start(bf16[7,96,384]{2,1,0:T(8,128)(2,1)} %after.21.refs_3_.refs_7_), channel_id=1, source_target_pairs={{0,1},{1,0},{2,3},{3,2},{4,5},{5,4},{6,7},{7,6},{8,9},{9,8},{10,11... | collective-permute-start | bytes 1548296 | tf_op jit(solution)/shard_map/ppermute | solution.py:26
  156.5 17.8 %collective-permute-start.26 = (bf16[1,5,96,384]{3,2,1,0:T(8,128)(2,1)S(1)}, bf16[1,5,96,384]{3,2,1,0:T(8,128)(2,1)S(1)}, u32[]{:S(2)}, u32[]{:S(2)}) collective-permute-start(bf16[1,5,96,384]{3,2,1,0:T(8,128)(2,1)S(1)} %add_convert_fusion), channel_id=1, source_target_pairs={{0,6},{1,7},{2,4},{3,5},{4,2},{5,3},{6,0},{7,1},{8,14},{9,15},{10,... | collective-permute-start | bytes 1105928 | tf_op jit(solution)/shard_map/ppermute | solution.py:26
  157.7 0.8 copy-start.25
  (5 other events, 3.6 us)

commit v23 on v22

--- a/solution.py
+++ b/solution.py
@@ -13,7 +13,7 @@
 EDGE = 16
 MARGIN = HALO - EDGE
 STEP = 64
-SPLIT = 2
+SPLIT = 3
 ROOT = math.sqrt(2.0 / math.pi)
 CUBIC = 0.044715
 SMALL = pl.CostEstimate(flops=1 << 20, bytes_accessed=1 << 16, transcendentals=0)
@@ -34,6 +34,26 @@
         input_output_aliases={0: 0},
         name="after",
     )(value, *earlier)
+
+def half_after(value, which, *earlier):
+    rows, width = value.shape[0] // 2, value.shape[1]
+    steps = 4
+    block = (rows // steps, width)
+
+    def kernel(value_ref, *refs):
+        refs[-1][...] = value_ref[...]
+
+    return pl.pallas_call(
+        kernel,
+        out_shape=jax.ShapeDtypeStruct((rows, width), value.dtype),
+        grid=(steps,),
+        in_specs=[pl.BlockSpec(block, lambda i: (i + which * steps, 0))] + [ANYWHERE] * len(earlier),
+        out_specs=pl.BlockSpec(block, lambda i: (i, 0)),
+        compiler_params=pltpu.CompilerParams(vmem_limit_bytes=16 << 20),
+        cost_estimate=SMALL,
+        name="half_after",
+    )(value, *earlier)
+
 
 def reduce_line(blocks, axis, count, unit):
     held, masks = [[0]], []
@@ -189,14 +209,14 @@
         copy.start()
     return copies
 
-def early_terms(place, layout, pieces, shifts, coarse, earlier):
+def early_terms(place, layout, pieces, shifts, coarse):
     both, columns = pieces[0].shape[1], shifts.shape[1]
     rows = sum(size for _, _, size, _ in layout)
     tile = 256
 
     def kernel(place, shifts_ref, *refs):
-        pieces, total = refs[: len(layout)], refs[len(layout) + len(earlier)]
-        held, shifts, sems, shift_sems = refs[len(layout) + len(earlier) + 1 :]
+        pieces, total = refs[: len(layout)], refs[len(layout)]
+        held, shifts, sems, shift_sems = refs[len(layout) + 1 :]
         copies = start_act(
             place, coarse, layout, pieces, shifts_ref, held, shifts, sems, shift_sems
         )
@@ -216,7 +236,7 @@
         grid_spec=pltpu.PrefetchScalarGridSpec(
             num_scalar_prefetch=1,
             grid=(1,),
-            in_specs=[ANYWHERE] * (1 + len(pieces) + len(earlier)),
+            in_specs=[ANYWHERE] * (1 + len(pieces)),
             out_specs=pl.BlockSpec((both, columns), lambda i, place: (0, 0)),
             scratch_shapes=[
                 pltpu.VMEM((rows, both), jnp.bfloat16),
@@ -228,7 +248,7 @@
         compiler_params=pltpu.CompilerParams(vmem_limit_bytes=48 << 20),
         cost_estimate=SMALL,
         name="weight_grad_early",
-    )(place, shifts, *pieces, *earlier)
+    )(place, shifts, *pieces)
 
 def late_terms(place, layout, pieces, shifts, early, coarse, scale, planes, taps, rows, earlier):
     both, columns = early.shape
@@ -506,14 +526,14 @@
     earlier = jnp.concatenate([zeros, trunk[:-1]])
     shifts = jnp.concatenate([later, trunk, earlier], axis=1)
     to_beside, to_below, own_window = kernel_messages(place, line, trunk_grad, coarse)
-    ready = (slope, shifts, to_beside)
-    top, bottom = after(beside[:half], *ready), after(below[half:], *ready)
+    ready = (slope, shifts, to_beside, *crossing)
+    top, bottom = half_after(beside, 0, *ready), half_after(below, 1, *ready)
     far_top, far_bottom = from_peer(top, "seq", 2), from_peer(bottom, "seq", 1)
 
     scale = 0.5 * float(fine * seqs * reps) ** (-0.5)
     near_rows = [(d, 0, coarse, 0) for d in range(3)]
     far_rows = [(3, 0, half, 0), (3, half, half, 0)]
-    early = early_terms(place, near_rows, [act, beside, below], shifts, coarse, crossing)
+    early = early_terms(place, near_rows, [act, beside, below], shifts, coarse)
     line_across[2] = after(line_across[2], early)
     lines = stack_planes(place, line_across)
     far_top, far_bottom = after(far_top, early), after(far_bottom, early)

time: 178 us -> 170 us (0.955)
  waiting for transfers between devices: 56.3 us -> 33.3 us
  local copies, waits for them, and re-layouts: 21.7 us -> 33 us
  Pallas kernels: 58.7 us -> 61.1 us
    ppermute x27, waiting for transfers between devices: 56.3 us -> 33.3 us  [from_peer(): return lax.ppermute(value, axis, [(i, i ^ distance) for i in range(peers)])]
    unnamed x52 -> x106, local copies, waits for them, and re-layouts: 11.6 us -> 25 us
    pallas_call x0 -> x2, Pallas kernels: none -> 5.64 us  [half_after(): pl.pallas_call(kernel, out_shape=jax.ShapeDtypeStruct((rows, width), valu...]
    slice x2 -> x0, local copies, waits for them, and re-layouts: 4.15 us -> none  [on_device_square(): top, bottom = (after(beside[:half], *ready), after(below[half:], *ready))]
    concatenate x1, other arithmetic: 2.98 us -> 5.41 us  [on_device_square(): shifts = jnp.concatenate([later, trunk, earlier], axis=1)]
    pallas_call x1, Pallas kernels: 2.82 us -> 0.76 us  [stack_planes(): pl.pallas_call(kernel, out_shape=jax.ShapeDtypeStruct((count, *shape), li...]
  transfers between devices with their start and end apart: 27 -> 27, of which waited for: 5 -> 6; matrix products, arithmetic and copies ran while one was open for 10% -> 10% of each run, Pallas kernels for 33% -> 36%
where the time goes in v23:
time: 170 us; the launch traced here: 169 us
  Pallas kernels  61.1 us (36%)
  waiting for transfers between devices  33.3 us (20%)
  local copies, waits for them, and re-layouts  33 us (19%)
  starting transfers between devices  27.9 us (16%)
  other arithmetic  12.6 us (7%)
    ppermute x27, waiting for transfers between devices, from_peer(): return lax.ppermute(value, axis, [(i, i ^ distance) for i in range(peers)])  33.3 us
    ppermute x27, starting transfers between devices, from_peer(): return lax.ppermute(value, axis, [(i, i ^ distance) for i in range(peers)])  27.9 us
    pallas_call x2, Pallas kernels, gradient_stage(): pl.pallas_call(body, out_shape=out_shape, grid_spec=pltpu.PrefetchScalarG...  25.9 us
    unnamed x106, local copies, waits for them, and re-layouts  25 us
    pallas_call x1, Pallas kernels, early_terms(): pl.pallas_call(kernel, out_shape=jax.ShapeDtypeStruct((both, columns), jn...  13.8 us
    pallas_call x1, Pallas kernels, late_terms(): pl.pallas_call(kernel, out_shape=(jax.ShapeDtypeStruct(shape, jnp.float32...  9.78 us
    pallas_call x2, Pallas kernels, half_after(): pl.pallas_call(kernel, out_shape=jax.ShapeDtypeStruct((rows, width), valu...  5.64 us
    concatenate x1, other arithmetic, on_device_square(): shifts = jnp.concatenate([later, trunk, earlier], axis=1)  5.41 us
  transfers between devices with their start and end apart: 27, of which 6 were waited for; matrix products, arithmetic and copies ran while one was open for 10% of the time, Pallas kernels for 36%

profile of v23, /device:TPU:9, one launch (start us, length us, event | category | flops | bytes accessed | tf_op | source)
XLA Modules:
  0.0 168.9 jit_solution(3199774322413478903)
XLA Ops:
  0.6 1.0 slice.54.refs_0_
  1.6 1.4 collective-permute-start.1
  3.0 0.9 slice_bitcast_fusion.2
  3.9 1.3 collective-permute-start.3
  5.2 1.2 collective-permute-start.4
  6.6 2.2 %collective-permute-start = (bf16[3,96,384]{2,1,0:T(8,128)(2,1)S(1)}, bf16[3,96,384]{2,1,0:T(8,128)(2,1)S(1)}, u32[]{:S(2)}, u32[]{:S(2)}) collective-permute-start(bf16[3,96,384]{2,1,0:T(8,128)(2,1)S(1)} %slice.54.refs_0_), channel_id=1, source_target_pairs={{0,2},{1,3},{2,0},{3,1},{4,6},{5,7},{6,4},{7,5},{8,10},{9,11},{10,... | collective-permute-start | bytes 663560 | tf_op jit(solution)/shard_map/ppermute | solution.py:26
  8.8 1.4 copy-done.12
  10.2 1.8 %act.1.refs_0_ = bf16[512,1536]{1,0:T(8,128)(2,1)S(1)} custom-call(bf16[1,1024,768]{2,1,0:T(8,128)(2,1)S(1)} %copy-done.12), custom_call_target="tpu_custom_call" | custom-call | flops 1048576 | bytes 65536 | tf_op jit(solution)/shard_map/act/pallas_call | solution.py:105
  12.0 1.1 copy-done.5
  14.5 1.3 collective-permute-start.10
  15.8 1.2 collective-permute-start.6
  17.1 2.1 %slice_bitcast_fusion.1 = (bf16[2047,384]{1,0:T(8,128)(2,1)}, bf16[2047,384]{1,0:T(8,128)(2,1)}) fusion(bf16[1,2048,384]{2,1,0:T(8,128)(2,1)S(1)} %copy-done.4), kind=kLoop, calls=%fused_computation.7 | loop fusion | bytes 6288384 | tf_op jit(solution)/shard_map/slice | solution.py:525
  20.1 2.1 %collective-permute-done.2.refs_2_.refs_3_ = bf16[3,96,384]{2,1,0:T(8,128)(2,1)S(1)} collective-permute-done((bf16[3,96,384]{2,1,0:T(8,128)(2,1)S(1)}, bf16[3,96,384]{2,1,0:T(8,128)(2,1)S(1)}, u32[]{:S(2)}, u32[]{:S(2)}) %collective-permute-start.2) | collective-permute-done | bytes 221216 | tf_op jit(solution)/shard_map/ppermute | solution.py:26
  23.3 5.4 %fusion.2.refs_1_.shifts_ref = bf16[2048,1152]{1,0:T(8,128)(2,1)} fusion(bf16[2047,384]{1,0:T(8,128)(2,1)} %get-tuple-element.17, bf16[2047,384]{1,0:T(8,128)(2,1)} %get-tuple-element.16, bf16[2048,384]{1,0:T(8,128)(2,1)S(1)} %bitcast.16), kind=kLoop, calls=%fused_computation.4 | loop fusion | flops 23592960 | bytes 9435648 | tf_op jit(solution)/shard_map/concatenate | solution.py:527
  28.7 2.3 %half_slope.1.refs_0_.refs_11_ = f32[2,512,768]{2,1,0:T(8,128)S(1)} custom-call(bf16[1,1024,768]{2,1,0:T(8,128)(2,1)S(1)} %copy-done.13), custom_call_target="tpu_custom_call" | custom-call | tf_op jit(solution)/shard_map/half_slope/pallas_call | solution.py:187
  31.0 1.6 copy-done.2
  32.7 0.9 copy-done.25
  33.7 0.9 copy-done.27
  34.6 0.9 copy-done.29
  36.5 1.0 kernel_messages.1
  37.5 12.9 %collective-permute-done.8.refs_4_.refs_3_ = bf16[4,2,96,384]{3,2,1,0:T(8,128)(2,1)S(1)} collective-permute-done((bf16[4,2,96,384]{3,2,1,0:T(8,128)(2,1)}, bf16[4,2,96,384]{3,2,1,0:T(8,128)(2,1)S(1)}, u32[]{:S(2)}, u32[]{:S(2)}) %collective-permute-start.8) | collective-permute-done | bytes 589856 | tf_op jit(solution)/shard_map/ppermute | solution.py:26
  50.5 2.3 %copy-done = bf16[2048,1152]{1,0:T(8,128)(2,1)S(1)} copy-done((bf16[2048,1152]{1,0:T(8,128)(2,1)S(1)}, bf16[2048,1152]{1,0:T(8,128)(2,1)}, u32[]{:S(2)}) %copy-start) | copy-done | bytes 4718616
  52.8 1.9 %copy-done.3 = f32[2,512,768]{2,1,0:T(8,128)S(1)} copy-done((f32[2,512,768]{2,1,0:T(8,128)S(1)}, f32[2,512,768]{2,1,0:T(8,128)}, u32[]{:S(2)}) %copy-start.3) | copy-done | bytes 3145752
  54.7 2.4 %half_after.3 = bf16[256,1536]{1,0:T(8,128)(2,1)S(1)} custom-call(bf16[512,1536]{1,0:T(8,128)(2,1)} %collective-permute-done.10.refs_2_.value_ref, f32[2,512,768]{2,1,0:T(8,128)S(1)} %copy-done.3, bf16[2048,1152]{1,0:T(8,128)(2,1)S(1)} %copy-done, bf16[21,96,384]{2,1,0:T(8,128)(2,1)S(1)} %get-tuple-element.9.refs_2_.refs_0_, ...), custom_call_target="tpu_custom_call" | custom-call | flops 1048576 | bytes 65536 | tf_op jit(solution)/shard_map/half_after/pallas_call | solution.py:46
  58.2 1.2 copy-done.17
  59.4 3.3 %half_after.2 = bf16[256,1536]{1,0:T(8,128)(2,1)} custom-call(bf16[512,1536]{1,0:T(8,128)(2,1)} %collective-permute-done.6.value_ref.refs_1_, f32[2,512,768]{2,1,0:T(8,128)S(1)} %copy-done.3, bf16[2048,1152]{1,0:T(8,128)(2,1)S(1)} %bitcast.15, bf16[21,96,384]{2,1,0:T(8,128)(2,1)S(1)} %get-tuple-element.9.refs_2_.refs_0_, ...), custom_call_target="tpu_custom_call" | custom-call | flops 1048576 | bytes 65536 | tf_op jit(solution)/shard_map/half_after/pallas_call | solution.py:46
  63.4 13.8 %weight_grad_early.1.refs_1_.early_ref = f32[1536,1152]{1,0:T(8,128)} custom-call(s32[2]{0:T(128)S(1)} %pad_add_fusion.place, bf16[2048,1152]{1,0:T(8,128)(2,1)} %fusion.2.refs_1_.shifts_ref, bf16[512,1536]{1,0:T(8,128)(2,1)S(1)} %copy-done.6, bf16[512,1536]{1,0:T(8,128)(2,1)} %collective-permute-done.6.value_ref.refs_1_, ...), custom_call_target="tpu_custom_call" | custom-call | flops 1048576 | bytes 65536 | tf_op jit(solution)/shard_map/weight_grad_early/pallas_call | solution.py:233
  78.2 1.4 collective-permute-done.9.refs_0_
  80.4 2.0 %collective-permute-start.12 = (bf16[21,96,384]{2,1,0:T(8,128)(2,1)}, bf16[21,96,384]{2,1,0:T(8,128)(2,1)}, u32[]{:S(2)}, u32[]{:S(2)}) collective-permute-start(bf16[21,96,384]{2,1,0:T(8,128)(2,1)} %after.14), channel_id=1, source_target_pairs={{0,8},{8,0},{16,24},{24,16},{1,9},{9,1},{17,25},{25,17},{2,10},{10... | collective-permute-start | bytes 4644872 | tf_op jit(solution)/shard_map/ppermute | solution.py:26
  83.3 1.1 copy-done.20
  85.1 3.0 %collective-permute-start.19 = (bf16[4,4,2,96,384]{4,3,2,1,0:T(8,128)(2,1)S(1)}, bf16[4,4,2,96,384]{4,3,2,1,0:T(8,128)(2,1)S(1)}, u32[]{:S(2)}, u32[]{:S(2)}) collective-permute-start(bf16[4,4,2,96,384]{4,3,2,1,0:T(8,128)(2,1)S(1)} %stack_planes.1.refs_9_.refs_10_.refs_11_.refs_5_), channel_id=1, source_target_pairs={{0,1},{1,0},{2,3},{3,2},{4,5},{5,4},{6,7},{7,6},{8,9},{9,8},{10,11... | collective-permute-start | bytes 7077896 | tf_op jit(solution)/shard_map/ppermute | solution.py:26
  88.1 9.8 %weight_grad_late.1 = (f32[4,5,96,384]{3,2,1,0:T(8,128)}, bf16[2,5,96,384]{3,2,1,0:T(8,128)(2,1)S(1)}, bf16[2,5,96,384]{3,2,1,0:T(8,128)(2,1)S(1)}) custom-call(s32[2]{0:T(128)S(1)} %pad_add_fusion.place, bf16[2048,1152]{1,0:T(8,128)(2,1)} %fusion.2.refs_1_.shifts_ref, f32[1536,1152]{1,0:T(8,128)} %weight_grad_early.1.refs_1_.early_ref, ...), custom_call_target="tpu_custom_call" | custom-call | flops 1048576 | bytes 65536 | tf_op jit(solution)/shard_map/weight_grad_late/pallas_call | solution.py:309
  98.7 1.8 %collective-permute-done.20 = bf16[2,5,96,384]{3,2,1,0:T(8,128)(2,1)S(1)} collective-permute-done((bf16[2,5,96,384]{3,2,1,0:T(8,128)(2,1)S(1)}, bf16[2,5,96,384]{3,2,1,0:T(8,128)(2,1)S(1)}, u32[]{:S(2)}, u32[]{:S(2)}) %collective-permute-start.20) | collective-permute-done | bytes 737312 | tf_op jit(solution)/shard_map/ppermute | solution.py:26
  100.9 11.9 %collective-permute-done.13.refs_2_.refs_7_ = bf16[21,96,384]{2,1,0:T(8,128)(2,1)} collective-permute-done((bf16[21,96,384]{2,1,0:T(8,128)(2,1)}, bf16[21,96,384]{2,1,0:T(8,128)(2,1)}, u32[]{:S(2)}, u32[]{:S(2)}) %collective-permute-start.13) | collective-permute-done | bytes 1548320 | tf_op jit(solution)/shard_map/ppermute | solution.py:26
  112.8 4.2 %collective-permute-start.17 = (bf16[21,96,384]{2,1,0:T(8,128)(2,1)}, bf16[21,96,384]{2,1,0:T(8,128)(2,1)S(1)}, u32[]{:S(2)}, u32[]{:S(2)}) collective-permute-start(bf16[21,96,384]{2,1,0:T(8,128)(2,1)} %collective-permute-done.13.refs_2_.refs_7_), channel_id=1, source_target_pairs={{0,1},{1,0},{2,3},{3,2},{4,5},{5,4},{6,7},{7,6},{8,9},{9,8},{10,11... | collective-permute-start | bytes 4644872 | tf_op jit(solution)/shard_map/ppermute | solution.py:26
  117.6 1.8 %add_convert_fusion.2 = (bf16[1,5,96,384]{3,2,1,0:T(8,128)(2,1)S(1)}, bf16[1,5,96,384]{3,2,1,0:T(8,128)(2,1)S(1)}) fusion(f32[4,5,96,384]{3,2,1,0:T(8,128)} %get-tuple-element.11, bf16[2,5,96,384]{3,2,1,0:T(8,128)(2,1)S(1)} %collective-permute-done.20, bf16[2,5,96,384]{3,2,1,0:T(8,128)(2,1)S(1)} %collective-permute-done.21), kind=kLoop, calls=%fused_computation.12 | loop fusion | flops 1105920 | bytes 2949120 | tf_op jit(solution)/shard_map/convert_element_type | solution.py:66
  119.3 0.9 pad_maximum_fusion
  120.5 2.0 %slice.75 = bf16[9,96,384]{2,1,0:T(8,128)(2,1)} slice(bf16[21,96,384]{2,1,0:T(8,128)(2,1)} %collective-permute-done.13.refs_2_.refs_7_), slice={[6:15], [0:96], [0:384]} | slice | bytes 1327104 | tf_op jit(solution)/shard_map/slice | solution.py:570
  122.6 1.3 collective-permute-start.23
  123.8 2.0 %slice.72 = bf16[9,96,384]{2,1,0:T(8,128)(2,1)} slice(bf16[21,96,384]{2,1,0:T(8,128)(2,1)} %collective-permute-done.12.refs_1_.refs_5_), slice={[0:9], [0:96], [0:384]} | slice | bytes 1327104 | tf_op jit(solution)/shard_map/slice | solution.py:569
  125.8 1.4 collective-permute-start.14
  127.3 1.1 copy-done.37
  128.4 14.2 %input_grad.2.refs_1_.refs_12_ = f32[2,512,768]{2,1,0:T(8,128)} custom-call(s32[2]{0:T(128)} %copy-done.32, bf16[6,96,384]{2,1,0:T(8,128)(2,1)} %copy-done.23, bf16[21,96,384]{2,1,0:T(8,128)(2,1)} %collective-permute-done.12.refs_1_.refs_5_, bf16[21,96,384]{2,1,0:T(8,128)(2,1)} %collective-permute-done.13.refs_2_.refs_7_, ...), custom_call_target="tpu_custom_call" | custom-call | flops 1048576 | bytes 65536 | tf_op jit(solution)/shard_map/input_grad/pallas_call | solution.py:467
  144.8 1.2 add_convert_fusion
  146.1 3.2 %collective-permute-start.26 = (bf16[1,5,96,384]{3,2,1,0:T(8,128)(2,1)S(1)}, bf16[1,5,96,384]{3,2,1,0:T(8,128)(2,1)S(1)}, u32[]{:S(2)}, u32[]{:S(2)}) collective-permute-start(bf16[1,5,96,384]{3,2,1,0:T(8,128)(2,1)S(1)} %add_convert_fusion), channel_id=1, source_target_pairs={{0,6},{1,7},{2,4},{3,5},{4,2},{5,3},{6,0},{7,1},{8,14},{9,15},{10,... | collective-permute-start | bytes 1105928 | tf_op jit(solution)/shard_map/ppermute | solution.py:26
  151.0 11.7 %input_grad.3.refs_1_ = bf16[1,1024,768]{2,1,0:T(8,128)(2,1)} custom-call(s32[2]{0:T(128)} %copy-done.32, bf16[6,96,384]{2,1,0:T(8,128)(2,1)} %copy-done.23, bf16[21,96,384]{2,1,0:T(8,128)(2,1)} %collective-permute-done.12.refs_1_.refs_5_, bf16[21,96,384]{2,1,0:T(8,128)(2,1)} %collective-permute-done.13.refs_2_.refs_7_, ...), custom_call_target="tpu_custom_call" | custom-call | flops 1048576 | bytes 65536 | tf_op jit(solution)/shard_map/input_grad/pallas_call | solution.py:467
  162.7 3.1 %collective-permute-done.26.refs_0_ = bf16[1,5,96,384]{3,2,1,0:T(8,128)(2,1)S(1)} collective-permute-done((bf16[1,5,96,384]{3,2,1,0:T(8,128)(2,1)S(1)}, bf16[1,5,96,384]{3,2,1,0:T(8,128)(2,1)S(1)}, u32[]{:S(2)}, u32[]{:S(2)}) %collective-permute-start.26) | collective-permute-done | bytes 368672 | tf_op jit(solution)/shard_map/ppermute | solution.py:26
  166.6 2.2 %add_bitcast_fusion = f32[5,96,384]{2,1,0:T(8,128)} fusion(bf16[1,5,96,384]{3,2,1,0:T(8,128)(2,1)} %after.19, f32[4,5,96,384]{3,2,1,0:T(8,128)} %get-tuple-element.11, bf16[2,5,96,384]{3,2,1,0:T(8,128)(2,1)S(1)} %copy-done.35, bf16[2,5,96,384]{3,2,1,0:T(8,128)(2,1)S(1)} %copy-done.40), kind=kLoop, calls=%fused_computation.9 | loop fusion | flops 1105920 | bytes 2580480 | tf_op jit(solution)/shard_map/add | solution.py:596
  (145 shorter events, 16.5 us)
Async XLA Ops:
  1.6 12.9 %copy-start.24 = (bf16[3,96,384]{2,1,0:T(8,128)(2,1)}, bf16[3,96,384]{2,1,0:T(8,128)(2,1)S(1)}, u32[]{:S(2)}) copy-start(bf16[3,96,384]{2,1,0:T(8,128)(2,1)S(1)} %slice.54.refs_0_) | copy-start | bytes 663556
  1.6 15.4 %collective-permute-start.1 = (bf16[3,96,384]{2,1,0:T(8,128)(2,1)S(1)}, bf16[3,96,384]{2,1,0:T(8,128)(2,1)S(1)}, u32[]{:S(2)}, u32[]{:S(2)}) collective-permute-start(bf16[3,96,384]{2,1,0:T(8,128)(2,1)S(1)} %slice.54.refs_0_), channel_id=1, source_target_pairs={{0,6},{1,7},{2,4},{3,5},{4,2},{5,3},{6,0},{7,1},{8,14},{9,15},{10,... | collective-permute-start | bytes 663560 | tf_op jit(solution)/shard_map/ppermute | solution.py:26
  3.9 9.2 %collective-permute-start.3 = (bf16[2,96,384]{2,1,0:T(8,128)(2,1)S(1)}, bf16[2,96,384]{2,1,0:T(8,128)(2,1)S(1)}, u32[]{:S(2)}, u32[]{:S(2)}) collective-permute-start(bf16[2,96,384]{2,1,0:T(8,128)(2,1)S(1)} %get-tuple-element.19), channel_id=1, source_target_pairs={{0,8},{8,0},{16,24},{24,16},{1,9},{9,1},{17,25},{25,17},{2,10},{10... | collective-permute-start | bytes 442376 | tf_op jit(solution)/shard_map/ppermute | solution.py:26
  5.2 8.0 %collective-permute-start.4 = (bf16[2,96,384]{2,1,0:T(8,128)(2,1)S(1)}, bf16[2,96,384]{2,1,0:T(8,128)(2,1)S(1)}, u32[]{:S(2)}, u32[]{:S(2)}) collective-permute-start(bf16[2,96,384]{2,1,0:T(8,128)(2,1)S(1)} %get-tuple-element.19), channel_id=1, source_target_pairs={{0,16},{8,24},{16,0},{24,8},{1,17},{9,25},{17,1},{25,9},{2,18},{10... | collective-permute-start | bytes 442376 | tf_op jit(solution)/shard_map/ppermute | solution.py:26
  6.4 6.7 %collective-permute-start.5 = (bf16[2,96,384]{2,1,0:T(8,128)(2,1)S(1)}, bf16[2,96,384]{2,1,0:T(8,128)(2,1)S(1)}, u32[]{:S(2)}, u32[]{:S(2)}) collective-permute-start(bf16[2,96,384]{2,1,0:T(8,128)(2,1)S(1)} %get-tuple-element.19), channel_id=1, source_target_pairs={{0,24},{8,16},{16,8},{24,0},{1,25},{9,17},{17,9},{25,1},{2,26},{10... | collective-permute-start | bytes 442376 | tf_op jit(solution)/shard_map/ppermute | solution.py:26
  6.6 13.5 %collective-permute-start = (bf16[3,96,384]{2,1,0:T(8,128)(2,1)S(1)}, bf16[3,96,384]{2,1,0:T(8,128)(2,1)S(1)}, u32[]{:S(2)}, u32[]{:S(2)}) collective-permute-start(bf16[3,96,384]{2,1,0:T(8,128)(2,1)S(1)} %slice.54.refs_0_), channel_id=1, source_target_pairs={{0,2},{1,3},{2,0},{3,1},{4,6},{5,7},{6,4},{7,5},{8,10},{9,11},{10,... | collective-permute-start | bytes 663560 | tf_op jit(solution)/shard_map/ppermute | solution.py:26
  13.1 3.9 %copy-start.4 = (bf16[1,2048,384]{2,1,0:T(8,128)(2,1)S(1)}, bf16[1,2048,384]{2,1,0:T(8,128)(2,1)}, u32[]{:S(2)}) copy-start(bf16[1,2048,384]{2,1,0:T(8,128)(2,1)} %refs_4_.1) | copy-start | bytes 4718596
  14.5 4.7 %copy-start.46 = (bf16[2,96,384]{2,1,0:T(8,128)(2,1)S(1)}, bf16[2,96,384]{2,1,0:T(8,128)(2,1)}, u32[]{:S(2)}) copy-start(bf16[2,96,384]{2,1,0:T(8,128)(2,1)} %copy-done.45) | copy-start | bytes 442372
  14.5 4.7 %copy-start.48 = (bf16[2,96,384]{2,1,0:T(8,128)(2,1)S(1)}, bf16[2,96,384]{2,1,0:T(8,128)(2,1)}, u32[]{:S(2)}) copy-start(bf16[2,96,384]{2,1,0:T(8,128)(2,1)} %copy-done.47) | copy-start | bytes 442372
  14.5 4.7 %copy-start.50 = (bf16[2,96,384]{2,1,0:T(8,128)(2,1)S(1)}, bf16[2,96,384]{2,1,0:T(8,128)(2,1)}, u32[]{:S(2)}) copy-start(bf16[2,96,384]{2,1,0:T(8,128)(2,1)} %copy-done.49) | copy-start | bytes 442372
  14.5 35.9 %collective-permute-start.10 = (bf16[512,1536]{1,0:T(8,128)(2,1)}, bf16[512,1536]{1,0:T(8,128)(2,1)}, u32[]{:S(2)}, u32[]{:S(2)}) collective-permute-start(bf16[512,1536]{1,0:T(8,128)(2,1)} %after.10.refs_1_.refs_0_), channel_id=1, source_target_pairs={{0,16},{8,24},{16,0},{24,8},{1,17},{9,25},{17,1},{25,9},{2,18},{10... | collective-permute-start | bytes 4718600 | tf_op jit(solution)/shard_map/ppermute | solution.py:26
  15.8 42.3 %collective-permute-start.6 = (bf16[512,1536]{1,0:T(8,128)(2,1)}, bf16[512,1536]{1,0:T(8,128)(2,1)}, u32[]{:S(2)}, u32[]{:S(2)}) collective-permute-start(bf16[512,1536]{1,0:T(8,128)(2,1)} %after.10.refs_1_.refs_0_), channel_id=1, source_target_pairs={{0,8},{8,0},{16,24},{24,16},{1,9},{9,1},{17,25},{25,17},{2,10},{10... | collective-permute-start | bytes 4718600 | tf_op jit(solution)/shard_map/ppermute | solution.py:26
  17.0 5.2 %collective-permute-start.2 = (bf16[3,96,384]{2,1,0:T(8,128)(2,1)S(1)}, bf16[3,96,384]{2,1,0:T(8,128)(2,1)S(1)}, u32[]{:S(2)}, u32[]{:S(2)}) collective-permute-start(bf16[3,96,384]{2,1,0:T(8,128)(2,1)S(1)} %collective-permute-done.1.refs_3_.refs_4_), channel_id=1, source_target_pairs={{0,2},{1,3},{2,0},{3,1},{4,6},{5,7},{6,4},{7,5},{8,10},{9,11},{10,... | collective-permute-start | bytes 663560 | tf_op jit(solution)/shard_map/ppermute | solution.py:26
  22.9 27.5 %collective-permute-start.8 = (bf16[4,2,96,384]{3,2,1,0:T(8,128)(2,1)}, bf16[4,2,96,384]{3,2,1,0:T(8,128)(2,1)S(1)}, u32[]{:S(2)}, u32[]{:S(2)}) collective-permute-start(bf16[4,2,96,384]{3,2,1,0:T(8,128)(2,1)} %after.11.refs_0_), channel_id=1, source_target_pairs={{0,6},{1,7},{2,4},{3,5},{4,2},{5,3},{6,0},{7,1},{8,14},{9,15},{10,... | collective-permute-start | bytes 1769480 | tf_op jit(solution)/shard_map/ppermute | solution.py:26
  22.9 27.5 %collective-permute-start.7 = (bf16[4,2,96,384]{3,2,1,0:T(8,128)(2,1)}, bf16[4,2,96,384]{3,2,1,0:T(8,128)(2,1)S(1)}, u32[]{:S(2)}, u32[]{:S(2)}) collective-permute-start(bf16[4,2,96,384]{3,2,1,0:T(8,128)(2,1)} %after.11.refs_0_), channel_id=1, source_target_pairs={{0,2},{1,3},{2,0},{3,1},{4,6},{5,7},{6,4},{7,5},{8,10},{9,11},{10,... | collective-permute-start | bytes 1769480 | tf_op jit(solution)/shard_map/ppermute | solution.py:26
  23.3 5.4 %copy-start.13 = (bf16[1,1024,768]{2,1,0:T(8,128)(2,1)S(1)}, bf16[1,1024,768]{2,1,0:T(8,128)(2,1)}, u32[]{:S(2)}) copy-start(bf16[1,1024,768]{2,1,0:T(8,128)(2,1)} %x_ref.3) | copy-start | bytes 4718596
  28.7 29.5 %slice-start = ((s8[4718592]{0:T(1024)(128)(4,1)}), s8[524288]{0:T(1024)(128)(4,1)S(1)}, s32[]{:S(2)}) async-start(s8[4718592]{0:T(1024)(128)(4,1)} %bitcast.14), calls=%async_computation | async-start | bytes 1048576
  36.5 51.6 %copy-start.32 = (s32[2]{0:T(128)}, s32[2]{0:T(128)S(1)}, u32[]{:S(2)}) copy-start(s32[2]{0:T(128)S(1)} %pad_add_fusion.place) | copy-start | bytes 28
  37.5 19.6 %copy-start.14 = (bf16[21,96,384]{2,1,0:T(8,128)(2,1)}, bf16[21,96,384]{2,1,0:T(8,128)(2,1)S(1)}, u32[]{:S(2)}) copy-start(bf16[21,96,384]{2,1,0:T(8,128)(2,1)S(1)} %get-tuple-element.10.refs_0_) | copy-start | bytes 4644868
  37.5 19.6 %copy-start.23 = (bf16[6,96,384]{2,1,0:T(8,128)(2,1)}, bf16[6,96,384]{2,1,0:T(8,128)(2,1)S(1)}, u32[]{:S(2)}) copy-start(bf16[6,96,384]{2,1,0:T(8,128)(2,1)S(1)} %get-tuple-element.8.refs_0_) | copy-start | bytes 1327108
  37.5 20.7 %copy-start.7 = (bf16[21,96,384]{2,1,0:T(8,128)(2,1)}, bf16[21,96,384]{2,1,0:T(8,128)(2,1)S(1)}, u32[]{:S(2)}) copy-start(bf16[21,96,384]{2,1,0:T(8,128)(2,1)S(1)} %get-tuple-element.9.refs_2_.refs_0_) | copy-start | bytes 4644868
  57.9 5.5 %copy-start.6 = (bf16[512,1536]{1,0:T(8,128)(2,1)S(1)}, bf16[512,1536]{1,0:T(8,128)(2,1)}, u32[]{:S(2)}) copy-start(bf16[512,1536]{1,0:T(8,128)(2,1)} %after.10.refs_1_.refs_0_) | copy-start | bytes 4718596
  57.9 19.3 %collective-permute-start.11 = (bf16[256,1536]{1,0:T(8,128)(2,1)S(1)}, bf16[256,1536]{1,0:T(8,128)(2,1)S(1)}, u32[]{:S(2)}, u32[]{:S(2)}) collective-permute-start(bf16[256,1536]{1,0:T(8,128)(2,1)S(1)} %half_after.3), channel_id=1, source_target_pairs={{0,8},{8,0},{16,24},{24,16},{1,9},{9,1},{17,25},{25,17},{2,10},{10... | collective-permute-start | bytes 2359304 | tf_op jit(solution)/shard_map/ppermute | solution.py:26
  62.7 16.9 %collective-permute-start.9 = (bf16[256,1536]{1,0:T(8,128)(2,1)}, bf16[256,1536]{1,0:T(8,128)(2,1)S(1)}, u32[]{:S(2)}, u32[]{:S(2)}) collective-permute-start(bf16[256,1536]{1,0:T(8,128)(2,1)} %half_after.2), channel_id=1, source_target_pairs={{0,16},{8,24},{16,0},{24,8},{1,17},{9,25},{17,1},{25,9},{2,18},{10... | collective-permute-start | bytes 2359304 | tf_op jit(solution)/shard_map/ppermute | solution.py:26
  63.0 19.4 %collective-permute-start.18 = (bf16[4,2,96,384]{3,2,1,0:T(8,128)(2,1)S(1)}, bf16[4,2,96,384]{3,2,1,0:T(8,128)(2,1)S(1)}, u32[]{:S(2)}, u32[]{:S(2)}) collective-permute-start(bf16[4,2,96,384]{3,2,1,0:T(8,128)(2,1)S(1)} %collective-permute-done.8.refs_4_.refs_3_), channel_id=1, source_target_pairs={{0,2},{1,3},{2,0},{3,1},{4,6},{5,7},{6,4},{7,5},{8,10},{9,11},{10,... | collective-permute-start | bytes 1769480 | tf_op jit(solution)/shard_map/ppermute | solution.py:26
  80.4 32.4 %collective-permute-start.13 = (bf16[21,96,384]{2,1,0:T(8,128)(2,1)}, bf16[21,96,384]{2,1,0:T(8,128)(2,1)}, u32[]{:S(2)}, u32[]{:S(2)}) collective-permute-start(bf16[21,96,384]{2,1,0:T(8,128)(2,1)} %after.15.refs_3_), channel_id=1, source_target_pairs={{0,16},{8,24},{16,0},{24,8},{1,17},{9,25},{17,1},{25,9},{2,18},{10... | collective-permute-start | bytes 4644872 | tf_op jit(solution)/shard_map/ppermute | solution.py:26
  80.4 36.6 %collective-permute-start.12 = (bf16[21,96,384]{2,1,0:T(8,128)(2,1)}, bf16[21,96,384]{2,1,0:T(8,128)(2,1)}, u32[]{:S(2)}, u32[]{:S(2)}) collective-permute-start(bf16[21,96,384]{2,1,0:T(8,128)(2,1)} %after.14), channel_id=1, source_target_pairs={{0,8},{8,0},{16,24},{24,16},{1,9},{9,1},{17,25},{25,17},{2,10},{10... | collective-permute-start | bytes 4644872 | tf_op jit(solution)/shard_map/ppermute | solution.py:26
  84.3 3.8 %copy-start.9 = (bf16[256,1536]{1,0:T(8,128)(2,1)S(1)}, bf16[256,1536]{1,0:T(8,128)(2,1)}, u32[]{:S(2)}) copy-start(bf16[256,1536]{1,0:T(8,128)(2,1)} %after.13.refs_2_.refs_1_) | copy-start | bytes 2359300
  84.3 3.8 %copy-start.11 = (bf16[256,1536]{1,0:T(8,128)(2,1)S(1)}, bf16[256,1536]{1,0:T(8,128)(2,1)}, u32[]{:S(2)}) copy-start(bf16[256,1536]{1,0:T(8,128)(2,1)} %after.12.refs_1_.refs_0_) | copy-start | bytes 2359300
  84.3 3.8 %copy-start.21 = (bf16[4,2,96,384]{3,2,1,0:T(8,128)(2,1)S(1)}, bf16[4,2,96,384]{3,2,1,0:T(8,128)(2,1)}, u32[]{:S(2)}) copy-start(bf16[4,2,96,384]{3,2,1,0:T(8,128)(2,1)} %after.16.refs_2_) | copy-start | bytes 1769476
  85.1 12.8 %copy-start.1 = (bf16[4,4,2,96,384]{4,3,2,1,0:T(8,128)(2,1)}, bf16[4,4,2,96,384]{4,3,2,1,0:T(8,128)(2,1)S(1)}, u32[]{:S(2)}) copy-start(bf16[4,4,2,96,384]{4,3,2,1,0:T(8,128)(2,1)S(1)} %stack_planes.1.refs_9_.refs_10_.refs_11_.refs_5_) | copy-start | bytes 7077892
  85.1 13.6 %copy-start.15 = (bf16[21,96,384]{2,1,0:T(8,128)(2,1)S(1)}, bf16[21,96,384]{2,1,0:T(8,128)(2,1)}, u32[]{:S(2)}) copy-start(bf16[21,96,384]{2,1,0:T(8,128)(2,1)} %after.15.refs_3_) | copy-start | bytes 4644868
  85.1 40.7 %collective-permute-start.19 = (bf16[4,4,2,96,384]{4,3,2,1,0:T(8,128)(2,1)S(1)}, bf16[4,4,2,96,384]{4,3,2,1,0:T(8,128)(2,1)S(1)}, u32[]{:S(2)}, u32[]{:S(2)}) collective-permute-start(bf16[4,4,2,96,384]{4,3,2,1,0:T(8,128)(2,1)S(1)} %stack_planes.1.refs_9_.refs_10_.refs_11_.refs_5_), channel_id=1, source_target_pairs={{0,1},{1,0},{2,3},{3,2},{4,5},{5,4},{6,7},{7,6},{8,9},{9,8},{10,11... | collective-permute-start | bytes 7077896 | tf_op jit(solution)/shard_map/ppermute | solution.py:26
  97.9 2.6 %collective-permute-start.20 = (bf16[2,5,96,384]{3,2,1,0:T(8,128)(2,1)S(1)}, bf16[2,5,96,384]{3,2,1,0:T(8,128)(2,1)S(1)}, u32[]{:S(2)}, u32[]{:S(2)}) collective-permute-start(bf16[2,5,96,384]{3,2,1,0:T(8,128)(2,1)S(1)} %get-tuple-element.12), channel_id=1, source_target_pairs={{0,1},{1,0},{2,3},{3,2},{4,5},{5,4},{6,7},{7,6},{8,9},{9,8},{10,11... | collective-permute-start | bytes 2211848 | tf_op jit(solution)/shard_map/ppermute | solution.py:26
  98.7 23.9 %collective-permute-start.15 = (bf16[21,96,384]{2,1,0:T(8,128)(2,1)S(1)}, bf16[21,96,384]{2,1,0:T(8,128)(2,1)S(1)}, u32[]{:S(2)}, u32[]{:S(2)}) collective-permute-start(bf16[21,96,384]{2,1,0:T(8,128)(2,1)S(1)} %copy-done.15), channel_id=1, source_target_pairs={{0,1},{1,0},{2,3},{3,2},{4,5},{5,4},{6,7},{7,6},{8,9},{9,8},{10,11... | collective-permute-start | bytes 4644872 | tf_op jit(solution)/shard_map/ppermute | solution.py:26
  100.5 22.1 %copy-start.39 = (bf16[2,5,96,384]{3,2,1,0:T(8,128)(2,1)}, bf16[2,5,96,384]{3,2,1,0:T(8,128)(2,1)S(1)}, u32[]{:S(2)}) copy-start(bf16[2,5,96,384]{3,2,1,0:T(8,128)(2,1)S(1)} %collective-permute-done.20) | copy-start | bytes 2211844
  100.5 17.1 %collective-permute-start.21 = (bf16[2,5,96,384]{3,2,1,0:T(8,128)(2,1)S(1)}, bf16[2,5,96,384]{3,2,1,0:T(8,128)(2,1)S(1)}, u32[]{:S(2)}, u32[]{:S(2)}) collective-permute-start(bf16[2,5,96,384]{3,2,1,0:T(8,128)(2,1)S(1)} %get-tuple-element.13), channel_id=1, source_target_pairs={{0,1},{1,0},{2,3},{3,2},{4,5},{5,4},{6,7},{7,6},{8,9},{9,8},{10,11... | collective-permute-start | bytes 2211848 | tf_op jit(solution)/shard_map/ppermute | solution.py:26
  112.8 14.4 %collective-permute-start.17 = (bf16[21,96,384]{2,1,0:T(8,128)(2,1)}, bf16[21,96,384]{2,1,0:T(8,128)(2,1)S(1)}, u32[]{:S(2)}, u32[]{:S(2)}) collective-permute-start(bf16[21,96,384]{2,1,0:T(8,128)(2,1)} %collective-permute-done.13.refs_2_.refs_7_), channel_id=1, source_target_pairs={{0,1},{1,0},{2,3},{3,2},{4,5},{5,4},{6,7},{7,6},{8,9},{9,8},{10,11... | collective-permute-start | bytes 4644872 | tf_op jit(solution)/shard_map/ppermute | solution.py:26
  117.0 10.2 %collective-permute-start.16 = (bf16[21,96,384]{2,1,0:T(8,128)(2,1)}, bf16[21,96,384]{2,1,0:T(8,128)(2,1)}, u32[]{:S(2)}, u32[]{:S(2)}) collective-permute-start(bf16[21,96,384]{2,1,0:T(8,128)(2,1)} %collective-permute-done.12.refs_1_.refs_5_), channel_id=1, source_target_pairs={{0,1},{1,0},{2,3},{3,2},{4,5},{5,4},{6,7},{7,6},{8,9},{9,8},{10,11... | collective-permute-start | bytes 4644872 | tf_op jit(solution)/shard_map/ppermute | solution.py:26
  117.6 5.0 %copy-start.41 = (bf16[2,5,96,384]{3,2,1,0:T(8,128)(2,1)}, bf16[2,5,96,384]{3,2,1,0:T(8,128)(2,1)S(1)}, u32[]{:S(2)}) copy-start(bf16[2,5,96,384]{3,2,1,0:T(8,128)(2,1)S(1)} %collective-permute-done.21) | copy-start | bytes 2211844
  120.3 22.3 %collective-permute-start.22 = (bf16[2,5,96,384]{3,2,1,0:T(8,128)(2,1)}, bf16[2,5,96,384]{3,2,1,0:T(8,128)(2,1)S(1)}, u32[]{:S(2)}, u32[]{:S(2)}) collective-permute-start(bf16[2,5,96,384]{3,2,1,0:T(8,128)(2,1)} %pad_maximum_fusion), channel_id=1, source_target_pairs={{0,2},{1,3},{2,0},{3,1},{4,6},{5,7},{6,4},{7,5},{8,10},{9,11},{10,... | collective-permute-start | bytes 2211848 | tf_op jit(solution)/shard_map/ppermute | solution.py:26
  122.6 4.7 %copy-start.36 = (bf16[21,96,384]{2,1,0:T(8,128)(2,1)}, bf16[21,96,384]{2,1,0:T(8,128)(2,1)S(1)}, u32[]{:S(2)}) copy-start(bf16[21,96,384]{2,1,0:T(8,128)(2,1)S(1)} %collective-permute-done.15.refs_4_) | copy-start | bytes 4644868
  122.6 20.1 %collective-permute-start.23 = (bf16[9,96,384]{2,1,0:T(8,128)(2,1)}, bf16[9,96,384]{2,1,0:T(8,128)(2,1)}, u32[]{:S(2)}, u32[]{:S(2)}) collective-permute-start(bf16[9,96,384]{2,1,0:T(8,128)(2,1)} %slice.75), channel_id=1, source_target_pairs={{0,8},{8,0},{16,24},{24,16},{1,9},{9,1},{17,25},{25,17},{2,10},{10... | collective-permute-start | bytes 1990664 | tf_op jit(solution)/shard_map/ppermute | solution.py:26
  125.8 18.2 %collective-permute-start.14 = (bf16[9,96,384]{2,1,0:T(8,128)(2,1)}, bf16[9,96,384]{2,1,0:T(8,128)(2,1)}, u32[]{:S(2)}, u32[]{:S(2)}) collective-permute-start(bf16[9,96,384]{2,1,0:T(8,128)(2,1)} %slice.72), channel_id=1, source_target_pairs={{0,16},{8,24},{16,0},{24,8},{1,17},{9,25},{17,1},{25,9},{2,18},{10... | collective-permute-start | bytes 1990664 | tf_op jit(solution)/shard_map/ppermute | solution.py:26
  143.5 5.8 %collective-permute-start.25 = (bf16[9,96,384]{2,1,0:T(8,128)(2,1)}, bf16[9,96,384]{2,1,0:T(8,128)(2,1)S(1)}, u32[]{:S(2)}, u32[]{:S(2)}) collective-permute-start(bf16[9,96,384]{2,1,0:T(8,128)(2,1)} %after.18.refs_4_.refs_9_), channel_id=1, source_target_pairs={{0,1},{1,0},{2,3},{3,2},{4,5},{5,4},{6,7},{7,6},{8,9},{9,8},{10,11... | collective-permute-start | bytes 1990664 | tf_op jit(solution)/shard_map/ppermute | solution.py:26
  144.0 5.3 %collective-permute-start.24 = (bf16[9,96,384]{2,1,0:T(8,128)(2,1)}, bf16[9,96,384]{2,1,0:T(8,128)(2,1)S(1)}, u32[]{:S(2)}, u32[]{:S(2)}) collective-permute-start(bf16[9,96,384]{2,1,0:T(8,128)(2,1)} %after.17.refs_3_.refs_7_), channel_id=1, source_target_pairs={{0,1},{1,0},{2,3},{3,2},{4,5},{5,4},{6,7},{7,6},{8,9},{9,8},{10,11... | collective-permute-start | bytes 1990664 | tf_op jit(solution)/shard_map/ppermute | solution.py:26
  146.1 19.8 %collective-permute-start.26 = (bf16[1,5,96,384]{3,2,1,0:T(8,128)(2,1)S(1)}, bf16[1,5,96,384]{3,2,1,0:T(8,128)(2,1)S(1)}, u32[]{:S(2)}, u32[]{:S(2)}) collective-permute-start(bf16[1,5,96,384]{3,2,1,0:T(8,128)(2,1)S(1)} %add_convert_fusion), channel_id=1, source_target_pairs={{0,6},{1,7},{2,4},{3,5},{4,2},{5,3},{6,0},{7,1},{8,14},{9,15},{10,... | collective-permute-start | bytes 1105928 | tf_op jit(solution)/shard_map/ppermute | solution.py:26
  162.7 3.9 %copy-start.40 = (bf16[2,5,96,384]{3,2,1,0:T(8,128)(2,1)S(1)}, bf16[2,5,96,384]{3,2,1,0:T(8,128)(2,1)}, u32[]{:S(2)}) copy-start(bf16[2,5,96,384]{3,2,1,0:T(8,128)(2,1)} %copy-done.39) | copy-start | bytes 2211844
  (32 other events, 42.3 us)

commit v24 on v22

--- a/solution.py
+++ b/solution.py
@@ -13,7 +13,7 @@
 EDGE = 16
 MARGIN = HALO - EDGE
 STEP = 64
-SPLIT = 2
+SPLIT = 3
 ROOT = math.sqrt(2.0 / math.pi)
 CUBIC = 0.044715
 SMALL = pl.CostEstimate(flops=1 << 20, bytes_accessed=1 << 16, transcendentals=0)
@@ -189,14 +189,14 @@
         copy.start()
     return copies
 
-def early_terms(place, layout, pieces, shifts, coarse, earlier):
+def early_terms(place, layout, pieces, shifts, coarse):
     both, columns = pieces[0].shape[1], shifts.shape[1]
     rows = sum(size for _, _, size, _ in layout)
     tile = 256
 
     def kernel(place, shifts_ref, *refs):
-        pieces, total = refs[: len(layout)], refs[len(layout) + len(earlier)]
-        held, shifts, sems, shift_sems = refs[len(layout) + len(earlier) + 1 :]
+        pieces, total = refs[: len(layout)], refs[len(layout)]
+        held, shifts, sems, shift_sems = refs[len(layout) + 1 :]
         copies = start_act(
             place, coarse, layout, pieces, shifts_ref, held, shifts, sems, shift_sems
         )
@@ -216,7 +216,7 @@
         grid_spec=pltpu.PrefetchScalarGridSpec(
             num_scalar_prefetch=1,
             grid=(1,),
-            in_specs=[ANYWHERE] * (1 + len(pieces) + len(earlier)),
+            in_specs=[ANYWHERE] * (1 + len(pieces)),
             out_specs=pl.BlockSpec((both, columns), lambda i, place: (0, 0)),
             scratch_shapes=[
                 pltpu.VMEM((rows, both), jnp.bfloat16),
@@ -228,7 +228,7 @@
         compiler_params=pltpu.CompilerParams(vmem_limit_bytes=48 << 20),
         cost_estimate=SMALL,
         name="weight_grad_early",
-    )(place, shifts, *pieces, *earlier)
+    )(place, shifts, *pieces)
 
 def late_terms(place, layout, pieces, shifts, early, coarse, scale, planes, taps, rows, earlier):
     both, columns = early.shape
@@ -506,14 +506,14 @@
     earlier = jnp.concatenate([zeros, trunk[:-1]])
     shifts = jnp.concatenate([later, trunk, earlier], axis=1)
     to_beside, to_below, own_window = kernel_messages(place, line, trunk_grad, coarse)
-    ready = (slope, shifts, to_beside)
+    ready = (slope, shifts, to_beside, *crossing)
     top, bottom = after(beside[:half], *ready), after(below[half:], *ready)
     far_top, far_bottom = from_peer(top, "seq", 2), from_peer(bottom, "seq", 1)
 
     scale = 0.5 * float(fine * seqs * reps) ** (-0.5)
     near_rows = [(d, 0, coarse, 0) for d in range(3)]
     far_rows = [(3, 0, half, 0), (3, half, half, 0)]
-    early = early_terms(place, near_rows, [act, beside, below], shifts, coarse, crossing)
+    early = early_terms(place, near_rows, [act, beside, below], shifts, coarse)
     line_across[2] = after(line_across[2], early)
     lines = stack_planes(place, line_across)
     far_top, far_bottom = after(far_top, early), after(far_bottom, early)

time: 178 us -> 161 us (0.904)
  waiting for transfers between devices: 56.3 us -> 28.3 us
  local copies, waits for them, and re-layouts: 21.7 us -> 31.6 us
  Pallas kernels: 58.7 us -> 56.9 us
    ppermute x27, waiting for transfers between devices: 56.3 us -> 28.3 us  [from_peer(): return lax.ppermute(value, axis, [(i, i ^ distance) for i in range(peers)])]
    unnamed x52 -> x92, local copies, waits for them, and re-layouts: 11.6 us -> 19.2 us
    concatenate x1, other arithmetic: 2.98 us -> 5.38 us  [on_device_square(): shifts = jnp.concatenate([later, trunk, earlier], axis=1)]
  transfers between devices with their start and end apart: 27 -> 27, of which waited for: 5 -> 5; matrix products, arithmetic and copies ran while one was open for 10% -> 14% of each run, Pallas kernels for 33% -> 36%
where the time goes in v24:
time: 161 us; the launch traced here: 159 us
  Pallas kernels  56.9 us (35%)
  local copies, waits for them, and re-layouts  31.6 us (20%)
  starting transfers between devices  29 us (18%)
  waiting for transfers between devices  28.3 us (18%)
  other arithmetic  12.6 us (8%)
    ppermute x27, starting transfers between devices, from_peer(): return lax.ppermute(value, axis, [(i, i ^ distance) for i in range(peers)])  29 us
    ppermute x27, waiting for transfers between devices, from_peer(): return lax.ppermute(value, axis, [(i, i ^ distance) for i in range(peers)])  28.3 us
    pallas_call x2, Pallas kernels, gradient_stage(): pl.pallas_call(body, out_shape=out_shape, grid_spec=pltpu.PrefetchScalarG...  26.2 us
    unnamed x92, local copies, waits for them, and re-layouts  19.2 us
    pallas_call x1, Pallas kernels, early_terms(): pl.pallas_call(kernel, out_shape=jax.ShapeDtypeStruct((both, columns), jn...  13.9 us
    pallas_call x1, Pallas kernels, late_terms(): pl.pallas_call(kernel, out_shape=(jax.ShapeDtypeStruct(shape, jnp.float32...  9.9 us
    concatenate x1, other arithmetic, on_device_square(): shifts = jnp.concatenate([later, trunk, earlier], axis=1)  5.38 us
    slice x2, local copies, waits for them, and re-layouts, on_device_square(): top, bottom = (after(beside[:half], *ready), after(below[half:], *ready))  4.15 us
  transfers between devices with their start and end apart: 27, of which 5 were waited for; matrix products, arithmetic and copies ran while one was open for 14% of the time, Pallas kernels for 36%

profile of v24, /device:TPU:9, one launch (start us, length us, event | category | flops | bytes accessed | tf_op | source)
XLA Modules:
  0.0 159.2 jit_solution(1832976297935078764)
XLA Ops:
  0.6 1.0 slice.60.refs_0_
  1.6 1.4 collective-permute-start.1
  3.0 0.9 slice_bitcast_fusion.2
  3.9 1.3 collective-permute-start.3
  5.2 1.2 collective-permute-start.4
  6.6 2.2 %collective-permute-start = (bf16[3,96,384]{2,1,0:T(8,128)(2,1)S(1)}, bf16[3,96,384]{2,1,0:T(8,128)(2,1)S(1)}, u32[]{:S(2)}, u32[]{:S(2)}) collective-permute-start(bf16[3,96,384]{2,1,0:T(8,128)(2,1)S(1)} %slice.60.refs_0_), channel_id=1, source_target_pairs={{0,2},{1,3},{2,0},{3,1},{4,6},{5,7},{6,4},{7,5},{8,10},{9,11},{10,... | collective-permute-start | bytes 663560 | tf_op jit(solution)/shard_map/ppermute | solution.py:26
  8.8 1.4 copy-done.10
  10.2 1.8 %act.1.refs_0_ = bf16[512,1536]{1,0:T(8,128)(2,1)S(1)} custom-call(bf16[1,1024,768]{2,1,0:T(8,128)(2,1)S(1)} %copy-done.10), custom_call_target="tpu_custom_call" | custom-call | flops 1048576 | bytes 65536 | tf_op jit(solution)/shard_map/act/pallas_call | solution.py:85
  12.0 1.1 copy-done.3
  14.5 1.2 collective-permute-start.10
  15.7 1.2 collective-permute-start.6
  17.0 2.1 %slice_bitcast_fusion.1 = (bf16[2047,384]{1,0:T(8,128)(2,1)}, bf16[2047,384]{1,0:T(8,128)(2,1)}) fusion(bf16[1,2048,384]{2,1,0:T(8,128)(2,1)S(1)} %copy-done.2), kind=kLoop, calls=%fused_computation.7 | loop fusion | bytes 6288384 | tf_op jit(solution)/shard_map/slice | solution.py:505
  19.1 0.9 pad_maximum_fusion.1.refs_0_
  20.0 2.1 %collective-permute-done.2.refs_2_.refs_3_ = bf16[3,96,384]{2,1,0:T(8,128)(2,1)S(1)} collective-permute-done((bf16[3,96,384]{2,1,0:T(8,128)(2,1)S(1)}, bf16[3,96,384]{2,1,0:T(8,128)(2,1)S(1)}, u32[]{:S(2)}, u32[]{:S(2)}) %collective-permute-start.2) | collective-permute-done | bytes 221216 | tf_op jit(solution)/shard_map/ppermute | solution.py:26
  23.2 5.4 %fusion.2.refs_2_.shifts_ref = bf16[2048,1152]{1,0:T(8,128)(2,1)} fusion(bf16[2047,384]{1,0:T(8,128)(2,1)} %get-tuple-element.17, bf16[2047,384]{1,0:T(8,128)(2,1)} %get-tuple-element.16, bf16[2048,384]{1,0:T(8,128)(2,1)S(1)} %bitcast.14), kind=kLoop, calls=%fused_computation.4 | loop fusion | flops 23592960 | bytes 9435648 | tf_op jit(solution)/shard_map/concatenate | solution.py:507
  28.6 2.3 %half_slope.1.refs_1_.refs_11_ = f32[2,512,768]{2,1,0:T(8,128)S(1)} custom-call(bf16[1,1024,768]{2,1,0:T(8,128)(2,1)S(1)} %copy-done.11), custom_call_target="tpu_custom_call" | custom-call | tf_op jit(solution)/shard_map/half_slope/pallas_call | solution.py:167
  30.9 1.6 %copy-done.1 = f32[2,512,768]{2,1,0:T(8,128)} copy-done((f32[2,512,768]{2,1,0:T(8,128)}, f32[2,512,768]{2,1,0:T(8,128)S(1)}, u32[]{:S(2)}) %copy-start.1) | copy-done | bytes 3145752
  32.7 0.9 copy-done.25
  33.6 1.0 kernel_messages.1
  34.6 1.1 copy-done.5
  35.7 1.2 copy-done.12
  36.9 11.7 %collective-permute-done.10.refs_2_ = bf16[512,1536]{1,0:T(8,128)(2,1)} collective-permute-done((bf16[512,1536]{1,0:T(8,128)(2,1)}, bf16[512,1536]{1,0:T(8,128)(2,1)}, u32[]{:S(2)}, u32[]{:S(2)}) %collective-permute-start.10) | collective-permute-done | bytes 1572896 | tf_op jit(solution)/shard_map/ppermute | solution.py:26
  48.6 2.1 %slice.81.refs_0_ = bf16[256,1536]{1,0:T(8,128)(2,1)} slice(bf16[512,1536]{1,0:T(8,128)(2,1)} %collective-permute-done.10.refs_2_), slice={[256:512], [0:1536]} | slice | bytes 1572864 | tf_op jit(solution)/shard_map/slice | solution.py:510
  51.7 1.2 collective-permute-start.11
  52.9 2.1 %slice.80.refs_0_ = bf16[256,1536]{1,0:T(8,128)(2,1)} slice(bf16[512,1536]{1,0:T(8,128)(2,1)} %collective-permute-done.6.refs_1_), slice={[0:256], [0:1536]} | slice | bytes 1572864 | tf_op jit(solution)/shard_map/slice | solution.py:510
  55.0 1.2 collective-permute-start.9
  56.4 13.9 %weight_grad_early.1.refs_1_.early_ref = f32[1536,1152]{1,0:T(8,128)} custom-call(s32[2]{0:T(128)S(1)} %pad_add_fusion.place, bf16[2048,1152]{1,0:T(8,128)(2,1)} %fusion.2.refs_2_.shifts_ref, bf16[512,1536]{1,0:T(8,128)(2,1)S(1)} %copy-done.4, bf16[512,1536]{1,0:T(8,128)(2,1)} %collective-permute-done.6.refs_1_, ...), custom_call_target="tpu_custom_call" | custom-call | flops 1048576 | bytes 65536 | tf_op jit(solution)/shard_map/weight_grad_early/pallas_call | solution.py:213
  70.3 0.9 copy-done.6
  72.1 1.3 collective-permute-start.13
  74.8 1.8 %stack_planes.1.refs_9_.refs_10_.refs_11_.refs_5_ = bf16[4,4,2,96,384]{4,3,2,1,0:T(8,128)(2,1)S(1)} custom-call(s32[2]{0:T(128)S(1)} %pad_add_fusion.place, bf16[4,2,96,384]{3,2,1,0:T(8,128)(2,1)S(1)} %copy-done.14, bf16[4,2,96,384]{3,2,1,0:T(8,128)(2,1)S(1)} %copy-done.18, bf16[4,2,96,384]{3,2,1,0:T(8,128)(2,1)} %after.20.refs_2_, ...), custom_call_target="tpu_custom_call" | custom-call | flops 1048576 | bytes 65536 | tf_op jit(solution)/shard_map/stack_planes/pallas_call | solution.py:471
  76.6 4.3 %collective-permute-start.19 = (bf16[4,4,2,96,384]{4,3,2,1,0:T(8,128)(2,1)S(1)}, bf16[4,4,2,96,384]{4,3,2,1,0:T(8,128)(2,1)S(1)}, u32[]{:S(2)}, u32[]{:S(2)}) collective-permute-start(bf16[4,4,2,96,384]{4,3,2,1,0:T(8,128)(2,1)S(1)} %stack_planes.1.refs_9_.refs_10_.refs_11_.refs_5_), channel_id=1, source_target_pairs={{0,1},{1,0},{2,3},{3,2},{4,5},{5,4},{6,7},{7,6},{8,9},{9,8},{10,11... | collective-permute-start | bytes 7077896 | tf_op jit(solution)/shard_map/ppermute | solution.py:26
  80.9 9.9 %weight_grad_late.1 = (f32[4,5,96,384]{3,2,1,0:T(8,128)}, bf16[2,5,96,384]{3,2,1,0:T(8,128)(2,1)S(1)}, bf16[2,5,96,384]{3,2,1,0:T(8,128)(2,1)S(1)}) custom-call(s32[2]{0:T(128)S(1)} %pad_add_fusion.place, bf16[2048,1152]{1,0:T(8,128)(2,1)} %fusion.2.refs_2_.shifts_ref, f32[1536,1152]{1,0:T(8,128)} %weight_grad_early.1.refs_1_.early_ref, ...), custom_call_target="tpu_custom_call" | custom-call | flops 1048576 | bytes 65536 | tf_op jit(solution)/shard_map/weight_grad_late/pallas_call | solution.py:289
  91.6 1.8 %collective-permute-done.20 = bf16[2,5,96,384]{3,2,1,0:T(8,128)(2,1)S(1)} collective-permute-done((bf16[2,5,96,384]{3,2,1,0:T(8,128)(2,1)S(1)}, bf16[2,5,96,384]{3,2,1,0:T(8,128)(2,1)S(1)}, u32[]{:S(2)}, u32[]{:S(2)}) %collective-permute-start.20) | collective-permute-done | bytes 737312 | tf_op jit(solution)/shard_map/ppermute | solution.py:26
  93.8 10.1 %collective-permute-done.13.refs_2_.refs_7_ = bf16[21,96,384]{2,1,0:T(8,128)(2,1)} collective-permute-done((bf16[21,96,384]{2,1,0:T(8,128)(2,1)}, bf16[21,96,384]{2,1,0:T(8,128)(2,1)}, u32[]{:S(2)}, u32[]{:S(2)}) %collective-permute-start.13) | collective-permute-done | bytes 1548320 | tf_op jit(solution)/shard_map/ppermute | solution.py:26
  103.8 4.9 %collective-permute-start.17 = (bf16[21,96,384]{2,1,0:T(8,128)(2,1)}, bf16[21,96,384]{2,1,0:T(8,128)(2,1)S(1)}, u32[]{:S(2)}, u32[]{:S(2)}) collective-permute-start(bf16[21,96,384]{2,1,0:T(8,128)(2,1)} %collective-permute-done.13.refs_2_.refs_7_), channel_id=1, source_target_pairs={{0,1},{1,0},{2,3},{3,2},{4,5},{5,4},{6,7},{7,6},{8,9},{9,8},{10,11... | collective-permute-start | bytes 4644872 | tf_op jit(solution)/shard_map/ppermute | solution.py:26
  108.7 1.3 collective-permute-start.16
  110.0 1.8 %add_convert_fusion.2 = (bf16[1,5,96,384]{3,2,1,0:T(8,128)(2,1)S(1)}, bf16[1,5,96,384]{3,2,1,0:T(8,128)(2,1)S(1)}) fusion(f32[4,5,96,384]{3,2,1,0:T(8,128)} %get-tuple-element.11, bf16[2,5,96,384]{3,2,1,0:T(8,128)(2,1)S(1)} %collective-permute-done.20, bf16[2,5,96,384]{3,2,1,0:T(8,128)(2,1)S(1)} %collective-permute-done.21), kind=kLoop, calls=%fused_computation.12 | loop fusion | flops 1105920 | bytes 2949120 | tf_op jit(solution)/shard_map/convert_element_type | solution.py:46
  111.8 0.9 pad_maximum_fusion
  113.0 2.0 %slice.85 = bf16[9,96,384]{2,1,0:T(8,128)(2,1)} slice(bf16[21,96,384]{2,1,0:T(8,128)(2,1)} %collective-permute-done.13.refs_2_.refs_7_), slice={[6:15], [0:96], [0:384]} | slice | bytes 1327104 | tf_op jit(solution)/shard_map/slice | solution.py:550
  115.3 2.3 %slice.82 = bf16[9,96,384]{2,1,0:T(8,128)(2,1)} slice(bf16[21,96,384]{2,1,0:T(8,128)(2,1)} %collective-permute-done.12.refs_1_.refs_5_), slice={[0:9], [0:96], [0:384]} | slice | bytes 1327104 | tf_op jit(solution)/shard_map/slice | solution.py:549
  117.6 1.2 collective-permute-start.14
  119.0 0.9 copy-done.31
  120.6 14.4 %input_grad.2.refs_1_.refs_12_ = f32[2,512,768]{2,1,0:T(8,128)} custom-call(s32[2]{0:T(128)} %copy-done.26, bf16[6,96,384]{2,1,0:T(8,128)(2,1)} %copy-done.19, bf16[21,96,384]{2,1,0:T(8,128)(2,1)} %collective-permute-done.12.refs_1_.refs_5_, bf16[21,96,384]{2,1,0:T(8,128)(2,1)} %collective-permute-done.13.refs_2_.refs_7_, ...), custom_call_target="tpu_custom_call" | custom-call | flops 1048576 | bytes 65536 | tf_op jit(solution)/shard_map/input_grad/pallas_call | solution.py:447
  137.2 1.2 add_convert_fusion
  138.5 1.8 %collective-permute-start.26 = (bf16[1,5,96,384]{3,2,1,0:T(8,128)(2,1)S(1)}, bf16[1,5,96,384]{3,2,1,0:T(8,128)(2,1)S(1)}, u32[]{:S(2)}, u32[]{:S(2)}) collective-permute-start(bf16[1,5,96,384]{3,2,1,0:T(8,128)(2,1)S(1)} %add_convert_fusion), channel_id=1, source_target_pairs={{0,6},{1,7},{2,4},{3,5},{4,2},{5,3},{6,0},{7,1},{8,14},{9,15},{10,... | collective-permute-start | bytes 1105928 | tf_op jit(solution)/shard_map/ppermute | solution.py:26
  141.9 11.7 %input_grad.3.refs_1_ = bf16[1,1024,768]{2,1,0:T(8,128)(2,1)} custom-call(s32[2]{0:T(128)} %copy-done.26, bf16[6,96,384]{2,1,0:T(8,128)(2,1)} %copy-done.19, bf16[21,96,384]{2,1,0:T(8,128)(2,1)} %collective-permute-done.12.refs_1_.refs_5_, bf16[21,96,384]{2,1,0:T(8,128)(2,1)} %collective-permute-done.13.refs_2_.refs_7_, ...), custom_call_target="tpu_custom_call" | custom-call | flops 1048576 | bytes 65536 | tf_op jit(solution)/shard_map/input_grad/pallas_call | solution.py:447
  153.7 2.6 %collective-permute-done.26.refs_0_ = bf16[1,5,96,384]{3,2,1,0:T(8,128)(2,1)S(1)} collective-permute-done((bf16[1,5,96,384]{3,2,1,0:T(8,128)(2,1)S(1)}, bf16[1,5,96,384]{3,2,1,0:T(8,128)(2,1)S(1)}, u32[]{:S(2)}, u32[]{:S(2)}) %collective-permute-start.26) | collective-permute-done | bytes 368672 | tf_op jit(solution)/shard_map/ppermute | solution.py:26
  157.0 2.2 %add_bitcast_fusion = f32[5,96,384]{2,1,0:T(8,128)} fusion(bf16[1,5,96,384]{3,2,1,0:T(8,128)(2,1)} %after.23, f32[4,5,96,384]{3,2,1,0:T(8,128)} %get-tuple-element.11, bf16[2,5,96,384]{3,2,1,0:T(8,128)(2,1)S(1)} %copy-done.29, bf16[2,5,96,384]{3,2,1,0:T(8,128)(2,1)S(1)} %copy-done.35), kind=kLoop, calls=%fused_computation.9 | loop fusion | flops 1105920 | bytes 2580480 | tf_op jit(solution)/shard_map/add | solution.py:576
  (132 shorter events, 13.4 us)
Async XLA Ops:
  1.6 15.4 %collective-permute-start.1 = (bf16[3,96,384]{2,1,0:T(8,128)(2,1)S(1)}, bf16[3,96,384]{2,1,0:T(8,128)(2,1)S(1)}, u32[]{:S(2)}, u32[]{:S(2)}) collective-permute-start(bf16[3,96,384]{2,1,0:T(8,128)(2,1)S(1)} %slice.60.refs_0_), channel_id=1, source_target_pairs={{0,6},{1,7},{2,4},{3,5},{4,2},{5,3},{6,0},{7,1},{8,14},{9,15},{10,... | collective-permute-start | bytes 663560 | tf_op jit(solution)/shard_map/ppermute | solution.py:26
  3.9 9.2 %collective-permute-start.3 = (bf16[2,96,384]{2,1,0:T(8,128)(2,1)S(1)}, bf16[2,96,384]{2,1,0:T(8,128)(2,1)S(1)}, u32[]{:S(2)}, u32[]{:S(2)}) collective-permute-start(bf16[2,96,384]{2,1,0:T(8,128)(2,1)S(1)} %get-tuple-element.19), channel_id=1, source_target_pairs={{0,8},{8,0},{16,24},{24,16},{1,9},{9,1},{17,25},{25,17},{2,10},{10... | collective-permute-start | bytes 442376 | tf_op jit(solution)/shard_map/ppermute | solution.py:26
  5.2 8.0 %collective-permute-start.4 = (bf16[2,96,384]{2,1,0:T(8,128)(2,1)S(1)}, bf16[2,96,384]{2,1,0:T(8,128)(2,1)S(1)}, u32[]{:S(2)}, u32[]{:S(2)}) collective-permute-start(bf16[2,96,384]{2,1,0:T(8,128)(2,1)S(1)} %get-tuple-element.19), channel_id=1, source_target_pairs={{0,16},{8,24},{16,0},{24,8},{1,17},{9,25},{17,1},{25,9},{2,18},{10... | collective-permute-start | bytes 442376 | tf_op jit(solution)/shard_map/ppermute | solution.py:26
  6.4 6.7 %collective-permute-start.5 = (bf16[2,96,384]{2,1,0:T(8,128)(2,1)S(1)}, bf16[2,96,384]{2,1,0:T(8,128)(2,1)S(1)}, u32[]{:S(2)}, u32[]{:S(2)}) collective-permute-start(bf16[2,96,384]{2,1,0:T(8,128)(2,1)S(1)} %get-tuple-element.19), channel_id=1, source_target_pairs={{0,24},{8,16},{16,8},{24,0},{1,25},{9,17},{17,9},{25,1},{2,26},{10... | collective-permute-start | bytes 442376 | tf_op jit(solution)/shard_map/ppermute | solution.py:26
  6.6 13.4 %collective-permute-start = (bf16[3,96,384]{2,1,0:T(8,128)(2,1)S(1)}, bf16[3,96,384]{2,1,0:T(8,128)(2,1)S(1)}, u32[]{:S(2)}, u32[]{:S(2)}) collective-permute-start(bf16[3,96,384]{2,1,0:T(8,128)(2,1)S(1)} %slice.60.refs_0_), channel_id=1, source_target_pairs={{0,2},{1,3},{2,0},{3,1},{4,6},{5,7},{6,4},{7,5},{8,10},{9,11},{10,... | collective-permute-start | bytes 663560 | tf_op jit(solution)/shard_map/ppermute | solution.py:26
  13.1 3.8 %copy-start.2 = (bf16[1,2048,384]{2,1,0:T(8,128)(2,1)S(1)}, bf16[1,2048,384]{2,1,0:T(8,128)(2,1)}, u32[]{:S(2)}) copy-start(bf16[1,2048,384]{2,1,0:T(8,128)(2,1)} %refs_4_.1) | copy-start | bytes 4718596
  14.5 4.6 %copy-start.41 = (bf16[2,96,384]{2,1,0:T(8,128)(2,1)S(1)}, bf16[2,96,384]{2,1,0:T(8,128)(2,1)}, u32[]{:S(2)}) copy-start(bf16[2,96,384]{2,1,0:T(8,128)(2,1)} %copy-done.40) | copy-start | bytes 442372
  14.5 4.6 %copy-start.43 = (bf16[2,96,384]{2,1,0:T(8,128)(2,1)S(1)}, bf16[2,96,384]{2,1,0:T(8,128)(2,1)}, u32[]{:S(2)}) copy-start(bf16[2,96,384]{2,1,0:T(8,128)(2,1)} %copy-done.42) | copy-start | bytes 442372
  14.5 4.6 %copy-start.45 = (bf16[2,96,384]{2,1,0:T(8,128)(2,1)S(1)}, bf16[2,96,384]{2,1,0:T(8,128)(2,1)}, u32[]{:S(2)}) copy-start(bf16[2,96,384]{2,1,0:T(8,128)(2,1)} %copy-done.44) | copy-start | bytes 442372
  14.5 34.1 %collective-permute-start.10 = (bf16[512,1536]{1,0:T(8,128)(2,1)}, bf16[512,1536]{1,0:T(8,128)(2,1)}, u32[]{:S(2)}, u32[]{:S(2)}) collective-permute-start(bf16[512,1536]{1,0:T(8,128)(2,1)} %after.12.refs_1_.refs_0_), channel_id=1, source_target_pairs={{0,16},{8,24},{16,0},{24,8},{1,17},{9,25},{17,1},{25,9},{2,18},{10... | collective-permute-start | bytes 4718600 | tf_op jit(solution)/shard_map/ppermute | solution.py:26
  15.7 37.2 %collective-permute-start.6 = (bf16[512,1536]{1,0:T(8,128)(2,1)}, bf16[512,1536]{1,0:T(8,128)(2,1)}, u32[]{:S(2)}, u32[]{:S(2)}) collective-permute-start(bf16[512,1536]{1,0:T(8,128)(2,1)} %after.12.refs_1_.refs_0_), channel_id=1, source_target_pairs={{0,8},{8,0},{16,24},{24,16},{1,9},{9,1},{17,25},{25,17},{2,10},{10... | collective-permute-start | bytes 4718600 | tf_op jit(solution)/shard_map/ppermute | solution.py:26
  17.0 2.1 %copy-start.20 = (bf16[3,96,384]{2,1,0:T(8,128)(2,1)}, bf16[3,96,384]{2,1,0:T(8,128)(2,1)S(1)}, u32[]{:S(2)}) copy-start(bf16[3,96,384]{2,1,0:T(8,128)(2,1)S(1)} %collective-permute-done.1.refs_3_.refs_4_) | copy-start | bytes 663556
  17.0 5.2 %collective-permute-start.2 = (bf16[3,96,384]{2,1,0:T(8,128)(2,1)S(1)}, bf16[3,96,384]{2,1,0:T(8,128)(2,1)S(1)}, u32[]{:S(2)}, u32[]{:S(2)}) collective-permute-start(bf16[3,96,384]{2,1,0:T(8,128)(2,1)S(1)} %collective-permute-done.1.refs_3_.refs_4_), channel_id=1, source_target_pairs={{0,2},{1,3},{2,0},{3,1},{4,6},{5,7},{6,4},{7,5},{8,10},{9,11},{10,... | collective-permute-start | bytes 663560 | tf_op jit(solution)/shard_map/ppermute | solution.py:26
  20.0 2.1 %copy-start.22 = (bf16[3,96,384]{2,1,0:T(8,128)(2,1)}, bf16[3,96,384]{2,1,0:T(8,128)(2,1)S(1)}, u32[]{:S(2)}) copy-start(bf16[3,96,384]{2,1,0:T(8,128)(2,1)S(1)} %collective-permute-done.refs_1_.refs_2_) | copy-start | bytes 663556
  22.9 27.8 %collective-permute-start.8 = (bf16[4,2,96,384]{3,2,1,0:T(8,128)(2,1)}, bf16[4,2,96,384]{3,2,1,0:T(8,128)(2,1)S(1)}, u32[]{:S(2)}, u32[]{:S(2)}) collective-permute-start(bf16[4,2,96,384]{3,2,1,0:T(8,128)(2,1)} %after.13.refs_0_), channel_id=1, source_target_pairs={{0,6},{1,7},{2,4},{3,5},{4,2},{5,3},{6,0},{7,1},{8,14},{9,15},{10,... | collective-permute-start | bytes 1769480 | tf_op jit(solution)/shard_map/ppermute | solution.py:26
  22.9 27.8 %collective-permute-start.7 = (bf16[4,2,96,384]{3,2,1,0:T(8,128)(2,1)}, bf16[4,2,96,384]{3,2,1,0:T(8,128)(2,1)S(1)}, u32[]{:S(2)}, u32[]{:S(2)}) collective-permute-start(bf16[4,2,96,384]{3,2,1,0:T(8,128)(2,1)} %after.13.refs_0_), channel_id=1, source_target_pairs={{0,2},{1,3},{2,0},{3,1},{4,6},{5,7},{6,4},{7,5},{8,10},{9,11},{10,... | collective-permute-start | bytes 1769480 | tf_op jit(solution)/shard_map/ppermute | solution.py:26
  23.2 5.4 %copy-start.11 = (bf16[1,1024,768]{2,1,0:T(8,128)(2,1)S(1)}, bf16[1,1024,768]{2,1,0:T(8,128)(2,1)}, u32[]{:S(2)}) copy-start(bf16[1,1024,768]{2,1,0:T(8,128)(2,1)} %x_ref.3) | copy-start | bytes 4718596
  28.6 4.1 %copy-start.21 = (bf16[3,96,384]{2,1,0:T(8,128)(2,1)S(1)}, bf16[3,96,384]{2,1,0:T(8,128)(2,1)}, u32[]{:S(2)}) copy-start(bf16[3,96,384]{2,1,0:T(8,128)(2,1)} %copy-done.20) | copy-start | bytes 663556
  28.6 4.1 %copy-start.23 = (bf16[3,96,384]{2,1,0:T(8,128)(2,1)S(1)}, bf16[3,96,384]{2,1,0:T(8,128)(2,1)}, u32[]{:S(2)}) copy-start(bf16[3,96,384]{2,1,0:T(8,128)(2,1)} %copy-done.22) | copy-start | bytes 663556
  30.9 1.6 %copy-start.1 = (f32[2,512,768]{2,1,0:T(8,128)}, f32[2,512,768]{2,1,0:T(8,128)S(1)}, u32[]{:S(2)}) copy-start(f32[2,512,768]{2,1,0:T(8,128)S(1)} %half_slope.1.refs_1_.refs_11_) | copy-start | bytes 9437188
  33.6 47.3 %copy-start.26 = (s32[2]{0:T(128)}, s32[2]{0:T(128)S(1)}, u32[]{:S(2)}) copy-start(s32[2]{0:T(128)S(1)} %pad_add_fusion.place) | copy-start | bytes 28
  36.9 13.8 %copy-start.19 = (bf16[6,96,384]{2,1,0:T(8,128)(2,1)}, bf16[6,96,384]{2,1,0:T(8,128)(2,1)S(1)}, u32[]{:S(2)}) copy-start(bf16[6,96,384]{2,1,0:T(8,128)(2,1)S(1)} %get-tuple-element.8.refs_0_) | copy-start | bytes 1327108
  51.7 18.6 %collective-permute-start.11 = (bf16[256,1536]{1,0:T(8,128)(2,1)}, bf16[256,1536]{1,0:T(8,128)(2,1)S(1)}, u32[]{:S(2)}, u32[]{:S(2)}) collective-permute-start(bf16[256,1536]{1,0:T(8,128)(2,1)} %after.16), channel_id=1, source_target_pairs={{0,8},{8,0},{16,24},{24,16},{1,9},{9,1},{17,25},{25,17},{2,10},{10... | collective-permute-start | bytes 2359304 | tf_op jit(solution)/shard_map/ppermute | solution.py:26
  55.0 16.2 %collective-permute-start.9 = (bf16[256,1536]{1,0:T(8,128)(2,1)}, bf16[256,1536]{1,0:T(8,128)(2,1)S(1)}, u32[]{:S(2)}, u32[]{:S(2)}) collective-permute-start(bf16[256,1536]{1,0:T(8,128)(2,1)} %after.14), channel_id=1, source_target_pairs={{0,16},{8,24},{16,0},{24,8},{1,17},{9,25},{17,1},{25,9},{2,18},{10... | collective-permute-start | bytes 2359304 | tf_op jit(solution)/shard_map/ppermute | solution.py:26
  56.3 17.4 %collective-permute-start.18 = (bf16[4,2,96,384]{3,2,1,0:T(8,128)(2,1)}, bf16[4,2,96,384]{3,2,1,0:T(8,128)(2,1)}, u32[]{:S(2)}, u32[]{:S(2)}) collective-permute-start(bf16[4,2,96,384]{3,2,1,0:T(8,128)(2,1)} %copy-done.15), channel_id=1, source_target_pairs={{0,2},{1,3},{2,0},{3,1},{4,6},{5,7},{6,4},{7,5},{8,10},{9,11},{10,... | collective-permute-start | bytes 1769480 | tf_op jit(solution)/shard_map/ppermute | solution.py:26
  72.1 31.7 %collective-permute-start.13 = (bf16[21,96,384]{2,1,0:T(8,128)(2,1)}, bf16[21,96,384]{2,1,0:T(8,128)(2,1)}, u32[]{:S(2)}, u32[]{:S(2)}) collective-permute-start(bf16[21,96,384]{2,1,0:T(8,128)(2,1)} %after.19.refs_3_), channel_id=1, source_target_pairs={{0,16},{8,24},{16,0},{24,8},{1,17},{9,25},{17,1},{25,9},{2,18},{10... | collective-permute-start | bytes 4644872 | tf_op jit(solution)/shard_map/ppermute | solution.py:26
  73.4 35.3 %collective-permute-start.12 = (bf16[21,96,384]{2,1,0:T(8,128)(2,1)}, bf16[21,96,384]{2,1,0:T(8,128)(2,1)}, u32[]{:S(2)}, u32[]{:S(2)}) collective-permute-start(bf16[21,96,384]{2,1,0:T(8,128)(2,1)} %after.18), channel_id=1, source_target_pairs={{0,8},{8,0},{16,24},{24,16},{1,9},{9,1},{17,25},{25,17},{2,10},{10... | collective-permute-start | bytes 4644872 | tf_op jit(solution)/shard_map/ppermute | solution.py:26
  74.8 6.1 %copy-start.7 = (bf16[256,1536]{1,0:T(8,128)(2,1)S(1)}, bf16[256,1536]{1,0:T(8,128)(2,1)}, u32[]{:S(2)}) copy-start(bf16[256,1536]{1,0:T(8,128)(2,1)} %after.17.refs_2_.refs_1_) | copy-start | bytes 2359300
  74.8 6.1 %copy-start.9 = (bf16[256,1536]{1,0:T(8,128)(2,1)S(1)}, bf16[256,1536]{1,0:T(8,128)(2,1)}, u32[]{:S(2)}) copy-start(bf16[256,1536]{1,0:T(8,128)(2,1)} %after.15.refs_1_.refs_0_) | copy-start | bytes 2359300
  76.6 14.2 %copy-start = (bf16[4,4,2,96,384]{4,3,2,1,0:T(8,128)(2,1)}, bf16[4,4,2,96,384]{4,3,2,1,0:T(8,128)(2,1)S(1)}, u32[]{:S(2)}) copy-start(bf16[4,4,2,96,384]{4,3,2,1,0:T(8,128)(2,1)S(1)} %stack_planes.1.refs_9_.refs_10_.refs_11_.refs_5_) | copy-start | bytes 7077892
  76.6 14.9 %copy-start.13 = (bf16[21,96,384]{2,1,0:T(8,128)(2,1)S(1)}, bf16[21,96,384]{2,1,0:T(8,128)(2,1)}, u32[]{:S(2)}) copy-start(bf16[21,96,384]{2,1,0:T(8,128)(2,1)} %after.19.refs_3_) | copy-start | bytes 4644868
  76.6 41.0 %collective-permute-start.19 = (bf16[4,4,2,96,384]{4,3,2,1,0:T(8,128)(2,1)S(1)}, bf16[4,4,2,96,384]{4,3,2,1,0:T(8,128)(2,1)S(1)}, u32[]{:S(2)}, u32[]{:S(2)}) collective-permute-start(bf16[4,4,2,96,384]{4,3,2,1,0:T(8,128)(2,1)S(1)} %stack_planes.1.refs_9_.refs_10_.refs_11_.refs_5_), channel_id=1, source_target_pairs={{0,1},{1,0},{2,3},{3,2},{4,5},{5,4},{6,7},{7,6},{8,9},{9,8},{10,11... | collective-permute-start | bytes 7077896 | tf_op jit(solution)/shard_map/ppermute | solution.py:26
  90.9 2.5 %collective-permute-start.20 = (bf16[2,5,96,384]{3,2,1,0:T(8,128)(2,1)S(1)}, bf16[2,5,96,384]{3,2,1,0:T(8,128)(2,1)S(1)}, u32[]{:S(2)}, u32[]{:S(2)}) collective-permute-start(bf16[2,5,96,384]{3,2,1,0:T(8,128)(2,1)S(1)} %get-tuple-element.12), channel_id=1, source_target_pairs={{0,1},{1,0},{2,3},{3,2},{4,5},{5,4},{6,7},{7,6},{8,9},{9,8},{10,11... | collective-permute-start | bytes 2211848 | tf_op jit(solution)/shard_map/ppermute | solution.py:26
  91.5 23.5 %collective-permute-start.15 = (bf16[21,96,384]{2,1,0:T(8,128)(2,1)S(1)}, bf16[21,96,384]{2,1,0:T(8,128)(2,1)S(1)}, u32[]{:S(2)}, u32[]{:S(2)}) collective-permute-start(bf16[21,96,384]{2,1,0:T(8,128)(2,1)S(1)} %copy-done.13), channel_id=1, source_target_pairs={{0,1},{1,0},{2,3},{3,2},{4,5},{5,4},{6,7},{7,6},{8,9},{9,8},{10,11... | collective-permute-start | bytes 4644872 | tf_op jit(solution)/shard_map/ppermute | solution.py:26
  93.4 21.6 %copy-start.34 = (bf16[2,5,96,384]{3,2,1,0:T(8,128)(2,1)}, bf16[2,5,96,384]{3,2,1,0:T(8,128)(2,1)S(1)}, u32[]{:S(2)}) copy-start(bf16[2,5,96,384]{3,2,1,0:T(8,128)(2,1)S(1)} %collective-permute-done.20) | copy-start | bytes 2211844
  93.4 16.6 %collective-permute-start.21 = (bf16[2,5,96,384]{3,2,1,0:T(8,128)(2,1)S(1)}, bf16[2,5,96,384]{3,2,1,0:T(8,128)(2,1)S(1)}, u32[]{:S(2)}, u32[]{:S(2)}) collective-permute-start(bf16[2,5,96,384]{3,2,1,0:T(8,128)(2,1)S(1)} %get-tuple-element.13), channel_id=1, source_target_pairs={{0,1},{1,0},{2,3},{3,2},{4,5},{5,4},{6,7},{7,6},{8,9},{9,8},{10,11... | collective-permute-start | bytes 2211848 | tf_op jit(solution)/shard_map/ppermute | solution.py:26
  103.8 15.0 %collective-permute-start.17 = (bf16[21,96,384]{2,1,0:T(8,128)(2,1)}, bf16[21,96,384]{2,1,0:T(8,128)(2,1)S(1)}, u32[]{:S(2)}, u32[]{:S(2)}) collective-permute-start(bf16[21,96,384]{2,1,0:T(8,128)(2,1)} %collective-permute-done.13.refs_2_.refs_7_), channel_id=1, source_target_pairs={{0,1},{1,0},{2,3},{3,2},{4,5},{5,4},{6,7},{7,6},{8,9},{9,8},{10,11... | collective-permute-start | bytes 4644872 | tf_op jit(solution)/shard_map/ppermute | solution.py:26
  108.7 10.1 %collective-permute-start.16 = (bf16[21,96,384]{2,1,0:T(8,128)(2,1)}, bf16[21,96,384]{2,1,0:T(8,128)(2,1)S(1)}, u32[]{:S(2)}, u32[]{:S(2)}) collective-permute-start(bf16[21,96,384]{2,1,0:T(8,128)(2,1)} %collective-permute-done.12.refs_1_.refs_5_), channel_id=1, source_target_pairs={{0,1},{1,0},{2,3},{3,2},{4,5},{5,4},{6,7},{7,6},{8,9},{9,8},{10,11... | collective-permute-start | bytes 4644872 | tf_op jit(solution)/shard_map/ppermute | solution.py:26
  110.0 5.0 %copy-start.36 = (bf16[2,5,96,384]{3,2,1,0:T(8,128)(2,1)}, bf16[2,5,96,384]{3,2,1,0:T(8,128)(2,1)S(1)}, u32[]{:S(2)}) copy-start(bf16[2,5,96,384]{3,2,1,0:T(8,128)(2,1)S(1)} %collective-permute-done.21) | copy-start | bytes 2211844
  112.7 22.3 %collective-permute-start.22 = (bf16[2,5,96,384]{3,2,1,0:T(8,128)(2,1)}, bf16[2,5,96,384]{3,2,1,0:T(8,128)(2,1)S(1)}, u32[]{:S(2)}, u32[]{:S(2)}) collective-permute-start(bf16[2,5,96,384]{3,2,1,0:T(8,128)(2,1)} %pad_maximum_fusion), channel_id=1, source_target_pairs={{0,2},{1,3},{2,0},{3,1},{4,6},{5,7},{6,4},{7,5},{8,10},{9,11},{10,... | collective-permute-start | bytes 2211848 | tf_op jit(solution)/shard_map/ppermute | solution.py:26
  115.0 3.8 %copy-start.30 = (bf16[21,96,384]{2,1,0:T(8,128)(2,1)}, bf16[21,96,384]{2,1,0:T(8,128)(2,1)S(1)}, u32[]{:S(2)}) copy-start(bf16[21,96,384]{2,1,0:T(8,128)(2,1)S(1)} %collective-permute-done.15.refs_4_) | copy-start | bytes 4644868
  115.0 20.0 %collective-permute-start.23 = (bf16[9,96,384]{2,1,0:T(8,128)(2,1)}, bf16[9,96,384]{2,1,0:T(8,128)(2,1)}, u32[]{:S(2)}, u32[]{:S(2)}) collective-permute-start(bf16[9,96,384]{2,1,0:T(8,128)(2,1)} %slice.85), channel_id=1, source_target_pairs={{0,8},{8,0},{16,24},{24,16},{1,9},{9,1},{17,25},{25,17},{2,10},{10... | collective-permute-start | bytes 1990664 | tf_op jit(solution)/shard_map/ppermute | solution.py:26
  117.6 18.9 %collective-permute-start.14 = (bf16[9,96,384]{2,1,0:T(8,128)(2,1)}, bf16[9,96,384]{2,1,0:T(8,128)(2,1)}, u32[]{:S(2)}, u32[]{:S(2)}) collective-permute-start(bf16[9,96,384]{2,1,0:T(8,128)(2,1)} %slice.82), channel_id=1, source_target_pairs={{0,16},{8,24},{16,0},{24,8},{1,17},{9,25},{17,1},{25,9},{2,18},{10... | collective-permute-start | bytes 1990664 | tf_op jit(solution)/shard_map/ppermute | solution.py:26
  118.8 1.7 %copy-start.32 = (bf16[21,96,384]{2,1,0:T(8,128)(2,1)}, bf16[21,96,384]{2,1,0:T(8,128)(2,1)S(1)}, u32[]{:S(2)}) copy-start(bf16[21,96,384]{2,1,0:T(8,128)(2,1)S(1)} %collective-permute-done.16.refs_6_) | copy-start | bytes 4644868
  135.9 4.4 %collective-permute-start.25 = (bf16[9,96,384]{2,1,0:T(8,128)(2,1)}, bf16[9,96,384]{2,1,0:T(8,128)(2,1)S(1)}, u32[]{:S(2)}, u32[]{:S(2)}) collective-permute-start(bf16[9,96,384]{2,1,0:T(8,128)(2,1)} %after.22.refs_4_.refs_9_), channel_id=1, source_target_pairs={{0,1},{1,0},{2,3},{3,2},{4,5},{5,4},{6,7},{7,6},{8,9},{9,8},{10,11... | collective-permute-start | bytes 1990664 | tf_op jit(solution)/shard_map/ppermute | solution.py:26
  136.5 3.7 %collective-permute-start.24 = (bf16[9,96,384]{2,1,0:T(8,128)(2,1)}, bf16[9,96,384]{2,1,0:T(8,128)(2,1)S(1)}, u32[]{:S(2)}, u32[]{:S(2)}) collective-permute-start(bf16[9,96,384]{2,1,0:T(8,128)(2,1)} %after.21.refs_3_.refs_7_), channel_id=1, source_target_pairs={{0,1},{1,0},{2,3},{3,2},{4,5},{5,4},{6,7},{7,6},{8,9},{9,8},{10,11... | collective-permute-start | bytes 1990664 | tf_op jit(solution)/shard_map/ppermute | solution.py:26
  138.5 17.8 %collective-permute-start.26 = (bf16[1,5,96,384]{3,2,1,0:T(8,128)(2,1)S(1)}, bf16[1,5,96,384]{3,2,1,0:T(8,128)(2,1)S(1)}, u32[]{:S(2)}, u32[]{:S(2)}) collective-permute-start(bf16[1,5,96,384]{3,2,1,0:T(8,128)(2,1)S(1)} %add_convert_fusion), channel_id=1, source_target_pairs={{0,6},{1,7},{2,4},{3,5},{4,2},{5,3},{6,0},{7,1},{8,14},{9,15},{10,... | collective-permute-start | bytes 1105928 | tf_op jit(solution)/shard_map/ppermute | solution.py:26
  153.7 3.3 %copy-start.35 = (bf16[2,5,96,384]{3,2,1,0:T(8,128)(2,1)S(1)}, bf16[2,5,96,384]{3,2,1,0:T(8,128)(2,1)}, u32[]{:S(2)}) copy-start(bf16[2,5,96,384]{3,2,1,0:T(8,128)(2,1)} %copy-done.34) | copy-start | bytes 2211844
  (25 other events, 25.6 us)

commit v25 on v24

--- a/solution.py
+++ b/solution.py
@@ -378,8 +378,14 @@
         late = []
         if last:
             sums, slopes, strip, skips, sum_sems, skip_sems = refs[6:]
-            late.append(pltpu.make_async_copy(begun_ref, sums, sum_sems.at[0]))
-            late.append(pltpu.make_async_copy(slope_ref, slopes, sum_sems.at[1]))
+
+            def row_copies(n):
+                span = pl.ds(pl.multiple_of(n * 2 * STEP, 2 * STEP), 2 * STEP)
+                pairs = ((begun_ref, sums), (slope_ref, slopes))
+                for number, (source, target) in enumerate(pairs):
+                    sem = sum_sems.at[number, n]
+                    yield pltpu.make_async_copy(source.at[:, span], target.at[:, span], sem)
+
             late += window_copies(lambda d, span: skips.at[me ^ d, span], skip_sems)
         for copy in early:
             copy.start()
@@ -388,6 +394,10 @@
             copy.start()
         for copy in late:
             copy.start()
+        if last:
+            for n in range(coarse // (2 * STEP)):
+                for copy in row_copies(n):
+                    copy.start()
         for copy in early:
             copy.wait()
         for k in range(taps):
@@ -411,6 +421,13 @@
         def _(i):
             base = pl.multiple_of(i * STEP, STEP)
             spot, span = pl.ds(base, STEP), pl.ds(pl.multiple_of(2 * base, 2 * STEP), 2 * STEP)
+            if last:
+
+                @pl.when(i % 2 == 0)
+                def _():
+                    for copy in row_copies(i // 2):
+                        copy.wait()
+
             for c in range(width // LANES):
                 lanes = slice(c * LANES, (c + 1) * LANES)
                 if last:
@@ -441,7 +458,7 @@
             pltpu.VMEM(planar, jnp.float32),
             pltpu.VMEM((width // LANES, 2 * STEP, LANES), jnp.float32),
             pltpu.VMEM((seqs, window, block), jnp.bfloat16),
-            pltpu.SemaphoreType.DMA((2,)),
+            pltpu.SemaphoreType.DMA((2, coarse // (2 * STEP))),
             pltpu.SemaphoreType.DMA((len(parts), window // rows)),
         ]
     return pl.pallas_call(

time: 161 us -> 161 us (level)
  no operation moved by 1% of the time
where the time goes in v25:
time: 161 us; the launch traced here: 159 us
  Pallas kernels  57.8 us (36%)
  local copies, waits for them, and re-layouts  31.6 us (20%)
  starting transfers between devices  29 us (18%)
  waiting for transfers between devices  27.4 us (17%)
  other arithmetic  12.6 us (8%)
    ppermute x27, starting transfers between devices, from_peer(): return lax.ppermute(value, axis, [(i, i ^ distance) for i in range(peers)])  29 us
    ppermute x27, waiting for transfers between devices, from_peer(): return lax.ppermute(value, axis, [(i, i ^ distance) for i in range(peers)])  27.4 us
    pallas_call x2, Pallas kernels, gradient_stage(): pl.pallas_call(body, out_shape=out_shape, grid_spec=pltpu.PrefetchScalarG...  27.1 us
    unnamed x92, local copies, waits for them, and re-layouts  19.2 us
    pallas_call x1, Pallas kernels, early_terms(): pl.pallas_call(kernel, out_shape=jax.ShapeDtypeStruct((both, columns), jn...  13.9 us
    pallas_call x1, Pallas kernels, late_terms(): pl.pallas_call(kernel, out_shape=(jax.ShapeDtypeStruct(shape, jnp.float32...  9.9 us
    concatenate x1, other arithmetic, on_device_square(): shifts = jnp.concatenate([later, trunk, earlier], axis=1)  5.38 us
    slice x2, local copies, waits for them, and re-layouts, on_device_square(): top, bottom = (after(beside[:half], *ready), after(below[half:], *ready))  4.15 us
  transfers between devices with their start and end apart: 27, of which 5 were waited for; matrix products, arithmetic and copies ran while one was open for 14% of the time, Pallas kernels for 36%

profile of v25, /device:TPU:9, one launch (start us, length us, event | category | flops | bytes accessed | tf_op | source)
XLA Modules:
  0.0 159.2 jit_solution(2460498971324322770)
XLA Ops:
  0.6 1.0 slice.60.refs_0_
  1.6 1.4 collective-permute-start.1
  3.0 0.9 slice_bitcast_fusion.2
  3.9 1.3 collective-permute-start.3
  5.2 1.2 collective-permute-start.4
  6.6 2.2 %collective-permute-start = (bf16[3,96,384]{2,1,0:T(8,128)(2,1)S(1)}, bf16[3,96,384]{2,1,0:T(8,128)(2,1)S(1)}, u32[]{:S(2)}, u32[]{:S(2)}) collective-permute-start(bf16[3,96,384]{2,1,0:T(8,128)(2,1)S(1)} %slice.60.refs_0_), channel_id=1, source_target_pairs={{0,2},{1,3},{2,0},{3,1},{4,6},{5,7},{6,4},{7,5},{8,10},{9,11},{10,... | collective-permute-start | bytes 663560 | tf_op jit(solution)/shard_map/ppermute | solution.py:26
  8.8 1.4 copy-done.10
  10.2 1.8 %act.1.refs_0_ = bf16[512,1536]{1,0:T(8,128)(2,1)S(1)} custom-call(bf16[1,1024,768]{2,1,0:T(8,128)(2,1)S(1)} %copy-done.10), custom_call_target="tpu_custom_call" | custom-call | flops 1048576 | bytes 65536 | tf_op jit(solution)/shard_map/act/pallas_call | solution.py:85
  12.0 1.1 copy-done.3
  14.5 1.2 collective-permute-start.10
  15.7 1.2 collective-permute-start.6
  17.0 2.1 %slice_bitcast_fusion.1 = (bf16[2047,384]{1,0:T(8,128)(2,1)}, bf16[2047,384]{1,0:T(8,128)(2,1)}) fusion(bf16[1,2048,384]{2,1,0:T(8,128)(2,1)S(1)} %copy-done.2), kind=kLoop, calls=%fused_computation.7 | loop fusion | bytes 6288384 | tf_op jit(solution)/shard_map/slice | solution.py:522
  19.1 0.9 pad_maximum_fusion.1.refs_0_
  20.0 2.1 %collective-permute-done.2.refs_2_.refs_3_ = bf16[3,96,384]{2,1,0:T(8,128)(2,1)S(1)} collective-permute-done((bf16[3,96,384]{2,1,0:T(8,128)(2,1)S(1)}, bf16[3,96,384]{2,1,0:T(8,128)(2,1)S(1)}, u32[]{:S(2)}, u32[]{:S(2)}) %collective-permute-start.2) | collective-permute-done | bytes 221216 | tf_op jit(solution)/shard_map/ppermute | solution.py:26
  23.2 5.4 %fusion.2.refs_2_.shifts_ref = bf16[2048,1152]{1,0:T(8,128)(2,1)} fusion(bf16[2047,384]{1,0:T(8,128)(2,1)} %get-tuple-element.17, bf16[2047,384]{1,0:T(8,128)(2,1)} %get-tuple-element.16, bf16[2048,384]{1,0:T(8,128)(2,1)S(1)} %bitcast.14), kind=kLoop, calls=%fused_computation.4 | loop fusion | flops 23592960 | bytes 9435648 | tf_op jit(solution)/shard_map/concatenate | solution.py:524
  28.6 2.3 %half_slope.1.refs_1_.refs_11_ = f32[2,512,768]{2,1,0:T(8,128)S(1)} custom-call(bf16[1,1024,768]{2,1,0:T(8,128)(2,1)S(1)} %copy-done.11), custom_call_target="tpu_custom_call" | custom-call | tf_op jit(solution)/shard_map/half_slope/pallas_call | solution.py:167
  30.9 1.6 %copy-done.1 = f32[2,512,768]{2,1,0:T(8,128)} copy-done((f32[2,512,768]{2,1,0:T(8,128)}, f32[2,512,768]{2,1,0:T(8,128)S(1)}, u32[]{:S(2)}) %copy-start.1) | copy-done | bytes 3145752
  32.7 0.9 copy-done.25
  33.6 1.0 kernel_messages.1
  34.6 1.1 copy-done.5
  35.7 1.2 copy-done.12
  36.9 11.7 %collective-permute-done.10.refs_2_ = bf16[512,1536]{1,0:T(8,128)(2,1)} collective-permute-done((bf16[512,1536]{1,0:T(8,128)(2,1)}, bf16[512,1536]{1,0:T(8,128)(2,1)}, u32[]{:S(2)}, u32[]{:S(2)}) %collective-permute-start.10) | collective-permute-done | bytes 1572896 | tf_op jit(solution)/shard_map/ppermute | solution.py:26
  48.6 2.1 %slice.81.refs_0_ = bf16[256,1536]{1,0:T(8,128)(2,1)} slice(bf16[512,1536]{1,0:T(8,128)(2,1)} %collective-permute-done.10.refs_2_), slice={[256:512], [0:1536]} | slice | bytes 1572864 | tf_op jit(solution)/shard_map/slice | solution.py:527
  51.7 1.2 collective-permute-start.11
  52.9 2.1 %slice.80.refs_0_ = bf16[256,1536]{1,0:T(8,128)(2,1)} slice(bf16[512,1536]{1,0:T(8,128)(2,1)} %collective-permute-done.6.refs_1_), slice={[0:256], [0:1536]} | slice | bytes 1572864 | tf_op jit(solution)/shard_map/slice | solution.py:527
  55.0 1.2 collective-permute-start.9
  56.4 13.9 %weight_grad_early.1.refs_1_.early_ref = f32[1536,1152]{1,0:T(8,128)} custom-call(s32[2]{0:T(128)S(1)} %pad_add_fusion.place, bf16[2048,1152]{1,0:T(8,128)(2,1)} %fusion.2.refs_2_.shifts_ref, bf16[512,1536]{1,0:T(8,128)(2,1)S(1)} %copy-done.4, bf16[512,1536]{1,0:T(8,128)(2,1)} %collective-permute-done.6.refs_1_, ...), custom_call_target="tpu_custom_call" | custom-call | flops 1048576 | bytes 65536 | tf_op jit(solution)/shard_map/weight_grad_early/pallas_call | solution.py:213
  70.3 0.9 copy-done.6
  72.1 1.3 collective-permute-start.13
  74.8 1.8 %stack_planes.1.refs_9_.refs_10_.refs_11_.refs_5_ = bf16[4,4,2,96,384]{4,3,2,1,0:T(8,128)(2,1)S(1)} custom-call(s32[2]{0:T(128)S(1)} %pad_add_fusion.place, bf16[4,2,96,384]{3,2,1,0:T(8,128)(2,1)S(1)} %copy-done.14, bf16[4,2,96,384]{3,2,1,0:T(8,128)(2,1)S(1)} %copy-done.18, bf16[4,2,96,384]{3,2,1,0:T(8,128)(2,1)} %after.20.refs_2_, ...), custom_call_target="tpu_custom_call" | custom-call | flops 1048576 | bytes 65536 | tf_op jit(solution)/shard_map/stack_planes/pallas_call | solution.py:488
  76.6 4.3 %collective-permute-start.19 = (bf16[4,4,2,96,384]{4,3,2,1,0:T(8,128)(2,1)S(1)}, bf16[4,4,2,96,384]{4,3,2,1,0:T(8,128)(2,1)S(1)}, u32[]{:S(2)}, u32[]{:S(2)}) collective-permute-start(bf16[4,4,2,96,384]{4,3,2,1,0:T(8,128)(2,1)S(1)} %stack_planes.1.refs_9_.refs_10_.refs_11_.refs_5_), channel_id=1, source_target_pairs={{0,1},{1,0},{2,3},{3,2},{4,5},{5,4},{6,7},{7,6},{8,9},{9,8},{10,11... | collective-permute-start | bytes 7077896 | tf_op jit(solution)/shard_map/ppermute | solution.py:26
  80.9 9.9 %weight_grad_late.1 = (f32[4,5,96,384]{3,2,1,0:T(8,128)}, bf16[2,5,96,384]{3,2,1,0:T(8,128)(2,1)S(1)}, bf16[2,5,96,384]{3,2,1,0:T(8,128)(2,1)S(1)}) custom-call(s32[2]{0:T(128)S(1)} %pad_add_fusion.place, bf16[2048,1152]{1,0:T(8,128)(2,1)} %fusion.2.refs_2_.shifts_ref, f32[1536,1152]{1,0:T(8,128)} %weight_grad_early.1.refs_1_.early_ref, ...), custom_call_target="tpu_custom_call" | custom-call | flops 1048576 | bytes 65536 | tf_op jit(solution)/shard_map/weight_grad_late/pallas_call | solution.py:289
  91.6 1.8 %collective-permute-done.20 = bf16[2,5,96,384]{3,2,1,0:T(8,128)(2,1)S(1)} collective-permute-done((bf16[2,5,96,384]{3,2,1,0:T(8,128)(2,1)S(1)}, bf16[2,5,96,384]{3,2,1,0:T(8,128)(2,1)S(1)}, u32[]{:S(2)}, u32[]{:S(2)}) %collective-permute-start.20) | collective-permute-done | bytes 737312 | tf_op jit(solution)/shard_map/ppermute | solution.py:26
  93.8 10.1 %collective-permute-done.13.refs_2_.refs_7_ = bf16[21,96,384]{2,1,0:T(8,128)(2,1)} collective-permute-done((bf16[21,96,384]{2,1,0:T(8,128)(2,1)}, bf16[21,96,384]{2,1,0:T(8,128)(2,1)}, u32[]{:S(2)}, u32[]{:S(2)}) %collective-permute-start.13) | collective-permute-done | bytes 1548320 | tf_op jit(solution)/shard_map/ppermute | solution.py:26
  103.8 4.9 %collective-permute-start.17 = (bf16[21,96,384]{2,1,0:T(8,128)(2,1)}, bf16[21,96,384]{2,1,0:T(8,128)(2,1)S(1)}, u32[]{:S(2)}, u32[]{:S(2)}) collective-permute-start(bf16[21,96,384]{2,1,0:T(8,128)(2,1)} %collective-permute-done.13.refs_2_.refs_7_), channel_id=1, source_target_pairs={{0,1},{1,0},{2,3},{3,2},{4,5},{5,4},{6,7},{7,6},{8,9},{9,8},{10,11... | collective-permute-start | bytes 4644872 | tf_op jit(solution)/shard_map/ppermute | solution.py:26
  108.7 1.3 collective-permute-start.16
  110.0 1.8 %add_convert_fusion.2 = (bf16[1,5,96,384]{3,2,1,0:T(8,128)(2,1)S(1)}, bf16[1,5,96,384]{3,2,1,0:T(8,128)(2,1)S(1)}) fusion(f32[4,5,96,384]{3,2,1,0:T(8,128)} %get-tuple-element.11, bf16[2,5,96,384]{3,2,1,0:T(8,128)(2,1)S(1)} %collective-permute-done.20, bf16[2,5,96,384]{3,2,1,0:T(8,128)(2,1)S(1)} %collective-permute-done.21), kind=kLoop, calls=%fused_computation.12 | loop fusion | flops 1105920 | bytes 2949120 | tf_op jit(solution)/shard_map/convert_element_type | solution.py:46
  111.8 0.9 pad_maximum_fusion
  113.0 2.0 %slice.85 = bf16[9,96,384]{2,1,0:T(8,128)(2,1)} slice(bf16[21,96,384]{2,1,0:T(8,128)(2,1)} %collective-permute-done.13.refs_2_.refs_7_), slice={[6:15], [0:96], [0:384]} | slice | bytes 1327104 | tf_op jit(solution)/shard_map/slice | solution.py:567
  115.3 2.3 %slice.82 = bf16[9,96,384]{2,1,0:T(8,128)(2,1)} slice(bf16[21,96,384]{2,1,0:T(8,128)(2,1)} %collective-permute-done.12.refs_1_.refs_5_), slice={[0:9], [0:96], [0:384]} | slice | bytes 1327104 | tf_op jit(solution)/shard_map/slice | solution.py:566
  117.6 1.2 collective-permute-start.14
  119.0 0.9 copy-done.31
  120.6 14.4 %input_grad.2.refs_1_.refs_12_ = f32[2,512,768]{2,1,0:T(8,128)} custom-call(s32[2]{0:T(128)} %copy-done.26, bf16[6,96,384]{2,1,0:T(8,128)(2,1)} %copy-done.19, bf16[21,96,384]{2,1,0:T(8,128)(2,1)} %collective-permute-done.12.refs_1_.refs_5_, bf16[21,96,384]{2,1,0:T(8,128)(2,1)} %collective-permute-done.13.refs_2_.refs_7_, ...), custom_call_target="tpu_custom_call" | custom-call | flops 1048576 | bytes 65536 | tf_op jit(solution)/shard_map/input_grad/pallas_call | solution.py:464
  137.2 1.2 add_convert_fusion
  138.5 1.8 %collective-permute-start.26 = (bf16[1,5,96,384]{3,2,1,0:T(8,128)(2,1)S(1)}, bf16[1,5,96,384]{3,2,1,0:T(8,128)(2,1)S(1)}, u32[]{:S(2)}, u32[]{:S(2)}) collective-permute-start(bf16[1,5,96,384]{3,2,1,0:T(8,128)(2,1)S(1)} %add_convert_fusion), channel_id=1, source_target_pairs={{0,6},{1,7},{2,4},{3,5},{4,2},{5,3},{6,0},{7,1},{8,14},{9,15},{10,... | collective-permute-start | bytes 1105928 | tf_op jit(solution)/shard_map/ppermute | solution.py:26
  141.9 12.6 %input_grad.3.refs_1_ = bf16[1,1024,768]{2,1,0:T(8,128)(2,1)} custom-call(s32[2]{0:T(128)} %copy-done.26, bf16[6,96,384]{2,1,0:T(8,128)(2,1)} %copy-done.19, bf16[21,96,384]{2,1,0:T(8,128)(2,1)} %collective-permute-done.12.refs_1_.refs_5_, bf16[21,96,384]{2,1,0:T(8,128)(2,1)} %collective-permute-done.13.refs_2_.refs_7_, ...), custom_call_target="tpu_custom_call" | custom-call | flops 1048576 | bytes 65536 | tf_op jit(solution)/shard_map/input_grad/pallas_call | solution.py:464
  154.6 1.7 %collective-permute-done.26.refs_0_ = bf16[1,5,96,384]{3,2,1,0:T(8,128)(2,1)S(1)} collective-permute-done((bf16[1,5,96,384]{3,2,1,0:T(8,128)(2,1)S(1)}, bf16[1,5,96,384]{3,2,1,0:T(8,128)(2,1)S(1)}, u32[]{:S(2)}, u32[]{:S(2)}) %collective-permute-start.26) | collective-permute-done | bytes 368672 | tf_op jit(solution)/shard_map/ppermute | solution.py:26
  157.0 2.2 %add_bitcast_fusion = f32[5,96,384]{2,1,0:T(8,128)} fusion(bf16[1,5,96,384]{3,2,1,0:T(8,128)(2,1)} %after.23, f32[4,5,96,384]{3,2,1,0:T(8,128)} %get-tuple-element.11, bf16[2,5,96,384]{3,2,1,0:T(8,128)(2,1)S(1)} %copy-done.29, bf16[2,5,96,384]{3,2,1,0:T(8,128)(2,1)S(1)} %copy-done.35), kind=kLoop, calls=%fused_computation.9 | loop fusion | flops 1105920 | bytes 2580480 | tf_op jit(solution)/shard_map/add | solution.py:593
  (132 shorter events, 13.4 us)
Async XLA Ops:
  1.6 15.4 %collective-permute-start.1 = (bf16[3,96,384]{2,1,0:T(8,128)(2,1)S(1)}, bf16[3,96,384]{2,1,0:T(8,128)(2,1)S(1)}, u32[]{:S(2)}, u32[]{:S(2)}) collective-permute-start(bf16[3,96,384]{2,1,0:T(8,128)(2,1)S(1)} %slice.60.refs_0_), channel_id=1, source_target_pairs={{0,6},{1,7},{2,4},{3,5},{4,2},{5,3},{6,0},{7,1},{8,14},{9,15},{10,... | collective-permute-start | bytes 663560 | tf_op jit(solution)/shard_map/ppermute | solution.py:26
  3.9 9.2 %collective-permute-start.3 = (bf16[2,96,384]{2,1,0:T(8,128)(2,1)S(1)}, bf16[2,96,384]{2,1,0:T(8,128)(2,1)S(1)}, u32[]{:S(2)}, u32[]{:S(2)}) collective-permute-start(bf16[2,96,384]{2,1,0:T(8,128)(2,1)S(1)} %get-tuple-element.19), channel_id=1, source_target_pairs={{0,8},{8,0},{16,24},{24,16},{1,9},{9,1},{17,25},{25,17},{2,10},{10... | collective-permute-start | bytes 442376 | tf_op jit(solution)/shard_map/ppermute | solution.py:26
  5.2 8.0 %collective-permute-start.4 = (bf16[2,96,384]{2,1,0:T(8,128)(2,1)S(1)}, bf16[2,96,384]{2,1,0:T(8,128)(2,1)S(1)}, u32[]{:S(2)}, u32[]{:S(2)}) collective-permute-start(bf16[2,96,384]{2,1,0:T(8,128)(2,1)S(1)} %get-tuple-element.19), channel_id=1, source_target_pairs={{0,16},{8,24},{16,0},{24,8},{1,17},{9,25},{17,1},{25,9},{2,18},{10... | collective-permute-start | bytes 442376 | tf_op jit(solution)/shard_map/ppermute | solution.py:26
  6.4 6.7 %collective-permute-start.5 = (bf16[2,96,384]{2,1,0:T(8,128)(2,1)S(1)}, bf16[2,96,384]{2,1,0:T(8,128)(2,1)S(1)}, u32[]{:S(2)}, u32[]{:S(2)}) collective-permute-start(bf16[2,96,384]{2,1,0:T(8,128)(2,1)S(1)} %get-tuple-element.19), channel_id=1, source_target_pairs={{0,24},{8,16},{16,8},{24,0},{1,25},{9,17},{17,9},{25,1},{2,26},{10... | collective-permute-start | bytes 442376 | tf_op jit(solution)/shard_map/ppermute | solution.py:26
  6.6 13.4 %collective-permute-start = (bf16[3,96,384]{2,1,0:T(8,128)(2,1)S(1)}, bf16[3,96,384]{2,1,0:T(8,128)(2,1)S(1)}, u32[]{:S(2)}, u32[]{:S(2)}) collective-permute-start(bf16[3,96,384]{2,1,0:T(8,128)(2,1)S(1)} %slice.60.refs_0_), channel_id=1, source_target_pairs={{0,2},{1,3},{2,0},{3,1},{4,6},{5,7},{6,4},{7,5},{8,10},{9,11},{10,... | collective-permute-start | bytes 663560 | tf_op jit(solution)/shard_map/ppermute | solution.py:26
  13.1 3.8 %copy-start.2 = (bf16[1,2048,384]{2,1,0:T(8,128)(2,1)S(1)}, bf16[1,2048,384]{2,1,0:T(8,128)(2,1)}, u32[]{:S(2)}) copy-start(bf16[1,2048,384]{2,1,0:T(8,128)(2,1)} %refs_4_.1) | copy-start | bytes 4718596
  14.5 4.6 %copy-start.41 = (bf16[2,96,384]{2,1,0:T(8,128)(2,1)S(1)}, bf16[2,96,384]{2,1,0:T(8,128)(2,1)}, u32[]{:S(2)}) copy-start(bf16[2,96,384]{2,1,0:T(8,128)(2,1)} %copy-done.40) | copy-start | bytes 442372
  14.5 4.6 %copy-start.43 = (bf16[2,96,384]{2,1,0:T(8,128)(2,1)S(1)}, bf16[2,96,384]{2,1,0:T(8,128)(2,1)}, u32[]{:S(2)}) copy-start(bf16[2,96,384]{2,1,0:T(8,128)(2,1)} %copy-done.42) | copy-start | bytes 442372
  14.5 4.6 %copy-start.45 = (bf16[2,96,384]{2,1,0:T(8,128)(2,1)S(1)}, bf16[2,96,384]{2,1,0:T(8,128)(2,1)}, u32[]{:S(2)}) copy-start(bf16[2,96,384]{2,1,0:T(8,128)(2,1)} %copy-done.44) | copy-start | bytes 442372
  14.5 34.1 %collective-permute-start.10 = (bf16[512,1536]{1,0:T(8,128)(2,1)}, bf16[512,1536]{1,0:T(8,128)(2,1)}, u32[]{:S(2)}, u32[]{:S(2)}) collective-permute-start(bf16[512,1536]{1,0:T(8,128)(2,1)} %after.12.refs_1_.refs_0_), channel_id=1, source_target_pairs={{0,16},{8,24},{16,0},{24,8},{1,17},{9,25},{17,1},{25,9},{2,18},{10... | collective-permute-start | bytes 4718600 | tf_op jit(solution)/shard_map/ppermute | solution.py:26
  15.7 37.2 %collective-permute-start.6 = (bf16[512,1536]{1,0:T(8,128)(2,1)}, bf16[512,1536]{1,0:T(8,128)(2,1)}, u32[]{:S(2)}, u32[]{:S(2)}) collective-permute-start(bf16[512,1536]{1,0:T(8,128)(2,1)} %after.12.refs_1_.refs_0_), channel_id=1, source_target_pairs={{0,8},{8,0},{16,24},{24,16},{1,9},{9,1},{17,25},{25,17},{2,10},{10... | collective-permute-start | bytes 4718600 | tf_op jit(solution)/shard_map/ppermute | solution.py:26
  17.0 2.1 %copy-start.20 = (bf16[3,96,384]{2,1,0:T(8,128)(2,1)}, bf16[3,96,384]{2,1,0:T(8,128)(2,1)S(1)}, u32[]{:S(2)}) copy-start(bf16[3,96,384]{2,1,0:T(8,128)(2,1)S(1)} %collective-permute-done.1.refs_3_.refs_4_) | copy-start | bytes 663556
  17.0 5.2 %collective-permute-start.2 = (bf16[3,96,384]{2,1,0:T(8,128)(2,1)S(1)}, bf16[3,96,384]{2,1,0:T(8,128)(2,1)S(1)}, u32[]{:S(2)}, u32[]{:S(2)}) collective-permute-start(bf16[3,96,384]{2,1,0:T(8,128)(2,1)S(1)} %collective-permute-done.1.refs_3_.refs_4_), channel_id=1, source_target_pairs={{0,2},{1,3},{2,0},{3,1},{4,6},{5,7},{6,4},{7,5},{8,10},{9,11},{10,... | collective-permute-start | bytes 663560 | tf_op jit(solution)/shard_map/ppermute | solution.py:26
  20.0 2.1 %copy-start.22 = (bf16[3,96,384]{2,1,0:T(8,128)(2,1)}, bf16[3,96,384]{2,1,0:T(8,128)(2,1)S(1)}, u32[]{:S(2)}) copy-start(bf16[3,96,384]{2,1,0:T(8,128)(2,1)S(1)} %collective-permute-done.refs_1_.refs_2_) | copy-start | bytes 663556
  22.9 27.8 %collective-permute-start.8 = (bf16[4,2,96,384]{3,2,1,0:T(8,128)(2,1)}, bf16[4,2,96,384]{3,2,1,0:T(8,128)(2,1)S(1)}, u32[]{:S(2)}, u32[]{:S(2)}) collective-permute-start(bf16[4,2,96,384]{3,2,1,0:T(8,128)(2,1)} %after.13.refs_0_), channel_id=1, source_target_pairs={{0,6},{1,7},{2,4},{3,5},{4,2},{5,3},{6,0},{7,1},{8,14},{9,15},{10,... | collective-permute-start | bytes 1769480 | tf_op jit(solution)/shard_map/ppermute | solution.py:26
  22.9 27.8 %collective-permute-start.7 = (bf16[4,2,96,384]{3,2,1,0:T(8,128)(2,1)}, bf16[4,2,96,384]{3,2,1,0:T(8,128)(2,1)S(1)}, u32[]{:S(2)}, u32[]{:S(2)}) collective-permute-start(bf16[4,2,96,384]{3,2,1,0:T(8,128)(2,1)} %after.13.refs_0_), channel_id=1, source_target_pairs={{0,2},{1,3},{2,0},{3,1},{4,6},{5,7},{6,4},{7,5},{8,10},{9,11},{10,... | collective-permute-start | bytes 1769480 | tf_op jit(solution)/shard_map/ppermute | solution.py:26
  23.2 5.4 %copy-start.11 = (bf16[1,1024,768]{2,1,0:T(8,128)(2,1)S(1)}, bf16[1,1024,768]{2,1,0:T(8,128)(2,1)}, u32[]{:S(2)}) copy-start(bf16[1,1024,768]{2,1,0:T(8,128)(2,1)} %x_ref.3) | copy-start | bytes 4718596
  28.6 4.1 %copy-start.21 = (bf16[3,96,384]{2,1,0:T(8,128)(2,1)S(1)}, bf16[3,96,384]{2,1,0:T(8,128)(2,1)}, u32[]{:S(2)}) copy-start(bf16[3,96,384]{2,1,0:T(8,128)(2,1)} %copy-done.20) | copy-start | bytes 663556
  28.6 4.1 %copy-start.23 = (bf16[3,96,384]{2,1,0:T(8,128)(2,1)S(1)}, bf16[3,96,384]{2,1,0:T(8,128)(2,1)}, u32[]{:S(2)}) copy-start(bf16[3,96,384]{2,1,0:T(8,128)(2,1)} %copy-done.22) | copy-start | bytes 663556
  30.9 1.6 %copy-start.1 = (f32[2,512,768]{2,1,0:T(8,128)}, f32[2,512,768]{2,1,0:T(8,128)S(1)}, u32[]{:S(2)}) copy-start(f32[2,512,768]{2,1,0:T(8,128)S(1)} %half_slope.1.refs_1_.refs_11_) | copy-start | bytes 9437188
  33.6 47.3 %copy-start.26 = (s32[2]{0:T(128)}, s32[2]{0:T(128)S(1)}, u32[]{:S(2)}) copy-start(s32[2]{0:T(128)S(1)} %pad_add_fusion.place) | copy-start | bytes 28
  36.9 13.8 %copy-start.19 = (bf16[6,96,384]{2,1,0:T(8,128)(2,1)}, bf16[6,96,384]{2,1,0:T(8,128)(2,1)S(1)}, u32[]{:S(2)}) copy-start(bf16[6,96,384]{2,1,0:T(8,128)(2,1)S(1)} %get-tuple-element.8.refs_0_) | copy-start | bytes 1327108
  51.7 18.6 %collective-permute-start.11 = (bf16[256,1536]{1,0:T(8,128)(2,1)}, bf16[256,1536]{1,0:T(8,128)(2,1)S(1)}, u32[]{:S(2)}, u32[]{:S(2)}) collective-permute-start(bf16[256,1536]{1,0:T(8,128)(2,1)} %after.16), channel_id=1, source_target_pairs={{0,8},{8,0},{16,24},{24,16},{1,9},{9,1},{17,25},{25,17},{2,10},{10... | collective-permute-start | bytes 2359304 | tf_op jit(solution)/shard_map/ppermute | solution.py:26
  55.0 16.2 %collective-permute-start.9 = (bf16[256,1536]{1,0:T(8,128)(2,1)}, bf16[256,1536]{1,0:T(8,128)(2,1)S(1)}, u32[]{:S(2)}, u32[]{:S(2)}) collective-permute-start(bf16[256,1536]{1,0:T(8,128)(2,1)} %after.14), channel_id=1, source_target_pairs={{0,16},{8,24},{16,0},{24,8},{1,17},{9,25},{17,1},{25,9},{2,18},{10... | collective-permute-start | bytes 2359304 | tf_op jit(solution)/shard_map/ppermute | solution.py:26
  56.3 17.4 %collective-permute-start.18 = (bf16[4,2,96,384]{3,2,1,0:T(8,128)(2,1)}, bf16[4,2,96,384]{3,2,1,0:T(8,128)(2,1)}, u32[]{:S(2)}, u32[]{:S(2)}) collective-permute-start(bf16[4,2,96,384]{3,2,1,0:T(8,128)(2,1)} %copy-done.15), channel_id=1, source_target_pairs={{0,2},{1,3},{2,0},{3,1},{4,6},{5,7},{6,4},{7,5},{8,10},{9,11},{10,... | collective-permute-start | bytes 1769480 | tf_op jit(solution)/shard_map/ppermute | solution.py:26
  72.1 31.7 %collective-permute-start.13 = (bf16[21,96,384]{2,1,0:T(8,128)(2,1)}, bf16[21,96,384]{2,1,0:T(8,128)(2,1)}, u32[]{:S(2)}, u32[]{:S(2)}) collective-permute-start(bf16[21,96,384]{2,1,0:T(8,128)(2,1)} %after.19.refs_3_), channel_id=1, source_target_pairs={{0,16},{8,24},{16,0},{24,8},{1,17},{9,25},{17,1},{25,9},{2,18},{10... | collective-permute-start | bytes 4644872 | tf_op jit(solution)/shard_map/ppermute | solution.py:26
  73.4 35.3 %collective-permute-start.12 = (bf16[21,96,384]{2,1,0:T(8,128)(2,1)}, bf16[21,96,384]{2,1,0:T(8,128)(2,1)}, u32[]{:S(2)}, u32[]{:S(2)}) collective-permute-start(bf16[21,96,384]{2,1,0:T(8,128)(2,1)} %after.18), channel_id=1, source_target_pairs={{0,8},{8,0},{16,24},{24,16},{1,9},{9,1},{17,25},{25,17},{2,10},{10... | collective-permute-start | bytes 4644872 | tf_op jit(solution)/shard_map/ppermute | solution.py:26
  74.8 6.1 %copy-start.7 = (bf16[256,1536]{1,0:T(8,128)(2,1)S(1)}, bf16[256,1536]{1,0:T(8,128)(2,1)}, u32[]{:S(2)}) copy-start(bf16[256,1536]{1,0:T(8,128)(2,1)} %after.17.refs_2_.refs_1_) | copy-start | bytes 2359300
  74.8 6.1 %copy-start.9 = (bf16[256,1536]{1,0:T(8,128)(2,1)S(1)}, bf16[256,1536]{1,0:T(8,128)(2,1)}, u32[]{:S(2)}) copy-start(bf16[256,1536]{1,0:T(8,128)(2,1)} %after.15.refs_1_.refs_0_) | copy-start | bytes 2359300
  76.6 14.2 %copy-start = (bf16[4,4,2,96,384]{4,3,2,1,0:T(8,128)(2,1)}, bf16[4,4,2,96,384]{4,3,2,1,0:T(8,128)(2,1)S(1)}, u32[]{:S(2)}) copy-start(bf16[4,4,2,96,384]{4,3,2,1,0:T(8,128)(2,1)S(1)} %stack_planes.1.refs_9_.refs_10_.refs_11_.refs_5_) | copy-start | bytes 7077892
  76.6 14.9 %copy-start.13 = (bf16[21,96,384]{2,1,0:T(8,128)(2,1)S(1)}, bf16[21,96,384]{2,1,0:T(8,128)(2,1)}, u32[]{:S(2)}) copy-start(bf16[21,96,384]{2,1,0:T(8,128)(2,1)} %after.19.refs_3_) | copy-start | bytes 4644868
  76.6 41.0 %collective-permute-start.19 = (bf16[4,4,2,96,384]{4,3,2,1,0:T(8,128)(2,1)S(1)}, bf16[4,4,2,96,384]{4,3,2,1,0:T(8,128)(2,1)S(1)}, u32[]{:S(2)}, u32[]{:S(2)}) collective-permute-start(bf16[4,4,2,96,384]{4,3,2,1,0:T(8,128)(2,1)S(1)} %stack_planes.1.refs_9_.refs_10_.refs_11_.refs_5_), channel_id=1, source_target_pairs={{0,1},{1,0},{2,3},{3,2},{4,5},{5,4},{6,7},{7,6},{8,9},{9,8},{10,11... | collective-permute-start | bytes 7077896 | tf_op jit(solution)/shard_map/ppermute | solution.py:26
  90.9 2.5 %collective-permute-start.20 = (bf16[2,5,96,384]{3,2,1,0:T(8,128)(2,1)S(1)}, bf16[2,5,96,384]{3,2,1,0:T(8,128)(2,1)S(1)}, u32[]{:S(2)}, u32[]{:S(2)}) collective-permute-start(bf16[2,5,96,384]{3,2,1,0:T(8,128)(2,1)S(1)} %get-tuple-element.12), channel_id=1, source_target_pairs={{0,1},{1,0},{2,3},{3,2},{4,5},{5,4},{6,7},{7,6},{8,9},{9,8},{10,11... | collective-permute-start | bytes 2211848 | tf_op jit(solution)/shard_map/ppermute | solution.py:26
  91.5 23.5 %collective-permute-start.15 = (bf16[21,96,384]{2,1,0:T(8,128)(2,1)S(1)}, bf16[21,96,384]{2,1,0:T(8,128)(2,1)S(1)}, u32[]{:S(2)}, u32[]{:S(2)}) collective-permute-start(bf16[21,96,384]{2,1,0:T(8,128)(2,1)S(1)} %copy-done.13), channel_id=1, source_target_pairs={{0,1},{1,0},{2,3},{3,2},{4,5},{5,4},{6,7},{7,6},{8,9},{9,8},{10,11... | collective-permute-start | bytes 4644872 | tf_op jit(solution)/shard_map/ppermute | solution.py:26
  93.4 21.6 %copy-start.34 = (bf16[2,5,96,384]{3,2,1,0:T(8,128)(2,1)}, bf16[2,5,96,384]{3,2,1,0:T(8,128)(2,1)S(1)}, u32[]{:S(2)}) copy-start(bf16[2,5,96,384]{3,2,1,0:T(8,128)(2,1)S(1)} %collective-permute-done.20) | copy-start | bytes 2211844
  93.4 16.6 %collective-permute-start.21 = (bf16[2,5,96,384]{3,2,1,0:T(8,128)(2,1)S(1)}, bf16[2,5,96,384]{3,2,1,0:T(8,128)(2,1)S(1)}, u32[]{:S(2)}, u32[]{:S(2)}) collective-permute-start(bf16[2,5,96,384]{3,2,1,0:T(8,128)(2,1)S(1)} %get-tuple-element.13), channel_id=1, source_target_pairs={{0,1},{1,0},{2,3},{3,2},{4,5},{5,4},{6,7},{7,6},{8,9},{9,8},{10,11... | collective-permute-start | bytes 2211848 | tf_op jit(solution)/shard_map/ppermute | solution.py:26
  103.8 15.0 %collective-permute-start.17 = (bf16[21,96,384]{2,1,0:T(8,128)(2,1)}, bf16[21,96,384]{2,1,0:T(8,128)(2,1)S(1)}, u32[]{:S(2)}, u32[]{:S(2)}) collective-permute-start(bf16[21,96,384]{2,1,0:T(8,128)(2,1)} %collective-permute-done.13.refs_2_.refs_7_), channel_id=1, source_target_pairs={{0,1},{1,0},{2,3},{3,2},{4,5},{5,4},{6,7},{7,6},{8,9},{9,8},{10,11... | collective-permute-start | bytes 4644872 | tf_op jit(solution)/shard_map/ppermute | solution.py:26
  108.7 10.1 %collective-permute-start.16 = (bf16[21,96,384]{2,1,0:T(8,128)(2,1)}, bf16[21,96,384]{2,1,0:T(8,128)(2,1)S(1)}, u32[]{:S(2)}, u32[]{:S(2)}) collective-permute-start(bf16[21,96,384]{2,1,0:T(8,128)(2,1)} %collective-permute-done.12.refs_1_.refs_5_), channel_id=1, source_target_pairs={{0,1},{1,0},{2,3},{3,2},{4,5},{5,4},{6,7},{7,6},{8,9},{9,8},{10,11... | collective-permute-start | bytes 4644872 | tf_op jit(solution)/shard_map/ppermute | solution.py:26
  110.0 5.0 %copy-start.36 = (bf16[2,5,96,384]{3,2,1,0:T(8,128)(2,1)}, bf16[2,5,96,384]{3,2,1,0:T(8,128)(2,1)S(1)}, u32[]{:S(2)}) copy-start(bf16[2,5,96,384]{3,2,1,0:T(8,128)(2,1)S(1)} %collective-permute-done.21) | copy-start | bytes 2211844
  112.7 22.3 %collective-permute-start.22 = (bf16[2,5,96,384]{3,2,1,0:T(8,128)(2,1)}, bf16[2,5,96,384]{3,2,1,0:T(8,128)(2,1)S(1)}, u32[]{:S(2)}, u32[]{:S(2)}) collective-permute-start(bf16[2,5,96,384]{3,2,1,0:T(8,128)(2,1)} %pad_maximum_fusion), channel_id=1, source_target_pairs={{0,2},{1,3},{2,0},{3,1},{4,6},{5,7},{6,4},{7,5},{8,10},{9,11},{10,... | collective-permute-start | bytes 2211848 | tf_op jit(solution)/shard_map/ppermute | solution.py:26
  115.0 3.8 %copy-start.30 = (bf16[21,96,384]{2,1,0:T(8,128)(2,1)}, bf16[21,96,384]{2,1,0:T(8,128)(2,1)S(1)}, u32[]{:S(2)}) copy-start(bf16[21,96,384]{2,1,0:T(8,128)(2,1)S(1)} %collective-permute-done.15.refs_4_) | copy-start | bytes 4644868
  115.0 20.0 %collective-permute-start.23 = (bf16[9,96,384]{2,1,0:T(8,128)(2,1)}, bf16[9,96,384]{2,1,0:T(8,128)(2,1)}, u32[]{:S(2)}, u32[]{:S(2)}) collective-permute-start(bf16[9,96,384]{2,1,0:T(8,128)(2,1)} %slice.85), channel_id=1, source_target_pairs={{0,8},{8,0},{16,24},{24,16},{1,9},{9,1},{17,25},{25,17},{2,10},{10... | collective-permute-start | bytes 1990664 | tf_op jit(solution)/shard_map/ppermute | solution.py:26
  117.6 18.9 %collective-permute-start.14 = (bf16[9,96,384]{2,1,0:T(8,128)(2,1)}, bf16[9,96,384]{2,1,0:T(8,128)(2,1)}, u32[]{:S(2)}, u32[]{:S(2)}) collective-permute-start(bf16[9,96,384]{2,1,0:T(8,128)(2,1)} %slice.82), channel_id=1, source_target_pairs={{0,16},{8,24},{16,0},{24,8},{1,17},{9,25},{17,1},{25,9},{2,18},{10... | collective-permute-start | bytes 1990664 | tf_op jit(solution)/shard_map/ppermute | solution.py:26
  118.8 1.7 %copy-start.32 = (bf16[21,96,384]{2,1,0:T(8,128)(2,1)}, bf16[21,96,384]{2,1,0:T(8,128)(2,1)S(1)}, u32[]{:S(2)}) copy-start(bf16[21,96,384]{2,1,0:T(8,128)(2,1)S(1)} %collective-permute-done.16.refs_6_) | copy-start | bytes 4644868
  135.9 4.4 %collective-permute-start.25 = (bf16[9,96,384]{2,1,0:T(8,128)(2,1)}, bf16[9,96,384]{2,1,0:T(8,128)(2,1)S(1)}, u32[]{:S(2)}, u32[]{:S(2)}) collective-permute-start(bf16[9,96,384]{2,1,0:T(8,128)(2,1)} %after.22.refs_4_.refs_9_), channel_id=1, source_target_pairs={{0,1},{1,0},{2,3},{3,2},{4,5},{5,4},{6,7},{7,6},{8,9},{9,8},{10,11... | collective-permute-start | bytes 1990664 | tf_op jit(solution)/shard_map/ppermute | solution.py:26
  136.5 3.7 %collective-permute-start.24 = (bf16[9,96,384]{2,1,0:T(8,128)(2,1)}, bf16[9,96,384]{2,1,0:T(8,128)(2,1)S(1)}, u32[]{:S(2)}, u32[]{:S(2)}) collective-permute-start(bf16[9,96,384]{2,1,0:T(8,128)(2,1)} %after.21.refs_3_.refs_7_), channel_id=1, source_target_pairs={{0,1},{1,0},{2,3},{3,2},{4,5},{5,4},{6,7},{7,6},{8,9},{9,8},{10,11... | collective-permute-start | bytes 1990664 | tf_op jit(solution)/shard_map/ppermute | solution.py:26
  138.5 17.8 %collective-permute-start.26 = (bf16[1,5,96,384]{3,2,1,0:T(8,128)(2,1)S(1)}, bf16[1,5,96,384]{3,2,1,0:T(8,128)(2,1)S(1)}, u32[]{:S(2)}, u32[]{:S(2)}) collective-permute-start(bf16[1,5,96,384]{3,2,1,0:T(8,128)(2,1)S(1)} %add_convert_fusion), channel_id=1, source_target_pairs={{0,6},{1,7},{2,4},{3,5},{4,2},{5,3},{6,0},{7,1},{8,14},{9,15},{10,... | collective-permute-start | bytes 1105928 | tf_op jit(solution)/shard_map/ppermute | solution.py:26
  154.6 2.4 %copy-start.35 = (bf16[2,5,96,384]{3,2,1,0:T(8,128)(2,1)S(1)}, bf16[2,5,96,384]{3,2,1,0:T(8,128)(2,1)}, u32[]{:S(2)}) copy-start(bf16[2,5,96,384]{3,2,1,0:T(8,128)(2,1)} %copy-done.34) | copy-start | bytes 2211844
  (25 other events, 25.6 us)

commit v26 on v24

--- a/solution.py
+++ b/solution.py
@@ -497,7 +497,7 @@
     act = after(activate(inputs), *across[1:])
     beside, below = from_peer(act, "seq", 1), from_peer(act, "seq", 2)
     slope = half_slope(inputs)
-    line = gather_line(weights[:SPLIT], "rep", planes, 2)
+    line = gather_line(after(weights[:SPLIT], last_taps), "rep", planes, 2)
     line_across = gather_line(after(jnp.stack(across), act, *line[1:]), "rep", planes, 2)
     crossing = (line_across[1], line_across[planes - 1])
     trunk = trunk_grad[0]

time: 161 us -> 164 us (1.019)
  local copies, waits for them, and re-layouts: 31.6 us -> 33.9 us
  waiting for transfers between devices: 28.3 us -> 30 us
    ppermute x27, waiting for transfers between devices: 28.3 us -> 30 us  [from_peer(): return lax.ppermute(value, axis, [(i, i ^ distance) for i in range(peers)])]
    unnamed x92 -> x94, local copies, waits for them, and re-layouts: 19.2 us -> 19.8 us
  transfers between devices with their start and end apart: 27 -> 27, of which waited for: 5 -> 5; matrix products, arithmetic and copies ran while one was open for 14% -> 13% of each run, Pallas kernels for 36% -> 35%
where the time goes in v26:
time: 164 us; the launch traced here: 163 us
  Pallas kernels  56.9 us (35%)
  local copies, waits for them, and re-layouts  33.9 us (21%)
  waiting for transfers between devices  30 us (18%)
  starting transfers between devices  28.3 us (17%)
  other arithmetic  12.6 us (8%)
    ppermute x27, waiting for transfers between devices, from_peer(): return lax.ppermute(value, axis, [(i, i ^ distance) for i in range(peers)])  30 us
    ppermute x27, starting transfers between devices, from_peer(): return lax.ppermute(value, axis, [(i, i ^ distance) for i in range(peers)])  28.3 us
    pallas_call x2, Pallas kernels, gradient_stage(): pl.pallas_call(body, out_shape=out_shape, grid_spec=pltpu.PrefetchScalarG...  26.1 us
    unnamed x94, local copies, waits for them, and re-layouts  19.8 us
    pallas_call x1, Pallas kernels, early_terms(): pl.pallas_call(kernel, out_shape=jax.ShapeDtypeStruct((both, columns), jn...  13.9 us
    pallas_call x1, Pallas kernels, late_terms(): pl.pallas_call(kernel, out_shape=(jax.ShapeDtypeStruct(shape, jnp.float32...  9.96 us
    concatenate x1, other arithmetic, on_device_square(): shifts = jnp.concatenate([later, trunk, earlier], axis=1)  5.47 us
    slice x2, local copies, waits for them, and re-layouts, on_device_square(): top, bottom = (after(beside[:half], *ready), after(below[half:], *ready))  4.14 us
  transfers between devices with their start and end apart: 27, of which 5 were waited for; matrix products, arithmetic and copies ran while one was open for 13% of the time, Pallas kernels for 35%

profile of v26, /device:TPU:9, one launch (start us, length us, event | category | flops | bytes accessed | tf_op | source)
XLA Modules:
  0.0 162.7 jit_solution(11108040905511074962)
XLA Ops:
  0.6 1.6 slice_bitcast_fusion.2
  2.2 1.6 %slice.60.refs_0_ = bf16[3,96,384]{2,1,0:T(8,128)(2,1)} slice(bf16[5,96,384]{2,1,0:T(8,128)(2,1)} %param.5), slice={[0:3], [0:96], [0:384]} | slice | bytes 442368 | tf_op jit(solution)/shard_map/slice | solution.py:500
  3.9 1.3 collective-permute-start.1
  5.2 1.2 collective-permute-start.3
  6.4 1.2 collective-permute-start.4
  7.8 2.2 %collective-permute-start = (bf16[3,96,384]{2,1,0:T(8,128)(2,1)}, bf16[3,96,384]{2,1,0:T(8,128)(2,1)S(1)}, u32[]{:S(2)}, u32[]{:S(2)}) collective-permute-start(bf16[3,96,384]{2,1,0:T(8,128)(2,1)} %after.13.refs_0_), channel_id=1, source_target_pairs={{0,2},{1,3},{2,0},{3,1},{4,6},{5,7},{6,4},{7,5},{8,10},{9,11},{10,... | collective-permute-start | bytes 663560 | tf_op jit(solution)/shard_map/ppermute | solution.py:26
  10.0 1.4 copy-done.10
  11.4 1.8 %act.1.refs_0_ = bf16[512,1536]{1,0:T(8,128)(2,1)S(1)} custom-call(bf16[1,1024,768]{2,1,0:T(8,128)(2,1)S(1)} %copy-done.10), custom_call_target="tpu_custom_call" | custom-call | flops 1048576 | bytes 65536 | tf_op jit(solution)/shard_map/act/pallas_call | solution.py:85
  13.2 1.1 copy-done.3
  15.8 1.2 collective-permute-start.10
  17.0 1.2 collective-permute-start.6
  18.2 2.1 %slice_bitcast_fusion.1 = (bf16[2047,384]{1,0:T(8,128)(2,1)}, bf16[2047,384]{1,0:T(8,128)(2,1)}) fusion(bf16[1,2048,384]{2,1,0:T(8,128)(2,1)S(1)} %copy-done.2), kind=kLoop, calls=%fused_computation.7 | loop fusion | bytes 6288384 | tf_op jit(solution)/shard_map/slice | solution.py:505
  20.4 0.9 pad_maximum_fusion.1.refs_0_
  21.3 2.1 %collective-permute-done.2.refs_2_.refs_3_ = bf16[3,96,384]{2,1,0:T(8,128)(2,1)S(1)} collective-permute-done((bf16[3,96,384]{2,1,0:T(8,128)(2,1)S(1)}, bf16[3,96,384]{2,1,0:T(8,128)(2,1)S(1)}, u32[]{:S(2)}, u32[]{:S(2)}) %collective-permute-start.2) | collective-permute-done | bytes 221216 | tf_op jit(solution)/shard_map/ppermute | solution.py:26
  24.8 5.5 %fusion.2.refs_2_.shifts_ref = bf16[2048,1152]{1,0:T(8,128)(2,1)} fusion(bf16[2047,384]{1,0:T(8,128)(2,1)} %get-tuple-element.17, bf16[2047,384]{1,0:T(8,128)(2,1)} %get-tuple-element.16, bf16[2048,384]{1,0:T(8,128)(2,1)S(1)} %bitcast.14), kind=kLoop, calls=%fused_computation.4 | loop fusion | flops 23592960 | bytes 9435648 | tf_op jit(solution)/shard_map/concatenate | solution.py:507
  30.3 2.3 %half_slope.1.refs_1_.refs_11_ = f32[2,512,768]{2,1,0:T(8,128)S(1)} custom-call(bf16[1,1024,768]{2,1,0:T(8,128)(2,1)S(1)} %copy-done.11), custom_call_target="tpu_custom_call" | custom-call | tf_op jit(solution)/shard_map/half_slope/pallas_call | solution.py:167
  32.7 1.6 copy-done.1
  34.4 0.9 copy-done.26
  35.3 1.0 kernel_messages.1
  36.3 1.1 copy-done.5
  37.5 1.1 copy-done.12
  38.6 11.3 %collective-permute-done.10.refs_2_ = bf16[512,1536]{1,0:T(8,128)(2,1)} collective-permute-done((bf16[512,1536]{1,0:T(8,128)(2,1)}, bf16[512,1536]{1,0:T(8,128)(2,1)}, u32[]{:S(2)}, u32[]{:S(2)}) %collective-permute-start.10) | collective-permute-done | bytes 1572896 | tf_op jit(solution)/shard_map/ppermute | solution.py:26
  49.9 2.1 %slice.81.refs_0_ = bf16[256,1536]{1,0:T(8,128)(2,1)} slice(bf16[512,1536]{1,0:T(8,128)(2,1)} %collective-permute-done.10.refs_2_), slice={[256:512], [0:1536]} | slice | bytes 1572864 | tf_op jit(solution)/shard_map/slice | solution.py:510
  53.0 1.2 collective-permute-start.11
  54.2 2.1 %slice.80.refs_0_ = bf16[256,1536]{1,0:T(8,128)(2,1)} slice(bf16[512,1536]{1,0:T(8,128)(2,1)} %collective-permute-done.6.refs_1_), slice={[0:256], [0:1536]} | slice | bytes 1572864 | tf_op jit(solution)/shard_map/slice | solution.py:510
  56.3 1.2 collective-permute-start.9
  58.3 13.9 %weight_grad_early.1.refs_1_.early_ref = f32[1536,1152]{1,0:T(8,128)} custom-call(s32[2]{0:T(128)S(1)} %pad_add_fusion.place, bf16[2048,1152]{1,0:T(8,128)(2,1)} %fusion.2.refs_2_.shifts_ref, bf16[512,1536]{1,0:T(8,128)(2,1)S(1)} %copy-done.4, bf16[512,1536]{1,0:T(8,128)(2,1)} %collective-permute-done.6.refs_1_, ...), custom_call_target="tpu_custom_call" | custom-call | flops 1048576 | bytes 65536 | tf_op jit(solution)/shard_map/weight_grad_early/pallas_call | solution.py:213
  72.3 0.9 copy-done.6
  73.2 0.9 copy-done.8
  76.1 1.8 %stack_planes.1.refs_9_.refs_10_.refs_11_.refs_5_ = bf16[4,4,2,96,384]{4,3,2,1,0:T(8,128)(2,1)S(1)} custom-call(s32[2]{0:T(128)S(1)} %pad_add_fusion.place, bf16[4,2,96,384]{3,2,1,0:T(8,128)(2,1)S(1)} %copy-done.14, bf16[4,2,96,384]{3,2,1,0:T(8,128)(2,1)S(1)} %copy-done.18, bf16[4,2,96,384]{3,2,1,0:T(8,128)(2,1)} %after.22.refs_2_, ...), custom_call_target="tpu_custom_call" | custom-call | flops 1048576 | bytes 65536 | tf_op jit(solution)/shard_map/stack_planes/pallas_call | solution.py:471
  78.0 4.2 %collective-permute-start.19 = (bf16[4,4,2,96,384]{4,3,2,1,0:T(8,128)(2,1)S(1)}, bf16[4,4,2,96,384]{4,3,2,1,0:T(8,128)(2,1)S(1)}, u32[]{:S(2)}, u32[]{:S(2)}) collective-permute-start(bf16[4,4,2,96,384]{4,3,2,1,0:T(8,128)(2,1)S(1)} %stack_planes.1.refs_9_.refs_10_.refs_11_.refs_5_), channel_id=1, source_target_pairs={{0,1},{1,0},{2,3},{3,2},{4,5},{5,4},{6,7},{7,6},{8,9},{9,8},{10,11... | collective-permute-start | bytes 7077896 | tf_op jit(solution)/shard_map/ppermute | solution.py:26
  82.2 10.0 %weight_grad_late.1 = (f32[4,5,96,384]{3,2,1,0:T(8,128)}, bf16[2,5,96,384]{3,2,1,0:T(8,128)(2,1)S(1)}, bf16[2,5,96,384]{3,2,1,0:T(8,128)(2,1)S(1)}) custom-call(s32[2]{0:T(128)S(1)} %pad_add_fusion.place, bf16[2048,1152]{1,0:T(8,128)(2,1)} %fusion.2.refs_2_.shifts_ref, f32[1536,1152]{1,0:T(8,128)} %weight_grad_early.1.refs_1_.early_ref, ...), custom_call_target="tpu_custom_call" | custom-call | flops 1048576 | bytes 65536 | tf_op jit(solution)/shard_map/weight_grad_late/pallas_call | solution.py:289
  92.9 1.8 %collective-permute-done.20 = bf16[2,5,96,384]{3,2,1,0:T(8,128)(2,1)S(1)} collective-permute-done((bf16[2,5,96,384]{3,2,1,0:T(8,128)(2,1)S(1)}, bf16[2,5,96,384]{3,2,1,0:T(8,128)(2,1)S(1)}, u32[]{:S(2)}, u32[]{:S(2)}) %collective-permute-start.20) | collective-permute-done | bytes 737312 | tf_op jit(solution)/shard_map/ppermute | solution.py:26
  95.0 11.4 %collective-permute-done.13.refs_2_.refs_7_ = bf16[21,96,384]{2,1,0:T(8,128)(2,1)} collective-permute-done((bf16[21,96,384]{2,1,0:T(8,128)(2,1)}, bf16[21,96,384]{2,1,0:T(8,128)(2,1)}, u32[]{:S(2)}, u32[]{:S(2)}) %collective-permute-start.13) | collective-permute-done | bytes 1548320 | tf_op jit(solution)/shard_map/ppermute | solution.py:26
  106.4 4.2 %collective-permute-start.17 = (bf16[21,96,384]{2,1,0:T(8,128)(2,1)}, bf16[21,96,384]{2,1,0:T(8,128)(2,1)S(1)}, u32[]{:S(2)}, u32[]{:S(2)}) collective-permute-start(bf16[21,96,384]{2,1,0:T(8,128)(2,1)} %collective-permute-done.13.refs_2_.refs_7_), channel_id=1, source_target_pairs={{0,1},{1,0},{2,3},{3,2},{4,5},{5,4},{6,7},{7,6},{8,9},{9,8},{10,11... | collective-permute-start | bytes 4644872 | tf_op jit(solution)/shard_map/ppermute | solution.py:26
  111.3 1.8 %add_convert_fusion.2 = (bf16[1,5,96,384]{3,2,1,0:T(8,128)(2,1)S(1)}, bf16[1,5,96,384]{3,2,1,0:T(8,128)(2,1)S(1)}) fusion(f32[4,5,96,384]{3,2,1,0:T(8,128)} %get-tuple-element.11, bf16[2,5,96,384]{3,2,1,0:T(8,128)(2,1)S(1)} %collective-permute-done.20, bf16[2,5,96,384]{3,2,1,0:T(8,128)(2,1)S(1)} %collective-permute-done.21), kind=kLoop, calls=%fused_computation.12 | loop fusion | flops 1105920 | bytes 2949120 | tf_op jit(solution)/shard_map/convert_element_type | solution.py:46
  113.1 0.9 pad_maximum_fusion
  114.0 1.3 collective-permute-start.22
  115.3 2.0 %slice.85 = bf16[9,96,384]{2,1,0:T(8,128)(2,1)} slice(bf16[21,96,384]{2,1,0:T(8,128)(2,1)} %collective-permute-done.13.refs_2_.refs_7_), slice={[6:15], [0:96], [0:384]} | slice | bytes 1327104 | tf_op jit(solution)/shard_map/slice | solution.py:550
  117.4 2.6 %slice.82 = bf16[9,96,384]{2,1,0:T(8,128)(2,1)} slice(bf16[21,96,384]{2,1,0:T(8,128)(2,1)} %collective-permute-done.12.refs_1_.refs_5_), slice={[0:9], [0:96], [0:384]} | slice | bytes 1327104 | tf_op jit(solution)/shard_map/slice | solution.py:549
  120.2 1.1 copy-done.28
  122.4 14.4 %input_grad.2.refs_1_.refs_12_ = f32[2,512,768]{2,1,0:T(8,128)} custom-call(s32[2]{0:T(128)} %copy-done.27, bf16[6,96,384]{2,1,0:T(8,128)(2,1)} %copy-done.20, bf16[21,96,384]{2,1,0:T(8,128)(2,1)} %collective-permute-done.12.refs_1_.refs_5_, bf16[21,96,384]{2,1,0:T(8,128)(2,1)} %collective-permute-done.13.refs_2_.refs_7_, ...), custom_call_target="tpu_custom_call" | custom-call | flops 1048576 | bytes 65536 | tf_op jit(solution)/shard_map/input_grad/pallas_call | solution.py:447
  139.0 1.2 add_convert_fusion
  140.3 2.6 %collective-permute-start.26 = (bf16[1,5,96,384]{3,2,1,0:T(8,128)(2,1)S(1)}, bf16[1,5,96,384]{3,2,1,0:T(8,128)(2,1)S(1)}, u32[]{:S(2)}, u32[]{:S(2)}) collective-permute-start(bf16[1,5,96,384]{3,2,1,0:T(8,128)(2,1)S(1)} %add_convert_fusion), channel_id=1, source_target_pairs={{0,6},{1,7},{2,4},{3,5},{4,2},{5,3},{6,0},{7,1},{8,14},{9,15},{10,... | collective-permute-start | bytes 1105928 | tf_op jit(solution)/shard_map/ppermute | solution.py:26
  142.9 0.9 copy-done.39
  144.7 11.6 %input_grad.3.refs_1_ = bf16[1,1024,768]{2,1,0:T(8,128)(2,1)} custom-call(s32[2]{0:T(128)} %copy-done.27, bf16[6,96,384]{2,1,0:T(8,128)(2,1)} %copy-done.20, bf16[21,96,384]{2,1,0:T(8,128)(2,1)} %collective-permute-done.12.refs_1_.refs_5_, bf16[21,96,384]{2,1,0:T(8,128)(2,1)} %collective-permute-done.13.refs_2_.refs_7_, ...), custom_call_target="tpu_custom_call" | custom-call | flops 1048576 | bytes 65536 | tf_op jit(solution)/shard_map/input_grad/pallas_call | solution.py:447
  156.3 3.4 %collective-permute-done.26.refs_0_ = bf16[1,5,96,384]{3,2,1,0:T(8,128)(2,1)S(1)} collective-permute-done((bf16[1,5,96,384]{3,2,1,0:T(8,128)(2,1)S(1)}, bf16[1,5,96,384]{3,2,1,0:T(8,128)(2,1)S(1)}, u32[]{:S(2)}, u32[]{:S(2)}) %collective-permute-start.26) | collective-permute-done | bytes 368672 | tf_op jit(solution)/shard_map/ppermute | solution.py:26
  160.5 2.2 %add_bitcast_fusion = f32[5,96,384]{2,1,0:T(8,128)} fusion(bf16[1,5,96,384]{3,2,1,0:T(8,128)(2,1)} %after.25, f32[4,5,96,384]{3,2,1,0:T(8,128)} %get-tuple-element.11, bf16[2,5,96,384]{3,2,1,0:T(8,128)(2,1)S(1)} %copy-done.30, bf16[2,5,96,384]{3,2,1,0:T(8,128)(2,1)S(1)} %copy-done.36), kind=kLoop, calls=%fused_computation.9 | loop fusion | flops 1105920 | bytes 2580480 | tf_op jit(solution)/shard_map/add | solution.py:576
  (135 shorter events, 13.9 us)
Async XLA Ops:
  3.9 14.3 %collective-permute-start.1 = (bf16[3,96,384]{2,1,0:T(8,128)(2,1)}, bf16[3,96,384]{2,1,0:T(8,128)(2,1)S(1)}, u32[]{:S(2)}, u32[]{:S(2)}) collective-permute-start(bf16[3,96,384]{2,1,0:T(8,128)(2,1)} %after.13.refs_0_), channel_id=1, source_target_pairs={{0,6},{1,7},{2,4},{3,5},{4,2},{5,3},{6,0},{7,1},{8,14},{9,15},{10,... | collective-permute-start | bytes 663560 | tf_op jit(solution)/shard_map/ppermute | solution.py:26
  5.2 9.2 %collective-permute-start.3 = (bf16[2,96,384]{2,1,0:T(8,128)(2,1)}, bf16[2,96,384]{2,1,0:T(8,128)(2,1)S(1)}, u32[]{:S(2)}, u32[]{:S(2)}) collective-permute-start(bf16[2,96,384]{2,1,0:T(8,128)(2,1)} %get-tuple-element.19.refs_1_), channel_id=1, source_target_pairs={{0,8},{8,0},{16,24},{24,16},{1,9},{9,1},{17,25},{25,17},{2,10},{10... | collective-permute-start | bytes 442376 | tf_op jit(solution)/shard_map/ppermute | solution.py:26
  6.4 8.0 %collective-permute-start.4 = (bf16[2,96,384]{2,1,0:T(8,128)(2,1)}, bf16[2,96,384]{2,1,0:T(8,128)(2,1)S(1)}, u32[]{:S(2)}, u32[]{:S(2)}) collective-permute-start(bf16[2,96,384]{2,1,0:T(8,128)(2,1)} %get-tuple-element.19.refs_1_), channel_id=1, source_target_pairs={{0,16},{8,24},{16,0},{24,8},{1,17},{9,25},{17,1},{25,9},{2,18},{10... | collective-permute-start | bytes 442376 | tf_op jit(solution)/shard_map/ppermute | solution.py:26
  7.6 6.7 %collective-permute-start.5 = (bf16[2,96,384]{2,1,0:T(8,128)(2,1)}, bf16[2,96,384]{2,1,0:T(8,128)(2,1)S(1)}, u32[]{:S(2)}, u32[]{:S(2)}) collective-permute-start(bf16[2,96,384]{2,1,0:T(8,128)(2,1)} %get-tuple-element.19.refs_1_), channel_id=1, source_target_pairs={{0,24},{8,16},{16,8},{24,0},{1,25},{9,17},{17,9},{25,1},{2,26},{10... | collective-permute-start | bytes 442376 | tf_op jit(solution)/shard_map/ppermute | solution.py:26
  7.8 13.5 %collective-permute-start = (bf16[3,96,384]{2,1,0:T(8,128)(2,1)}, bf16[3,96,384]{2,1,0:T(8,128)(2,1)S(1)}, u32[]{:S(2)}, u32[]{:S(2)}) collective-permute-start(bf16[3,96,384]{2,1,0:T(8,128)(2,1)} %after.13.refs_0_), channel_id=1, source_target_pairs={{0,2},{1,3},{2,0},{3,1},{4,6},{5,7},{6,4},{7,5},{8,10},{9,11},{10,... | collective-permute-start | bytes 663560 | tf_op jit(solution)/shard_map/ppermute | solution.py:26
  14.3 3.9 %copy-start.2 = (bf16[1,2048,384]{2,1,0:T(8,128)(2,1)S(1)}, bf16[1,2048,384]{2,1,0:T(8,128)(2,1)}, u32[]{:S(2)}) copy-start(bf16[1,2048,384]{2,1,0:T(8,128)(2,1)} %refs_4_.1) | copy-start | bytes 4718596
  15.8 4.6 %copy-start.42 = (bf16[2,96,384]{2,1,0:T(8,128)(2,1)S(1)}, bf16[2,96,384]{2,1,0:T(8,128)(2,1)}, u32[]{:S(2)}) copy-start(bf16[2,96,384]{2,1,0:T(8,128)(2,1)} %copy-done.41) | copy-start | bytes 442372
  15.8 4.6 %copy-start.44 = (bf16[2,96,384]{2,1,0:T(8,128)(2,1)S(1)}, bf16[2,96,384]{2,1,0:T(8,128)(2,1)}, u32[]{:S(2)}) copy-start(bf16[2,96,384]{2,1,0:T(8,128)(2,1)} %copy-done.43) | copy-start | bytes 442372
  15.8 4.6 %copy-start.46 = (bf16[2,96,384]{2,1,0:T(8,128)(2,1)S(1)}, bf16[2,96,384]{2,1,0:T(8,128)(2,1)}, u32[]{:S(2)}) copy-start(bf16[2,96,384]{2,1,0:T(8,128)(2,1)} %copy-done.45) | copy-start | bytes 442372
  15.8 34.1 %collective-permute-start.10 = (bf16[512,1536]{1,0:T(8,128)(2,1)}, bf16[512,1536]{1,0:T(8,128)(2,1)}, u32[]{:S(2)}, u32[]{:S(2)}) collective-permute-start(bf16[512,1536]{1,0:T(8,128)(2,1)} %after.14.refs_1_.refs_0_), channel_id=1, source_target_pairs={{0,16},{8,24},{16,0},{24,8},{1,17},{9,25},{17,1},{25,9},{2,18},{10... | collective-permute-start | bytes 4718600 | tf_op jit(solution)/shard_map/ppermute | solution.py:26
  17.0 37.2 %collective-permute-start.6 = (bf16[512,1536]{1,0:T(8,128)(2,1)}, bf16[512,1536]{1,0:T(8,128)(2,1)}, u32[]{:S(2)}, u32[]{:S(2)}) collective-permute-start(bf16[512,1536]{1,0:T(8,128)(2,1)} %after.14.refs_1_.refs_0_), channel_id=1, source_target_pairs={{0,8},{8,0},{16,24},{24,16},{1,9},{9,1},{17,25},{25,17},{2,10},{10... | collective-permute-start | bytes 4718600 | tf_op jit(solution)/shard_map/ppermute | solution.py:26
  18.2 2.1 %copy-start.21 = (bf16[3,96,384]{2,1,0:T(8,128)(2,1)}, bf16[3,96,384]{2,1,0:T(8,128)(2,1)S(1)}, u32[]{:S(2)}) copy-start(bf16[3,96,384]{2,1,0:T(8,128)(2,1)S(1)} %collective-permute-done.1.refs_3_.refs_4_) | copy-start | bytes 663556
  18.2 5.2 %collective-permute-start.2 = (bf16[3,96,384]{2,1,0:T(8,128)(2,1)S(1)}, bf16[3,96,384]{2,1,0:T(8,128)(2,1)S(1)}, u32[]{:S(2)}, u32[]{:S(2)}) collective-permute-start(bf16[3,96,384]{2,1,0:T(8,128)(2,1)S(1)} %collective-permute-done.1.refs_3_.refs_4_), channel_id=1, source_target_pairs={{0,2},{1,3},{2,0},{3,1},{4,6},{5,7},{6,4},{7,5},{8,10},{9,11},{10,... | collective-permute-start | bytes 663560 | tf_op jit(solution)/shard_map/ppermute | solution.py:26
  21.3 2.1 %copy-start.23 = (bf16[3,96,384]{2,1,0:T(8,128)(2,1)}, bf16[3,96,384]{2,1,0:T(8,128)(2,1)S(1)}, u32[]{:S(2)}) copy-start(bf16[3,96,384]{2,1,0:T(8,128)(2,1)S(1)} %collective-permute-done.refs_1_.refs_2_) | copy-start | bytes 663556
  24.1 27.9 %collective-permute-start.8 = (bf16[4,2,96,384]{3,2,1,0:T(8,128)(2,1)}, bf16[4,2,96,384]{3,2,1,0:T(8,128)(2,1)S(1)}, u32[]{:S(2)}, u32[]{:S(2)}) collective-permute-start(bf16[4,2,96,384]{3,2,1,0:T(8,128)(2,1)} %after.15.refs_0_), channel_id=1, source_target_pairs={{0,6},{1,7},{2,4},{3,5},{4,2},{5,3},{6,0},{7,1},{8,14},{9,15},{10,... | collective-permute-start | bytes 1769480 | tf_op jit(solution)/shard_map/ppermute | solution.py:26
  24.1 27.9 %collective-permute-start.7 = (bf16[4,2,96,384]{3,2,1,0:T(8,128)(2,1)}, bf16[4,2,96,384]{3,2,1,0:T(8,128)(2,1)S(1)}, u32[]{:S(2)}, u32[]{:S(2)}) collective-permute-start(bf16[4,2,96,384]{3,2,1,0:T(8,128)(2,1)} %after.15.refs_0_), channel_id=1, source_target_pairs={{0,2},{1,3},{2,0},{3,1},{4,6},{5,7},{6,4},{7,5},{8,10},{9,11},{10,... | collective-permute-start | bytes 1769480 | tf_op jit(solution)/shard_map/ppermute | solution.py:26
  24.8 5.5 %copy-start.11 = (bf16[1,1024,768]{2,1,0:T(8,128)(2,1)S(1)}, bf16[1,1024,768]{2,1,0:T(8,128)(2,1)}, u32[]{:S(2)}) copy-start(bf16[1,1024,768]{2,1,0:T(8,128)(2,1)} %x_ref.3) | copy-start | bytes 4718596
  30.3 4.1 %copy-start.19 = (bf16[3,96,384]{2,1,0:T(8,128)(2,1)S(1)}, bf16[3,96,384]{2,1,0:T(8,128)(2,1)}, u32[]{:S(2)}) copy-start(bf16[3,96,384]{2,1,0:T(8,128)(2,1)} %after.13.refs_0_) | copy-start | bytes 663556
  30.3 4.1 %copy-start.22 = (bf16[3,96,384]{2,1,0:T(8,128)(2,1)S(1)}, bf16[3,96,384]{2,1,0:T(8,128)(2,1)}, u32[]{:S(2)}) copy-start(bf16[3,96,384]{2,1,0:T(8,128)(2,1)} %copy-done.21) | copy-start | bytes 663556
  30.3 4.1 %copy-start.24 = (bf16[3,96,384]{2,1,0:T(8,128)(2,1)S(1)}, bf16[3,96,384]{2,1,0:T(8,128)(2,1)}, u32[]{:S(2)}) copy-start(bf16[3,96,384]{2,1,0:T(8,128)(2,1)} %copy-done.23) | copy-start | bytes 663556
  35.3 46.9 %copy-start.27 = (s32[2]{0:T(128)}, s32[2]{0:T(128)S(1)}, u32[]{:S(2)}) copy-start(s32[2]{0:T(128)S(1)} %pad_add_fusion.place) | copy-start | bytes 28
  38.6 13.3 %copy-start.20 = (bf16[6,96,384]{2,1,0:T(8,128)(2,1)}, bf16[6,96,384]{2,1,0:T(8,128)(2,1)S(1)}, u32[]{:S(2)}) copy-start(bf16[6,96,384]{2,1,0:T(8,128)(2,1)S(1)} %get-tuple-element.8.refs_0_) | copy-start | bytes 1327108
  53.0 19.3 %collective-permute-start.11 = (bf16[256,1536]{1,0:T(8,128)(2,1)}, bf16[256,1536]{1,0:T(8,128)(2,1)S(1)}, u32[]{:S(2)}, u32[]{:S(2)}) collective-permute-start(bf16[256,1536]{1,0:T(8,128)(2,1)} %after.18), channel_id=1, source_target_pairs={{0,8},{8,0},{16,24},{24,16},{1,9},{9,1},{17,25},{25,17},{2,10},{10... | collective-permute-start | bytes 2359304 | tf_op jit(solution)/shard_map/ppermute | solution.py:26
  56.3 16.9 %collective-permute-start.9 = (bf16[256,1536]{1,0:T(8,128)(2,1)}, bf16[256,1536]{1,0:T(8,128)(2,1)S(1)}, u32[]{:S(2)}, u32[]{:S(2)}) collective-permute-start(bf16[256,1536]{1,0:T(8,128)(2,1)} %after.16), channel_id=1, source_target_pairs={{0,16},{8,24},{16,0},{24,8},{1,17},{9,25},{17,1},{25,9},{2,18},{10... | collective-permute-start | bytes 2359304 | tf_op jit(solution)/shard_map/ppermute | solution.py:26
  57.6 17.4 %collective-permute-start.18 = (bf16[4,2,96,384]{3,2,1,0:T(8,128)(2,1)}, bf16[4,2,96,384]{3,2,1,0:T(8,128)(2,1)}, u32[]{:S(2)}, u32[]{:S(2)}) collective-permute-start(bf16[4,2,96,384]{3,2,1,0:T(8,128)(2,1)} %copy-done.15), channel_id=1, source_target_pairs={{0,2},{1,3},{2,0},{3,1},{4,6},{5,7},{6,4},{7,5},{8,10},{9,11},{10,... | collective-permute-start | bytes 1769480 | tf_op jit(solution)/shard_map/ppermute | solution.py:26
  74.1 32.4 %collective-permute-start.13 = (bf16[21,96,384]{2,1,0:T(8,128)(2,1)}, bf16[21,96,384]{2,1,0:T(8,128)(2,1)}, u32[]{:S(2)}, u32[]{:S(2)}) collective-permute-start(bf16[21,96,384]{2,1,0:T(8,128)(2,1)} %after.21.refs_3_), channel_id=1, source_target_pairs={{0,16},{8,24},{16,0},{24,8},{1,17},{9,25},{17,1},{25,9},{2,18},{10... | collective-permute-start | bytes 4644872 | tf_op jit(solution)/shard_map/ppermute | solution.py:26
  74.7 36.0 %collective-permute-start.12 = (bf16[21,96,384]{2,1,0:T(8,128)(2,1)}, bf16[21,96,384]{2,1,0:T(8,128)(2,1)}, u32[]{:S(2)}, u32[]{:S(2)}) collective-permute-start(bf16[21,96,384]{2,1,0:T(8,128)(2,1)} %after.20), channel_id=1, source_target_pairs={{0,8},{8,0},{16,24},{24,16},{1,9},{9,1},{17,25},{25,17},{2,10},{10... | collective-permute-start | bytes 4644872 | tf_op jit(solution)/shard_map/ppermute | solution.py:26
  76.1 6.1 %copy-start.7 = (bf16[256,1536]{1,0:T(8,128)(2,1)S(1)}, bf16[256,1536]{1,0:T(8,128)(2,1)}, u32[]{:S(2)}) copy-start(bf16[256,1536]{1,0:T(8,128)(2,1)} %after.19.refs_2_.refs_1_) | copy-start | bytes 2359300
  76.1 6.1 %copy-start.9 = (bf16[256,1536]{1,0:T(8,128)(2,1)S(1)}, bf16[256,1536]{1,0:T(8,128)(2,1)}, u32[]{:S(2)}) copy-start(bf16[256,1536]{1,0:T(8,128)(2,1)} %after.17.refs_1_.refs_0_) | copy-start | bytes 2359300
  78.0 14.2 %copy-start = (bf16[4,4,2,96,384]{4,3,2,1,0:T(8,128)(2,1)}, bf16[4,4,2,96,384]{4,3,2,1,0:T(8,128)(2,1)S(1)}, u32[]{:S(2)}) copy-start(bf16[4,4,2,96,384]{4,3,2,1,0:T(8,128)(2,1)S(1)} %stack_planes.1.refs_9_.refs_10_.refs_11_.refs_5_) | copy-start | bytes 7077892
  78.0 14.9 %copy-start.13 = (bf16[21,96,384]{2,1,0:T(8,128)(2,1)S(1)}, bf16[21,96,384]{2,1,0:T(8,128)(2,1)}, u32[]{:S(2)}) copy-start(bf16[21,96,384]{2,1,0:T(8,128)(2,1)} %after.21.refs_3_) | copy-start | bytes 4644868
  78.0 42.0 %collective-permute-start.19 = (bf16[4,4,2,96,384]{4,3,2,1,0:T(8,128)(2,1)S(1)}, bf16[4,4,2,96,384]{4,3,2,1,0:T(8,128)(2,1)S(1)}, u32[]{:S(2)}, u32[]{:S(2)}) collective-permute-start(bf16[4,4,2,96,384]{4,3,2,1,0:T(8,128)(2,1)S(1)} %stack_planes.1.refs_9_.refs_10_.refs_11_.refs_5_), channel_id=1, source_target_pairs={{0,1},{1,0},{2,3},{3,2},{4,5},{5,4},{6,7},{7,6},{8,9},{9,8},{10,11... | collective-permute-start | bytes 7077896 | tf_op jit(solution)/shard_map/ppermute | solution.py:26
  92.2 2.5 %collective-permute-start.20 = (bf16[2,5,96,384]{3,2,1,0:T(8,128)(2,1)S(1)}, bf16[2,5,96,384]{3,2,1,0:T(8,128)(2,1)S(1)}, u32[]{:S(2)}, u32[]{:S(2)}) collective-permute-start(bf16[2,5,96,384]{3,2,1,0:T(8,128)(2,1)S(1)} %get-tuple-element.12), channel_id=1, source_target_pairs={{0,1},{1,0},{2,3},{3,2},{4,5},{5,4},{6,7},{7,6},{8,9},{9,8},{10,11... | collective-permute-start | bytes 2211848 | tf_op jit(solution)/shard_map/ppermute | solution.py:26
  92.8 24.5 %collective-permute-start.15 = (bf16[21,96,384]{2,1,0:T(8,128)(2,1)S(1)}, bf16[21,96,384]{2,1,0:T(8,128)(2,1)S(1)}, u32[]{:S(2)}, u32[]{:S(2)}) collective-permute-start(bf16[21,96,384]{2,1,0:T(8,128)(2,1)S(1)} %copy-done.13), channel_id=1, source_target_pairs={{0,1},{1,0},{2,3},{3,2},{4,5},{5,4},{6,7},{7,6},{8,9},{9,8},{10,11... | collective-permute-start | bytes 4644872 | tf_op jit(solution)/shard_map/ppermute | solution.py:26
  94.7 22.7 %copy-start.35 = (bf16[2,5,96,384]{3,2,1,0:T(8,128)(2,1)}, bf16[2,5,96,384]{3,2,1,0:T(8,128)(2,1)S(1)}, u32[]{:S(2)}) copy-start(bf16[2,5,96,384]{3,2,1,0:T(8,128)(2,1)S(1)} %collective-permute-done.20) | copy-start | bytes 2211844
  94.7 16.7 %collective-permute-start.21 = (bf16[2,5,96,384]{3,2,1,0:T(8,128)(2,1)S(1)}, bf16[2,5,96,384]{3,2,1,0:T(8,128)(2,1)S(1)}, u32[]{:S(2)}, u32[]{:S(2)}) collective-permute-start(bf16[2,5,96,384]{3,2,1,0:T(8,128)(2,1)S(1)} %get-tuple-element.13), channel_id=1, source_target_pairs={{0,1},{1,0},{2,3},{3,2},{4,5},{5,4},{6,7},{7,6},{8,9},{9,8},{10,11... | collective-permute-start | bytes 2211848 | tf_op jit(solution)/shard_map/ppermute | solution.py:26
  106.4 13.7 %collective-permute-start.17 = (bf16[21,96,384]{2,1,0:T(8,128)(2,1)}, bf16[21,96,384]{2,1,0:T(8,128)(2,1)S(1)}, u32[]{:S(2)}, u32[]{:S(2)}) collective-permute-start(bf16[21,96,384]{2,1,0:T(8,128)(2,1)} %collective-permute-done.13.refs_2_.refs_7_), channel_id=1, source_target_pairs={{0,1},{1,0},{2,3},{3,2},{4,5},{5,4},{6,7},{7,6},{8,9},{9,8},{10,11... | collective-permute-start | bytes 4644872 | tf_op jit(solution)/shard_map/ppermute | solution.py:26
  110.7 9.5 %collective-permute-start.16 = (bf16[21,96,384]{2,1,0:T(8,128)(2,1)}, bf16[21,96,384]{2,1,0:T(8,128)(2,1)S(1)}, u32[]{:S(2)}, u32[]{:S(2)}) collective-permute-start(bf16[21,96,384]{2,1,0:T(8,128)(2,1)} %collective-permute-done.12.refs_1_.refs_5_), channel_id=1, source_target_pairs={{0,1},{1,0},{2,3},{3,2},{4,5},{5,4},{6,7},{7,6},{8,9},{9,8},{10,11... | collective-permute-start | bytes 4644872 | tf_op jit(solution)/shard_map/ppermute | solution.py:26
  111.3 6.0 %copy-start.37 = (bf16[2,5,96,384]{3,2,1,0:T(8,128)(2,1)}, bf16[2,5,96,384]{3,2,1,0:T(8,128)(2,1)S(1)}, u32[]{:S(2)}) copy-start(bf16[2,5,96,384]{3,2,1,0:T(8,128)(2,1)S(1)} %collective-permute-done.21) | copy-start | bytes 2211844
  114.0 22.8 %collective-permute-start.22 = (bf16[2,5,96,384]{3,2,1,0:T(8,128)(2,1)}, bf16[2,5,96,384]{3,2,1,0:T(8,128)(2,1)S(1)}, u32[]{:S(2)}, u32[]{:S(2)}) collective-permute-start(bf16[2,5,96,384]{3,2,1,0:T(8,128)(2,1)} %pad_maximum_fusion), channel_id=1, source_target_pairs={{0,2},{1,3},{2,0},{3,1},{4,6},{5,7},{6,4},{7,5},{8,10},{9,11},{10,... | collective-permute-start | bytes 2211848 | tf_op jit(solution)/shard_map/ppermute | solution.py:26
  117.3 2.9 %copy-start.31 = (bf16[21,96,384]{2,1,0:T(8,128)(2,1)}, bf16[21,96,384]{2,1,0:T(8,128)(2,1)S(1)}, u32[]{:S(2)}) copy-start(bf16[21,96,384]{2,1,0:T(8,128)(2,1)S(1)} %collective-permute-done.15.refs_4_) | copy-start | bytes 4644868
  117.3 19.5 %collective-permute-start.23 = (bf16[9,96,384]{2,1,0:T(8,128)(2,1)}, bf16[9,96,384]{2,1,0:T(8,128)(2,1)}, u32[]{:S(2)}, u32[]{:S(2)}) collective-permute-start(bf16[9,96,384]{2,1,0:T(8,128)(2,1)} %slice.85), channel_id=1, source_target_pairs={{0,8},{8,0},{16,24},{24,16},{1,9},{9,1},{17,25},{25,17},{2,10},{10... | collective-permute-start | bytes 1990664 | tf_op jit(solution)/shard_map/ppermute | solution.py:26
  120.0 18.1 %collective-permute-start.14 = (bf16[9,96,384]{2,1,0:T(8,128)(2,1)}, bf16[9,96,384]{2,1,0:T(8,128)(2,1)}, u32[]{:S(2)}, u32[]{:S(2)}) collective-permute-start(bf16[9,96,384]{2,1,0:T(8,128)(2,1)} %slice.82), channel_id=1, source_target_pairs={{0,16},{8,24},{16,0},{24,8},{1,17},{9,25},{17,1},{25,9},{2,18},{10... | collective-permute-start | bytes 1990664 | tf_op jit(solution)/shard_map/ppermute | solution.py:26
  120.2 2.2 %copy-start.33 = (bf16[21,96,384]{2,1,0:T(8,128)(2,1)}, bf16[21,96,384]{2,1,0:T(8,128)(2,1)S(1)}, u32[]{:S(2)}) copy-start(bf16[21,96,384]{2,1,0:T(8,128)(2,1)S(1)} %collective-permute-done.16.refs_6_) | copy-start | bytes 4644868
  137.7 5.2 %collective-permute-start.25 = (bf16[9,96,384]{2,1,0:T(8,128)(2,1)}, bf16[9,96,384]{2,1,0:T(8,128)(2,1)S(1)}, u32[]{:S(2)}, u32[]{:S(2)}) collective-permute-start(bf16[9,96,384]{2,1,0:T(8,128)(2,1)} %after.24.refs_4_.refs_9_), channel_id=1, source_target_pairs={{0,1},{1,0},{2,3},{3,2},{4,5},{5,4},{6,7},{7,6},{8,9},{9,8},{10,11... | collective-permute-start | bytes 1990664 | tf_op jit(solution)/shard_map/ppermute | solution.py:26
  138.0 4.9 %collective-permute-start.24 = (bf16[9,96,384]{2,1,0:T(8,128)(2,1)}, bf16[9,96,384]{2,1,0:T(8,128)(2,1)S(1)}, u32[]{:S(2)}, u32[]{:S(2)}) collective-permute-start(bf16[9,96,384]{2,1,0:T(8,128)(2,1)} %after.23.refs_3_.refs_7_), channel_id=1, source_target_pairs={{0,1},{1,0},{2,3},{3,2},{4,5},{5,4},{6,7},{7,6},{8,9},{9,8},{10,11... | collective-permute-start | bytes 1990664 | tf_op jit(solution)/shard_map/ppermute | solution.py:26
  140.3 19.4 %collective-permute-start.26 = (bf16[1,5,96,384]{3,2,1,0:T(8,128)(2,1)S(1)}, bf16[1,5,96,384]{3,2,1,0:T(8,128)(2,1)S(1)}, u32[]{:S(2)}, u32[]{:S(2)}) collective-permute-start(bf16[1,5,96,384]{3,2,1,0:T(8,128)(2,1)S(1)} %add_convert_fusion), channel_id=1, source_target_pairs={{0,6},{1,7},{2,4},{3,5},{4,2},{5,3},{6,0},{7,1},{8,14},{9,15},{10,... | collective-permute-start | bytes 1105928 | tf_op jit(solution)/shard_map/ppermute | solution.py:26
  156.3 4.2 %copy-start.36 = (bf16[2,5,96,384]{3,2,1,0:T(8,128)(2,1)S(1)}, bf16[2,5,96,384]{3,2,1,0:T(8,128)(2,1)}, u32[]{:S(2)}) copy-start(bf16[2,5,96,384]{3,2,1,0:T(8,128)(2,1)} %copy-done.35) | copy-start | bytes 2211844
  (26 other events, 28.5 us)

commit v27 on v24

--- a/solution.py
+++ b/solution.py
@@ -12,7 +12,7 @@
 HALO = 32
 EDGE = 16
 MARGIN = HALO - EDGE
-STEP = 64
+STEP = 128
 SPLIT = 3
 ROOT = math.sqrt(2.0 / math.pi)
 CUBIC = 0.044715

time: 161 us -> 161 us (level)
  no operation moved by 1% of the time
where the time goes in v27:
time: 161 us; the launch traced here: 160 us
  Pallas kernels  57.1 us (35%)
  local copies, waits for them, and re-layouts  31.6 us (20%)
  starting transfers between devices  29.2 us (18%)
  waiting for transfers between devices  28.3 us (18%)
  other arithmetic  12.6 us (8%)
    ppermute x27, starting transfers between devices, from_peer(): return lax.ppermute(value, axis, [(i, i ^ distance) for i in range(peers)])  29.2 us
    ppermute x27, waiting for transfers between devices, from_peer(): return lax.ppermute(value, axis, [(i, i ^ distance) for i in range(peers)])  28.3 us
    pallas_call x2, Pallas kernels, gradient_stage(): pl.pallas_call(body, out_shape=out_shape, grid_spec=pltpu.PrefetchScalarG...  26.1 us
    unnamed x92, local copies, waits for them, and re-layouts  19.2 us
    pallas_call x1, Pallas kernels, early_terms(): pl.pallas_call(kernel, out_shape=jax.ShapeDtypeStruct((both, columns), jn...  13.9 us
    pallas_call x1, Pallas kernels, late_terms(): pl.pallas_call(kernel, out_shape=(jax.ShapeDtypeStruct(shape, jnp.float32...  9.9 us
    concatenate x1, other arithmetic, on_device_square(): shifts = jnp.concatenate([later, trunk, earlier], axis=1)  5.38 us
    slice x2, local copies, waits for them, and re-layouts, on_device_square(): top, bottom = (after(beside[:half], *ready), after(below[half:], *ready))  4.15 us
  transfers between devices with their start and end apart: 27, of which 5 were waited for; matrix products, arithmetic and copies ran while one was open for 14% of the time, Pallas kernels for 36%

profile of v27, /device:TPU:9, one launch (start us, length us, event | category | flops | bytes accessed | tf_op | source)
XLA Modules:
  0.0 159.7 jit_solution(8076710030341209393)
XLA Ops:
  0.6 1.0 slice.60.refs_0_
  1.6 1.4 collective-permute-start.1
  3.0 0.9 slice_bitcast_fusion.2
  3.9 1.3 collective-permute-start.3
  5.2 1.2 collective-permute-start.4
  6.6 2.2 %collective-permute-start = (bf16[3,96,384]{2,1,0:T(8,128)(2,1)S(1)}, bf16[3,96,384]{2,1,0:T(8,128)(2,1)S(1)}, u32[]{:S(2)}, u32[]{:S(2)}) collective-permute-start(bf16[3,96,384]{2,1,0:T(8,128)(2,1)S(1)} %slice.60.refs_0_), channel_id=1, source_target_pairs={{0,2},{1,3},{2,0},{3,1},{4,6},{5,7},{6,4},{7,5},{8,10},{9,11},{10,... | collective-permute-start | bytes 663560 | tf_op jit(solution)/shard_map/ppermute | solution.py:26
  8.8 1.4 copy-done.10
  10.2 2.1 %act.1.refs_0_ = bf16[512,1536]{1,0:T(8,128)(2,1)S(1)} custom-call(bf16[1,1024,768]{2,1,0:T(8,128)(2,1)S(1)} %copy-done.10), custom_call_target="tpu_custom_call" | custom-call | flops 1048576 | bytes 65536 | tf_op jit(solution)/shard_map/act/pallas_call | solution.py:85
  12.3 1.1 copy-done.3
  14.8 1.2 collective-permute-start.10
  16.0 1.2 collective-permute-start.6
  17.3 2.1 %slice_bitcast_fusion.1 = (bf16[2047,384]{1,0:T(8,128)(2,1)}, bf16[2047,384]{1,0:T(8,128)(2,1)}) fusion(bf16[1,2048,384]{2,1,0:T(8,128)(2,1)S(1)} %copy-done.2), kind=kLoop, calls=%fused_computation.7 | loop fusion | bytes 6288384 | tf_op jit(solution)/shard_map/slice | solution.py:505
  19.4 0.9 pad_maximum_fusion.1.refs_0_
  20.3 2.1 %collective-permute-done.2.refs_2_.refs_3_ = bf16[3,96,384]{2,1,0:T(8,128)(2,1)S(1)} collective-permute-done((bf16[3,96,384]{2,1,0:T(8,128)(2,1)S(1)}, bf16[3,96,384]{2,1,0:T(8,128)(2,1)S(1)}, u32[]{:S(2)}, u32[]{:S(2)}) %collective-permute-start.2) | collective-permute-done | bytes 221216 | tf_op jit(solution)/shard_map/ppermute | solution.py:26
  23.5 5.4 %fusion.2.refs_2_.shifts_ref = bf16[2048,1152]{1,0:T(8,128)(2,1)} fusion(bf16[2047,384]{1,0:T(8,128)(2,1)} %get-tuple-element.17, bf16[2047,384]{1,0:T(8,128)(2,1)} %get-tuple-element.16, bf16[2048,384]{1,0:T(8,128)(2,1)S(1)} %bitcast.14), kind=kLoop, calls=%fused_computation.4 | loop fusion | flops 23592960 | bytes 9435648 | tf_op jit(solution)/shard_map/concatenate | solution.py:507
  28.9 2.3 %half_slope.1.refs_1_.refs_11_ = f32[2,512,768]{2,1,0:T(8,128)S(1)} custom-call(bf16[1,1024,768]{2,1,0:T(8,128)(2,1)S(1)} %copy-done.11), custom_call_target="tpu_custom_call" | custom-call | tf_op jit(solution)/shard_map/half_slope/pallas_call | solution.py:167
  31.2 1.6 %copy-done.1 = f32[2,512,768]{2,1,0:T(8,128)} copy-done((f32[2,512,768]{2,1,0:T(8,128)}, f32[2,512,768]{2,1,0:T(8,128)S(1)}, u32[]{:S(2)}) %copy-start.1) | copy-done | bytes 3145752
  32.9 0.9 copy-done.25
  33.9 1.0 kernel_messages.1
  34.9 1.1 copy-done.5
  36.0 1.2 copy-done.12
  37.2 11.7 %collective-permute-done.10.refs_2_ = bf16[512,1536]{1,0:T(8,128)(2,1)} collective-permute-done((bf16[512,1536]{1,0:T(8,128)(2,1)}, bf16[512,1536]{1,0:T(8,128)(2,1)}, u32[]{:S(2)}, u32[]{:S(2)}) %collective-permute-start.10) | collective-permute-done | bytes 1572896 | tf_op jit(solution)/shard_map/ppermute | solution.py:26
  48.9 2.1 %slice.81.refs_0_ = bf16[256,1536]{1,0:T(8,128)(2,1)} slice(bf16[512,1536]{1,0:T(8,128)(2,1)} %collective-permute-done.10.refs_2_), slice={[256:512], [0:1536]} | slice | bytes 1572864 | tf_op jit(solution)/shard_map/slice | solution.py:510
  52.0 1.2 collective-permute-start.11
  53.2 2.1 %slice.80.refs_0_ = bf16[256,1536]{1,0:T(8,128)(2,1)} slice(bf16[512,1536]{1,0:T(8,128)(2,1)} %collective-permute-done.6.refs_1_), slice={[0:256], [0:1536]} | slice | bytes 1572864 | tf_op jit(solution)/shard_map/slice | solution.py:510
  55.3 1.2 collective-permute-start.9
  56.7 13.9 %weight_grad_early.1.refs_1_.early_ref = f32[1536,1152]{1,0:T(8,128)} custom-call(s32[2]{0:T(128)S(1)} %pad_add_fusion.place, bf16[2048,1152]{1,0:T(8,128)(2,1)} %fusion.2.refs_2_.shifts_ref, bf16[512,1536]{1,0:T(8,128)(2,1)S(1)} %copy-done.4, bf16[512,1536]{1,0:T(8,128)(2,1)} %collective-permute-done.6.refs_1_, ...), custom_call_target="tpu_custom_call" | custom-call | flops 1048576 | bytes 65536 | tf_op jit(solution)/shard_map/weight_grad_early/pallas_call | solution.py:213
  70.6 0.9 copy-done.6
  72.4 1.2 collective-permute-start.13
  75.1 1.8 %stack_planes.1.refs_9_.refs_10_.refs_11_.refs_5_ = bf16[4,4,2,96,384]{4,3,2,1,0:T(8,128)(2,1)S(1)} custom-call(s32[2]{0:T(128)S(1)} %pad_add_fusion.place, bf16[4,2,96,384]{3,2,1,0:T(8,128)(2,1)S(1)} %copy-done.14, bf16[4,2,96,384]{3,2,1,0:T(8,128)(2,1)S(1)} %copy-done.18, bf16[4,2,96,384]{3,2,1,0:T(8,128)(2,1)} %after.20.refs_2_, ...), custom_call_target="tpu_custom_call" | custom-call | flops 1048576 | bytes 65536 | tf_op jit(solution)/shard_map/stack_planes/pallas_call | solution.py:471
  76.9 4.3 %collective-permute-start.19 = (bf16[4,4,2,96,384]{4,3,2,1,0:T(8,128)(2,1)S(1)}, bf16[4,4,2,96,384]{4,3,2,1,0:T(8,128)(2,1)S(1)}, u32[]{:S(2)}, u32[]{:S(2)}) collective-permute-start(bf16[4,4,2,96,384]{4,3,2,1,0:T(8,128)(2,1)S(1)} %stack_planes.1.refs_9_.refs_10_.refs_11_.refs_5_), channel_id=1, source_target_pairs={{0,1},{1,0},{2,3},{3,2},{4,5},{5,4},{6,7},{7,6},{8,9},{9,8},{10,11... | collective-permute-start | bytes 7077896 | tf_op jit(solution)/shard_map/ppermute | solution.py:26
  81.2 9.9 %weight_grad_late.1 = (f32[4,5,96,384]{3,2,1,0:T(8,128)}, bf16[2,5,96,384]{3,2,1,0:T(8,128)(2,1)S(1)}, bf16[2,5,96,384]{3,2,1,0:T(8,128)(2,1)S(1)}) custom-call(s32[2]{0:T(128)S(1)} %pad_add_fusion.place, bf16[2048,1152]{1,0:T(8,128)(2,1)} %fusion.2.refs_2_.shifts_ref, f32[1536,1152]{1,0:T(8,128)} %weight_grad_early.1.refs_1_.early_ref, ...), custom_call_target="tpu_custom_call" | custom-call | flops 1048576 | bytes 65536 | tf_op jit(solution)/shard_map/weight_grad_late/pallas_call | solution.py:289
  91.9 1.8 %collective-permute-done.20 = bf16[2,5,96,384]{3,2,1,0:T(8,128)(2,1)S(1)} collective-permute-done((bf16[2,5,96,384]{3,2,1,0:T(8,128)(2,1)S(1)}, bf16[2,5,96,384]{3,2,1,0:T(8,128)(2,1)S(1)}, u32[]{:S(2)}, u32[]{:S(2)}) %collective-permute-start.20) | collective-permute-done | bytes 737312 | tf_op jit(solution)/shard_map/ppermute | solution.py:26
  94.0 10.1 %collective-permute-done.13.refs_2_.refs_7_ = bf16[21,96,384]{2,1,0:T(8,128)(2,1)} collective-permute-done((bf16[21,96,384]{2,1,0:T(8,128)(2,1)}, bf16[21,96,384]{2,1,0:T(8,128)(2,1)}, u32[]{:S(2)}, u32[]{:S(2)}) %collective-permute-start.13) | collective-permute-done | bytes 1548320 | tf_op jit(solution)/shard_map/ppermute | solution.py:26
  104.1 4.9 %collective-permute-start.17 = (bf16[21,96,384]{2,1,0:T(8,128)(2,1)}, bf16[21,96,384]{2,1,0:T(8,128)(2,1)S(1)}, u32[]{:S(2)}, u32[]{:S(2)}) collective-permute-start(bf16[21,96,384]{2,1,0:T(8,128)(2,1)} %collective-permute-done.13.refs_2_.refs_7_), channel_id=1, source_target_pairs={{0,1},{1,0},{2,3},{3,2},{4,5},{5,4},{6,7},{7,6},{8,9},{9,8},{10,11... | collective-permute-start | bytes 4644872 | tf_op jit(solution)/shard_map/ppermute | solution.py:26
  109.0 1.3 collective-permute-start.16
  110.3 1.8 %add_convert_fusion.2 = (bf16[1,5,96,384]{3,2,1,0:T(8,128)(2,1)S(1)}, bf16[1,5,96,384]{3,2,1,0:T(8,128)(2,1)S(1)}) fusion(f32[4,5,96,384]{3,2,1,0:T(8,128)} %get-tuple-element.11, bf16[2,5,96,384]{3,2,1,0:T(8,128)(2,1)S(1)} %collective-permute-done.20, bf16[2,5,96,384]{3,2,1,0:T(8,128)(2,1)S(1)} %collective-permute-done.21), kind=kLoop, calls=%fused_computation.12 | loop fusion | flops 1105920 | bytes 2949120 | tf_op jit(solution)/shard_map/convert_element_type | solution.py:46
  112.0 0.9 pad_maximum_fusion
  113.3 2.0 %slice.85 = bf16[9,96,384]{2,1,0:T(8,128)(2,1)} slice(bf16[21,96,384]{2,1,0:T(8,128)(2,1)} %collective-permute-done.13.refs_2_.refs_7_), slice={[6:15], [0:96], [0:384]} | slice | bytes 1327104 | tf_op jit(solution)/shard_map/slice | solution.py:550
  115.6 2.3 %slice.82 = bf16[9,96,384]{2,1,0:T(8,128)(2,1)} slice(bf16[21,96,384]{2,1,0:T(8,128)(2,1)} %collective-permute-done.12.refs_1_.refs_5_), slice={[0:9], [0:96], [0:384]} | slice | bytes 1327104 | tf_op jit(solution)/shard_map/slice | solution.py:549
  117.9 1.2 collective-permute-start.14
  119.3 0.9 copy-done.31
  120.9 14.2 %input_grad.2.refs_1_.refs_12_ = f32[2,512,768]{2,1,0:T(8,128)} custom-call(s32[2]{0:T(128)} %copy-done.26, bf16[6,96,384]{2,1,0:T(8,128)(2,1)} %copy-done.19, bf16[21,96,384]{2,1,0:T(8,128)(2,1)} %collective-permute-done.12.refs_1_.refs_5_, bf16[21,96,384]{2,1,0:T(8,128)(2,1)} %collective-permute-done.13.refs_2_.refs_7_, ...), custom_call_target="tpu_custom_call" | custom-call | flops 1048576 | bytes 65536 | tf_op jit(solution)/shard_map/input_grad/pallas_call | solution.py:447
  137.3 1.2 add_convert_fusion
  138.5 2.0 %collective-permute-start.26 = (bf16[1,5,96,384]{3,2,1,0:T(8,128)(2,1)S(1)}, bf16[1,5,96,384]{3,2,1,0:T(8,128)(2,1)S(1)}, u32[]{:S(2)}, u32[]{:S(2)}) collective-permute-start(bf16[1,5,96,384]{3,2,1,0:T(8,128)(2,1)S(1)} %add_convert_fusion), channel_id=1, source_target_pairs={{0,6},{1,7},{2,4},{3,5},{4,2},{5,3},{6,0},{7,1},{8,14},{9,15},{10,... | collective-permute-start | bytes 1105928 | tf_op jit(solution)/shard_map/ppermute | solution.py:26
  142.3 11.9 %input_grad.3.refs_1_ = bf16[1,1024,768]{2,1,0:T(8,128)(2,1)} custom-call(s32[2]{0:T(128)} %copy-done.26, bf16[6,96,384]{2,1,0:T(8,128)(2,1)} %copy-done.19, bf16[21,96,384]{2,1,0:T(8,128)(2,1)} %collective-permute-done.12.refs_1_.refs_5_, bf16[21,96,384]{2,1,0:T(8,128)(2,1)} %collective-permute-done.13.refs_2_.refs_7_, ...), custom_call_target="tpu_custom_call" | custom-call | flops 1048576 | bytes 65536 | tf_op jit(solution)/shard_map/input_grad/pallas_call | solution.py:447
  154.2 2.5 %collective-permute-done.26.refs_0_ = bf16[1,5,96,384]{3,2,1,0:T(8,128)(2,1)S(1)} collective-permute-done((bf16[1,5,96,384]{3,2,1,0:T(8,128)(2,1)S(1)}, bf16[1,5,96,384]{3,2,1,0:T(8,128)(2,1)S(1)}, u32[]{:S(2)}, u32[]{:S(2)}) %collective-permute-start.26) | collective-permute-done | bytes 368672 | tf_op jit(solution)/shard_map/ppermute | solution.py:26
  157.4 2.2 %add_bitcast_fusion = f32[5,96,384]{2,1,0:T(8,128)} fusion(bf16[1,5,96,384]{3,2,1,0:T(8,128)(2,1)} %after.23, f32[4,5,96,384]{3,2,1,0:T(8,128)} %get-tuple-element.11, bf16[2,5,96,384]{3,2,1,0:T(8,128)(2,1)S(1)} %copy-done.29, bf16[2,5,96,384]{3,2,1,0:T(8,128)(2,1)S(1)} %copy-done.35), kind=kLoop, calls=%fused_computation.9 | loop fusion | flops 1105920 | bytes 2580480 | tf_op jit(solution)/shard_map/add | solution.py:576
  (132 shorter events, 13.4 us)
Async XLA Ops:
  1.6 15.7 %collective-permute-start.1 = (bf16[3,96,384]{2,1,0:T(8,128)(2,1)S(1)}, bf16[3,96,384]{2,1,0:T(8,128)(2,1)S(1)}, u32[]{:S(2)}, u32[]{:S(2)}) collective-permute-start(bf16[3,96,384]{2,1,0:T(8,128)(2,1)S(1)} %slice.60.refs_0_), channel_id=1, source_target_pairs={{0,6},{1,7},{2,4},{3,5},{4,2},{5,3},{6,0},{7,1},{8,14},{9,15},{10,... | collective-permute-start | bytes 663560 | tf_op jit(solution)/shard_map/ppermute | solution.py:26
  3.9 9.5 %collective-permute-start.3 = (bf16[2,96,384]{2,1,0:T(8,128)(2,1)S(1)}, bf16[2,96,384]{2,1,0:T(8,128)(2,1)S(1)}, u32[]{:S(2)}, u32[]{:S(2)}) collective-permute-start(bf16[2,96,384]{2,1,0:T(8,128)(2,1)S(1)} %get-tuple-element.19), channel_id=1, source_target_pairs={{0,8},{8,0},{16,24},{24,16},{1,9},{9,1},{17,25},{25,17},{2,10},{10... | collective-permute-start | bytes 442376 | tf_op jit(solution)/shard_map/ppermute | solution.py:26
  5.2 8.3 %collective-permute-start.4 = (bf16[2,96,384]{2,1,0:T(8,128)(2,1)S(1)}, bf16[2,96,384]{2,1,0:T(8,128)(2,1)S(1)}, u32[]{:S(2)}, u32[]{:S(2)}) collective-permute-start(bf16[2,96,384]{2,1,0:T(8,128)(2,1)S(1)} %get-tuple-element.19), channel_id=1, source_target_pairs={{0,16},{8,24},{16,0},{24,8},{1,17},{9,25},{17,1},{25,9},{2,18},{10... | collective-permute-start | bytes 442376 | tf_op jit(solution)/shard_map/ppermute | solution.py:26
  6.4 7.0 %collective-permute-start.5 = (bf16[2,96,384]{2,1,0:T(8,128)(2,1)S(1)}, bf16[2,96,384]{2,1,0:T(8,128)(2,1)S(1)}, u32[]{:S(2)}, u32[]{:S(2)}) collective-permute-start(bf16[2,96,384]{2,1,0:T(8,128)(2,1)S(1)} %get-tuple-element.19), channel_id=1, source_target_pairs={{0,24},{8,16},{16,8},{24,0},{1,25},{9,17},{17,9},{25,1},{2,26},{10... | collective-permute-start | bytes 442376 | tf_op jit(solution)/shard_map/ppermute | solution.py:26
  6.6 13.7 %collective-permute-start = (bf16[3,96,384]{2,1,0:T(8,128)(2,1)S(1)}, bf16[3,96,384]{2,1,0:T(8,128)(2,1)S(1)}, u32[]{:S(2)}, u32[]{:S(2)}) collective-permute-start(bf16[3,96,384]{2,1,0:T(8,128)(2,1)S(1)} %slice.60.refs_0_), channel_id=1, source_target_pairs={{0,2},{1,3},{2,0},{3,1},{4,6},{5,7},{6,4},{7,5},{8,10},{9,11},{10,... | collective-permute-start | bytes 663560 | tf_op jit(solution)/shard_map/ppermute | solution.py:26
  13.4 3.8 %copy-start.2 = (bf16[1,2048,384]{2,1,0:T(8,128)(2,1)S(1)}, bf16[1,2048,384]{2,1,0:T(8,128)(2,1)}, u32[]{:S(2)}) copy-start(bf16[1,2048,384]{2,1,0:T(8,128)(2,1)} %refs_4_.1) | copy-start | bytes 4718596
  14.8 4.6 %copy-start.41 = (bf16[2,96,384]{2,1,0:T(8,128)(2,1)S(1)}, bf16[2,96,384]{2,1,0:T(8,128)(2,1)}, u32[]{:S(2)}) copy-start(bf16[2,96,384]{2,1,0:T(8,128)(2,1)} %copy-done.40) | copy-start | bytes 442372
  14.8 4.6 %copy-start.43 = (bf16[2,96,384]{2,1,0:T(8,128)(2,1)S(1)}, bf16[2,96,384]{2,1,0:T(8,128)(2,1)}, u32[]{:S(2)}) copy-start(bf16[2,96,384]{2,1,0:T(8,128)(2,1)} %copy-done.42) | copy-start | bytes 442372
  14.8 4.6 %copy-start.45 = (bf16[2,96,384]{2,1,0:T(8,128)(2,1)S(1)}, bf16[2,96,384]{2,1,0:T(8,128)(2,1)}, u32[]{:S(2)}) copy-start(bf16[2,96,384]{2,1,0:T(8,128)(2,1)} %copy-done.44) | copy-start | bytes 442372
  14.8 34.1 %collective-permute-start.10 = (bf16[512,1536]{1,0:T(8,128)(2,1)}, bf16[512,1536]{1,0:T(8,128)(2,1)}, u32[]{:S(2)}, u32[]{:S(2)}) collective-permute-start(bf16[512,1536]{1,0:T(8,128)(2,1)} %after.12.refs_1_.refs_0_), channel_id=1, source_target_pairs={{0,16},{8,24},{16,0},{24,8},{1,17},{9,25},{17,1},{25,9},{2,18},{10... | collective-permute-start | bytes 4718600 | tf_op jit(solution)/shard_map/ppermute | solution.py:26
  16.0 37.2 %collective-permute-start.6 = (bf16[512,1536]{1,0:T(8,128)(2,1)}, bf16[512,1536]{1,0:T(8,128)(2,1)}, u32[]{:S(2)}, u32[]{:S(2)}) collective-permute-start(bf16[512,1536]{1,0:T(8,128)(2,1)} %after.12.refs_1_.refs_0_), channel_id=1, source_target_pairs={{0,8},{8,0},{16,24},{24,16},{1,9},{9,1},{17,25},{25,17},{2,10},{10... | collective-permute-start | bytes 4718600 | tf_op jit(solution)/shard_map/ppermute | solution.py:26
  17.2 2.1 %copy-start.20 = (bf16[3,96,384]{2,1,0:T(8,128)(2,1)}, bf16[3,96,384]{2,1,0:T(8,128)(2,1)S(1)}, u32[]{:S(2)}) copy-start(bf16[3,96,384]{2,1,0:T(8,128)(2,1)S(1)} %collective-permute-done.1.refs_3_.refs_4_) | copy-start | bytes 663556
  17.2 5.2 %collective-permute-start.2 = (bf16[3,96,384]{2,1,0:T(8,128)(2,1)S(1)}, bf16[3,96,384]{2,1,0:T(8,128)(2,1)S(1)}, u32[]{:S(2)}, u32[]{:S(2)}) collective-permute-start(bf16[3,96,384]{2,1,0:T(8,128)(2,1)S(1)} %collective-permute-done.1.refs_3_.refs_4_), channel_id=1, source_target_pairs={{0,2},{1,3},{2,0},{3,1},{4,6},{5,7},{6,4},{7,5},{8,10},{9,11},{10,... | collective-permute-start | bytes 663560 | tf_op jit(solution)/shard_map/ppermute | solution.py:26
  20.3 2.1 %copy-start.22 = (bf16[3,96,384]{2,1,0:T(8,128)(2,1)}, bf16[3,96,384]{2,1,0:T(8,128)(2,1)S(1)}, u32[]{:S(2)}) copy-start(bf16[3,96,384]{2,1,0:T(8,128)(2,1)S(1)} %collective-permute-done.refs_1_.refs_2_) | copy-start | bytes 663556
  23.1 27.8 %collective-permute-start.8 = (bf16[4,2,96,384]{3,2,1,0:T(8,128)(2,1)}, bf16[4,2,96,384]{3,2,1,0:T(8,128)(2,1)S(1)}, u32[]{:S(2)}, u32[]{:S(2)}) collective-permute-start(bf16[4,2,96,384]{3,2,1,0:T(8,128)(2,1)} %after.13.refs_0_), channel_id=1, source_target_pairs={{0,6},{1,7},{2,4},{3,5},{4,2},{5,3},{6,0},{7,1},{8,14},{9,15},{10,... | collective-permute-start | bytes 1769480 | tf_op jit(solution)/shard_map/ppermute | solution.py:26
  23.1 27.8 %collective-permute-start.7 = (bf16[4,2,96,384]{3,2,1,0:T(8,128)(2,1)}, bf16[4,2,96,384]{3,2,1,0:T(8,128)(2,1)S(1)}, u32[]{:S(2)}, u32[]{:S(2)}) collective-permute-start(bf16[4,2,96,384]{3,2,1,0:T(8,128)(2,1)} %after.13.refs_0_), channel_id=1, source_target_pairs={{0,2},{1,3},{2,0},{3,1},{4,6},{5,7},{6,4},{7,5},{8,10},{9,11},{10,... | collective-permute-start | bytes 1769480 | tf_op jit(solution)/shard_map/ppermute | solution.py:26
  23.5 5.4 %copy-start.11 = (bf16[1,1024,768]{2,1,0:T(8,128)(2,1)S(1)}, bf16[1,1024,768]{2,1,0:T(8,128)(2,1)}, u32[]{:S(2)}) copy-start(bf16[1,1024,768]{2,1,0:T(8,128)(2,1)} %x_ref.3) | copy-start | bytes 4718596
  28.9 4.1 %copy-start.21 = (bf16[3,96,384]{2,1,0:T(8,128)(2,1)S(1)}, bf16[3,96,384]{2,1,0:T(8,128)(2,1)}, u32[]{:S(2)}) copy-start(bf16[3,96,384]{2,1,0:T(8,128)(2,1)} %copy-done.20) | copy-start | bytes 663556
  28.9 4.1 %copy-start.23 = (bf16[3,96,384]{2,1,0:T(8,128)(2,1)S(1)}, bf16[3,96,384]{2,1,0:T(8,128)(2,1)}, u32[]{:S(2)}) copy-start(bf16[3,96,384]{2,1,0:T(8,128)(2,1)} %copy-done.22) | copy-start | bytes 663556
  31.2 1.6 %copy-start.1 = (f32[2,512,768]{2,1,0:T(8,128)}, f32[2,512,768]{2,1,0:T(8,128)S(1)}, u32[]{:S(2)}) copy-start(f32[2,512,768]{2,1,0:T(8,128)S(1)} %half_slope.1.refs_1_.refs_11_) | copy-start | bytes 9437188
  33.9 47.3 %copy-start.26 = (s32[2]{0:T(128)}, s32[2]{0:T(128)S(1)}, u32[]{:S(2)}) copy-start(s32[2]{0:T(128)S(1)} %pad_add_fusion.place) | copy-start | bytes 28
  37.2 13.8 %copy-start.19 = (bf16[6,96,384]{2,1,0:T(8,128)(2,1)}, bf16[6,96,384]{2,1,0:T(8,128)(2,1)S(1)}, u32[]{:S(2)}) copy-start(bf16[6,96,384]{2,1,0:T(8,128)(2,1)S(1)} %get-tuple-element.8.refs_0_) | copy-start | bytes 1327108
  52.0 18.6 %collective-permute-start.11 = (bf16[256,1536]{1,0:T(8,128)(2,1)}, bf16[256,1536]{1,0:T(8,128)(2,1)S(1)}, u32[]{:S(2)}, u32[]{:S(2)}) collective-permute-start(bf16[256,1536]{1,0:T(8,128)(2,1)} %after.16), channel_id=1, source_target_pairs={{0,8},{8,0},{16,24},{24,16},{1,9},{9,1},{17,25},{25,17},{2,10},{10... | collective-permute-start | bytes 2359304 | tf_op jit(solution)/shard_map/ppermute | solution.py:26
  55.3 16.2 %collective-permute-start.9 = (bf16[256,1536]{1,0:T(8,128)(2,1)}, bf16[256,1536]{1,0:T(8,128)(2,1)S(1)}, u32[]{:S(2)}, u32[]{:S(2)}) collective-permute-start(bf16[256,1536]{1,0:T(8,128)(2,1)} %after.14), channel_id=1, source_target_pairs={{0,16},{8,24},{16,0},{24,8},{1,17},{9,25},{17,1},{25,9},{2,18},{10... | collective-permute-start | bytes 2359304 | tf_op jit(solution)/shard_map/ppermute | solution.py:26
  56.6 17.4 %collective-permute-start.18 = (bf16[4,2,96,384]{3,2,1,0:T(8,128)(2,1)}, bf16[4,2,96,384]{3,2,1,0:T(8,128)(2,1)}, u32[]{:S(2)}, u32[]{:S(2)}) collective-permute-start(bf16[4,2,96,384]{3,2,1,0:T(8,128)(2,1)} %copy-done.15), channel_id=1, source_target_pairs={{0,2},{1,3},{2,0},{3,1},{4,6},{5,7},{6,4},{7,5},{8,10},{9,11},{10,... | collective-permute-start | bytes 1769480 | tf_op jit(solution)/shard_map/ppermute | solution.py:26
  72.4 31.7 %collective-permute-start.13 = (bf16[21,96,384]{2,1,0:T(8,128)(2,1)}, bf16[21,96,384]{2,1,0:T(8,128)(2,1)}, u32[]{:S(2)}, u32[]{:S(2)}) collective-permute-start(bf16[21,96,384]{2,1,0:T(8,128)(2,1)} %after.19.refs_3_), channel_id=1, source_target_pairs={{0,16},{8,24},{16,0},{24,8},{1,17},{9,25},{17,1},{25,9},{2,18},{10... | collective-permute-start | bytes 4644872 | tf_op jit(solution)/shard_map/ppermute | solution.py:26
  73.7 35.3 %collective-permute-start.12 = (bf16[21,96,384]{2,1,0:T(8,128)(2,1)}, bf16[21,96,384]{2,1,0:T(8,128)(2,1)}, u32[]{:S(2)}, u32[]{:S(2)}) collective-permute-start(bf16[21,96,384]{2,1,0:T(8,128)(2,1)} %after.18), channel_id=1, source_target_pairs={{0,8},{8,0},{16,24},{24,16},{1,9},{9,1},{17,25},{25,17},{2,10},{10... | collective-permute-start | bytes 4644872 | tf_op jit(solution)/shard_map/ppermute | solution.py:26
  75.1 6.1 %copy-start.7 = (bf16[256,1536]{1,0:T(8,128)(2,1)S(1)}, bf16[256,1536]{1,0:T(8,128)(2,1)}, u32[]{:S(2)}) copy-start(bf16[256,1536]{1,0:T(8,128)(2,1)} %after.17.refs_2_.refs_1_) | copy-start | bytes 2359300
  75.1 6.1 %copy-start.9 = (bf16[256,1536]{1,0:T(8,128)(2,1)S(1)}, bf16[256,1536]{1,0:T(8,128)(2,1)}, u32[]{:S(2)}) copy-start(bf16[256,1536]{1,0:T(8,128)(2,1)} %after.15.refs_1_.refs_0_) | copy-start | bytes 2359300
  76.9 14.2 %copy-start = (bf16[4,4,2,96,384]{4,3,2,1,0:T(8,128)(2,1)}, bf16[4,4,2,96,384]{4,3,2,1,0:T(8,128)(2,1)S(1)}, u32[]{:S(2)}) copy-start(bf16[4,4,2,96,384]{4,3,2,1,0:T(8,128)(2,1)S(1)} %stack_planes.1.refs_9_.refs_10_.refs_11_.refs_5_) | copy-start | bytes 7077892
  76.9 14.9 %copy-start.13 = (bf16[21,96,384]{2,1,0:T(8,128)(2,1)S(1)}, bf16[21,96,384]{2,1,0:T(8,128)(2,1)}, u32[]{:S(2)}) copy-start(bf16[21,96,384]{2,1,0:T(8,128)(2,1)} %after.19.refs_3_) | copy-start | bytes 4644868
  76.9 41.0 %collective-permute-start.19 = (bf16[4,4,2,96,384]{4,3,2,1,0:T(8,128)(2,1)S(1)}, bf16[4,4,2,96,384]{4,3,2,1,0:T(8,128)(2,1)S(1)}, u32[]{:S(2)}, u32[]{:S(2)}) collective-permute-start(bf16[4,4,2,96,384]{4,3,2,1,0:T(8,128)(2,1)S(1)} %stack_planes.1.refs_9_.refs_10_.refs_11_.refs_5_), channel_id=1, source_target_pairs={{0,1},{1,0},{2,3},{3,2},{4,5},{5,4},{6,7},{7,6},{8,9},{9,8},{10,11... | collective-permute-start | bytes 7077896 | tf_op jit(solution)/shard_map/ppermute | solution.py:26
  91.1 2.5 %collective-permute-start.20 = (bf16[2,5,96,384]{3,2,1,0:T(8,128)(2,1)S(1)}, bf16[2,5,96,384]{3,2,1,0:T(8,128)(2,1)S(1)}, u32[]{:S(2)}, u32[]{:S(2)}) collective-permute-start(bf16[2,5,96,384]{3,2,1,0:T(8,128)(2,1)S(1)} %get-tuple-element.12), channel_id=1, source_target_pairs={{0,1},{1,0},{2,3},{3,2},{4,5},{5,4},{6,7},{7,6},{8,9},{9,8},{10,11... | collective-permute-start | bytes 2211848 | tf_op jit(solution)/shard_map/ppermute | solution.py:26
  91.8 23.5 %collective-permute-start.15 = (bf16[21,96,384]{2,1,0:T(8,128)(2,1)S(1)}, bf16[21,96,384]{2,1,0:T(8,128)(2,1)S(1)}, u32[]{:S(2)}, u32[]{:S(2)}) collective-permute-start(bf16[21,96,384]{2,1,0:T(8,128)(2,1)S(1)} %copy-done.13), channel_id=1, source_target_pairs={{0,1},{1,0},{2,3},{3,2},{4,5},{5,4},{6,7},{7,6},{8,9},{9,8},{10,11... | collective-permute-start | bytes 4644872 | tf_op jit(solution)/shard_map/ppermute | solution.py:26
  93.7 21.6 %copy-start.34 = (bf16[2,5,96,384]{3,2,1,0:T(8,128)(2,1)}, bf16[2,5,96,384]{3,2,1,0:T(8,128)(2,1)S(1)}, u32[]{:S(2)}) copy-start(bf16[2,5,96,384]{3,2,1,0:T(8,128)(2,1)S(1)} %collective-permute-done.20) | copy-start | bytes 2211844
  93.7 16.6 %collective-permute-start.21 = (bf16[2,5,96,384]{3,2,1,0:T(8,128)(2,1)S(1)}, bf16[2,5,96,384]{3,2,1,0:T(8,128)(2,1)S(1)}, u32[]{:S(2)}, u32[]{:S(2)}) collective-permute-start(bf16[2,5,96,384]{3,2,1,0:T(8,128)(2,1)S(1)} %get-tuple-element.13), channel_id=1, source_target_pairs={{0,1},{1,0},{2,3},{3,2},{4,5},{5,4},{6,7},{7,6},{8,9},{9,8},{10,11... | collective-permute-start | bytes 2211848 | tf_op jit(solution)/shard_map/ppermute | solution.py:26
  104.1 15.0 %collective-permute-start.17 = (bf16[21,96,384]{2,1,0:T(8,128)(2,1)}, bf16[21,96,384]{2,1,0:T(8,128)(2,1)S(1)}, u32[]{:S(2)}, u32[]{:S(2)}) collective-permute-start(bf16[21,96,384]{2,1,0:T(8,128)(2,1)} %collective-permute-done.13.refs_2_.refs_7_), channel_id=1, source_target_pairs={{0,1},{1,0},{2,3},{3,2},{4,5},{5,4},{6,7},{7,6},{8,9},{9,8},{10,11... | collective-permute-start | bytes 4644872 | tf_op jit(solution)/shard_map/ppermute | solution.py:26
  109.0 10.1 %collective-permute-start.16 = (bf16[21,96,384]{2,1,0:T(8,128)(2,1)}, bf16[21,96,384]{2,1,0:T(8,128)(2,1)S(1)}, u32[]{:S(2)}, u32[]{:S(2)}) collective-permute-start(bf16[21,96,384]{2,1,0:T(8,128)(2,1)} %collective-permute-done.12.refs_1_.refs_5_), channel_id=1, source_target_pairs={{0,1},{1,0},{2,3},{3,2},{4,5},{5,4},{6,7},{7,6},{8,9},{9,8},{10,11... | collective-permute-start | bytes 4644872 | tf_op jit(solution)/shard_map/ppermute | solution.py:26
  110.3 5.0 %copy-start.36 = (bf16[2,5,96,384]{3,2,1,0:T(8,128)(2,1)}, bf16[2,5,96,384]{3,2,1,0:T(8,128)(2,1)S(1)}, u32[]{:S(2)}) copy-start(bf16[2,5,96,384]{3,2,1,0:T(8,128)(2,1)S(1)} %collective-permute-done.21) | copy-start | bytes 2211844
  113.0 22.1 %collective-permute-start.22 = (bf16[2,5,96,384]{3,2,1,0:T(8,128)(2,1)}, bf16[2,5,96,384]{3,2,1,0:T(8,128)(2,1)S(1)}, u32[]{:S(2)}, u32[]{:S(2)}) collective-permute-start(bf16[2,5,96,384]{3,2,1,0:T(8,128)(2,1)} %pad_maximum_fusion), channel_id=1, source_target_pairs={{0,2},{1,3},{2,0},{3,1},{4,6},{5,7},{6,4},{7,5},{8,10},{9,11},{10,... | collective-permute-start | bytes 2211848 | tf_op jit(solution)/shard_map/ppermute | solution.py:26
  115.3 3.8 %copy-start.30 = (bf16[21,96,384]{2,1,0:T(8,128)(2,1)}, bf16[21,96,384]{2,1,0:T(8,128)(2,1)S(1)}, u32[]{:S(2)}) copy-start(bf16[21,96,384]{2,1,0:T(8,128)(2,1)S(1)} %collective-permute-done.15.refs_4_) | copy-start | bytes 4644868
  115.3 19.8 %collective-permute-start.23 = (bf16[9,96,384]{2,1,0:T(8,128)(2,1)}, bf16[9,96,384]{2,1,0:T(8,128)(2,1)}, u32[]{:S(2)}, u32[]{:S(2)}) collective-permute-start(bf16[9,96,384]{2,1,0:T(8,128)(2,1)} %slice.85), channel_id=1, source_target_pairs={{0,8},{8,0},{16,24},{24,16},{1,9},{9,1},{17,25},{25,17},{2,10},{10... | collective-permute-start | bytes 1990664 | tf_op jit(solution)/shard_map/ppermute | solution.py:26
  117.9 18.7 %collective-permute-start.14 = (bf16[9,96,384]{2,1,0:T(8,128)(2,1)}, bf16[9,96,384]{2,1,0:T(8,128)(2,1)}, u32[]{:S(2)}, u32[]{:S(2)}) collective-permute-start(bf16[9,96,384]{2,1,0:T(8,128)(2,1)} %slice.82), channel_id=1, source_target_pairs={{0,16},{8,24},{16,0},{24,8},{1,17},{9,25},{17,1},{25,9},{2,18},{10... | collective-permute-start | bytes 1990664 | tf_op jit(solution)/shard_map/ppermute | solution.py:26
  119.1 1.7 %copy-start.32 = (bf16[21,96,384]{2,1,0:T(8,128)(2,1)}, bf16[21,96,384]{2,1,0:T(8,128)(2,1)S(1)}, u32[]{:S(2)}) copy-start(bf16[21,96,384]{2,1,0:T(8,128)(2,1)S(1)} %collective-permute-done.16.refs_6_) | copy-start | bytes 4644868
  136.0 4.6 %collective-permute-start.25 = (bf16[9,96,384]{2,1,0:T(8,128)(2,1)}, bf16[9,96,384]{2,1,0:T(8,128)(2,1)S(1)}, u32[]{:S(2)}, u32[]{:S(2)}) collective-permute-start(bf16[9,96,384]{2,1,0:T(8,128)(2,1)} %after.22.refs_4_.refs_9_), channel_id=1, source_target_pairs={{0,1},{1,0},{2,3},{3,2},{4,5},{5,4},{6,7},{7,6},{8,9},{9,8},{10,11... | collective-permute-start | bytes 1990664 | tf_op jit(solution)/shard_map/ppermute | solution.py:26
  136.6 4.0 %collective-permute-start.24 = (bf16[9,96,384]{2,1,0:T(8,128)(2,1)}, bf16[9,96,384]{2,1,0:T(8,128)(2,1)S(1)}, u32[]{:S(2)}, u32[]{:S(2)}) collective-permute-start(bf16[9,96,384]{2,1,0:T(8,128)(2,1)} %after.21.refs_3_.refs_7_), channel_id=1, source_target_pairs={{0,1},{1,0},{2,3},{3,2},{4,5},{5,4},{6,7},{7,6},{8,9},{9,8},{10,11... | collective-permute-start | bytes 1990664 | tf_op jit(solution)/shard_map/ppermute | solution.py:26
  138.5 18.2 %collective-permute-start.26 = (bf16[1,5,96,384]{3,2,1,0:T(8,128)(2,1)S(1)}, bf16[1,5,96,384]{3,2,1,0:T(8,128)(2,1)S(1)}, u32[]{:S(2)}, u32[]{:S(2)}) collective-permute-start(bf16[1,5,96,384]{3,2,1,0:T(8,128)(2,1)S(1)} %add_convert_fusion), channel_id=1, source_target_pairs={{0,6},{1,7},{2,4},{3,5},{4,2},{5,3},{6,0},{7,1},{8,14},{9,15},{10,... | collective-permute-start | bytes 1105928 | tf_op jit(solution)/shard_map/ppermute | solution.py:26
  154.2 3.3 %copy-start.35 = (bf16[2,5,96,384]{3,2,1,0:T(8,128)(2,1)S(1)}, bf16[2,5,96,384]{3,2,1,0:T(8,128)(2,1)}, u32[]{:S(2)}) copy-start(bf16[2,5,96,384]{3,2,1,0:T(8,128)(2,1)} %copy-done.34) | copy-start | bytes 2211844
  (25 other events, 25.6 us)
